TPU v7x, 32 devices: a whole 2x2x4 slice. The times are simulated.
32 devices in a mesh: grp: 16 (over z, y, core), hd: 2 (over x).
Axes of the slice: x: 2, y: 2, z: 4, core: 2. Of those that a mesh axis runs over, the one named last changes fastest.
Arguments:
- tokens: bfloat16 [4096, 1536], P(('grp', 'hd')), may hold values from -6 to 6
- positions: int32 [4096], P('grp'), may hold values from -1 to 127, as said below
- attn_gain: float32 [1536], replicated, may hold values from 0.1 to 1.9
- w_query: bfloat16 [1536, 1536], P(None, 'hd'), may hold values from -0.15625 to 0.15625
- w_keyval: bfloat16 [1536, 8, 128], P(None, 'hd'), may hold values from -0.15625 to 0.15625
- w_out: bfloat16 [1536, 1536], P(None, 'grp'), may hold values from -0.15625 to 0.15625
- moe_gain: float32 [1536], replicated, may hold values from 0.1 to 1.9
- router: bfloat16 [1536, 40], replicated, may hold values from -0.15625 to 0.15625
- w_gate_up: bfloat16 [2, 1536, 1024], P('hd', 'grp'), may hold values from -0.15625 to 0.15625
- w_down: bfloat16 [2, 512, 1536], P('hd', 'grp'), may hold values from -0.25 to 0.25
- expert_ids: int32 [4096, 8], P(('grp', 'hd')), may hold values from 0 to 39, as said below
- cache_slot: int32 [4096], P('grp'), may hold values from -1 to 8191, as said below
- kv_cache: bfloat16 [8192, 8, 128], P('grp', 'hd'), may hold values from -6 to 6
Outputs:
- layer_out: bfloat16 [4096, 1536], P(('grp', 'hd'))
- cache_after: bfloat16 [8192, 8, 128], P('grp', 'hd')
Inputs may be any that keep to these rules, and one draw needn't show every extreme that they name: Inside each segment the positions count up by one from 0 over consecutive tokens; a segment holds at most 128 tokens, and the one starting at token 0 holds exactly 128; padding tokens have -1. `expert_ids`: each row names 8 different experts. In each aligned block of 128 rows (the rows of one device) each expert below 2 is named by at most 32 rows, and some expert below 2 by exactly 32. A token has -1 exactly when its position is -1; other tokens have distinct slots. cache_slot // 512 is the slot's owner. The tokens of one aligned block of 256 tokens hold at most 32 slots of any one owner, and the first block holds exactly 32 slots of the last owner.
All inputs are finite; a program needn't handle non-finite values.
Results may differ from a plain program's by a relative error of at most 0.0095.
Values may be sent and summed in bfloat16 or wider, within the bound.
No kernel may reach another device: no remote copies, remote signals or barrier semaphores. Data moves between devices by JAX's collectives and lax.ppermute only.
A program may use at most 64 MiB of HBM per device.

v0:
```python
import functools

import jax
import jax.numpy as jnp
import numpy as np
from jax import lax
from jax.experimental import pallas as pl
from jax.experimental.pallas import tpu as pltpu
from jax.sharding import PartitionSpec as P

norm_eps = 1e-05
rope_base = 10000.0
bf16 = jnp.bfloat16
f32 = jnp.float32
LAST_DIMS = (((1,), (1,)), ((), ()))


def ring_cycle(groups):
    rows = groups // 4
    return [2 * r for r in range(rows)] + [2 * r + 1 for r in reversed(range(rows))]


def ring_pairs(groups):
    cycle = ring_cycle(groups)
    count = len(cycle)
    pairs = []
    for place, pair in enumerate(cycle):
        pairs.append((2 * pair, 2 * cycle[(place + 1) % count]))
        pairs.append((2 * pair + 1, 2 * cycle[(place - 1) % count] + 1))
    return pairs


def sibling_pairs(groups):
    return [(g, g ^ 1) for g in range(groups)]


def ring_sources(groups, me):
    count = groups // 2
    rows = count // 2
    side, pair = me % 2, me // 2
    row, col = pair // 2, pair % 2
    place = jnp.where(col == 0, row, count - 1 - row)

    def block(core, steps):
        there = (place + (2 * core - 1) * steps + count) % count
        other = jnp.where(there < rows, 2 * there, 2 * (count - 1 - there) + 1)
        return [2 * other + core, 2 * other + 1 - core]

    full = (count - 1) // 2
    listed = [me, me + 1 - 2 * side]
    for core in (side, 1 - side):
        for steps in range(1, full + 1):
            listed += block(core, steps)
    return listed + [block(side, count // 2)[0], block(1 - side, count // 2)[0]]


def ring_gather(unit, groups):
    across = functools.partial(lax.ppermute, axis_name="grp", perm=ring_pairs(groups))
    beside = functools.partial(lax.ppermute, axis_name="grp", perm=sibling_pairs(groups))
    held = jnp.concatenate([unit, beside(unit)], axis=0)
    parts = [held]
    mine = []
    for _ in range((groups // 2 - 1) // 2):
        held = across(held)
        mine.append(held)
    last = across(held[: unit.shape[0]])
    return parts + mine + [beside(part) for part in mine] + [last, beside(last)]


def start_parts(groups, parts, unit_rows, pieces, sems):
    sources = ring_sources(groups, lax.axis_index("grp"))
    copies = []
    shard = 0
    for part in parts:
        for unit in range(part.shape[0] // unit_rows):
            for first, rows, lanes, target, scale, offset, to_lane in pieces:
                at = pl.multiple_of(sources[shard] * scale + offset, 16)
                copy = pltpu.make_async_copy(
                    part.at[pl.ds(unit * unit_rows + first, rows), lanes],
                    target.at[pl.ds(at, rows), to_lane],
                    sems.at[len(copies)],
                )
                copy.start()
                copies.append(copy)
            shard += 1
    return copies


VMEM = pl.BlockSpec(memory_space=pltpu.VMEM)
ANY = pl.BlockSpec(memory_space=pl.ANY)
PARAMS = pltpu.CompilerParams(vmem_limit_bytes=40 << 20)


def cost(flops, nbytes):
    return pl.CostEstimate(flops=flops, bytes_accessed=nbytes, transcendentals=0)


def normalized(floats, gain):
    factor = lax.rsqrt(jnp.mean(floats * floats, axis=-1, keepdims=True) + norm_eps)
    return (floats * factor * gain).astype(bf16)


def fetch(pairs, sems):
    copies = []
    for index, (source, target) in enumerate(pairs):
        copies.append(pltpu.make_async_copy(source, target, sems.at[index]))
        copies[-1].start()
    return copies


def pack_kernel(up, down, w_out, expert_unit, out_unit, sems):
    width = up.shape[1]
    rest = down.shape[1] - width
    up_rows, down_rows = up.shape[0], down.shape[0]
    half = down_rows // 2
    lane = lax.axis_index("hd")
    first = pl.multiple_of(lane * out_unit.shape[1], out_unit.shape[1])
    tail = up_rows + down_rows
    copies = fetch(
        [
            (w_out.at[:, pl.ds(first, out_unit.shape[1])], out_unit),
            (up, expert_unit.at[pl.ds(0, up_rows), :]),
            (down.at[:, pl.ds(0, width)], expert_unit.at[pl.ds(up_rows, down_rows), :]),
            (down.at[pl.ds(0, half), pl.ds(width, rest)], expert_unit.at[pl.ds(tail, half), pl.ds(0, rest)]),
            (
                down.at[pl.ds(half, half), pl.ds(width, rest)],
                expert_unit.at[pl.ds(tail, half), pl.ds(rest, rest)],
            ),
        ],
        sems,
    )
    for copy in copies:
        copy.wait()


def pack(up, down, w_out_t):
    unit = (up.shape[0] + down.shape[0] + down.shape[0] // 2, up.shape[1])
    return pl.pallas_call(
        pack_kernel,
        out_shape=(
            jax.ShapeDtypeStruct(unit, bf16),
            jax.ShapeDtypeStruct((w_out_t.shape[0], w_out_t.shape[1] // 2), bf16),
        ),
        in_specs=[ANY] * 3,
        out_specs=(ANY, ANY),
        scratch_shapes=[pltpu.SemaphoreType.DMA((5,))],
        compiler_params=PARAMS,
        cost_estimate=cost(0, 4 * unit[0] * unit[1]),
        name="pack",
    )(up, down, w_out_t)


def as_column(row, eye):
    return jnp.sum(jnp.where(eye, row, 0.0), axis=1, keepdims=True)


def prepare_kernel(
    groups, slots_dev, positions, slots, ids, cosine, sine, past, named, place, spread, send, tags
):
    lane = lax.axis_index("hd")
    block = positions.shape[1]

    def iota(shape, dim):
        return lax.broadcasted_iota(jnp.int32, shape, dim)

    eye = iota((block, block), 0) == iota((block, block), 1)
    reach = as_column(jnp.maximum(positions[...], 0).astype(f32), eye)
    past[...] = jnp.broadcast_to(reach, past.shape)
    column = iota((8, 128), 1)
    exponent = (column % 32).astype(f32) * (-2.0 / 64)
    inverse_freq = jnp.exp(exponent * np.float32(np.log(rope_base)))[:1, :]
    angles = reach * inverse_freq
    cosine[...] = jnp.cos(angles)
    turned = jnp.sin(angles)
    sine[...] = jnp.where(iota(angles.shape, 1) % 64 < 32, -turned, turned)

    tokens = ids.shape[1]
    experts = named.shape[1]
    cap = place.shape[0] // 2
    expert = iota((experts, tokens), 0)
    hit = jnp.zeros((experts, tokens), f32)
    for index in range(ids.shape[0]):
        hit = jnp.where(ids[index : index + 1, :] == expert, 1.0, hit)
    small_eye = (iota((tokens, tokens), 0) == iota((tokens, tokens), 1)).astype(f32)
    named[...] = lax.dot_general(small_eye, hit, LAST_DIMS, preferred_element_type=f32)
    upto = (iota((tokens, tokens), 0) <= iota((tokens, tokens), 1)).astype(f32)
    rank = jnp.dot(hit[:8, :], upto, preferred_element_type=f32) - 1.0
    slot = iota((2 * cap, tokens), 0).astype(f32)
    placed = jnp.zeros((2 * cap, tokens), f32)
    for live in range(2):
        order = jnp.where(lane == live, 0, cap).astype(f32)
        member = hit[live : live + 1, :] > 0.0
        placed = jnp.where(member & (slot == rank[live : live + 1, :] + order), 1.0, placed)
    place[...] = placed.astype(bf16)
    spread[...] = lax.dot_general(small_eye, placed, LAST_DIMS, preferred_element_type=f32).astype(bf16)

    where = slots[...]
    owner = jnp.where(where >= 0, where // slots_dev, -1)
    owner_hit = (iota((groups, block), 0) == owner).astype(f32)
    before = (iota((block, block), 0) <= iota((block, block), 1)).astype(f32)
    running = jnp.dot(owner_hit, before, preferred_element_type=f32)
    owner_rank = jnp.sum(owner_hit * running, axis=0, keepdims=True) - 1.0
    capc = send.shape[0] // groups
    row = jnp.where(owner >= 0, owner * capc + owner_rank.astype(jnp.int32), -1)
    send[...] = (iota(send.shape, 0) == row).astype(bf16)
    inside = jnp.where(where >= 0, where % slots_dev, 0)
    high = as_column((inside // 64 + 1).astype(f32), eye)
    low = as_column((inside % 64).astype(f32), eye)
    spot = iota(tags.shape, 1)
    tags[...] = jnp.where(spot == 0, high, jnp.where(spot == 1, low, 0.0)).astype(bf16)


def prepare(groups, slots_dev, positions, slots, ids, experts):
    block, tokens = positions.shape[0], ids.shape[0]
    cap = tokens // 4
    capc = 2 * block // groups
    shapes = [
        ((block, 128), f32),
        ((block, 128), f32),
        ((block, 128), f32),
        ((tokens, experts), f32),
        ((2 * cap, tokens), bf16),
        ((tokens, 2 * cap), bf16),
        ((groups * capc, block), bf16),
        ((block, 128), bf16),
    ]
    return pl.pallas_call(
        functools.partial(prepare_kernel, groups, slots_dev),
        out_shape=tuple(jax.ShapeDtypeStruct(shape, kind) for shape, kind in shapes),
        in_specs=[VMEM] * 3,
        out_specs=(VMEM,) * len(shapes),
        compiler_params=PARAMS,
        cost_estimate=cost(0, 1 << 20),
        name="prepare",
    )(positions[None], slots[None], ids.T)


def project_kernel(
    own, other, gain, cosine, sine, w_query, w_keyval, q_out, kv_out, seam_out, raw, rows, sems
):
    count = own.shape[0]
    lane = lax.axis_index("hd")
    mine = pl.multiple_of(lane * count, count)
    theirs = pl.multiple_of((1 - lane) * count, count)
    copies = fetch([(own, raw.at[0]), (other, raw.at[1])], sems)
    cos_q, sin_q = cosine[...], sine[...]
    column = lax.broadcasted_iota(jnp.int32, cos_q.shape, 1)
    lower = column % 64 < 32
    cos_kv = jnp.where(column < 64, cos_q, 1.0)
    sin_kv = jnp.where(column < 64, sin_q, 0.0)
    for index, first in ((0, mine), (1, theirs)):
        copies[index].wait()
        rows[pl.ds(first, count), :] = normalized(raw[index].astype(f32), gain[...])
    width = 256
    for weights, out, cos, sin in ((w_keyval, kv_out, cos_kv, sin_kv), (w_query, q_out, cos_q, sin_q)):
        for first in range(0, weights.shape[1], width):
            made = jnp.dot(rows[...], weights[:, first : first + width], preferred_element_type=f32)
            for part in range(0, width, 128):
                here = made[:, part : part + 128]
                turned = jnp.where(lower, pltpu.roll(here, 96, 1), pltpu.roll(here, 32, 1))
                done = (here * cos + turned * sin).astype(bf16)
                out[:, first + part : first + part + 128] = done
                if out is kv_out:
                    seam_out[:, first + part : first + part + 128] = done[count:, :]


def project(own, other, gain, cosine, sine, w_query, flat_kv):
    count, width = own.shape
    made = w_query.shape[1] + flat_kv.shape[1]
    return pl.pallas_call(
        project_kernel,
        out_shape=(
            jax.ShapeDtypeStruct((2 * count, w_query.shape[1]), bf16),
            jax.ShapeDtypeStruct((2 * count, flat_kv.shape[1]), bf16),
            jax.ShapeDtypeStruct((count, flat_kv.shape[1]), bf16),
        ),
        in_specs=[ANY] * 2 + [VMEM] * 5,
        out_specs=(VMEM, VMEM, VMEM),
        scratch_shapes=[
            pltpu.VMEM((2, count, width), bf16),
            pltpu.VMEM((2 * count, width), bf16),
            pltpu.SemaphoreType.DMA((2,)),
        ],
        compiler_params=PARAMS,
        cost_estimate=cost(4 * count * width * made, 2 * width * made),
        name="project",
    )(own, other, gain, cosine, sine, w_query, flat_kv)


def attend_kernel(flip, groups, unit_rows, n_parts, q, kv, seam, past, *refs):
    parts, (out, window, mixed, w_out, sems, seam_sem) = refs[:n_parts], refs[n_parts:]
    count = seam.shape[0]
    all_lanes = pl.ds(0, w_out.shape[1])
    copies = start_parts(
        groups, parts, unit_rows, [(0, unit_rows, all_lanes, w_out, unit_rows, 0, all_lanes)], sems
    )
    lane = lax.axis_index("hd")
    which = (1 - lane) if flip else lane
    first = pl.multiple_of(which * count, count)

    @pl.when(which == 0)
    def _():
        copy = pltpu.make_async_copy(seam, window.at[pl.ds(0, count), :], seam_sem)
        copy.start()
        copy.wait()

    @pl.when(which != 0)
    def _():
        window[:count, :] = kv[:count, :]

    window[count:, :] = kv[pl.ds(first, count), :]
    head = 64
    kv_heads = kv.shape[1] // (2 * head)
    per_kv = q.shape[1] // head // kv_heads
    shape = (per_kv * count, 2 * count)
    row = lax.broadcasted_iota(jnp.int32, shape, 0) % count + count
    col = lax.broadcasted_iota(jnp.int32, shape, 1)
    reach = past[pl.ds(first, count), :][:, :1].astype(jnp.int32)
    reach = jnp.concatenate([reach] * per_kv, axis=0)
    visible = (col <= row) & (col >= row - reach)
    for kv_head in range(kv_heads):
        lanes = 2 * head * kv_head
        keys = window[:, lanes : lanes + head]
        values = window[:, lanes + head : lanes + 2 * head]
        at = kv_head * per_kv * head
        query = jnp.concatenate(
            [q[pl.ds(first, count), at + i * head : at + (i + 1) * head] for i in range(per_kv)], axis=0
        )
        scores = lax.dot_general(query, keys, LAST_DIMS, preferred_element_type=f32)
        raised = jnp.where(visible, jnp.exp(scores * head ** (-0.5)), 0.0)
        probs = (raised / jnp.sum(raised, axis=-1, keepdims=True)).astype(bf16)
        made = jnp.dot(probs, values, preferred_element_type=f32).astype(bf16)
        for i in range(per_kv):
            mixed[:, at + i * head : at + (i + 1) * head] = made[i * count : (i + 1) * count, :]
    for copy in copies:
        copy.wait()
    out[...] = lax.dot_general(
        mixed[...], w_out[...], LAST_DIMS, preferred_element_type=f32
    ).astype(out.dtype)


def attend(flip, out_type, groups, q, kv, seam, past, parts, unit):
    count = seam.shape[0]
    width = groups * unit.shape[0]
    return pl.pallas_call(
        functools.partial(attend_kernel, flip, groups, unit.shape[0], len(parts)),
        out_shape=jax.ShapeDtypeStruct((count, width), out_type),
        in_specs=[VMEM, VMEM, ANY, VMEM] + [ANY] * len(parts),
        out_specs=VMEM,
        scratch_shapes=[
            pltpu.VMEM((2 * count, kv.shape[1]), bf16),
            pltpu.VMEM((count, q.shape[1]), bf16),
            pltpu.VMEM((width, unit.shape[1]), bf16),
            pltpu.SemaphoreType.DMA((groups,)),
            pltpu.SemaphoreType.DMA,
        ],
        compiler_params=PARAMS,
        cost_estimate=cost(2 * count * width * unit.shape[1], 2 * width * unit.shape[1]),
        name="attend_send" if flip else "attend_keep",
    )(q, kv, seam, past, *parts)


def route_kernel(tokens, mine, arrived, gain, router, named, place, residual, gates, own, sent, got, sems):
    copies = fetch([(arrived, got)], sems)
    copies[0].wait()
    added = tokens[...].astype(f32) + (mine[...] + got[...].astype(f32))
    residual[...] = added.astype(bf16)
    moe_in = normalized(added.astype(bf16).astype(f32), gain[...])
    rows = jnp.dot(place[...], moe_in, preferred_element_type=f32).astype(bf16)
    cap = own.shape[0]
    own[...] = rows[:cap, :]
    sent[...] = rows[cap:, :]
    logits = lax.dot_general(moe_in, router[...], LAST_DIMS, preferred_element_type=f32)
    raised = jnp.where(named[...] > 0, jnp.exp(logits), 0.0)
    gates[...] = raised / jnp.sum(raised, axis=-1, keepdims=True)


def route(tokens, mine, arrived, gain, router_t, named, place):
    cap = place.shape[0] // 2
    return pl.pallas_call(
        route_kernel,
        out_shape=(
            jax.ShapeDtypeStruct(tokens.shape, bf16),
            jax.ShapeDtypeStruct(named.shape, f32),
            jax.ShapeDtypeStruct((cap, tokens.shape[1]), bf16),
            jax.ShapeDtypeStruct((cap, tokens.shape[1]), bf16),
        ),
        in_specs=[VMEM, VMEM, ANY] + [VMEM] * 4,
        out_specs=(VMEM,) * 4,
        scratch_shapes=[pltpu.VMEM(tokens.shape, bf16), pltpu.SemaphoreType.DMA((1,))],
        compiler_params=PARAMS,
        cost_estimate=cost(0, 2 << 20),
        name="route",
    )(tokens, mine, arrived, gain, router_t, named, place)


def expert_kernel(groups, unit_rows, up_rows, down_rows, n_parts, own, other, *refs):
    parts = refs[:n_parts]
    own_out, other_out, rows, gate_up, down, sems, row_sems = refs[n_parts:]
    width = gate_up.shape[1]
    rest = down.shape[1] - width
    half = down_rows // 2
    count = own.shape[0]
    arriving = fetch(
        [(own, rows.at[pl.ds(0, count), :]), (other, rows.at[pl.ds(count, count), :])], row_sems
    )
    copies = start_parts(
        groups,
        parts,
        unit_rows,
        [(0, up_rows, pl.ds(0, width), gate_up, up_rows, 0, pl.ds(0, width))],
        sems.at[0],
    )
    tail = up_rows + down_rows
    later = start_parts(
        groups,
        parts,
        unit_rows,
        [
            (up_rows, down_rows, pl.ds(0, width), down, down_rows, 0, pl.ds(0, width)),
            (tail, half, pl.ds(0, rest), down, down_rows, 0, pl.ds(width, rest)),
            (tail, half, pl.ds(rest, rest), down, down_rows, half, pl.ds(width, rest)),
        ],
        sems.at[1],
    )
    for copy in arriving + copies:
        copy.wait()
    both = jnp.dot(rows[...], gate_up[...], preferred_element_type=f32)
    gate, up = both[:, : width // 2], both[:, width // 2 :]
    hidden = (gate / (1.0 + jnp.exp(-gate)) * up).astype(bf16)
    for copy in later:
        copy.wait()
    made = jnp.dot(hidden, down[...], preferred_element_type=f32).astype(bf16)
    own_out[...] = made[:count, :]
    other_out[...] = made[count:, :]


def expert(groups, own, other, parts, unit, up_rows, down_rows):
    count, model = own.shape
    return pl.pallas_call(
        functools.partial(expert_kernel, groups, unit.shape[0], up_rows, down_rows, len(parts)),
        out_shape=(jax.ShapeDtypeStruct(own.shape, bf16),) * 2,
        in_specs=[ANY] * (2 + len(parts)),
        out_specs=(VMEM, VMEM),
        scratch_shapes=[
            pltpu.VMEM((2 * count, model), bf16),
            pltpu.VMEM((groups * up_rows, unit.shape[1]), bf16),
            pltpu.VMEM((groups * down_rows, model), bf16),
            pltpu.SemaphoreType.DMA((2, 3 * groups)),
            pltpu.SemaphoreType.DMA((2,)),
        ],
        compiler_params=PARAMS,
        cost_estimate=cost(4 * count * unit.shape[1] * unit.shape[0] * groups, 4 << 20),
        name="expert",
    )(own, other, *parts)


def combine_kernel(residual, gates, spread, own, returned, out, got, sems):
    lane = lax.axis_index("hd")
    copies = fetch([(own, got.at[0]), (returned, got.at[1])], sems)
    count = own.shape[0]
    column = lax.broadcasted_iota(jnp.int32, gates.shape, 1)
    total = jnp.zeros(residual.shape, f32)
    for index in range(2):
        live = lane if index == 0 else 1 - lane
        weight = jnp.sum(jnp.where(column == live, gates[...], 0.0), axis=-1, keepdims=True)
        copies[index].wait()
        picked = jnp.dot(
            spread[:, index * count : (index + 1) * count], got[index], preferred_element_type=f32
        )
        total += weight * picked
    out[...] = (residual[...].astype(f32) + total).astype(bf16)


def combine(residual, gates, spread, own, returned):
    return pl.pallas_call(
        combine_kernel,
        out_shape=jax.ShapeDtypeStruct(residual.shape, bf16),
        in_specs=[VMEM] * 3 + [ANY] * 2,
        out_specs=VMEM,
        scratch_shapes=[pltpu.VMEM((2,) + own.shape, bf16), pltpu.SemaphoreType.DMA((2,))],
        compiler_params=PARAMS,
        cost_estimate=cost(0, 1 << 20),
        name="combine",
    )(residual, gates, spread, own, returned)


def two_lane_shards(
    tokens,
    positions,
    attn_gain,
    w_query,
    w_keyval,
    w_out,
    moe_gain,
    router,
    w_gate_up,
    w_down,
    expert_ids,
    cache_slot,
    kv_cache,
):
    groups = lax.axis_size("grp")
    tok_rows, model = tokens.shape
    block = positions.shape[0]
    kv_local, head2 = w_keyval.shape[1:]
    kv_width = kv_local * head2
    slots_dev = kv_cache.shape[0]
    capc = 2 * block // groups
    swap = functools.partial(lax.ppermute, axis_name="hd", perm=[(0, 1), (1, 0)])

    other_tokens = swap(tokens)
    up, down = w_gate_up[0], w_down[0]
    expert_unit, out_unit = pack(up, down, w_out.T)
    out_parts = ring_gather(out_unit, groups)
    expert_parts = ring_gather(expert_unit, groups)
    cosine, sine, past, named, place, spread, send, tags = prepare(
        groups, slots_dev, positions, cache_slot, expert_ids, router.shape[1]
    )

    q, kv, tail = project(
        tokens,
        other_tokens,
        attn_gain[None],
        cosine,
        sine,
        w_query,
        w_keyval.reshape(model, kv_width),
    )
    seam = lax.ppermute(tail, "grp", [(g, g + 1) for g in range(groups - 1)])
    sent = attend(True, bf16, groups, q, kv, seam, past, out_parts, out_unit)
    arrived = swap(sent)
    mine = attend(False, f32, groups, q, kv, seam, past, out_parts, out_unit)

    outgoing = jnp.dot(
        send, jnp.concatenate([kv, tags], axis=1), preferred_element_type=f32
    ).astype(bf16)
    arrived_cache = lax.all_to_all(
        outgoing.reshape(groups, capc, kv_width + 128), "grp", split_axis=0, concat_axis=0, tiled=True
    ).reshape(groups * capc, kv_width + 128)
    numbers = arrived_cache[:, kv_width : kv_width + 2].astype(jnp.int32)
    write_rows = numbers[:, 0] * 64 + numbers[:, 1] - 64
    write_hit = write_rows[None, :] == jnp.arange(slots_dev, dtype=jnp.int32)[:, None]
    written = jnp.dot(
        write_hit.astype(bf16), arrived_cache[:, :kv_width], preferred_element_type=f32
    ).astype(bf16)
    cache_after = jnp.where(
        jnp.any(write_hit, axis=1)[:, None, None], written.reshape(kv_cache.shape), kv_cache
    )

    residual, gates, own_rows, sent_rows = route(
        tokens, mine, arrived, moe_gain[None], router.T, named, place
    )
    landed = swap(sent_rows)
    own_made, back = expert(
        groups, own_rows, landed, expert_parts, expert_unit, up.shape[0], down.shape[0]
    )
    returned = swap(back)
    layer_out = combine(residual, gates, spread, own_made, returned)
    return (layer_out, cache_after)


def passed_along(value, axis, steps):
    count = lax.axis_size(axis)
    initial, last = (max(0, -steps), min(count, count - steps))
    return lax.ppermute(value, axis, [(source, source + steps) for source in range(initial, last)])


def rms_norm(row_set, norm_gain):
    floats = row_set.astype(jnp.float32)
    factor = lax.rsqrt(jnp.mean(floats * floats, axis=-1, keepdims=True) + norm_eps)
    return (floats * factor * norm_gain).astype(jnp.bfloat16)


def rotate(vectors, angle_pos):
    halves = vectors.shape[-1] // 2
    inverse_freq = rope_base ** (-2.0 * jnp.arange(halves, dtype=jnp.float32) / vectors.shape[-1])
    angles = angle_pos[:, None, None] * inverse_freq[None, None, :]
    cosine = jnp.cos(angles)
    sine_part = jnp.sin(angles)
    first_half = vectors[..., :halves]
    second_half = vectors[..., halves:]
    return jnp.concatenate(
        [
            first_half * cosine - second_half * sine_part,
            second_half * cosine + first_half * sine_part,
        ],
        axis=-1,
    )


def expert_rows(row_set, gate_up, down_rows):
    gate_and_up = jnp.dot(row_set, gate_up, preferred_element_type=jnp.float32)
    inner_width = gate_and_up.shape[1] // 2
    hidden = (jax.nn.silu(gate_and_up[:, :inner_width]) * gate_and_up[:, inner_width:]).astype(
        jnp.bfloat16
    )
    return jnp.dot(hidden, down_rows, preferred_element_type=jnp.float32).astype(jnp.bfloat16)


def attend_rows(query_blk, keys_blk, vals_blk, visible, scale_qk):
    scores = (
        jnp.einsum("qkgd,skd->kgqs", query_blk, keys_blk, preferred_element_type=jnp.float32)
        * scale_qk
    )
    weights_f = jnp.where(visible[None, None], jnp.exp(scores), 0.0)
    prob_bf = (weights_f / jnp.sum(weights_f, axis=-1, keepdims=True)).astype(jnp.bfloat16)
    return jnp.einsum("kgqs,skd->qkgd", prob_bf, vals_blk, preferred_element_type=jnp.float32)


def shards(
    tokens,
    positions,
    attn_gain,
    w_query,
    w_keyval,
    w_out,
    moe_gain,
    router,
    w_gate_up,
    w_down,
    expert_ids,
    cache_slot,
    kv_cache,
):
    lane_count = lax.axis_size("hd")
    group_count = lax.axis_size("grp")
    tok_rows = tokens.shape[0]
    model_width = tokens.shape[1]
    block_len = positions.shape[0]
    seg_most = block_len // 2
    head_dim = w_keyval.shape[2] // 2
    kv_local = w_keyval.shape[1]
    q_local = w_query.shape[1] // head_dim
    per_kv = q_local // kv_local
    expert_cap = tok_rows // 4
    normed = rms_norm(tokens, attn_gain)
    flat_kv = w_keyval.reshape(model_width, kv_local * 2 * head_dim)
    section = lax.all_gather(normed, "hd", axis=0, tiled=True)
    projected = jnp.concatenate(
        [
            jnp.dot(section, w_query, preferred_element_type=jnp.float32),
            jnp.dot(section, flat_kv, preferred_element_type=jnp.float32),
        ],
        axis=1,
    )
    angle_pos = jnp.maximum(positions, 0).astype(jnp.float32)
    queries = rotate(
        projected[:, : q_local * head_dim].reshape(block_len, q_local, head_dim), angle_pos
    ).astype(jnp.bfloat16)
    key_val = projected[:, q_local * head_dim :].reshape(block_len, kv_local, 2 * head_dim)
    rotated = rotate(key_val[:, :, :head_dim], angle_pos).astype(jnp.bfloat16)
    stored = jnp.concatenate([rotated, key_val[:, :, head_dim:].astype(jnp.bfloat16)], axis=2)
    seam_rows = passed_along(stored[block_len - seg_most :], "grp", 1)
    window = jnp.concatenate([seam_rows, stored], axis=0)
    scale_qk = head_dim ** (-0.5)
    local_rows = jnp.arange(block_len, dtype=jnp.int32)
    lowest = local_rows - jnp.maximum(positions, 0)
    pieces_out = []
    for q_block in range(2):
        first_row = q_block * seg_most
        rows_here = first_row + jnp.arange(seg_most, dtype=jnp.int32)
        cols_here = first_row - seg_most + jnp.arange(2 * seg_most, dtype=jnp.int32)
        low_here = lowest[first_row : first_row + seg_most]
        visible = (cols_here[None, :] >= low_here[:, None]) & (
            cols_here[None, :] <= rows_here[:, None]
        )
        query_blk = queries[first_row : first_row + seg_most].reshape(
            seg_most, kv_local, per_kv, head_dim
        )
        keys_blk = window[first_row : first_row + 2 * seg_most, :, :head_dim]
        vals_blk = window[first_row : first_row + 2 * seg_most, :, head_dim:]
        mixed_rows = attend_rows(query_blk, keys_blk, vals_blk, visible, scale_qk)
        pieces_out.append(mixed_rows.reshape(seg_most, q_local * head_dim).astype(jnp.bfloat16))
    attended = jnp.concatenate(pieces_out, axis=0)
    slots_dev = kv_cache.shape[0]
    capc = 2 * block_len // group_count
    live_slot = cache_slot >= 0
    owners = jnp.where(live_slot, cache_slot // slots_dev, group_count)
    owner_hit = (owners[:, None] == jnp.arange(group_count, dtype=jnp.int32)[None, :]).astype(
        jnp.bfloat16
    )
    lower_tri = (local_rows[:, None] >= local_rows[None, :]).astype(jnp.bfloat16)
    running = jnp.dot(lower_tri, owner_hit, preferred_element_type=jnp.float32)
    owner_rank = jnp.sum(running * owner_hit.astype(jnp.float32), axis=1).astype(jnp.int32) - 1
    send_rows = jnp.where(live_slot, owners * capc + owner_rank, group_count * capc)
    outgoing_cache = (
        jnp.zeros((group_count * capc, kv_local, 2 * head_dim), jnp.bfloat16)
        .at[send_rows]
        .set(stored, mode="drop")
    )
    outgoing_slots = (
        jnp.full((group_count * capc,), -1, jnp.int32)
        .at[send_rows]
        .set(cache_slot % slots_dev, mode="drop")
    )
    arrived, arrived_slots = (
        lax.all_to_all(
            outgoing_cache.reshape(group_count, capc, kv_local, 2 * head_dim),
            "grp",
            split_axis=0,
            concat_axis=0,
            tiled=True,
        ),
        lax.all_to_all(
            outgoing_slots.reshape(group_count, capc),
            "grp",
            split_axis=0,
            concat_axis=0,
            tiled=True,
        ),
    )
    flat_slots = arrived_slots.reshape(group_count * capc)
    write_rows = jnp.where(flat_slots >= 0, flat_slots, slots_dev).astype(jnp.int32)
    cache_after = kv_cache.at[write_rows].set(
        arrived.reshape(group_count * capc, kv_local, 2 * head_dim), mode="drop"
    )
    by_token = lax.all_to_all(attended, "hd", split_axis=0, concat_axis=1, tiled=True)
    attn_proj = jnp.dot(
        by_token,
        lax.all_gather(w_out, "grp", axis=1, tiled=True),
        preferred_element_type=jnp.float32,
    )
    residual = (tokens.astype(jnp.float32) + attn_proj).astype(jnp.bfloat16)
    moe_in = rms_norm(residual, moe_gain)
    logits = jnp.dot(moe_in, router, preferred_element_type=jnp.float32)
    expert_range = jnp.arange(router.shape[1], dtype=jnp.int32)
    matches_all = expert_ids[:, :, None] == expert_range[None, None, :]
    chosen = jnp.sum(jnp.where(matches_all, logits[:, None, :], 0.0), axis=2)
    raised = jnp.exp(chosen)
    gates = raised / jnp.sum(raised, axis=1, keepdims=True)
    live_range = jnp.arange(lane_count, dtype=jnp.int32)
    matches = expert_ids[:, :, None] == live_range[None, None, :]
    member = jnp.any(matches, axis=1)
    weighting = jnp.sum(jnp.where(matches, gates[:, :, None], 0.0), axis=1)
    ranking = jnp.cumsum(member.astype(jnp.int32), axis=0) - 1
    target = jnp.where(member, live_range[None, :] * expert_cap + ranking, -1)
    slot_range = jnp.arange(lane_count * expert_cap, dtype=jnp.int32)
    slot_hits = target[None, :, :] == slot_range[:, None, None]
    placing = jnp.any(slot_hits, axis=2).astype(jnp.bfloat16)
    outgoing = (
        jnp.dot(placing, moe_in, preferred_element_type=jnp.float32)
        .astype(jnp.bfloat16)
        .reshape(lane_count, expert_cap, model_width)
    )
    gate_up_all, down_all = (
        lax.all_gather(w_gate_up, "grp", axis=1, tiled=True),
        lax.all_gather(w_down, "grp", axis=1, tiled=True),
    )
    gate_up_mat = gate_up_all[0]
    down_mat = down_all[0]
    landed = lax.all_to_all(outgoing, "hd", split_axis=0, concat_axis=0, tiled=True)
    results = expert_rows(landed.reshape(-1, model_width), gate_up_mat, down_mat).reshape(landed.shape)
    returned = lax.all_to_all(results, "hd", split_axis=0, concat_axis=0, tiled=True)
    flat_returned = returned.reshape(-1, model_width)
    fetched = flat_returned[jnp.maximum(target, 0)]
    used_weight = jnp.where(member, weighting, 0.0)
    moe_total = jnp.sum(used_weight[:, :, None] * fetched.astype(jnp.float32), axis=1)
    layer_out = (residual.astype(jnp.float32) + moe_total).astype(jnp.bfloat16)
    return (layer_out, cache_after)


def solution(mesh):
    two_lanes = mesh.shape["hd"] == 2 and mesh.shape["grp"] % 8 == 0
    return jax.shard_map(
        two_lane_shards if two_lanes else shards,
        mesh=mesh,
        in_specs=(
            P(("grp", "hd"), None),
            P("grp"),
            P(),
            P(None, "hd"),
            P(None, "hd", None),
            P(None, "grp"),
            P(),
            P(),
            P("hd", "grp", None),
            P("hd", "grp", None),
            P(("grp", "hd"), None),
            P("grp"),
            P("grp", "hd", None),
        ),
        out_specs=(P(("grp", "hd"), None), P("grp", "hd", None)),
        check_vma=False,
    )
```

profile of v0, /device:TPU:0, one launch (start us, length us, event | category | flops | bytes accessed | tf_op | source)
XLA Modules:
  0.0 115.8 jit_solution(572726529249864790)
XLA Ops:
  4.3 2.6 %collective-permute-start = (bf16[128,1536]{1,0:T(8,128)(2,1)}, bf16[128,1536]{1,0:T(8,128)(2,1)S(1)}, u32[]{:S(2)}, u32[]{:S(2)}) collective-permute-start(bf16[128,1536]{1,0:T(8,128)(2,1)} %tokens.1), channel_id=1, source_target_pairs={{0,1},{1,0},{2,3},{3,2},{4,5},{5,4},{6,7},{7,6},{8,9},{9,8},{10,11... | collective-permute-start | bytes 1179656 | tf_op jit(solution)/shard_map/ppermute | solution.py:512
  7.8 1.8 %copy.22 = bf16[192,8,4,128]{3,1,2,0:T(8,128)(2,1)S(1)} copy(bf16[192,8,4,128]{3,2,1,0:T(4,128)(2,1)} %bitcast.24) | data formatting | bytes 3145728
  10.4 1.6 %collective-permute-start.14 = (bf16[288,1024]{1,0:T(8,128)(2,1)S(1)}, bf16[288,1024]{1,0:T(8,128)(2,1)}, u32[]{:S(2)}, u32[]{:S(2)}) collective-permute-start(bf16[288,1024]{1,0:T(8,128)(2,1)S(1)} %constant_dynamic-update-slice_fusion.2.refs_0_), channel_id=1, source_target_pairs={{0,8},{2,6},{8,16},{10,2},{16,24},{18,10},{24,28},{26,18},{28,20},... | collective-permute-start | bytes 1769480 | tf_op jit(solution)/shard_map/ppermute | solution.py:64
  12.1 1.6 %collective-permute-start.3 = (bf16[192,768]{1,0:T(8,128)(2,1)S(1)}, bf16[192,768]{1,0:T(8,128)(2,1)S(1)}, u32[]{:S(2)}, u32[]{:S(2)}) collective-permute-start(bf16[192,768]{1,0:T(8,128)(2,1)S(1)} %constant_dynamic-update-slice_fusion.refs_0_), channel_id=1, source_target_pairs={{0,8},{2,6},{8,16},{10,2},{16,24},{18,10},{24,28},{26,18},{28,20},... | collective-permute-start | bytes 884744 | tf_op jit(solution)/shard_map/ppermute | solution.py:64
  13.7 3.0 %collective-permute-done.other = bf16[128,1536]{1,0:T(8,128)(2,1)S(1)} collective-permute-done((bf16[128,1536]{1,0:T(8,128)(2,1)}, bf16[128,1536]{1,0:T(8,128)(2,1)S(1)}, u32[]{:S(2)}, u32[]{:S(2)}) %collective-permute-start) | collective-permute-done | bytes 393248 | tf_op jit(solution)/shard_map/ppermute | solution.py:512
  16.8 2.2 %project.1 = (bf16[256,768]{1,0:T(8,128)(2,1)S(1)}, bf16[256,512]{1,0:T(8,128)(2,1)S(1)}, bf16[128,512]{1,0:T(8,128)(2,1)S(1)}) custom-call(bf16[128,1536]{1,0:T(8,128)(2,1)S(1)} %copy-done.1, bf16[128,1536]{1,0:T(8,128)(2,1)S(1)} %collective-permute-done.other, f32[1,1536]{1,0:T(1,128)S(1)} %broadcast_in_dim.23.gain, ...), custom_call_target="tpu_custom_call" | custom-call | flops 1006632960 | bytes 3932160 | tf_op jit(solution)/shard_map/project/pallas_call | solution.py:270
  19.0 1.2 %convolution_convert_fusion = bf16[512,640]{1,0:T(8,128)(2,1)} fusion(bf16[512,256]{1,0:T(8,128)(2,1)S(1)} %get-tuple-element.38, bf16[256,128]{1,0:T(8,128)(2,1)S(1)} %get-tuple-element.39, bf16[256,512]{1,0:T(8,128)(2,1)S(1)} %get-tuple-element.24.kv), kind=kOutput, calls=%fused_computation.1 | convolution fusion | flops 168755200 | bytes 1245184 | tf_op jit(solution)/shard_map/dot_general | solution.py:535
  20.3 6.3 %all-to-all-start = ((bf16[16,32,640]{2,1,0:T(8,128)(2,1)}), bf16[16,32,640]{2,1,0:T(8,128)(2,1)}, u32[]{:S(2)}, u32[]{:S(2)}) async-start(bf16[16,32,640]{2,1,0:T(8,128)(2,1)} %bitcast.23), calls=%async_computation | async-start | bytes 1310720 | tf_op jit(solution)/shard_map/all_to_all | solution.py:538
  26.5 1.9 %collective-permute-start.15 = (bf16[288,1024]{1,0:T(8,128)(2,1)}, bf16[288,1024]{1,0:T(8,128)(2,1)}, u32[]{:S(2)}, u32[]{:S(2)}) collective-permute-start(bf16[288,1024]{1,0:T(8,128)(2,1)} %collective-permute-done.14.refs_1_), channel_id=1, source_target_pairs={{0,8},{2,6},{8,16},{10,2},{16,24},{18,10},{24,28},{26,18},{28,20},... | collective-permute-start | bytes 1769480 | tf_op jit(solution)/shard_map/ppermute | solution.py:64
  28.5 1.5 %collective-permute-start.4 = (bf16[192,768]{1,0:T(8,128)(2,1)S(1)}, bf16[192,768]{1,0:T(8,128)(2,1)S(1)}, u32[]{:S(2)}, u32[]{:S(2)}) collective-permute-start(bf16[192,768]{1,0:T(8,128)(2,1)S(1)} %collective-permute-done.3.refs_1_), channel_id=1, source_target_pairs={{0,8},{2,6},{8,16},{10,2},{16,24},{18,10},{24,28},{26,18},{28,20},... | collective-permute-start | bytes 884744 | tf_op jit(solution)/shard_map/ppermute | solution.py:64
  29.9 17.6 %collective-permute-done.4.refs_2_ = bf16[192,768]{1,0:T(8,128)(2,1)S(1)} collective-permute-done((bf16[192,768]{1,0:T(8,128)(2,1)S(1)}, bf16[192,768]{1,0:T(8,128)(2,1)S(1)}, u32[]{:S(2)}, u32[]{:S(2)}) %collective-permute-start.4) | collective-permute-done | bytes 294944 | tf_op jit(solution)/shard_map/ppermute | solution.py:64
  47.6 5.2 %collective-permute-start.5 = (bf16[192,768]{1,0:T(8,128)(2,1)S(1)}, bf16[192,768]{1,0:T(8,128)(2,1)S(1)}, u32[]{:S(2)}, u32[]{:S(2)}) collective-permute-start(bf16[192,768]{1,0:T(8,128)(2,1)S(1)} %collective-permute-done.4.refs_2_), channel_id=1, source_target_pairs={{0,8},{2,6},{8,16},{10,2},{16,24},{18,10},{24,28},{26,18},{28,20},... | collective-permute-start | bytes 884744 | tf_op jit(solution)/shard_map/ppermute | solution.py:64
  52.8 2.5 %collective-permute-start.16 = (bf16[288,1024]{1,0:T(8,128)(2,1)}, bf16[288,1024]{1,0:T(8,128)(2,1)S(1)}, u32[]{:S(2)}, u32[]{:S(2)}) collective-permute-start(bf16[288,1024]{1,0:T(8,128)(2,1)} %collective-permute-done.15.refs_2_), channel_id=1, source_target_pairs={{0,8},{2,6},{8,16},{10,2},{16,24},{18,10},{24,28},{26,18},{28,20},... | collective-permute-start | bytes 1769480 | tf_op jit(solution)/shard_map/ppermute | solution.py:64
  55.3 1.3 %collective-permute-start.1 = (bf16[128,512]{1,0:T(8,128)(2,1)}, bf16[128,512]{1,0:T(8,128)(2,1)S(1)}, u32[]{:S(2)}, u32[]{:S(2)}) collective-permute-start(bf16[128,512]{1,0:T(8,128)(2,1)} %copy-done.13), channel_id=1, source_target_pairs={{0,2},{2,4},{4,6},{6,8},{8,10},{10,12},{12,14},{14,16},{16,18},{18... | collective-permute-start | bytes 393224 | tf_op jit(solution)/shard_map/ppermute | solution.py:530
  57.2 2.4 %collective-permute-start.9 = (bf16[96,768]{1,0:T(8,128)(2,1)S(1)}, bf16[96,768]{1,0:T(8,128)(2,1)S(1)}, u32[]{:S(2)}, u32[]{:S(2)}) collective-permute-start(bf16[96,768]{1,0:T(8,128)(2,1)S(1)} %slice.24), channel_id=1, source_target_pairs={{0,8},{2,6},{8,16},{10,2},{16,24},{18,10},{24,28},{26,18},{28,20},... | collective-permute-start | bytes 442376 | tf_op jit(solution)/shard_map/ppermute | solution.py:66
  59.6 2.7 %collective-permute-start.8 = (bf16[192,768]{1,0:T(8,128)(2,1)S(1)}, bf16[192,768]{1,0:T(8,128)(2,1)S(1)}, u32[]{:S(2)}, u32[]{:S(2)}) collective-permute-start(bf16[192,768]{1,0:T(8,128)(2,1)S(1)} %collective-permute-done.5.refs_3_), channel_id=1, source_target_pairs={{0,2},{2,0},{4,6},{6,4},{8,10},{10,8},{12,14},{14,12},{16,18},{18,... | collective-permute-start | bytes 884744 | tf_op jit(solution)/shard_map/ppermute | solution.py:67
  62.3 2.7 %collective-permute-done.9.refs_7_ = bf16[96,768]{1,0:T(8,128)(2,1)S(1)} collective-permute-done((bf16[96,768]{1,0:T(8,128)(2,1)S(1)}, bf16[96,768]{1,0:T(8,128)(2,1)S(1)}, u32[]{:S(2)}, u32[]{:S(2)}) %collective-permute-start.9) | collective-permute-done | bytes 147488 | tf_op jit(solution)/shard_map/ppermute | solution.py:66
  64.9 1.3 %collective-permute-start.10 = (bf16[96,768]{1,0:T(8,128)(2,1)S(1)}, bf16[96,768]{1,0:T(8,128)(2,1)S(1)}, u32[]{:S(2)}, u32[]{:S(2)}) collective-permute-start(bf16[96,768]{1,0:T(8,128)(2,1)S(1)} %collective-permute-done.9.refs_7_), channel_id=1, source_target_pairs={{0,2},{2,0},{4,6},{6,4},{8,10},{10,8},{12,14},{14,12},{16,18},{18,... | collective-permute-start | bytes 442376 | tf_op jit(solution)/shard_map/ppermute | solution.py:67
  67.2 6.9 %attend_send.1 = bf16[128,1536]{1,0:T(8,128)(2,1)} custom-call(bf16[256,768]{1,0:T(8,128)(2,1)S(1)} %get-tuple-element.23.q, bf16[256,512]{1,0:T(8,128)(2,1)S(1)} %get-tuple-element.24.kv, bf16[128,512]{1,0:T(8,128)(2,1)S(1)} %collective-permute-done.1.seam, f32[256,128]{1,0:T(8,128)S(1)} %get-tuple-element.26.past, ...), custom_call_target="tpu_custom_call" | custom-call | flops 301989888 | bytes 2359296 | tf_op jit(solution)/shard_map/attend_send/pallas_call | solution.py:345
  74.1 1.8 %collective-permute-start.11 = (bf16[128,1536]{1,0:T(8,128)(2,1)}, bf16[128,1536]{1,0:T(8,128)(2,1)}, u32[]{:S(2)}, u32[]{:S(2)}) collective-permute-start(bf16[128,1536]{1,0:T(8,128)(2,1)} %attend_send.1), channel_id=1, source_target_pairs={{0,1},{1,0},{2,3},{3,2},{4,5},{5,4},{6,7},{7,6},{8,9},{9,8},{10,11... | collective-permute-start | bytes 1179656 | tf_op jit(solution)/shard_map/ppermute | solution.py:532
  76.8 6.3 %attend_keep.1.mine = f32[128,1536]{1,0:T(8,128)S(1)} custom-call(bf16[256,768]{1,0:T(8,128)(2,1)S(1)} %get-tuple-element.23.q, bf16[256,512]{1,0:T(8,128)(2,1)S(1)} %get-tuple-element.24.kv, bf16[128,512]{1,0:T(8,128)(2,1)S(1)} %collective-permute-done.1.seam, f32[256,128]{1,0:T(8,128)S(1)} %get-tuple-element.26.past, ...), custom_call_target="tpu_custom_call" | custom-call | flops 301989888 | bytes 2359296 | tf_op jit(solution)/shard_map/attend_keep/pallas_call | solution.py:345
  84.0 1.7 %collective-permute-start.20 = (bf16[144,1024]{1,0:T(8,128)(2,1)}, bf16[144,1024]{1,0:T(8,128)(2,1)S(1)}, u32[]{:S(2)}, u32[]{:S(2)}) collective-permute-start(bf16[144,1024]{1,0:T(8,128)(2,1)} %slice.25), channel_id=1, source_target_pairs={{0,8},{2,6},{8,16},{10,2},{16,24},{18,10},{24,28},{26,18},{28,20},... | collective-permute-start | bytes 884744 | tf_op jit(solution)/shard_map/ppermute | solution.py:66
  85.7 1.3 %collective-permute-start.19 = (bf16[288,1024]{1,0:T(8,128)(2,1)S(1)}, bf16[288,1024]{1,0:T(8,128)(2,1)}, u32[]{:S(2)}, u32[]{:S(2)}) collective-permute-start(bf16[288,1024]{1,0:T(8,128)(2,1)S(1)} %collective-permute-done.16.refs_3_), channel_id=1, source_target_pairs={{0,2},{2,0},{4,6},{6,4},{8,10},{10,8},{12,14},{14,12},{16,18},{18,... | collective-permute-start | bytes 1769480 | tf_op jit(solution)/shard_map/ppermute | solution.py:67
  88.3 3.5 %collective-permute-done.20.refs_7_ = bf16[144,1024]{1,0:T(8,128)(2,1)S(1)} collective-permute-done((bf16[144,1024]{1,0:T(8,128)(2,1)}, bf16[144,1024]{1,0:T(8,128)(2,1)S(1)}, u32[]{:S(2)}, u32[]{:S(2)}) %collective-permute-start.20) | collective-permute-done | bytes 294944 | tf_op jit(solution)/shard_map/ppermute | solution.py:66
  91.8 2.3 %convolution_convert_fusion.1 = bf16[512,512]{0,1:T(8,128)(2,1)} fusion(bf16[512,640]{1,0:T(8,128)(2,1)} %bitcast.8, s32[512]{0:T(512)S(1)} %fusion.7), kind=kOutput, calls=%fused_computation.2 | convolution fusion | flops 268959744 | bytes 1050624 | tf_op jit(solution)/shard_map/dot_general | solution.py:544
  94.1 2.1 %copy.19 = bf16[512,4,128]{2,1,0:T(4,128)(2,1)} copy(bf16[512,4,128]{0,2,1:T(8,128)(2,1)} %bitcast.25) | data formatting | bytes 1048576 | tf_op jit(solution)/shard_map/reshape | solution.py:548
  96.9 1.7 %route.1 = (bf16[128,1536]{1,0:T(8,128)(2,1)S(1)}, f32[128,40]{1,0:T(8,128)S(1)}, bf16[32,1536]{1,0:T(8,128)(2,1)S(1)}, bf16[32,1536]{1,0:T(8,128)(2,1)S(1)}) custom-call(bf16[128,1536]{1,0:T(8,128)(2,1)S(1)} %copy-done.1, f32[128,1536]{1,0:T(8,128)S(1)} %attend_keep.1.mine, bf16[128,1536]{1,0:T(8,128)(2,1)} %collective-permute-done.11.arrived, ...), custom_call_target="tpu_custom_call" | custom-call | bytes 2097152 | tf_op jit(solution)/shard_map/route/pallas_call | solution.py:380
  99.0 4.9 %collective-permute-done.12.other = bf16[32,1536]{1,0:T(8,128)(2,1)S(1)} collective-permute-done((bf16[32,1536]{1,0:T(8,128)(2,1)S(1)}, bf16[32,1536]{1,0:T(8,128)(2,1)S(1)}, u32[]{:S(2)}, u32[]{:S(2)}) %collective-permute-start.12) | collective-permute-done | bytes 98336 | tf_op jit(solution)/shard_map/ppermute | solution.py:554
  103.9 5.4 %expert.1 = (bf16[32,1536]{1,0:T(8,128)(2,1)S(1)}, bf16[32,1536]{1,0:T(8,128)(2,1)S(1)}) custom-call(bf16[32,1536]{1,0:T(8,128)(2,1)S(1)} %get-tuple-element.33.own, bf16[32,1536]{1,0:T(8,128)(2,1)S(1)} %collective-permute-done.12.other, bf16[288,1024]{1,0:T(8,128)(2,1)S(1)} %constant_dynamic-update-slice_fusion.2.refs_0_, ...), custom_call_target="tpu_custom_call" | custom-call | flops 301989888 | bytes 4194304 | tf_op jit(solution)/shard_map/expert/pallas_call | solution.py:440
  109.7 2.5 %broadcast_select_fusion = bf16[512,4,128]{2,1,0:T(4,128)(2,1)} fusion(bf16[512,4,128]{2,1,0:T(4,128)(2,1)S(1)} %copy-done.14, bf16[512,4,128]{2,1,0:T(4,128)(2,1)S(1)} %copy-done.15, pred[512]{0:T(512)(128)(4,1)S(1)} %fusion), kind=kLoop, calls=%fused_computation.7 | loop fusion | flops 262144 | bytes 1573376 | tf_op jit(solution)/shard_map/jit(_where)/select_n | solution.py:547
  112.1 1.8 %collective-permute-done.22.returned = bf16[32,1536]{1,0:T(8,128)(2,1)S(1)} collective-permute-done((bf16[32,1536]{1,0:T(8,128)(2,1)S(1)}, bf16[32,1536]{1,0:T(8,128)(2,1)S(1)}, u32[]{:S(2)}, u32[]{:S(2)}) %collective-permute-start.22) | collective-permute-done | bytes 98336 | tf_op jit(solution)/shard_map/ppermute | solution.py:558
  114.0 1.6 %combine.1 = bf16[128,1536]{1,0:T(8,128)(2,1)} custom-call(bf16[128,1536]{1,0:T(8,128)(2,1)S(1)} %get-tuple-element.30.residual, f32[128,40]{1,0:T(8,128)S(1)} %get-tuple-element.31.gates, bf16[128,64]{1,0:T(8,128)(2,1)S(1)} %get-tuple-element.32.spread, bf16[32,1536]{1,0:T(8,128)(2,1)S(1)} %get-tuple-element.36.own, ...), custom_call_target="tpu_custom_call" | custom-call | bytes 1048576 | tf_op jit(solution)/shard_map/combine/pallas_call | solution.py:476
  (74 shorter events, 11.4 us)
Async XLA Ops:
  3.8 6.6 %collective-permute-start.13 = (bf16[144,1024]{1,0:T(8,128)(2,1)S(1)}, bf16[144,1024]{1,0:T(8,128)(2,1)S(1)}, u32[]{:S(2)}, u32[]{:S(2)}) collective-permute-start(bf16[144,1024]{1,0:T(8,128)(2,1)S(1)} %get-tuple-element.35), channel_id=1, source_target_pairs={{0,2},{2,0},{4,6},{6,4},{8,10},{10,8},{12,14},{14,12},{16,18},{18,... | collective-permute-start | bytes 884744 | tf_op jit(solution)/shard_map/ppermute | solution.py:60
  4.3 12.5 %collective-permute-start = (bf16[128,1536]{1,0:T(8,128)(2,1)}, bf16[128,1536]{1,0:T(8,128)(2,1)S(1)}, u32[]{:S(2)}, u32[]{:S(2)}) collective-permute-start(bf16[128,1536]{1,0:T(8,128)(2,1)} %tokens.1), channel_id=1, source_target_pairs={{0,1},{1,0},{2,3},{3,2},{4,5},{5,4},{6,7},{7,6},{8,9},{9,8},{10,11... | collective-permute-start | bytes 1179656 | tf_op jit(solution)/shard_map/ppermute | solution.py:512
  6.9 5.2 %collective-permute-start.2 = (bf16[96,768]{1,0:T(8,128)(2,1)S(1)}, bf16[96,768]{1,0:T(8,128)(2,1)S(1)}, u32[]{:S(2)}, u32[]{:S(2)}) collective-permute-start(bf16[96,768]{1,0:T(8,128)(2,1)S(1)} %get-tuple-element.27), channel_id=1, source_target_pairs={{0,2},{2,0},{4,6},{6,4},{8,10},{10,8},{12,14},{14,12},{16,18},{18,... | collective-permute-start | bytes 442376 | tf_op jit(solution)/shard_map/ppermute | solution.py:60
  7.8 9.0 %copy-start = (bf16[1536,768]{1,0:T(8,128)(2,1)S(1)}, bf16[1536,768]{1,0:T(8,128)(2,1)}, u32[]{:S(2)}) copy-start(bf16[1536,768]{1,0:T(8,128)(2,1)} %w_query.1) | copy-start | bytes 7077892
  7.8 9.0 %copy-start.1 = (bf16[128,1536]{1,0:T(8,128)(2,1)S(1)}, bf16[128,1536]{1,0:T(8,128)(2,1)}, u32[]{:S(2)}) copy-start(bf16[128,1536]{1,0:T(8,128)(2,1)} %tokens.1) | copy-start | bytes 1179652
  10.4 8.6 %copy-start.8 = (bf16[64,128]{1,0:T(8,128)(2,1)}, bf16[64,128]{1,0:T(8,128)(2,1)S(1)}, u32[]{:S(2)}) copy-start(bf16[64,128]{1,0:T(8,128)(2,1)S(1)} %get-tuple-element.29.place) | copy-start | bytes 49156
  10.4 16.1 %collective-permute-start.14 = (bf16[288,1024]{1,0:T(8,128)(2,1)S(1)}, bf16[288,1024]{1,0:T(8,128)(2,1)}, u32[]{:S(2)}, u32[]{:S(2)}) collective-permute-start(bf16[288,1024]{1,0:T(8,128)(2,1)S(1)} %constant_dynamic-update-slice_fusion.2.refs_0_), channel_id=1, source_target_pairs={{0,8},{2,6},{8,16},{10,2},{16,24},{18,10},{24,28},{26,18},{28,20},... | collective-permute-start | bytes 1769480 | tf_op jit(solution)/shard_map/ppermute | solution.py:64
  12.1 16.4 %collective-permute-start.3 = (bf16[192,768]{1,0:T(8,128)(2,1)S(1)}, bf16[192,768]{1,0:T(8,128)(2,1)S(1)}, u32[]{:S(2)}, u32[]{:S(2)}) collective-permute-start(bf16[192,768]{1,0:T(8,128)(2,1)S(1)} %constant_dynamic-update-slice_fusion.refs_0_), channel_id=1, source_target_pairs={{0,8},{2,6},{8,16},{10,2},{16,24},{18,10},{24,28},{26,18},{28,20},... | collective-permute-start | bytes 884744 | tf_op jit(solution)/shard_map/ppermute | solution.py:64
  19.0 47.2 %copy-start.16 = (f32[1536]{0:T(1024)S(1)}, f32[1536]{0:T(1024)}, u32[]{:S(2)}) copy-start(f32[1536]{0:T(1024)} %param.19) | copy-start | bytes 18436
  20.3 66.8 %all-to-all-start = ((bf16[16,32,640]{2,1,0:T(8,128)(2,1)}), bf16[16,32,640]{2,1,0:T(8,128)(2,1)}, u32[]{:S(2)}, u32[]{:S(2)}) async-start(bf16[16,32,640]{2,1,0:T(8,128)(2,1)} %bitcast.23), calls=%async_computation | async-start | bytes 1310720 | tf_op jit(solution)/shard_map/all_to_all | solution.py:538
  26.5 26.3 %collective-permute-start.15 = (bf16[288,1024]{1,0:T(8,128)(2,1)}, bf16[288,1024]{1,0:T(8,128)(2,1)}, u32[]{:S(2)}, u32[]{:S(2)}) collective-permute-start(bf16[288,1024]{1,0:T(8,128)(2,1)} %collective-permute-done.14.refs_1_), channel_id=1, source_target_pairs={{0,8},{2,6},{8,16},{10,2},{16,24},{18,10},{24,28},{26,18},{28,20},... | collective-permute-start | bytes 1769480 | tf_op jit(solution)/shard_map/ppermute | solution.py:64
  28.5 45.6 %copy-start.2 = (bf16[192,768]{1,0:T(8,128)(2,1)}, bf16[192,768]{1,0:T(8,128)(2,1)S(1)}, u32[]{:S(2)}) copy-start(bf16[192,768]{1,0:T(8,128)(2,1)S(1)} %collective-permute-done.3.refs_1_) | copy-start | bytes 884740
  28.5 19.1 %collective-permute-start.4 = (bf16[192,768]{1,0:T(8,128)(2,1)S(1)}, bf16[192,768]{1,0:T(8,128)(2,1)S(1)}, u32[]{:S(2)}, u32[]{:S(2)}) collective-permute-start(bf16[192,768]{1,0:T(8,128)(2,1)S(1)} %collective-permute-done.3.refs_1_), channel_id=1, source_target_pairs={{0,8},{2,6},{8,16},{10,2},{16,24},{18,10},{24,28},{26,18},{28,20},... | collective-permute-start | bytes 884744 | tf_op jit(solution)/shard_map/ppermute | solution.py:64
  47.6 9.6 %collective-permute-start.5 = (bf16[192,768]{1,0:T(8,128)(2,1)S(1)}, bf16[192,768]{1,0:T(8,128)(2,1)S(1)}, u32[]{:S(2)}, u32[]{:S(2)}) collective-permute-start(bf16[192,768]{1,0:T(8,128)(2,1)S(1)} %collective-permute-done.4.refs_2_), channel_id=1, source_target_pairs={{0,8},{2,6},{8,16},{10,2},{16,24},{18,10},{24,28},{26,18},{28,20},... | collective-permute-start | bytes 884744 | tf_op jit(solution)/shard_map/ppermute | solution.py:64
  52.8 30.5 %collective-permute-start.16 = (bf16[288,1024]{1,0:T(8,128)(2,1)}, bf16[288,1024]{1,0:T(8,128)(2,1)S(1)}, u32[]{:S(2)}, u32[]{:S(2)}) collective-permute-start(bf16[288,1024]{1,0:T(8,128)(2,1)} %collective-permute-done.15.refs_2_), channel_id=1, source_target_pairs={{0,8},{2,6},{8,16},{10,2},{16,24},{18,10},{24,28},{26,18},{28,20},... | collective-permute-start | bytes 1769480 | tf_op jit(solution)/shard_map/ppermute | solution.py:64
  55.3 4.3 %collective-permute-start.1 = (bf16[128,512]{1,0:T(8,128)(2,1)}, bf16[128,512]{1,0:T(8,128)(2,1)S(1)}, u32[]{:S(2)}, u32[]{:S(2)}) collective-permute-start(bf16[128,512]{1,0:T(8,128)(2,1)} %copy-done.13), channel_id=1, source_target_pairs={{0,2},{2,4},{4,6},{6,8},{8,10},{10,12},{12,14},{14,16},{16,18},{18... | collective-permute-start | bytes 393224 | tf_op jit(solution)/shard_map/ppermute | solution.py:530
  56.6 9.6 %collective-permute-start.6 = (bf16[192,768]{1,0:T(8,128)(2,1)S(1)}, bf16[192,768]{1,0:T(8,128)(2,1)S(1)}, u32[]{:S(2)}, u32[]{:S(2)}) collective-permute-start(bf16[192,768]{1,0:T(8,128)(2,1)S(1)} %collective-permute-done.3.refs_1_), channel_id=1, source_target_pairs={{0,2},{2,0},{4,6},{6,4},{8,10},{10,8},{12,14},{14,12},{16,18},{18,... | collective-permute-start | bytes 884744 | tf_op jit(solution)/shard_map/ppermute | solution.py:67
  56.9 9.4 %collective-permute-start.7 = (bf16[192,768]{1,0:T(8,128)(2,1)S(1)}, bf16[192,768]{1,0:T(8,128)(2,1)S(1)}, u32[]{:S(2)}, u32[]{:S(2)}) collective-permute-start(bf16[192,768]{1,0:T(8,128)(2,1)S(1)} %collective-permute-done.4.refs_2_), channel_id=1, source_target_pairs={{0,2},{2,0},{4,6},{6,4},{8,10},{10,8},{12,14},{14,12},{16,18},{18,... | collective-permute-start | bytes 884744 | tf_op jit(solution)/shard_map/ppermute | solution.py:67
  57.2 7.8 %collective-permute-start.9 = (bf16[96,768]{1,0:T(8,128)(2,1)S(1)}, bf16[96,768]{1,0:T(8,128)(2,1)S(1)}, u32[]{:S(2)}, u32[]{:S(2)}) collective-permute-start(bf16[96,768]{1,0:T(8,128)(2,1)S(1)} %slice.24), channel_id=1, source_target_pairs={{0,8},{2,6},{8,16},{10,2},{16,24},{18,10},{24,28},{26,18},{28,20},... | collective-permute-start | bytes 442376 | tf_op jit(solution)/shard_map/ppermute | solution.py:66
  59.6 7.6 %collective-permute-start.8 = (bf16[192,768]{1,0:T(8,128)(2,1)S(1)}, bf16[192,768]{1,0:T(8,128)(2,1)S(1)}, u32[]{:S(2)}, u32[]{:S(2)}) collective-permute-start(bf16[192,768]{1,0:T(8,128)(2,1)S(1)} %collective-permute-done.5.refs_3_), channel_id=1, source_target_pairs={{0,2},{2,0},{4,6},{6,4},{8,10},{10,8},{12,14},{14,12},{16,18},{18,... | collective-permute-start | bytes 884744 | tf_op jit(solution)/shard_map/ppermute | solution.py:67
  64.9 2.3 %collective-permute-start.10 = (bf16[96,768]{1,0:T(8,128)(2,1)S(1)}, bf16[96,768]{1,0:T(8,128)(2,1)S(1)}, u32[]{:S(2)}, u32[]{:S(2)}) collective-permute-start(bf16[96,768]{1,0:T(8,128)(2,1)S(1)} %collective-permute-done.9.refs_7_), channel_id=1, source_target_pairs={{0,2},{2,0},{4,6},{6,4},{8,10},{10,8},{12,14},{14,12},{16,18},{18,... | collective-permute-start | bytes 442376 | tf_op jit(solution)/shard_map/ppermute | solution.py:67
  66.2 32.8 %collective-permute-start.17 = (bf16[288,1024]{1,0:T(8,128)(2,1)}, bf16[288,1024]{1,0:T(8,128)(2,1)}, u32[]{:S(2)}, u32[]{:S(2)}) collective-permute-start(bf16[288,1024]{1,0:T(8,128)(2,1)} %collective-permute-done.14.refs_1_), channel_id=1, source_target_pairs={{0,2},{2,0},{4,6},{6,4},{8,10},{10,8},{12,14},{14,12},{16,18},{18,... | collective-permute-start | bytes 1769480 | tf_op jit(solution)/shard_map/ppermute | solution.py:67
  74.1 22.1 %collective-permute-start.11 = (bf16[128,1536]{1,0:T(8,128)(2,1)}, bf16[128,1536]{1,0:T(8,128)(2,1)}, u32[]{:S(2)}, u32[]{:S(2)}) collective-permute-start(bf16[128,1536]{1,0:T(8,128)(2,1)} %attend_send.1), channel_id=1, source_target_pairs={{0,1},{1,0},{2,3},{3,2},{4,5},{5,4},{6,7},{7,6},{8,9},{9,8},{10,11... | collective-permute-start | bytes 1179656 | tf_op jit(solution)/shard_map/ppermute | solution.py:532
  83.1 20.8 %collective-permute-start.18 = (bf16[288,1024]{1,0:T(8,128)(2,1)}, bf16[288,1024]{1,0:T(8,128)(2,1)S(1)}, u32[]{:S(2)}, u32[]{:S(2)}) collective-permute-start(bf16[288,1024]{1,0:T(8,128)(2,1)} %collective-permute-done.15.refs_2_), channel_id=1, source_target_pairs={{0,2},{2,0},{4,6},{6,4},{8,10},{10,8},{12,14},{14,12},{16,18},{18,... | collective-permute-start | bytes 1769480 | tf_op jit(solution)/shard_map/ppermute | solution.py:67
  84.0 7.8 %collective-permute-start.20 = (bf16[144,1024]{1,0:T(8,128)(2,1)}, bf16[144,1024]{1,0:T(8,128)(2,1)S(1)}, u32[]{:S(2)}, u32[]{:S(2)}) collective-permute-start(bf16[144,1024]{1,0:T(8,128)(2,1)} %slice.25), channel_id=1, source_target_pairs={{0,8},{2,6},{8,16},{10,2},{16,24},{18,10},{24,28},{26,18},{28,20},... | collective-permute-start | bytes 884744 | tf_op jit(solution)/shard_map/ppermute | solution.py:66
  85.7 18.1 %collective-permute-start.19 = (bf16[288,1024]{1,0:T(8,128)(2,1)S(1)}, bf16[288,1024]{1,0:T(8,128)(2,1)}, u32[]{:S(2)}, u32[]{:S(2)}) collective-permute-start(bf16[288,1024]{1,0:T(8,128)(2,1)S(1)} %collective-permute-done.16.refs_3_), channel_id=1, source_target_pairs={{0,2},{2,0},{4,6},{6,4},{8,10},{10,8},{12,14},{14,12},{16,18},{18,... | collective-permute-start | bytes 1769480 | tf_op jit(solution)/shard_map/ppermute | solution.py:67
  88.0 8.2 %copy-start.6 = (bf16[1536,40]{0,1:T(8,128)(2,1)S(1)}, bf16[1536,40]{0,1:T(8,128)(2,1)}, u32[]{:S(2)}) copy-start(bf16[1536,40]{0,1:T(8,128)(2,1)} %param.20) | copy-start | bytes 368644
  91.8 12.1 %collective-permute-start.21 = (bf16[144,1024]{1,0:T(8,128)(2,1)S(1)}, bf16[144,1024]{1,0:T(8,128)(2,1)}, u32[]{:S(2)}, u32[]{:S(2)}) collective-permute-start(bf16[144,1024]{1,0:T(8,128)(2,1)S(1)} %collective-permute-done.20.refs_7_), channel_id=1, source_target_pairs={{0,2},{2,0},{4,6},{6,4},{8,10},{10,8},{12,14},{14,12},{16,18},{18,... | collective-permute-start | bytes 884744 | tf_op jit(solution)/shard_map/ppermute | solution.py:67
  98.6 5.3 %collective-permute-start.12 = (bf16[32,1536]{1,0:T(8,128)(2,1)S(1)}, bf16[32,1536]{1,0:T(8,128)(2,1)S(1)}, u32[]{:S(2)}, u32[]{:S(2)}) collective-permute-start(bf16[32,1536]{1,0:T(8,128)(2,1)S(1)} %get-tuple-element.34), channel_id=1, source_target_pairs={{0,1},{1,0},{2,3},{3,2},{4,5},{5,4},{6,7},{7,6},{8,9},{9,8},{10,11... | collective-permute-start | bytes 294920 | tf_op jit(solution)/shard_map/ppermute | solution.py:554
  103.9 5.8 %copy-start.14 = (bf16[512,4,128]{2,1,0:T(4,128)(2,1)S(1)}, bf16[512,4,128]{2,1,0:T(4,128)(2,1)}, u32[]{:S(2)}) copy-start(bf16[512,4,128]{2,1,0:T(4,128)(2,1)} %copy.19) | copy-start | bytes 1572868
  103.9 5.8 %copy-start.15 = (bf16[512,4,128]{2,1,0:T(4,128)(2,1)S(1)}, bf16[512,4,128]{2,1,0:T(4,128)(2,1)}, u32[]{:S(2)}) copy-start(bf16[512,4,128]{2,1,0:T(4,128)(2,1)} %param.25) | copy-start | bytes 1572868
  109.3 4.7 %collective-permute-start.22 = (bf16[32,1536]{1,0:T(8,128)(2,1)S(1)}, bf16[32,1536]{1,0:T(8,128)(2,1)S(1)}, u32[]{:S(2)}, u32[]{:S(2)}) collective-permute-start(bf16[32,1536]{1,0:T(8,128)(2,1)S(1)} %get-tuple-element.37), channel_id=1, source_target_pairs={{0,1},{1,0},{2,3},{3,2},{4,5},{5,4},{6,7},{7,6},{8,9},{9,8},{10,11... | collective-permute-start | bytes 294920 | tf_op jit(solution)/shard_map/ppermute | solution.py:558
  (9 other events, 11.4 us)
where the time goes:
time: 116 us
  starting transfers between devices  37.7 us (33%)
  waiting for transfers between devices  34.5 us (30%)
  Pallas kernels  25.1 us (22%)
  local copies, waits for them, and re-layouts  9.95 us (9%)
  other arithmetic  3.83 us (3%)
  matrix products  3.59 us (3%)
    ppermute x6, waiting for transfers between devices, ring_gather(): held = across(held)  17.7 us
    ppermute x6, starting transfers between devices, ring_gather(): held = across(held)  14.3 us
    pallas_call x2, Pallas kernels, attend(): pl.pallas_call(functools.partial(attend_kernel, flip, groups, unit.shape[...  13.2 us
    unnamed x37, local copies, waits for them, and re-layouts  6.38 us
    all_to_all x1, starting transfers between devices, two_lane_shards(): lax.all_to_all(outgoing.reshape(groups, capc, kv_width + 128), 'grp', spl...  6.25 us
    ppermute x2, waiting for transfers between devices, ring_gather(): last = across(held[:unit.shape[0]])  6.2 us
    ppermute x8, starting transfers between devices, ring_gather(): return parts + mine + [beside(part) for part in mine] + [last, beside(last)]  6.04 us
    pallas_call x1, Pallas kernels, expert(): pl.pallas_call(functools.partial(expert_kernel, groups, unit.shape[0], up...  5.38 us
  transfers between devices with their start and end apart: 24, of which 7 were waited for; matrix products, arithmetic and copies ran while one was open for 11% of the time, Pallas kernels for 15%

commit v1 on v0

--- a/solution.py
+++ b/solution.py
@@ -54,17 +54,33 @@
     return listed + [block(side, count // 2)[0], block(1 - side, count // 2)[0]]
 
 
-def ring_gather(unit, groups):
-    across = functools.partial(lax.ppermute, axis_name="grp", perm=ring_pairs(groups))
-    beside = functools.partial(lax.ppermute, axis_name="grp", perm=sibling_pairs(groups))
-    held = jnp.concatenate([unit, beside(unit)], axis=0)
-    parts = [held]
-    mine = []
-    for _ in range((groups // 2 - 1) // 2):
-        held = across(held)
-        mine.append(held)
-    last = across(held[: unit.shape[0]])
-    return parts + mine + [beside(part) for part in mine] + [last, beside(last)]
+class Ring:
+    def __init__(self, unit, groups):
+        self.across = functools.partial(lax.ppermute, axis_name="grp", perm=ring_pairs(groups))
+        self.beside = functools.partial(lax.ppermute, axis_name="grp", perm=sibling_pairs(groups))
+        self.full = (groups // 2 - 1) // 2
+        self.unit = unit
+        self.mine = [jnp.concatenate([unit, self.beside(unit)], axis=0)]
+        self.near = []
+
+    def step(self):
+        held = self.mine[-1]
+        if len(self.mine) > self.full:
+            held = held[: self.unit.shape[0]]
+        self.mine.append(self.across(held))
+
+    def pin(self, *others):
+        done = lax.optimization_barrier((self.mine[-1],) + others)
+        self.mine[-1] = done[0]
+        return done[1:] if len(others) > 1 else done[1]
+
+    def share(self):
+        for index in range(1 + len(self.near), len(self.mine)):
+            self.near.append(self.beside(self.mine[index]))
+
+    def parts(self):
+        full = self.full
+        return self.mine[: full + 1] + self.near[:full] + [self.mine[full + 1], self.near[full]]
 
 
 def start_parts(groups, parts, unit_rows, pieces, sems):
@@ -88,6 +104,7 @@
 
 VMEM = pl.BlockSpec(memory_space=pltpu.VMEM)
 ANY = pl.BlockSpec(memory_space=pl.ANY)
+HBM = pl.BlockSpec(memory_space=pltpu.HBM)
 PARAMS = pltpu.CompilerParams(vmem_limit_bytes=40 << 20)
 
 
@@ -141,7 +158,7 @@
             jax.ShapeDtypeStruct(unit, bf16),
             jax.ShapeDtypeStruct((w_out_t.shape[0], w_out_t.shape[1] // 2), bf16),
         ),
-        in_specs=[ANY] * 3,
+        in_specs=[HBM] * 3,
         out_specs=(ANY, ANY),
         scratch_shapes=[pltpu.SemaphoreType.DMA((5,))],
         compiler_params=PARAMS,
@@ -287,77 +304,86 @@
     )(own, other, gain, cosine, sine, w_query, flat_kv)
 
 
-def attend_kernel(flip, groups, unit_rows, n_parts, q, kv, seam, past, *refs):
-    parts, (out, window, mixed, w_out, sems, seam_sem) = refs[:n_parts], refs[n_parts:]
+def attend_kernel(q, kv, seam, past, mixed, window, sem):
     count = seam.shape[0]
+    copy = pltpu.make_async_copy(seam, window.at[pl.ds(0, count), :], sem)
+    copy.start()
+    window[count:, :] = kv[...]
+    head = 64
+    kv_heads = kv.shape[1] // (2 * head)
+    per_kv = q.shape[1] // head // kv_heads
+    shape = (count, 2 * count)
+    row = lax.broadcasted_iota(jnp.int32, shape, 0) + count
+    col = lax.broadcasted_iota(jnp.int32, shape, 1)
+    for half in (1, 0):
+        first = half * count
+        if half == 0:
+            copy.wait()
+        reach = past[first : first + count, :1].astype(jnp.int32)
+        visible = (col <= row) & (col >= row - reach)
+        for kv_head in range(kv_heads):
+            lanes = 2 * head * kv_head
+            keys = window[first : first + 2 * count, lanes : lanes + head]
+            values = window[first : first + 2 * count, lanes + head : lanes + 2 * head]
+            for index in range(per_kv):
+                at = (kv_head * per_kv + index) * head
+                query = q[first : first + count, at : at + head]
+                scores = lax.dot_general(query, keys, LAST_DIMS, preferred_element_type=f32)
+                raised = jnp.where(visible, jnp.exp(scores * head ** (-0.5)), 0.0)
+                probs = (raised / jnp.sum(raised, axis=-1, keepdims=True)).astype(bf16)
+                made = jnp.dot(probs, values, preferred_element_type=f32)
+                mixed[first : first + count, at : at + head] = made.astype(bf16)
+
+
+def attend(q, kv, seam, past):
+    count = seam.shape[0]
+    return pl.pallas_call(
+        attend_kernel,
+        out_shape=jax.ShapeDtypeStruct(q.shape, bf16),
+        in_specs=[VMEM, VMEM, ANY, VMEM],
+        out_specs=VMEM,
+        scratch_shapes=[
+            pltpu.VMEM((3 * count, kv.shape[1]), bf16),
+            pltpu.SemaphoreType.DMA,
+        ],
+        compiler_params=PARAMS,
+        cost_estimate=cost(8 * count * count * q.shape[1], 1 << 20),
+        name="attend",
+    )(q, kv, seam, past)
+
+
+def outward_kernel(flip, groups, unit_rows, n_parts, mixed, *refs):
+    parts, (out, w_out, sems) = refs[:n_parts], refs[n_parts:]
     all_lanes = pl.ds(0, w_out.shape[1])
     copies = start_parts(
         groups, parts, unit_rows, [(0, unit_rows, all_lanes, w_out, unit_rows, 0, all_lanes)], sems
     )
+    count = out.shape[0]
     lane = lax.axis_index("hd")
-    which = (1 - lane) if flip else lane
-    first = pl.multiple_of(which * count, count)
-
-    @pl.when(which == 0)
-    def _():
-        copy = pltpu.make_async_copy(seam, window.at[pl.ds(0, count), :], seam_sem)
-        copy.start()
-        copy.wait()
-
-    @pl.when(which != 0)
-    def _():
-        window[:count, :] = kv[:count, :]
-
-    window[count:, :] = kv[pl.ds(first, count), :]
-    head = 64
-    kv_heads = kv.shape[1] // (2 * head)
-    per_kv = q.shape[1] // head // kv_heads
-    shape = (per_kv * count, 2 * count)
-    row = lax.broadcasted_iota(jnp.int32, shape, 0) % count + count
-    col = lax.broadcasted_iota(jnp.int32, shape, 1)
-    reach = past[pl.ds(first, count), :][:, :1].astype(jnp.int32)
-    reach = jnp.concatenate([reach] * per_kv, axis=0)
-    visible = (col <= row) & (col >= row - reach)
-    for kv_head in range(kv_heads):
-        lanes = 2 * head * kv_head
-        keys = window[:, lanes : lanes + head]
-        values = window[:, lanes + head : lanes + 2 * head]
-        at = kv_head * per_kv * head
-        query = jnp.concatenate(
-            [q[pl.ds(first, count), at + i * head : at + (i + 1) * head] for i in range(per_kv)], axis=0
-        )
-        scores = lax.dot_general(query, keys, LAST_DIMS, preferred_element_type=f32)
-        raised = jnp.where(visible, jnp.exp(scores * head ** (-0.5)), 0.0)
-        probs = (raised / jnp.sum(raised, axis=-1, keepdims=True)).astype(bf16)
-        made = jnp.dot(probs, values, preferred_element_type=f32).astype(bf16)
-        for i in range(per_kv):
-            mixed[:, at + i * head : at + (i + 1) * head] = made[i * count : (i + 1) * count, :]
+    first = pl.multiple_of(((1 - lane) if flip else lane) * count, count)
     for copy in copies:
         copy.wait()
     out[...] = lax.dot_general(
-        mixed[...], w_out[...], LAST_DIMS, preferred_element_type=f32
+        mixed[pl.ds(first, count), :], w_out[...], LAST_DIMS, preferred_element_type=f32
     ).astype(out.dtype)
 
 
-def attend(flip, out_type, groups, q, kv, seam, past, parts, unit):
-    count = seam.shape[0]
+def outward(flip, out_type, groups, mixed, parts, unit):
+    count = mixed.shape[0] // 2
     width = groups * unit.shape[0]
     return pl.pallas_call(
-        functools.partial(attend_kernel, flip, groups, unit.shape[0], len(parts)),
+        functools.partial(outward_kernel, flip, groups, unit.shape[0], len(parts)),
         out_shape=jax.ShapeDtypeStruct((count, width), out_type),
-        in_specs=[VMEM, VMEM, ANY, VMEM] + [ANY] * len(parts),
+        in_specs=[VMEM] + [ANY] * len(parts),
         out_specs=VMEM,
         scratch_shapes=[
-            pltpu.VMEM((2 * count, kv.shape[1]), bf16),
-            pltpu.VMEM((count, q.shape[1]), bf16),
             pltpu.VMEM((width, unit.shape[1]), bf16),
             pltpu.SemaphoreType.DMA((groups,)),
-            pltpu.SemaphoreType.DMA,
         ],
         compiler_params=PARAMS,
         cost_estimate=cost(2 * count * width * unit.shape[1], 2 * width * unit.shape[1]),
-        name="attend_send" if flip else "attend_keep",
-    )(q, kv, seam, past, *parts)
+        name="outward_send" if flip else "outward_keep",
+    )(mixed, *parts)
 
 
 def route_kernel(tokens, mine, arrived, gain, router, named, place, residual, gates, own, sent, got, sems):
@@ -512,12 +538,15 @@
     other_tokens = swap(tokens)
     up, down = w_gate_up[0], w_down[0]
     expert_unit, out_unit = pack(up, down, w_out.T)
-    out_parts = ring_gather(out_unit, groups)
-    expert_parts = ring_gather(expert_unit, groups)
+    out_ring = Ring(out_unit, groups)
+    out_ring.step()
+    expert_ring = Ring(expert_unit, groups)
+    expert_ring.step()
     cosine, sine, past, named, place, spread, send, tags = prepare(
         groups, slots_dev, positions, cache_slot, expert_ids, router.shape[1]
     )
-
+    other_tokens = out_ring.pin(other_tokens)
+    out_ring.step()
     q, kv, tail = project(
         tokens,
         other_tokens,
@@ -527,14 +556,31 @@
         w_query,
         w_keyval.reshape(model, kv_width),
     )
+    q, kv = out_ring.pin(q, kv)
     seam = lax.ppermute(tail, "grp", [(g, g + 1) for g in range(groups - 1)])
-    sent = attend(True, bf16, groups, q, kv, seam, past, out_parts, out_unit)
+    out_ring.step()
+    out_ring.share()
+    q, kv = expert_ring.pin(q, kv)
+    expert_ring.step()
+    mixed = attend(q, kv, seam, past)
+    mixed = out_ring.pin(mixed)
+    out_ring.step()
+    out_ring.share()
+    mixed = expert_ring.pin(mixed)
+    expert_ring.step()
+    expert_ring.share()
+    out_parts = out_ring.parts()
+    sent = outward(True, bf16, groups, mixed, out_parts, out_unit)
     arrived = swap(sent)
-    mine = attend(False, f32, groups, q, kv, seam, past, out_parts, out_unit)
+    mixed, send = lax.optimization_barrier((mixed, send, sent))[:2]
+    mine = outward(False, f32, groups, mixed, out_parts, out_unit)
 
     outgoing = jnp.dot(
         send, jnp.concatenate([kv, tags], axis=1), preferred_element_type=f32
     ).astype(bf16)
+    outgoing = expert_ring.pin(outgoing)
+    expert_ring.step()
+    expert_ring.share()
     arrived_cache = lax.all_to_all(
         outgoing.reshape(groups, capc, kv_width + 128), "grp", split_axis=0, concat_axis=0, tiled=True
     ).reshape(groups * capc, kv_width + 128)
@@ -553,7 +599,7 @@
     )
     landed = swap(sent_rows)
     own_made, back = expert(
-        groups, own_rows, landed, expert_parts, expert_unit, up.shape[0], down.shape[0]
+        groups, own_rows, landed, expert_ring.parts(), expert_unit, up.shape[0], down.shape[0]
     )
     returned = swap(back)
     layer_out = combine(residual, gates, spread, own_made, returned)

time: 116 us -> 118 us (1.017)
  the two profiles are of different devices: /device:TPU:0 before, /device:TPU:14 now
where the time goes in v1:
time: 118 us
  waiting for transfers between devices  54.1 us (46%)
  Pallas kernels  25.5 us (22%)
  starting transfers between devices  21.7 us (18%)
  local copies, waits for them, and re-layouts  8.68 us (7%)
  other arithmetic  3.86 us (3%)
  matrix products  2.78 us (2%)
    ppermute x8, waiting for transfers between devices, step(): self.mine.append(self.across(held))  30.5 us
    pallas_call x2, Pallas kernels, outward(): pl.pallas_call(functools.partial(outward_kernel, flip, groups, unit.shape...  9.09 us
    ppermute x1, waiting for transfers between devices, two_lane_shards(): other_tokens = swap(tokens)  8.92 us
    all_to_all x1, starting transfers between devices, two_lane_shards(): lax.all_to_all(outgoing.reshape(groups, capc, kv_width + 128), 'grp', spl...  8.29 us
    pallas_call x1, Pallas kernels, expert(): pl.pallas_call(functools.partial(expert_kernel, groups, unit.shape[0], up...  7.85 us
    unnamed x53, local copies, waits for them, and re-layouts  7.6 us
    ppermute x8, starting transfers between devices, step(): self.mine.append(self.across(held))  6.35 us
    ppermute x1, waiting for transfers between devices, two_lane_shards(): landed = swap(sent_rows)  4.67 us
  transfers between devices with their start and end apart: 24, of which 10 were waited for; matrix products, arithmetic and copies ran while one was open for 2% of the time, Pallas kernels for 21%

profile of v1, /device:TPU:14, one launch (start us, length us, event | category | flops | bytes accessed | tf_op | source)
XLA Modules:
  0.0 117.7 jit_solution(6842673270641877707)
XLA Ops:
  0.6 1.0 copy-done.15
  1.6 0.9 copy-done.16
  2.5 0.9 copy-done.18
  6.7 8.9 %collective-permute-done.4.other = bf16[128,1536]{1,0:T(8,128)(2,1)S(1)} collective-permute-done((bf16[128,1536]{1,0:T(8,128)(2,1)}, bf16[128,1536]{1,0:T(8,128)(2,1)S(1)}, u32[]{:S(2)}, u32[]{:S(2)}) %collective-permute-start.4) | collective-permute-done | bytes 393248 | tf_op jit(solution)/shard_map/ppermute | solution.py:538
  17.9 2.2 %project.1 = (bf16[256,768]{1,0:T(8,128)(2,1)S(1)}, bf16[256,512]{1,0:T(8,128)(2,1)S(1)}, bf16[128,512]{1,0:T(8,128)(2,1)S(1)}) custom-call(bf16[128,1536]{1,0:T(8,128)(2,1)S(1)} %copy-done.1, bf16[128,1536]{1,0:T(8,128)(2,1)S(1)} %collective-permute-done.4.other, f32[1,1536]{1,0:T(1,128)S(1)} %broadcast_in_dim.23.gain, ...), custom_call_target="tpu_custom_call" | custom-call | flops 1006632960 | bytes 3932160 | tf_op jit(solution)/shard_map/project/pallas_call | solution.py:287
  20.1 2.3 %collective-permute-done.5.refs_2_ = bf16[192,768]{1,0:T(8,128)(2,1)S(1)} collective-permute-done((bf16[192,768]{1,0:T(8,128)(2,1)S(1)}, bf16[192,768]{1,0:T(8,128)(2,1)S(1)}, u32[]{:S(2)}, u32[]{:S(2)}) %collective-permute-start.5) | collective-permute-done | bytes 294944 | tf_op jit(solution)/shard_map/ppermute | solution.py:70
  23.4 2.3 %collective-permute-start.8 = (bf16[128,512]{1,0:T(8,128)(2,1)S(1)}, bf16[128,512]{1,0:T(8,128)(2,1)S(1)}, u32[]{:S(2)}, u32[]{:S(2)}) collective-permute-start(bf16[128,512]{1,0:T(8,128)(2,1)S(1)} %get-tuple-element.51), channel_id=1, source_target_pairs={{0,2},{2,4},{4,6},{6,8},{8,10},{10,12},{12,14},{14,16},{16,18},{18... | collective-permute-start | bytes 393224 | tf_op jit(solution)/shard_map/ppermute | solution.py:560
  25.7 3.9 %collective-permute-done.8.seam = bf16[128,512]{1,0:T(8,128)(2,1)S(1)} collective-permute-done((bf16[128,512]{1,0:T(8,128)(2,1)S(1)}, bf16[128,512]{1,0:T(8,128)(2,1)S(1)}, u32[]{:S(2)}, u32[]{:S(2)}) %collective-permute-start.8) | collective-permute-done | bytes 131104 | tf_op jit(solution)/shard_map/ppermute | solution.py:560
  29.6 2.8 %attend.1.mixed = bf16[256,768]{1,0:T(8,128)(2,1)S(1)} custom-call(bf16[256,768]{1,0:T(8,128)(2,1)S(1)} %get-tuple-element.49.q, bf16[256,512]{1,0:T(8,128)(2,1)S(1)} %get-tuple-element.50.kv, bf16[128,512]{1,0:T(8,128)(2,1)S(1)} %collective-permute-done.8.seam, f32[256,128]{1,0:T(8,128)S(1)} %get-tuple-element.52.past), custom_call_target="tpu_custom_call" | custom-call | flops 100663296 | bytes 1048576 | tf_op jit(solution)/shard_map/attend/pallas_call | solution.py:340
  32.5 3.0 %collective-permute-done.7.refs_3_ = bf16[192,768]{1,0:T(8,128)(2,1)S(1)} collective-permute-done((bf16[192,768]{1,0:T(8,128)(2,1)S(1)}, bf16[192,768]{1,0:T(8,128)(2,1)S(1)}, u32[]{:S(2)}, u32[]{:S(2)}) %collective-permute-start.7) | collective-permute-done | bytes 294944 | tf_op jit(solution)/shard_map/ppermute | solution.py:70
  35.5 2.6 %collective-permute-start.16 = (bf16[288,1024]{1,0:T(8,128)(2,1)S(1)}, bf16[288,1024]{1,0:T(8,128)(2,1)S(1)}, u32[]{:S(2)}, u32[]{:S(2)}) collective-permute-start(bf16[288,1024]{1,0:T(8,128)(2,1)S(1)} %collective-permute-done.6.refs_2_), channel_id=1, source_target_pairs={{0,8},{2,6},{8,16},{10,2},{16,24},{18,10},{24,28},{26,18},{28,20},... | collective-permute-start | bytes 1769480 | tf_op jit(solution)/shard_map/ppermute | solution.py:70
  39.1 7.9 %collective-permute-done.12.refs_7_ = bf16[96,768]{1,0:T(8,128)(2,1)S(1)} collective-permute-done((bf16[96,768]{1,0:T(8,128)(2,1)S(1)}, bf16[96,768]{1,0:T(8,128)(2,1)S(1)}, u32[]{:S(2)}, u32[]{:S(2)}) %collective-permute-start.12) | collective-permute-done | bytes 147488 | tf_op jit(solution)/shard_map/ppermute | solution.py:70
  47.1 1.3 %collective-permute-done.13.refs_8_ = bf16[96,768]{1,0:T(8,128)(2,1)S(1)} collective-permute-done((bf16[96,768]{1,0:T(8,128)(2,1)S(1)}, bf16[96,768]{1,0:T(8,128)(2,1)S(1)}, u32[]{:S(2)}, u32[]{:S(2)}) %collective-permute-start.13) | collective-permute-done | bytes 147488 | tf_op jit(solution)/shard_map/ppermute | solution.py:79
  48.4 4.6 %outward_send.1 = bf16[128,1536]{1,0:T(8,128)(2,1)S(1)} custom-call(bf16[256,768]{1,0:T(8,128)(2,1)S(1)} %attend.1.mixed, bf16[192,768]{1,0:T(8,128)(2,1)S(1)} %constant_dynamic-update-slice_fusion.2.refs_0_, bf16[192,768]{1,0:T(8,128)(2,1)S(1)} %collective-permute-done.3.refs_1_, bf16[192,768]{1,0:T(8,128)(2,1)S(1)} %collective-permute-done.5.refs_2_, ...), custom_call_target="tpu_custom_call" | custom-call | flops 301989888 | bytes 2359296 | tf_op jit(solution)/shard_map/outward_send/pallas_call | solution.py:374
  53.1 1.2 %convolution_convert_fusion = bf16[512,640]{1,0:T(8,128)(2,1)} fusion(bf16[512,256]{1,0:T(8,128)(2,1)S(1)} %get-tuple-element.66, bf16[256,128]{1,0:T(8,128)(2,1)S(1)} %get-tuple-element.67, bf16[256,512]{1,0:T(8,128)(2,1)S(1)} %get-tuple-element.50.kv), kind=kOutput, calls=%fused_computation.1 | convolution fusion | flops 168755200 | bytes 1245184 | tf_op jit(solution)/shard_map/dot_general | solution.py:578
  54.3 8.3 %all-to-all-start = ((bf16[16,32,640]{2,1,0:T(8,128)(2,1)}), bf16[16,32,640]{2,1,0:T(8,128)(2,1)}, u32[]{:S(2)}, u32[]{:S(2)}) async-start(bf16[16,32,640]{2,1,0:T(8,128)(2,1)} %bitcast.23), calls=%async_computation | async-start | bytes 1310720 | tf_op jit(solution)/shard_map/all_to_all | solution.py:584
  63.2 0.8 collective-permute-start.20
  63.9 0.8 collective-permute-start.19
  65.2 17.3 %collective-permute-done.20.refs_7_ = bf16[144,1024]{1,0:T(8,128)(2,1)S(1)} collective-permute-done((bf16[144,1024]{1,0:T(8,128)(2,1)S(1)}, bf16[144,1024]{1,0:T(8,128)(2,1)S(1)}, u32[]{:S(2)}, u32[]{:S(2)}) %collective-permute-start.20) | collective-permute-done | bytes 294944 | tf_op jit(solution)/shard_map/ppermute | solution.py:70
  83.3 1.0 copy-done.3
  84.3 1.0 copy-done.5
  85.2 0.9 copy-done.11
  86.1 0.9 copy-done.13
  87.0 4.5 %outward_keep.1.mine = f32[128,1536]{1,0:T(8,128)S(1)} custom-call(bf16[256,768]{1,0:T(8,128)(2,1)S(1)} %attend.1.mixed, bf16[192,768]{1,0:T(8,128)(2,1)S(1)} %constant_dynamic-update-slice_fusion.2.refs_0_, bf16[192,768]{1,0:T(8,128)(2,1)S(1)} %collective-permute-done.3.refs_1_, bf16[192,768]{1,0:T(8,128)(2,1)S(1)} %collective-permute-done.5.refs_2_, ...), custom_call_target="tpu_custom_call" | custom-call | flops 301989888 | bytes 2359296 | tf_op jit(solution)/shard_map/outward_keep/pallas_call | solution.py:374
  91.6 0.9 route.1
  93.1 4.7 %collective-permute-done.15.other = bf16[32,1536]{1,0:T(8,128)(2,1)S(1)} collective-permute-done((bf16[32,1536]{1,0:T(8,128)(2,1)S(1)}, bf16[32,1536]{1,0:T(8,128)(2,1)S(1)}, u32[]{:S(2)}, u32[]{:S(2)}) %collective-permute-start.15) | collective-permute-done | bytes 98336 | tf_op jit(solution)/shard_map/ppermute | solution.py:600
  97.8 7.8 %expert.1 = (bf16[32,1536]{1,0:T(8,128)(2,1)S(1)}, bf16[32,1536]{1,0:T(8,128)(2,1)S(1)}) custom-call(bf16[32,1536]{1,0:T(8,128)(2,1)S(1)} %get-tuple-element.63.own, bf16[32,1536]{1,0:T(8,128)(2,1)S(1)} %collective-permute-done.15.other, bf16[288,1024]{1,0:T(8,128)(2,1)S(1)} %constant_dynamic-update-slice_fusion.refs_0_, bf16[288,1024]{1,0:T(8,128)(2,1)S(1)} %copy-done.7, ...), custom_call_target="tpu_custom_call" | custom-call | flops 301989888 | bytes 4194304 | tf_op jit(solution)/shard_map/expert/pallas_call | solution.py:466
  106.2 4.1 %collective-permute-done.22.returned = bf16[32,1536]{1,0:T(8,128)(2,1)S(1)} collective-permute-done((bf16[32,1536]{1,0:T(8,128)(2,1)S(1)}, bf16[32,1536]{1,0:T(8,128)(2,1)S(1)}, u32[]{:S(2)}, u32[]{:S(2)}) %collective-permute-start.22) | collective-permute-done | bytes 98336 | tf_op jit(solution)/shard_map/ppermute | solution.py:604
  110.3 1.6 %combine.1 = bf16[128,1536]{1,0:T(8,128)(2,1)} custom-call(bf16[128,1536]{1,0:T(8,128)(2,1)S(1)} %get-tuple-element.60.residual, f32[128,40]{1,0:T(8,128)S(1)} %get-tuple-element.61.gates, bf16[128,64]{1,0:T(8,128)(2,1)S(1)} %get-tuple-element.62.spread, bf16[32,1536]{1,0:T(8,128)(2,1)S(1)} %get-tuple-element.69.own, ...), custom_call_target="tpu_custom_call" | custom-call | bytes 1048576 | tf_op jit(solution)/shard_map/combine/pallas_call | solution.py:502
  111.9 0.9 slice_convert_fusion
  113.1 1.6 %convolution_convert_fusion.1 = bf16[512,512]{0,1:T(8,128)(2,1)S(1)} fusion(bf16[512,640]{1,0:T(8,128)(2,1)} %bitcast.8, s32[512]{0:T(512)S(1)} %fusion.7), kind=kOutput, calls=%fused_computation.2 | convolution fusion | flops 268959744 | bytes 1050624 | tf_op jit(solution)/shard_map/dot_general | solution.py:590
  115.2 2.5 %broadcast_select_fusion = bf16[512,4,128]{2,1,0:T(4,128)(2,1)} fusion(bf16[512,4,128]{2,1,0:T(4,128)(2,1)S(1)} %copy.19, bf16[512,4,128]{2,1,0:T(4,128)(2,1)S(1)} %copy-done.23, pred[512]{0:T(512)(128)(4,1)S(1)} %fusion), kind=kLoop, calls=%fused_computation.7 | loop fusion | flops 262144 | bytes 1573376 | tf_op jit(solution)/shard_map/jit(_where)/select_n | solution.py:593
  (91 shorter events, 11.3 us)
Async XLA Ops:
  3.4 12.7 %copy-start.24 = (f32[1536]{0:T(1024)S(1)}, f32[1536]{0:T(1024)}, u32[]{:S(2)}) copy-start(f32[1536]{0:T(1024)} %param.15) | copy-start | bytes 18436
  3.4 12.7 %copy-start.22 = (bf16[1536,4,128]{2,1,0:T(4,128)(2,1)S(1)}, bf16[1536,4,128]{2,1,0:T(4,128)(2,1)}, u32[]{:S(2)}) copy-start(bf16[1536,4,128]{2,1,0:T(4,128)(2,1)} %param.17) | copy-start | bytes 4718596
  3.8 2.4 %collective-permute-start = (bf16[144,1024]{1,0:T(8,128)(2,1)S(1)}, bf16[144,1024]{1,0:T(8,128)(2,1)S(1)}, u32[]{:S(2)}, u32[]{:S(2)}) collective-permute-start(bf16[144,1024]{1,0:T(8,128)(2,1)S(1)} %get-tuple-element.37), channel_id=1, source_target_pairs={{0,2},{2,0},{4,6},{6,4},{8,10},{10,8},{12,14},{14,12},{16,18},{18,... | collective-permute-start | bytes 884744 | tf_op jit(solution)/shard_map/ppermute | solution.py:63
  3.9 1.8 %collective-permute-start.2 = (bf16[96,768]{1,0:T(8,128)(2,1)S(1)}, bf16[96,768]{1,0:T(8,128)(2,1)S(1)}, u32[]{:S(2)}, u32[]{:S(2)}) collective-permute-start(bf16[96,768]{1,0:T(8,128)(2,1)S(1)} %get-tuple-element.38), channel_id=1, source_target_pairs={{0,2},{2,0},{4,6},{6,4},{8,10},{10,8},{12,14},{14,12},{16,18},{18,... | collective-permute-start | bytes 442376 | tf_op jit(solution)/shard_map/ppermute | solution.py:63
  4.4 11.3 %collective-permute-start.4 = (bf16[128,1536]{1,0:T(8,128)(2,1)}, bf16[128,1536]{1,0:T(8,128)(2,1)S(1)}, u32[]{:S(2)}, u32[]{:S(2)}) collective-permute-start(bf16[128,1536]{1,0:T(8,128)(2,1)} %tokens.1), channel_id=1, source_target_pairs={{0,1},{1,0},{2,3},{3,2},{4,5},{5,4},{6,7},{7,6},{8,9},{9,8},{10,11... | collective-permute-start | bytes 1179656 | tf_op jit(solution)/shard_map/ppermute | solution.py:538
  5.7 10.0 %collective-permute-start.3 = (bf16[192,768]{1,0:T(8,128)(2,1)S(1)}, bf16[192,768]{1,0:T(8,128)(2,1)S(1)}, u32[]{:S(2)}, u32[]{:S(2)}) collective-permute-start(bf16[192,768]{1,0:T(8,128)(2,1)S(1)} %constant_dynamic-update-slice_fusion.2.refs_0_), channel_id=1, source_target_pairs={{0,8},{2,6},{8,16},{10,2},{16,24},{18,10},{24,28},{26,18},{28,20},... | collective-permute-start | bytes 884744 | tf_op jit(solution)/shard_map/ppermute | solution.py:70
  6.2 16.2 %collective-permute-start.1 = (bf16[288,1024]{1,0:T(8,128)(2,1)S(1)}, bf16[288,1024]{1,0:T(8,128)(2,1)S(1)}, u32[]{:S(2)}, u32[]{:S(2)}) collective-permute-start(bf16[288,1024]{1,0:T(8,128)(2,1)S(1)} %constant_dynamic-update-slice_fusion.refs_0_), channel_id=1, source_target_pairs={{0,8},{2,6},{8,16},{10,2},{16,24},{18,10},{24,28},{26,18},{28,20},... | collective-permute-start | bytes 1769480 | tf_op jit(solution)/shard_map/ppermute | solution.py:70
  15.7 6.7 %collective-permute-start.5 = (bf16[192,768]{1,0:T(8,128)(2,1)S(1)}, bf16[192,768]{1,0:T(8,128)(2,1)S(1)}, u32[]{:S(2)}, u32[]{:S(2)}) collective-permute-start(bf16[192,768]{1,0:T(8,128)(2,1)S(1)} %collective-permute-done.3.refs_1_), channel_id=1, source_target_pairs={{0,8},{2,6},{8,16},{10,2},{16,24},{18,10},{24,28},{26,18},{28,20},... | collective-permute-start | bytes 884744 | tf_op jit(solution)/shard_map/ppermute | solution.py:70
  22.4 30.6 %copy-start.6 = (bf16[288,1024]{1,0:T(8,128)(2,1)}, bf16[288,1024]{1,0:T(8,128)(2,1)S(1)}, u32[]{:S(2)}) copy-start(bf16[288,1024]{1,0:T(8,128)(2,1)S(1)} %collective-permute-done.1.refs_1_) | copy-start | bytes 1769476
  22.4 13.0 %collective-permute-start.6 = (bf16[288,1024]{1,0:T(8,128)(2,1)S(1)}, bf16[288,1024]{1,0:T(8,128)(2,1)S(1)}, u32[]{:S(2)}, u32[]{:S(2)}) collective-permute-start(bf16[288,1024]{1,0:T(8,128)(2,1)S(1)} %collective-permute-done.1.refs_1_), channel_id=1, source_target_pairs={{0,8},{2,6},{8,16},{10,2},{16,24},{18,10},{24,28},{26,18},{28,20},... | collective-permute-start | bytes 1769480 | tf_op jit(solution)/shard_map/ppermute | solution.py:70
  22.9 12.6 %collective-permute-start.7 = (bf16[192,768]{1,0:T(8,128)(2,1)S(1)}, bf16[192,768]{1,0:T(8,128)(2,1)S(1)}, u32[]{:S(2)}, u32[]{:S(2)}) collective-permute-start(bf16[192,768]{1,0:T(8,128)(2,1)S(1)} %collective-permute-done.5.refs_2_), channel_id=1, source_target_pairs={{0,8},{2,6},{8,16},{10,2},{16,24},{18,10},{24,28},{26,18},{28,20},... | collective-permute-start | bytes 884744 | tf_op jit(solution)/shard_map/ppermute | solution.py:70
  23.4 6.3 %collective-permute-start.8 = (bf16[128,512]{1,0:T(8,128)(2,1)S(1)}, bf16[128,512]{1,0:T(8,128)(2,1)S(1)}, u32[]{:S(2)}, u32[]{:S(2)}) collective-permute-start(bf16[128,512]{1,0:T(8,128)(2,1)S(1)} %get-tuple-element.51), channel_id=1, source_target_pairs={{0,2},{2,4},{4,6},{6,8},{8,10},{10,12},{12,14},{14,16},{16,18},{18... | collective-permute-start | bytes 393224 | tf_op jit(solution)/shard_map/ppermute | solution.py:560
  35.5 17.6 %copy-start.8 = (bf16[288,1024]{1,0:T(8,128)(2,1)}, bf16[288,1024]{1,0:T(8,128)(2,1)S(1)}, u32[]{:S(2)}) copy-start(bf16[288,1024]{1,0:T(8,128)(2,1)S(1)} %collective-permute-done.6.refs_2_) | copy-start | bytes 1769476
  35.5 18.9 %collective-permute-start.16 = (bf16[288,1024]{1,0:T(8,128)(2,1)S(1)}, bf16[288,1024]{1,0:T(8,128)(2,1)S(1)}, u32[]{:S(2)}, u32[]{:S(2)}) collective-permute-start(bf16[288,1024]{1,0:T(8,128)(2,1)S(1)} %collective-permute-done.6.refs_2_), channel_id=1, source_target_pairs={{0,8},{2,6},{8,16},{10,2},{16,24},{18,10},{24,28},{26,18},{28,20},... | collective-permute-start | bytes 1769480 | tf_op jit(solution)/shard_map/ppermute | solution.py:70
  38.1 9.1 %collective-permute-start.9 = (bf16[192,768]{1,0:T(8,128)(2,1)S(1)}, bf16[192,768]{1,0:T(8,128)(2,1)S(1)}, u32[]{:S(2)}, u32[]{:S(2)}) collective-permute-start(bf16[192,768]{1,0:T(8,128)(2,1)S(1)} %collective-permute-done.3.refs_1_), channel_id=1, source_target_pairs={{0,2},{2,0},{4,6},{6,4},{8,10},{10,8},{12,14},{14,12},{16,18},{18,... | collective-permute-start | bytes 884744 | tf_op jit(solution)/shard_map/ppermute | solution.py:79
  38.1 8.9 %collective-permute-start.12 = (bf16[96,768]{1,0:T(8,128)(2,1)S(1)}, bf16[96,768]{1,0:T(8,128)(2,1)S(1)}, u32[]{:S(2)}, u32[]{:S(2)}) collective-permute-start(bf16[96,768]{1,0:T(8,128)(2,1)S(1)} %slice.18), channel_id=1, source_target_pairs={{0,8},{2,6},{8,16},{10,2},{16,24},{18,10},{24,28},{26,18},{28,20},... | collective-permute-start | bytes 442376 | tf_op jit(solution)/shard_map/ppermute | solution.py:70
  38.6 8.5 %collective-permute-start.10 = (bf16[192,768]{1,0:T(8,128)(2,1)S(1)}, bf16[192,768]{1,0:T(8,128)(2,1)S(1)}, u32[]{:S(2)}, u32[]{:S(2)}) collective-permute-start(bf16[192,768]{1,0:T(8,128)(2,1)S(1)} %collective-permute-done.5.refs_2_), channel_id=1, source_target_pairs={{0,2},{2,0},{4,6},{6,4},{8,10},{10,8},{12,14},{14,12},{16,18},{18,... | collective-permute-start | bytes 884744 | tf_op jit(solution)/shard_map/ppermute | solution.py:79
  38.7 9.7 %collective-permute-start.11 = (bf16[192,768]{1,0:T(8,128)(2,1)S(1)}, bf16[192,768]{1,0:T(8,128)(2,1)S(1)}, u32[]{:S(2)}, u32[]{:S(2)}) collective-permute-start(bf16[192,768]{1,0:T(8,128)(2,1)S(1)} %collective-permute-done.7.refs_3_), channel_id=1, source_target_pairs={{0,2},{2,0},{4,6},{6,4},{8,10},{10,8},{12,14},{14,12},{16,18},{18,... | collective-permute-start | bytes 884744 | tf_op jit(solution)/shard_map/ppermute | solution.py:79
  47.0 6.0 %copy-start.10 = (bf16[96,768]{1,0:T(8,128)(2,1)}, bf16[96,768]{1,0:T(8,128)(2,1)S(1)}, u32[]{:S(2)}) copy-start(bf16[96,768]{1,0:T(8,128)(2,1)S(1)} %collective-permute-done.12.refs_7_) | copy-start | bytes 442372
  47.0 1.4 %collective-permute-start.13 = (bf16[96,768]{1,0:T(8,128)(2,1)S(1)}, bf16[96,768]{1,0:T(8,128)(2,1)S(1)}, u32[]{:S(2)}, u32[]{:S(2)}) collective-permute-start(bf16[96,768]{1,0:T(8,128)(2,1)S(1)} %collective-permute-done.12.refs_7_), channel_id=1, source_target_pairs={{0,2},{2,0},{4,6},{6,4},{8,10},{10,8},{12,14},{14,12},{16,18},{18,... | collective-permute-start | bytes 442376 | tf_op jit(solution)/shard_map/ppermute | solution.py:79
  47.1 5.9 %copy-start.2 = (bf16[192,768]{1,0:T(8,128)(2,1)}, bf16[192,768]{1,0:T(8,128)(2,1)S(1)}, u32[]{:S(2)}) copy-start(bf16[192,768]{1,0:T(8,128)(2,1)S(1)} %collective-permute-done.10.refs_5_) | copy-start | bytes 884740
  54.3 57.6 %all-to-all-start = ((bf16[16,32,640]{2,1,0:T(8,128)(2,1)}), bf16[16,32,640]{2,1,0:T(8,128)(2,1)}, u32[]{:S(2)}, u32[]{:S(2)}) async-start(bf16[16,32,640]{2,1,0:T(8,128)(2,1)} %bitcast.23), calls=%async_computation | async-start | bytes 1310720 | tf_op jit(solution)/shard_map/all_to_all | solution.py:584
  62.6 30.4 %collective-permute-start.17 = (bf16[288,1024]{1,0:T(8,128)(2,1)}, bf16[288,1024]{1,0:T(8,128)(2,1)S(1)}, u32[]{:S(2)}, u32[]{:S(2)}) collective-permute-start(bf16[288,1024]{1,0:T(8,128)(2,1)} %copy-done.6), channel_id=1, source_target_pairs={{0,2},{2,0},{4,6},{6,4},{8,10},{10,8},{12,14},{14,12},{16,18},{18,... | collective-permute-start | bytes 1769480 | tf_op jit(solution)/shard_map/ppermute | solution.py:79
  62.8 35.0 %collective-permute-start.18 = (bf16[288,1024]{1,0:T(8,128)(2,1)}, bf16[288,1024]{1,0:T(8,128)(2,1)S(1)}, u32[]{:S(2)}, u32[]{:S(2)}) collective-permute-start(bf16[288,1024]{1,0:T(8,128)(2,1)} %copy-done.8), channel_id=1, source_target_pairs={{0,2},{2,0},{4,6},{6,4},{8,10},{10,8},{12,14},{14,12},{16,18},{18,... | collective-permute-start | bytes 1769480 | tf_op jit(solution)/shard_map/ppermute | solution.py:79
  63.2 19.4 %collective-permute-start.20 = (bf16[144,1024]{1,0:T(8,128)(2,1)S(1)}, bf16[144,1024]{1,0:T(8,128)(2,1)S(1)}, u32[]{:S(2)}, u32[]{:S(2)}) collective-permute-start(bf16[144,1024]{1,0:T(8,128)(2,1)S(1)} %slice.19), channel_id=1, source_target_pairs={{0,8},{2,6},{8,16},{10,2},{16,24},{18,10},{24,28},{26,18},{28,20},... | collective-permute-start | bytes 884744 | tf_op jit(solution)/shard_map/ppermute | solution.py:70
  63.9 33.8 %collective-permute-start.19 = (bf16[288,1024]{1,0:T(8,128)(2,1)S(1)}, bf16[288,1024]{1,0:T(8,128)(2,1)S(1)}, u32[]{:S(2)}, u32[]{:S(2)}) collective-permute-start(bf16[288,1024]{1,0:T(8,128)(2,1)S(1)} %collective-permute-done.16.refs_3_), channel_id=1, source_target_pairs={{0,2},{2,0},{4,6},{6,4},{8,10},{10,8},{12,14},{14,12},{16,18},{18,... | collective-permute-start | bytes 1769480 | tf_op jit(solution)/shard_map/ppermute | solution.py:79
  64.7 26.8 %collective-permute-start.14 = (bf16[128,1536]{1,0:T(8,128)(2,1)}, bf16[128,1536]{1,0:T(8,128)(2,1)S(1)}, u32[]{:S(2)}, u32[]{:S(2)}) collective-permute-start(bf16[128,1536]{1,0:T(8,128)(2,1)} %copy-done.14), channel_id=1, source_target_pairs={{0,1},{1,0},{2,3},{3,2},{4,5},{5,4},{6,7},{7,6},{8,9},{9,8},{10,11... | collective-permute-start | bytes 1179656 | tf_op jit(solution)/shard_map/ppermute | solution.py:574
  82.6 15.2 %collective-permute-start.21 = (bf16[144,1024]{1,0:T(8,128)(2,1)S(1)}, bf16[144,1024]{1,0:T(8,128)(2,1)S(1)}, u32[]{:S(2)}, u32[]{:S(2)}) collective-permute-start(bf16[144,1024]{1,0:T(8,128)(2,1)S(1)} %collective-permute-done.20.refs_7_), channel_id=1, source_target_pairs={{0,2},{2,0},{4,6},{6,4},{8,10},{10,8},{12,14},{14,12},{16,18},{18,... | collective-permute-start | bytes 884744 | tf_op jit(solution)/shard_map/ppermute | solution.py:79
  91.5 6.2 %copy-start.7 = (bf16[288,1024]{1,0:T(8,128)(2,1)S(1)}, bf16[288,1024]{1,0:T(8,128)(2,1)}, u32[]{:S(2)}) copy-start(bf16[288,1024]{1,0:T(8,128)(2,1)} %copy-done.6) | copy-start | bytes 1769476
  91.5 6.2 %copy-start.9 = (bf16[288,1024]{1,0:T(8,128)(2,1)S(1)}, bf16[288,1024]{1,0:T(8,128)(2,1)}, u32[]{:S(2)}) copy-start(bf16[288,1024]{1,0:T(8,128)(2,1)} %copy-done.8) | copy-start | bytes 1769476
  92.5 5.3 %collective-permute-start.15 = (bf16[32,1536]{1,0:T(8,128)(2,1)S(1)}, bf16[32,1536]{1,0:T(8,128)(2,1)S(1)}, u32[]{:S(2)}, u32[]{:S(2)}) collective-permute-start(bf16[32,1536]{1,0:T(8,128)(2,1)S(1)} %get-tuple-element.64), channel_id=1, source_target_pairs={{0,1},{1,0},{2,3},{3,2},{4,5},{5,4},{6,7},{7,6},{8,9},{9,8},{10,11... | collective-permute-start | bytes 294920 | tf_op jit(solution)/shard_map/ppermute | solution.py:600
  105.6 4.7 %collective-permute-start.22 = (bf16[32,1536]{1,0:T(8,128)(2,1)S(1)}, bf16[32,1536]{1,0:T(8,128)(2,1)S(1)}, u32[]{:S(2)}, u32[]{:S(2)}) collective-permute-start(bf16[32,1536]{1,0:T(8,128)(2,1)S(1)} %get-tuple-element.70), channel_id=1, source_target_pairs={{0,1},{1,0},{2,3},{3,2},{4,5},{5,4},{6,7},{7,6},{8,9},{9,8},{10,11... | collective-permute-start | bytes 294920 | tf_op jit(solution)/shard_map/ppermute | solution.py:604
  (17 other events, 29.4 us)

commit v2 on v1

--- a/solution.py
+++ b/solution.py
@@ -55,18 +55,18 @@
 
 
 class Ring:
-    def __init__(self, unit, groups):
+    def __init__(self, pair, groups):
         self.across = functools.partial(lax.ppermute, axis_name="grp", perm=ring_pairs(groups))
         self.beside = functools.partial(lax.ppermute, axis_name="grp", perm=sibling_pairs(groups))
         self.full = (groups // 2 - 1) // 2
-        self.unit = unit
-        self.mine = [jnp.concatenate([unit, self.beside(unit)], axis=0)]
+        self.unit_rows = pair.shape[0] // 2
+        self.mine = [pair]
         self.near = []
 
     def step(self):
         held = self.mine[-1]
         if len(self.mine) > self.full:
-            held = held[: self.unit.shape[0]]
+            held = held[: self.unit_rows]
         self.mine.append(self.across(held))
 
     def pin(self, *others):
@@ -83,23 +83,16 @@
         return self.mine[: full + 1] + self.near[:full] + [self.mine[full + 1], self.near[full]]
 
 
-def start_parts(groups, parts, unit_rows, pieces, sems):
+def place_parts(groups, parts, unit_rows, pieces):
     sources = ring_sources(groups, lax.axis_index("grp"))
-    copies = []
     shard = 0
     for part in parts:
         for unit in range(part.shape[0] // unit_rows):
-            for first, rows, lanes, target, scale, offset, to_lane in pieces:
-                at = pl.multiple_of(sources[shard] * scale + offset, 16)
-                copy = pltpu.make_async_copy(
-                    part.at[pl.ds(unit * unit_rows + first, rows), lanes],
-                    target.at[pl.ds(at, rows), to_lane],
-                    sems.at[len(copies)],
-                )
-                copy.start()
-                copies.append(copy)
+            for first, rows, target, lane in pieces:
+                at = pl.multiple_of(sources[shard] * rows, rows)
+                start = unit * unit_rows + first
+                target[pl.ds(at, rows), lane : lane + part.shape[1]] = part[start : start + rows, :]
             shard += 1
-    return copies
 
 
 VMEM = pl.BlockSpec(memory_space=pltpu.VMEM)
@@ -125,46 +118,47 @@
     return copies
 
 
-def pack_kernel(up, down, w_out, expert_unit, out_unit, sems):
-    width = up.shape[1]
-    rest = down.shape[1] - width
-    up_rows, down_rows = up.shape[0], down.shape[0]
-    half = down_rows // 2
+def pack_kernel(*refs):
+    sources, (expert_pair, out_pair, sems) = refs[:6], refs[6:]
+    width = expert_pair.shape[1]
     lane = lax.axis_index("hd")
-    first = pl.multiple_of(lane * out_unit.shape[1], out_unit.shape[1])
-    tail = up_rows + down_rows
-    copies = fetch(
-        [
-            (w_out.at[:, pl.ds(first, out_unit.shape[1])], out_unit),
-            (up, expert_unit.at[pl.ds(0, up_rows), :]),
-            (down.at[:, pl.ds(0, width)], expert_unit.at[pl.ds(up_rows, down_rows), :]),
-            (down.at[pl.ds(0, half), pl.ds(width, rest)], expert_unit.at[pl.ds(tail, half), pl.ds(0, rest)]),
-            (
-                down.at[pl.ds(half, half), pl.ds(width, rest)],
-                expert_unit.at[pl.ds(tail, half), pl.ds(rest, rest)],
-            ),
-        ],
-        sems,
-    )
-    for copy in copies:
+    first = pl.multiple_of(lane * out_pair.shape[1], out_pair.shape[1])
+    pairs = []
+    row = 0
+    for index in range(2):
+        up, down, w_out = sources[3 * index : 3 * index + 3]
+        count = w_out.shape[0]
+        pairs.append(
+            (w_out.at[:, pl.ds(first, out_pair.shape[1])], out_pair.at[pl.ds(index * count, count), :])
+        )
+        for source in (up, down):
+            for at in range(0, source.shape[1], width):
+                pairs.append(
+                    (source.at[:, pl.ds(at, width)], expert_pair.at[pl.ds(row, source.shape[0]), :])
+                )
+                row += source.shape[0]
+    for copy in fetch(pairs, sems):
         copy.wait()
 
 
-def pack(up, down, w_out_t):
-    unit = (up.shape[0] + down.shape[0] + down.shape[0] // 2, up.shape[1])
+def pack(own, beside):
+    up, down, w_out_t = own
+    width = up.shape[1] // 2
+    pieces = [up.shape[1] // width, down.shape[1] // width]
+    unit_rows = pieces[0] * up.shape[0] + pieces[1] * down.shape[0]
     return pl.pallas_call(
         pack_kernel,
         out_shape=(
-            jax.ShapeDtypeStruct(unit, bf16),
-            jax.ShapeDtypeStruct((w_out_t.shape[0], w_out_t.shape[1] // 2), bf16),
+            jax.ShapeDtypeStruct((2 * unit_rows, width), bf16),
+            jax.ShapeDtypeStruct((2 * w_out_t.shape[0], w_out_t.shape[1] // 2), bf16),
         ),
-        in_specs=[HBM] * 3,
+        in_specs=[ANY] * 6,
         out_specs=(ANY, ANY),
-        scratch_shapes=[pltpu.SemaphoreType.DMA((5,))],
-        compiler_params=PARAMS,
-        cost_estimate=cost(0, 4 * unit[0] * unit[1]),
+        scratch_shapes=[pltpu.SemaphoreType.DMA((2 + 2 * sum(pieces),))],
+        compiler_params=PARAMS,
+        cost_estimate=cost(0, 0),
         name="pack",
-    )(up, down, w_out_t)
+    )(*own, *beside)
 
 
 def as_column(row, eye):
@@ -353,35 +347,28 @@
 
 
 def outward_kernel(flip, groups, unit_rows, n_parts, mixed, *refs):
-    parts, (out, w_out, sems) = refs[:n_parts], refs[n_parts:]
-    all_lanes = pl.ds(0, w_out.shape[1])
-    copies = start_parts(
-        groups, parts, unit_rows, [(0, unit_rows, all_lanes, w_out, unit_rows, 0, all_lanes)], sems
-    )
+    parts, (out, w_out) = refs[:n_parts], refs[n_parts:]
+    place_parts(groups, parts, unit_rows, [(0, unit_rows, w_out, 0)])
     count = out.shape[0]
     lane = lax.axis_index("hd")
     first = pl.multiple_of(((1 - lane) if flip else lane) * count, count)
-    for copy in copies:
-        copy.wait()
     out[...] = lax.dot_general(
         mixed[pl.ds(first, count), :], w_out[...], LAST_DIMS, preferred_element_type=f32
     ).astype(out.dtype)
 
 
-def outward(flip, out_type, groups, mixed, parts, unit):
+def outward(flip, out_type, groups, mixed, parts, unit_rows):
     count = mixed.shape[0] // 2
-    width = groups * unit.shape[0]
-    return pl.pallas_call(
-        functools.partial(outward_kernel, flip, groups, unit.shape[0], len(parts)),
+    width = groups * unit_rows
+    depth = parts[0].shape[1]
+    return pl.pallas_call(
+        functools.partial(outward_kernel, flip, groups, unit_rows, len(parts)),
         out_shape=jax.ShapeDtypeStruct((count, width), out_type),
-        in_specs=[VMEM] + [ANY] * len(parts),
+        in_specs=[VMEM] * (1 + len(parts)),
         out_specs=VMEM,
-        scratch_shapes=[
-            pltpu.VMEM((width, unit.shape[1]), bf16),
-            pltpu.SemaphoreType.DMA((groups,)),
-        ],
-        compiler_params=PARAMS,
-        cost_estimate=cost(2 * count * width * unit.shape[1], 2 * width * unit.shape[1]),
+        scratch_shapes=[pltpu.VMEM((width, depth), bf16)],
+        compiler_params=PARAMS,
+        cost_estimate=cost(2 * count * width * depth, 2 * width * depth),
         name="outward_send" if flip else "outward_keep",
     )(mixed, *parts)
 
@@ -420,79 +407,56 @@
     )(tokens, mine, arrived, gain, router_t, named, place)
 
 
-def expert_kernel(groups, unit_rows, up_rows, down_rows, n_parts, own, other, *refs):
+def expert_kernel(groups, up_rows, down_rows, n_parts, own, other, *refs):
     parts = refs[:n_parts]
-    own_out, other_out, rows, gate_up, down, sems, row_sems = refs[n_parts:]
-    width = gate_up.shape[1]
-    rest = down.shape[1] - width
-    half = down_rows // 2
+    own_out, other_out, rows, gate_up, down = refs[n_parts:]
+    width = parts[0].shape[1]
     count = own.shape[0]
-    arriving = fetch(
-        [(own, rows.at[pl.ds(0, count), :]), (other, rows.at[pl.ds(count, count), :])], row_sems
-    )
-    copies = start_parts(
-        groups,
-        parts,
-        unit_rows,
-        [(0, up_rows, pl.ds(0, width), gate_up, up_rows, 0, pl.ds(0, width))],
-        sems.at[0],
-    )
-    tail = up_rows + down_rows
-    later = start_parts(
-        groups,
-        parts,
-        unit_rows,
-        [
-            (up_rows, down_rows, pl.ds(0, width), down, down_rows, 0, pl.ds(0, width)),
-            (tail, half, pl.ds(0, rest), down, down_rows, 0, pl.ds(width, rest)),
-            (tail, half, pl.ds(rest, rest), down, down_rows, half, pl.ds(width, rest)),
-        ],
-        sems.at[1],
-    )
-    for copy in arriving + copies:
-        copy.wait()
+    rows[:count, :] = own[...]
+    rows[count:, :] = other[...]
+    pieces = [(i * up_rows, up_rows, gate_up, i * width) for i in range(2)]
+    pieces += [
+        (2 * up_rows + i * down_rows, down_rows, down, i * width) for i in range(down.shape[1] // width)
+    ]
+    unit_rows = pieces[-1][0] + down_rows
+    place_parts(groups, parts, unit_rows, pieces)
     both = jnp.dot(rows[...], gate_up[...], preferred_element_type=f32)
-    gate, up = both[:, : width // 2], both[:, width // 2 :]
+    gate, up = both[:, :width], both[:, width:]
     hidden = (gate / (1.0 + jnp.exp(-gate)) * up).astype(bf16)
-    for copy in later:
-        copy.wait()
     made = jnp.dot(hidden, down[...], preferred_element_type=f32).astype(bf16)
     own_out[...] = made[:count, :]
     other_out[...] = made[count:, :]
 
 
-def expert(groups, own, other, parts, unit, up_rows, down_rows):
+def expert(groups, own, other, parts, up_rows, down_rows):
     count, model = own.shape
-    return pl.pallas_call(
-        functools.partial(expert_kernel, groups, unit.shape[0], up_rows, down_rows, len(parts)),
+    width = parts[0].shape[1]
+    return pl.pallas_call(
+        functools.partial(expert_kernel, groups, up_rows, down_rows, len(parts)),
         out_shape=(jax.ShapeDtypeStruct(own.shape, bf16),) * 2,
-        in_specs=[ANY] * (2 + len(parts)),
+        in_specs=[VMEM] * (2 + len(parts)),
         out_specs=(VMEM, VMEM),
         scratch_shapes=[
             pltpu.VMEM((2 * count, model), bf16),
-            pltpu.VMEM((groups * up_rows, unit.shape[1]), bf16),
+            pltpu.VMEM((groups * up_rows, 2 * width), bf16),
             pltpu.VMEM((groups * down_rows, model), bf16),
-            pltpu.SemaphoreType.DMA((2, 3 * groups)),
-            pltpu.SemaphoreType.DMA((2,)),
         ],
         compiler_params=PARAMS,
-        cost_estimate=cost(4 * count * unit.shape[1] * unit.shape[0] * groups, 4 << 20),
+        cost_estimate=cost(4 * count * width * 9 * down_rows * groups, 4 << 20),
         name="expert",
     )(own, other, *parts)
 
 
-def combine_kernel(residual, gates, spread, own, returned, out, got, sems):
+def combine_kernel(residual, gates, spread, own, returned, out):
     lane = lax.axis_index("hd")
-    copies = fetch([(own, got.at[0]), (returned, got.at[1])], sems)
     count = own.shape[0]
     column = lax.broadcasted_iota(jnp.int32, gates.shape, 1)
     total = jnp.zeros(residual.shape, f32)
-    for index in range(2):
+    for index, made in ((0, own), (1, returned)):
         live = lane if index == 0 else 1 - lane
         weight = jnp.sum(jnp.where(column == live, gates[...], 0.0), axis=-1, keepdims=True)
-        copies[index].wait()
         picked = jnp.dot(
-            spread[:, index * count : (index + 1) * count], got[index], preferred_element_type=f32
+            spread[:, index * count : (index + 1) * count], made[...], preferred_element_type=f32
         )
         total += weight * picked
     out[...] = (residual[...].astype(f32) + total).astype(bf16)
@@ -502,13 +466,79 @@
     return pl.pallas_call(
         combine_kernel,
         out_shape=jax.ShapeDtypeStruct(residual.shape, bf16),
-        in_specs=[VMEM] * 3 + [ANY] * 2,
+        in_specs=[VMEM] * 5,
         out_specs=VMEM,
-        scratch_shapes=[pltpu.VMEM((2,) + own.shape, bf16), pltpu.SemaphoreType.DMA((2,))],
         compiler_params=PARAMS,
         cost_estimate=cost(0, 1 << 20),
         name="combine",
     )(residual, gates, spread, own, returned)
+
+
+def bundle_kernel(send, kv, tags, out):
+    groups, rows, _ = out.shape
+    heads = kv.shape[1] // 128
+    capc = send.shape[0] // groups
+    packed = jnp.dot(send[...], kv[...], preferred_element_type=f32).astype(bf16)
+    tagged = jnp.dot(send[...], tags[...], preferred_element_type=f32)
+    one = (lax.broadcasted_iota(jnp.int32, (16, 128), 0) == lax.broadcasted_iota(jnp.int32, (16, 128), 1))
+    for owner in range(groups):
+        mine = slice(owner * capc, (owner + 1) * capc)
+        for head in range(heads):
+            out[owner, head * capc : (head + 1) * capc, :] = packed[mine, head * 128 : (head + 1) * 128]
+        wide = jnp.concatenate([tagged[mine, :], jnp.zeros((128 - capc, 128), f32)], axis=0)
+        out[owner, heads * capc :, :] = lax.dot_general(
+            one.astype(f32), wide, LAST_DIMS, preferred_element_type=f32
+        ).astype(bf16)
+
+
+def bundle(groups, send, kv, tags):
+    rows = send.shape[0] // groups * (kv.shape[1] // 128) + 16
+    return pl.pallas_call(
+        bundle_kernel,
+        out_shape=jax.ShapeDtypeStruct((groups, rows, 128), bf16),
+        in_specs=[VMEM] * 3,
+        out_specs=VMEM,
+        compiler_params=PARAMS,
+        cost_estimate=cost(0, 1 << 20),
+        name="bundle",
+    )(send, kv, tags)
+
+
+def write_kernel(arrived, cache, out, rows):
+    groups, size, _ = arrived.shape
+    slots, heads, _ = cache.shape
+    capc = (size - 16) // heads
+    high, low = [], []
+    for source in range(groups):
+        for head in range(heads):
+            rows[source * capc : (source + 1) * capc, head * 128 : (head + 1) * 128] = arrived[
+                source, head * capc : (head + 1) * capc, :
+            ]
+        numbers = arrived[source, heads * capc :, :].astype(f32)
+        high.append(numbers[0:1, :capc])
+        low.append(numbers[1:2, :capc])
+    slot = jnp.concatenate(high, axis=1) * 64.0 + jnp.concatenate(low, axis=1) - 64.0
+    hit = (lax.broadcasted_iota(jnp.int32, (slots, slot.shape[1]), 0).astype(f32) == slot).astype(f32)
+    known = jnp.max(hit, axis=1, keepdims=True) > 0.0
+    made = jnp.dot(hit.astype(bf16), rows[...], preferred_element_type=f32)
+    for head in range(heads):
+        here = made[:, head * 128 : (head + 1) * 128]
+        out[:, head, :] = jnp.where(known, here, cache[:, head, :].astype(f32)).astype(bf16)
+
+
+def write(arrived, cache):
+    slots, heads, lanes = cache.shape
+    capc = (arrived.shape[1] - 16) // heads
+    return pl.pallas_call(
+        write_kernel,
+        out_shape=jax.ShapeDtypeStruct(cache.shape, bf16),
+        in_specs=[VMEM] * 2,
+        out_specs=VMEM,
+        scratch_shapes=[pltpu.VMEM((arrived.shape[0] * capc, heads * lanes), bf16)],
+        compiler_params=PARAMS,
+        cost_estimate=cost(0, 1 << 20),
+        name="write",
+    )(arrived, cache)
 
 
 def two_lane_shards(
@@ -532,19 +562,23 @@
     kv_local, head2 = w_keyval.shape[1:]
     kv_width = kv_local * head2
     slots_dev = kv_cache.shape[0]
-    capc = 2 * block // groups
     swap = functools.partial(lax.ppermute, axis_name="hd", perm=[(0, 1), (1, 0)])
 
     other_tokens = swap(tokens)
     up, down = w_gate_up[0], w_down[0]
-    expert_unit, out_unit = pack(up, down, w_out.T)
-    out_ring = Ring(out_unit, groups)
+    own = (up, down, w_out.T)
+    expert_pair, out_pair = pack(
+        own, [lax.ppermute(part, "grp", sibling_pairs(groups)) for part in own]
+    )
+    out_ring = Ring(out_pair, groups)
     out_ring.step()
-    expert_ring = Ring(expert_unit, groups)
+    expert_ring = Ring(expert_pair, groups)
     expert_ring.step()
     cosine, sine, past, named, place, spread, send, tags = prepare(
         groups, slots_dev, positions, cache_slot, expert_ids, router.shape[1]
     )
+    other_tokens = out_ring.pin(other_tokens)
+    out_ring.step()
     other_tokens = out_ring.pin(other_tokens)
     out_ring.step()
     q, kv, tail = project(
@@ -556,53 +590,36 @@
         w_query,
         w_keyval.reshape(model, kv_width),
     )
-    q, kv = out_ring.pin(q, kv)
     seam = lax.ppermute(tail, "grp", [(g, g + 1) for g in range(groups - 1)])
+    seam = out_ring.pin(seam)
     out_ring.step()
     out_ring.share()
-    q, kv = expert_ring.pin(q, kv)
+    seam = expert_ring.pin(seam)
     expert_ring.step()
     mixed = attend(q, kv, seam, past)
-    mixed = out_ring.pin(mixed)
-    out_ring.step()
-    out_ring.share()
-    mixed = expert_ring.pin(mixed)
+    out_parts = out_ring.parts()
+    sent = outward(True, bf16, groups, mixed, out_parts, out_ring.unit_rows)
+    arrived = swap(sent)
+    mine = outward(False, f32, groups, mixed, out_parts, out_ring.unit_rows)
+    outgoing = bundle(groups, send, kv, tags)
+    mine = expert_ring.pin(mine)
+    expert_ring.step()
+    mine, arrived = expert_ring.pin(mine, arrived)
     expert_ring.step()
     expert_ring.share()
-    out_parts = out_ring.parts()
-    sent = outward(True, bf16, groups, mixed, out_parts, out_unit)
-    arrived = swap(sent)
-    mixed, send = lax.optimization_barrier((mixed, send, sent))[:2]
-    mine = outward(False, f32, groups, mixed, out_parts, out_unit)
-
-    outgoing = jnp.dot(
-        send, jnp.concatenate([kv, tags], axis=1), preferred_element_type=f32
-    ).astype(bf16)
-    outgoing = expert_ring.pin(outgoing)
-    expert_ring.step()
-    expert_ring.share()
-    arrived_cache = lax.all_to_all(
-        outgoing.reshape(groups, capc, kv_width + 128), "grp", split_axis=0, concat_axis=0, tiled=True
-    ).reshape(groups * capc, kv_width + 128)
-    numbers = arrived_cache[:, kv_width : kv_width + 2].astype(jnp.int32)
-    write_rows = numbers[:, 0] * 64 + numbers[:, 1] - 64
-    write_hit = write_rows[None, :] == jnp.arange(slots_dev, dtype=jnp.int32)[:, None]
-    written = jnp.dot(
-        write_hit.astype(bf16), arrived_cache[:, :kv_width], preferred_element_type=f32
-    ).astype(bf16)
-    cache_after = jnp.where(
-        jnp.any(write_hit, axis=1)[:, None, None], written.reshape(kv_cache.shape), kv_cache
-    )
 
     residual, gates, own_rows, sent_rows = route(
         tokens, mine, arrived, moe_gain[None], router.T, named, place
     )
     landed = swap(sent_rows)
+    outgoing = lax.optimization_barrier((outgoing, sent_rows))[0]
+    arrived_cache = lax.all_to_all(outgoing, "grp", split_axis=0, concat_axis=0, tiled=True)
     own_made, back = expert(
-        groups, own_rows, landed, expert_ring.parts(), expert_unit, up.shape[0], down.shape[0]
+        groups, own_rows, landed, expert_ring.parts(), up.shape[0], down.shape[0]
     )
     returned = swap(back)
     layer_out = combine(residual, gates, spread, own_made, returned)
+    cache_after = write(arrived_cache, kv_cache)
     return (layer_out, cache_after)
 
 

time: 118 us -> 105 us (0.89)
  the two profiles are of different devices: /device:TPU:14 before, /device:TPU:12 now
where the time goes in v2:
time: 105 us
  waiting for transfers between devices  57.5 us (55%)
  starting transfers between devices  22.9 us (22%)
  Pallas kernels  16.3 us (16%)
  local copies, waits for them, and re-layouts  6.98 us (7%)
    ppermute x8, waiting for transfers between devices, step(): self.mine.append(self.across(held))  31.3 us
    ppermute x1, waiting for transfers between devices, two_lane_shards(): arrived = swap(sent)  8.34 us
    all_to_all x1, starting transfers between devices, two_lane_shards(): lax.all_to_all(outgoing, 'grp', split_axis=0, concat_axis=0, tiled=True)  7.29 us
    unnamed x37, local copies, waits for them, and re-layouts  6.94 us
    ppermute x1, waiting for transfers between devices, two_lane_shards(): other_tokens = swap(tokens)  6.48 us
    ppermute x1, waiting for transfers between devices, two_lane_shards(): seam = lax.ppermute(tail, 'grp', [(g, g + 1) for g in range(groups - 1)])  4.36 us
    ppermute x1, waiting for transfers between devices, two_lane_shards(): landed = swap(sent_rows)  3.71 us
    ppermute x8, starting transfers between devices, step(): self.mine.append(self.across(held))  3.54 us
  transfers between devices with their start and end apart: 25, of which 9 were waited for; matrix products, arithmetic and copies ran while one was open for 2% of the time, Pallas kernels for 12%

profile of v2, /device:TPU:12, one launch (start us, length us, event | category | flops | bytes accessed | tf_op | source)
XLA Modules:
  0.0 104.5 jit_solution(15172219840948972235)
XLA Ops:
  1.3 1.5 %collective-permute-start.5 = (bf16[128,1536]{1,0:T(8,128)(2,1)}, bf16[128,1536]{1,0:T(8,128)(2,1)S(1)}, u32[]{:S(2)}, u32[]{:S(2)}) collective-permute-start(bf16[128,1536]{1,0:T(8,128)(2,1)} %tokens.1), channel_id=1, source_target_pairs={{0,1},{1,0},{2,3},{3,2},{4,5},{5,4},{6,7},{7,6},{8,9},{9,8},{10,11... | collective-permute-start | bytes 1179656 | tf_op jit(solution)/shard_map/ppermute | solution.py:567
  2.9 1.0 copy-done.5
  3.9 0.9 copy-done.6
  4.8 0.9 copy-done.8
  6.5 6.5 %collective-permute-done.5.other = bf16[128,1536]{1,0:T(8,128)(2,1)S(1)} collective-permute-done((bf16[128,1536]{1,0:T(8,128)(2,1)}, bf16[128,1536]{1,0:T(8,128)(2,1)S(1)}, u32[]{:S(2)}, u32[]{:S(2)}) %collective-permute-start.5) | collective-permute-done | bytes 393248 | tf_op jit(solution)/shard_map/ppermute | solution.py:567
  13.7 6.0 %collective-permute-done.6.refs_2_ = bf16[192,768]{1,0:T(8,128)(2,1)S(1)} collective-permute-done((bf16[192,768]{1,0:T(8,128)(2,1)S(1)}, bf16[192,768]{1,0:T(8,128)(2,1)S(1)}, u32[]{:S(2)}, u32[]{:S(2)}) %collective-permute-start.6) | collective-permute-done | bytes 294944 | tf_op jit(solution)/shard_map/ppermute | solution.py:70
  20.2 1.8 %copy.17 = bf16[192,8,4,128]{3,1,2,0:T(8,128)(2,1)S(1)} copy(bf16[192,8,4,128]{3,2,1,0:T(4,128)(2,1)} %bitcast.22) | data formatting | bytes 3145728
  22.8 2.2 %project.1 = (bf16[256,768]{1,0:T(8,128)(2,1)S(1)}, bf16[256,512]{1,0:T(8,128)(2,1)S(1)}, bf16[128,512]{1,0:T(8,128)(2,1)S(1)}) custom-call(bf16[128,1536]{1,0:T(8,128)(2,1)S(1)} %copy-done.1, bf16[128,1536]{1,0:T(8,128)(2,1)S(1)} %collective-permute-done.5.other, f32[1,1536]{1,0:T(1,128)S(1)} %broadcast_in_dim.12.gain, ...), custom_call_target="tpu_custom_call" | custom-call | flops 1006632960 | bytes 3932160 | tf_op jit(solution)/shard_map/project/pallas_call | solution.py:281
  25.0 1.9 %collective-permute-start.8 = (bf16[128,512]{1,0:T(8,128)(2,1)S(1)}, bf16[128,512]{1,0:T(8,128)(2,1)S(1)}, u32[]{:S(2)}, u32[]{:S(2)}) collective-permute-start(bf16[128,512]{1,0:T(8,128)(2,1)S(1)} %get-tuple-element.43), channel_id=1, source_target_pairs={{0,2},{2,4},{4,6},{6,8},{8,10},{10,12},{12,14},{14,16},{16,18},{18... | collective-permute-start | bytes 393224 | tf_op jit(solution)/shard_map/ppermute | solution.py:593
  27.0 4.4 %collective-permute-done.8.seam = bf16[128,512]{1,0:T(8,128)(2,1)S(1)} collective-permute-done((bf16[128,512]{1,0:T(8,128)(2,1)S(1)}, bf16[128,512]{1,0:T(8,128)(2,1)S(1)}, u32[]{:S(2)}, u32[]{:S(2)}) %collective-permute-start.8) | collective-permute-done | bytes 131104 | tf_op jit(solution)/shard_map/ppermute | solution.py:593
  31.6 1.3 %collective-permute-start.10 = (bf16[192,768]{1,0:T(8,128)(2,1)S(1)}, bf16[192,768]{1,0:T(8,128)(2,1)S(1)}, u32[]{:S(2)}, u32[]{:S(2)}) collective-permute-start(bf16[192,768]{1,0:T(8,128)(2,1)S(1)} %collective-permute-done.4.refs_1_), channel_id=1, source_target_pairs={{0,2},{2,0},{4,6},{6,4},{8,10},{10,8},{12,14},{14,12},{16,18},{18,... | collective-permute-start | bytes 884744 | tf_op jit(solution)/shard_map/ppermute | solution.py:79
  34.0 8.8 %collective-permute-done.13.refs_7_ = bf16[96,768]{1,0:T(8,128)(2,1)S(1)} collective-permute-done((bf16[96,768]{1,0:T(8,128)(2,1)S(1)}, bf16[96,768]{1,0:T(8,128)(2,1)S(1)}, u32[]{:S(2)}, u32[]{:S(2)}) %collective-permute-start.13) | collective-permute-done | bytes 147488 | tf_op jit(solution)/shard_map/ppermute | solution.py:70
  42.8 2.9 %attend.1.mixed = bf16[256,768]{1,0:T(8,128)(2,1)S(1)} custom-call(bf16[256,768]{1,0:T(8,128)(2,1)S(1)} %get-tuple-element.46.q, bf16[256,512]{1,0:T(8,128)(2,1)S(1)} %get-tuple-element.47.kv, bf16[128,512]{1,0:T(8,128)(2,1)S(1)} %collective-permute-done.8.seam, f32[256,128]{1,0:T(8,128)S(1)} %get-tuple-element.49.past), custom_call_target="tpu_custom_call" | custom-call | flops 100663296 | bytes 1048576 | tf_op jit(solution)/shard_map/attend/pallas_call | solution.py:334
  45.7 1.1 %outward_keep.1.mine = f32[128,1536]{1,0:T(8,128)S(1)} custom-call(bf16[256,768]{1,0:T(8,128)(2,1)S(1)} %attend.1.mixed, bf16[192,768]{1,0:T(8,128)(2,1)S(1)} %get-tuple-element.36.refs_0_, bf16[192,768]{1,0:T(8,128)(2,1)S(1)} %collective-permute-done.4.refs_1_, bf16[192,768]{1,0:T(8,128)(2,1)S(1)} %collective-permute-done.6.refs_2_, ...), custom_call_target="tpu_custom_call" | custom-call | flops 301989888 | bytes 2359296 | tf_op jit(solution)/shard_map/outward_keep/pallas_call | solution.py:364
  47.2 1.1 %outward_send.1 = bf16[128,1536]{1,0:T(8,128)(2,1)S(1)} custom-call(bf16[256,768]{1,0:T(8,128)(2,1)S(1)} %attend.1.mixed, bf16[192,768]{1,0:T(8,128)(2,1)S(1)} %get-tuple-element.36.refs_0_, bf16[192,768]{1,0:T(8,128)(2,1)S(1)} %collective-permute-done.4.refs_1_, bf16[192,768]{1,0:T(8,128)(2,1)S(1)} %collective-permute-done.6.refs_2_, ...), custom_call_target="tpu_custom_call" | custom-call | flops 301989888 | bytes 2359296 | tf_op jit(solution)/shard_map/outward_send/pallas_call | solution.py:364
  48.3 1.8 %collective-permute-start.16 = (bf16[128,1536]{1,0:T(8,128)(2,1)S(1)}, bf16[128,1536]{1,0:T(8,128)(2,1)S(1)}, u32[]{:S(2)}, u32[]{:S(2)}) collective-permute-start(bf16[128,1536]{1,0:T(8,128)(2,1)S(1)} %outward_send.1), channel_id=1, source_target_pairs={{0,1},{1,0},{2,3},{3,2},{4,5},{5,4},{6,7},{7,6},{8,9},{9,8},{10,11... | collective-permute-start | bytes 1179656 | tf_op jit(solution)/shard_map/ppermute | solution.py:602
  50.2 1.4 %bundle.1 = bf16[16,144,128]{2,1,0:T(8,128)(2,1)} custom-call(bf16[512,256]{1,0:T(8,128)(2,1)S(1)} %get-tuple-element.65.send, bf16[256,512]{1,0:T(8,128)(2,1)S(1)} %get-tuple-element.47.kv, bf16[256,128]{1,0:T(8,128)(2,1)S(1)} %get-tuple-element.66.tags), custom_call_target="tpu_custom_call" | custom-call | bytes 1048576 | tf_op jit(solution)/shard_map/bundle/pallas_call | solution.py:496
  51.5 8.3 %collective-permute-done.16.arrived = bf16[128,1536]{1,0:T(8,128)(2,1)S(1)} collective-permute-done((bf16[128,1536]{1,0:T(8,128)(2,1)S(1)}, bf16[128,1536]{1,0:T(8,128)(2,1)S(1)}, u32[]{:S(2)}, u32[]{:S(2)}) %collective-permute-start.16) | collective-permute-done | bytes 393248 | tf_op jit(solution)/shard_map/ppermute | solution.py:602
  59.9 0.9 route.1
  60.8 0.7 copy-done.3
  62.1 7.3 %all-to-all-start = ((bf16[16,144,128]{2,1,0:T(8,128)(2,1)}), bf16[16,144,128]{2,1,0:T(8,128)(2,1)S(1)}, u32[]{:S(2)}, u32[]{:S(2)}) async-start(bf16[16,144,128]{2,1,0:T(8,128)(2,1)} %bundle.1), calls=%async_computation | async-start | bytes 1179648 | tf_op jit(solution)/shard_map/all_to_all | solution.py:616
  70.0 0.8 collective-permute-start.21
  70.8 0.8 collective-permute-start.20
  71.5 16.5 %collective-permute-done.21.refs_7_ = bf16[288,512]{1,0:T(8,128)(2,1)S(1)} collective-permute-done((bf16[288,512]{1,0:T(8,128)(2,1)S(1)}, bf16[288,512]{1,0:T(8,128)(2,1)S(1)}, u32[]{:S(2)}, u32[]{:S(2)}) %collective-permute-start.21) | collective-permute-done | bytes 294944 | tf_op jit(solution)/shard_map/ppermute | solution.py:70
  88.0 1.5 %collective-permute-start.17 = (bf16[32,1536]{1,0:T(8,128)(2,1)S(1)}, bf16[32,1536]{1,0:T(8,128)(2,1)S(1)}, u32[]{:S(2)}, u32[]{:S(2)}) collective-permute-start(bf16[32,1536]{1,0:T(8,128)(2,1)S(1)} %get-tuple-element.61), channel_id=1, source_target_pairs={{0,1},{1,0},{2,3},{3,2},{4,5},{5,4},{6,7},{7,6},{8,9},{9,8},{10,11... | collective-permute-start | bytes 294920 | tf_op jit(solution)/shard_map/ppermute | solution.py:614
  89.5 3.7 %collective-permute-done.17.other = bf16[32,1536]{1,0:T(8,128)(2,1)S(1)} collective-permute-done((bf16[32,1536]{1,0:T(8,128)(2,1)S(1)}, bf16[32,1536]{1,0:T(8,128)(2,1)S(1)}, u32[]{:S(2)}, u32[]{:S(2)}) %collective-permute-start.17) | collective-permute-done | bytes 98336 | tf_op jit(solution)/shard_map/ppermute | solution.py:614
  93.2 0.9 copy-done.10
  94.1 1.3 %expert.1 = (bf16[32,1536]{1,0:T(8,128)(2,1)S(1)}, bf16[32,1536]{1,0:T(8,128)(2,1)S(1)}) custom-call(bf16[32,1536]{1,0:T(8,128)(2,1)S(1)} %copy-done.10, bf16[32,1536]{1,0:T(8,128)(2,1)S(1)} %collective-permute-done.17.other, bf16[576,512]{1,0:T(8,128)(2,1)S(1)} %get-tuple-element.35.refs_0_, bf16[576,512]{1,0:T(8,128)(2,1)S(1)} %collective-permute-done.3.refs_1_, ...), custom_call_target="tpu_custom_call" | custom-call | flops 301989888 | bytes 4194304 | tf_op jit(solution)/shard_map/expert/pallas_call | solution.py:434
  95.4 1.6 %collective-permute-start.23 = (bf16[32,1536]{1,0:T(8,128)(2,1)S(1)}, bf16[32,1536]{1,0:T(8,128)(2,1)S(1)}, u32[]{:S(2)}, u32[]{:S(2)}) collective-permute-start(bf16[32,1536]{1,0:T(8,128)(2,1)S(1)} %get-tuple-element.64), channel_id=1, source_target_pairs={{0,1},{1,0},{2,3},{3,2},{4,5},{5,4},{6,7},{7,6},{8,9},{9,8},{10,11... | collective-permute-start | bytes 294920 | tf_op jit(solution)/shard_map/ppermute | solution.py:620
  97.0 3.1 %collective-permute-done.23.returned = bf16[32,1536]{1,0:T(8,128)(2,1)S(1)} collective-permute-done((bf16[32,1536]{1,0:T(8,128)(2,1)S(1)}, bf16[32,1536]{1,0:T(8,128)(2,1)S(1)}, u32[]{:S(2)}, u32[]{:S(2)}) %collective-permute-start.23) | collective-permute-done | bytes 98336 | tf_op jit(solution)/shard_map/ppermute | solution.py:620
  100.1 1.1 %combine.1 = bf16[128,1536]{1,0:T(8,128)(2,1)} custom-call(bf16[128,1536]{1,0:T(8,128)(2,1)S(1)} %copy-done.4, f32[128,40]{1,0:T(8,128)S(1)} %get-tuple-element.58.gates, bf16[128,64]{1,0:T(8,128)(2,1)S(1)} %copy-done.12, bf16[32,1536]{1,0:T(8,128)(2,1)S(1)} %get-tuple-element.63.own, bf16[32,1536]{1,0:T(8,128)(2,1)S(1)} %collective-permute-done.23.returned), custom_call_target="tpu_custom_call" | custom-call | bytes 1048576 | tf_op jit(solution)/shard_map/combine/pallas_call | solution.py:466
  101.3 3.3 %write.1 = bf16[512,4,128]{2,1,0:T(4,128)(2,1)} custom-call(bf16[16,144,128]{2,1,0:T(8,128)(2,1)S(1)} %all-to-all-done.arrived, bf16[512,4,128]{2,1,0:T(4,128)(2,1)S(1)} %copy-done.2), custom_call_target="tpu_custom_call" | custom-call | bytes 1048576 | tf_op jit(solution)/shard_map/write/pallas_call | solution.py:532
  (70 shorter events, 6.3 us)
Async XLA Ops:
  0.6 2.3 %collective-permute-start.2 = (bf16[96,1536]{1,0:T(8,128)(2,1)}, bf16[96,1536]{1,0:T(8,128)(2,1)S(1)}, u32[]{:S(2)}, u32[]{:S(2)}) collective-permute-start(bf16[96,1536]{1,0:T(8,128)(2,1)} %bitcast.12), channel_id=1, source_target_pairs={{0,2},{2,0},{4,6},{6,4},{8,10},{10,8},{12,14},{14,12},{16,18},{18,... | collective-permute-start | bytes 884744 | tf_op jit(solution)/shard_map/ppermute | solution.py:571
  0.7 2.2 %collective-permute-start = (bf16[96,1024]{1,0:T(8,128)(2,1)}, bf16[96,1024]{1,0:T(8,128)(2,1)S(1)}, u32[]{:S(2)}, u32[]{:S(2)}) collective-permute-start(bf16[96,1024]{1,0:T(8,128)(2,1)} %bitcast.14), channel_id=1, source_target_pairs={{0,2},{2,0},{4,6},{6,4},{8,10},{10,8},{12,14},{14,12},{16,18},{18,... | collective-permute-start | bytes 589832 | tf_op jit(solution)/shard_map/ppermute | solution.py:571
  1.2 1.7 %collective-permute-start.1 = (bf16[32,1536]{1,0:T(8,128)(2,1)}, bf16[32,1536]{1,0:T(8,128)(2,1)S(1)}, u32[]{:S(2)}, u32[]{:S(2)}) collective-permute-start(bf16[32,1536]{1,0:T(8,128)(2,1)} %bitcast.17), channel_id=1, source_target_pairs={{0,2},{2,0},{4,6},{6,4},{8,10},{10,8},{12,14},{14,12},{16,18},{18,... | collective-permute-start | bytes 294920 | tf_op jit(solution)/shard_map/ppermute | solution.py:571
  1.3 11.7 %collective-permute-start.5 = (bf16[128,1536]{1,0:T(8,128)(2,1)}, bf16[128,1536]{1,0:T(8,128)(2,1)S(1)}, u32[]{:S(2)}, u32[]{:S(2)}) collective-permute-start(bf16[128,1536]{1,0:T(8,128)(2,1)} %tokens.1), channel_id=1, source_target_pairs={{0,1},{1,0},{2,3},{3,2},{4,5},{5,4},{6,7},{7,6},{8,9},{9,8},{10,11... | collective-permute-start | bytes 1179656 | tf_op jit(solution)/shard_map/ppermute | solution.py:567
  6.0 7.0 %collective-permute-start.4 = (bf16[192,768]{1,0:T(8,128)(2,1)S(1)}, bf16[192,768]{1,0:T(8,128)(2,1)S(1)}, u32[]{:S(2)}, u32[]{:S(2)}) collective-permute-start(bf16[192,768]{1,0:T(8,128)(2,1)S(1)} %get-tuple-element.36.refs_0_), channel_id=1, source_target_pairs={{0,8},{2,6},{8,16},{10,2},{16,24},{18,10},{24,28},{26,18},{28,20},... | collective-permute-start | bytes 884744 | tf_op jit(solution)/shard_map/ppermute | solution.py:70
  13.0 6.7 %collective-permute-start.6 = (bf16[192,768]{1,0:T(8,128)(2,1)S(1)}, bf16[192,768]{1,0:T(8,128)(2,1)S(1)}, u32[]{:S(2)}, u32[]{:S(2)}) collective-permute-start(bf16[192,768]{1,0:T(8,128)(2,1)S(1)} %collective-permute-done.4.refs_1_), channel_id=1, source_target_pairs={{0,8},{2,6},{8,16},{10,2},{16,24},{18,10},{24,28},{26,18},{28,20},... | collective-permute-start | bytes 884744 | tf_op jit(solution)/shard_map/ppermute | solution.py:70
  13.4 17.9 %collective-permute-start.3 = (bf16[576,512]{1,0:T(8,128)(2,1)S(1)}, bf16[576,512]{1,0:T(8,128)(2,1)S(1)}, u32[]{:S(2)}, u32[]{:S(2)}) collective-permute-start(bf16[576,512]{1,0:T(8,128)(2,1)S(1)} %get-tuple-element.35.refs_0_), channel_id=1, source_target_pairs={{0,8},{2,6},{8,16},{10,2},{16,24},{18,10},{24,28},{26,18},{28,20},... | collective-permute-start | bytes 1769480 | tf_op jit(solution)/shard_map/ppermute | solution.py:70
  19.7 11.6 %collective-permute-start.7 = (bf16[192,768]{1,0:T(8,128)(2,1)S(1)}, bf16[192,768]{1,0:T(8,128)(2,1)S(1)}, u32[]{:S(2)}, u32[]{:S(2)}) collective-permute-start(bf16[192,768]{1,0:T(8,128)(2,1)S(1)} %collective-permute-done.6.refs_2_), channel_id=1, source_target_pairs={{0,8},{2,6},{8,16},{10,2},{16,24},{18,10},{24,28},{26,18},{28,20},... | collective-permute-start | bytes 884744 | tf_op jit(solution)/shard_map/ppermute | solution.py:70
  20.2 2.6 %copy-start = (bf16[1536,768]{1,0:T(8,128)(2,1)S(1)}, bf16[1536,768]{1,0:T(8,128)(2,1)}, u32[]{:S(2)}) copy-start(bf16[1536,768]{1,0:T(8,128)(2,1)} %w_query.1) | copy-start | bytes 7077892
  20.2 2.6 %copy-start.1 = (bf16[128,1536]{1,0:T(8,128)(2,1)S(1)}, bf16[128,1536]{1,0:T(8,128)(2,1)}, u32[]{:S(2)}) copy-start(bf16[128,1536]{1,0:T(8,128)(2,1)} %tokens.1) | copy-start | bytes 1179652
  25.0 6.3 %collective-permute-start.8 = (bf16[128,512]{1,0:T(8,128)(2,1)S(1)}, bf16[128,512]{1,0:T(8,128)(2,1)S(1)}, u32[]{:S(2)}, u32[]{:S(2)}) collective-permute-start(bf16[128,512]{1,0:T(8,128)(2,1)S(1)} %get-tuple-element.43), channel_id=1, source_target_pairs={{0,2},{2,4},{4,6},{6,8},{8,10},{10,12},{12,14},{14,16},{16,18},{18... | collective-permute-start | bytes 393224 | tf_op jit(solution)/shard_map/ppermute | solution.py:593
  31.3 15.5 %collective-permute-start.9 = (bf16[576,512]{1,0:T(8,128)(2,1)S(1)}, bf16[576,512]{1,0:T(8,128)(2,1)S(1)}, u32[]{:S(2)}, u32[]{:S(2)}) collective-permute-start(bf16[576,512]{1,0:T(8,128)(2,1)S(1)} %collective-permute-done.3.refs_1_), channel_id=1, source_target_pairs={{0,8},{2,6},{8,16},{10,2},{16,24},{18,10},{24,28},{26,18},{28,20},... | collective-permute-start | bytes 1769480 | tf_op jit(solution)/shard_map/ppermute | solution.py:70
  31.6 14.1 %collective-permute-start.10 = (bf16[192,768]{1,0:T(8,128)(2,1)S(1)}, bf16[192,768]{1,0:T(8,128)(2,1)S(1)}, u32[]{:S(2)}, u32[]{:S(2)}) collective-permute-start(bf16[192,768]{1,0:T(8,128)(2,1)S(1)} %collective-permute-done.4.refs_1_), channel_id=1, source_target_pairs={{0,2},{2,0},{4,6},{6,4},{8,10},{10,8},{12,14},{14,12},{16,18},{18,... | collective-permute-start | bytes 884744 | tf_op jit(solution)/shard_map/ppermute | solution.py:79
  32.9 9.9 %collective-permute-start.13 = (bf16[96,768]{1,0:T(8,128)(2,1)S(1)}, bf16[96,768]{1,0:T(8,128)(2,1)S(1)}, u32[]{:S(2)}, u32[]{:S(2)}) collective-permute-start(bf16[96,768]{1,0:T(8,128)(2,1)S(1)} %slice.6), channel_id=1, source_target_pairs={{0,8},{2,6},{8,16},{10,2},{16,24},{18,10},{24,28},{26,18},{28,20},... | collective-permute-start | bytes 442376 | tf_op jit(solution)/shard_map/ppermute | solution.py:70
  33.5 12.2 %collective-permute-start.11 = (bf16[192,768]{1,0:T(8,128)(2,1)S(1)}, bf16[192,768]{1,0:T(8,128)(2,1)S(1)}, u32[]{:S(2)}, u32[]{:S(2)}) collective-permute-start(bf16[192,768]{1,0:T(8,128)(2,1)S(1)} %collective-permute-done.6.refs_2_), channel_id=1, source_target_pairs={{0,2},{2,0},{4,6},{6,4},{8,10},{10,8},{12,14},{14,12},{16,18},{18,... | collective-permute-start | bytes 884744 | tf_op jit(solution)/shard_map/ppermute | solution.py:79
  33.7 12.0 %collective-permute-start.12 = (bf16[192,768]{1,0:T(8,128)(2,1)S(1)}, bf16[192,768]{1,0:T(8,128)(2,1)S(1)}, u32[]{:S(2)}, u32[]{:S(2)}) collective-permute-start(bf16[192,768]{1,0:T(8,128)(2,1)S(1)} %collective-permute-done.7.refs_3_), channel_id=1, source_target_pairs={{0,2},{2,0},{4,6},{6,4},{8,10},{10,8},{12,14},{14,12},{16,18},{18,... | collective-permute-start | bytes 884744 | tf_op jit(solution)/shard_map/ppermute | solution.py:79
  42.8 2.9 %collective-permute-start.14 = (bf16[96,768]{1,0:T(8,128)(2,1)S(1)}, bf16[96,768]{1,0:T(8,128)(2,1)S(1)}, u32[]{:S(2)}, u32[]{:S(2)}) collective-permute-start(bf16[96,768]{1,0:T(8,128)(2,1)S(1)} %collective-permute-done.13.refs_7_), channel_id=1, source_target_pairs={{0,2},{2,0},{4,6},{6,4},{8,10},{10,8},{12,14},{14,12},{16,18},{18,... | collective-permute-start | bytes 442376 | tf_op jit(solution)/shard_map/ppermute | solution.py:79
  46.9 3.3 %copy-start.17 = (f32[1536]{0:T(1024)S(1)}, f32[1536]{0:T(1024)}, u32[]{:S(2)}) copy-start(f32[1536]{0:T(1024)} %param.19) | copy-start | bytes 18436
  46.9 13.0 %copy-start.7 = (bf16[1536,40]{0,1:T(8,128)(2,1)S(1)}, bf16[1536,40]{0,1:T(8,128)(2,1)}, u32[]{:S(2)}) copy-start(bf16[1536,40]{0,1:T(8,128)(2,1)} %param.20) | copy-start | bytes 368644
  46.9 13.0 %collective-permute-start.15 = (bf16[576,512]{1,0:T(8,128)(2,1)S(1)}, bf16[576,512]{1,0:T(8,128)(2,1)S(1)}, u32[]{:S(2)}, u32[]{:S(2)}) collective-permute-start(bf16[576,512]{1,0:T(8,128)(2,1)S(1)} %collective-permute-done.9.refs_2_), channel_id=1, source_target_pairs={{0,8},{2,6},{8,16},{10,2},{16,24},{18,10},{24,28},{26,18},{28,20},... | collective-permute-start | bytes 1769480 | tf_op jit(solution)/shard_map/ppermute | solution.py:70
  48.3 11.5 %collective-permute-start.16 = (bf16[128,1536]{1,0:T(8,128)(2,1)S(1)}, bf16[128,1536]{1,0:T(8,128)(2,1)S(1)}, u32[]{:S(2)}, u32[]{:S(2)}) collective-permute-start(bf16[128,1536]{1,0:T(8,128)(2,1)S(1)} %outward_send.1), channel_id=1, source_target_pairs={{0,1},{1,0},{2,3},{3,2},{4,5},{5,4},{6,7},{7,6},{8,9},{9,8},{10,11... | collective-permute-start | bytes 1179656 | tf_op jit(solution)/shard_map/ppermute | solution.py:602
  62.1 39.1 %all-to-all-start = ((bf16[16,144,128]{2,1,0:T(8,128)(2,1)}), bf16[16,144,128]{2,1,0:T(8,128)(2,1)S(1)}, u32[]{:S(2)}, u32[]{:S(2)}) async-start(bf16[16,144,128]{2,1,0:T(8,128)(2,1)} %bundle.1), calls=%async_computation | async-start | bytes 1179648 | tf_op jit(solution)/shard_map/all_to_all | solution.py:616
  69.4 20.1 %collective-permute-start.18 = (bf16[576,512]{1,0:T(8,128)(2,1)S(1)}, bf16[576,512]{1,0:T(8,128)(2,1)S(1)}, u32[]{:S(2)}, u32[]{:S(2)}) collective-permute-start(bf16[576,512]{1,0:T(8,128)(2,1)S(1)} %collective-permute-done.3.refs_1_), channel_id=1, source_target_pairs={{0,2},{2,0},{4,6},{6,4},{8,10},{10,8},{12,14},{14,12},{16,18},{18,... | collective-permute-start | bytes 1769480 | tf_op jit(solution)/shard_map/ppermute | solution.py:79
  69.6 19.9 %collective-permute-start.19 = (bf16[576,512]{1,0:T(8,128)(2,1)S(1)}, bf16[576,512]{1,0:T(8,128)(2,1)S(1)}, u32[]{:S(2)}, u32[]{:S(2)}) collective-permute-start(bf16[576,512]{1,0:T(8,128)(2,1)S(1)} %collective-permute-done.9.refs_2_), channel_id=1, source_target_pairs={{0,2},{2,0},{4,6},{6,4},{8,10},{10,8},{12,14},{14,12},{16,18},{18,... | collective-permute-start | bytes 1769480 | tf_op jit(solution)/shard_map/ppermute | solution.py:79
  70.0 18.0 %collective-permute-start.21 = (bf16[288,512]{1,0:T(8,128)(2,1)S(1)}, bf16[288,512]{1,0:T(8,128)(2,1)S(1)}, u32[]{:S(2)}, u32[]{:S(2)}) collective-permute-start(bf16[288,512]{1,0:T(8,128)(2,1)S(1)} %slice.7), channel_id=1, source_target_pairs={{0,8},{2,6},{8,16},{10,2},{16,24},{18,10},{24,28},{26,18},{28,20},... | collective-permute-start | bytes 884744 | tf_op jit(solution)/shard_map/ppermute | solution.py:70
  70.8 22.4 %collective-permute-start.20 = (bf16[576,512]{1,0:T(8,128)(2,1)S(1)}, bf16[576,512]{1,0:T(8,128)(2,1)S(1)}, u32[]{:S(2)}, u32[]{:S(2)}) collective-permute-start(bf16[576,512]{1,0:T(8,128)(2,1)S(1)} %collective-permute-done.15.refs_3_), channel_id=1, source_target_pairs={{0,2},{2,0},{4,6},{6,4},{8,10},{10,8},{12,14},{14,12},{16,18},{18,... | collective-permute-start | bytes 1769480 | tf_op jit(solution)/shard_map/ppermute | solution.py:79
  88.0 5.2 %collective-permute-start.22 = (bf16[288,512]{1,0:T(8,128)(2,1)S(1)}, bf16[288,512]{1,0:T(8,128)(2,1)S(1)}, u32[]{:S(2)}, u32[]{:S(2)}) collective-permute-start(bf16[288,512]{1,0:T(8,128)(2,1)S(1)} %collective-permute-done.21.refs_7_), channel_id=1, source_target_pairs={{0,2},{2,0},{4,6},{6,4},{8,10},{10,8},{12,14},{14,12},{16,18},{18,... | collective-permute-start | bytes 884744 | tf_op jit(solution)/shard_map/ppermute | solution.py:79
  88.0 5.2 %collective-permute-start.17 = (bf16[32,1536]{1,0:T(8,128)(2,1)S(1)}, bf16[32,1536]{1,0:T(8,128)(2,1)S(1)}, u32[]{:S(2)}, u32[]{:S(2)}) collective-permute-start(bf16[32,1536]{1,0:T(8,128)(2,1)S(1)} %get-tuple-element.61), channel_id=1, source_target_pairs={{0,1},{1,0},{2,3},{3,2},{4,5},{5,4},{6,7},{7,6},{8,9},{9,8},{10,11... | collective-permute-start | bytes 294920 | tf_op jit(solution)/shard_map/ppermute | solution.py:614
  94.1 6.0 %copy-start.4 = (bf16[128,1536]{1,0:T(8,128)(2,1)S(1)}, bf16[128,1536]{1,0:T(8,128)(2,1)}, u32[]{:S(2)}) copy-start(bf16[128,1536]{1,0:T(8,128)(2,1)} %copy-done.3) | copy-start | bytes 1179652
  94.1 6.0 %copy-start.12 = (bf16[128,64]{1,0:T(8,128)(2,1)S(1)}, bf16[128,64]{1,0:T(8,128)(2,1)}, u32[]{:S(2)}) copy-start(bf16[128,64]{1,0:T(8,128)(2,1)} %copy-done.11) | copy-start | bytes 49156
  94.1 7.2 %copy-start.2 = (bf16[512,4,128]{2,1,0:T(4,128)(2,1)S(1)}, bf16[512,4,128]{2,1,0:T(4,128)(2,1)}, u32[]{:S(2)}) copy-start(bf16[512,4,128]{2,1,0:T(4,128)(2,1)} %cache.1) | copy-start | bytes 1572868
  95.4 4.7 %collective-permute-start.23 = (bf16[32,1536]{1,0:T(8,128)(2,1)S(1)}, bf16[32,1536]{1,0:T(8,128)(2,1)S(1)}, u32[]{:S(2)}, u32[]{:S(2)}) collective-permute-start(bf16[32,1536]{1,0:T(8,128)(2,1)S(1)} %get-tuple-element.64), channel_id=1, source_target_pairs={{0,1},{1,0},{2,3},{3,2},{4,5},{5,4},{6,7},{7,6},{8,9},{9,8},{10,11... | collective-permute-start | bytes 294920 | tf_op jit(solution)/shard_map/ppermute | solution.py:620
  (11 other events, 14.9 us)

commit v3 on v2

--- a/solution.py
+++ b/solution.py
@@ -101,8 +101,7 @@
 PARAMS = pltpu.CompilerParams(vmem_limit_bytes=40 << 20)
 
 
-def cost(flops, nbytes):
-    return pl.CostEstimate(flops=flops, bytes_accessed=nbytes, transcendentals=0)
+LITTLE = pl.CostEstimate(flops=1, bytes_accessed=1, transcendentals=0)
 
 
 def normalized(floats, gain):
@@ -142,6 +141,7 @@
 
 
 def pack(own, beside):
+    own = [pltpu.with_memory_space_constraint(part, pltpu.HBM) for part in own]
     up, down, w_out_t = own
     width = up.shape[1] // 2
     pieces = [up.shape[1] // width, down.shape[1] // width]
@@ -156,7 +156,7 @@
         out_specs=(ANY, ANY),
         scratch_shapes=[pltpu.SemaphoreType.DMA((2 + 2 * sum(pieces),))],
         compiler_params=PARAMS,
-        cost_estimate=cost(0, 0),
+        cost_estimate=LITTLE,
         name="pack",
     )(*own, *beside)
 
@@ -241,7 +241,7 @@
         in_specs=[VMEM] * 3,
         out_specs=(VMEM,) * len(shapes),
         compiler_params=PARAMS,
-        cost_estimate=cost(0, 1 << 20),
+        cost_estimate=LITTLE,
         name="prepare",
     )(positions[None], slots[None], ids.T)
 
@@ -293,7 +293,7 @@
             pltpu.SemaphoreType.DMA((2,)),
         ],
         compiler_params=PARAMS,
-        cost_estimate=cost(4 * count * width * made, 2 * width * made),
+        cost_estimate=LITTLE,
         name="project",
     )(own, other, gain, cosine, sine, w_query, flat_kv)
 
@@ -341,7 +341,7 @@
             pltpu.SemaphoreType.DMA,
         ],
         compiler_params=PARAMS,
-        cost_estimate=cost(8 * count * count * q.shape[1], 1 << 20),
+        cost_estimate=LITTLE,
         name="attend",
     )(q, kv, seam, past)
 
@@ -368,43 +368,59 @@
         out_specs=VMEM,
         scratch_shapes=[pltpu.VMEM((width, depth), bf16)],
         compiler_params=PARAMS,
-        cost_estimate=cost(2 * count * width * depth, 2 * width * depth),
+        cost_estimate=LITTLE,
         name="outward_send" if flip else "outward_keep",
     )(mixed, *parts)
 
 
-def route_kernel(tokens, mine, arrived, gain, router, named, place, residual, gates, own, sent, got, sems):
-    copies = fetch([(arrived, got)], sems)
-    copies[0].wait()
-    added = tokens[...].astype(f32) + (mine[...] + got[...].astype(f32))
-    residual[...] = added.astype(bf16)
-    moe_in = normalized(added.astype(bf16).astype(f32), gain[...])
-    rows = jnp.dot(place[...], moe_in, preferred_element_type=f32).astype(bf16)
-    cap = own.shape[0]
-    own[...] = rows[:cap, :]
-    sent[...] = rows[cap:, :]
-    logits = lax.dot_general(moe_in, router[...], LAST_DIMS, preferred_element_type=f32)
-    raised = jnp.where(named[...] > 0, jnp.exp(logits), 0.0)
-    gates[...] = raised / jnp.sum(raised, axis=-1, keepdims=True)
-
-
-def route(tokens, mine, arrived, gain, router_t, named, place):
+def route_kernel(tokens, mine, arrived, gain, place, residual, moe_in, sent):
+    added = (tokens[...].astype(f32) + (mine[...] + arrived[...].astype(f32))).astype(bf16)
+    residual[...] = added
+    moe_in[...] = normalized(added.astype(f32), gain[...])
+    cap = sent.shape[0]
+    rows = jnp.dot(place[cap:, :], moe_in[...], preferred_element_type=f32)
+    sent[...] = rows.astype(bf16)
+
+
+def route(tokens, mine, arrived, gain, place):
     cap = place.shape[0] // 2
     return pl.pallas_call(
         route_kernel,
         out_shape=(
             jax.ShapeDtypeStruct(tokens.shape, bf16),
-            jax.ShapeDtypeStruct(named.shape, f32),
-            jax.ShapeDtypeStruct((cap, tokens.shape[1]), bf16),
+            jax.ShapeDtypeStruct(tokens.shape, bf16),
             jax.ShapeDtypeStruct((cap, tokens.shape[1]), bf16),
         ),
-        in_specs=[VMEM, VMEM, ANY] + [VMEM] * 4,
-        out_specs=(VMEM,) * 4,
-        scratch_shapes=[pltpu.VMEM(tokens.shape, bf16), pltpu.SemaphoreType.DMA((1,))],
-        compiler_params=PARAMS,
-        cost_estimate=cost(0, 2 << 20),
+        in_specs=[VMEM] * 5,
+        out_specs=(VMEM,) * 3,
+        compiler_params=PARAMS,
+        cost_estimate=LITTLE,
         name="route",
-    )(tokens, mine, arrived, gain, router_t, named, place)
+    )(tokens, mine, arrived, gain, place)
+
+
+def gate_kernel(moe_in, router, named, place, gates, own):
+    cap = own.shape[0]
+    own[...] = jnp.dot(place[:cap, :], moe_in[...], preferred_element_type=f32).astype(bf16)
+    logits = lax.dot_general(moe_in[...], router[...], LAST_DIMS, preferred_element_type=f32)
+    raised = jnp.where(named[...] > 0, jnp.exp(logits), 0.0)
+    gates[...] = raised / jnp.sum(raised, axis=-1, keepdims=True)
+
+
+def gate(moe_in, router_t, named, place):
+    cap = place.shape[0] // 2
+    return pl.pallas_call(
+        gate_kernel,
+        out_shape=(
+            jax.ShapeDtypeStruct(named.shape, f32),
+            jax.ShapeDtypeStruct((cap, moe_in.shape[1]), bf16),
+        ),
+        in_specs=[VMEM] * 4,
+        out_specs=(VMEM,) * 2,
+        compiler_params=PARAMS,
+        cost_estimate=LITTLE,
+        name="gate",
+    )(moe_in, router_t, named, place)
 
 
 def expert_kernel(groups, up_rows, down_rows, n_parts, own, other, *refs):
@@ -442,7 +458,7 @@
             pltpu.VMEM((groups * down_rows, model), bf16),
         ],
         compiler_params=PARAMS,
-        cost_estimate=cost(4 * count * width * 9 * down_rows * groups, 4 << 20),
+        cost_estimate=LITTLE,
         name="expert",
     )(own, other, *parts)
 
@@ -469,7 +485,7 @@
         in_specs=[VMEM] * 5,
         out_specs=VMEM,
         compiler_params=PARAMS,
-        cost_estimate=cost(0, 1 << 20),
+        cost_estimate=LITTLE,
         name="combine",
     )(residual, gates, spread, own, returned)
 
@@ -499,7 +515,7 @@
         in_specs=[VMEM] * 3,
         out_specs=VMEM,
         compiler_params=PARAMS,
-        cost_estimate=cost(0, 1 << 20),
+        cost_estimate=LITTLE,
         name="bundle",
     )(send, kv, tags)
 
@@ -536,7 +552,7 @@
         out_specs=VMEM,
         scratch_shapes=[pltpu.VMEM((arrived.shape[0] * capc, heads * lanes), bf16)],
         compiler_params=PARAMS,
-        cost_estimate=cost(0, 1 << 20),
+        cost_estimate=LITTLE,
         name="write",
     )(arrived, cache)
 
@@ -564,62 +580,64 @@
     slots_dev = kv_cache.shape[0]
     swap = functools.partial(lax.ppermute, axis_name="hd", perm=[(0, 1), (1, 0)])
 
+    together = lax.optimization_barrier
+
     other_tokens = swap(tokens)
-    up, down = w_gate_up[0], w_down[0]
-    own = (up, down, w_out.T)
-    expert_pair, out_pair = pack(
-        own, [lax.ppermute(part, "grp", sibling_pairs(groups)) for part in own]
-    )
+    own = (w_gate_up[0], w_down[0], w_out.T)
+    up_rows, down_rows = own[0].shape[0], own[1].shape[0]
+    beside = [lax.ppermute(part, "grp", sibling_pairs(groups)) for part in own]
+    flat_kv = w_keyval.reshape(model, kv_width)
+    cosine, sine, past, named, place, spread, send, tags = prepare(
+        groups, slots_dev, positions, cache_slot, expert_ids, router.shape[1]
+    )
+    beside, cosine, flat_kv = together((beside, cosine, flat_kv))
+    expert_pair, out_pair = pack(own, beside)
     out_ring = Ring(out_pair, groups)
     out_ring.step()
     expert_ring = Ring(expert_pair, groups)
     expert_ring.step()
-    cosine, sine, past, named, place, spread, send, tags = prepare(
-        groups, slots_dev, positions, cache_slot, expert_ids, router.shape[1]
-    )
     other_tokens = out_ring.pin(other_tokens)
     out_ring.step()
-    other_tokens = out_ring.pin(other_tokens)
+
+    q, kv, tail = project(
+        tokens, other_tokens, attn_gain[None], cosine, sine, w_query, flat_kv
+    )
+    seam = lax.ppermute(tail, "grp", [(g, g + 1) for g in range(groups - 1)])
+    outgoing = bundle(groups, send, kv, tags)
+    outgoing = out_ring.pin(outgoing)
     out_ring.step()
-    q, kv, tail = project(
-        tokens,
-        other_tokens,
-        attn_gain[None],
-        cosine,
-        sine,
-        w_query,
-        w_keyval.reshape(model, kv_width),
-    )
-    seam = lax.ppermute(tail, "grp", [(g, g + 1) for g in range(groups - 1)])
+    seam, q = together((seam, q, outgoing))[:2]
+    seam = expert_ring.pin(seam)
+    expert_ring.step()
     seam = out_ring.pin(seam)
     out_ring.step()
+    mixed = attend(q, kv, seam, past)
+    mixed = out_ring.pin(mixed)
+    out_ring.mine[-1] = expert_ring.pin(out_ring.mine[-1])
     out_ring.share()
-    seam = expert_ring.pin(seam)
     expert_ring.step()
-    mixed = attend(q, kv, seam, past)
-    out_parts = out_ring.parts()
-    sent = outward(True, bf16, groups, mixed, out_parts, out_ring.unit_rows)
+    sent = outward(True, bf16, groups, mixed, out_ring.parts(), out_ring.unit_rows)
     arrived = swap(sent)
-    mine = outward(False, f32, groups, mixed, out_parts, out_ring.unit_rows)
-    outgoing = bundle(groups, send, kv, tags)
+    mixed = together((mixed, sent))[0]
+    mine = outward(False, f32, groups, mixed, out_ring.parts(), out_ring.unit_rows)
+    gain, router_t = together((moe_gain[None], router.T, mine))[:2]
     mine = expert_ring.pin(mine)
+    expert_ring.share()
     expert_ring.step()
-    mine, arrived = expert_ring.pin(mine, arrived)
-    expert_ring.step()
+
+    residual, moe_in, sent_rows = route(tokens, mine, arrived, gain, place)
+    landed = swap(sent_rows)
+    gates, own_rows = gate(moe_in, router_t, named, place)
+    outgoing = together((outgoing, own_rows))[0]
+    landed = expert_ring.pin(landed)
     expert_ring.share()
-
-    residual, gates, own_rows, sent_rows = route(
-        tokens, mine, arrived, moe_gain[None], router.T, named, place
-    )
-    landed = swap(sent_rows)
-    outgoing = lax.optimization_barrier((outgoing, sent_rows))[0]
     arrived_cache = lax.all_to_all(outgoing, "grp", split_axis=0, concat_axis=0, tiled=True)
     own_made, back = expert(
-        groups, own_rows, landed, expert_ring.parts(), up.shape[0], down.shape[0]
+        groups, own_rows, landed, expert_ring.parts(), up_rows, down_rows
     )
     returned = swap(back)
+    cache_after = write(arrived_cache, kv_cache)
     layer_out = combine(residual, gates, spread, own_made, returned)
-    cache_after = write(arrived_cache, kv_cache)
     return (layer_out, cache_after)
 
 

time: 105 us -> 99.6 us (0.949)
  starting transfers between devices: 22.9 us -> 20 us
  waiting for transfers between devices: 57.5 us -> 54.8 us
    ppermute x1, waiting for transfers between devices: 4.36 us -> 0.01 us  [two_lane_shards(): seam = lax.ppermute(tail, 'grp', [(g, g + 1) for g in range(groups - 1)])]
    ppermute x8, waiting for transfers between devices: 31.3 us -> 35.6 us  [step(): self.mine.append(self.across(held))]
    ppermute x1, waiting for transfers between devices: 8.34 us -> 4.4 us  [two_lane_shards(): arrived = swap(sent)]
    ppermute x1, waiting for transfers between devices: 6.48 us -> 3.34 us  [two_lane_shards(): other_tokens = swap(tokens)]
    ppermute x8, waiting for transfers between devices: 0.02 us -> 2.85 us  [share(): self.near.append(self.beside(self.mine[index]))]
    ppermute x8, starting transfers between devices: 3.54 us -> 4.95 us  [step(): self.mine.append(self.across(held))]
    ppermute x1, starting transfers between devices: 1.82 us -> 0.59 us  [two_lane_shards(): arrived = swap(sent)]
    ppermute x8, starting transfers between devices: 3.11 us -> 1.89 us  [share(): self.near.append(self.beside(self.mine[index]))]
  transfers between devices with their start and end apart: 25 -> 25, of which waited for: 9 -> 12; matrix products, arithmetic and copies ran while one was open for 2% -> 2% of each run, Pallas kernels for 12% -> 13%
where the time goes in v3:
time: 99.6 us; the launch traced here: 99.3 us
  waiting for transfers between devices  54.8 us (55%)
  starting transfers between devices  20 us (20%)
  Pallas kernels  17.1 us (17%)
  local copies, waits for them, and re-layouts  6.49 us (7%)
    ppermute x8, waiting for transfers between devices, step(): self.mine.append(self.across(held))  35.6 us
    all_to_all x1, starting transfers between devices, two_lane_shards(): lax.all_to_all(outgoing, 'grp', split_axis=0, concat_axis=0, tiled=True)  7.17 us
    unnamed x33, local copies, waits for them, and re-layouts  6.45 us
    ppermute x8, starting transfers between devices, step(): self.mine.append(self.across(held))  4.95 us
    ppermute x1, waiting for transfers between devices, two_lane_shards(): arrived = swap(sent)  4.4 us
    ppermute x1, waiting for transfers between devices, two_lane_shards(): landed = swap(sent_rows)  4.37 us
    ppermute x1, waiting for transfers between devices, two_lane_shards(): returned = swap(back)  4.28 us
    ppermute x1, waiting for transfers between devices, two_lane_shards(): other_tokens = swap(tokens)  3.34 us
  transfers between devices with their start and end apart: 25, of which 12 were waited for; matrix products, arithmetic and copies ran while one was open for 2% of the time, Pallas kernels for 13%

profile of v3, /device:TPU:12, one launch (start us, length us, event | category | flops | bytes accessed | tf_op | source)
XLA Modules:
  0.0 99.3 jit_solution(9318928527834189003)
XLA Ops:
  1.3 1.5 %collective-permute-start.5 = (bf16[128,1536]{1,0:T(8,128)(2,1)}, bf16[128,1536]{1,0:T(8,128)(2,1)S(1)}, u32[]{:S(2)}, u32[]{:S(2)}) collective-permute-start(bf16[128,1536]{1,0:T(8,128)(2,1)} %tokens.1), channel_id=1, source_target_pairs={{0,1},{1,0},{2,3},{3,2},{4,5},{5,4},{6,7},{7,6},{8,9},{9,8},{10,11... | collective-permute-start | bytes 1179656 | tf_op jit(solution)/shard_map/ppermute | solution.py:585
  4.8 0.7 prepare.1
  5.6 1.8 %copy.17 = bf16[192,8,4,128]{3,1,2,0:T(8,128)(2,1)S(1)} copy(bf16[192,8,4,128]{3,2,1,0:T(4,128)(2,1)} %bitcast.16) | data formatting | bytes 3145728
  7.5 1.1 %pack.1 = (bf16[576,512]{1,0:T(8,128)(2,1)S(1)}, bf16[192,768]{1,0:T(8,128)(2,1)S(1)}) custom-call(bf16[96,1024]{1,0:T(8,128)(2,1)} %bitcast.20, bf16[32,1536]{1,0:T(8,128)(2,1)} %bitcast.22, bf16[96,1536]{1,0:T(8,128)(2,1)} %bitcast.18, bf16[96,1024]{1,0:T(8,128)(2,1)S(1)} %collective-permute-done.refs_3_, ...), custom_call_target="tpu_custom_call" | custom-call | flops 1 | bytes 1 | tf_op jit(solution)/shard_map/pack/pallas_call | solution.py:149
  9.6 3.3 %collective-permute-done.5.other = bf16[128,1536]{1,0:T(8,128)(2,1)S(1)} collective-permute-done((bf16[128,1536]{1,0:T(8,128)(2,1)}, bf16[128,1536]{1,0:T(8,128)(2,1)S(1)}, u32[]{:S(2)}, u32[]{:S(2)}) %collective-permute-start.5) | collective-permute-done | bytes 393248 | tf_op jit(solution)/shard_map/ppermute | solution.py:585
  13.0 2.4 %collective-permute-done.4.refs_1_ = bf16[192,768]{1,0:T(8,128)(2,1)S(1)} collective-permute-done((bf16[192,768]{1,0:T(8,128)(2,1)S(1)}, bf16[192,768]{1,0:T(8,128)(2,1)S(1)}, u32[]{:S(2)}, u32[]{:S(2)}) %collective-permute-start.4) | collective-permute-done | bytes 294944 | tf_op jit(solution)/shard_map/ppermute | solution.py:70
  15.9 2.2 %project.1 = (bf16[256,768]{1,0:T(8,128)(2,1)S(1)}, bf16[256,512]{1,0:T(8,128)(2,1)S(1)}, bf16[128,512]{1,0:T(8,128)(2,1)S(1)}) custom-call(bf16[128,1536]{1,0:T(8,128)(2,1)S(1)} %copy-done.1, bf16[128,1536]{1,0:T(8,128)(2,1)S(1)} %collective-permute-done.5.other, f32[1,1536]{1,0:T(1,128)S(1)} %broadcast_in_dim.14.gain, ...), custom_call_target="tpu_custom_call" | custom-call | flops 1 | bytes 1 | tf_op jit(solution)/shard_map/project/pallas_call | solution.py:281
  18.1 2.1 %collective-permute-start.6 = (bf16[128,512]{1,0:T(8,128)(2,1)S(1)}, bf16[128,512]{1,0:T(8,128)(2,1)S(1)}, u32[]{:S(2)}, u32[]{:S(2)}) collective-permute-start(bf16[128,512]{1,0:T(8,128)(2,1)S(1)} %get-tuple-element.59), channel_id=1, source_target_pairs={{0,2},{2,4},{4,6},{6,8},{8,10},{10,12},{12,14},{14,16},{16,18},{18... | collective-permute-start | bytes 393224 | tf_op jit(solution)/shard_map/ppermute | solution.py:605
  20.2 1.4 %bundle.1 = bf16[16,144,128]{2,1,0:T(8,128)(2,1)} custom-call(bf16[512,256]{1,0:T(8,128)(2,1)S(1)} %get-tuple-element.62.send, bf16[256,512]{1,0:T(8,128)(2,1)S(1)} %get-tuple-element.63.kv, bf16[256,128]{1,0:T(8,128)(2,1)S(1)} %get-tuple-element.64.tags), custom_call_target="tpu_custom_call" | custom-call | flops 1 | bytes 1 | tf_op jit(solution)/shard_map/bundle/pallas_call | solution.py:512
  21.5 3.3 %collective-permute-done.7.refs_2_ = bf16[192,768]{1,0:T(8,128)(2,1)S(1)} collective-permute-done((bf16[192,768]{1,0:T(8,128)(2,1)S(1)}, bf16[192,768]{1,0:T(8,128)(2,1)S(1)}, u32[]{:S(2)}, u32[]{:S(2)}) %collective-permute-start.7) | collective-permute-done | bytes 294944 | tf_op jit(solution)/shard_map/ppermute | solution.py:70
  24.9 1.0 %collective-permute-start.8 = (bf16[576,512]{1,0:T(8,128)(2,1)S(1)}, bf16[576,512]{1,0:T(8,128)(2,1)S(1)}, u32[]{:S(2)}, u32[]{:S(2)}) collective-permute-start(bf16[576,512]{1,0:T(8,128)(2,1)S(1)} %collective-permute-done.3.refs_1_), channel_id=1, source_target_pairs={{0,8},{2,6},{8,16},{10,2},{16,24},{18,10},{24,28},{26,18},{28,20},... | collective-permute-start | bytes 1769480 | tf_op jit(solution)/shard_map/ppermute | solution.py:70
  26.0 12.0 %collective-permute-done.9.refs_3_ = bf16[192,768]{1,0:T(8,128)(2,1)S(1)} collective-permute-done((bf16[192,768]{1,0:T(8,128)(2,1)S(1)}, bf16[192,768]{1,0:T(8,128)(2,1)S(1)}, u32[]{:S(2)}, u32[]{:S(2)}) %collective-permute-start.9) | collective-permute-done | bytes 294944 | tf_op jit(solution)/shard_map/ppermute | solution.py:70
  37.9 1.1 %collective-permute-start.10 = (bf16[96,768]{1,0:T(8,128)(2,1)S(1)}, bf16[96,768]{1,0:T(8,128)(2,1)S(1)}, u32[]{:S(2)}, u32[]{:S(2)}) collective-permute-start(bf16[96,768]{1,0:T(8,128)(2,1)S(1)} %slice.6), channel_id=1, source_target_pairs={{0,8},{2,6},{8,16},{10,2},{16,24},{18,10},{24,28},{26,18},{28,20},... | collective-permute-start | bytes 442376 | tf_op jit(solution)/shard_map/ppermute | solution.py:70
  39.5 2.8 %attend.1.mixed = bf16[256,768]{1,0:T(8,128)(2,1)S(1)} custom-call(bf16[256,768]{1,0:T(8,128)(2,1)S(1)} %get-tuple-element.71.q, bf16[256,512]{1,0:T(8,128)(2,1)S(1)} %get-tuple-element.63.kv, bf16[128,512]{1,0:T(8,128)(2,1)S(1)} %collective-permute-done.6.seam, f32[256,128]{1,0:T(8,128)S(1)} %get-tuple-element.73.past), custom_call_target="tpu_custom_call" | custom-call | flops 1 | bytes 1 | tf_op jit(solution)/shard_map/attend/pallas_call | solution.py:334
  42.4 1.2 %collective-permute-done.10.refs_7_ = bf16[96,768]{1,0:T(8,128)(2,1)S(1)} collective-permute-done((bf16[96,768]{1,0:T(8,128)(2,1)S(1)}, bf16[96,768]{1,0:T(8,128)(2,1)S(1)}, u32[]{:S(2)}, u32[]{:S(2)}) %collective-permute-start.10) | collective-permute-done | bytes 147488 | tf_op jit(solution)/shard_map/ppermute | solution.py:70
  44.3 1.3 %collective-permute-done.15.refs_8_ = bf16[96,768]{1,0:T(8,128)(2,1)S(1)} collective-permute-done((bf16[96,768]{1,0:T(8,128)(2,1)S(1)}, bf16[96,768]{1,0:T(8,128)(2,1)S(1)}, u32[]{:S(2)}, u32[]{:S(2)}) %collective-permute-start.15) | collective-permute-done | bytes 147488 | tf_op jit(solution)/shard_map/ppermute | solution.py:79
  45.5 1.1 %outward_send.1 = bf16[128,1536]{1,0:T(8,128)(2,1)S(1)} custom-call(bf16[256,768]{1,0:T(8,128)(2,1)S(1)} %attend.1.mixed, bf16[192,768]{1,0:T(8,128)(2,1)S(1)} %get-tuple-element.54.refs_0_, bf16[192,768]{1,0:T(8,128)(2,1)S(1)} %collective-permute-done.4.refs_1_, bf16[192,768]{1,0:T(8,128)(2,1)S(1)} %collective-permute-done.7.refs_2_, ...), custom_call_target="tpu_custom_call" | custom-call | flops 1 | bytes 1 | tf_op jit(solution)/shard_map/outward_send/pallas_call | solution.py:364
  47.3 1.1 %outward_keep.1.mine = f32[128,1536]{1,0:T(8,128)S(1)} custom-call(bf16[256,768]{1,0:T(8,128)(2,1)S(1)} %attend.1.mixed, bf16[192,768]{1,0:T(8,128)(2,1)S(1)} %get-tuple-element.54.refs_0_, bf16[192,768]{1,0:T(8,128)(2,1)S(1)} %collective-permute-done.4.refs_1_, bf16[192,768]{1,0:T(8,128)(2,1)S(1)} %collective-permute-done.7.refs_2_, ...), custom_call_target="tpu_custom_call" | custom-call | flops 1 | bytes 1 | tf_op jit(solution)/shard_map/outward_keep/pallas_call | solution.py:364
  48.5 5.1 %collective-permute-done.11.refs_3_ = bf16[576,512]{1,0:T(8,128)(2,1)S(1)} collective-permute-done((bf16[576,512]{1,0:T(8,128)(2,1)S(1)}, bf16[576,512]{1,0:T(8,128)(2,1)S(1)}, u32[]{:S(2)}, u32[]{:S(2)}) %collective-permute-start.11) | collective-permute-done | bytes 589856 | tf_op jit(solution)/shard_map/ppermute | solution.py:70
  53.5 4.4 %collective-permute-done.16.arrived = bf16[128,1536]{1,0:T(8,128)(2,1)S(1)} collective-permute-done((bf16[128,1536]{1,0:T(8,128)(2,1)S(1)}, bf16[128,1536]{1,0:T(8,128)(2,1)S(1)}, u32[]{:S(2)}, u32[]{:S(2)}) %collective-permute-start.16) | collective-permute-done | bytes 393248 | tf_op jit(solution)/shard_map/ppermute | solution.py:620
  58.4 0.7 copy-done.3
  60.4 7.2 %all-to-all-start = ((bf16[16,144,128]{2,1,0:T(8,128)(2,1)}), bf16[16,144,128]{2,1,0:T(8,128)(2,1)S(1)}, u32[]{:S(2)}, u32[]{:S(2)}) async-start(bf16[16,144,128]{2,1,0:T(8,128)(2,1)} %bundle.1), calls=%async_computation | async-start | bytes 1179648 | tf_op jit(solution)/shard_map/all_to_all | solution.py:634
  67.6 0.8 collective-permute-start.17
  68.4 0.8 collective-permute-start.19
  70.3 4.4 %collective-permute-done.18.other = bf16[32,1536]{1,0:T(8,128)(2,1)S(1)} collective-permute-done((bf16[32,1536]{1,0:T(8,128)(2,1)}, bf16[32,1536]{1,0:T(8,128)(2,1)S(1)}, u32[]{:S(2)}, u32[]{:S(2)}) %collective-permute-start.18) | collective-permute-done | bytes 98336 | tf_op jit(solution)/shard_map/ppermute | solution.py:629
  74.6 11.5 %collective-permute-done.17.refs_7_ = bf16[288,512]{1,0:T(8,128)(2,1)S(1)} collective-permute-done((bf16[288,512]{1,0:T(8,128)(2,1)S(1)}, bf16[288,512]{1,0:T(8,128)(2,1)S(1)}, u32[]{:S(2)}, u32[]{:S(2)}) %collective-permute-start.17) | collective-permute-done | bytes 294944 | tf_op jit(solution)/shard_map/ppermute | solution.py:70
  86.2 1.6 %collective-permute-done.22.refs_8_ = bf16[288,512]{1,0:T(8,128)(2,1)S(1)} collective-permute-done((bf16[288,512]{1,0:T(8,128)(2,1)S(1)}, bf16[288,512]{1,0:T(8,128)(2,1)S(1)}, u32[]{:S(2)}, u32[]{:S(2)}) %collective-permute-start.22) | collective-permute-done | bytes 294944 | tf_op jit(solution)/shard_map/ppermute | solution.py:79
  87.7 0.9 copy-done.7
  88.6 1.3 %expert.1 = (bf16[32,1536]{1,0:T(8,128)(2,1)S(1)}, bf16[32,1536]{1,0:T(8,128)(2,1)S(1)}) custom-call(bf16[32,1536]{1,0:T(8,128)(2,1)S(1)} %copy-done.7, bf16[32,1536]{1,0:T(8,128)(2,1)S(1)} %collective-permute-done.18.other, bf16[576,512]{1,0:T(8,128)(2,1)S(1)} %get-tuple-element.53.refs_0_, bf16[576,512]{1,0:T(8,128)(2,1)S(1)} %collective-permute-done.3.refs_1_, ...), custom_call_target="tpu_custom_call" | custom-call | flops 1 | bytes 1 | tf_op jit(solution)/shard_map/expert/pallas_call | solution.py:450
  90.6 4.3 %collective-permute-done.23.returned = bf16[32,1536]{1,0:T(8,128)(2,1)S(1)} collective-permute-done((bf16[32,1536]{1,0:T(8,128)(2,1)S(1)}, bf16[32,1536]{1,0:T(8,128)(2,1)S(1)}, u32[]{:S(2)}, u32[]{:S(2)}) %collective-permute-start.23) | collective-permute-done | bytes 98336 | tf_op jit(solution)/shard_map/ppermute | solution.py:638
  94.9 1.1 %combine.1 = bf16[128,1536]{1,0:T(8,128)(2,1)} custom-call(bf16[128,1536]{1,0:T(8,128)(2,1)S(1)} %copy-done.4, f32[128,40]{1,0:T(8,128)S(1)} %get-tuple-element.86.gates, bf16[128,64]{1,0:T(8,128)(2,1)S(1)} %copy-done.9, bf16[32,1536]{1,0:T(8,128)(2,1)S(1)} %get-tuple-element.93.own, bf16[32,1536]{1,0:T(8,128)(2,1)S(1)} %collective-permute-done.23.returned), custom_call_target="tpu_custom_call" | custom-call | flops 1 | bytes 1 | tf_op jit(solution)/shard_map/combine/pallas_call | solution.py:482
  96.0 3.3 %write.1 = bf16[512,4,128]{2,1,0:T(4,128)(2,1)} custom-call(bf16[16,144,128]{2,1,0:T(8,128)(2,1)S(1)} %all-to-all-done.arrived, bf16[512,4,128]{2,1,0:T(4,128)(2,1)S(1)} %copy-done.2), custom_call_target="tpu_custom_call" | custom-call | flops 1 | bytes 1 | tf_op jit(solution)/shard_map/write/pallas_call | solution.py:548
  (67 shorter events, 9.4 us)
Async XLA Ops:
  0.6 6.8 %collective-permute-start.2 = (bf16[96,1536]{1,0:T(8,128)(2,1)}, bf16[96,1536]{1,0:T(8,128)(2,1)S(1)}, u32[]{:S(2)}, u32[]{:S(2)}) collective-permute-start(bf16[96,1536]{1,0:T(8,128)(2,1)} %bitcast.17), channel_id=1, source_target_pairs={{0,2},{2,0},{4,6},{6,4},{8,10},{10,8},{12,14},{14,12},{16,18},{18,... | collective-permute-start | bytes 884744 | tf_op jit(solution)/shard_map/ppermute | solution.py:588
  0.7 6.7 %collective-permute-start = (bf16[96,1024]{1,0:T(8,128)(2,1)}, bf16[96,1024]{1,0:T(8,128)(2,1)S(1)}, u32[]{:S(2)}, u32[]{:S(2)}) collective-permute-start(bf16[96,1024]{1,0:T(8,128)(2,1)} %bitcast.19), channel_id=1, source_target_pairs={{0,2},{2,0},{4,6},{6,4},{8,10},{10,8},{12,14},{14,12},{16,18},{18,... | collective-permute-start | bytes 589832 | tf_op jit(solution)/shard_map/ppermute | solution.py:588
  1.2 6.2 %collective-permute-start.1 = (bf16[32,1536]{1,0:T(8,128)(2,1)}, bf16[32,1536]{1,0:T(8,128)(2,1)S(1)}, u32[]{:S(2)}, u32[]{:S(2)}) collective-permute-start(bf16[32,1536]{1,0:T(8,128)(2,1)} %bitcast.21), channel_id=1, source_target_pairs={{0,2},{2,0},{4,6},{6,4},{8,10},{10,8},{12,14},{14,12},{16,18},{18,... | collective-permute-start | bytes 294920 | tf_op jit(solution)/shard_map/ppermute | solution.py:588
  1.3 11.7 %collective-permute-start.5 = (bf16[128,1536]{1,0:T(8,128)(2,1)}, bf16[128,1536]{1,0:T(8,128)(2,1)S(1)}, u32[]{:S(2)}, u32[]{:S(2)}) collective-permute-start(bf16[128,1536]{1,0:T(8,128)(2,1)} %tokens.1), channel_id=1, source_target_pairs={{0,1},{1,0},{2,3},{3,2},{4,5},{5,4},{6,7},{7,6},{8,9},{9,8},{10,11... | collective-permute-start | bytes 1179656 | tf_op jit(solution)/shard_map/ppermute | solution.py:585
  5.5 10.3 %copy-start.14 = (f32[1536]{0:T(1024)S(1)}, f32[1536]{0:T(1024)}, u32[]{:S(2)}) copy-start(f32[1536]{0:T(1024)} %param.15) | copy-start | bytes 18436
  5.6 10.3 %copy-start = (bf16[1536,768]{1,0:T(8,128)(2,1)S(1)}, bf16[1536,768]{1,0:T(8,128)(2,1)}, u32[]{:S(2)}) copy-start(bf16[1536,768]{1,0:T(8,128)(2,1)} %w_query.1) | copy-start | bytes 7077892
  5.6 10.3 %copy-start.1 = (bf16[128,1536]{1,0:T(8,128)(2,1)S(1)}, bf16[128,1536]{1,0:T(8,128)(2,1)}, u32[]{:S(2)}) copy-start(bf16[128,1536]{1,0:T(8,128)(2,1)} %tokens.1) | copy-start | bytes 1179652
  8.6 6.8 %collective-permute-start.4 = (bf16[192,768]{1,0:T(8,128)(2,1)S(1)}, bf16[192,768]{1,0:T(8,128)(2,1)S(1)}, u32[]{:S(2)}, u32[]{:S(2)}) collective-permute-start(bf16[192,768]{1,0:T(8,128)(2,1)S(1)} %get-tuple-element.54.refs_0_), channel_id=1, source_target_pairs={{0,8},{2,6},{8,16},{10,2},{16,24},{18,10},{24,28},{26,18},{28,20},... | collective-permute-start | bytes 884744 | tf_op jit(solution)/shard_map/ppermute | solution.py:70
  9.1 15.8 %collective-permute-start.3 = (bf16[576,512]{1,0:T(8,128)(2,1)S(1)}, bf16[576,512]{1,0:T(8,128)(2,1)S(1)}, u32[]{:S(2)}, u32[]{:S(2)}) collective-permute-start(bf16[576,512]{1,0:T(8,128)(2,1)S(1)} %get-tuple-element.53.refs_0_), channel_id=1, source_target_pairs={{0,8},{2,6},{8,16},{10,2},{16,24},{18,10},{24,28},{26,18},{28,20},... | collective-permute-start | bytes 1769480 | tf_op jit(solution)/shard_map/ppermute | solution.py:70
  15.4 9.5 %collective-permute-start.7 = (bf16[192,768]{1,0:T(8,128)(2,1)S(1)}, bf16[192,768]{1,0:T(8,128)(2,1)S(1)}, u32[]{:S(2)}, u32[]{:S(2)}) collective-permute-start(bf16[192,768]{1,0:T(8,128)(2,1)S(1)} %collective-permute-done.4.refs_1_), channel_id=1, source_target_pairs={{0,8},{2,6},{8,16},{10,2},{16,24},{18,10},{24,28},{26,18},{28,20},... | collective-permute-start | bytes 884744 | tf_op jit(solution)/shard_map/ppermute | solution.py:70
  18.1 6.8 %collective-permute-start.6 = (bf16[128,512]{1,0:T(8,128)(2,1)S(1)}, bf16[128,512]{1,0:T(8,128)(2,1)S(1)}, u32[]{:S(2)}, u32[]{:S(2)}) collective-permute-start(bf16[128,512]{1,0:T(8,128)(2,1)S(1)} %get-tuple-element.59), channel_id=1, source_target_pairs={{0,2},{2,4},{4,6},{6,8},{8,10},{10,12},{12,14},{14,16},{16,18},{18... | collective-permute-start | bytes 393224 | tf_op jit(solution)/shard_map/ppermute | solution.py:605
  24.9 18.8 %collective-permute-start.8 = (bf16[576,512]{1,0:T(8,128)(2,1)S(1)}, bf16[576,512]{1,0:T(8,128)(2,1)S(1)}, u32[]{:S(2)}, u32[]{:S(2)}) collective-permute-start(bf16[576,512]{1,0:T(8,128)(2,1)S(1)} %collective-permute-done.3.refs_1_), channel_id=1, source_target_pairs={{0,8},{2,6},{8,16},{10,2},{16,24},{18,10},{24,28},{26,18},{28,20},... | collective-permute-start | bytes 1769480 | tf_op jit(solution)/shard_map/ppermute | solution.py:70
  25.9 12.0 %collective-permute-start.9 = (bf16[192,768]{1,0:T(8,128)(2,1)S(1)}, bf16[192,768]{1,0:T(8,128)(2,1)S(1)}, u32[]{:S(2)}, u32[]{:S(2)}) collective-permute-start(bf16[192,768]{1,0:T(8,128)(2,1)S(1)} %collective-permute-done.7.refs_2_), channel_id=1, source_target_pairs={{0,8},{2,6},{8,16},{10,2},{16,24},{18,10},{24,28},{26,18},{28,20},... | collective-permute-start | bytes 884744 | tf_op jit(solution)/shard_map/ppermute | solution.py:70
  37.9 5.7 %collective-permute-start.10 = (bf16[96,768]{1,0:T(8,128)(2,1)S(1)}, bf16[96,768]{1,0:T(8,128)(2,1)S(1)}, u32[]{:S(2)}, u32[]{:S(2)}) collective-permute-start(bf16[96,768]{1,0:T(8,128)(2,1)S(1)} %slice.6), channel_id=1, source_target_pairs={{0,8},{2,6},{8,16},{10,2},{16,24},{18,10},{24,28},{26,18},{28,20},... | collective-permute-start | bytes 442376 | tf_op jit(solution)/shard_map/ppermute | solution.py:70
  39.0 5.2 %collective-permute-start.12 = (bf16[192,768]{1,0:T(8,128)(2,1)S(1)}, bf16[192,768]{1,0:T(8,128)(2,1)S(1)}, u32[]{:S(2)}, u32[]{:S(2)}) collective-permute-start(bf16[192,768]{1,0:T(8,128)(2,1)S(1)} %collective-permute-done.4.refs_1_), channel_id=1, source_target_pairs={{0,2},{2,0},{4,6},{6,4},{8,10},{10,8},{12,14},{14,12},{16,18},{18,... | collective-permute-start | bytes 884744 | tf_op jit(solution)/shard_map/ppermute | solution.py:79
  39.0 5.2 %collective-permute-start.13 = (bf16[192,768]{1,0:T(8,128)(2,1)S(1)}, bf16[192,768]{1,0:T(8,128)(2,1)S(1)}, u32[]{:S(2)}, u32[]{:S(2)}) collective-permute-start(bf16[192,768]{1,0:T(8,128)(2,1)S(1)} %collective-permute-done.7.refs_2_), channel_id=1, source_target_pairs={{0,2},{2,0},{4,6},{6,4},{8,10},{10,8},{12,14},{14,12},{16,18},{18,... | collective-permute-start | bytes 884744 | tf_op jit(solution)/shard_map/ppermute | solution.py:79
  39.5 4.7 %collective-permute-start.14 = (bf16[192,768]{1,0:T(8,128)(2,1)S(1)}, bf16[192,768]{1,0:T(8,128)(2,1)S(1)}, u32[]{:S(2)}, u32[]{:S(2)}) collective-permute-start(bf16[192,768]{1,0:T(8,128)(2,1)S(1)} %collective-permute-done.9.refs_3_), channel_id=1, source_target_pairs={{0,2},{2,0},{4,6},{6,4},{8,10},{10,8},{12,14},{14,12},{16,18},{18,... | collective-permute-start | bytes 884744 | tf_op jit(solution)/shard_map/ppermute | solution.py:79
  43.6 9.9 %collective-permute-start.11 = (bf16[576,512]{1,0:T(8,128)(2,1)S(1)}, bf16[576,512]{1,0:T(8,128)(2,1)S(1)}, u32[]{:S(2)}, u32[]{:S(2)}) collective-permute-start(bf16[576,512]{1,0:T(8,128)(2,1)S(1)} %collective-permute-done.8.refs_2_), channel_id=1, source_target_pairs={{0,8},{2,6},{8,16},{10,2},{16,24},{18,10},{24,28},{26,18},{28,20},... | collective-permute-start | bytes 1769480 | tf_op jit(solution)/shard_map/ppermute | solution.py:70
  44.2 1.4 %collective-permute-start.15 = (bf16[96,768]{1,0:T(8,128)(2,1)S(1)}, bf16[96,768]{1,0:T(8,128)(2,1)S(1)}, u32[]{:S(2)}, u32[]{:S(2)}) collective-permute-start(bf16[96,768]{1,0:T(8,128)(2,1)S(1)} %collective-permute-done.10.refs_7_), channel_id=1, source_target_pairs={{0,2},{2,0},{4,6},{6,4},{8,10},{10,8},{12,14},{14,12},{16,18},{18,... | collective-permute-start | bytes 442376 | tf_op jit(solution)/shard_map/ppermute | solution.py:79
  46.7 11.2 %collective-permute-start.16 = (bf16[128,1536]{1,0:T(8,128)(2,1)S(1)}, bf16[128,1536]{1,0:T(8,128)(2,1)S(1)}, u32[]{:S(2)}, u32[]{:S(2)}) collective-permute-start(bf16[128,1536]{1,0:T(8,128)(2,1)S(1)} %outward_send.1), channel_id=1, source_target_pairs={{0,1},{1,0},{2,3},{3,2},{4,5},{5,4},{6,7},{7,6},{8,9},{9,8},{10,11... | collective-permute-start | bytes 1179656 | tf_op jit(solution)/shard_map/ppermute | solution.py:620
  48.5 10.7 %copy-start.5 = (bf16[1536,40]{0,1:T(8,128)(2,1)S(1)}, bf16[1536,40]{0,1:T(8,128)(2,1)}, u32[]{:S(2)}) copy-start(bf16[1536,40]{0,1:T(8,128)(2,1)} %param.20) | copy-start | bytes 368644
  60.4 35.6 %all-to-all-start = ((bf16[16,144,128]{2,1,0:T(8,128)(2,1)}), bf16[16,144,128]{2,1,0:T(8,128)(2,1)S(1)}, u32[]{:S(2)}, u32[]{:S(2)}) async-start(bf16[16,144,128]{2,1,0:T(8,128)(2,1)} %bundle.1), calls=%async_computation | async-start | bytes 1179648 | tf_op jit(solution)/shard_map/all_to_all | solution.py:634
  67.6 27.3 %copy-start.9 = (bf16[128,64]{1,0:T(8,128)(2,1)S(1)}, bf16[128,64]{1,0:T(8,128)(2,1)}, u32[]{:S(2)}) copy-start(bf16[128,64]{1,0:T(8,128)(2,1)} %copy-done.8) | copy-start | bytes 49156
  67.6 18.5 %collective-permute-start.17 = (bf16[288,512]{1,0:T(8,128)(2,1)S(1)}, bf16[288,512]{1,0:T(8,128)(2,1)S(1)}, u32[]{:S(2)}, u32[]{:S(2)}) collective-permute-start(bf16[288,512]{1,0:T(8,128)(2,1)S(1)} %slice.7), channel_id=1, source_target_pairs={{0,8},{2,6},{8,16},{10,2},{16,24},{18,10},{24,28},{26,18},{28,20},... | collective-permute-start | bytes 884744 | tf_op jit(solution)/shard_map/ppermute | solution.py:70
  68.4 17.7 %collective-permute-start.19 = (bf16[576,512]{1,0:T(8,128)(2,1)S(1)}, bf16[576,512]{1,0:T(8,128)(2,1)S(1)}, u32[]{:S(2)}, u32[]{:S(2)}) collective-permute-start(bf16[576,512]{1,0:T(8,128)(2,1)S(1)} %collective-permute-done.3.refs_1_), channel_id=1, source_target_pairs={{0,2},{2,0},{4,6},{6,4},{8,10},{10,8},{12,14},{14,12},{16,18},{18,... | collective-permute-start | bytes 1769480 | tf_op jit(solution)/shard_map/ppermute | solution.py:79
  69.2 17.0 %collective-permute-start.20 = (bf16[576,512]{1,0:T(8,128)(2,1)S(1)}, bf16[576,512]{1,0:T(8,128)(2,1)S(1)}, u32[]{:S(2)}, u32[]{:S(2)}) collective-permute-start(bf16[576,512]{1,0:T(8,128)(2,1)S(1)} %collective-permute-done.8.refs_2_), channel_id=1, source_target_pairs={{0,2},{2,0},{4,6},{6,4},{8,10},{10,8},{12,14},{14,12},{16,18},{18,... | collective-permute-start | bytes 1769480 | tf_op jit(solution)/shard_map/ppermute | solution.py:79
  69.2 18.5 %collective-permute-start.21 = (bf16[576,512]{1,0:T(8,128)(2,1)S(1)}, bf16[576,512]{1,0:T(8,128)(2,1)S(1)}, u32[]{:S(2)}, u32[]{:S(2)}) collective-permute-start(bf16[576,512]{1,0:T(8,128)(2,1)S(1)} %collective-permute-done.11.refs_3_), channel_id=1, source_target_pairs={{0,2},{2,0},{4,6},{6,4},{8,10},{10,8},{12,14},{14,12},{16,18},{18,... | collective-permute-start | bytes 1769480 | tf_op jit(solution)/shard_map/ppermute | solution.py:79
  69.7 25.1 %copy-start.4 = (bf16[128,1536]{1,0:T(8,128)(2,1)S(1)}, bf16[128,1536]{1,0:T(8,128)(2,1)}, u32[]{:S(2)}) copy-start(bf16[128,1536]{1,0:T(8,128)(2,1)} %copy-done.3) | copy-start | bytes 1179652
  69.7 26.3 %copy-start.2 = (bf16[512,4,128]{2,1,0:T(4,128)(2,1)S(1)}, bf16[512,4,128]{2,1,0:T(4,128)(2,1)}, u32[]{:S(2)}) copy-start(bf16[512,4,128]{2,1,0:T(4,128)(2,1)} %cache.1) | copy-start | bytes 1572868
  69.7 4.9 %collective-permute-start.18 = (bf16[32,1536]{1,0:T(8,128)(2,1)}, bf16[32,1536]{1,0:T(8,128)(2,1)S(1)}, u32[]{:S(2)}, u32[]{:S(2)}) collective-permute-start(bf16[32,1536]{1,0:T(8,128)(2,1)} %copy-done.13), channel_id=1, source_target_pairs={{0,1},{1,0},{2,3},{3,2},{4,5},{5,4},{6,7},{7,6},{8,9},{9,8},{10,11... | collective-permute-start | bytes 294920 | tf_op jit(solution)/shard_map/ppermute | solution.py:629
  86.1 1.6 %collective-permute-start.22 = (bf16[288,512]{1,0:T(8,128)(2,1)S(1)}, bf16[288,512]{1,0:T(8,128)(2,1)S(1)}, u32[]{:S(2)}, u32[]{:S(2)}) collective-permute-start(bf16[288,512]{1,0:T(8,128)(2,1)S(1)} %collective-permute-done.17.refs_7_), channel_id=1, source_target_pairs={{0,2},{2,0},{4,6},{6,4},{8,10},{10,8},{12,14},{14,12},{16,18},{18,... | collective-permute-start | bytes 884744 | tf_op jit(solution)/shard_map/ppermute | solution.py:79
  90.0 4.9 %collective-permute-start.23 = (bf16[32,1536]{1,0:T(8,128)(2,1)S(1)}, bf16[32,1536]{1,0:T(8,128)(2,1)S(1)}, u32[]{:S(2)}, u32[]{:S(2)}) collective-permute-start(bf16[32,1536]{1,0:T(8,128)(2,1)S(1)} %get-tuple-element.94), channel_id=1, source_target_pairs={{0,1},{1,0},{2,3},{3,2},{4,5},{5,4},{6,7},{7,6},{8,9},{9,8},{10,11... | collective-permute-start | bytes 294920 | tf_op jit(solution)/shard_map/ppermute | solution.py:638
  (9 other events, 11.8 us)

commit v4 on v3

--- a/solution.py
+++ b/solution.py
@@ -165,9 +165,15 @@
     return jnp.sum(jnp.where(eye, row, 0.0), axis=1, keepdims=True)
 
 
-def prepare_kernel(
-    groups, slots_dev, positions, slots, ids, cosine, sine, past, named, place, spread, send, tags
-):
+def prepare_kernel(groups, slots_dev, *refs):
+    sources, (cosine, sine, past, named, place, spread, send, tags, gain, late_gain, router) = (
+        refs[:6],
+        refs[6:17],
+    )
+    positions, slots, ids, sems = refs[17:]
+    copies = fetch(list(zip(sources, (positions, slots, ids, gain, late_gain, router))), sems)
+    for copy in copies:
+        copy.wait()
     lane = lax.axis_index("hd")
     block = positions.shape[1]
 
@@ -221,8 +227,9 @@
     tags[...] = jnp.where(spot == 0, high, jnp.where(spot == 1, low, 0.0)).astype(bf16)
 
 
-def prepare(groups, slots_dev, positions, slots, ids, experts):
+def prepare(groups, slots_dev, positions, slots, ids, gain, late_gain, router):
     block, tokens = positions.shape[0], ids.shape[0]
+    model, experts = router.shape
     cap = tokens // 4
     capc = 2 * block // groups
     shapes = [
@@ -234,16 +241,26 @@
         ((tokens, 2 * cap), bf16),
         ((groups * capc, block), bf16),
         ((block, 128), bf16),
+        ((1, model), f32),
+        ((1, model), f32),
+        ((experts, model), bf16),
     ]
+    sources = (positions[None], slots[None], ids.T, gain[None], late_gain[None], router.T)
     return pl.pallas_call(
         functools.partial(prepare_kernel, groups, slots_dev),
         out_shape=tuple(jax.ShapeDtypeStruct(shape, kind) for shape, kind in shapes),
-        in_specs=[VMEM] * 3,
+        in_specs=[ANY] * 6,
         out_specs=(VMEM,) * len(shapes),
+        scratch_shapes=[
+            pltpu.VMEM((1, block), jnp.int32),
+            pltpu.VMEM((1, block), jnp.int32),
+            pltpu.VMEM(ids.shape[::-1], jnp.int32),
+            pltpu.SemaphoreType.DMA((6,)),
+        ],
         compiler_params=PARAMS,
         cost_estimate=LITTLE,
         name="prepare",
-    )(positions[None], slots[None], ids.T)
+    )(*[pltpu.with_memory_space_constraint(source, pltpu.HBM) for source in sources])
 
 
 def project_kernel(
@@ -587,21 +604,20 @@
     up_rows, down_rows = own[0].shape[0], own[1].shape[0]
     beside = [lax.ppermute(part, "grp", sibling_pairs(groups)) for part in own]
     flat_kv = w_keyval.reshape(model, kv_width)
-    cosine, sine, past, named, place, spread, send, tags = prepare(
-        groups, slots_dev, positions, cache_slot, expert_ids, router.shape[1]
-    )
-    beside, cosine, flat_kv = together((beside, cosine, flat_kv))
+    beside, flat_kv = together((beside, flat_kv))
     expert_pair, out_pair = pack(own, beside)
     out_ring = Ring(out_pair, groups)
     out_ring.step()
     expert_ring = Ring(expert_pair, groups)
     expert_ring.step()
-    other_tokens = out_ring.pin(other_tokens)
+    positions = together((positions, out_pair))[0]
+    cosine, sine, past, named, place, spread, send, tags, gain, late_gain, router_t = prepare(
+        groups, slots_dev, positions, cache_slot, expert_ids, attn_gain, moe_gain, router
+    )
+    other_tokens, cosine = out_ring.pin(other_tokens, cosine)
     out_ring.step()
 
-    q, kv, tail = project(
-        tokens, other_tokens, attn_gain[None], cosine, sine, w_query, flat_kv
-    )
+    q, kv, tail = project(tokens, other_tokens, gain, cosine, sine, w_query, flat_kv)
     seam = lax.ppermute(tail, "grp", [(g, g + 1) for g in range(groups - 1)])
     outgoing = bundle(groups, send, kv, tags)
     outgoing = out_ring.pin(outgoing)
@@ -609,10 +625,9 @@
     seam, q = together((seam, q, outgoing))[:2]
     seam = expert_ring.pin(seam)
     expert_ring.step()
-    seam = out_ring.pin(seam)
-    out_ring.step()
     mixed = attend(q, kv, seam, past)
     mixed = out_ring.pin(mixed)
+    out_ring.step()
     out_ring.mine[-1] = expert_ring.pin(out_ring.mine[-1])
     out_ring.share()
     expert_ring.step()
@@ -620,23 +635,23 @@
     arrived = swap(sent)
     mixed = together((mixed, sent))[0]
     mine = outward(False, f32, groups, mixed, out_ring.parts(), out_ring.unit_rows)
-    gain, router_t = together((moe_gain[None], router.T, mine))[:2]
-    mine = expert_ring.pin(mine)
+    outgoing, mine = together((outgoing, mine))
+    arrived_cache = lax.all_to_all(outgoing, "grp", split_axis=0, concat_axis=0, tiled=True)
+
+    residual, moe_in, sent_rows = route(tokens, mine, arrived, late_gain, place)
+    landed = swap(sent_rows)
+    gates, own_rows = gate(moe_in, router_t, named, place)
+    landed, own_rows = expert_ring.pin(landed, own_rows)
     expert_ring.share()
     expert_ring.step()
-
-    residual, moe_in, sent_rows = route(tokens, mine, arrived, gain, place)
-    landed = swap(sent_rows)
-    gates, own_rows = gate(moe_in, router_t, named, place)
-    outgoing = together((outgoing, own_rows))[0]
-    landed = expert_ring.pin(landed)
     expert_ring.share()
-    arrived_cache = lax.all_to_all(outgoing, "grp", split_axis=0, concat_axis=0, tiled=True)
     own_made, back = expert(
         groups, own_rows, landed, expert_ring.parts(), up_rows, down_rows
     )
     returned = swap(back)
+    arrived_cache = together((arrived_cache, back))[0]
     cache_after = write(arrived_cache, kv_cache)
+    returned, cache_after = together((returned, cache_after))
     layer_out = combine(residual, gates, spread, own_made, returned)
     return (layer_out, cache_after)
 

time: 99.6 us -> 84.3 us (0.85)
  the two profiles are of different devices: /device:TPU:12 before, /device:TPU:0 now
where the time goes in v4:
time: 84.3 us; the launch traced here: 83.9 us
  starting transfers between devices  32.6 us (39%)
  waiting for transfers between devices  23.7 us (28%)
  Pallas kernels  21.6 us (26%)
  local copies, waits for them, and re-layouts  5.19 us (6%)
  between operations  0.86 us (1%)
    ppermute x8, starting transfers between devices, step(): self.mine.append(self.across(held))  17.8 us
    ppermute x8, waiting for transfers between devices, step(): self.mine.append(self.across(held))  16.2 us
    all_to_all x1, starting transfers between devices, two_lane_shards(): lax.all_to_all(outgoing, 'grp', split_axis=0, concat_axis=0, tiled=True)  4.69 us
    unnamed x31, local copies, waits for them, and re-layouts  3.96 us
    pallas_call x1, Pallas kernels, write(): pl.pallas_call(write_kernel, out_shape=jax.ShapeDtypeStruct(cache.shape,...  3.27 us
    pallas_call x1, Pallas kernels, expert(): pl.pallas_call(functools.partial(expert_kernel, groups, up_rows, down_row...  3.04 us
    pallas_call x2, Pallas kernels, outward(): pl.pallas_call(functools.partial(outward_kernel, flip, groups, unit_rows,...  3.03 us
    ppermute x1, waiting for transfers between devices, two_lane_shards(): arrived = swap(sent)  2.98 us
  transfers between devices with their start and end apart: 25, of which 9 were waited for; matrix products, arithmetic and copies ran while one was open for 4% of the time, Pallas kernels for 24%

profile of v4, /device:TPU:0, one launch (start us, length us, event | category | flops | bytes accessed | tf_op | source)
XLA Modules:
  0.0 83.9 jit_solution(16314283829804414317)
XLA Ops:
  1.7 2.6 %collective-permute-start.4 = (bf16[128,1536]{1,0:T(8,128)(2,1)}, bf16[128,1536]{1,0:T(8,128)(2,1)S(1)}, u32[]{:S(2)}, u32[]{:S(2)}) collective-permute-start(bf16[128,1536]{1,0:T(8,128)(2,1)} %tokens.1), channel_id=1, source_target_pairs={{0,1},{1,0},{2,3},{3,2},{4,5},{5,4},{6,7},{7,6},{8,9},{9,8},{10,11... | collective-permute-start | bytes 1179656 | tf_op jit(solution)/shard_map/ppermute | solution.py:602
  4.2 1.8 %copy.17 = bf16[192,8,4,128]{3,1,2,0:T(8,128)(2,1)S(1)} copy(bf16[192,8,4,128]{3,2,1,0:T(4,128)(2,1)} %bitcast.12) | data formatting | bytes 3145728
  6.1 1.1 %pack.1 = (bf16[576,512]{1,0:T(8,128)(2,1)S(1)}, bf16[192,768]{1,0:T(8,128)(2,1)S(1)}) custom-call(bf16[96,1024]{1,0:T(8,128)(2,1)} %bitcast.16, bf16[32,1536]{1,0:T(8,128)(2,1)} %bitcast.19, bf16[96,1536]{1,0:T(8,128)(2,1)} %bitcast.14, bf16[96,1024]{1,0:T(8,128)(2,1)S(1)} %collective-permute-done.refs_3_, ...), custom_call_target="tpu_custom_call" | custom-call | flops 1 | bytes 1 | tf_op jit(solution)/shard_map/pack/pallas_call | solution.py:149
  7.3 1.6 %collective-permute-start.3 = (bf16[192,768]{1,0:T(8,128)(2,1)S(1)}, bf16[192,768]{1,0:T(8,128)(2,1)S(1)}, u32[]{:S(2)}, u32[]{:S(2)}) collective-permute-start(bf16[192,768]{1,0:T(8,128)(2,1)S(1)} %get-tuple-element.55.refs_0_), channel_id=1, source_target_pairs={{0,8},{2,6},{8,16},{10,2},{16,24},{18,10},{24,28},{26,18},{28,20},... | collective-permute-start | bytes 884744 | tf_op jit(solution)/shard_map/ppermute | solution.py:70
  8.9 1.6 %collective-permute-start.8 = (bf16[576,512]{1,0:T(8,128)(2,1)S(1)}, bf16[576,512]{1,0:T(8,128)(2,1)S(1)}, u32[]{:S(2)}, u32[]{:S(2)}) collective-permute-start(bf16[576,512]{1,0:T(8,128)(2,1)S(1)} %get-tuple-element.72.refs_0_), channel_id=1, source_target_pairs={{0,8},{2,6},{8,16},{10,2},{16,24},{18,10},{24,28},{26,18},{28,20},... | collective-permute-start | bytes 1769480 | tf_op jit(solution)/shard_map/ppermute | solution.py:70
  11.7 1.7 %prepare.1 = (f32[256,128]{1,0:T(8,128)S(1)}, f32[256,128]{1,0:T(8,128)S(1)}, f32[256,128]{1,0:T(8,128)S(1)}, f32[128,40]{1,0:T(8,128)S(1)}, bf16[64,128]{1,0:T(...) custom-call(s32[1,256]{1,0:T(1,128)} %bitcast.21, ...), custom_call_target="tpu_custom_call" | custom-call | flops 1 | bytes 1 | tf_op jit(solution)/shard_map/prepare/pallas_call | solution.py:249
  14.1 1.8 %collective-permute-start.5 = (bf16[192,768]{1,0:T(8,128)(2,1)S(1)}, bf16[192,768]{1,0:T(8,128)(2,1)S(1)}, u32[]{:S(2)}, u32[]{:S(2)}) collective-permute-start(bf16[192,768]{1,0:T(8,128)(2,1)S(1)} %collective-permute-done.3.refs_1_), channel_id=1, source_target_pairs={{0,8},{2,6},{8,16},{10,2},{16,24},{18,10},{24,28},{26,18},{28,20},... | collective-permute-start | bytes 884744 | tf_op jit(solution)/shard_map/ppermute | solution.py:70
  16.0 2.2 %project.1 = (bf16[256,768]{1,0:T(8,128)(2,1)S(1)}, bf16[256,512]{1,0:T(8,128)(2,1)S(1)}, bf16[128,512]{1,0:T(8,128)(2,1)S(1)}) custom-call(bf16[128,1536]{1,0:T(8,128)(2,1)S(1)} %copy-done.1, bf16[128,1536]{1,0:T(8,128)(2,1)S(1)} %collective-permute-done.4.other, f32[1,1536]{1,0:T(1,128)S(1)} %get-tuple-element.61.gain, ...), custom_call_target="tpu_custom_call" | custom-call | flops 1 | bytes 1 | tf_op jit(solution)/shard_map/project/pallas_call | solution.py:298
  18.2 1.3 %collective-permute-start.7 = (bf16[128,512]{1,0:T(8,128)(2,1)S(1)}, bf16[128,512]{1,0:T(8,128)(2,1)S(1)}, u32[]{:S(2)}, u32[]{:S(2)}) collective-permute-start(bf16[128,512]{1,0:T(8,128)(2,1)S(1)} %get-tuple-element.69), channel_id=1, source_target_pairs={{0,2},{2,4},{4,6},{6,8},{8,10},{10,12},{12,14},{14,16},{16,18},{18... | collective-permute-start | bytes 393224 | tf_op jit(solution)/shard_map/ppermute | solution.py:621
  19.5 1.4 %bundle.1 = bf16[16,144,128]{2,1,0:T(8,128)(2,1)} custom-call(bf16[512,256]{1,0:T(8,128)(2,1)S(1)} %get-tuple-element.59.send, bf16[256,512]{1,0:T(8,128)(2,1)S(1)} %get-tuple-element.65.kv, bf16[256,128]{1,0:T(8,128)(2,1)S(1)} %get-tuple-element.66.tags), custom_call_target="tpu_custom_call" | custom-call | flops 1 | bytes 1 | tf_op jit(solution)/shard_map/bundle/pallas_call | solution.py:529
  20.9 2.6 %collective-permute-done.5.refs_2_ = bf16[192,768]{1,0:T(8,128)(2,1)S(1)} collective-permute-done((bf16[192,768]{1,0:T(8,128)(2,1)S(1)}, bf16[192,768]{1,0:T(8,128)(2,1)S(1)}, u32[]{:S(2)}, u32[]{:S(2)}) %collective-permute-start.5) | collective-permute-done | bytes 294944 | tf_op jit(solution)/shard_map/ppermute | solution.py:70
  23.5 3.5 %collective-permute-start.12 = (bf16[576,512]{1,0:T(8,128)(2,1)S(1)}, bf16[576,512]{1,0:T(8,128)(2,1)}, u32[]{:S(2)}, u32[]{:S(2)}) collective-permute-start(bf16[576,512]{1,0:T(8,128)(2,1)S(1)} %collective-permute-done.8.refs_1_), channel_id=1, source_target_pairs={{0,8},{2,6},{8,16},{10,2},{16,24},{18,10},{24,28},{26,18},{28,20},... | collective-permute-start | bytes 1769480 | tf_op jit(solution)/shard_map/ppermute | solution.py:70
  27.0 1.6 %collective-permute-start.6 = (bf16[192,768]{1,0:T(8,128)(2,1)S(1)}, bf16[192,768]{1,0:T(8,128)(2,1)S(1)}, u32[]{:S(2)}, u32[]{:S(2)}) collective-permute-start(bf16[192,768]{1,0:T(8,128)(2,1)S(1)} %collective-permute-done.5.refs_2_), channel_id=1, source_target_pairs={{0,8},{2,6},{8,16},{10,2},{16,24},{18,10},{24,28},{26,18},{28,20},... | collective-permute-start | bytes 884744 | tf_op jit(solution)/shard_map/ppermute | solution.py:70
  28.6 2.8 %attend.1.mixed = bf16[256,768]{1,0:T(8,128)(2,1)S(1)} custom-call(bf16[256,768]{1,0:T(8,128)(2,1)S(1)} %get-tuple-element.71.q, bf16[256,512]{1,0:T(8,128)(2,1)S(1)} %get-tuple-element.65.kv, bf16[128,512]{1,0:T(8,128)(2,1)S(1)} %collective-permute-done.7.seam, f32[256,128]{1,0:T(8,128)S(1)} %get-tuple-element.75.past), custom_call_target="tpu_custom_call" | custom-call | flops 1 | bytes 1 | tf_op jit(solution)/shard_map/attend/pallas_call | solution.py:351
  31.4 6.1 %collective-permute-done.6.refs_3_ = bf16[192,768]{1,0:T(8,128)(2,1)S(1)} collective-permute-done((bf16[192,768]{1,0:T(8,128)(2,1)S(1)}, bf16[192,768]{1,0:T(8,128)(2,1)S(1)}, u32[]{:S(2)}, u32[]{:S(2)}) %collective-permute-start.6) | collective-permute-done | bytes 294944 | tf_op jit(solution)/shard_map/ppermute | solution.py:70
  37.6 2.5 %collective-permute-start.13 = (bf16[96,768]{1,0:T(8,128)(2,1)S(1)}, bf16[96,768]{1,0:T(8,128)(2,1)S(1)}, u32[]{:S(2)}, u32[]{:S(2)}) collective-permute-start(bf16[96,768]{1,0:T(8,128)(2,1)S(1)} %slice.6), channel_id=1, source_target_pairs={{0,8},{2,6},{8,16},{10,2},{16,24},{18,10},{24,28},{26,18},{28,20},... | collective-permute-start | bytes 442376 | tf_op jit(solution)/shard_map/ppermute | solution.py:70
  40.6 2.2 %collective-permute-done.13.refs_7_ = bf16[96,768]{1,0:T(8,128)(2,1)S(1)} collective-permute-done((bf16[96,768]{1,0:T(8,128)(2,1)S(1)}, bf16[96,768]{1,0:T(8,128)(2,1)S(1)}, u32[]{:S(2)}, u32[]{:S(2)}) %collective-permute-start.13) | collective-permute-done | bytes 147488 | tf_op jit(solution)/shard_map/ppermute | solution.py:70
  42.8 2.5 %collective-permute-start.16 = (bf16[576,512]{1,0:T(8,128)(2,1)}, bf16[576,512]{1,0:T(8,128)(2,1)S(1)}, u32[]{:S(2)}, u32[]{:S(2)}) collective-permute-start(bf16[576,512]{1,0:T(8,128)(2,1)} %collective-permute-done.12.refs_2_), channel_id=1, source_target_pairs={{0,8},{2,6},{8,16},{10,2},{16,24},{18,10},{24,28},{26,18},{28,20},... | collective-permute-start | bytes 1769480 | tf_op jit(solution)/shard_map/ppermute | solution.py:70
  45.3 1.9 %outward_send.1 = bf16[128,1536]{1,0:T(8,128)(2,1)} custom-call(bf16[256,768]{1,0:T(8,128)(2,1)S(1)} %attend.1.mixed, bf16[192,768]{1,0:T(8,128)(2,1)S(1)} %get-tuple-element.55.refs_0_, bf16[192,768]{1,0:T(8,128)(2,1)S(1)} %collective-permute-done.3.refs_1_, bf16[192,768]{1,0:T(8,128)(2,1)S(1)} %collective-permute-done.5.refs_2_, ...), custom_call_target="tpu_custom_call" | custom-call | flops 1 | bytes 1 | tf_op jit(solution)/shard_map/outward_send/pallas_call | solution.py:381
  47.2 1.5 %collective-permute-start.15 = (bf16[128,1536]{1,0:T(8,128)(2,1)}, bf16[128,1536]{1,0:T(8,128)(2,1)}, u32[]{:S(2)}, u32[]{:S(2)}) collective-permute-start(bf16[128,1536]{1,0:T(8,128)(2,1)} %outward_send.1), channel_id=1, source_target_pairs={{0,1},{1,0},{2,3},{3,2},{4,5},{5,4},{6,7},{7,6},{8,9},{9,8},{10,11... | collective-permute-start | bytes 1179656 | tf_op jit(solution)/shard_map/ppermute | solution.py:635
  49.8 4.7 %all-to-all-start = ((bf16[16,144,128]{2,1,0:T(8,128)(2,1)}), bf16[16,144,128]{2,1,0:T(8,128)(2,1)S(1)}, u32[]{:S(2)}, u32[]{:S(2)}) async-start(bf16[16,144,128]{2,1,0:T(8,128)(2,1)} %bundle.1), calls=%async_computation | async-start | bytes 1179648 | tf_op jit(solution)/shard_map/all_to_all | solution.py:639
  54.5 3.0 %collective-permute-done.15.arrived = bf16[128,1536]{1,0:T(8,128)(2,1)} collective-permute-done((bf16[128,1536]{1,0:T(8,128)(2,1)}, bf16[128,1536]{1,0:T(8,128)(2,1)}, u32[]{:S(2)}, u32[]{:S(2)}) %collective-permute-start.15) | collective-permute-done | bytes 393248 | tf_op jit(solution)/shard_map/ppermute | solution.py:635
  58.2 1.4 %route.1 = (bf16[128,1536]{1,0:T(8,128)(2,1)S(1)}, bf16[128,1536]{1,0:T(8,128)(2,1)S(1)}, bf16[32,1536]{1,0:T(8,128)(2,1)S(1)}) custom-call(bf16[128,1536]{1,0:T(8,128)(2,1)S(1)} %copy-done.1, f32[128,1536]{1,0:T(8,128)S(1)} %outward_keep.1.mine, bf16[128,1536]{1,0:T(8,128)(2,1)} %collective-permute-done.15.arrived, f32[1,1536]{1,0:T(1,128)S(1)} %copy-done.12, ...), custom_call_target="tpu_custom_call" | custom-call | flops 1 | bytes 1 | tf_op jit(solution)/shard_map/route/pallas_call | solution.py:404
  60.4 1.5 %collective-permute-start.17 = (bf16[32,1536]{1,0:T(8,128)(2,1)S(1)}, bf16[32,1536]{1,0:T(8,128)(2,1)S(1)}, u32[]{:S(2)}, u32[]{:S(2)}) collective-permute-start(bf16[32,1536]{1,0:T(8,128)(2,1)S(1)} %get-tuple-element.91), channel_id=1, source_target_pairs={{0,1},{1,0},{2,3},{3,2},{4,5},{5,4},{6,7},{7,6},{8,9},{9,8},{10,11... | collective-permute-start | bytes 294920 | tf_op jit(solution)/shard_map/ppermute | solution.py:642
  62.8 2.2 %collective-permute-done.17.other = bf16[32,1536]{1,0:T(8,128)(2,1)S(1)} collective-permute-done((bf16[32,1536]{1,0:T(8,128)(2,1)S(1)}, bf16[32,1536]{1,0:T(8,128)(2,1)S(1)}, u32[]{:S(2)}, u32[]{:S(2)}) %collective-permute-start.17) | collective-permute-done | bytes 98336 | tf_op jit(solution)/shard_map/ppermute | solution.py:642
  65.1 2.7 %collective-permute-start.21 = (bf16[288,512]{1,0:T(8,128)(2,1)S(1)}, bf16[288,512]{1,0:T(8,128)(2,1)S(1)}, u32[]{:S(2)}, u32[]{:S(2)}) collective-permute-start(bf16[288,512]{1,0:T(8,128)(2,1)S(1)} %slice.7), channel_id=1, source_target_pairs={{0,8},{2,6},{8,16},{10,2},{16,24},{18,10},{24,28},{26,18},{28,20},... | collective-permute-start | bytes 884744 | tf_op jit(solution)/shard_map/ppermute | solution.py:70
  67.8 5.3 %collective-permute-done.21.refs_7_ = bf16[288,512]{1,0:T(8,128)(2,1)S(1)} collective-permute-done((bf16[288,512]{1,0:T(8,128)(2,1)S(1)}, bf16[288,512]{1,0:T(8,128)(2,1)S(1)}, u32[]{:S(2)}, u32[]{:S(2)}) %collective-permute-start.21) | collective-permute-done | bytes 294944 | tf_op jit(solution)/shard_map/ppermute | solution.py:70
  73.1 1.6 %collective-permute-done.22.refs_8_ = bf16[288,512]{1,0:T(8,128)(2,1)S(1)} collective-permute-done((bf16[288,512]{1,0:T(8,128)(2,1)S(1)}, bf16[288,512]{1,0:T(8,128)(2,1)S(1)}, u32[]{:S(2)}, u32[]{:S(2)}) %collective-permute-start.22) | collective-permute-done | bytes 294944 | tf_op jit(solution)/shard_map/ppermute | solution.py:79
  74.7 3.0 %expert.1 = (bf16[32,1536]{1,0:T(8,128)(2,1)S(1)}, bf16[32,1536]{1,0:T(8,128)(2,1)}) custom-call(bf16[32,1536]{1,0:T(8,128)(2,1)S(1)} %get-tuple-element.93.own, bf16[32,1536]{1,0:T(8,128)(2,1)S(1)} %collective-permute-done.17.other, bf16[576,512]{1,0:T(8,128)(2,1)S(1)} %get-tuple-element.72.refs_0_, bf16[576,512]{1,0:T(8,128)(2,1)S(1)} %collective-permute-done.8.refs_1_, ...), custom_call_target="tpu_custom_call" | custom-call | flops 1 | bytes 1 | tf_op jit(solution)/shard_map/expert/pallas_call | solution.py:467
  77.7 1.2 %collective-permute-start.23 = (bf16[32,1536]{1,0:T(8,128)(2,1)}, bf16[32,1536]{1,0:T(8,128)(2,1)S(1)}, u32[]{:S(2)}, u32[]{:S(2)}) collective-permute-start(bf16[32,1536]{1,0:T(8,128)(2,1)} %get-tuple-element.97), channel_id=1, source_target_pairs={{0,1},{1,0},{2,3},{3,2},{4,5},{5,4},{6,7},{7,6},{8,9},{9,8},{10,11... | collective-permute-start | bytes 294920 | tf_op jit(solution)/shard_map/ppermute | solution.py:651
  78.9 3.3 %write.1 = bf16[512,4,128]{2,1,0:T(4,128)(2,1)} custom-call(bf16[16,144,128]{2,1,0:T(8,128)(2,1)S(1)} %all-to-all-done.arrived, bf16[512,4,128]{2,1,0:T(4,128)(2,1)S(1)} %copy-done.2), custom_call_target="tpu_custom_call" | custom-call | flops 1 | bytes 1 | tf_op jit(solution)/shard_map/write/pallas_call | solution.py:565
  82.7 1.1 %combine.1 = bf16[128,1536]{1,0:T(8,128)(2,1)} custom-call(bf16[128,1536]{1,0:T(8,128)(2,1)S(1)} %copy-done.4, f32[128,40]{1,0:T(8,128)S(1)} %get-tuple-element.88.gates, bf16[128,64]{1,0:T(8,128)(2,1)S(1)} %copy-done.10, bf16[32,1536]{1,0:T(8,128)(2,1)S(1)} %get-tuple-element.96.own, bf16[32,1536]{1,0:T(8,128)(2,1)S(1)} %collective-permute-done.23.returned), custom_call_target="tpu_custom_call" | custom-call | flops 1 | bytes 1 | tf_op jit(solution)/shard_map/combine/pallas_call | solution.py:499
  (65 shorter events, 7.6 us)
Async XLA Ops:
  0.6 5.5 %collective-permute-start.2 = (bf16[96,1536]{1,0:T(8,128)(2,1)}, bf16[96,1536]{1,0:T(8,128)(2,1)S(1)}, u32[]{:S(2)}, u32[]{:S(2)}) collective-permute-start(bf16[96,1536]{1,0:T(8,128)(2,1)} %bitcast.13), channel_id=1, source_target_pairs={{0,2},{2,0},{4,6},{6,4},{8,10},{10,8},{12,14},{14,12},{16,18},{18,... | collective-permute-start | bytes 884744 | tf_op jit(solution)/shard_map/ppermute | solution.py:605
  1.1 4.9 %collective-permute-start = (bf16[96,1024]{1,0:T(8,128)(2,1)}, bf16[96,1024]{1,0:T(8,128)(2,1)S(1)}, u32[]{:S(2)}, u32[]{:S(2)}) collective-permute-start(bf16[96,1024]{1,0:T(8,128)(2,1)} %bitcast.15), channel_id=1, source_target_pairs={{0,2},{2,0},{4,6},{6,4},{8,10},{10,8},{12,14},{14,12},{16,18},{18,... | collective-permute-start | bytes 589832 | tf_op jit(solution)/shard_map/ppermute | solution.py:605
  1.2 4.8 %collective-permute-start.1 = (bf16[32,1536]{1,0:T(8,128)(2,1)}, bf16[32,1536]{1,0:T(8,128)(2,1)S(1)}, u32[]{:S(2)}, u32[]{:S(2)}) collective-permute-start(bf16[32,1536]{1,0:T(8,128)(2,1)} %bitcast.18), channel_id=1, source_target_pairs={{0,2},{2,0},{4,6},{6,4},{8,10},{10,8},{12,14},{14,12},{16,18},{18,... | collective-permute-start | bytes 294920 | tf_op jit(solution)/shard_map/ppermute | solution.py:605
  1.7 12.5 %collective-permute-start.4 = (bf16[128,1536]{1,0:T(8,128)(2,1)}, bf16[128,1536]{1,0:T(8,128)(2,1)S(1)}, u32[]{:S(2)}, u32[]{:S(2)}) collective-permute-start(bf16[128,1536]{1,0:T(8,128)(2,1)} %tokens.1), channel_id=1, source_target_pairs={{0,1},{1,0},{2,3},{3,2},{4,5},{5,4},{6,7},{7,6},{8,9},{9,8},{10,11... | collective-permute-start | bytes 1179656 | tf_op jit(solution)/shard_map/ppermute | solution.py:602
  4.2 6.2 %copy-start.13 = (f32[1536]{0:T(1024)S(1)}, f32[1536]{0:T(1024)}, u32[]{:S(2)}) copy-start(f32[1536]{0:T(1024)} %param.15) | copy-start | bytes 18436
  4.2 6.8 %copy-start.14 = (f32[1536]{0:T(1024)S(1)}, f32[1536]{0:T(1024)}, u32[]{:S(2)}) copy-start(f32[1536]{0:T(1024)} %param.19) | copy-start | bytes 18436
  4.2 11.8 %copy-start = (bf16[1536,768]{1,0:T(8,128)(2,1)S(1)}, bf16[1536,768]{1,0:T(8,128)(2,1)}, u32[]{:S(2)}) copy-start(bf16[1536,768]{1,0:T(8,128)(2,1)} %w_query.1) | copy-start | bytes 7077892
  4.2 11.8 %copy-start.1 = (bf16[128,1536]{1,0:T(8,128)(2,1)S(1)}, bf16[128,1536]{1,0:T(8,128)(2,1)}, u32[]{:S(2)}) copy-start(bf16[128,1536]{1,0:T(8,128)(2,1)} %tokens.1) | copy-start | bytes 1179652
  7.3 6.9 %collective-permute-start.3 = (bf16[192,768]{1,0:T(8,128)(2,1)S(1)}, bf16[192,768]{1,0:T(8,128)(2,1)S(1)}, u32[]{:S(2)}, u32[]{:S(2)}) collective-permute-start(bf16[192,768]{1,0:T(8,128)(2,1)S(1)} %get-tuple-element.55.refs_0_), channel_id=1, source_target_pairs={{0,8},{2,6},{8,16},{10,2},{16,24},{18,10},{24,28},{26,18},{28,20},... | collective-permute-start | bytes 884744 | tf_op jit(solution)/shard_map/ppermute | solution.py:70
  8.9 14.6 %collective-permute-start.8 = (bf16[576,512]{1,0:T(8,128)(2,1)S(1)}, bf16[576,512]{1,0:T(8,128)(2,1)S(1)}, u32[]{:S(2)}, u32[]{:S(2)}) collective-permute-start(bf16[576,512]{1,0:T(8,128)(2,1)S(1)} %get-tuple-element.72.refs_0_), channel_id=1, source_target_pairs={{0,8},{2,6},{8,16},{10,2},{16,24},{18,10},{24,28},{26,18},{28,20},... | collective-permute-start | bytes 1769480 | tf_op jit(solution)/shard_map/ppermute | solution.py:70
  14.1 9.4 %collective-permute-start.5 = (bf16[192,768]{1,0:T(8,128)(2,1)S(1)}, bf16[192,768]{1,0:T(8,128)(2,1)S(1)}, u32[]{:S(2)}, u32[]{:S(2)}) collective-permute-start(bf16[192,768]{1,0:T(8,128)(2,1)S(1)} %collective-permute-done.3.refs_1_), channel_id=1, source_target_pairs={{0,8},{2,6},{8,16},{10,2},{16,24},{18,10},{24,28},{26,18},{28,20},... | collective-permute-start | bytes 884744 | tf_op jit(solution)/shard_map/ppermute | solution.py:70
  18.2 5.3 %collective-permute-start.7 = (bf16[128,512]{1,0:T(8,128)(2,1)S(1)}, bf16[128,512]{1,0:T(8,128)(2,1)S(1)}, u32[]{:S(2)}, u32[]{:S(2)}) collective-permute-start(bf16[128,512]{1,0:T(8,128)(2,1)S(1)} %get-tuple-element.69), channel_id=1, source_target_pairs={{0,2},{2,4},{4,6},{6,8},{8,10},{10,12},{12,14},{14,16},{16,18},{18... | collective-permute-start | bytes 393224 | tf_op jit(solution)/shard_map/ppermute | solution.py:621
  23.5 19.3 %collective-permute-start.12 = (bf16[576,512]{1,0:T(8,128)(2,1)S(1)}, bf16[576,512]{1,0:T(8,128)(2,1)}, u32[]{:S(2)}, u32[]{:S(2)}) collective-permute-start(bf16[576,512]{1,0:T(8,128)(2,1)S(1)} %collective-permute-done.8.refs_1_), channel_id=1, source_target_pairs={{0,8},{2,6},{8,16},{10,2},{16,24},{18,10},{24,28},{26,18},{28,20},... | collective-permute-start | bytes 1769480 | tf_op jit(solution)/shard_map/ppermute | solution.py:70
  27.0 10.6 %collective-permute-start.6 = (bf16[192,768]{1,0:T(8,128)(2,1)S(1)}, bf16[192,768]{1,0:T(8,128)(2,1)S(1)}, u32[]{:S(2)}, u32[]{:S(2)}) collective-permute-start(bf16[192,768]{1,0:T(8,128)(2,1)S(1)} %collective-permute-done.5.refs_2_), channel_id=1, source_target_pairs={{0,8},{2,6},{8,16},{10,2},{16,24},{18,10},{24,28},{26,18},{28,20},... | collective-permute-start | bytes 884744 | tf_op jit(solution)/shard_map/ppermute | solution.py:70
  37.6 5.2 %collective-permute-start.13 = (bf16[96,768]{1,0:T(8,128)(2,1)S(1)}, bf16[96,768]{1,0:T(8,128)(2,1)S(1)}, u32[]{:S(2)}, u32[]{:S(2)}) collective-permute-start(bf16[96,768]{1,0:T(8,128)(2,1)S(1)} %slice.6), channel_id=1, source_target_pairs={{0,8},{2,6},{8,16},{10,2},{16,24},{18,10},{24,28},{26,18},{28,20},... | collective-permute-start | bytes 442376 | tf_op jit(solution)/shard_map/ppermute | solution.py:70
  40.1 5.2 %collective-permute-start.9 = (bf16[192,768]{1,0:T(8,128)(2,1)S(1)}, bf16[192,768]{1,0:T(8,128)(2,1)S(1)}, u32[]{:S(2)}, u32[]{:S(2)}) collective-permute-start(bf16[192,768]{1,0:T(8,128)(2,1)S(1)} %collective-permute-done.3.refs_1_), channel_id=1, source_target_pairs={{0,2},{2,0},{4,6},{6,4},{8,10},{10,8},{12,14},{14,12},{16,18},{18,... | collective-permute-start | bytes 884744 | tf_op jit(solution)/shard_map/ppermute | solution.py:79
  40.1 5.2 %collective-permute-start.10 = (bf16[192,768]{1,0:T(8,128)(2,1)S(1)}, bf16[192,768]{1,0:T(8,128)(2,1)S(1)}, u32[]{:S(2)}, u32[]{:S(2)}) collective-permute-start(bf16[192,768]{1,0:T(8,128)(2,1)S(1)} %collective-permute-done.5.refs_2_), channel_id=1, source_target_pairs={{0,2},{2,0},{4,6},{6,4},{8,10},{10,8},{12,14},{14,12},{16,18},{18,... | collective-permute-start | bytes 884744 | tf_op jit(solution)/shard_map/ppermute | solution.py:79
  40.6 4.6 %collective-permute-start.11 = (bf16[192,768]{1,0:T(8,128)(2,1)S(1)}, bf16[192,768]{1,0:T(8,128)(2,1)S(1)}, u32[]{:S(2)}, u32[]{:S(2)}) collective-permute-start(bf16[192,768]{1,0:T(8,128)(2,1)S(1)} %collective-permute-done.6.refs_3_), channel_id=1, source_target_pairs={{0,2},{2,0},{4,6},{6,4},{8,10},{10,8},{12,14},{14,12},{16,18},{18,... | collective-permute-start | bytes 884744 | tf_op jit(solution)/shard_map/ppermute | solution.py:79
  42.8 2.5 %collective-permute-start.14 = (bf16[96,768]{1,0:T(8,128)(2,1)S(1)}, bf16[96,768]{1,0:T(8,128)(2,1)S(1)}, u32[]{:S(2)}, u32[]{:S(2)}) collective-permute-start(bf16[96,768]{1,0:T(8,128)(2,1)S(1)} %collective-permute-done.13.refs_7_), channel_id=1, source_target_pairs={{0,2},{2,0},{4,6},{6,4},{8,10},{10,8},{12,14},{14,12},{16,18},{18,... | collective-permute-start | bytes 442376 | tf_op jit(solution)/shard_map/ppermute | solution.py:79
  42.8 20.0 %collective-permute-start.16 = (bf16[576,512]{1,0:T(8,128)(2,1)}, bf16[576,512]{1,0:T(8,128)(2,1)S(1)}, u32[]{:S(2)}, u32[]{:S(2)}) collective-permute-start(bf16[576,512]{1,0:T(8,128)(2,1)} %collective-permute-done.12.refs_2_), channel_id=1, source_target_pairs={{0,8},{2,6},{8,16},{10,2},{16,24},{18,10},{24,28},{26,18},{28,20},... | collective-permute-start | bytes 1769480 | tf_op jit(solution)/shard_map/ppermute | solution.py:70
  47.2 10.3 %collective-permute-start.15 = (bf16[128,1536]{1,0:T(8,128)(2,1)}, bf16[128,1536]{1,0:T(8,128)(2,1)}, u32[]{:S(2)}, u32[]{:S(2)}) collective-permute-start(bf16[128,1536]{1,0:T(8,128)(2,1)} %outward_send.1), channel_id=1, source_target_pairs={{0,1},{1,0},{2,3},{3,2},{4,5},{5,4},{6,7},{7,6},{8,9},{9,8},{10,11... | collective-permute-start | bytes 1179656 | tf_op jit(solution)/shard_map/ppermute | solution.py:635
  49.8 29.0 %all-to-all-start = ((bf16[16,144,128]{2,1,0:T(8,128)(2,1)}), bf16[16,144,128]{2,1,0:T(8,128)(2,1)S(1)}, u32[]{:S(2)}, u32[]{:S(2)}) async-start(bf16[16,144,128]{2,1,0:T(8,128)(2,1)} %bundle.1), calls=%async_computation | async-start | bytes 1179648 | tf_op jit(solution)/shard_map/all_to_all | solution.py:639
  54.5 7.9 %copy-start.6 = (bf16[40,1536]{1,0:T(8,128)(2,1)S(1)}, bf16[40,1536]{1,0:T(8,128)(2,1)}, u32[]{:S(2)}) copy-start(bf16[40,1536]{1,0:T(8,128)(2,1)} %copy-done.5) | copy-start | bytes 368644
  54.5 7.9 %copy-start.8 = (f32[128,40]{1,0:T(8,128)S(1)}, f32[128,40]{1,0:T(8,128)}, u32[]{:S(2)}) copy-start(f32[128,40]{1,0:T(8,128)} %copy-done.7) | copy-start | bytes 61444
  60.4 4.6 %collective-permute-start.17 = (bf16[32,1536]{1,0:T(8,128)(2,1)S(1)}, bf16[32,1536]{1,0:T(8,128)(2,1)S(1)}, u32[]{:S(2)}, u32[]{:S(2)}) collective-permute-start(bf16[32,1536]{1,0:T(8,128)(2,1)S(1)} %get-tuple-element.91), channel_id=1, source_target_pairs={{0,1},{1,0},{2,3},{3,2},{4,5},{5,4},{6,7},{7,6},{8,9},{9,8},{10,11... | collective-permute-start | bytes 294920 | tf_op jit(solution)/shard_map/ppermute | solution.py:642
  61.9 11.2 %collective-permute-start.18 = (bf16[576,512]{1,0:T(8,128)(2,1)S(1)}, bf16[576,512]{1,0:T(8,128)(2,1)S(1)}, u32[]{:S(2)}, u32[]{:S(2)}) collective-permute-start(bf16[576,512]{1,0:T(8,128)(2,1)S(1)} %collective-permute-done.8.refs_1_), channel_id=1, source_target_pairs={{0,2},{2,0},{4,6},{6,4},{8,10},{10,8},{12,14},{14,12},{16,18},{18,... | collective-permute-start | bytes 1769480 | tf_op jit(solution)/shard_map/ppermute | solution.py:79
  61.9 11.2 %collective-permute-start.19 = (bf16[576,512]{1,0:T(8,128)(2,1)}, bf16[576,512]{1,0:T(8,128)(2,1)S(1)}, u32[]{:S(2)}, u32[]{:S(2)}) collective-permute-start(bf16[576,512]{1,0:T(8,128)(2,1)} %collective-permute-done.12.refs_2_), channel_id=1, source_target_pairs={{0,2},{2,0},{4,6},{6,4},{8,10},{10,8},{12,14},{14,12},{16,18},{18,... | collective-permute-start | bytes 1769480 | tf_op jit(solution)/shard_map/ppermute | solution.py:79
  65.1 13.8 %copy-start.2 = (bf16[512,4,128]{2,1,0:T(4,128)(2,1)S(1)}, bf16[512,4,128]{2,1,0:T(4,128)(2,1)}, u32[]{:S(2)}) copy-start(bf16[512,4,128]{2,1,0:T(4,128)(2,1)} %cache.1) | copy-start | bytes 1572868
  65.1 8.0 %collective-permute-start.21 = (bf16[288,512]{1,0:T(8,128)(2,1)S(1)}, bf16[288,512]{1,0:T(8,128)(2,1)S(1)}, u32[]{:S(2)}, u32[]{:S(2)}) collective-permute-start(bf16[288,512]{1,0:T(8,128)(2,1)S(1)} %slice.7), channel_id=1, source_target_pairs={{0,8},{2,6},{8,16},{10,2},{16,24},{18,10},{24,28},{26,18},{28,20},... | collective-permute-start | bytes 884744 | tf_op jit(solution)/shard_map/ppermute | solution.py:70
  67.8 6.9 %collective-permute-start.20 = (bf16[576,512]{1,0:T(8,128)(2,1)S(1)}, bf16[576,512]{1,0:T(8,128)(2,1)S(1)}, u32[]{:S(2)}, u32[]{:S(2)}) collective-permute-start(bf16[576,512]{1,0:T(8,128)(2,1)S(1)} %collective-permute-done.16.refs_3_), channel_id=1, source_target_pairs={{0,2},{2,0},{4,6},{6,4},{8,10},{10,8},{12,14},{14,12},{16,18},{18,... | collective-permute-start | bytes 1769480 | tf_op jit(solution)/shard_map/ppermute | solution.py:79
  73.1 1.6 %collective-permute-start.22 = (bf16[288,512]{1,0:T(8,128)(2,1)S(1)}, bf16[288,512]{1,0:T(8,128)(2,1)S(1)}, u32[]{:S(2)}, u32[]{:S(2)}) collective-permute-start(bf16[288,512]{1,0:T(8,128)(2,1)S(1)} %collective-permute-done.21.refs_7_), channel_id=1, source_target_pairs={{0,2},{2,0},{4,6},{6,4},{8,10},{10,8},{12,14},{14,12},{16,18},{18,... | collective-permute-start | bytes 884744 | tf_op jit(solution)/shard_map/ppermute | solution.py:79
  77.7 5.0 %collective-permute-start.23 = (bf16[32,1536]{1,0:T(8,128)(2,1)}, bf16[32,1536]{1,0:T(8,128)(2,1)S(1)}, u32[]{:S(2)}, u32[]{:S(2)}) collective-permute-start(bf16[32,1536]{1,0:T(8,128)(2,1)} %get-tuple-element.97), channel_id=1, source_target_pairs={{0,1},{1,0},{2,3},{3,2},{4,5},{5,4},{6,7},{7,6},{8,9},{9,8},{10,11... | collective-permute-start | bytes 294920 | tf_op jit(solution)/shard_map/ppermute | solution.py:651
  (8 other events, 24.6 us)

commit v5 on v4

--- a/solution.py
+++ b/solution.py
@@ -102,6 +102,14 @@
 
 
 LITTLE = pl.CostEstimate(flops=1, bytes_accessed=1, transcendentals=0)
+
+
+def takes(us):
+    return pl.CostEstimate(flops=int(us * 1.15e9), bytes_accessed=1, transcendentals=0)
+
+
+def reads(nbytes):
+    return pl.CostEstimate(flops=1, bytes_accessed=nbytes, transcendentals=0)
 
 
 def normalized(floats, gain):
@@ -170,10 +178,12 @@
         refs[:6],
         refs[6:17],
     )
-    positions, slots, ids, sems = refs[17:]
-    copies = fetch(list(zip(sources, (positions, slots, ids, gain, late_gain, router))), sems)
+    positions, slots, ids, flat_gains, flat_late, sems = refs[17:]
+    copies = fetch(list(zip(sources, (positions, slots, ids, flat_gains, flat_late, router))), sems)
     for copy in copies:
         copy.wait()
+    gain[...] = flat_gains[...].reshape(gain.shape)
+    late_gain[...] = flat_late[...].reshape(late_gain.shape)
     lane = lax.axis_index("hd")
     block = positions.shape[1]
 
@@ -245,7 +255,7 @@
         ((1, model), f32),
         ((experts, model), bf16),
     ]
-    sources = (positions[None], slots[None], ids.T, gain[None], late_gain[None], router.T)
+    sources = (positions[None], slots[None], ids.T, gain, late_gain, router.T)
     return pl.pallas_call(
         functools.partial(prepare_kernel, groups, slots_dev),
         out_shape=tuple(jax.ShapeDtypeStruct(shape, kind) for shape, kind in shapes),
@@ -255,6 +265,8 @@
             pltpu.VMEM((1, block), jnp.int32),
             pltpu.VMEM((1, block), jnp.int32),
             pltpu.VMEM(ids.shape[::-1], jnp.int32),
+            pltpu.VMEM((model,), f32),
+            pltpu.VMEM((model,), f32),
             pltpu.SemaphoreType.DMA((6,)),
         ],
         compiler_params=PARAMS,
@@ -310,7 +322,7 @@
             pltpu.SemaphoreType.DMA((2,)),
         ],
         compiler_params=PARAMS,
-        cost_estimate=LITTLE,
+        cost_estimate=takes(6),
         name="project",
     )(own, other, gain, cosine, sine, w_query, flat_kv)
 
@@ -358,7 +370,7 @@
             pltpu.SemaphoreType.DMA,
         ],
         compiler_params=PARAMS,
-        cost_estimate=LITTLE,
+        cost_estimate=takes(4),
         name="attend",
     )(q, kv, seam, past)
 
@@ -385,7 +397,7 @@
         out_specs=VMEM,
         scratch_shapes=[pltpu.VMEM((width, depth), bf16)],
         compiler_params=PARAMS,
-        cost_estimate=LITTLE,
+        cost_estimate=reads(2 * width * depth),
         name="outward_send" if flip else "outward_keep",
     )(mixed, *parts)
 
@@ -411,7 +423,7 @@
         in_specs=[VMEM] * 5,
         out_specs=(VMEM,) * 3,
         compiler_params=PARAMS,
-        cost_estimate=LITTLE,
+        cost_estimate=reads(10 * tokens.shape[0] * tokens.shape[1]),
         name="route",
     )(tokens, mine, arrived, gain, place)
 
@@ -435,7 +447,7 @@
         in_specs=[VMEM] * 4,
         out_specs=(VMEM,) * 2,
         compiler_params=PARAMS,
-        cost_estimate=LITTLE,
+        cost_estimate=reads(1 << 20),
         name="gate",
     )(moe_in, router_t, named, place)
 
@@ -475,7 +487,7 @@
             pltpu.VMEM((groups * down_rows, model), bf16),
         ],
         compiler_params=PARAMS,
-        cost_estimate=LITTLE,
+        cost_estimate=reads(2 * groups * 2 * (up_rows * 2 * width + down_rows * model)),
         name="expert",
     )(own, other, *parts)
 
@@ -502,7 +514,7 @@
         in_specs=[VMEM] * 5,
         out_specs=VMEM,
         compiler_params=PARAMS,
-        cost_estimate=LITTLE,
+        cost_estimate=reads(6 * residual.shape[0] * residual.shape[1]),
         name="combine",
     )(residual, gates, spread, own, returned)
 
@@ -532,7 +544,7 @@
         in_specs=[VMEM] * 3,
         out_specs=VMEM,
         compiler_params=PARAMS,
-        cost_estimate=LITTLE,
+        cost_estimate=takes(2),
         name="bundle",
     )(send, kv, tags)
 
@@ -569,7 +581,7 @@
         out_specs=VMEM,
         scratch_shapes=[pltpu.VMEM((arrived.shape[0] * capc, heads * lanes), bf16)],
         compiler_params=PARAMS,
-        cost_estimate=LITTLE,
+        cost_estimate=reads(1 << 21),
         name="write",
     )(arrived, cache)
 
@@ -604,27 +616,25 @@
     up_rows, down_rows = own[0].shape[0], own[1].shape[0]
     beside = [lax.ppermute(part, "grp", sibling_pairs(groups)) for part in own]
     flat_kv = w_keyval.reshape(model, kv_width)
-    beside, flat_kv = together((beside, flat_kv))
+    cosine, sine, past, named, place, spread, send, tags, gain, late_gain, router_t = prepare(
+        groups, slots_dev, positions, cache_slot, expert_ids, attn_gain, moe_gain, router
+    )
+    beside, cosine, flat_kv = together((beside, cosine, flat_kv))
     expert_pair, out_pair = pack(own, beside)
     out_ring = Ring(out_pair, groups)
     out_ring.step()
     expert_ring = Ring(expert_pair, groups)
     expert_ring.step()
-    positions = together((positions, out_pair))[0]
-    cosine, sine, past, named, place, spread, send, tags, gain, late_gain, router_t = prepare(
-        groups, slots_dev, positions, cache_slot, expert_ids, attn_gain, moe_gain, router
-    )
-    other_tokens, cosine = out_ring.pin(other_tokens, cosine)
+    other_tokens = out_ring.pin(other_tokens)
     out_ring.step()
 
     q, kv, tail = project(tokens, other_tokens, gain, cosine, sine, w_query, flat_kv)
     seam = lax.ppermute(tail, "grp", [(g, g + 1) for g in range(groups - 1)])
-    outgoing = bundle(groups, send, kv, tags)
-    outgoing = out_ring.pin(outgoing)
+    kv_now = expert_ring.pin(kv)
+    expert_ring.step()
+    outgoing = bundle(groups, send, kv_now, tags)
+    seam, outgoing = out_ring.pin(seam, outgoing)
     out_ring.step()
-    seam, q = together((seam, q, outgoing))[:2]
-    seam = expert_ring.pin(seam)
-    expert_ring.step()
     mixed = attend(q, kv, seam, past)
     mixed = out_ring.pin(mixed)
     out_ring.step()
@@ -635,15 +645,16 @@
     arrived = swap(sent)
     mixed = together((mixed, sent))[0]
     mine = outward(False, f32, groups, mixed, out_ring.parts(), out_ring.unit_rows)
+    mine = expert_ring.pin(mine)
+    expert_ring.share()
+    expert_ring.step()
     outgoing, mine = together((outgoing, mine))
     arrived_cache = lax.all_to_all(outgoing, "grp", split_axis=0, concat_axis=0, tiled=True)
 
     residual, moe_in, sent_rows = route(tokens, mine, arrived, late_gain, place)
     landed = swap(sent_rows)
     gates, own_rows = gate(moe_in, router_t, named, place)
-    landed, own_rows = expert_ring.pin(landed, own_rows)
-    expert_ring.share()
-    expert_ring.step()
+    own_rows = expert_ring.pin(own_rows)
     expert_ring.share()
     own_made, back = expert(
         groups, own_rows, landed, expert_ring.parts(), up_rows, down_rows

time: 84.3 us -> 88.3 us (1.047)
  the two profiles are of different devices: /device:TPU:0 before, /device:TPU:12 now
where the time goes in v5:
time: 88.3 us; the launch traced here: 87.9 us
  waiting for transfers between devices  44.4 us (50%)
  starting transfers between devices  19.7 us (22%)
  Pallas kernels  17.9 us (20%)
  local copies, waits for them, and re-layouts  4.89 us (6%)
    ppermute x8, waiting for transfers between devices, step(): self.mine.append(self.across(held))  23.2 us
    ppermute x1, waiting for transfers between devices, two_lane_shards(): arrived = swap(sent)  8.81 us
    all_to_all x1, starting transfers between devices, two_lane_shards(): lax.all_to_all(outgoing, 'grp', split_axis=0, concat_axis=0, tiled=True)  7.13 us
    unnamed x31, local copies, waits for them, and re-layouts  4.86 us
    ppermute x8, starting transfers between devices, step(): self.mine.append(self.across(held))  4.7 us
    ppermute x1, waiting for transfers between devices, two_lane_shards(): landed = swap(sent_rows)  4.67 us
    ppermute x1, waiting for transfers between devices, two_lane_shards(): other_tokens = swap(tokens)  4.3 us
    pallas_call x1, Pallas kernels, write(): pl.pallas_call(write_kernel, out_shape=jax.ShapeDtypeStruct(cache.shape,...  3.27 us
  transfers between devices with their start and end apart: 25, of which 16 were waited for; matrix products, arithmetic and copies ran while one was open for 2% of the time, Pallas kernels for 19%

profile of v5, /device:TPU:12, one launch (start us, length us, event | category | flops | bytes accessed | tf_op | source)
XLA Modules:
  0.0 87.9 jit_solution(8281320698169046335)
XLA Ops:
  1.3 1.5 %collective-permute-start.4 = (bf16[128,1536]{1,0:T(8,128)(2,1)}, bf16[128,1536]{1,0:T(8,128)(2,1)S(1)}, u32[]{:S(2)}, u32[]{:S(2)}) collective-permute-start(bf16[128,1536]{1,0:T(8,128)(2,1)} %tokens.1), channel_id=1, source_target_pairs={{0,1},{1,0},{2,3},{3,2},{4,5},{5,4},{6,7},{7,6},{8,9},{9,8},{10,11... | collective-permute-start | bytes 1179656 | tf_op jit(solution)/shard_map/ppermute | solution.py:614
  2.8 1.7 %prepare.1 = (f32[256,128]{1,0:T(8,128)S(1)}, f32[256,128]{1,0:T(8,128)S(1)}, f32[256,128]{1,0:T(8,128)S(1)}, f32[128,40]{1,0:T(8,128)S(1)}, bf16[64,128]{1,0:T(...) custom-call(s32[1,256]{1,0:T(1,128)} %bitcast.21, ...), custom_call_target="tpu_custom_call" | custom-call | flops 1 | bytes 1 | tf_op jit(solution)/shard_map/prepare/pallas_call | solution.py:259
  4.6 1.8 %copy.17 = bf16[192,8,4,128]{3,1,2,0:T(8,128)(2,1)S(1)} copy(bf16[192,8,4,128]{3,2,1,0:T(4,128)(2,1)} %bitcast.12) | data formatting | bytes 3145728
  6.5 1.1 %pack.1 = (bf16[576,512]{1,0:T(8,128)(2,1)S(1)}, bf16[192,768]{1,0:T(8,128)(2,1)S(1)}) custom-call(bf16[96,1024]{1,0:T(8,128)(2,1)} %bitcast.16, bf16[32,1536]{1,0:T(8,128)(2,1)} %bitcast.19, bf16[96,1536]{1,0:T(8,128)(2,1)} %bitcast.14, bf16[96,1024]{1,0:T(8,128)(2,1)S(1)} %collective-permute-done.refs_3_, ...), custom_call_target="tpu_custom_call" | custom-call | flops 1 | bytes 1 | tf_op jit(solution)/shard_map/pack/pallas_call | solution.py:157
  8.7 4.3 %collective-permute-done.4.other = bf16[128,1536]{1,0:T(8,128)(2,1)S(1)} collective-permute-done((bf16[128,1536]{1,0:T(8,128)(2,1)}, bf16[128,1536]{1,0:T(8,128)(2,1)S(1)}, u32[]{:S(2)}, u32[]{:S(2)}) %collective-permute-start.4) | collective-permute-done | bytes 393248 | tf_op jit(solution)/shard_map/ppermute | solution.py:614
  13.0 1.5 %collective-permute-done.3.refs_1_ = bf16[192,768]{1,0:T(8,128)(2,1)S(1)} collective-permute-done((bf16[192,768]{1,0:T(8,128)(2,1)S(1)}, bf16[192,768]{1,0:T(8,128)(2,1)S(1)}, u32[]{:S(2)}, u32[]{:S(2)}) %collective-permute-start.3) | collective-permute-done | bytes 294944 | tf_op jit(solution)/shard_map/ppermute | solution.py:70
  14.9 2.2 %project.1 = (bf16[256,768]{1,0:T(8,128)(2,1)S(1)}, bf16[256,512]{1,0:T(8,128)(2,1)S(1)}, bf16[128,512]{1,0:T(8,128)(2,1)S(1)}) custom-call(bf16[128,1536]{1,0:T(8,128)(2,1)S(1)} %copy-done.4, bf16[128,1536]{1,0:T(8,128)(2,1)S(1)} %collective-permute-done.4.other, f32[1,1536]{1,0:T(1,128)S(1)} %get-tuple-element.58.gain, ...), custom_call_target="tpu_custom_call" | custom-call | flops 6899999744 | bytes 1 | tf_op jit(solution)/shard_map/project/pallas_call | solution.py:310
  17.1 2.1 %collective-permute-start.6 = (bf16[128,512]{1,0:T(8,128)(2,1)S(1)}, bf16[128,512]{1,0:T(8,128)(2,1)S(1)}, u32[]{:S(2)}, u32[]{:S(2)}) collective-permute-start(bf16[128,512]{1,0:T(8,128)(2,1)S(1)} %get-tuple-element.62), channel_id=1, source_target_pairs={{0,2},{2,4},{4,6},{6,8},{8,10},{10,12},{12,14},{14,16},{16,18},{18... | collective-permute-start | bytes 393224 | tf_op jit(solution)/shard_map/ppermute | solution.py:632
  19.1 1.6 %collective-permute-done.7.refs_1_ = bf16[576,512]{1,0:T(8,128)(2,1)S(1)} collective-permute-done((bf16[576,512]{1,0:T(8,128)(2,1)S(1)}, bf16[576,512]{1,0:T(8,128)(2,1)S(1)}, u32[]{:S(2)}, u32[]{:S(2)}) %collective-permute-start.7) | collective-permute-done | bytes 589856 | tf_op jit(solution)/shard_map/ppermute | solution.py:70
  21.7 0.8 copy-done.2
  22.6 0.8 collective-permute-done.6.seam
  23.4 0.6 collective-permute-done.5.refs_2_
  23.9 1.1 %collective-permute-start.9 = (bf16[192,768]{1,0:T(8,128)(2,1)S(1)}, bf16[192,768]{1,0:T(8,128)(2,1)S(1)}, u32[]{:S(2)}, u32[]{:S(2)}) collective-permute-start(bf16[192,768]{1,0:T(8,128)(2,1)S(1)} %collective-permute-done.5.refs_2_), channel_id=1, source_target_pairs={{0,8},{2,6},{8,16},{10,2},{16,24},{18,10},{24,28},{26,18},{28,20},... | collective-permute-start | bytes 884744 | tf_op jit(solution)/shard_map/ppermute | solution.py:70
  25.0 2.8 %attend.1.mixed = bf16[256,768]{1,0:T(8,128)(2,1)S(1)} custom-call(bf16[256,768]{1,0:T(8,128)(2,1)S(1)} %get-tuple-element.71.q, bf16[256,512]{1,0:T(8,128)(2,1)S(1)} %get-tuple-element.66.kv, bf16[128,512]{1,0:T(8,128)(2,1)S(1)} %collective-permute-done.6.seam, f32[256,128]{1,0:T(8,128)S(1)} %get-tuple-element.73.past), custom_call_target="tpu_custom_call" | custom-call | flops 4600000000 | bytes 1 | tf_op jit(solution)/shard_map/attend/pallas_call | solution.py:363
  27.8 6.0 %collective-permute-done.9.refs_3_ = bf16[192,768]{1,0:T(8,128)(2,1)S(1)} collective-permute-done((bf16[192,768]{1,0:T(8,128)(2,1)S(1)}, bf16[192,768]{1,0:T(8,128)(2,1)S(1)}, u32[]{:S(2)}, u32[]{:S(2)}) %collective-permute-start.9) | collective-permute-done | bytes 294944 | tf_op jit(solution)/shard_map/ppermute | solution.py:70
  34.3 4.7 %collective-permute-done.10.refs_7_ = bf16[96,768]{1,0:T(8,128)(2,1)S(1)} collective-permute-done((bf16[96,768]{1,0:T(8,128)(2,1)S(1)}, bf16[96,768]{1,0:T(8,128)(2,1)S(1)}, u32[]{:S(2)}, u32[]{:S(2)}) %collective-permute-start.10) | collective-permute-done | bytes 147488 | tf_op jit(solution)/shard_map/ppermute | solution.py:70
  40.5 0.6 collective-permute-done.12.refs_4_
  42.1 1.1 %outward_send.1 = bf16[128,1536]{1,0:T(8,128)(2,1)S(1)} custom-call(bf16[256,768]{1,0:T(8,128)(2,1)S(1)} %attend.1.mixed, bf16[192,768]{1,0:T(8,128)(2,1)S(1)} %get-tuple-element.55.refs_0_, bf16[192,768]{1,0:T(8,128)(2,1)S(1)} %collective-permute-done.3.refs_1_, bf16[192,768]{1,0:T(8,128)(2,1)S(1)} %collective-permute-done.5.refs_2_, ...), custom_call_target="tpu_custom_call" | custom-call | flops 1 | bytes 2359296 | tf_op jit(solution)/shard_map/outward_send/pallas_call | solution.py:393
  43.3 1.1 %outward_keep.1.mine = f32[128,1536]{1,0:T(8,128)S(1)} custom-call(bf16[256,768]{1,0:T(8,128)(2,1)S(1)} %attend.1.mixed, bf16[192,768]{1,0:T(8,128)(2,1)S(1)} %get-tuple-element.55.refs_0_, bf16[192,768]{1,0:T(8,128)(2,1)S(1)} %collective-permute-done.3.refs_1_, bf16[192,768]{1,0:T(8,128)(2,1)S(1)} %collective-permute-done.5.refs_2_, ...), custom_call_target="tpu_custom_call" | custom-call | flops 1 | bytes 2359296 | tf_op jit(solution)/shard_map/outward_keep/pallas_call | solution.py:393
  44.4 4.6 %collective-permute-done.11.refs_3_ = bf16[576,512]{1,0:T(8,128)(2,1)S(1)} collective-permute-done((bf16[576,512]{1,0:T(8,128)(2,1)S(1)}, bf16[576,512]{1,0:T(8,128)(2,1)S(1)}, u32[]{:S(2)}, u32[]{:S(2)}) %collective-permute-start.11) | collective-permute-done | bytes 589856 | tf_op jit(solution)/shard_map/ppermute | solution.py:70
  49.0 7.1 %all-to-all-start = ((bf16[16,144,128]{2,1,0:T(8,128)(2,1)}), bf16[16,144,128]{2,1,0:T(8,128)(2,1)S(1)}, u32[]{:S(2)}, u32[]{:S(2)}) async-start(bf16[16,144,128]{2,1,0:T(8,128)(2,1)} %copy-done.2), calls=%async_computation | async-start | bytes 1179648 | tf_op jit(solution)/shard_map/all_to_all | solution.py:652
  56.1 0.6 collective-permute-start.16
  56.8 0.8 collective-permute-start.17
  58.6 8.8 %collective-permute-done.16.arrived = bf16[128,1536]{1,0:T(8,128)(2,1)S(1)} collective-permute-done((bf16[128,1536]{1,0:T(8,128)(2,1)S(1)}, bf16[128,1536]{1,0:T(8,128)(2,1)S(1)}, u32[]{:S(2)}, u32[]{:S(2)}) %collective-permute-start.16) | collective-permute-done | bytes 393248 | tf_op jit(solution)/shard_map/ppermute | solution.py:645
  67.4 1.0 %copy-done.5 = bf16[128,1536]{1,0:T(8,128)(2,1)S(1)} copy-done((bf16[128,1536]{1,0:T(8,128)(2,1)S(1)}, bf16[128,1536]{1,0:T(8,128)(2,1)}, u32[]{:S(2)}) %copy-start.5) | copy-done | bytes 393240
  68.4 0.7 copy-done.13
  70.4 4.3 %collective-permute-done.17.refs_7_ = bf16[288,512]{1,0:T(8,128)(2,1)S(1)} collective-permute-done((bf16[288,512]{1,0:T(8,128)(2,1)S(1)}, bf16[288,512]{1,0:T(8,128)(2,1)S(1)}, u32[]{:S(2)}, u32[]{:S(2)}) %collective-permute-start.17) | collective-permute-done | bytes 294944 | tf_op jit(solution)/shard_map/ppermute | solution.py:70
  75.2 4.7 %collective-permute-done.18.other = bf16[32,1536]{1,0:T(8,128)(2,1)S(1)} collective-permute-done((bf16[32,1536]{1,0:T(8,128)(2,1)S(1)}, bf16[32,1536]{1,0:T(8,128)(2,1)S(1)}, u32[]{:S(2)}, u32[]{:S(2)}) %collective-permute-start.18) | collective-permute-done | bytes 98336 | tf_op jit(solution)/shard_map/ppermute | solution.py:655
  79.9 2.0 %expert.1 = (bf16[32,1536]{1,0:T(8,128)(2,1)S(1)}, bf16[32,1536]{1,0:T(8,128)(2,1)}) custom-call(bf16[32,1536]{1,0:T(8,128)(2,1)S(1)} %get-tuple-element.91.own, bf16[32,1536]{1,0:T(8,128)(2,1)S(1)} %collective-permute-done.18.other, bf16[576,512]{1,0:T(8,128)(2,1)S(1)} %get-tuple-element.64.refs_0_, bf16[576,512]{1,0:T(8,128)(2,1)S(1)} %collective-permute-done.7.refs_1_, ...), custom_call_target="tpu_custom_call" | custom-call | flops 1 | bytes 9437184 | tf_op jit(solution)/shard_map/expert/pallas_call | solution.py:479
  82.4 3.3 %write.1 = bf16[512,4,128]{2,1,0:T(4,128)(2,1)} custom-call(bf16[16,144,128]{2,1,0:T(8,128)(2,1)S(1)} %all-to-all-done.arrived, bf16[512,4,128]{2,1,0:T(4,128)(2,1)S(1)} %copy-done.3), custom_call_target="tpu_custom_call" | custom-call | flops 1 | bytes 2097152 | tf_op jit(solution)/shard_map/write/pallas_call | solution.py:577
  85.7 1.0 %collective-permute-done.23.returned = bf16[32,1536]{1,0:T(8,128)(2,1)S(1)} collective-permute-done((bf16[32,1536]{1,0:T(8,128)(2,1)}, bf16[32,1536]{1,0:T(8,128)(2,1)S(1)}, u32[]{:S(2)}, u32[]{:S(2)}) %collective-permute-start.23) | collective-permute-done | bytes 98336 | tf_op jit(solution)/shard_map/ppermute | solution.py:662
  86.7 1.1 %combine.1 = bf16[128,1536]{1,0:T(8,128)(2,1)} custom-call(bf16[128,1536]{1,0:T(8,128)(2,1)S(1)} %get-tuple-element.83.residual, f32[128,40]{1,0:T(8,128)S(1)} %get-tuple-element.87.gates, bf16[128,64]{1,0:T(8,128)(2,1)S(1)} %copy-done.11, bf16[32,1536]{1,0:T(8,128)(2,1)S(1)} %get-tuple-element.94.own, bf16[32,1536]{1,0:T(8,128)(2,1)S(1)} %collective-permute-done.23.returned), custom_call_target="tpu_custom_call" | custom-call | flops 1 | bytes 1179648 | tf_op jit(solution)/shard_map/combine/pallas_call | solution.py:511
  (63 shorter events, 9.6 us)
Async XLA Ops:
  0.6 5.9 %collective-permute-start.2 = (bf16[96,1536]{1,0:T(8,128)(2,1)}, bf16[96,1536]{1,0:T(8,128)(2,1)S(1)}, u32[]{:S(2)}, u32[]{:S(2)}) collective-permute-start(bf16[96,1536]{1,0:T(8,128)(2,1)} %bitcast.13), channel_id=1, source_target_pairs={{0,2},{2,0},{4,6},{6,4},{8,10},{10,8},{12,14},{14,12},{16,18},{18,... | collective-permute-start | bytes 884744 | tf_op jit(solution)/shard_map/ppermute | solution.py:617
  0.7 5.8 %collective-permute-start = (bf16[96,1024]{1,0:T(8,128)(2,1)}, bf16[96,1024]{1,0:T(8,128)(2,1)S(1)}, u32[]{:S(2)}, u32[]{:S(2)}) collective-permute-start(bf16[96,1024]{1,0:T(8,128)(2,1)} %bitcast.15), channel_id=1, source_target_pairs={{0,2},{2,0},{4,6},{6,4},{8,10},{10,8},{12,14},{14,12},{16,18},{18,... | collective-permute-start | bytes 589832 | tf_op jit(solution)/shard_map/ppermute | solution.py:617
  1.2 5.3 %collective-permute-start.1 = (bf16[32,1536]{1,0:T(8,128)(2,1)}, bf16[32,1536]{1,0:T(8,128)(2,1)S(1)}, u32[]{:S(2)}, u32[]{:S(2)}) collective-permute-start(bf16[32,1536]{1,0:T(8,128)(2,1)} %bitcast.18), channel_id=1, source_target_pairs={{0,2},{2,0},{4,6},{6,4},{8,10},{10,8},{12,14},{14,12},{16,18},{18,... | collective-permute-start | bytes 294920 | tf_op jit(solution)/shard_map/ppermute | solution.py:617
  1.3 11.7 %collective-permute-start.4 = (bf16[128,1536]{1,0:T(8,128)(2,1)}, bf16[128,1536]{1,0:T(8,128)(2,1)S(1)}, u32[]{:S(2)}, u32[]{:S(2)}) collective-permute-start(bf16[128,1536]{1,0:T(8,128)(2,1)} %tokens.1), channel_id=1, source_target_pairs={{0,1},{1,0},{2,3},{3,2},{4,5},{5,4},{6,7},{7,6},{8,9},{9,8},{10,11... | collective-permute-start | bytes 1179656 | tf_op jit(solution)/shard_map/ppermute | solution.py:614
  4.5 1.9 %copy-start.6 = (bf16[40,1536]{1,0:T(8,128)(2,1)}, bf16[40,1536]{1,0:T(8,128)(2,1)S(1)}, u32[]{:S(2)}) copy-start(bf16[40,1536]{1,0:T(8,128)(2,1)S(1)} %get-tuple-element.85.router) | copy-start | bytes 368644
  4.6 10.3 %copy-start.4 = (bf16[128,1536]{1,0:T(8,128)(2,1)S(1)}, bf16[128,1536]{1,0:T(8,128)(2,1)}, u32[]{:S(2)}) copy-start(bf16[128,1536]{1,0:T(8,128)(2,1)} %tokens.1) | copy-start | bytes 1179652
  4.6 10.3 %copy-start.14 = (bf16[1536,768]{1,0:T(8,128)(2,1)S(1)}, bf16[1536,768]{1,0:T(8,128)(2,1)}, u32[]{:S(2)}) copy-start(bf16[1536,768]{1,0:T(8,128)(2,1)} %w_query.1) | copy-start | bytes 7077892
  7.7 6.8 %collective-permute-start.3 = (bf16[192,768]{1,0:T(8,128)(2,1)S(1)}, bf16[192,768]{1,0:T(8,128)(2,1)S(1)}, u32[]{:S(2)}, u32[]{:S(2)}) collective-permute-start(bf16[192,768]{1,0:T(8,128)(2,1)S(1)} %get-tuple-element.55.refs_0_), channel_id=1, source_target_pairs={{0,8},{2,6},{8,16},{10,2},{16,24},{18,10},{24,28},{26,18},{28,20},... | collective-permute-start | bytes 884744 | tf_op jit(solution)/shard_map/ppermute | solution.py:70
  8.2 12.6 %collective-permute-start.7 = (bf16[576,512]{1,0:T(8,128)(2,1)S(1)}, bf16[576,512]{1,0:T(8,128)(2,1)S(1)}, u32[]{:S(2)}, u32[]{:S(2)}) collective-permute-start(bf16[576,512]{1,0:T(8,128)(2,1)S(1)} %get-tuple-element.64.refs_0_), channel_id=1, source_target_pairs={{0,8},{2,6},{8,16},{10,2},{16,24},{18,10},{24,28},{26,18},{28,20},... | collective-permute-start | bytes 1769480 | tf_op jit(solution)/shard_map/ppermute | solution.py:70
  14.4 9.5 %collective-permute-start.5 = (bf16[192,768]{1,0:T(8,128)(2,1)S(1)}, bf16[192,768]{1,0:T(8,128)(2,1)S(1)}, u32[]{:S(2)}, u32[]{:S(2)}) collective-permute-start(bf16[192,768]{1,0:T(8,128)(2,1)S(1)} %collective-permute-done.3.refs_1_), channel_id=1, source_target_pairs={{0,8},{2,6},{8,16},{10,2},{16,24},{18,10},{24,28},{26,18},{28,20},... | collective-permute-start | bytes 884744 | tf_op jit(solution)/shard_map/ppermute | solution.py:70
  17.1 6.3 %collective-permute-start.6 = (bf16[128,512]{1,0:T(8,128)(2,1)S(1)}, bf16[128,512]{1,0:T(8,128)(2,1)S(1)}, u32[]{:S(2)}, u32[]{:S(2)}) collective-permute-start(bf16[128,512]{1,0:T(8,128)(2,1)S(1)} %get-tuple-element.62), channel_id=1, source_target_pairs={{0,2},{2,4},{4,6},{6,8},{8,10},{10,12},{12,14},{14,16},{16,18},{18... | collective-permute-start | bytes 393224 | tf_op jit(solution)/shard_map/ppermute | solution.py:632
  20.8 18.3 %collective-permute-start.8 = (bf16[576,512]{1,0:T(8,128)(2,1)S(1)}, bf16[576,512]{1,0:T(8,128)(2,1)S(1)}, u32[]{:S(2)}, u32[]{:S(2)}) collective-permute-start(bf16[576,512]{1,0:T(8,128)(2,1)S(1)} %collective-permute-done.7.refs_1_), channel_id=1, source_target_pairs={{0,8},{2,6},{8,16},{10,2},{16,24},{18,10},{24,28},{26,18},{28,20},... | collective-permute-start | bytes 1769480 | tf_op jit(solution)/shard_map/ppermute | solution.py:70
  23.9 9.9 %collective-permute-start.9 = (bf16[192,768]{1,0:T(8,128)(2,1)S(1)}, bf16[192,768]{1,0:T(8,128)(2,1)S(1)}, u32[]{:S(2)}, u32[]{:S(2)}) collective-permute-start(bf16[192,768]{1,0:T(8,128)(2,1)S(1)} %collective-permute-done.5.refs_2_), channel_id=1, source_target_pairs={{0,8},{2,6},{8,16},{10,2},{16,24},{18,10},{24,28},{26,18},{28,20},... | collective-permute-start | bytes 884744 | tf_op jit(solution)/shard_map/ppermute | solution.py:70
  33.8 5.2 %collective-permute-start.10 = (bf16[96,768]{1,0:T(8,128)(2,1)S(1)}, bf16[96,768]{1,0:T(8,128)(2,1)S(1)}, u32[]{:S(2)}, u32[]{:S(2)}) collective-permute-start(bf16[96,768]{1,0:T(8,128)(2,1)S(1)} %slice.6), channel_id=1, source_target_pairs={{0,8},{2,6},{8,16},{10,2},{16,24},{18,10},{24,28},{26,18},{28,20},... | collective-permute-start | bytes 442376 | tf_op jit(solution)/shard_map/ppermute | solution.py:70
  39.0 4.2 %copy-start = (bf16[576,512]{1,0:T(8,128)(2,1)}, bf16[576,512]{1,0:T(8,128)(2,1)S(1)}, u32[]{:S(2)}) copy-start(bf16[576,512]{1,0:T(8,128)(2,1)S(1)} %collective-permute-done.8.refs_2_) | copy-start | bytes 1769476
  39.0 10.0 %collective-permute-start.11 = (bf16[576,512]{1,0:T(8,128)(2,1)S(1)}, bf16[576,512]{1,0:T(8,128)(2,1)S(1)}, u32[]{:S(2)}, u32[]{:S(2)}) collective-permute-start(bf16[576,512]{1,0:T(8,128)(2,1)S(1)} %collective-permute-done.8.refs_2_), channel_id=1, source_target_pairs={{0,8},{2,6},{8,16},{10,2},{16,24},{18,10},{24,28},{26,18},{28,20},... | collective-permute-start | bytes 1769480 | tf_op jit(solution)/shard_map/ppermute | solution.py:70
  39.5 1.6 %collective-permute-start.12 = (bf16[192,768]{1,0:T(8,128)(2,1)S(1)}, bf16[192,768]{1,0:T(8,128)(2,1)S(1)}, u32[]{:S(2)}, u32[]{:S(2)}) collective-permute-start(bf16[192,768]{1,0:T(8,128)(2,1)S(1)} %collective-permute-done.3.refs_1_), channel_id=1, source_target_pairs={{0,2},{2,0},{4,6},{6,4},{8,10},{10,8},{12,14},{14,12},{16,18},{18,... | collective-permute-start | bytes 884744 | tf_op jit(solution)/shard_map/ppermute | solution.py:79
  39.6 1.9 %collective-permute-start.13 = (bf16[192,768]{1,0:T(8,128)(2,1)S(1)}, bf16[192,768]{1,0:T(8,128)(2,1)S(1)}, u32[]{:S(2)}, u32[]{:S(2)}) collective-permute-start(bf16[192,768]{1,0:T(8,128)(2,1)S(1)} %collective-permute-done.5.refs_2_), channel_id=1, source_target_pairs={{0,2},{2,0},{4,6},{6,4},{8,10},{10,8},{12,14},{14,12},{16,18},{18,... | collective-permute-start | bytes 884744 | tf_op jit(solution)/shard_map/ppermute | solution.py:79
  40.0 1.9 %collective-permute-start.14 = (bf16[192,768]{1,0:T(8,128)(2,1)S(1)}, bf16[192,768]{1,0:T(8,128)(2,1)S(1)}, u32[]{:S(2)}, u32[]{:S(2)}) collective-permute-start(bf16[192,768]{1,0:T(8,128)(2,1)S(1)} %collective-permute-done.9.refs_3_), channel_id=1, source_target_pairs={{0,2},{2,0},{4,6},{6,4},{8,10},{10,8},{12,14},{14,12},{16,18},{18,... | collective-permute-start | bytes 884744 | tf_op jit(solution)/shard_map/ppermute | solution.py:79
  40.1 2.0 %collective-permute-start.15 = (bf16[96,768]{1,0:T(8,128)(2,1)S(1)}, bf16[96,768]{1,0:T(8,128)(2,1)S(1)}, u32[]{:S(2)}, u32[]{:S(2)}) collective-permute-start(bf16[96,768]{1,0:T(8,128)(2,1)S(1)} %collective-permute-done.10.refs_7_), channel_id=1, source_target_pairs={{0,2},{2,0},{4,6},{6,4},{8,10},{10,8},{12,14},{14,12},{16,18},{18,... | collective-permute-start | bytes 442376 | tf_op jit(solution)/shard_map/ppermute | solution.py:79
  49.0 33.4 %all-to-all-start = ((bf16[16,144,128]{2,1,0:T(8,128)(2,1)}), bf16[16,144,128]{2,1,0:T(8,128)(2,1)S(1)}, u32[]{:S(2)}, u32[]{:S(2)}) async-start(bf16[16,144,128]{2,1,0:T(8,128)(2,1)} %copy-done.2), calls=%async_computation | async-start | bytes 1179648 | tf_op jit(solution)/shard_map/all_to_all | solution.py:652
  56.1 23.8 %copy-start.1 = (bf16[576,512]{1,0:T(8,128)(2,1)S(1)}, bf16[576,512]{1,0:T(8,128)(2,1)}, u32[]{:S(2)}) copy-start(bf16[576,512]{1,0:T(8,128)(2,1)} %copy-done) | copy-start | bytes 1769476
  56.1 11.2 %collective-permute-start.16 = (bf16[128,1536]{1,0:T(8,128)(2,1)S(1)}, bf16[128,1536]{1,0:T(8,128)(2,1)S(1)}, u32[]{:S(2)}, u32[]{:S(2)}) collective-permute-start(bf16[128,1536]{1,0:T(8,128)(2,1)S(1)} %outward_send.1), channel_id=1, source_target_pairs={{0,1},{1,0},{2,3},{3,2},{4,5},{5,4},{6,7},{7,6},{8,9},{9,8},{10,11... | collective-permute-start | bytes 1179656 | tf_op jit(solution)/shard_map/ppermute | solution.py:645
  56.8 17.9 %collective-permute-start.17 = (bf16[288,512]{1,0:T(8,128)(2,1)S(1)}, bf16[288,512]{1,0:T(8,128)(2,1)S(1)}, u32[]{:S(2)}, u32[]{:S(2)}) collective-permute-start(bf16[288,512]{1,0:T(8,128)(2,1)S(1)} %slice.7), channel_id=1, source_target_pairs={{0,8},{2,6},{8,16},{10,2},{16,24},{18,10},{24,28},{26,18},{28,20},... | collective-permute-start | bytes 884744 | tf_op jit(solution)/shard_map/ppermute | solution.py:70
  57.6 17.7 %collective-permute-start.19 = (bf16[576,512]{1,0:T(8,128)(2,1)S(1)}, bf16[576,512]{1,0:T(8,128)(2,1)S(1)}, u32[]{:S(2)}, u32[]{:S(2)}) collective-permute-start(bf16[576,512]{1,0:T(8,128)(2,1)S(1)} %collective-permute-done.7.refs_1_), channel_id=1, source_target_pairs={{0,2},{2,0},{4,6},{6,4},{8,10},{10,8},{12,14},{14,12},{16,18},{18,... | collective-permute-start | bytes 1769480 | tf_op jit(solution)/shard_map/ppermute | solution.py:79
  58.1 17.2 %collective-permute-start.20 = (bf16[576,512]{1,0:T(8,128)(2,1)}, bf16[576,512]{1,0:T(8,128)(2,1)S(1)}, u32[]{:S(2)}, u32[]{:S(2)}) collective-permute-start(bf16[576,512]{1,0:T(8,128)(2,1)} %copy-done), channel_id=1, source_target_pairs={{0,2},{2,0},{4,6},{6,4},{8,10},{10,8},{12,14},{14,12},{16,18},{18,... | collective-permute-start | bytes 1769480 | tf_op jit(solution)/shard_map/ppermute | solution.py:79
  58.1 21.8 %collective-permute-start.21 = (bf16[576,512]{1,0:T(8,128)(2,1)S(1)}, bf16[576,512]{1,0:T(8,128)(2,1)S(1)}, u32[]{:S(2)}, u32[]{:S(2)}) collective-permute-start(bf16[576,512]{1,0:T(8,128)(2,1)S(1)} %collective-permute-done.11.refs_3_), channel_id=1, source_target_pairs={{0,2},{2,0},{4,6},{6,4},{8,10},{10,8},{12,14},{14,12},{16,18},{18,... | collective-permute-start | bytes 1769480 | tf_op jit(solution)/shard_map/ppermute | solution.py:79
  74.7 5.2 %collective-permute-start.22 = (bf16[288,512]{1,0:T(8,128)(2,1)S(1)}, bf16[288,512]{1,0:T(8,128)(2,1)S(1)}, u32[]{:S(2)}, u32[]{:S(2)}) collective-permute-start(bf16[288,512]{1,0:T(8,128)(2,1)S(1)} %collective-permute-done.17.refs_7_), channel_id=1, source_target_pairs={{0,2},{2,0},{4,6},{6,4},{8,10},{10,8},{12,14},{14,12},{16,18},{18,... | collective-permute-start | bytes 884744 | tf_op jit(solution)/shard_map/ppermute | solution.py:79
  74.7 7.7 %copy-start.3 = (bf16[512,4,128]{2,1,0:T(4,128)(2,1)S(1)}, bf16[512,4,128]{2,1,0:T(4,128)(2,1)}, u32[]{:S(2)}) copy-start(bf16[512,4,128]{2,1,0:T(4,128)(2,1)} %cache.1) | copy-start | bytes 1572868
  74.7 5.2 %collective-permute-start.18 = (bf16[32,1536]{1,0:T(8,128)(2,1)S(1)}, bf16[32,1536]{1,0:T(8,128)(2,1)S(1)}, u32[]{:S(2)}, u32[]{:S(2)}) collective-permute-start(bf16[32,1536]{1,0:T(8,128)(2,1)S(1)} %get-tuple-element.92), channel_id=1, source_target_pairs={{0,1},{1,0},{2,3},{3,2},{4,5},{5,4},{6,7},{7,6},{8,9},{9,8},{10,11... | collective-permute-start | bytes 294920 | tf_op jit(solution)/shard_map/ppermute | solution.py:655
  81.9 4.8 %copy-start.11 = (bf16[128,64]{1,0:T(8,128)(2,1)S(1)}, bf16[128,64]{1,0:T(8,128)(2,1)}, u32[]{:S(2)}) copy-start(bf16[128,64]{1,0:T(8,128)(2,1)} %copy-done.10) | copy-start | bytes 49156
  81.9 4.8 %collective-permute-start.23 = (bf16[32,1536]{1,0:T(8,128)(2,1)}, bf16[32,1536]{1,0:T(8,128)(2,1)S(1)}, u32[]{:S(2)}, u32[]{:S(2)}) collective-permute-start(bf16[32,1536]{1,0:T(8,128)(2,1)} %get-tuple-element.95), channel_id=1, source_target_pairs={{0,1},{1,0},{2,3},{3,2},{4,5},{5,4},{6,7},{7,6},{8,9},{9,8},{10,11... | collective-permute-start | bytes 294920 | tf_op jit(solution)/shard_map/ppermute | solution.py:662
  (8 other events, 10.0 us)

commit v6 on v5

--- a/solution.py
+++ b/solution.py
@@ -98,7 +98,7 @@
 VMEM = pl.BlockSpec(memory_space=pltpu.VMEM)
 ANY = pl.BlockSpec(memory_space=pl.ANY)
 HBM = pl.BlockSpec(memory_space=pltpu.HBM)
-PARAMS = pltpu.CompilerParams(vmem_limit_bytes=40 << 20)
+PARAMS = pltpu.CompilerParams(vmem_limit_bytes=16 << 20)
 
 
 LITTLE = pl.CostEstimate(flops=1, bytes_accessed=1, transcendentals=0)
@@ -322,7 +322,7 @@
             pltpu.SemaphoreType.DMA((2,)),
         ],
         compiler_params=PARAMS,
-        cost_estimate=takes(6),
+        cost_estimate=takes(8),
         name="project",
     )(own, other, gain, cosine, sine, w_query, flat_kv)
 
@@ -615,17 +615,17 @@
     own = (w_gate_up[0], w_down[0], w_out.T)
     up_rows, down_rows = own[0].shape[0], own[1].shape[0]
     beside = [lax.ppermute(part, "grp", sibling_pairs(groups)) for part in own]
-    flat_kv = w_keyval.reshape(model, kv_width)
-    cosine, sine, past, named, place, spread, send, tags, gain, late_gain, router_t = prepare(
-        groups, slots_dev, positions, cache_slot, expert_ids, attn_gain, moe_gain, router
-    )
-    beside, cosine, flat_kv = together((beside, cosine, flat_kv))
     expert_pair, out_pair = pack(own, beside)
     out_ring = Ring(out_pair, groups)
     out_ring.step()
     expert_ring = Ring(expert_pair, groups)
     expert_ring.step()
-    other_tokens = out_ring.pin(other_tokens)
+    w_keyval, positions = together((w_keyval, positions, out_pair))[:2]
+    flat_kv = w_keyval.reshape(model, kv_width)
+    cosine, sine, past, named, place, spread, send, tags, gain, late_gain, router_t = prepare(
+        groups, slots_dev, positions, cache_slot, expert_ids, attn_gain, moe_gain, router
+    )
+    other_tokens, cosine, flat_kv = out_ring.pin(other_tokens, cosine, flat_kv)
     out_ring.step()
 
     q, kv, tail = project(tokens, other_tokens, gain, cosine, sine, w_query, flat_kv)
@@ -636,6 +636,8 @@
     seam, outgoing = out_ring.pin(seam, outgoing)
     out_ring.step()
     mixed = attend(q, kv, seam, past)
+    outgoing, mixed = together((outgoing, mixed))
+    arrived_cache = lax.all_to_all(outgoing, "grp", split_axis=0, concat_axis=0, tiled=True)
     mixed = out_ring.pin(mixed)
     out_ring.step()
     out_ring.mine[-1] = expert_ring.pin(out_ring.mine[-1])
@@ -648,8 +650,6 @@
     mine = expert_ring.pin(mine)
     expert_ring.share()
     expert_ring.step()
-    outgoing, mine = together((outgoing, mine))
-    arrived_cache = lax.all_to_all(outgoing, "grp", split_axis=0, concat_axis=0, tiled=True)
 
     residual, moe_in, sent_rows = route(tokens, mine, arrived, late_gain, place)
     landed = swap(sent_rows)

time: 88.3 us -> 76.8 us (0.87)
  the two profiles are of different devices: /device:TPU:12 before, /device:TPU:16 now
where the time goes in v6:
time: 76.8 us; the launch traced here: 76.5 us
  starting transfers between devices  27.4 us (36%)
  waiting for transfers between devices  25.9 us (34%)
  Pallas kernels  18.3 us (24%)
  local copies, waits for them, and re-layouts  4.02 us (5%)
  between operations  0.84 us (1%)
    ppermute x8, starting transfers between devices, step(): self.mine.append(self.across(held))  12.4 us
    ppermute x8, waiting for transfers between devices, step(): self.mine.append(self.across(held))  11.4 us
    ppermute x1, waiting for transfers between devices, two_lane_shards(): arrived = swap(sent)  5.83 us
    all_to_all x1, starting transfers between devices, two_lane_shards(): lax.all_to_all(outgoing, 'grp', split_axis=0, concat_axis=0, tiled=True)  4.82 us
    unnamed x23, local copies, waits for them, and re-layouts  3.99 us
    ppermute x1, waiting for transfers between devices, two_lane_shards(): landed = swap(sent_rows)  3.71 us
    pallas_call x1, Pallas kernels, write(): pl.pallas_call(write_kernel, out_shape=jax.ShapeDtypeStruct(cache.shape,...  3.27 us
    pallas_call x1, Pallas kernels, attend(): pl.pallas_call(attend_kernel, out_shape=jax.ShapeDtypeStruct(q.shape, bf1...  2.83 us
  transfers between devices with their start and end apart: 25, of which 13 were waited for; matrix products, arithmetic and copies ran while one was open for 2% of the time, Pallas kernels for 22%

profile of v6, /device:TPU:16, one launch (start us, length us, event | category | flops | bytes accessed | tf_op | source)
XLA Modules:
  0.0 76.5 jit_solution(8974244188369905805)
XLA Ops:
  1.3 1.5 %collective-permute-start.5 = (bf16[128,1536]{1,0:T(8,128)(2,1)}, bf16[128,1536]{1,0:T(8,128)(2,1)S(1)}, u32[]{:S(2)}, u32[]{:S(2)}) collective-permute-start(bf16[128,1536]{1,0:T(8,128)(2,1)} %tokens.1), channel_id=1, source_target_pairs={{0,1},{1,0},{2,3},{3,2},{4,5},{5,4},{6,7},{7,6},{8,9},{9,8},{10,11... | collective-permute-start | bytes 1179656 | tf_op jit(solution)/shard_map/ppermute | solution.py:614
  2.9 1.1 %pack.1 = (bf16[576,512]{1,0:T(8,128)(2,1)S(1)}, bf16[192,768]{1,0:T(8,128)(2,1)S(1)}) custom-call(bf16[96,1024]{1,0:T(8,128)(2,1)} %bitcast.16, bf16[32,1536]{1,0:T(8,128)(2,1)} %bitcast.19, bf16[96,1536]{1,0:T(8,128)(2,1)} %bitcast.14, bf16[96,1024]{1,0:T(8,128)(2,1)S(1)} %collective-permute-done.refs_3_, ...), custom_call_target="tpu_custom_call" | custom-call | flops 1 | bytes 1 | tf_op jit(solution)/shard_map/pack/pallas_call | solution.py:157
  4.1 1.6 %collective-permute-start.4 = (bf16[192,768]{1,0:T(8,128)(2,1)S(1)}, bf16[192,768]{1,0:T(8,128)(2,1)S(1)}, u32[]{:S(2)}, u32[]{:S(2)}) collective-permute-start(bf16[192,768]{1,0:T(8,128)(2,1)S(1)} %get-tuple-element.51.refs_0_), channel_id=1, source_target_pairs={{0,8},{2,6},{8,16},{10,2},{16,24},{18,10},{24,28},{26,18},{28,20},... | collective-permute-start | bytes 884744 | tf_op jit(solution)/shard_map/ppermute | solution.py:70
  5.7 1.5 %collective-permute-start.3 = (bf16[576,512]{1,0:T(8,128)(2,1)S(1)}, bf16[576,512]{1,0:T(8,128)(2,1)S(1)}, u32[]{:S(2)}, u32[]{:S(2)}) collective-permute-start(bf16[576,512]{1,0:T(8,128)(2,1)S(1)} %get-tuple-element.50.refs_0_), channel_id=1, source_target_pairs={{0,8},{2,6},{8,16},{10,2},{16,24},{18,10},{24,28},{26,18},{28,20},... | collective-permute-start | bytes 1769480 | tf_op jit(solution)/shard_map/ppermute | solution.py:70
  7.2 1.7 %prepare.1 = (f32[256,128]{1,0:T(8,128)S(1)}, f32[256,128]{1,0:T(8,128)S(1)}, f32[256,128]{1,0:T(8,128)S(1)}, f32[128,40]{1,0:T(8,128)S(1)}, bf16[64,128]{1,0:T(...) custom-call(s32[1,256]{1,0:T(1,128)} %bitcast.21, ...), custom_call_target="tpu_custom_call" | custom-call | flops 1 | bytes 1 | tf_op jit(solution)/shard_map/prepare/pallas_call | solution.py:259
  10.2 1.8 %copy.17 = bf16[192,8,4,128]{3,1,2,0:T(8,128)(2,1)S(1)} copy(bf16[192,8,4,128]{3,2,1,0:T(4,128)(2,1)} %bitcast.12) | data formatting | bytes 3145728
  12.1 0.9 %collective-permute-done.5.other = bf16[128,1536]{1,0:T(8,128)(2,1)S(1)} collective-permute-done((bf16[128,1536]{1,0:T(8,128)(2,1)}, bf16[128,1536]{1,0:T(8,128)(2,1)S(1)}, u32[]{:S(2)}, u32[]{:S(2)}) %collective-permute-start.5) | collective-permute-done | bytes 393248 | tf_op jit(solution)/shard_map/ppermute | solution.py:614
  13.0 1.6 %collective-permute-start.7 = (bf16[192,768]{1,0:T(8,128)(2,1)S(1)}, bf16[192,768]{1,0:T(8,128)(2,1)S(1)}, u32[]{:S(2)}, u32[]{:S(2)}) collective-permute-start(bf16[192,768]{1,0:T(8,128)(2,1)S(1)} %collective-permute-done.4.refs_1_), channel_id=1, source_target_pairs={{0,8},{2,6},{8,16},{10,2},{16,24},{18,10},{24,28},{26,18},{28,20},... | collective-permute-start | bytes 884744 | tf_op jit(solution)/shard_map/ppermute | solution.py:70
  14.5 2.2 %project.1 = (bf16[256,768]{1,0:T(8,128)(2,1)S(1)}, bf16[256,512]{1,0:T(8,128)(2,1)S(1)}, bf16[128,512]{1,0:T(8,128)(2,1)S(1)}) custom-call(bf16[128,1536]{1,0:T(8,128)(2,1)S(1)} %copy-done.4, bf16[128,1536]{1,0:T(8,128)(2,1)S(1)} %collective-permute-done.5.other, f32[1,1536]{1,0:T(1,128)S(1)} %get-tuple-element.56.gain, ...), custom_call_target="tpu_custom_call" | custom-call | flops 9200000000 | bytes 1 | tf_op jit(solution)/shard_map/project/pallas_call | solution.py:310
  16.8 1.9 %collective-permute-start.8 = (bf16[128,512]{1,0:T(8,128)(2,1)S(1)}, bf16[128,512]{1,0:T(8,128)(2,1)S(1)}, u32[]{:S(2)}, u32[]{:S(2)}) collective-permute-start(bf16[128,512]{1,0:T(8,128)(2,1)S(1)} %get-tuple-element.63), channel_id=1, source_target_pairs={{0,2},{2,4},{4,6},{6,8},{8,10},{10,12},{12,14},{14,16},{16,18},{18... | collective-permute-start | bytes 393224 | tf_op jit(solution)/shard_map/ppermute | solution.py:632
  18.7 1.6 %collective-permute-start.6 = (bf16[576,512]{1,0:T(8,128)(2,1)S(1)}, bf16[576,512]{1,0:T(8,128)(2,1)}, u32[]{:S(2)}, u32[]{:S(2)}) collective-permute-start(bf16[576,512]{1,0:T(8,128)(2,1)S(1)} %collective-permute-done.3.refs_1_), channel_id=1, source_target_pairs={{0,8},{2,6},{8,16},{10,2},{16,24},{18,10},{24,28},{26,18},{28,20},... | collective-permute-start | bytes 1769480 | tf_op jit(solution)/shard_map/ppermute | solution.py:70
  20.8 0.8 %copy-done.2 = bf16[16,144,128]{2,1,0:T(8,128)(2,1)} copy-done((bf16[16,144,128]{2,1,0:T(8,128)(2,1)}, bf16[16,144,128]{2,1,0:T(8,128)(2,1)S(1)}, u32[]{:S(2)}) %copy-start.2) | copy-done | bytes 589848
  21.7 2.3 %collective-permute-done.8.seam = bf16[128,512]{1,0:T(8,128)(2,1)S(1)} collective-permute-done((bf16[128,512]{1,0:T(8,128)(2,1)S(1)}, bf16[128,512]{1,0:T(8,128)(2,1)S(1)}, u32[]{:S(2)}, u32[]{:S(2)}) %collective-permute-start.8) | collective-permute-done | bytes 131104 | tf_op jit(solution)/shard_map/ppermute | solution.py:632
  24.0 1.6 %collective-permute-start.9 = (bf16[192,768]{1,0:T(8,128)(2,1)S(1)}, bf16[192,768]{1,0:T(8,128)(2,1)S(1)}, u32[]{:S(2)}, u32[]{:S(2)}) collective-permute-start(bf16[192,768]{1,0:T(8,128)(2,1)S(1)} %collective-permute-done.7.refs_2_), channel_id=1, source_target_pairs={{0,8},{2,6},{8,16},{10,2},{16,24},{18,10},{24,28},{26,18},{28,20},... | collective-permute-start | bytes 884744 | tf_op jit(solution)/shard_map/ppermute | solution.py:70
  25.6 2.8 %attend.1.mixed = bf16[256,768]{1,0:T(8,128)(2,1)S(1)} custom-call(bf16[256,768]{1,0:T(8,128)(2,1)S(1)} %get-tuple-element.69.q, bf16[256,512]{1,0:T(8,128)(2,1)S(1)} %get-tuple-element.65.kv, bf16[128,512]{1,0:T(8,128)(2,1)S(1)} %collective-permute-done.8.seam, f32[256,128]{1,0:T(8,128)S(1)} %get-tuple-element.71.past), custom_call_target="tpu_custom_call" | custom-call | flops 4600000000 | bytes 1 | tf_op jit(solution)/shard_map/attend/pallas_call | solution.py:363
  28.4 3.4 %collective-permute-done.9.refs_3_ = bf16[192,768]{1,0:T(8,128)(2,1)S(1)} collective-permute-done((bf16[192,768]{1,0:T(8,128)(2,1)S(1)}, bf16[192,768]{1,0:T(8,128)(2,1)S(1)}, u32[]{:S(2)}, u32[]{:S(2)}) %collective-permute-start.9) | collective-permute-done | bytes 294944 | tf_op jit(solution)/shard_map/ppermute | solution.py:70
  31.8 1.6 %collective-permute-start.10 = (bf16[96,768]{1,0:T(8,128)(2,1)S(1)}, bf16[96,768]{1,0:T(8,128)(2,1)S(1)}, u32[]{:S(2)}, u32[]{:S(2)}) collective-permute-start(bf16[96,768]{1,0:T(8,128)(2,1)S(1)} %slice.6), channel_id=1, source_target_pairs={{0,8},{2,6},{8,16},{10,2},{16,24},{18,10},{24,28},{26,18},{28,20},... | collective-permute-start | bytes 442376 | tf_op jit(solution)/shard_map/ppermute | solution.py:70
  33.4 3.6 %collective-permute-done.10.refs_7_ = bf16[96,768]{1,0:T(8,128)(2,1)S(1)} collective-permute-done((bf16[96,768]{1,0:T(8,128)(2,1)S(1)}, bf16[96,768]{1,0:T(8,128)(2,1)S(1)}, u32[]{:S(2)}, u32[]{:S(2)}) %collective-permute-start.10) | collective-permute-done | bytes 147488 | tf_op jit(solution)/shard_map/ppermute | solution.py:70
  37.0 1.5 %collective-permute-start.11 = (bf16[576,512]{1,0:T(8,128)(2,1)}, bf16[576,512]{1,0:T(8,128)(2,1)S(1)}, u32[]{:S(2)}, u32[]{:S(2)}) collective-permute-start(bf16[576,512]{1,0:T(8,128)(2,1)} %collective-permute-done.6.refs_2_), channel_id=1, source_target_pairs={{0,8},{2,6},{8,16},{10,2},{16,24},{18,10},{24,28},{26,18},{28,20},... | collective-permute-start | bytes 1769480 | tf_op jit(solution)/shard_map/ppermute | solution.py:70
  38.5 4.8 %all-to-all-start = ((bf16[16,144,128]{2,1,0:T(8,128)(2,1)}), bf16[16,144,128]{2,1,0:T(8,128)(2,1)S(1)}, u32[]{:S(2)}, u32[]{:S(2)}) async-start(bf16[16,144,128]{2,1,0:T(8,128)(2,1)} %copy-done.2), calls=%async_computation | async-start | bytes 1179648 | tf_op jit(solution)/shard_map/all_to_all | solution.py:640
  46.0 1.1 %outward_send.1 = bf16[128,1536]{1,0:T(8,128)(2,1)S(1)} custom-call(bf16[256,768]{1,0:T(8,128)(2,1)S(1)} %attend.1.mixed, bf16[192,768]{1,0:T(8,128)(2,1)S(1)} %get-tuple-element.51.refs_0_, bf16[192,768]{1,0:T(8,128)(2,1)S(1)} %collective-permute-done.4.refs_1_, bf16[192,768]{1,0:T(8,128)(2,1)S(1)} %collective-permute-done.7.refs_2_, ...), custom_call_target="tpu_custom_call" | custom-call | flops 1 | bytes 2359296 | tf_op jit(solution)/shard_map/outward_send/pallas_call | solution.py:393
  47.2 1.6 %collective-permute-start.16 = (bf16[128,1536]{1,0:T(8,128)(2,1)S(1)}, bf16[128,1536]{1,0:T(8,128)(2,1)S(1)}, u32[]{:S(2)}, u32[]{:S(2)}) collective-permute-start(bf16[128,1536]{1,0:T(8,128)(2,1)S(1)} %outward_send.1), channel_id=1, source_target_pairs={{0,1},{1,0},{2,3},{3,2},{4,5},{5,4},{6,7},{7,6},{8,9},{9,8},{10,11... | collective-permute-start | bytes 1179656 | tf_op jit(solution)/shard_map/ppermute | solution.py:647
  48.7 1.1 %outward_keep.1.mine = f32[128,1536]{1,0:T(8,128)S(1)} custom-call(bf16[256,768]{1,0:T(8,128)(2,1)S(1)} %attend.1.mixed, bf16[192,768]{1,0:T(8,128)(2,1)S(1)} %get-tuple-element.51.refs_0_, bf16[192,768]{1,0:T(8,128)(2,1)S(1)} %collective-permute-done.4.refs_1_, bf16[192,768]{1,0:T(8,128)(2,1)S(1)} %collective-permute-done.7.refs_2_, ...), custom_call_target="tpu_custom_call" | custom-call | flops 1 | bytes 2359296 | tf_op jit(solution)/shard_map/outward_keep/pallas_call | solution.py:393
  50.7 1.4 %collective-permute-start.17 = (bf16[288,512]{1,0:T(8,128)(2,1)S(1)}, bf16[288,512]{1,0:T(8,128)(2,1)S(1)}, u32[]{:S(2)}, u32[]{:S(2)}) collective-permute-start(bf16[288,512]{1,0:T(8,128)(2,1)S(1)} %slice.7), channel_id=1, source_target_pairs={{0,8},{2,6},{8,16},{10,2},{16,24},{18,10},{24,28},{26,18},{28,20},... | collective-permute-start | bytes 884744 | tf_op jit(solution)/shard_map/ppermute | solution.py:70
  52.6 5.8 %collective-permute-done.16.arrived = bf16[128,1536]{1,0:T(8,128)(2,1)S(1)} collective-permute-done((bf16[128,1536]{1,0:T(8,128)(2,1)S(1)}, bf16[128,1536]{1,0:T(8,128)(2,1)S(1)}, u32[]{:S(2)}, u32[]{:S(2)}) %collective-permute-start.16) | collective-permute-done | bytes 393248 | tf_op jit(solution)/shard_map/ppermute | solution.py:647
  59.3 3.6 %collective-permute-done.17.refs_7_ = bf16[288,512]{1,0:T(8,128)(2,1)S(1)} collective-permute-done((bf16[288,512]{1,0:T(8,128)(2,1)S(1)}, bf16[288,512]{1,0:T(8,128)(2,1)S(1)}, u32[]{:S(2)}, u32[]{:S(2)}) %collective-permute-start.17) | collective-permute-done | bytes 294944 | tf_op jit(solution)/shard_map/ppermute | solution.py:70
  62.9 1.5 %collective-permute-start.18 = (bf16[32,1536]{1,0:T(8,128)(2,1)S(1)}, bf16[32,1536]{1,0:T(8,128)(2,1)S(1)}, u32[]{:S(2)}, u32[]{:S(2)}) collective-permute-start(bf16[32,1536]{1,0:T(8,128)(2,1)S(1)} %get-tuple-element.90), channel_id=1, source_target_pairs={{0,1},{1,0},{2,3},{3,2},{4,5},{5,4},{6,7},{7,6},{8,9},{9,8},{10,11... | collective-permute-start | bytes 294920 | tf_op jit(solution)/shard_map/ppermute | solution.py:655
  64.4 3.7 %collective-permute-done.18.other = bf16[32,1536]{1,0:T(8,128)(2,1)S(1)} collective-permute-done((bf16[32,1536]{1,0:T(8,128)(2,1)S(1)}, bf16[32,1536]{1,0:T(8,128)(2,1)S(1)}, u32[]{:S(2)}, u32[]{:S(2)}) %collective-permute-start.18) | collective-permute-done | bytes 98336 | tf_op jit(solution)/shard_map/ppermute | solution.py:655
  68.1 2.4 %expert.1 = (bf16[32,1536]{1,0:T(8,128)(2,1)S(1)}, bf16[32,1536]{1,0:T(8,128)(2,1)S(1)}) custom-call(bf16[32,1536]{1,0:T(8,128)(2,1)S(1)} %get-tuple-element.89.own, bf16[32,1536]{1,0:T(8,128)(2,1)S(1)} %collective-permute-done.18.other, bf16[576,512]{1,0:T(8,128)(2,1)S(1)} %get-tuple-element.50.refs_0_, bf16[576,512]{1,0:T(8,128)(2,1)S(1)} %copy-done.1, ...), custom_call_target="tpu_custom_call" | custom-call | flops 1 | bytes 9437184 | tf_op jit(solution)/shard_map/expert/pallas_call | solution.py:479
  70.5 1.5 %collective-permute-start.23 = (bf16[32,1536]{1,0:T(8,128)(2,1)S(1)}, bf16[32,1536]{1,0:T(8,128)(2,1)S(1)}, u32[]{:S(2)}, u32[]{:S(2)}) collective-permute-start(bf16[32,1536]{1,0:T(8,128)(2,1)S(1)} %get-tuple-element.93), channel_id=1, source_target_pairs={{0,1},{1,0},{2,3},{3,2},{4,5},{5,4},{6,7},{7,6},{8,9},{9,8},{10,11... | collective-permute-start | bytes 294920 | tf_op jit(solution)/shard_map/ppermute | solution.py:662
  72.1 3.3 %write.1 = bf16[512,4,128]{2,1,0:T(4,128)(2,1)} custom-call(bf16[16,144,128]{2,1,0:T(8,128)(2,1)S(1)} %all-to-all-done.arrived, bf16[512,4,128]{2,1,0:T(4,128)(2,1)S(1)} %copy-done.3), custom_call_target="tpu_custom_call" | custom-call | flops 1 | bytes 2097152 | tf_op jit(solution)/shard_map/write/pallas_call | solution.py:577
  75.4 1.1 %combine.1 = bf16[128,1536]{1,0:T(8,128)(2,1)} custom-call(bf16[128,1536]{1,0:T(8,128)(2,1)S(1)} %get-tuple-element.81.residual, f32[128,40]{1,0:T(8,128)S(1)} %get-tuple-element.85.gates, bf16[128,64]{1,0:T(8,128)(2,1)S(1)} %get-tuple-element.86.spread, bf16[32,1536]{1,0:T(8,128)(2,1)S(1)} %get-tuple-element.92.own, ...), custom_call_target="tpu_custom_call" | custom-call | flops 1 | bytes 1179648 | tf_op jit(solution)/shard_map/combine/pallas_call | solution.py:511
  (55 shorter events, 7.4 us)
Async XLA Ops:
  0.6 2.3 %collective-permute-start.2 = (bf16[96,1536]{1,0:T(8,128)(2,1)}, bf16[96,1536]{1,0:T(8,128)(2,1)S(1)}, u32[]{:S(2)}, u32[]{:S(2)}) collective-permute-start(bf16[96,1536]{1,0:T(8,128)(2,1)} %bitcast.13), channel_id=1, source_target_pairs={{0,2},{2,0},{4,6},{6,4},{8,10},{10,8},{12,14},{14,12},{16,18},{18,... | collective-permute-start | bytes 884744 | tf_op jit(solution)/shard_map/ppermute | solution.py:617
  0.7 2.2 %collective-permute-start = (bf16[96,1024]{1,0:T(8,128)(2,1)}, bf16[96,1024]{1,0:T(8,128)(2,1)S(1)}, u32[]{:S(2)}, u32[]{:S(2)}) collective-permute-start(bf16[96,1024]{1,0:T(8,128)(2,1)} %bitcast.15), channel_id=1, source_target_pairs={{0,2},{2,0},{4,6},{6,4},{8,10},{10,8},{12,14},{14,12},{16,18},{18,... | collective-permute-start | bytes 589832 | tf_op jit(solution)/shard_map/ppermute | solution.py:617
  1.2 1.7 %collective-permute-start.1 = (bf16[32,1536]{1,0:T(8,128)(2,1)}, bf16[32,1536]{1,0:T(8,128)(2,1)S(1)}, u32[]{:S(2)}, u32[]{:S(2)}) collective-permute-start(bf16[32,1536]{1,0:T(8,128)(2,1)} %bitcast.18), channel_id=1, source_target_pairs={{0,2},{2,0},{4,6},{6,4},{8,10},{10,8},{12,14},{14,12},{16,18},{18,... | collective-permute-start | bytes 294920 | tf_op jit(solution)/shard_map/ppermute | solution.py:617
  1.3 11.7 %collective-permute-start.5 = (bf16[128,1536]{1,0:T(8,128)(2,1)}, bf16[128,1536]{1,0:T(8,128)(2,1)S(1)}, u32[]{:S(2)}, u32[]{:S(2)}) collective-permute-start(bf16[128,1536]{1,0:T(8,128)(2,1)} %tokens.1), channel_id=1, source_target_pairs={{0,1},{1,0},{2,3},{3,2},{4,5},{5,4},{6,7},{7,6},{8,9},{9,8},{10,11... | collective-permute-start | bytes 1179656 | tf_op jit(solution)/shard_map/ppermute | solution.py:614
  4.1 8.9 %collective-permute-start.4 = (bf16[192,768]{1,0:T(8,128)(2,1)S(1)}, bf16[192,768]{1,0:T(8,128)(2,1)S(1)}, u32[]{:S(2)}, u32[]{:S(2)}) collective-permute-start(bf16[192,768]{1,0:T(8,128)(2,1)S(1)} %get-tuple-element.51.refs_0_), channel_id=1, source_target_pairs={{0,8},{2,6},{8,16},{10,2},{16,24},{18,10},{24,28},{26,18},{28,20},... | collective-permute-start | bytes 884744 | tf_op jit(solution)/shard_map/ppermute | solution.py:70
  5.7 13.0 %collective-permute-start.3 = (bf16[576,512]{1,0:T(8,128)(2,1)S(1)}, bf16[576,512]{1,0:T(8,128)(2,1)S(1)}, u32[]{:S(2)}, u32[]{:S(2)}) collective-permute-start(bf16[576,512]{1,0:T(8,128)(2,1)S(1)} %get-tuple-element.50.refs_0_), channel_id=1, source_target_pairs={{0,8},{2,6},{8,16},{10,2},{16,24},{18,10},{24,28},{26,18},{28,20},... | collective-permute-start | bytes 1769480 | tf_op jit(solution)/shard_map/ppermute | solution.py:70
  10.2 4.3 %copy-start.4 = (bf16[128,1536]{1,0:T(8,128)(2,1)S(1)}, bf16[128,1536]{1,0:T(8,128)(2,1)}, u32[]{:S(2)}) copy-start(bf16[128,1536]{1,0:T(8,128)(2,1)} %tokens.1) | copy-start | bytes 1179652
  10.2 4.3 %copy-start.10 = (bf16[1536,768]{1,0:T(8,128)(2,1)S(1)}, bf16[1536,768]{1,0:T(8,128)(2,1)}, u32[]{:S(2)}) copy-start(bf16[1536,768]{1,0:T(8,128)(2,1)} %w_query.1) | copy-start | bytes 7077892
  13.0 11.0 %collective-permute-start.7 = (bf16[192,768]{1,0:T(8,128)(2,1)S(1)}, bf16[192,768]{1,0:T(8,128)(2,1)S(1)}, u32[]{:S(2)}, u32[]{:S(2)}) collective-permute-start(bf16[192,768]{1,0:T(8,128)(2,1)S(1)} %collective-permute-done.4.refs_1_), channel_id=1, source_target_pairs={{0,8},{2,6},{8,16},{10,2},{16,24},{18,10},{24,28},{26,18},{28,20},... | collective-permute-start | bytes 884744 | tf_op jit(solution)/shard_map/ppermute | solution.py:70
  16.8 7.2 %collective-permute-start.8 = (bf16[128,512]{1,0:T(8,128)(2,1)S(1)}, bf16[128,512]{1,0:T(8,128)(2,1)S(1)}, u32[]{:S(2)}, u32[]{:S(2)}) collective-permute-start(bf16[128,512]{1,0:T(8,128)(2,1)S(1)} %get-tuple-element.63), channel_id=1, source_target_pairs={{0,2},{2,4},{4,6},{6,8},{8,10},{10,12},{12,14},{14,16},{16,18},{18... | collective-permute-start | bytes 393224 | tf_op jit(solution)/shard_map/ppermute | solution.py:632
  18.7 18.3 %collective-permute-start.6 = (bf16[576,512]{1,0:T(8,128)(2,1)S(1)}, bf16[576,512]{1,0:T(8,128)(2,1)}, u32[]{:S(2)}, u32[]{:S(2)}) collective-permute-start(bf16[576,512]{1,0:T(8,128)(2,1)S(1)} %collective-permute-done.3.refs_1_), channel_id=1, source_target_pairs={{0,8},{2,6},{8,16},{10,2},{16,24},{18,10},{24,28},{26,18},{28,20},... | collective-permute-start | bytes 1769480 | tf_op jit(solution)/shard_map/ppermute | solution.py:70
  24.0 7.9 %collective-permute-start.9 = (bf16[192,768]{1,0:T(8,128)(2,1)S(1)}, bf16[192,768]{1,0:T(8,128)(2,1)S(1)}, u32[]{:S(2)}, u32[]{:S(2)}) collective-permute-start(bf16[192,768]{1,0:T(8,128)(2,1)S(1)} %collective-permute-done.7.refs_2_), channel_id=1, source_target_pairs={{0,8},{2,6},{8,16},{10,2},{16,24},{18,10},{24,28},{26,18},{28,20},... | collective-permute-start | bytes 884744 | tf_op jit(solution)/shard_map/ppermute | solution.py:70
  31.8 5.2 %collective-permute-start.10 = (bf16[96,768]{1,0:T(8,128)(2,1)S(1)}, bf16[96,768]{1,0:T(8,128)(2,1)S(1)}, u32[]{:S(2)}, u32[]{:S(2)}) collective-permute-start(bf16[96,768]{1,0:T(8,128)(2,1)S(1)} %slice.6), channel_id=1, source_target_pairs={{0,8},{2,6},{8,16},{10,2},{16,24},{18,10},{24,28},{26,18},{28,20},... | collective-permute-start | bytes 442376 | tf_op jit(solution)/shard_map/ppermute | solution.py:70
  37.0 13.6 %collective-permute-start.11 = (bf16[576,512]{1,0:T(8,128)(2,1)}, bf16[576,512]{1,0:T(8,128)(2,1)S(1)}, u32[]{:S(2)}, u32[]{:S(2)}) collective-permute-start(bf16[576,512]{1,0:T(8,128)(2,1)} %collective-permute-done.6.refs_2_), channel_id=1, source_target_pairs={{0,8},{2,6},{8,16},{10,2},{16,24},{18,10},{24,28},{26,18},{28,20},... | collective-permute-start | bytes 1769480 | tf_op jit(solution)/shard_map/ppermute | solution.py:70
  38.5 33.5 %all-to-all-start = ((bf16[16,144,128]{2,1,0:T(8,128)(2,1)}), bf16[16,144,128]{2,1,0:T(8,128)(2,1)S(1)}, u32[]{:S(2)}, u32[]{:S(2)}) async-start(bf16[16,144,128]{2,1,0:T(8,128)(2,1)} %copy-done.2), calls=%async_computation | async-start | bytes 1179648 | tf_op jit(solution)/shard_map/all_to_all | solution.py:640
  43.4 1.6 %collective-permute-start.12 = (bf16[192,768]{1,0:T(8,128)(2,1)S(1)}, bf16[192,768]{1,0:T(8,128)(2,1)S(1)}, u32[]{:S(2)}, u32[]{:S(2)}) collective-permute-start(bf16[192,768]{1,0:T(8,128)(2,1)S(1)} %collective-permute-done.4.refs_1_), channel_id=1, source_target_pairs={{0,2},{2,0},{4,6},{6,4},{8,10},{10,8},{12,14},{14,12},{16,18},{18,... | collective-permute-start | bytes 884744 | tf_op jit(solution)/shard_map/ppermute | solution.py:79
  43.5 1.9 %collective-permute-start.13 = (bf16[192,768]{1,0:T(8,128)(2,1)S(1)}, bf16[192,768]{1,0:T(8,128)(2,1)S(1)}, u32[]{:S(2)}, u32[]{:S(2)}) collective-permute-start(bf16[192,768]{1,0:T(8,128)(2,1)S(1)} %collective-permute-done.7.refs_2_), channel_id=1, source_target_pairs={{0,2},{2,0},{4,6},{6,4},{8,10},{10,8},{12,14},{14,12},{16,18},{18,... | collective-permute-start | bytes 884744 | tf_op jit(solution)/shard_map/ppermute | solution.py:79
  43.9 1.9 %collective-permute-start.14 = (bf16[192,768]{1,0:T(8,128)(2,1)S(1)}, bf16[192,768]{1,0:T(8,128)(2,1)S(1)}, u32[]{:S(2)}, u32[]{:S(2)}) collective-permute-start(bf16[192,768]{1,0:T(8,128)(2,1)S(1)} %collective-permute-done.9.refs_3_), channel_id=1, source_target_pairs={{0,2},{2,0},{4,6},{6,4},{8,10},{10,8},{12,14},{14,12},{16,18},{18,... | collective-permute-start | bytes 884744 | tf_op jit(solution)/shard_map/ppermute | solution.py:79
  44.0 2.0 %collective-permute-start.15 = (bf16[96,768]{1,0:T(8,128)(2,1)S(1)}, bf16[96,768]{1,0:T(8,128)(2,1)S(1)}, u32[]{:S(2)}, u32[]{:S(2)}) collective-permute-start(bf16[96,768]{1,0:T(8,128)(2,1)S(1)} %collective-permute-done.10.refs_7_), channel_id=1, source_target_pairs={{0,2},{2,0},{4,6},{6,4},{8,10},{10,8},{12,14},{14,12},{16,18},{18,... | collective-permute-start | bytes 442376 | tf_op jit(solution)/shard_map/ppermute | solution.py:79
  47.2 4.9 %copy-start.1 = (bf16[576,512]{1,0:T(8,128)(2,1)S(1)}, bf16[576,512]{1,0:T(8,128)(2,1)}, u32[]{:S(2)}) copy-start(bf16[576,512]{1,0:T(8,128)(2,1)} %copy-done) | copy-start | bytes 1769476
  47.2 11.2 %copy-start.5 = (bf16[128,1536]{1,0:T(8,128)(2,1)S(1)}, bf16[128,1536]{1,0:T(8,128)(2,1)}, u32[]{:S(2)}) copy-start(bf16[128,1536]{1,0:T(8,128)(2,1)} %tokens.1) | copy-start | bytes 1179652
  47.2 11.2 %collective-permute-start.16 = (bf16[128,1536]{1,0:T(8,128)(2,1)S(1)}, bf16[128,1536]{1,0:T(8,128)(2,1)S(1)}, u32[]{:S(2)}, u32[]{:S(2)}) collective-permute-start(bf16[128,1536]{1,0:T(8,128)(2,1)S(1)} %outward_send.1), channel_id=1, source_target_pairs={{0,1},{1,0},{2,3},{3,2},{4,5},{5,4},{6,7},{7,6},{8,9},{9,8},{10,11... | collective-permute-start | bytes 1179656 | tf_op jit(solution)/shard_map/ppermute | solution.py:647
  49.9 9.0 %copy-start.7 = (bf16[40,1536]{1,0:T(8,128)(2,1)S(1)}, bf16[40,1536]{1,0:T(8,128)(2,1)}, u32[]{:S(2)}) copy-start(bf16[40,1536]{1,0:T(8,128)(2,1)} %copy-done.6) | copy-start | bytes 368644
  49.9 9.0 %copy-start.9 = (f32[128,40]{1,0:T(8,128)S(1)}, f32[128,40]{1,0:T(8,128)}, u32[]{:S(2)}) copy-start(f32[128,40]{1,0:T(8,128)} %copy-done.8) | copy-start | bytes 61444
  50.7 12.3 %collective-permute-start.17 = (bf16[288,512]{1,0:T(8,128)(2,1)S(1)}, bf16[288,512]{1,0:T(8,128)(2,1)S(1)}, u32[]{:S(2)}, u32[]{:S(2)}) collective-permute-start(bf16[288,512]{1,0:T(8,128)(2,1)S(1)} %slice.7), channel_id=1, source_target_pairs={{0,8},{2,6},{8,16},{10,2},{16,24},{18,10},{24,28},{26,18},{28,20},... | collective-permute-start | bytes 884744 | tf_op jit(solution)/shard_map/ppermute | solution.py:70
  52.1 12.4 %collective-permute-start.19 = (bf16[576,512]{1,0:T(8,128)(2,1)S(1)}, bf16[576,512]{1,0:T(8,128)(2,1)S(1)}, u32[]{:S(2)}, u32[]{:S(2)}) collective-permute-start(bf16[576,512]{1,0:T(8,128)(2,1)S(1)} %copy-done.1), channel_id=1, source_target_pairs={{0,2},{2,0},{4,6},{6,4},{8,10},{10,8},{12,14},{14,12},{16,18},{18,... | collective-permute-start | bytes 1769480 | tf_op jit(solution)/shard_map/ppermute | solution.py:79
  52.1 12.4 %collective-permute-start.20 = (bf16[576,512]{1,0:T(8,128)(2,1)}, bf16[576,512]{1,0:T(8,128)(2,1)S(1)}, u32[]{:S(2)}, u32[]{:S(2)}) collective-permute-start(bf16[576,512]{1,0:T(8,128)(2,1)} %collective-permute-done.6.refs_2_), channel_id=1, source_target_pairs={{0,2},{2,0},{4,6},{6,4},{8,10},{10,8},{12,14},{14,12},{16,18},{18,... | collective-permute-start | bytes 1769480 | tf_op jit(solution)/shard_map/ppermute | solution.py:79
  52.6 15.6 %collective-permute-start.21 = (bf16[576,512]{1,0:T(8,128)(2,1)S(1)}, bf16[576,512]{1,0:T(8,128)(2,1)S(1)}, u32[]{:S(2)}, u32[]{:S(2)}) collective-permute-start(bf16[576,512]{1,0:T(8,128)(2,1)S(1)} %collective-permute-done.11.refs_3_), channel_id=1, source_target_pairs={{0,2},{2,0},{4,6},{6,4},{8,10},{10,8},{12,14},{14,12},{16,18},{18,... | collective-permute-start | bytes 1769480 | tf_op jit(solution)/shard_map/ppermute | solution.py:79
  62.9 5.2 %collective-permute-start.22 = (bf16[288,512]{1,0:T(8,128)(2,1)S(1)}, bf16[288,512]{1,0:T(8,128)(2,1)S(1)}, u32[]{:S(2)}, u32[]{:S(2)}) collective-permute-start(bf16[288,512]{1,0:T(8,128)(2,1)S(1)} %collective-permute-done.17.refs_7_), channel_id=1, source_target_pairs={{0,2},{2,0},{4,6},{6,4},{8,10},{10,8},{12,14},{14,12},{16,18},{18,... | collective-permute-start | bytes 884744 | tf_op jit(solution)/shard_map/ppermute | solution.py:79
  62.9 9.2 %copy-start.3 = (bf16[512,4,128]{2,1,0:T(4,128)(2,1)S(1)}, bf16[512,4,128]{2,1,0:T(4,128)(2,1)}, u32[]{:S(2)}) copy-start(bf16[512,4,128]{2,1,0:T(4,128)(2,1)} %cache.1) | copy-start | bytes 1572868
  62.9 5.2 %collective-permute-start.18 = (bf16[32,1536]{1,0:T(8,128)(2,1)S(1)}, bf16[32,1536]{1,0:T(8,128)(2,1)S(1)}, u32[]{:S(2)}, u32[]{:S(2)}) collective-permute-start(bf16[32,1536]{1,0:T(8,128)(2,1)S(1)} %get-tuple-element.90), channel_id=1, source_target_pairs={{0,1},{1,0},{2,3},{3,2},{4,5},{5,4},{6,7},{7,6},{8,9},{9,8},{10,11... | collective-permute-start | bytes 294920 | tf_op jit(solution)/shard_map/ppermute | solution.py:655
  70.5 4.8 %collective-permute-start.23 = (bf16[32,1536]{1,0:T(8,128)(2,1)S(1)}, bf16[32,1536]{1,0:T(8,128)(2,1)S(1)}, u32[]{:S(2)}, u32[]{:S(2)}) collective-permute-start(bf16[32,1536]{1,0:T(8,128)(2,1)S(1)} %get-tuple-element.93), channel_id=1, source_target_pairs={{0,1},{1,0},{2,3},{3,2},{4,5},{5,4},{6,7},{7,6},{8,9},{9,8},{10,11... | collective-permute-start | bytes 294920 | tf_op jit(solution)/shard_map/ppermute | solution.py:662
  (4 other events, 4.2 us)

commit v7 on v6

--- a/solution.py
+++ b/solution.py
@@ -74,8 +74,8 @@
         self.mine[-1] = done[0]
         return done[1:] if len(others) > 1 else done[1]
 
-    def share(self):
-        for index in range(1 + len(self.near), len(self.mine)):
+    def share(self, upto=None):
+        for index in range(1 + len(self.near), 1 + (upto or len(self.mine) - 1)):
             self.near.append(self.beside(self.mine[index]))
 
     def parts(self):
@@ -104,8 +104,8 @@
 LITTLE = pl.CostEstimate(flops=1, bytes_accessed=1, transcendentals=0)
 
 
-def takes(us):
-    return pl.CostEstimate(flops=int(us * 1.15e9), bytes_accessed=1, transcendentals=0)
+def takes(us, nbytes=1):
+    return pl.CostEstimate(flops=int(us * 1.15e9), bytes_accessed=nbytes, transcendentals=0)
 
 
 def reads(nbytes):
@@ -173,13 +173,19 @@
     return jnp.sum(jnp.where(eye, row, 0.0), axis=1, keepdims=True)
 
 
+def named_experts(ids, experts):
+    tokens = ids.shape[1]
+    expert = lax.broadcasted_iota(jnp.int32, (experts, tokens), 0)
+    hit = jnp.zeros((experts, tokens), f32)
+    for index in range(ids.shape[0]):
+        hit = jnp.where(ids[index : index + 1, :] == expert, 1.0, hit)
+    return hit
+
+
 def prepare_kernel(groups, slots_dev, *refs):
-    sources, (cosine, sine, past, named, place, spread, send, tags, gain, late_gain, router) = (
-        refs[:6],
-        refs[6:17],
-    )
-    positions, slots, ids, flat_gains, flat_late, sems = refs[17:]
-    copies = fetch(list(zip(sources, (positions, slots, ids, flat_gains, flat_late, router))), sems)
+    sources, (cosine, sine, past, place, spread, send, tags, gain, late_gain) = refs[:5], refs[5:14]
+    positions, slots, ids, flat_gains, flat_late, sems = refs[14:]
+    copies = fetch(list(zip(sources, (positions, slots, ids, flat_gains, flat_late))), sems)
     for copy in copies:
         copy.wait()
     gain[...] = flat_gains[...].reshape(gain.shape)
@@ -202,16 +208,11 @@
     sine[...] = jnp.where(iota(angles.shape, 1) % 64 < 32, -turned, turned)
 
     tokens = ids.shape[1]
-    experts = named.shape[1]
     cap = place.shape[0] // 2
-    expert = iota((experts, tokens), 0)
-    hit = jnp.zeros((experts, tokens), f32)
-    for index in range(ids.shape[0]):
-        hit = jnp.where(ids[index : index + 1, :] == expert, 1.0, hit)
+    hit = named_experts(ids, 8)
     small_eye = (iota((tokens, tokens), 0) == iota((tokens, tokens), 1)).astype(f32)
-    named[...] = lax.dot_general(small_eye, hit, LAST_DIMS, preferred_element_type=f32)
     upto = (iota((tokens, tokens), 0) <= iota((tokens, tokens), 1)).astype(f32)
-    rank = jnp.dot(hit[:8, :], upto, preferred_element_type=f32) - 1.0
+    rank = jnp.dot(hit, upto, preferred_element_type=f32) - 1.0
     slot = iota((2 * cap, tokens), 0).astype(f32)
     placed = jnp.zeros((2 * cap, tokens), f32)
     for live in range(2):
@@ -237,29 +238,27 @@
     tags[...] = jnp.where(spot == 0, high, jnp.where(spot == 1, low, 0.0)).astype(bf16)
 
 
-def prepare(groups, slots_dev, positions, slots, ids, gain, late_gain, router):
+def prepare(groups, slots_dev, positions, slots, ids, gain, late_gain):
     block, tokens = positions.shape[0], ids.shape[0]
-    model, experts = router.shape
+    model = gain.shape[0]
     cap = tokens // 4
     capc = 2 * block // groups
     shapes = [
         ((block, 128), f32),
         ((block, 128), f32),
         ((block, 128), f32),
-        ((tokens, experts), f32),
         ((2 * cap, tokens), bf16),
         ((tokens, 2 * cap), bf16),
         ((groups * capc, block), bf16),
         ((block, 128), bf16),
         ((1, model), f32),
         ((1, model), f32),
-        ((experts, model), bf16),
     ]
-    sources = (positions[None], slots[None], ids.T, gain, late_gain, router.T)
+    sources = (positions[None], slots[None], ids.T, gain, late_gain)
     return pl.pallas_call(
         functools.partial(prepare_kernel, groups, slots_dev),
         out_shape=tuple(jax.ShapeDtypeStruct(shape, kind) for shape, kind in shapes),
-        in_specs=[ANY] * 6,
+        in_specs=[ANY] * 5,
         out_specs=(VMEM,) * len(shapes),
         scratch_shapes=[
             pltpu.VMEM((1, block), jnp.int32),
@@ -267,7 +266,7 @@
             pltpu.VMEM(ids.shape[::-1], jnp.int32),
             pltpu.VMEM((model,), f32),
             pltpu.VMEM((model,), f32),
-            pltpu.SemaphoreType.DMA((6,)),
+            pltpu.SemaphoreType.DMA((5,)),
         ],
         compiler_params=PARAMS,
         cost_estimate=LITTLE,
@@ -423,33 +422,38 @@
         in_specs=[VMEM] * 5,
         out_specs=(VMEM,) * 3,
         compiler_params=PARAMS,
-        cost_estimate=reads(10 * tokens.shape[0] * tokens.shape[1]),
+        cost_estimate=takes(2, 10 * tokens.shape[0] * tokens.shape[1]),
         name="route",
     )(tokens, mine, arrived, gain, place)
 
 
-def gate_kernel(moe_in, router, named, place, gates, own):
+def gate_kernel(moe_in, router, ids, place, gates, own):
     cap = own.shape[0]
     own[...] = jnp.dot(place[:cap, :], moe_in[...], preferred_element_type=f32).astype(bf16)
+    hit = named_experts(ids, router.shape[0])
+    tokens = ids.shape[1]
+    row = lax.broadcasted_iota(jnp.int32, (tokens, tokens), 0)
+    eye = (row == lax.broadcasted_iota(jnp.int32, (tokens, tokens), 1)).astype(f32)
+    named = lax.dot_general(eye, hit, LAST_DIMS, preferred_element_type=f32)
     logits = lax.dot_general(moe_in[...], router[...], LAST_DIMS, preferred_element_type=f32)
-    raised = jnp.where(named[...] > 0, jnp.exp(logits), 0.0)
+    raised = jnp.where(named > 0, jnp.exp(logits), 0.0)
     gates[...] = raised / jnp.sum(raised, axis=-1, keepdims=True)
 
 
-def gate(moe_in, router_t, named, place):
+def gate(moe_in, router_t, ids_t, place):
     cap = place.shape[0] // 2
     return pl.pallas_call(
         gate_kernel,
         out_shape=(
-            jax.ShapeDtypeStruct(named.shape, f32),
+            jax.ShapeDtypeStruct((moe_in.shape[0], router_t.shape[0]), f32),
             jax.ShapeDtypeStruct((cap, moe_in.shape[1]), bf16),
         ),
         in_specs=[VMEM] * 4,
         out_specs=(VMEM,) * 2,
         compiler_params=PARAMS,
-        cost_estimate=reads(1 << 20),
+        cost_estimate=LITTLE,
         name="gate",
-    )(moe_in, router_t, named, place)
+    )(moe_in, router_t, ids_t, place)
 
 
 def expert_kernel(groups, up_rows, down_rows, n_parts, own, other, *refs):
@@ -622,39 +626,45 @@
     expert_ring.step()
     w_keyval, positions = together((w_keyval, positions, out_pair))[:2]
     flat_kv = w_keyval.reshape(model, kv_width)
-    cosine, sine, past, named, place, spread, send, tags, gain, late_gain, router_t = prepare(
-        groups, slots_dev, positions, cache_slot, expert_ids, attn_gain, moe_gain, router
+    cosine, sine, past, place, spread, send, tags, gain, late_gain = prepare(
+        groups, slots_dev, positions, cache_slot, expert_ids, attn_gain, moe_gain
     )
     other_tokens, cosine, flat_kv = out_ring.pin(other_tokens, cosine, flat_kv)
     out_ring.step()
 
     q, kv, tail = project(tokens, other_tokens, gain, cosine, sine, w_query, flat_kv)
     seam = lax.ppermute(tail, "grp", [(g, g + 1) for g in range(groups - 1)])
-    kv_now = expert_ring.pin(kv)
+    kv_now = out_ring.pin(kv)
+    out_ring.step()
+    kv_now = expert_ring.pin(kv_now)
     expert_ring.step()
     outgoing = bundle(groups, send, kv_now, tags)
-    seam, outgoing = out_ring.pin(seam, outgoing)
-    out_ring.step()
+    seam, outgoing = together((seam, outgoing))
+    out_ring.share(2)
     mixed = attend(q, kv, seam, past)
-    outgoing, mixed = together((outgoing, mixed))
-    arrived_cache = lax.all_to_all(outgoing, "grp", split_axis=0, concat_axis=0, tiled=True)
+    mixed, out_ring.near = together((mixed, out_ring.near))
     mixed = out_ring.pin(mixed)
     out_ring.step()
-    out_ring.mine[-1] = expert_ring.pin(out_ring.mine[-1])
+    out_ring.share(3)
+    mixed, out_ring.near = together((mixed, out_ring.near))
+    mixed = out_ring.pin(mixed)
     out_ring.share()
-    expert_ring.step()
     sent = outward(True, bf16, groups, mixed, out_ring.parts(), out_ring.unit_rows)
     arrived = swap(sent)
-    mixed = together((mixed, sent))[0]
+    mixed, outgoing = together((mixed, outgoing, sent))[:2]
     mine = outward(False, f32, groups, mixed, out_ring.parts(), out_ring.unit_rows)
+    arrived_cache = lax.all_to_all(outgoing, "grp", split_axis=0, concat_axis=0, tiled=True)
     mine = expert_ring.pin(mine)
     expert_ring.share()
     expert_ring.step()
 
     residual, moe_in, sent_rows = route(tokens, mine, arrived, late_gain, place)
     landed = swap(sent_rows)
-    gates, own_rows = gate(moe_in, router_t, named, place)
-    own_rows = expert_ring.pin(own_rows)
+    moe_in = expert_ring.pin(moe_in)
+    expert_ring.share()
+    expert_ring.step()
+    gates, own_rows = gate(moe_in, router.T, expert_ids.T, place)
+    landed, own_rows = expert_ring.pin(landed, own_rows)
     expert_ring.share()
     own_made, back = expert(
         groups, own_rows, landed, expert_ring.parts(), up_rows, down_rows

time: 76.8 us -> 77.8 us (1.013)
  starting transfers between devices: 27.4 us -> 23.1 us
  waiting for transfers between devices: 25.9 us -> 28 us
  local copies, waits for them, and re-layouts: 4.02 us -> 5.61 us
  Pallas kernels: 18.3 us -> 19.8 us
    ppermute x1, waiting for transfers between devices: 5.83 us -> 2.32 us  [two_lane_shards(): arrived = swap(sent)]
    ppermute x8, waiting for transfers between devices: 11.4 us -> 14 us  [step(): self.mine.append(self.across(held))]
    ppermute x8, waiting for transfers between devices: 1.62 us -> 4.18 us  [share(): self.near.append(self.beside(self.mine[index]))]
    ppermute x1, waiting for transfers between devices: 2.27 us -> 0.67 us  [two_lane_shards(): seam = lax.ppermute(tail, 'grp', [(g, g + 1) for g in range(groups - 1)])]
    unnamed x23, local copies, waits for them, and re-layouts: 3.99 us -> 5.58 us
    ppermute x1, waiting for transfers between devices: 0.01 us -> 1.24 us  [two_lane_shards(): returned = swap(back)]
    ppermute x8, starting transfers between devices: 12.4 us -> 11.2 us  [step(): self.mine.append(self.across(held))]
    pallas_call x1, Pallas kernels: 0.46 us -> 1.47 us  [route(): pl.pallas_call(route_kernel, out_shape=(jax.ShapeDtypeStruct(tokens.shape...]
  transfers between devices with their start and end apart: 25 -> 25, of which waited for: 13 -> 13; matrix products, arithmetic and copies ran while one was open for 2% -> 2% of each run, Pallas kernels for 22% -> 24%
where the time goes in v7:
time: 77.8 us; the launch traced here: 77.4 us
  waiting for transfers between devices  28 us (36%)
  starting transfers between devices  23.1 us (30%)
  Pallas kernels  19.8 us (25%)
  local copies, waits for them, and re-layouts  5.61 us (7%)
  between operations  0.83 us (1%)
    ppermute x8, waiting for transfers between devices, step(): self.mine.append(self.across(held))  14 us
    ppermute x8, starting transfers between devices, step(): self.mine.append(self.across(held))  11.2 us
    unnamed x23, local copies, waits for them, and re-layouts  5.58 us
    all_to_all x1, starting transfers between devices, two_lane_shards(): lax.all_to_all(outgoing, 'grp', split_axis=0, concat_axis=0, tiled=True)  4.7 us
    ppermute x1, waiting for transfers between devices, two_lane_shards(): landed = swap(sent_rows)  4.26 us
    ppermute x8, waiting for transfers between devices, share(): self.near.append(self.beside(self.mine[index]))  4.18 us
    pallas_call x1, Pallas kernels, write(): pl.pallas_call(write_kernel, out_shape=jax.ShapeDtypeStruct(cache.shape,...  3.27 us
    pallas_call x1, Pallas kernels, expert(): pl.pallas_call(functools.partial(expert_kernel, groups, up_rows, down_row...  3.02 us
  transfers between devices with their start and end apart: 25, of which 13 were waited for; matrix products, arithmetic and copies ran while one was open for 2% of the time, Pallas kernels for 24%

profile of v7, /device:TPU:16, one launch (start us, length us, event | category | flops | bytes accessed | tf_op | source)
XLA Modules:
  0.0 77.4 jit_solution(7240906471832716093)
XLA Ops:
  1.3 1.5 %collective-permute-start.5 = (bf16[128,1536]{1,0:T(8,128)(2,1)}, bf16[128,1536]{1,0:T(8,128)(2,1)S(1)}, u32[]{:S(2)}, u32[]{:S(2)}) collective-permute-start(bf16[128,1536]{1,0:T(8,128)(2,1)} %tokens.1), channel_id=1, source_target_pairs={{0,1},{1,0},{2,3},{3,2},{4,5},{5,4},{6,7},{7,6},{8,9},{9,8},{10,11... | collective-permute-start | bytes 1179656 | tf_op jit(solution)/shard_map/ppermute | solution.py:618
  2.9 1.1 %pack.1 = (bf16[576,512]{1,0:T(8,128)(2,1)S(1)}, bf16[192,768]{1,0:T(8,128)(2,1)S(1)}) custom-call(bf16[96,1024]{1,0:T(8,128)(2,1)} %bitcast.19, bf16[32,1536]{1,0:T(8,128)(2,1)} %bitcast.21, bf16[96,1536]{1,0:T(8,128)(2,1)} %bitcast.17, bf16[96,1024]{1,0:T(8,128)(2,1)S(1)} %collective-permute-done.refs_3_, ...), custom_call_target="tpu_custom_call" | custom-call | flops 1 | bytes 1 | tf_op jit(solution)/shard_map/pack/pallas_call | solution.py:157
  4.1 1.6 %collective-permute-start.4 = (bf16[192,768]{1,0:T(8,128)(2,1)S(1)}, bf16[192,768]{1,0:T(8,128)(2,1)S(1)}, u32[]{:S(2)}, u32[]{:S(2)}) collective-permute-start(bf16[192,768]{1,0:T(8,128)(2,1)S(1)} %get-tuple-element.59.refs_0_), channel_id=1, source_target_pairs={{0,8},{2,6},{8,16},{10,2},{16,24},{18,10},{24,28},{26,18},{28,20},... | collective-permute-start | bytes 884744 | tf_op jit(solution)/shard_map/ppermute | solution.py:70
  5.7 1.5 %collective-permute-start.3 = (bf16[576,512]{1,0:T(8,128)(2,1)S(1)}, bf16[576,512]{1,0:T(8,128)(2,1)S(1)}, u32[]{:S(2)}, u32[]{:S(2)}) collective-permute-start(bf16[576,512]{1,0:T(8,128)(2,1)S(1)} %get-tuple-element.58.refs_0_), channel_id=1, source_target_pairs={{0,8},{2,6},{8,16},{10,2},{16,24},{18,10},{24,28},{26,18},{28,20},... | collective-permute-start | bytes 1769480 | tf_op jit(solution)/shard_map/ppermute | solution.py:70
  7.2 1.5 %prepare.1 = (f32[256,128]{1,0:T(8,128)S(1)}, f32[256,128]{1,0:T(8,128)S(1)}, f32[256,128]{1,0:T(8,128)S(1)}, bf16[64,128]{1,0:T(8,128)(2,1)S(1)}, bf16[128,64]{...) custom-call(s32[1,256]{1,0:T(1,128)} %bitcast.22, ...), custom_call_target="tpu_custom_call" | custom-call | flops 1 | bytes 1 | tf_op jit(solution)/shard_map/prepare/pallas_call | solution.py:258
  9.9 1.8 %copy.17 = bf16[192,8,4,128]{3,1,2,0:T(8,128)(2,1)S(1)} copy(bf16[192,8,4,128]{3,2,1,0:T(4,128)(2,1)} %bitcast.15) | data formatting | bytes 3145728
  11.8 1.2 %collective-permute-done.5.other = bf16[128,1536]{1,0:T(8,128)(2,1)S(1)} collective-permute-done((bf16[128,1536]{1,0:T(8,128)(2,1)}, bf16[128,1536]{1,0:T(8,128)(2,1)S(1)}, u32[]{:S(2)}, u32[]{:S(2)}) %collective-permute-start.5) | collective-permute-done | bytes 393248 | tf_op jit(solution)/shard_map/ppermute | solution.py:618
  13.0 1.6 %collective-permute-start.6 = (bf16[192,768]{1,0:T(8,128)(2,1)S(1)}, bf16[192,768]{1,0:T(8,128)(2,1)S(1)}, u32[]{:S(2)}, u32[]{:S(2)}) collective-permute-start(bf16[192,768]{1,0:T(8,128)(2,1)S(1)} %collective-permute-done.4.refs_1_), channel_id=1, source_target_pairs={{0,8},{2,6},{8,16},{10,2},{16,24},{18,10},{24,28},{26,18},{28,20},... | collective-permute-start | bytes 884744 | tf_op jit(solution)/shard_map/ppermute | solution.py:70
  14.6 2.2 %project.1 = (bf16[256,768]{1,0:T(8,128)(2,1)S(1)}, bf16[256,512]{1,0:T(8,128)(2,1)S(1)}, bf16[128,512]{1,0:T(8,128)(2,1)S(1)}) custom-call(bf16[128,1536]{1,0:T(8,128)(2,1)S(1)} %copy-done.7, bf16[128,1536]{1,0:T(8,128)(2,1)S(1)} %collective-permute-done.5.other, f32[1,1536]{1,0:T(1,128)S(1)} %get-tuple-element.65.gain, ...), custom_call_target="tpu_custom_call" | custom-call | flops 9200000000 | bytes 1 | tf_op jit(solution)/shard_map/project/pallas_call | solution.py:309
  16.8 1.9 %collective-permute-start.9 = (bf16[128,512]{1,0:T(8,128)(2,1)S(1)}, bf16[128,512]{1,0:T(8,128)(2,1)S(1)}, u32[]{:S(2)}, u32[]{:S(2)}) collective-permute-start(bf16[128,512]{1,0:T(8,128)(2,1)S(1)} %get-tuple-element.74), channel_id=1, source_target_pairs={{0,2},{2,4},{4,6},{6,8},{8,10},{10,12},{12,14},{14,16},{16,18},{18... | collective-permute-start | bytes 393224 | tf_op jit(solution)/shard_map/ppermute | solution.py:636
  18.7 1.6 %collective-permute-done.6.refs_2_ = bf16[192,768]{1,0:T(8,128)(2,1)S(1)} collective-permute-done((bf16[192,768]{1,0:T(8,128)(2,1)S(1)}, bf16[192,768]{1,0:T(8,128)(2,1)S(1)}, u32[]{:S(2)}, u32[]{:S(2)}) %collective-permute-start.6) | collective-permute-done | bytes 294944 | tf_op jit(solution)/shard_map/ppermute | solution.py:70
  20.3 1.6 %collective-permute-start.8 = (bf16[192,768]{1,0:T(8,128)(2,1)S(1)}, bf16[192,768]{1,0:T(8,128)(2,1)S(1)}, u32[]{:S(2)}, u32[]{:S(2)}) collective-permute-start(bf16[192,768]{1,0:T(8,128)(2,1)S(1)} %collective-permute-done.6.refs_2_), channel_id=1, source_target_pairs={{0,8},{2,6},{8,16},{10,2},{16,24},{18,10},{24,28},{26,18},{28,20},... | collective-permute-start | bytes 884744 | tf_op jit(solution)/shard_map/ppermute | solution.py:70
  24.0 1.6 %collective-permute-start.7 = (bf16[576,512]{1,0:T(8,128)(2,1)S(1)}, bf16[576,512]{1,0:T(8,128)(2,1)}, u32[]{:S(2)}, u32[]{:S(2)}) collective-permute-start(bf16[576,512]{1,0:T(8,128)(2,1)S(1)} %collective-permute-done.3.refs_1_), channel_id=1, source_target_pairs={{0,8},{2,6},{8,16},{10,2},{16,24},{18,10},{24,28},{26,18},{28,20},... | collective-permute-start | bytes 1769480 | tf_op jit(solution)/shard_map/ppermute | solution.py:70
  25.5 2.8 %attend.1.mixed = bf16[256,768]{1,0:T(8,128)(2,1)S(1)} custom-call(bf16[256,768]{1,0:T(8,128)(2,1)S(1)} %get-tuple-element.73.q, bf16[256,512]{1,0:T(8,128)(2,1)S(1)} %get-tuple-element.76.kv, bf16[128,512]{1,0:T(8,128)(2,1)S(1)} %collective-permute-done.9.seam, f32[256,128]{1,0:T(8,128)S(1)} %get-tuple-element.79.past), custom_call_target="tpu_custom_call" | custom-call | flops 4600000000 | bytes 1 | tf_op jit(solution)/shard_map/attend/pallas_call | solution.py:362
  28.8 1.2 %collective-permute-done.13.refs_6_ = bf16[192,768]{1,0:T(8,128)(2,1)S(1)} collective-permute-done((bf16[192,768]{1,0:T(8,128)(2,1)S(1)}, bf16[192,768]{1,0:T(8,128)(2,1)S(1)}, u32[]{:S(2)}, u32[]{:S(2)}) %collective-permute-start.13) | collective-permute-done | bytes 294944 | tf_op jit(solution)/shard_map/ppermute | solution.py:79
  30.0 5.4 %collective-permute-done.12.refs_7_ = bf16[96,768]{1,0:T(8,128)(2,1)S(1)} collective-permute-done((bf16[96,768]{1,0:T(8,128)(2,1)S(1)}, bf16[96,768]{1,0:T(8,128)(2,1)S(1)}, u32[]{:S(2)}, u32[]{:S(2)}) %collective-permute-start.12) | collective-permute-done | bytes 147488 | tf_op jit(solution)/shard_map/ppermute | solution.py:70
  35.4 1.4 %collective-permute-done.14.refs_8_ = bf16[96,768]{1,0:T(8,128)(2,1)S(1)} collective-permute-done((bf16[96,768]{1,0:T(8,128)(2,1)S(1)}, bf16[96,768]{1,0:T(8,128)(2,1)S(1)}, u32[]{:S(2)}, u32[]{:S(2)}) %collective-permute-start.14) | collective-permute-done | bytes 147488 | tf_op jit(solution)/shard_map/ppermute | solution.py:79
  36.8 1.1 %outward_send.1 = bf16[128,1536]{1,0:T(8,128)(2,1)S(1)} custom-call(bf16[256,768]{1,0:T(8,128)(2,1)S(1)} %attend.1.mixed, bf16[192,768]{1,0:T(8,128)(2,1)S(1)} %get-tuple-element.59.refs_0_, bf16[192,768]{1,0:T(8,128)(2,1)S(1)} %collective-permute-done.4.refs_1_, bf16[192,768]{1,0:T(8,128)(2,1)S(1)} %collective-permute-done.6.refs_2_, ...), custom_call_target="tpu_custom_call" | custom-call | flops 1 | bytes 2359296 | tf_op jit(solution)/shard_map/outward_send/pallas_call | solution.py:392
  37.9 1.6 %collective-permute-start.15 = (bf16[128,1536]{1,0:T(8,128)(2,1)S(1)}, bf16[128,1536]{1,0:T(8,128)(2,1)}, u32[]{:S(2)}, u32[]{:S(2)}) collective-permute-start(bf16[128,1536]{1,0:T(8,128)(2,1)S(1)} %outward_send.1), channel_id=1, source_target_pairs={{0,1},{1,0},{2,3},{3,2},{4,5},{5,4},{6,7},{7,6},{8,9},{9,8},{10,11... | collective-permute-start | bytes 1179656 | tf_op jit(solution)/shard_map/ppermute | solution.py:653
  40.6 1.6 %collective-permute-start.16 = (bf16[576,512]{1,0:T(8,128)(2,1)}, bf16[576,512]{1,0:T(8,128)(2,1)S(1)}, u32[]{:S(2)}, u32[]{:S(2)}) collective-permute-start(bf16[576,512]{1,0:T(8,128)(2,1)} %collective-permute-done.7.refs_2_), channel_id=1, source_target_pairs={{0,8},{2,6},{8,16},{10,2},{16,24},{18,10},{24,28},{26,18},{28,20},... | collective-permute-start | bytes 1769480 | tf_op jit(solution)/shard_map/ppermute | solution.py:70
  42.3 4.7 %all-to-all-start = ((bf16[16,144,128]{2,1,0:T(8,128)(2,1)}), bf16[16,144,128]{2,1,0:T(8,128)(2,1)S(1)}, u32[]{:S(2)}, u32[]{:S(2)}) async-start(bf16[16,144,128]{2,1,0:T(8,128)(2,1)} %copy-done), calls=%async_computation | async-start | bytes 1179648 | tf_op jit(solution)/shard_map/all_to_all | solution.py:656
  47.0 2.3 %collective-permute-done.15.arrived = bf16[128,1536]{1,0:T(8,128)(2,1)} collective-permute-done((bf16[128,1536]{1,0:T(8,128)(2,1)S(1)}, bf16[128,1536]{1,0:T(8,128)(2,1)}, u32[]{:S(2)}, u32[]{:S(2)}) %collective-permute-start.15) | collective-permute-done | bytes 393248 | tf_op jit(solution)/shard_map/ppermute | solution.py:653
  51.0 1.5 %route.1 = (bf16[128,1536]{1,0:T(8,128)(2,1)S(1)}, bf16[128,1536]{1,0:T(8,128)(2,1)S(1)}, bf16[32,1536]{1,0:T(8,128)(2,1)S(1)}) custom-call(bf16[128,1536]{1,0:T(8,128)(2,1)S(1)} %copy-done.8, f32[128,1536]{1,0:T(8,128)S(1)} %outward_keep.1.mine, bf16[128,1536]{1,0:T(8,128)(2,1)} %collective-permute-done.15.arrived, f32[1,1536]{1,0:T(1,128)S(1)} %copy-done.10, ...), custom_call_target="tpu_custom_call" | custom-call | flops 2300000000 | bytes 1966080 | tf_op jit(solution)/shard_map/route/pallas_call | solution.py:415
  52.5 1.9 %collective-permute-done.16.refs_3_ = bf16[576,512]{1,0:T(8,128)(2,1)S(1)} collective-permute-done((bf16[576,512]{1,0:T(8,128)(2,1)}, bf16[576,512]{1,0:T(8,128)(2,1)S(1)}, u32[]{:S(2)}, u32[]{:S(2)}) %collective-permute-start.16) | collective-permute-done | bytes 589856 | tf_op jit(solution)/shard_map/ppermute | solution.py:70
  54.4 1.4 %collective-permute-start.17 = (bf16[288,512]{1,0:T(8,128)(2,1)S(1)}, bf16[288,512]{1,0:T(8,128)(2,1)S(1)}, u32[]{:S(2)}, u32[]{:S(2)}) collective-permute-start(bf16[288,512]{1,0:T(8,128)(2,1)S(1)} %slice.7), channel_id=1, source_target_pairs={{0,8},{2,6},{8,16},{10,2},{16,24},{18,10},{24,28},{26,18},{28,20},... | collective-permute-start | bytes 884744 | tf_op jit(solution)/shard_map/ppermute | solution.py:70
  57.2 4.3 %collective-permute-done.18.other = bf16[32,1536]{1,0:T(8,128)(2,1)S(1)} collective-permute-done((bf16[32,1536]{1,0:T(8,128)(2,1)S(1)}, bf16[32,1536]{1,0:T(8,128)(2,1)S(1)}, u32[]{:S(2)}, u32[]{:S(2)}) %collective-permute-start.18) | collective-permute-done | bytes 98336 | tf_op jit(solution)/shard_map/ppermute | solution.py:662
  61.5 5.1 %collective-permute-done.17.refs_7_ = bf16[288,512]{1,0:T(8,128)(2,1)S(1)} collective-permute-done((bf16[288,512]{1,0:T(8,128)(2,1)S(1)}, bf16[288,512]{1,0:T(8,128)(2,1)S(1)}, u32[]{:S(2)}, u32[]{:S(2)}) %collective-permute-start.17) | collective-permute-done | bytes 294944 | tf_op jit(solution)/shard_map/ppermute | solution.py:70
  66.6 1.6 %collective-permute-done.22.refs_8_ = bf16[288,512]{1,0:T(8,128)(2,1)S(1)} collective-permute-done((bf16[288,512]{1,0:T(8,128)(2,1)S(1)}, bf16[288,512]{1,0:T(8,128)(2,1)S(1)}, u32[]{:S(2)}, u32[]{:S(2)}) %collective-permute-start.22) | collective-permute-done | bytes 294944 | tf_op jit(solution)/shard_map/ppermute | solution.py:79
  68.2 3.0 %expert.1 = (bf16[32,1536]{1,0:T(8,128)(2,1)S(1)}, bf16[32,1536]{1,0:T(8,128)(2,1)}) custom-call(bf16[32,1536]{1,0:T(8,128)(2,1)S(1)} %get-tuple-element.105.own, bf16[32,1536]{1,0:T(8,128)(2,1)S(1)} %collective-permute-done.18.other, bf16[576,512]{1,0:T(8,128)(2,1)S(1)} %get-tuple-element.58.refs_0_, bf16[576,512]{1,0:T(8,128)(2,1)S(1)} %collective-permute-done.3.refs_1_, ...), custom_call_target="tpu_custom_call" | custom-call | flops 1 | bytes 9437184 | tf_op jit(solution)/shard_map/expert/pallas_call | solution.py:483
  71.7 3.3 %write.1 = bf16[512,4,128]{2,1,0:T(4,128)(2,1)} custom-call(bf16[16,144,128]{2,1,0:T(8,128)(2,1)S(1)} %all-to-all-done.arrived, bf16[512,4,128]{2,1,0:T(4,128)(2,1)S(1)} %copy-done.1), custom_call_target="tpu_custom_call" | custom-call | flops 1 | bytes 2097152 | tf_op jit(solution)/shard_map/write/pallas_call | solution.py:581
  75.0 1.2 %collective-permute-done.23.returned = bf16[32,1536]{1,0:T(8,128)(2,1)S(1)} collective-permute-done((bf16[32,1536]{1,0:T(8,128)(2,1)}, bf16[32,1536]{1,0:T(8,128)(2,1)S(1)}, u32[]{:S(2)}, u32[]{:S(2)}) %collective-permute-start.23) | collective-permute-done | bytes 98336 | tf_op jit(solution)/shard_map/ppermute | solution.py:672
  76.3 1.1 %combine.1 = bf16[128,1536]{1,0:T(8,128)(2,1)} custom-call(bf16[128,1536]{1,0:T(8,128)(2,1)S(1)} %get-tuple-element.96.residual, f32[128,40]{1,0:T(8,128)S(1)} %get-tuple-element.100.gates, bf16[128,64]{1,0:T(8,128)(2,1)S(1)} %copy-done.4, bf16[32,1536]{1,0:T(8,128)(2,1)S(1)} %get-tuple-element.108.own, bf16[32,1536]{1,0:T(8,128)(2,1)S(1)} %collective-permute-done.23.returned), custom_call_target="tpu_custom_call" | custom-call | flops 1 | bytes 1179648 | tf_op jit(solution)/shard_map/combine/pallas_call | solution.py:515
  (55 shorter events, 9.3 us)
Async XLA Ops:
  0.6 2.3 %collective-permute-start.2 = (bf16[96,1536]{1,0:T(8,128)(2,1)}, bf16[96,1536]{1,0:T(8,128)(2,1)S(1)}, u32[]{:S(2)}, u32[]{:S(2)}) collective-permute-start(bf16[96,1536]{1,0:T(8,128)(2,1)} %bitcast.16), channel_id=1, source_target_pairs={{0,2},{2,0},{4,6},{6,4},{8,10},{10,8},{12,14},{14,12},{16,18},{18,... | collective-permute-start | bytes 884744 | tf_op jit(solution)/shard_map/ppermute | solution.py:621
  0.7 2.2 %collective-permute-start = (bf16[96,1024]{1,0:T(8,128)(2,1)}, bf16[96,1024]{1,0:T(8,128)(2,1)S(1)}, u32[]{:S(2)}, u32[]{:S(2)}) collective-permute-start(bf16[96,1024]{1,0:T(8,128)(2,1)} %bitcast.18), channel_id=1, source_target_pairs={{0,2},{2,0},{4,6},{6,4},{8,10},{10,8},{12,14},{14,12},{16,18},{18,... | collective-permute-start | bytes 589832 | tf_op jit(solution)/shard_map/ppermute | solution.py:621
  1.2 1.7 %collective-permute-start.1 = (bf16[32,1536]{1,0:T(8,128)(2,1)}, bf16[32,1536]{1,0:T(8,128)(2,1)S(1)}, u32[]{:S(2)}, u32[]{:S(2)}) collective-permute-start(bf16[32,1536]{1,0:T(8,128)(2,1)} %bitcast.20), channel_id=1, source_target_pairs={{0,2},{2,0},{4,6},{6,4},{8,10},{10,8},{12,14},{14,12},{16,18},{18,... | collective-permute-start | bytes 294920 | tf_op jit(solution)/shard_map/ppermute | solution.py:621
  1.3 11.7 %collective-permute-start.5 = (bf16[128,1536]{1,0:T(8,128)(2,1)}, bf16[128,1536]{1,0:T(8,128)(2,1)S(1)}, u32[]{:S(2)}, u32[]{:S(2)}) collective-permute-start(bf16[128,1536]{1,0:T(8,128)(2,1)} %tokens.1), channel_id=1, source_target_pairs={{0,1},{1,0},{2,3},{3,2},{4,5},{5,4},{6,7},{7,6},{8,9},{9,8},{10,11... | collective-permute-start | bytes 1179656 | tf_op jit(solution)/shard_map/ppermute | solution.py:618
  4.1 8.9 %collective-permute-start.4 = (bf16[192,768]{1,0:T(8,128)(2,1)S(1)}, bf16[192,768]{1,0:T(8,128)(2,1)S(1)}, u32[]{:S(2)}, u32[]{:S(2)}) collective-permute-start(bf16[192,768]{1,0:T(8,128)(2,1)S(1)} %get-tuple-element.59.refs_0_), channel_id=1, source_target_pairs={{0,8},{2,6},{8,16},{10,2},{16,24},{18,10},{24,28},{26,18},{28,20},... | collective-permute-start | bytes 884744 | tf_op jit(solution)/shard_map/ppermute | solution.py:70
  5.7 16.2 %collective-permute-start.3 = (bf16[576,512]{1,0:T(8,128)(2,1)S(1)}, bf16[576,512]{1,0:T(8,128)(2,1)S(1)}, u32[]{:S(2)}, u32[]{:S(2)}) collective-permute-start(bf16[576,512]{1,0:T(8,128)(2,1)S(1)} %get-tuple-element.58.refs_0_), channel_id=1, source_target_pairs={{0,8},{2,6},{8,16},{10,2},{16,24},{18,10},{24,28},{26,18},{28,20},... | collective-permute-start | bytes 1769480 | tf_op jit(solution)/shard_map/ppermute | solution.py:70
  9.9 4.6 %copy-start.6 = (bf16[1536,768]{1,0:T(8,128)(2,1)S(1)}, bf16[1536,768]{1,0:T(8,128)(2,1)}, u32[]{:S(2)}) copy-start(bf16[1536,768]{1,0:T(8,128)(2,1)} %w_query.1) | copy-start | bytes 7077892
  9.9 4.6 %copy-start.7 = (bf16[128,1536]{1,0:T(8,128)(2,1)S(1)}, bf16[128,1536]{1,0:T(8,128)(2,1)}, u32[]{:S(2)}) copy-start(bf16[128,1536]{1,0:T(8,128)(2,1)} %tokens.1) | copy-start | bytes 1179652
  13.0 15.4 %collective-permute-start.10 = (bf16[192,768]{1,0:T(8,128)(2,1)S(1)}, bf16[192,768]{1,0:T(8,128)(2,1)S(1)}, u32[]{:S(2)}, u32[]{:S(2)}) collective-permute-start(bf16[192,768]{1,0:T(8,128)(2,1)S(1)} %collective-permute-done.4.refs_1_), channel_id=1, source_target_pairs={{0,2},{2,0},{4,6},{6,4},{8,10},{10,8},{12,14},{14,12},{16,18},{18,... | collective-permute-start | bytes 884744 | tf_op jit(solution)/shard_map/ppermute | solution.py:79
  13.0 7.3 %collective-permute-start.6 = (bf16[192,768]{1,0:T(8,128)(2,1)S(1)}, bf16[192,768]{1,0:T(8,128)(2,1)S(1)}, u32[]{:S(2)}, u32[]{:S(2)}) collective-permute-start(bf16[192,768]{1,0:T(8,128)(2,1)S(1)} %collective-permute-done.4.refs_1_), channel_id=1, source_target_pairs={{0,8},{2,6},{8,16},{10,2},{16,24},{18,10},{24,28},{26,18},{28,20},... | collective-permute-start | bytes 884744 | tf_op jit(solution)/shard_map/ppermute | solution.py:70
  16.8 7.2 %collective-permute-start.9 = (bf16[128,512]{1,0:T(8,128)(2,1)S(1)}, bf16[128,512]{1,0:T(8,128)(2,1)S(1)}, u32[]{:S(2)}, u32[]{:S(2)}) collective-permute-start(bf16[128,512]{1,0:T(8,128)(2,1)S(1)} %get-tuple-element.74), channel_id=1, source_target_pairs={{0,2},{2,4},{4,6},{6,8},{8,10},{10,12},{12,14},{14,16},{16,18},{18... | collective-permute-start | bytes 393224 | tf_op jit(solution)/shard_map/ppermute | solution.py:636
  20.3 8.1 %collective-permute-start.11 = (bf16[192,768]{1,0:T(8,128)(2,1)S(1)}, bf16[192,768]{1,0:T(8,128)(2,1)S(1)}, u32[]{:S(2)}, u32[]{:S(2)}) collective-permute-start(bf16[192,768]{1,0:T(8,128)(2,1)S(1)} %collective-permute-done.6.refs_2_), channel_id=1, source_target_pairs={{0,2},{2,0},{4,6},{6,4},{8,10},{10,8},{12,14},{14,12},{16,18},{18,... | collective-permute-start | bytes 884744 | tf_op jit(solution)/shard_map/ppermute | solution.py:79
  20.3 8.1 %collective-permute-start.8 = (bf16[192,768]{1,0:T(8,128)(2,1)S(1)}, bf16[192,768]{1,0:T(8,128)(2,1)S(1)}, u32[]{:S(2)}, u32[]{:S(2)}) collective-permute-start(bf16[192,768]{1,0:T(8,128)(2,1)S(1)} %collective-permute-done.6.refs_2_), channel_id=1, source_target_pairs={{0,8},{2,6},{8,16},{10,2},{16,24},{18,10},{24,28},{26,18},{28,20},... | collective-permute-start | bytes 884744 | tf_op jit(solution)/shard_map/ppermute | solution.py:70
  24.0 16.7 %collective-permute-start.7 = (bf16[576,512]{1,0:T(8,128)(2,1)S(1)}, bf16[576,512]{1,0:T(8,128)(2,1)}, u32[]{:S(2)}, u32[]{:S(2)}) collective-permute-start(bf16[576,512]{1,0:T(8,128)(2,1)S(1)} %collective-permute-done.3.refs_1_), channel_id=1, source_target_pairs={{0,8},{2,6},{8,16},{10,2},{16,24},{18,10},{24,28},{26,18},{28,20},... | collective-permute-start | bytes 1769480 | tf_op jit(solution)/shard_map/ppermute | solution.py:70
  28.4 1.6 %collective-permute-start.13 = (bf16[192,768]{1,0:T(8,128)(2,1)S(1)}, bf16[192,768]{1,0:T(8,128)(2,1)S(1)}, u32[]{:S(2)}, u32[]{:S(2)}) collective-permute-start(bf16[192,768]{1,0:T(8,128)(2,1)S(1)} %collective-permute-done.8.refs_3_), channel_id=1, source_target_pairs={{0,2},{2,0},{4,6},{6,4},{8,10},{10,8},{12,14},{14,12},{16,18},{18,... | collective-permute-start | bytes 884744 | tf_op jit(solution)/shard_map/ppermute | solution.py:79
  28.5 6.9 %collective-permute-start.12 = (bf16[96,768]{1,0:T(8,128)(2,1)S(1)}, bf16[96,768]{1,0:T(8,128)(2,1)S(1)}, u32[]{:S(2)}, u32[]{:S(2)}) collective-permute-start(bf16[96,768]{1,0:T(8,128)(2,1)S(1)} %slice.6), channel_id=1, source_target_pairs={{0,8},{2,6},{8,16},{10,2},{16,24},{18,10},{24,28},{26,18},{28,20},... | collective-permute-start | bytes 442376 | tf_op jit(solution)/shard_map/ppermute | solution.py:70
  35.4 1.4 %collective-permute-start.14 = (bf16[96,768]{1,0:T(8,128)(2,1)S(1)}, bf16[96,768]{1,0:T(8,128)(2,1)S(1)}, u32[]{:S(2)}, u32[]{:S(2)}) collective-permute-start(bf16[96,768]{1,0:T(8,128)(2,1)S(1)} %collective-permute-done.12.refs_7_), channel_id=1, source_target_pairs={{0,2},{2,0},{4,6},{6,4},{8,10},{10,8},{12,14},{14,12},{16,18},{18,... | collective-permute-start | bytes 442376 | tf_op jit(solution)/shard_map/ppermute | solution.py:79
  37.9 11.3 %collective-permute-start.15 = (bf16[128,1536]{1,0:T(8,128)(2,1)S(1)}, bf16[128,1536]{1,0:T(8,128)(2,1)}, u32[]{:S(2)}, u32[]{:S(2)}) collective-permute-start(bf16[128,1536]{1,0:T(8,128)(2,1)S(1)} %outward_send.1), channel_id=1, source_target_pairs={{0,1},{1,0},{2,3},{3,2},{4,5},{5,4},{6,7},{7,6},{8,9},{9,8},{10,11... | collective-permute-start | bytes 1179656 | tf_op jit(solution)/shard_map/ppermute | solution.py:653
  40.6 13.7 %collective-permute-start.16 = (bf16[576,512]{1,0:T(8,128)(2,1)}, bf16[576,512]{1,0:T(8,128)(2,1)S(1)}, u32[]{:S(2)}, u32[]{:S(2)}) collective-permute-start(bf16[576,512]{1,0:T(8,128)(2,1)} %collective-permute-done.7.refs_2_), channel_id=1, source_target_pairs={{0,8},{2,6},{8,16},{10,2},{16,24},{18,10},{24,28},{26,18},{28,20},... | collective-permute-start | bytes 1769480 | tf_op jit(solution)/shard_map/ppermute | solution.py:70
  42.3 29.5 %all-to-all-start = ((bf16[16,144,128]{2,1,0:T(8,128)(2,1)}), bf16[16,144,128]{2,1,0:T(8,128)(2,1)S(1)}, u32[]{:S(2)}, u32[]{:S(2)}) async-start(bf16[16,144,128]{2,1,0:T(8,128)(2,1)} %copy-done), calls=%async_computation | async-start | bytes 1179648 | tf_op jit(solution)/shard_map/all_to_all | solution.py:656
  49.3 1.0 %copy-start.8 = (bf16[128,1536]{1,0:T(8,128)(2,1)S(1)}, bf16[128,1536]{1,0:T(8,128)(2,1)}, u32[]{:S(2)}) copy-start(bf16[128,1536]{1,0:T(8,128)(2,1)} %tokens.1) | copy-start | bytes 1179652
  51.0 5.9 %copy-start.2 = (bf16[1536,40]{0,1:T(8,128)(2,1)S(1)}, bf16[1536,40]{0,1:T(8,128)(2,1)}, u32[]{:S(2)}) copy-start(bf16[1536,40]{0,1:T(8,128)(2,1)} %param.20) | copy-start | bytes 368644
  51.0 5.9 %copy-start.5 = (s32[128,8]{0,1:T(8,128)S(1)}, s32[128,8]{0,1:T(8,128)}, u32[]{:S(2)}) copy-start(s32[128,8]{0,1:T(8,128)} %param.23) | copy-start | bytes 12292
  54.4 12.2 %collective-permute-start.17 = (bf16[288,512]{1,0:T(8,128)(2,1)S(1)}, bf16[288,512]{1,0:T(8,128)(2,1)S(1)}, u32[]{:S(2)}, u32[]{:S(2)}) collective-permute-start(bf16[288,512]{1,0:T(8,128)(2,1)S(1)} %slice.7), channel_id=1, source_target_pairs={{0,8},{2,6},{8,16},{10,2},{16,24},{18,10},{24,28},{26,18},{28,20},... | collective-permute-start | bytes 884744 | tf_op jit(solution)/shard_map/ppermute | solution.py:70
  55.8 10.8 %collective-permute-start.19 = (bf16[576,512]{1,0:T(8,128)(2,1)S(1)}, bf16[576,512]{1,0:T(8,128)(2,1)S(1)}, u32[]{:S(2)}, u32[]{:S(2)}) collective-permute-start(bf16[576,512]{1,0:T(8,128)(2,1)S(1)} %collective-permute-done.3.refs_1_), channel_id=1, source_target_pairs={{0,2},{2,0},{4,6},{6,4},{8,10},{10,8},{12,14},{14,12},{16,18},{18,... | collective-permute-start | bytes 1769480 | tf_op jit(solution)/shard_map/ppermute | solution.py:79
  55.8 10.8 %collective-permute-start.20 = (bf16[576,512]{1,0:T(8,128)(2,1)}, bf16[576,512]{1,0:T(8,128)(2,1)S(1)}, u32[]{:S(2)}, u32[]{:S(2)}) collective-permute-start(bf16[576,512]{1,0:T(8,128)(2,1)} %collective-permute-done.7.refs_2_), channel_id=1, source_target_pairs={{0,2},{2,0},{4,6},{6,4},{8,10},{10,8},{12,14},{14,12},{16,18},{18,... | collective-permute-start | bytes 1769480 | tf_op jit(solution)/shard_map/ppermute | solution.py:79
  56.3 11.9 %collective-permute-start.21 = (bf16[576,512]{1,0:T(8,128)(2,1)S(1)}, bf16[576,512]{1,0:T(8,128)(2,1)S(1)}, u32[]{:S(2)}, u32[]{:S(2)}) collective-permute-start(bf16[576,512]{1,0:T(8,128)(2,1)S(1)} %collective-permute-done.16.refs_3_), channel_id=1, source_target_pairs={{0,2},{2,0},{4,6},{6,4},{8,10},{10,8},{12,14},{14,12},{16,18},{18,... | collective-permute-start | bytes 1769480 | tf_op jit(solution)/shard_map/ppermute | solution.py:79
  56.3 5.2 %collective-permute-start.18 = (bf16[32,1536]{1,0:T(8,128)(2,1)S(1)}, bf16[32,1536]{1,0:T(8,128)(2,1)S(1)}, u32[]{:S(2)}, u32[]{:S(2)}) collective-permute-start(bf16[32,1536]{1,0:T(8,128)(2,1)S(1)} %get-tuple-element.103), channel_id=1, source_target_pairs={{0,1},{1,0},{2,3},{3,2},{4,5},{5,4},{6,7},{7,6},{8,9},{9,8},{10,11... | collective-permute-start | bytes 294920 | tf_op jit(solution)/shard_map/ppermute | solution.py:662
  66.6 5.2 %copy-start.1 = (bf16[512,4,128]{2,1,0:T(4,128)(2,1)S(1)}, bf16[512,4,128]{2,1,0:T(4,128)(2,1)}, u32[]{:S(2)}) copy-start(bf16[512,4,128]{2,1,0:T(4,128)(2,1)} %cache.1) | copy-start | bytes 1572868
  66.6 1.6 %collective-permute-start.22 = (bf16[288,512]{1,0:T(8,128)(2,1)S(1)}, bf16[288,512]{1,0:T(8,128)(2,1)S(1)}, u32[]{:S(2)}, u32[]{:S(2)}) collective-permute-start(bf16[288,512]{1,0:T(8,128)(2,1)S(1)} %collective-permute-done.17.refs_7_), channel_id=1, source_target_pairs={{0,2},{2,0},{4,6},{6,4},{8,10},{10,8},{12,14},{14,12},{16,18},{18,... | collective-permute-start | bytes 884744 | tf_op jit(solution)/shard_map/ppermute | solution.py:79
  71.2 5.1 %copy-start.4 = (bf16[128,64]{1,0:T(8,128)(2,1)S(1)}, bf16[128,64]{1,0:T(8,128)(2,1)}, u32[]{:S(2)}) copy-start(bf16[128,64]{1,0:T(8,128)(2,1)} %copy-done.3) | copy-start | bytes 49156
  71.2 5.1 %collective-permute-start.23 = (bf16[32,1536]{1,0:T(8,128)(2,1)}, bf16[32,1536]{1,0:T(8,128)(2,1)S(1)}, u32[]{:S(2)}, u32[]{:S(2)}) collective-permute-start(bf16[32,1536]{1,0:T(8,128)(2,1)} %get-tuple-element.109), channel_id=1, source_target_pairs={{0,1},{1,0},{2,3},{3,2},{4,5},{5,4},{6,7},{7,6},{8,9},{9,8},{10,11... | collective-permute-start | bytes 294920 | tf_op jit(solution)/shard_map/ppermute | solution.py:672
  (4 other events, 2.8 us)

commit v8 on v7

--- a/solution.py
+++ b/solution.py
@@ -104,8 +104,10 @@
 LITTLE = pl.CostEstimate(flops=1, bytes_accessed=1, transcendentals=0)
 
 
-def takes(us, nbytes=1):
-    return pl.CostEstimate(flops=int(us * 1.15e9), bytes_accessed=nbytes, transcendentals=0)
+def takes(us):
+    return pl.CostEstimate(
+        flops=int(us * 1.15e9), bytes_accessed=int(us * 8e6), transcendentals=0
+    )
 
 
 def reads(nbytes):
@@ -183,13 +185,12 @@
 
 
 def prepare_kernel(groups, slots_dev, *refs):
-    sources, (cosine, sine, past, place, spread, send, tags, gain, late_gain) = refs[:5], refs[5:14]
-    positions, slots, ids, flat_gains, flat_late, sems = refs[14:]
-    copies = fetch(list(zip(sources, (positions, slots, ids, flat_gains, flat_late))), sems)
+    sources, (cosine, sine, past, place, send, tags, gain) = refs[:4], refs[4:11]
+    positions, slots, ids, flat_gain, sems = refs[11:]
+    copies = fetch(list(zip(sources, (positions, slots, ids, flat_gain))), sems)
     for copy in copies:
         copy.wait()
-    gain[...] = flat_gains[...].reshape(gain.shape)
-    late_gain[...] = flat_late[...].reshape(late_gain.shape)
+    gain[...] = flat_gain[...].reshape(gain.shape)
     lane = lax.axis_index("hd")
     block = positions.shape[1]
 
@@ -210,7 +211,6 @@
     tokens = ids.shape[1]
     cap = place.shape[0] // 2
     hit = named_experts(ids, 8)
-    small_eye = (iota((tokens, tokens), 0) == iota((tokens, tokens), 1)).astype(f32)
     upto = (iota((tokens, tokens), 0) <= iota((tokens, tokens), 1)).astype(f32)
     rank = jnp.dot(hit, upto, preferred_element_type=f32) - 1.0
     slot = iota((2 * cap, tokens), 0).astype(f32)
@@ -220,7 +220,6 @@
         member = hit[live : live + 1, :] > 0.0
         placed = jnp.where(member & (slot == rank[live : live + 1, :] + order), 1.0, placed)
     place[...] = placed.astype(bf16)
-    spread[...] = lax.dot_general(small_eye, placed, LAST_DIMS, preferred_element_type=f32).astype(bf16)
 
     where = slots[...]
     owner = jnp.where(where >= 0, where // slots_dev, -1)
@@ -238,7 +237,7 @@
     tags[...] = jnp.where(spot == 0, high, jnp.where(spot == 1, low, 0.0)).astype(bf16)
 
 
-def prepare(groups, slots_dev, positions, slots, ids, gain, late_gain):
+def prepare(groups, slots_dev, positions, slots, ids, gain):
     block, tokens = positions.shape[0], ids.shape[0]
     model = gain.shape[0]
     cap = tokens // 4
@@ -248,25 +247,22 @@
         ((block, 128), f32),
         ((block, 128), f32),
         ((2 * cap, tokens), bf16),
-        ((tokens, 2 * cap), bf16),
         ((groups * capc, block), bf16),
         ((block, 128), bf16),
         ((1, model), f32),
-        ((1, model), f32),
     ]
-    sources = (positions[None], slots[None], ids.T, gain, late_gain)
+    sources = (positions[None], slots[None], ids.T, gain)
     return pl.pallas_call(
         functools.partial(prepare_kernel, groups, slots_dev),
         out_shape=tuple(jax.ShapeDtypeStruct(shape, kind) for shape, kind in shapes),
-        in_specs=[ANY] * 5,
+        in_specs=[ANY] * 4,
         out_specs=(VMEM,) * len(shapes),
         scratch_shapes=[
             pltpu.VMEM((1, block), jnp.int32),
             pltpu.VMEM((1, block), jnp.int32),
             pltpu.VMEM(ids.shape[::-1], jnp.int32),
             pltpu.VMEM((model,), f32),
-            pltpu.VMEM((model,), f32),
-            pltpu.SemaphoreType.DMA((5,)),
+            pltpu.SemaphoreType.DMA((4,)),
         ],
         compiler_params=PARAMS,
         cost_estimate=LITTLE,
@@ -374,35 +370,62 @@
     )(q, kv, seam, past)
 
 
-def outward_kernel(flip, groups, unit_rows, n_parts, mixed, *refs):
-    parts, (out, w_out) = refs[:n_parts], refs[n_parts:]
+def outward_rows(flip, groups, unit_rows, mixed, parts, w_out):
     place_parts(groups, parts, unit_rows, [(0, unit_rows, w_out, 0)])
-    count = out.shape[0]
+    count = mixed.shape[0] // 2
     lane = lax.axis_index("hd")
     first = pl.multiple_of(((1 - lane) if flip else lane) * count, count)
-    out[...] = lax.dot_general(
+    return lax.dot_general(
         mixed[pl.ds(first, count), :], w_out[...], LAST_DIMS, preferred_element_type=f32
-    ).astype(out.dtype)
-
-
-def outward(flip, out_type, groups, mixed, parts, unit_rows):
+    )
+
+
+def send_kernel(groups, unit_rows, n_parts, mixed, *refs):
+    parts, (out, w_out) = refs[:n_parts], refs[n_parts:]
+    out[...] = outward_rows(True, groups, unit_rows, mixed, parts, w_out).astype(bf16)
+
+
+def keep_kernel(groups, unit_rows, n_parts, mixed, tokens, flat_gain, *refs):
+    parts, (out, gain, w_out) = refs[:n_parts], refs[n_parts:]
+    gain[...] = flat_gain[...].reshape(gain.shape)
+    made = outward_rows(False, groups, unit_rows, mixed, parts, w_out)
+    out[...] = tokens[...].astype(f32) + made
+
+
+def outward_send(groups, mixed, parts, unit_rows):
     count = mixed.shape[0] // 2
-    width = groups * unit_rows
-    depth = parts[0].shape[1]
-    return pl.pallas_call(
-        functools.partial(outward_kernel, flip, groups, unit_rows, len(parts)),
-        out_shape=jax.ShapeDtypeStruct((count, width), out_type),
+    width, depth = groups * unit_rows, parts[0].shape[1]
+    return pl.pallas_call(
+        functools.partial(send_kernel, groups, unit_rows, len(parts)),
+        out_shape=jax.ShapeDtypeStruct((count, width), bf16),
         in_specs=[VMEM] * (1 + len(parts)),
         out_specs=VMEM,
         scratch_shapes=[pltpu.VMEM((width, depth), bf16)],
         compiler_params=PARAMS,
         cost_estimate=reads(2 * width * depth),
-        name="outward_send" if flip else "outward_keep",
+        name="outward_send",
     )(mixed, *parts)
 
 
-def route_kernel(tokens, mine, arrived, gain, place, residual, moe_in, sent):
-    added = (tokens[...].astype(f32) + (mine[...] + arrived[...].astype(f32))).astype(bf16)
+def outward_keep(groups, mixed, tokens, gain, parts, unit_rows):
+    width, depth = groups * unit_rows, parts[0].shape[1]
+    return pl.pallas_call(
+        functools.partial(keep_kernel, groups, unit_rows, len(parts)),
+        out_shape=(
+            jax.ShapeDtypeStruct(tokens.shape, f32),
+            jax.ShapeDtypeStruct((1, width), f32),
+        ),
+        in_specs=[VMEM] * (3 + len(parts)),
+        out_specs=(VMEM, VMEM),
+        scratch_shapes=[pltpu.VMEM((width, depth), bf16)],
+        compiler_params=PARAMS,
+        cost_estimate=reads(2 * width * depth),
+        name="outward_keep",
+    )(mixed, tokens, gain, *parts)
+
+
+def route_kernel(mine, arrived, gain, place, residual, moe_in, sent):
+    added = (mine[...] + arrived[...].astype(f32)).astype(bf16)
     residual[...] = added
     moe_in[...] = normalized(added.astype(f32), gain[...])
     cap = sent.shape[0]
@@ -410,24 +433,24 @@
     sent[...] = rows.astype(bf16)
 
 
-def route(tokens, mine, arrived, gain, place):
+def route(mine, arrived, gain, place):
     cap = place.shape[0] // 2
     return pl.pallas_call(
         route_kernel,
         out_shape=(
-            jax.ShapeDtypeStruct(tokens.shape, bf16),
-            jax.ShapeDtypeStruct(tokens.shape, bf16),
-            jax.ShapeDtypeStruct((cap, tokens.shape[1]), bf16),
+            jax.ShapeDtypeStruct(mine.shape, bf16),
+            jax.ShapeDtypeStruct(mine.shape, bf16),
+            jax.ShapeDtypeStruct((cap, mine.shape[1]), bf16),
         ),
-        in_specs=[VMEM] * 5,
+        in_specs=[VMEM] * 4,
         out_specs=(VMEM,) * 3,
         compiler_params=PARAMS,
-        cost_estimate=takes(2, 10 * tokens.shape[0] * tokens.shape[1]),
+        cost_estimate=takes(2),
         name="route",
-    )(tokens, mine, arrived, gain, place)
-
-
-def gate_kernel(moe_in, router, ids, place, gates, own):
+    )(mine, arrived, gain, place)
+
+
+def gate_kernel(moe_in, router, ids, place, gates, own, spread):
     cap = own.shape[0]
     own[...] = jnp.dot(place[:cap, :], moe_in[...], preferred_element_type=f32).astype(bf16)
     hit = named_experts(ids, router.shape[0])
@@ -435,6 +458,9 @@
     row = lax.broadcasted_iota(jnp.int32, (tokens, tokens), 0)
     eye = (row == lax.broadcasted_iota(jnp.int32, (tokens, tokens), 1)).astype(f32)
     named = lax.dot_general(eye, hit, LAST_DIMS, preferred_element_type=f32)
+    spread[...] = lax.dot_general(
+        eye.astype(bf16), place[...], LAST_DIMS, preferred_element_type=f32
+    ).astype(bf16)
     logits = lax.dot_general(moe_in[...], router[...], LAST_DIMS, preferred_element_type=f32)
     raised = jnp.where(named > 0, jnp.exp(logits), 0.0)
     gates[...] = raised / jnp.sum(raised, axis=-1, keepdims=True)
@@ -447,9 +473,10 @@
         out_shape=(
             jax.ShapeDtypeStruct((moe_in.shape[0], router_t.shape[0]), f32),
             jax.ShapeDtypeStruct((cap, moe_in.shape[1]), bf16),
+            jax.ShapeDtypeStruct(place.shape[::-1], bf16),
         ),
         in_specs=[VMEM] * 4,
-        out_specs=(VMEM,) * 2,
+        out_specs=(VMEM,) * 3,
         compiler_params=PARAMS,
         cost_estimate=LITTLE,
         name="gate",
@@ -548,14 +575,14 @@
         in_specs=[VMEM] * 3,
         out_specs=VMEM,
         compiler_params=PARAMS,
-        cost_estimate=takes(2),
+        cost_estimate=LITTLE,
         name="bundle",
     )(send, kv, tags)
 
 
-def write_kernel(arrived, cache, out, rows):
+def write_kernel(heads, arrived, cache, out, rows, wide, known):
     groups, size, _ = arrived.shape
-    slots, heads, _ = cache.shape
+    slots = cache.shape[0] // heads
     capc = (size - 16) // heads
     high, low = [], []
     for source in range(groups):
@@ -567,27 +594,36 @@
         high.append(numbers[0:1, :capc])
         low.append(numbers[1:2, :capc])
     slot = jnp.concatenate(high, axis=1) * 64.0 + jnp.concatenate(low, axis=1) - 64.0
-    hit = (lax.broadcasted_iota(jnp.int32, (slots, slot.shape[1]), 0).astype(f32) == slot).astype(f32)
-    known = jnp.max(hit, axis=1, keepdims=True) > 0.0
-    made = jnp.dot(hit.astype(bf16), rows[...], preferred_element_type=f32)
+    row = lax.broadcasted_iota(jnp.int32, (slots, slot.shape[1]), 0).astype(f32)
+    hit = (row == slot).astype(bf16)
+    made = jnp.dot(hit, rows[...], preferred_element_type=f32)
+    found = jnp.dot(hit, jnp.ones((slot.shape[1], 128), bf16), preferred_element_type=f32)
     for head in range(heads):
-        here = made[:, head * 128 : (head + 1) * 128]
-        out[:, head, :] = jnp.where(known, here, cache[:, head, :].astype(f32)).astype(bf16)
+        wide[pl.ds(head, slots, heads), :] = made[:, head * 128 : (head + 1) * 128]
+        known[pl.ds(head, slots, heads), :] = found
+    old = cache[...].astype(f32)
+    out[...] = jnp.where(known[...] > 0.0, wide[...], old).astype(bf16)
 
 
 def write(arrived, cache):
     slots, heads, lanes = cache.shape
     capc = (arrived.shape[1] - 16) // heads
-    return pl.pallas_call(
-        write_kernel,
-        out_shape=jax.ShapeDtypeStruct(cache.shape, bf16),
+    flat = (slots * heads, lanes)
+    written = pl.pallas_call(
+        functools.partial(write_kernel, heads),
+        out_shape=jax.ShapeDtypeStruct(flat, bf16),
         in_specs=[VMEM] * 2,
         out_specs=VMEM,
-        scratch_shapes=[pltpu.VMEM((arrived.shape[0] * capc, heads * lanes), bf16)],
+        scratch_shapes=[
+            pltpu.VMEM((arrived.shape[0] * capc, heads * lanes), bf16),
+            pltpu.VMEM(flat, f32),
+            pltpu.VMEM(flat, f32),
+        ],
         compiler_params=PARAMS,
         cost_estimate=reads(1 << 21),
         name="write",
-    )(arrived, cache)
+    )(arrived, cache.reshape(flat))
+    return written.reshape(cache.shape)
 
 
 def two_lane_shards(
@@ -626,20 +662,18 @@
     expert_ring.step()
     w_keyval, positions = together((w_keyval, positions, out_pair))[:2]
     flat_kv = w_keyval.reshape(model, kv_width)
-    cosine, sine, past, place, spread, send, tags, gain, late_gain = prepare(
-        groups, slots_dev, positions, cache_slot, expert_ids, attn_gain, moe_gain
+    cosine, sine, past, place, send, tags, gain = prepare(
+        groups, slots_dev, positions, cache_slot, expert_ids, attn_gain
     )
     other_tokens, cosine, flat_kv = out_ring.pin(other_tokens, cosine, flat_kv)
     out_ring.step()
 
     q, kv, tail = project(tokens, other_tokens, gain, cosine, sine, w_query, flat_kv)
     seam = lax.ppermute(tail, "grp", [(g, g + 1) for g in range(groups - 1)])
-    kv_now = out_ring.pin(kv)
+    seam, q = out_ring.pin(seam, q)
     out_ring.step()
-    kv_now = expert_ring.pin(kv_now)
+    q = expert_ring.pin(q)
     expert_ring.step()
-    outgoing = bundle(groups, send, kv_now, tags)
-    seam, outgoing = together((seam, outgoing))
     out_ring.share(2)
     mixed = attend(q, kv, seam, past)
     mixed, out_ring.near = together((mixed, out_ring.near))
@@ -649,21 +683,25 @@
     mixed, out_ring.near = together((mixed, out_ring.near))
     mixed = out_ring.pin(mixed)
     out_ring.share()
-    sent = outward(True, bf16, groups, mixed, out_ring.parts(), out_ring.unit_rows)
+    sent = outward_send(groups, mixed, out_ring.parts(), out_ring.unit_rows)
     arrived = swap(sent)
-    mixed, outgoing = together((mixed, outgoing, sent))[:2]
-    mine = outward(False, f32, groups, mixed, out_ring.parts(), out_ring.unit_rows)
+    mixed = together((mixed, sent))[0]
+    mine, late_gain = outward_keep(
+        groups, mixed, tokens, moe_gain, out_ring.parts(), out_ring.unit_rows
+    )
+    kv, mine = together((kv, mine))
+    outgoing = bundle(groups, send, kv, tags)
     arrived_cache = lax.all_to_all(outgoing, "grp", split_axis=0, concat_axis=0, tiled=True)
     mine = expert_ring.pin(mine)
     expert_ring.share()
     expert_ring.step()
 
-    residual, moe_in, sent_rows = route(tokens, mine, arrived, late_gain, place)
+    residual, moe_in, sent_rows = route(mine, arrived, late_gain, place)
     landed = swap(sent_rows)
     moe_in = expert_ring.pin(moe_in)
     expert_ring.share()
     expert_ring.step()
-    gates, own_rows = gate(moe_in, router.T, expert_ids.T, place)
+    gates, own_rows, spread = gate(moe_in, router.T, expert_ids.T, place)
     landed, own_rows = expert_ring.pin(landed, own_rows)
     expert_ring.share()
     own_made, back = expert(

time: 77.8 us -> 81.3 us (1.045)
  the two profiles are of different devices: /device:TPU:16 before, /device:TPU:12 now
where the time goes in v8:
time: 81.3 us; the launch traced here: 80.9 us
  waiting for transfers between devices  35.4 us (44%)
  starting transfers between devices  21.6 us (27%)
  Pallas kernels  17.8 us (22%)
  local copies, waits for them, and re-layouts  5.26 us (6%)
  between operations  0.85 us (1%)
    ppermute x8, waiting for transfers between devices, step(): self.mine.append(self.across(held))  18.4 us
    all_to_all x1, starting transfers between devices, two_lane_shards(): lax.all_to_all(outgoing, 'grp', split_axis=0, concat_axis=0, tiled=True)  7.16 us
    unnamed x29, local copies, waits for them, and re-layouts  5.22 us
    ppermute x1, waiting for transfers between devices, two_lane_shards(): other_tokens = swap(tokens)  4.69 us
    ppermute x8, waiting for transfers between devices, share(): self.near.append(self.beside(self.mine[index]))  3.96 us
    ppermute x8, starting transfers between devices, share(): self.near.append(self.beside(self.mine[index]))  3.93 us
    ppermute x1, waiting for transfers between devices, two_lane_shards(): landed = swap(sent_rows)  3.74 us
    ppermute x8, starting transfers between devices, step(): self.mine.append(self.across(held))  3.36 us
  transfers between devices with their start and end apart: 25, of which 11 were waited for; matrix products, arithmetic and copies ran while one was open for 2% of the time, Pallas kernels for 21%

profile of v8, /device:TPU:12, one launch (start us, length us, event | category | flops | bytes accessed | tf_op | source)
XLA Modules:
  0.0 80.9 jit_solution(6850011023794505133)
XLA Ops:
  1.3 1.5 %collective-permute-start.5 = (bf16[128,1536]{1,0:T(8,128)(2,1)}, bf16[128,1536]{1,0:T(8,128)(2,1)S(1)}, u32[]{:S(2)}, u32[]{:S(2)}) collective-permute-start(bf16[128,1536]{1,0:T(8,128)(2,1)} %tokens.1), channel_id=1, source_target_pairs={{0,1},{1,0},{2,3},{3,2},{4,5},{5,4},{6,7},{7,6},{8,9},{9,8},{10,11... | collective-permute-start | bytes 1179656 | tf_op jit(solution)/shard_map/ppermute | solution.py:654
  2.9 1.1 %pack.1 = (bf16[576,512]{1,0:T(8,128)(2,1)S(1)}, bf16[192,768]{1,0:T(8,128)(2,1)S(1)}) custom-call(bf16[96,1024]{1,0:T(8,128)(2,1)} %bitcast.23, bf16[32,1536]{1,0:T(8,128)(2,1)} %bitcast.25, bf16[96,1536]{1,0:T(8,128)(2,1)} %bitcast.21, bf16[96,1024]{1,0:T(8,128)(2,1)S(1)} %collective-permute-done.refs_3_, ...), custom_call_target="tpu_custom_call" | custom-call | flops 1 | bytes 1 | tf_op jit(solution)/shard_map/pack/pallas_call | solution.py:159
  4.9 1.5 %prepare.1 = (f32[256,128]{1,0:T(8,128)S(1)}, f32[256,128]{1,0:T(8,128)S(1)}, f32[256,128]{1,0:T(8,128)S(1)}, bf16[64,128]{1,0:T(8,128)(2,1)S(1)}, bf16[512,256]...) custom-call(s32[1,256]{1,0:T(1,128)} %bitcast.26, s32[1,256]{1,0:T(1,128)} %bitcast.27, ...), custom_call_target="tpu_custom_call" | custom-call | flops 1 | bytes 1 | tf_op jit(solution)/shard_map/prepare/pallas_call | solution.py:255
  6.4 1.8 %copy.17 = bf16[192,8,4,128]{3,1,2,0:T(8,128)(2,1)S(1)} copy(bf16[192,8,4,128]{3,2,1,0:T(4,128)(2,1)} %bitcast.18) | data formatting | bytes 3145728
  8.3 4.7 %collective-permute-done.5.other = bf16[128,1536]{1,0:T(8,128)(2,1)S(1)} collective-permute-done((bf16[128,1536]{1,0:T(8,128)(2,1)}, bf16[128,1536]{1,0:T(8,128)(2,1)S(1)}, u32[]{:S(2)}, u32[]{:S(2)}) %collective-permute-start.5) | collective-permute-done | bytes 393248 | tf_op jit(solution)/shard_map/ppermute | solution.py:654
  13.4 2.2 %project.1 = (bf16[256,768]{1,0:T(8,128)(2,1)S(1)}, bf16[256,512]{1,0:T(8,128)(2,1)S(1)}, bf16[128,512]{1,0:T(8,128)(2,1)S(1)}) custom-call(bf16[128,1536]{1,0:T(8,128)(2,1)S(1)} %copy-done.1, bf16[128,1536]{1,0:T(8,128)(2,1)S(1)} %collective-permute-done.5.other, f32[1,1536]{1,0:T(1,128)S(1)} %get-tuple-element.66.gain, ...), custom_call_target="tpu_custom_call" | custom-call | flops 9200000000 | bytes 64000000 | tf_op jit(solution)/shard_map/project/pallas_call | solution.py:305
  15.6 2.4 %collective-permute-start.7 = (bf16[128,512]{1,0:T(8,128)(2,1)S(1)}, bf16[128,512]{1,0:T(8,128)(2,1)S(1)}, u32[]{:S(2)}, u32[]{:S(2)}) collective-permute-start(bf16[128,512]{1,0:T(8,128)(2,1)S(1)} %get-tuple-element.70), channel_id=1, source_target_pairs={{0,2},{2,4},{4,6},{6,8},{8,10},{10,12},{12,14},{14,16},{16,18},{18... | collective-permute-start | bytes 393224 | tf_op jit(solution)/shard_map/ppermute | solution.py:672
  18.0 2.3 %collective-permute-start.10 = (bf16[192,768]{1,0:T(8,128)(2,1)S(1)}, bf16[192,768]{1,0:T(8,128)(2,1)S(1)}, u32[]{:S(2)}, u32[]{:S(2)}) collective-permute-start(bf16[192,768]{1,0:T(8,128)(2,1)S(1)} %collective-permute-done.4.refs_1_), channel_id=1, source_target_pairs={{0,2},{2,0},{4,6},{6,4},{8,10},{10,8},{12,14},{14,12},{16,18},{18,... | collective-permute-start | bytes 884744 | tf_op jit(solution)/shard_map/ppermute | solution.py:79
  20.4 1.5 %collective-permute-done.7.seam = bf16[128,512]{1,0:T(8,128)(2,1)S(1)} collective-permute-done((bf16[128,512]{1,0:T(8,128)(2,1)S(1)}, bf16[128,512]{1,0:T(8,128)(2,1)S(1)}, u32[]{:S(2)}, u32[]{:S(2)}) %collective-permute-start.7) | collective-permute-done | bytes 131104 | tf_op jit(solution)/shard_map/ppermute | solution.py:672
  22.7 2.8 %attend.1.mixed = bf16[256,768]{1,0:T(8,128)(2,1)S(1)} custom-call(bf16[256,768]{1,0:T(8,128)(2,1)S(1)} %get-tuple-element.76.q, bf16[256,512]{1,0:T(8,128)(2,1)S(1)} %get-tuple-element.111.kv, bf16[128,512]{1,0:T(8,128)(2,1)S(1)} %collective-permute-done.7.seam, f32[256,128]{1,0:T(8,128)S(1)} %get-tuple-element.78.past), custom_call_target="tpu_custom_call" | custom-call | flops 4600000000 | bytes 32000000 | tf_op jit(solution)/shard_map/attend/pallas_call | solution.py:358
  25.6 3.4 %collective-permute-done.9.refs_3_ = bf16[192,768]{1,0:T(8,128)(2,1)S(1)} collective-permute-done((bf16[192,768]{1,0:T(8,128)(2,1)S(1)}, bf16[192,768]{1,0:T(8,128)(2,1)S(1)}, u32[]{:S(2)}, u32[]{:S(2)}) %collective-permute-start.9) | collective-permute-done | bytes 294944 | tf_op jit(solution)/shard_map/ppermute | solution.py:70
  29.5 1.0 %collective-permute-done.13.refs_6_ = bf16[192,768]{1,0:T(8,128)(2,1)S(1)} collective-permute-done((bf16[192,768]{1,0:T(8,128)(2,1)S(1)}, bf16[192,768]{1,0:T(8,128)(2,1)S(1)}, u32[]{:S(2)}, u32[]{:S(2)}) %collective-permute-start.13) | collective-permute-done | bytes 294944 | tf_op jit(solution)/shard_map/ppermute | solution.py:79
  30.5 6.3 %collective-permute-done.12.refs_7_ = bf16[96,768]{1,0:T(8,128)(2,1)S(1)} collective-permute-done((bf16[96,768]{1,0:T(8,128)(2,1)S(1)}, bf16[96,768]{1,0:T(8,128)(2,1)S(1)}, u32[]{:S(2)}, u32[]{:S(2)}) %collective-permute-start.12) | collective-permute-done | bytes 147488 | tf_op jit(solution)/shard_map/ppermute | solution.py:70
  36.9 1.4 %collective-permute-done.14.refs_8_ = bf16[96,768]{1,0:T(8,128)(2,1)S(1)} collective-permute-done((bf16[96,768]{1,0:T(8,128)(2,1)S(1)}, bf16[96,768]{1,0:T(8,128)(2,1)S(1)}, u32[]{:S(2)}, u32[]{:S(2)}) %collective-permute-start.14) | collective-permute-done | bytes 147488 | tf_op jit(solution)/shard_map/ppermute | solution.py:79
  38.2 1.1 %outward_send.1 = bf16[128,1536]{1,0:T(8,128)(2,1)S(1)} custom-call(bf16[256,768]{1,0:T(8,128)(2,1)S(1)} %attend.1.mixed, bf16[192,768]{1,0:T(8,128)(2,1)S(1)} %get-tuple-element.60.refs_0_, bf16[192,768]{1,0:T(8,128)(2,1)S(1)} %collective-permute-done.4.refs_1_, bf16[192,768]{1,0:T(8,128)(2,1)S(1)} %collective-permute-done.6.refs_2_, ...), custom_call_target="tpu_custom_call" | custom-call | flops 1 | bytes 2359296 | tf_op jit(solution)/shard_map/outward_send/pallas_call | solution.py:398
  39.4 1.6 %collective-permute-start.15 = (bf16[128,1536]{1,0:T(8,128)(2,1)S(1)}, bf16[128,1536]{1,0:T(8,128)(2,1)}, u32[]{:S(2)}, u32[]{:S(2)}) collective-permute-start(bf16[128,1536]{1,0:T(8,128)(2,1)S(1)} %outward_send.1), channel_id=1, source_target_pairs={{0,1},{1,0},{2,3},{3,2},{4,5},{5,4},{6,7},{7,6},{8,9},{9,8},{10,11... | collective-permute-start | bytes 1179656 | tf_op jit(solution)/shard_map/ppermute | solution.py:687
  40.9 1.1 %outward_keep.1 = (f32[128,1536]{1,0:T(8,128)S(1)}, f32[1,1536]{1,0:T(1,128)S(1)}) custom-call(bf16[256,768]{1,0:T(8,128)(2,1)S(1)} %attend.1.mixed, bf16[128,1536]{1,0:T(8,128)(2,1)S(1)} %copy-done.1, f32[1536]{0:T(1024)S(1)} %copy-done.10, bf16[192,768]{1,0:T(8,128)(2,1)S(1)} %get-tuple-element.60.refs_0_, ...), custom_call_target="tpu_custom_call" | custom-call | flops 1 | bytes 2359296 | tf_op jit(solution)/shard_map/outward_keep/pallas_call | solution.py:412
  42.1 0.9 %copy-done.12 = f32[128,1536]{1,0:T(8,128)} copy-done((f32[128,1536]{1,0:T(8,128)}, f32[128,1536]{1,0:T(8,128)S(1)}, u32[]{:S(2)}) %copy-start.12) | copy-done | bytes 786456
  43.4 1.4 %bundle.1 = bf16[16,144,128]{2,1,0:T(8,128)(2,1)} custom-call(bf16[512,256]{1,0:T(8,128)(2,1)S(1)} %get-tuple-element.110.send, bf16[256,512]{1,0:T(8,128)(2,1)S(1)} %get-tuple-element.111.kv, bf16[256,128]{1,0:T(8,128)(2,1)S(1)} %get-tuple-element.112.tags), custom_call_target="tpu_custom_call" | custom-call | flops 1 | bytes 1 | tf_op jit(solution)/shard_map/bundle/pallas_call | solution.py:572
  44.8 7.2 %all-to-all-start = ((bf16[16,144,128]{2,1,0:T(8,128)(2,1)}), bf16[16,144,128]{2,1,0:T(8,128)(2,1)S(1)}, u32[]{:S(2)}, u32[]{:S(2)}) async-start(bf16[16,144,128]{2,1,0:T(8,128)(2,1)} %bundle.1), calls=%async_computation | async-start | bytes 1179648 | tf_op jit(solution)/shard_map/all_to_all | solution.py:694
  52.0 1.1 %copy-done.13 = f32[128,1536]{1,0:T(8,128)S(1)} copy-done((f32[128,1536]{1,0:T(8,128)S(1)}, f32[128,1536]{1,0:T(8,128)}, u32[]{:S(2)}) %copy-start.13) | copy-done | bytes 786456
  53.1 1.4 %route.1 = (bf16[128,1536]{1,0:T(8,128)(2,1)S(1)}, bf16[128,1536]{1,0:T(8,128)(2,1)S(1)}, bf16[32,1536]{1,0:T(8,128)(2,1)S(1)}) custom-call(f32[128,1536]{1,0:T(8,128)S(1)} %copy-done.13, bf16[128,1536]{1,0:T(8,128)(2,1)} %collective-permute-done.15.arrived, f32[1,1536]{1,0:T(1,128)S(1)} %get-tuple-element.94.gain, bf16[64,128]{1,0:T(8,128)(2,1)S(1)} %get-tuple-element.95.place), custom_call_target="tpu_custom_call" | custom-call | flops 2300000000 | bytes 16000000 | tf_op jit(solution)/shard_map/route/pallas_call | solution.py:438
  54.6 0.7 copy-done.2
  55.9 0.8 collective-permute-start.19
  58.1 3.7 %collective-permute-done.18.other = bf16[32,1536]{1,0:T(8,128)(2,1)S(1)} collective-permute-done((bf16[32,1536]{1,0:T(8,128)(2,1)S(1)}, bf16[32,1536]{1,0:T(8,128)(2,1)S(1)}, u32[]{:S(2)}, u32[]{:S(2)}) %collective-permute-start.18) | collective-permute-done | bytes 98336 | tf_op jit(solution)/shard_map/ppermute | solution.py:700
  61.8 8.7 %collective-permute-done.17.refs_7_ = bf16[288,512]{1,0:T(8,128)(2,1)S(1)} collective-permute-done((bf16[288,512]{1,0:T(8,128)(2,1)S(1)}, bf16[288,512]{1,0:T(8,128)(2,1)S(1)}, u32[]{:S(2)}, u32[]{:S(2)}) %collective-permute-start.17) | collective-permute-done | bytes 294944 | tf_op jit(solution)/shard_map/ppermute | solution.py:70
  70.5 1.6 %collective-permute-done.22.refs_8_ = bf16[288,512]{1,0:T(8,128)(2,1)S(1)} collective-permute-done((bf16[288,512]{1,0:T(8,128)(2,1)S(1)}, bf16[288,512]{1,0:T(8,128)(2,1)S(1)}, u32[]{:S(2)}, u32[]{:S(2)}) %collective-permute-start.22) | collective-permute-done | bytes 294944 | tf_op jit(solution)/shard_map/ppermute | solution.py:79
  72.1 2.0 %expert.1 = (bf16[32,1536]{1,0:T(8,128)(2,1)S(1)}, bf16[32,1536]{1,0:T(8,128)(2,1)}) custom-call(bf16[32,1536]{1,0:T(8,128)(2,1)S(1)} %get-tuple-element.105.own, bf16[32,1536]{1,0:T(8,128)(2,1)S(1)} %collective-permute-done.18.other, bf16[576,512]{1,0:T(8,128)(2,1)S(1)} %get-tuple-element.59.refs_0_, bf16[576,512]{1,0:T(8,128)(2,1)S(1)} %collective-permute-done.3.refs_1_, ...), custom_call_target="tpu_custom_call" | custom-call | flops 1 | bytes 9437184 | tf_op jit(solution)/shard_map/expert/pallas_call | solution.py:510
  74.1 0.6 copy-done.5
  75.2 1.5 %write.1 = bf16[2048,128]{1,0:T(8,128)(2,1)} custom-call(bf16[16,144,128]{2,1,0:T(8,128)(2,1)S(1)} %all-to-all-done.arrived, bf16[2048,128]{1,0:T(8,128)(2,1)S(1)} %bitcast.14), custom_call_target="tpu_custom_call" | custom-call | flops 1 | bytes 2097152 | tf_op jit(solution)/shard_map/write/pallas_call | solution.py:612
  76.8 3.0 %collective-permute-done.23.returned = bf16[32,1536]{1,0:T(8,128)(2,1)S(1)} collective-permute-done((bf16[32,1536]{1,0:T(8,128)(2,1)}, bf16[32,1536]{1,0:T(8,128)(2,1)S(1)}, u32[]{:S(2)}, u32[]{:S(2)}) %collective-permute-start.23) | collective-permute-done | bytes 98336 | tf_op jit(solution)/shard_map/ppermute | solution.py:710
  79.8 1.1 %combine.1 = bf16[128,1536]{1,0:T(8,128)(2,1)} custom-call(bf16[128,1536]{1,0:T(8,128)(2,1)S(1)} %copy-done.3, f32[128,40]{1,0:T(8,128)S(1)} %get-tuple-element.100.gates, bf16[128,64]{1,0:T(8,128)(2,1)S(1)} %copy-done.8, bf16[32,1536]{1,0:T(8,128)(2,1)S(1)} %copy-done.6, bf16[32,1536]{1,0:T(8,128)(2,1)S(1)} %collective-permute-done.23.returned), custom_call_target="tpu_custom_call" | custom-call | flops 1 | bytes 1179648 | tf_op jit(solution)/shard_map/combine/pallas_call | solution.py:542
  (61 shorter events, 6.6 us)
Async XLA Ops:
  0.6 2.3 %collective-permute-start.2 = (bf16[96,1536]{1,0:T(8,128)(2,1)}, bf16[96,1536]{1,0:T(8,128)(2,1)S(1)}, u32[]{:S(2)}, u32[]{:S(2)}) collective-permute-start(bf16[96,1536]{1,0:T(8,128)(2,1)} %bitcast.20), channel_id=1, source_target_pairs={{0,2},{2,0},{4,6},{6,4},{8,10},{10,8},{12,14},{14,12},{16,18},{18,... | collective-permute-start | bytes 884744 | tf_op jit(solution)/shard_map/ppermute | solution.py:657
  0.7 2.2 %collective-permute-start = (bf16[96,1024]{1,0:T(8,128)(2,1)}, bf16[96,1024]{1,0:T(8,128)(2,1)S(1)}, u32[]{:S(2)}, u32[]{:S(2)}) collective-permute-start(bf16[96,1024]{1,0:T(8,128)(2,1)} %bitcast.22), channel_id=1, source_target_pairs={{0,2},{2,0},{4,6},{6,4},{8,10},{10,8},{12,14},{14,12},{16,18},{18,... | collective-permute-start | bytes 589832 | tf_op jit(solution)/shard_map/ppermute | solution.py:657
  1.2 1.7 %collective-permute-start.1 = (bf16[32,1536]{1,0:T(8,128)(2,1)}, bf16[32,1536]{1,0:T(8,128)(2,1)S(1)}, u32[]{:S(2)}, u32[]{:S(2)}) collective-permute-start(bf16[32,1536]{1,0:T(8,128)(2,1)} %bitcast.24), channel_id=1, source_target_pairs={{0,2},{2,0},{4,6},{6,4},{8,10},{10,8},{12,14},{14,12},{16,18},{18,... | collective-permute-start | bytes 294920 | tf_op jit(solution)/shard_map/ppermute | solution.py:657
  1.3 11.7 %collective-permute-start.5 = (bf16[128,1536]{1,0:T(8,128)(2,1)}, bf16[128,1536]{1,0:T(8,128)(2,1)S(1)}, u32[]{:S(2)}, u32[]{:S(2)}) collective-permute-start(bf16[128,1536]{1,0:T(8,128)(2,1)} %tokens.1), channel_id=1, source_target_pairs={{0,1},{1,0},{2,3},{3,2},{4,5},{5,4},{6,7},{7,6},{8,9},{9,8},{10,11... | collective-permute-start | bytes 1179656 | tf_op jit(solution)/shard_map/ppermute | solution.py:654
  4.1 8.9 %collective-permute-start.4 = (bf16[192,768]{1,0:T(8,128)(2,1)S(1)}, bf16[192,768]{1,0:T(8,128)(2,1)S(1)}, u32[]{:S(2)}, u32[]{:S(2)}) collective-permute-start(bf16[192,768]{1,0:T(8,128)(2,1)S(1)} %get-tuple-element.60.refs_0_), channel_id=1, source_target_pairs={{0,8},{2,6},{8,16},{10,2},{16,24},{18,10},{24,28},{26,18},{28,20},... | collective-permute-start | bytes 884744 | tf_op jit(solution)/shard_map/ppermute | solution.py:70
  4.6 18.1 %collective-permute-start.3 = (bf16[576,512]{1,0:T(8,128)(2,1)S(1)}, bf16[576,512]{1,0:T(8,128)(2,1)S(1)}, u32[]{:S(2)}, u32[]{:S(2)}) collective-permute-start(bf16[576,512]{1,0:T(8,128)(2,1)S(1)} %get-tuple-element.59.refs_0_), channel_id=1, source_target_pairs={{0,8},{2,6},{8,16},{10,2},{16,24},{18,10},{24,28},{26,18},{28,20},... | collective-permute-start | bytes 1769480 | tf_op jit(solution)/shard_map/ppermute | solution.py:70
  6.4 7.0 %copy-start.1 = (bf16[128,1536]{1,0:T(8,128)(2,1)S(1)}, bf16[128,1536]{1,0:T(8,128)(2,1)}, u32[]{:S(2)}) copy-start(bf16[128,1536]{1,0:T(8,128)(2,1)} %tokens.1) | copy-start | bytes 1179652
  6.4 7.0 %copy-start.11 = (bf16[1536,768]{1,0:T(8,128)(2,1)S(1)}, bf16[1536,768]{1,0:T(8,128)(2,1)}, u32[]{:S(2)}) copy-start(bf16[1536,768]{1,0:T(8,128)(2,1)} %w_query.1) | copy-start | bytes 7077892
  13.0 8.9 %collective-permute-start.6 = (bf16[192,768]{1,0:T(8,128)(2,1)S(1)}, bf16[192,768]{1,0:T(8,128)(2,1)S(1)}, u32[]{:S(2)}, u32[]{:S(2)}) collective-permute-start(bf16[192,768]{1,0:T(8,128)(2,1)S(1)} %collective-permute-done.4.refs_1_), channel_id=1, source_target_pairs={{0,8},{2,6},{8,16},{10,2},{16,24},{18,10},{24,28},{26,18},{28,20},... | collective-permute-start | bytes 884744 | tf_op jit(solution)/shard_map/ppermute | solution.py:70
  15.6 6.3 %collective-permute-start.7 = (bf16[128,512]{1,0:T(8,128)(2,1)S(1)}, bf16[128,512]{1,0:T(8,128)(2,1)S(1)}, u32[]{:S(2)}, u32[]{:S(2)}) collective-permute-start(bf16[128,512]{1,0:T(8,128)(2,1)S(1)} %get-tuple-element.70), channel_id=1, source_target_pairs={{0,2},{2,4},{4,6},{6,8},{8,10},{10,12},{12,14},{14,16},{16,18},{18... | collective-permute-start | bytes 393224 | tf_op jit(solution)/shard_map/ppermute | solution.py:672
  18.0 7.5 %collective-permute-start.10 = (bf16[192,768]{1,0:T(8,128)(2,1)S(1)}, bf16[192,768]{1,0:T(8,128)(2,1)S(1)}, u32[]{:S(2)}, u32[]{:S(2)}) collective-permute-start(bf16[192,768]{1,0:T(8,128)(2,1)S(1)} %collective-permute-done.4.refs_1_), channel_id=1, source_target_pairs={{0,2},{2,0},{4,6},{6,4},{8,10},{10,8},{12,14},{14,12},{16,18},{18,... | collective-permute-start | bytes 884744 | tf_op jit(solution)/shard_map/ppermute | solution.py:79
  21.9 3.7 %collective-permute-start.11 = (bf16[192,768]{1,0:T(8,128)(2,1)S(1)}, bf16[192,768]{1,0:T(8,128)(2,1)S(1)}, u32[]{:S(2)}, u32[]{:S(2)}) collective-permute-start(bf16[192,768]{1,0:T(8,128)(2,1)S(1)} %collective-permute-done.6.refs_2_), channel_id=1, source_target_pairs={{0,2},{2,0},{4,6},{6,4},{8,10},{10,8},{12,14},{14,12},{16,18},{18,... | collective-permute-start | bytes 884744 | tf_op jit(solution)/shard_map/ppermute | solution.py:79
  22.2 6.7 %collective-permute-start.9 = (bf16[192,768]{1,0:T(8,128)(2,1)S(1)}, bf16[192,768]{1,0:T(8,128)(2,1)S(1)}, u32[]{:S(2)}, u32[]{:S(2)}) collective-permute-start(bf16[192,768]{1,0:T(8,128)(2,1)S(1)} %collective-permute-done.6.refs_2_), channel_id=1, source_target_pairs={{0,8},{2,6},{8,16},{10,2},{16,24},{18,10},{24,28},{26,18},{28,20},... | collective-permute-start | bytes 884744 | tf_op jit(solution)/shard_map/ppermute | solution.py:70
  22.7 20.3 %collective-permute-start.8 = (bf16[576,512]{1,0:T(8,128)(2,1)S(1)}, bf16[576,512]{1,0:T(8,128)(2,1)S(1)}, u32[]{:S(2)}, u32[]{:S(2)}) collective-permute-start(bf16[576,512]{1,0:T(8,128)(2,1)S(1)} %collective-permute-done.3.refs_1_), channel_id=1, source_target_pairs={{0,8},{2,6},{8,16},{10,2},{16,24},{18,10},{24,28},{26,18},{28,20},... | collective-permute-start | bytes 1769480 | tf_op jit(solution)/shard_map/ppermute | solution.py:70
  29.0 1.6 %collective-permute-start.13 = (bf16[192,768]{1,0:T(8,128)(2,1)S(1)}, bf16[192,768]{1,0:T(8,128)(2,1)S(1)}, u32[]{:S(2)}, u32[]{:S(2)}) collective-permute-start(bf16[192,768]{1,0:T(8,128)(2,1)S(1)} %collective-permute-done.9.refs_3_), channel_id=1, source_target_pairs={{0,2},{2,0},{4,6},{6,4},{8,10},{10,8},{12,14},{14,12},{16,18},{18,... | collective-permute-start | bytes 884744 | tf_op jit(solution)/shard_map/ppermute | solution.py:79
  29.0 12.0 %copy-start.10 = (f32[1536]{0:T(1024)S(1)}, f32[1536]{0:T(1024)}, u32[]{:S(2)}) copy-start(f32[1536]{0:T(1024)} %flat_gain.1) | copy-start | bytes 18436
  29.0 7.9 %collective-permute-start.12 = (bf16[96,768]{1,0:T(8,128)(2,1)S(1)}, bf16[96,768]{1,0:T(8,128)(2,1)S(1)}, u32[]{:S(2)}, u32[]{:S(2)}) collective-permute-start(bf16[96,768]{1,0:T(8,128)(2,1)S(1)} %slice.6), channel_id=1, source_target_pairs={{0,8},{2,6},{8,16},{10,2},{16,24},{18,10},{24,28},{26,18},{28,20},... | collective-permute-start | bytes 442376 | tf_op jit(solution)/shard_map/ppermute | solution.py:70
  36.9 1.4 %collective-permute-start.14 = (bf16[96,768]{1,0:T(8,128)(2,1)S(1)}, bf16[96,768]{1,0:T(8,128)(2,1)S(1)}, u32[]{:S(2)}, u32[]{:S(2)}) collective-permute-start(bf16[96,768]{1,0:T(8,128)(2,1)S(1)} %collective-permute-done.12.refs_7_), channel_id=1, source_target_pairs={{0,2},{2,0},{4,6},{6,4},{8,10},{10,8},{12,14},{14,12},{16,18},{18,... | collective-permute-start | bytes 442376 | tf_op jit(solution)/shard_map/ppermute | solution.py:79
  39.4 12.6 %collective-permute-start.15 = (bf16[128,1536]{1,0:T(8,128)(2,1)S(1)}, bf16[128,1536]{1,0:T(8,128)(2,1)}, u32[]{:S(2)}, u32[]{:S(2)}) collective-permute-start(bf16[128,1536]{1,0:T(8,128)(2,1)S(1)} %outward_send.1), channel_id=1, source_target_pairs={{0,1},{1,0},{2,3},{3,2},{4,5},{5,4},{6,7},{7,6},{8,9},{9,8},{10,11... | collective-permute-start | bytes 1179656 | tf_op jit(solution)/shard_map/ppermute | solution.py:687
  43.0 11.6 %collective-permute-start.16 = (bf16[576,512]{1,0:T(8,128)(2,1)S(1)}, bf16[576,512]{1,0:T(8,128)(2,1)S(1)}, u32[]{:S(2)}, u32[]{:S(2)}) collective-permute-start(bf16[576,512]{1,0:T(8,128)(2,1)S(1)} %collective-permute-done.8.refs_2_), channel_id=1, source_target_pairs={{0,8},{2,6},{8,16},{10,2},{16,24},{18,10},{24,28},{26,18},{28,20},... | collective-permute-start | bytes 1769480 | tf_op jit(solution)/shard_map/ppermute | solution.py:70
  44.8 30.5 %all-to-all-start = ((bf16[16,144,128]{2,1,0:T(8,128)(2,1)}), bf16[16,144,128]{2,1,0:T(8,128)(2,1)S(1)}, u32[]{:S(2)}, u32[]{:S(2)}) async-start(bf16[16,144,128]{2,1,0:T(8,128)(2,1)} %bundle.1), calls=%async_computation | async-start | bytes 1179648 | tf_op jit(solution)/shard_map/all_to_all | solution.py:694
  55.3 15.2 %collective-permute-start.17 = (bf16[288,512]{1,0:T(8,128)(2,1)S(1)}, bf16[288,512]{1,0:T(8,128)(2,1)S(1)}, u32[]{:S(2)}, u32[]{:S(2)}) collective-permute-start(bf16[288,512]{1,0:T(8,128)(2,1)S(1)} %slice.7), channel_id=1, source_target_pairs={{0,8},{2,6},{8,16},{10,2},{16,24},{18,10},{24,28},{26,18},{28,20},... | collective-permute-start | bytes 884744 | tf_op jit(solution)/shard_map/ppermute | solution.py:70
  55.9 14.7 %collective-permute-start.19 = (bf16[576,512]{1,0:T(8,128)(2,1)S(1)}, bf16[576,512]{1,0:T(8,128)(2,1)S(1)}, u32[]{:S(2)}, u32[]{:S(2)}) collective-permute-start(bf16[576,512]{1,0:T(8,128)(2,1)S(1)} %collective-permute-done.3.refs_1_), channel_id=1, source_target_pairs={{0,2},{2,0},{4,6},{6,4},{8,10},{10,8},{12,14},{14,12},{16,18},{18,... | collective-permute-start | bytes 1769480 | tf_op jit(solution)/shard_map/ppermute | solution.py:79
  56.6 13.9 %collective-permute-start.20 = (bf16[576,512]{1,0:T(8,128)(2,1)S(1)}, bf16[576,512]{1,0:T(8,128)(2,1)S(1)}, u32[]{:S(2)}, u32[]{:S(2)}) collective-permute-start(bf16[576,512]{1,0:T(8,128)(2,1)S(1)} %collective-permute-done.8.refs_2_), channel_id=1, source_target_pairs={{0,2},{2,0},{4,6},{6,4},{8,10},{10,8},{12,14},{14,12},{16,18},{18,... | collective-permute-start | bytes 1769480 | tf_op jit(solution)/shard_map/ppermute | solution.py:79
  56.6 15.5 %collective-permute-start.21 = (bf16[576,512]{1,0:T(8,128)(2,1)S(1)}, bf16[576,512]{1,0:T(8,128)(2,1)S(1)}, u32[]{:S(2)}, u32[]{:S(2)}) collective-permute-start(bf16[576,512]{1,0:T(8,128)(2,1)S(1)} %collective-permute-done.16.refs_3_), channel_id=1, source_target_pairs={{0,2},{2,0},{4,6},{6,4},{8,10},{10,8},{12,14},{14,12},{16,18},{18,... | collective-permute-start | bytes 1769480 | tf_op jit(solution)/shard_map/ppermute | solution.py:79
  57.1 4.7 %collective-permute-start.18 = (bf16[32,1536]{1,0:T(8,128)(2,1)S(1)}, bf16[32,1536]{1,0:T(8,128)(2,1)S(1)}, u32[]{:S(2)}, u32[]{:S(2)}) collective-permute-start(bf16[32,1536]{1,0:T(8,128)(2,1)S(1)} %get-tuple-element.103), channel_id=1, source_target_pairs={{0,1},{1,0},{2,3},{3,2},{4,5},{5,4},{6,7},{7,6},{8,9},{9,8},{10,11... | collective-permute-start | bytes 294920 | tf_op jit(solution)/shard_map/ppermute | solution.py:700
  58.1 16.0 %copy-start.7 = (bf16[128,64]{1,0:T(8,128)(2,1)}, bf16[128,64]{1,0:T(8,128)(2,1)S(1)}, u32[]{:S(2)}) copy-start(bf16[128,64]{1,0:T(8,128)(2,1)S(1)} %get-tuple-element.101.spread) | copy-start | bytes 49156
  70.5 1.6 %collective-permute-start.22 = (bf16[288,512]{1,0:T(8,128)(2,1)S(1)}, bf16[288,512]{1,0:T(8,128)(2,1)S(1)}, u32[]{:S(2)}, u32[]{:S(2)}) collective-permute-start(bf16[288,512]{1,0:T(8,128)(2,1)S(1)} %collective-permute-done.17.refs_7_), channel_id=1, source_target_pairs={{0,2},{2,0},{4,6},{6,4},{8,10},{10,8},{12,14},{14,12},{16,18},{18,... | collective-permute-start | bytes 884744 | tf_op jit(solution)/shard_map/ppermute | solution.py:79
  74.7 5.1 %copy-start.3 = (bf16[128,1536]{1,0:T(8,128)(2,1)S(1)}, bf16[128,1536]{1,0:T(8,128)(2,1)}, u32[]{:S(2)}) copy-start(bf16[128,1536]{1,0:T(8,128)(2,1)} %copy-done.2) | copy-start | bytes 1179652
  74.7 5.1 %copy-start.6 = (bf16[32,1536]{1,0:T(8,128)(2,1)S(1)}, bf16[32,1536]{1,0:T(8,128)(2,1)}, u32[]{:S(2)}) copy-start(bf16[32,1536]{1,0:T(8,128)(2,1)} %copy-done.5) | copy-start | bytes 294916
  74.7 5.1 %copy-start.8 = (bf16[128,64]{1,0:T(8,128)(2,1)S(1)}, bf16[128,64]{1,0:T(8,128)(2,1)}, u32[]{:S(2)}) copy-start(bf16[128,64]{1,0:T(8,128)(2,1)} %copy-done.7) | copy-start | bytes 49156
  74.7 5.0 %collective-permute-start.23 = (bf16[32,1536]{1,0:T(8,128)(2,1)}, bf16[32,1536]{1,0:T(8,128)(2,1)S(1)}, u32[]{:S(2)}, u32[]{:S(2)}) collective-permute-start(bf16[32,1536]{1,0:T(8,128)(2,1)} %get-tuple-element.109), channel_id=1, source_target_pairs={{0,1},{1,0},{2,3},{3,2},{4,5},{5,4},{6,7},{7,6},{8,9},{9,8},{10,11... | collective-permute-start | bytes 294920 | tf_op jit(solution)/shard_map/ppermute | solution.py:710
  (7 other events, 17.3 us)

commit v9 on v8

--- a/solution.py
+++ b/solution.py
@@ -322,92 +322,109 @@
     )(own, other, gain, cosine, sine, w_query, flat_kv)
 
 
-def attend_kernel(q, kv, seam, past, mixed, window, sem):
-    count = seam.shape[0]
-    copy = pltpu.make_async_copy(seam, window.at[pl.ds(0, count), :], sem)
-    copy.start()
-    window[count:, :] = kv[...]
+def attend_rows_kernel(first, q, kv, seam, past, mixed, window, sem):
+    count = q.shape[0] // 2
+    if first == 0:
+        copy = pltpu.make_async_copy(seam, window.at[pl.ds(0, count), :], sem)
+        copy.start()
+        window[count:, :] = kv[:count, :]
+        copy.wait()
+        keyed = window
+    else:
+        keyed = kv
     head = 64
     kv_heads = kv.shape[1] // (2 * head)
     per_kv = q.shape[1] // head // kv_heads
     shape = (count, 2 * count)
     row = lax.broadcasted_iota(jnp.int32, shape, 0) + count
     col = lax.broadcasted_iota(jnp.int32, shape, 1)
-    for half in (1, 0):
-        first = half * count
-        if half == 0:
-            copy.wait()
-        reach = past[first : first + count, :1].astype(jnp.int32)
-        visible = (col <= row) & (col >= row - reach)
-        for kv_head in range(kv_heads):
-            lanes = 2 * head * kv_head
-            keys = window[first : first + 2 * count, lanes : lanes + head]
-            values = window[first : first + 2 * count, lanes + head : lanes + 2 * head]
-            for index in range(per_kv):
-                at = (kv_head * per_kv + index) * head
-                query = q[first : first + count, at : at + head]
-                scores = lax.dot_general(query, keys, LAST_DIMS, preferred_element_type=f32)
-                raised = jnp.where(visible, jnp.exp(scores * head ** (-0.5)), 0.0)
-                probs = (raised / jnp.sum(raised, axis=-1, keepdims=True)).astype(bf16)
-                made = jnp.dot(probs, values, preferred_element_type=f32)
-                mixed[first : first + count, at : at + head] = made.astype(bf16)
-
-
-def attend(q, kv, seam, past):
-    count = seam.shape[0]
-    return pl.pallas_call(
-        attend_kernel,
-        out_shape=jax.ShapeDtypeStruct(q.shape, bf16),
+    reach = past[first : first + count, :1].astype(jnp.int32)
+    visible = (col <= row) & (col >= row - reach)
+    for kv_head in range(kv_heads):
+        lanes = 2 * head * kv_head
+        keys = keyed[:, lanes : lanes + head]
+        values = keyed[:, lanes + head : lanes + 2 * head]
+        for index in range(per_kv):
+            at = (kv_head * per_kv + index) * head
+            query = q[first : first + count, at : at + head]
+            scores = lax.dot_general(query, keys, LAST_DIMS, preferred_element_type=f32)
+            raised = jnp.where(visible, jnp.exp(scores * head ** (-0.5)), 0.0)
+            probs = (raised / jnp.sum(raised, axis=-1, keepdims=True)).astype(bf16)
+            made = jnp.dot(probs, values, preferred_element_type=f32)
+            mixed[:, at : at + head] = made.astype(bf16)
+
+
+def attend_late(q, kv, past):
+    def kernel(q, kv, past, mixed):
+        attend_rows_kernel(q.shape[0] // 2, q, kv, None, past, mixed, None, None)
+
+    return pl.pallas_call(
+        kernel,
+        out_shape=jax.ShapeDtypeStruct((q.shape[0] // 2, q.shape[1]), bf16),
+        in_specs=[VMEM] * 3,
+        out_specs=VMEM,
+        compiler_params=PARAMS,
+        cost_estimate=takes(2),
+        name="attend_late",
+    )(q, kv, past)
+
+
+def attend_early(q, kv, seam, past):
+    return pl.pallas_call(
+        functools.partial(attend_rows_kernel, 0),
+        out_shape=jax.ShapeDtypeStruct((q.shape[0] // 2, q.shape[1]), bf16),
         in_specs=[VMEM, VMEM, ANY, VMEM],
         out_specs=VMEM,
-        scratch_shapes=[
-            pltpu.VMEM((3 * count, kv.shape[1]), bf16),
-            pltpu.SemaphoreType.DMA,
-        ],
-        compiler_params=PARAMS,
-        cost_estimate=takes(4),
-        name="attend",
+        scratch_shapes=[pltpu.VMEM(kv.shape, bf16), pltpu.SemaphoreType.DMA],
+        compiler_params=PARAMS,
+        cost_estimate=takes(2),
+        name="attend_early",
     )(q, kv, seam, past)
 
 
-def outward_rows(flip, groups, unit_rows, mixed, parts, w_out):
+def outward_rows(flip, groups, unit_rows, early, late, parts, w_out, rows):
     place_parts(groups, parts, unit_rows, [(0, unit_rows, w_out, 0)])
-    count = mixed.shape[0] // 2
     lane = lax.axis_index("hd")
-    first = pl.multiple_of(((1 - lane) if flip else lane) * count, count)
-    return lax.dot_general(
-        mixed[pl.ds(first, count), :], w_out[...], LAST_DIMS, preferred_element_type=f32
-    )
-
-
-def send_kernel(groups, unit_rows, n_parts, mixed, *refs):
-    parts, (out, w_out) = refs[:n_parts], refs[n_parts:]
-    out[...] = outward_rows(True, groups, unit_rows, mixed, parts, w_out).astype(bf16)
-
-
-def keep_kernel(groups, unit_rows, n_parts, mixed, tokens, flat_gain, *refs):
-    parts, (out, gain, w_out) = refs[:n_parts], refs[n_parts:]
+    which = (1 - lane) if flip else lane
+
+    @pl.when(which == 0)
+    def _():
+        rows[...] = early[...]
+
+    @pl.when(which != 0)
+    def _():
+        rows[...] = late[...]
+
+    return lax.dot_general(rows[...], w_out[...], LAST_DIMS, preferred_element_type=f32)
+
+
+def send_kernel(groups, unit_rows, n_parts, early, late, *refs):
+    parts, (out, w_out, rows) = refs[:n_parts], refs[n_parts:]
+    out[...] = outward_rows(True, groups, unit_rows, early, late, parts, w_out, rows).astype(bf16)
+
+
+def keep_kernel(groups, unit_rows, n_parts, early, late, tokens, flat_gain, *refs):
+    parts, (out, gain, w_out, rows) = refs[:n_parts], refs[n_parts:]
     gain[...] = flat_gain[...].reshape(gain.shape)
-    made = outward_rows(False, groups, unit_rows, mixed, parts, w_out)
+    made = outward_rows(False, groups, unit_rows, early, late, parts, w_out, rows)
     out[...] = tokens[...].astype(f32) + made
 
 
-def outward_send(groups, mixed, parts, unit_rows):
-    count = mixed.shape[0] // 2
+def outward_send(groups, early, late, parts, unit_rows):
     width, depth = groups * unit_rows, parts[0].shape[1]
     return pl.pallas_call(
         functools.partial(send_kernel, groups, unit_rows, len(parts)),
-        out_shape=jax.ShapeDtypeStruct((count, width), bf16),
-        in_specs=[VMEM] * (1 + len(parts)),
+        out_shape=jax.ShapeDtypeStruct((early.shape[0], width), bf16),
+        in_specs=[VMEM] * (2 + len(parts)),
         out_specs=VMEM,
-        scratch_shapes=[pltpu.VMEM((width, depth), bf16)],
+        scratch_shapes=[pltpu.VMEM((width, depth), bf16), pltpu.VMEM(early.shape, bf16)],
         compiler_params=PARAMS,
         cost_estimate=reads(2 * width * depth),
         name="outward_send",
-    )(mixed, *parts)
-
-
-def outward_keep(groups, mixed, tokens, gain, parts, unit_rows):
+    )(early, late, *parts)
+
+
+def outward_keep(groups, early, late, tokens, gain, parts, unit_rows):
     width, depth = groups * unit_rows, parts[0].shape[1]
     return pl.pallas_call(
         functools.partial(keep_kernel, groups, unit_rows, len(parts)),
@@ -415,13 +432,13 @@
             jax.ShapeDtypeStruct(tokens.shape, f32),
             jax.ShapeDtypeStruct((1, width), f32),
         ),
-        in_specs=[VMEM] * (3 + len(parts)),
+        in_specs=[VMEM] * (4 + len(parts)),
         out_specs=(VMEM, VMEM),
-        scratch_shapes=[pltpu.VMEM((width, depth), bf16)],
+        scratch_shapes=[pltpu.VMEM((width, depth), bf16), pltpu.VMEM(early.shape, bf16)],
         compiler_params=PARAMS,
         cost_estimate=reads(2 * width * depth),
         name="outward_keep",
-    )(mixed, tokens, gain, *parts)
+    )(early, late, tokens, gain, *parts)
 
 
 def route_kernel(mine, arrived, gain, place, residual, moe_in, sent):
@@ -670,48 +687,49 @@
 
     q, kv, tail = project(tokens, other_tokens, gain, cosine, sine, w_query, flat_kv)
     seam = lax.ppermute(tail, "grp", [(g, g + 1) for g in range(groups - 1)])
-    seam, q = out_ring.pin(seam, q)
+    q = out_ring.pin(q)
     out_ring.step()
-    q = expert_ring.pin(q)
+    out_ring.share(2)
+    late = attend_late(q, kv, past)
+    seam, late = together((seam, late))
+    seam = expert_ring.pin(seam)
     expert_ring.step()
-    out_ring.share(2)
-    mixed = attend(q, kv, seam, past)
-    mixed, out_ring.near = together((mixed, out_ring.near))
-    mixed = out_ring.pin(mixed)
+    early = attend_early(q, kv, seam, past)
+    early, out_ring.near = together((early, out_ring.near))
+    early = out_ring.pin(early)
     out_ring.step()
     out_ring.share(3)
-    mixed, out_ring.near = together((mixed, out_ring.near))
-    mixed = out_ring.pin(mixed)
-    out_ring.share()
-    sent = outward_send(groups, mixed, out_ring.parts(), out_ring.unit_rows)
-    arrived = swap(sent)
-    mixed = together((mixed, sent))[0]
-    mine, late_gain = outward_keep(
-        groups, mixed, tokens, moe_gain, out_ring.parts(), out_ring.unit_rows
-    )
-    kv, mine = together((kv, mine))
+    early, kv, out_ring.near = together((early, kv, out_ring.near))
     outgoing = bundle(groups, send, kv, tags)
     arrived_cache = lax.all_to_all(outgoing, "grp", split_axis=0, concat_axis=0, tiled=True)
+    early, outgoing = together((early, outgoing))
+    early = out_ring.pin(early)
+    early = expert_ring.pin(early)
+    expert_ring.step()
+    out_ring.share()
+    sent = outward_send(groups, early, late, out_ring.parts(), out_ring.unit_rows)
+    arrived = swap(sent)
+    early = together((early, sent))[0]
+    mine, late_gain = outward_keep(
+        groups, early, late, tokens, moe_gain, out_ring.parts(), out_ring.unit_rows
+    )
     mine = expert_ring.pin(mine)
     expert_ring.share()
     expert_ring.step()
+    arrived, mine = expert_ring.pin(arrived, mine)
+    expert_ring.share()
 
     residual, moe_in, sent_rows = route(mine, arrived, late_gain, place)
     landed = swap(sent_rows)
-    moe_in = expert_ring.pin(moe_in)
-    expert_ring.share()
-    expert_ring.step()
     gates, own_rows, spread = gate(moe_in, router.T, expert_ids.T, place)
-    landed, own_rows = expert_ring.pin(landed, own_rows)
-    expert_ring.share()
+    landed, own_rows = together((landed, own_rows))
     own_made, back = expert(
         groups, own_rows, landed, expert_ring.parts(), up_rows, down_rows
     )
     returned = swap(back)
-    arrived_cache = together((arrived_cache, back))[0]
+    layer_out = combine(residual, gates, spread, own_made, returned)
+    layer_out, arrived_cache = together((layer_out, arrived_cache))
     cache_after = write(arrived_cache, kv_cache)
-    returned, cache_after = together((returned, cache_after))
-    layer_out = combine(residual, gates, spread, own_made, returned)
     return (layer_out, cache_after)
 
 

time: 81.3 us -> 78 us (0.959)
  the two profiles are of different devices: /device:TPU:12 before, /device:TPU:18 now
where the time goes in v9:
time: 78 us; the launch traced here: 77.6 us
  waiting for transfers between devices  31.7 us (41%)
  starting transfers between devices  22.7 us (29%)
  Pallas kernels  17.2 us (22%)
  local copies, waits for them, and re-layouts  5.08 us (7%)
  between operations  0.87 us (1%)
    ppermute x8, starting transfers between devices, step(): self.mine.append(self.across(held))  11.7 us
    ppermute x8, waiting for transfers between devices, step(): self.mine.append(self.across(held))  10.3 us
    ppermute x1, waiting for transfers between devices, two_lane_shards(): arrived = swap(sent)  6.81 us
    unnamed x35, local copies, waits for them, and re-layouts  5.05 us
    all_to_all x1, starting transfers between devices, two_lane_shards(): lax.all_to_all(outgoing, 'grp', split_axis=0, concat_axis=0, tiled=True)  4.82 us
    ppermute x1, waiting for transfers between devices, two_lane_shards(): landed = swap(sent_rows)  4.25 us
    ppermute x1, waiting for transfers between devices, two_lane_shards(): returned = swap(back)  4.09 us
    pallas_call x1, Pallas kernels, expert(): pl.pallas_call(functools.partial(expert_kernel, groups, up_rows, down_row...  2.44 us
  transfers between devices with their start and end apart: 25, of which 12 were waited for; matrix products, arithmetic and copies ran while one was open for 2% of the time, Pallas kernels for 20%

profile of v9, /device:TPU:18, one launch (start us, length us, event | category | flops | bytes accessed | tf_op | source)
XLA Modules:
  0.0 77.6 jit_solution(11706043580296729879)
XLA Ops:
  1.8 1.1 %collective-permute-done.1.refs_4_ = bf16[32,1536]{1,0:T(8,128)(2,1)S(1)} collective-permute-done((bf16[32,1536]{1,0:T(8,128)(2,1)}, bf16[32,1536]{1,0:T(8,128)(2,1)S(1)}, u32[]{:S(2)}, u32[]{:S(2)}) %collective-permute-start.1) | collective-permute-done | bytes 98336 | tf_op jit(solution)/shard_map/ppermute | solution.py:674
  2.9 1.1 %pack.1 = (bf16[576,512]{1,0:T(8,128)(2,1)S(1)}, bf16[192,768]{1,0:T(8,128)(2,1)S(1)}) custom-call(bf16[96,1024]{1,0:T(8,128)(2,1)} %bitcast.23, bf16[32,1536]{1,0:T(8,128)(2,1)} %bitcast.25, bf16[96,1536]{1,0:T(8,128)(2,1)} %bitcast.21, bf16[96,1024]{1,0:T(8,128)(2,1)S(1)} %collective-permute-done.refs_3_, ...), custom_call_target="tpu_custom_call" | custom-call | flops 1 | bytes 1 | tf_op jit(solution)/shard_map/pack/pallas_call | solution.py:159
  4.1 1.6 %collective-permute-start.4 = (bf16[192,768]{1,0:T(8,128)(2,1)S(1)}, bf16[192,768]{1,0:T(8,128)(2,1)S(1)}, u32[]{:S(2)}, u32[]{:S(2)}) collective-permute-start(bf16[192,768]{1,0:T(8,128)(2,1)S(1)} %get-tuple-element.62.refs_0_), channel_id=1, source_target_pairs={{0,8},{2,6},{8,16},{10,2},{16,24},{18,10},{24,28},{26,18},{28,20},... | collective-permute-start | bytes 884744 | tf_op jit(solution)/shard_map/ppermute | solution.py:70
  5.7 1.5 %collective-permute-start.3 = (bf16[576,512]{1,0:T(8,128)(2,1)S(1)}, bf16[576,512]{1,0:T(8,128)(2,1)S(1)}, u32[]{:S(2)}, u32[]{:S(2)}) collective-permute-start(bf16[576,512]{1,0:T(8,128)(2,1)S(1)} %get-tuple-element.61.refs_0_), channel_id=1, source_target_pairs={{0,8},{2,6},{8,16},{10,2},{16,24},{18,10},{24,28},{26,18},{28,20},... | collective-permute-start | bytes 1769480 | tf_op jit(solution)/shard_map/ppermute | solution.py:70
  7.2 1.5 %prepare.1 = (f32[256,128]{1,0:T(8,128)S(1)}, f32[256,128]{1,0:T(8,128)S(1)}, f32[256,128]{1,0:T(8,128)S(1)}, bf16[64,128]{1,0:T(8,128)(2,1)S(1)}, bf16[512,256]...) custom-call(s32[1,256]{1,0:T(1,128)} %bitcast.26, s32[1,256]{1,0:T(1,128)} %bitcast.27, ...), custom_call_target="tpu_custom_call" | custom-call | flops 1 | bytes 1 | tf_op jit(solution)/shard_map/prepare/pallas_call | solution.py:255
  8.7 1.8 %copy.17 = bf16[192,8,4,128]{3,1,2,0:T(8,128)(2,1)S(1)} copy(bf16[192,8,4,128]{3,2,1,0:T(4,128)(2,1)} %bitcast.18) | data formatting | bytes 3145728
  10.6 2.4 %collective-permute-done.5.other = bf16[128,1536]{1,0:T(8,128)(2,1)S(1)} collective-permute-done((bf16[128,1536]{1,0:T(8,128)(2,1)}, bf16[128,1536]{1,0:T(8,128)(2,1)S(1)}, u32[]{:S(2)}, u32[]{:S(2)}) %collective-permute-start.5) | collective-permute-done | bytes 393248 | tf_op jit(solution)/shard_map/ppermute | solution.py:671
  13.0 1.6 %collective-permute-start.7 = (bf16[192,768]{1,0:T(8,128)(2,1)S(1)}, bf16[192,768]{1,0:T(8,128)(2,1)S(1)}, u32[]{:S(2)}, u32[]{:S(2)}) collective-permute-start(bf16[192,768]{1,0:T(8,128)(2,1)S(1)} %collective-permute-done.4.refs_1_), channel_id=1, source_target_pairs={{0,8},{2,6},{8,16},{10,2},{16,24},{18,10},{24,28},{26,18},{28,20},... | collective-permute-start | bytes 884744 | tf_op jit(solution)/shard_map/ppermute | solution.py:70
  14.6 2.2 %project.1 = (bf16[256,768]{1,0:T(8,128)(2,1)S(1)}, bf16[256,512]{1,0:T(8,128)(2,1)S(1)}, bf16[128,512]{1,0:T(8,128)(2,1)S(1)}) custom-call(bf16[128,1536]{1,0:T(8,128)(2,1)S(1)} %copy-done.11, bf16[128,1536]{1,0:T(8,128)(2,1)S(1)} %collective-permute-done.5.other, f32[1,1536]{1,0:T(1,128)S(1)} %get-tuple-element.67.gain, ...), custom_call_target="tpu_custom_call" | custom-call | flops 9200000000 | bytes 64000000 | tf_op jit(solution)/shard_map/project/pallas_call | solution.py:305
  16.8 2.4 %collective-permute-start.6 = (bf16[128,512]{1,0:T(8,128)(2,1)S(1)}, bf16[128,512]{1,0:T(8,128)(2,1)S(1)}, u32[]{:S(2)}, u32[]{:S(2)}) collective-permute-start(bf16[128,512]{1,0:T(8,128)(2,1)S(1)} %get-tuple-element.71), channel_id=1, source_target_pairs={{0,2},{2,4},{4,6},{6,8},{8,10},{10,12},{12,14},{14,16},{16,18},{18... | collective-permute-start | bytes 393224 | tf_op jit(solution)/shard_map/ppermute | solution.py:689
  19.2 1.1 %collective-permute-done.7.refs_2_ = bf16[192,768]{1,0:T(8,128)(2,1)S(1)} collective-permute-done((bf16[192,768]{1,0:T(8,128)(2,1)S(1)}, bf16[192,768]{1,0:T(8,128)(2,1)S(1)}, u32[]{:S(2)}, u32[]{:S(2)}) %collective-permute-start.7) | collective-permute-done | bytes 294944 | tf_op jit(solution)/shard_map/ppermute | solution.py:70
  20.3 1.6 %collective-permute-start.9 = (bf16[192,768]{1,0:T(8,128)(2,1)S(1)}, bf16[192,768]{1,0:T(8,128)(2,1)S(1)}, u32[]{:S(2)}, u32[]{:S(2)}) collective-permute-start(bf16[192,768]{1,0:T(8,128)(2,1)S(1)} %collective-permute-done.7.refs_2_), channel_id=1, source_target_pairs={{0,8},{2,6},{8,16},{10,2},{16,24},{18,10},{24,28},{26,18},{28,20},... | collective-permute-start | bytes 884744 | tf_op jit(solution)/shard_map/ppermute | solution.py:70
  21.9 1.3 %attend_late.1.late = bf16[128,768]{1,0:T(8,128)(2,1)S(1)} custom-call(bf16[256,768]{1,0:T(8,128)(2,1)S(1)} %get-tuple-element.74.q, bf16[256,512]{1,0:T(8,128)(2,1)S(1)} %get-tuple-element.88.kv, f32[256,128]{1,0:T(8,128)S(1)} %get-tuple-element.76.past), custom_call_target="tpu_custom_call" | custom-call | flops 2300000000 | bytes 16000000 | tf_op jit(solution)/shard_map/attend_late/pallas_call | solution.py:361
  24.0 1.6 %collective-permute-start.8 = (bf16[576,512]{1,0:T(8,128)(2,1)S(1)}, bf16[576,512]{1,0:T(8,128)(2,1)}, u32[]{:S(2)}, u32[]{:S(2)}) collective-permute-start(bf16[576,512]{1,0:T(8,128)(2,1)S(1)} %collective-permute-done.3.refs_1_), channel_id=1, source_target_pairs={{0,8},{2,6},{8,16},{10,2},{16,24},{18,10},{24,28},{26,18},{28,20},... | collective-permute-start | bytes 1769480 | tf_op jit(solution)/shard_map/ppermute | solution.py:70
  25.6 1.5 %attend_early.1.early = bf16[128,768]{1,0:T(8,128)(2,1)S(1)} custom-call(bf16[256,768]{1,0:T(8,128)(2,1)S(1)} %get-tuple-element.74.q, bf16[256,512]{1,0:T(8,128)(2,1)S(1)} %get-tuple-element.88.kv, bf16[128,512]{1,0:T(8,128)(2,1)S(1)} %collective-permute-done.6.seam, f32[256,128]{1,0:T(8,128)S(1)} %get-tuple-element.76.past), custom_call_target="tpu_custom_call" | custom-call | flops 2300000000 | bytes 16000000 | tf_op jit(solution)/shard_map/attend_early/pallas_call | solution.py:373
  27.8 1.0 %collective-permute-start.12 = (bf16[96,768]{1,0:T(8,128)(2,1)S(1)}, bf16[96,768]{1,0:T(8,128)(2,1)S(1)}, u32[]{:S(2)}, u32[]{:S(2)}) collective-permute-start(bf16[96,768]{1,0:T(8,128)(2,1)S(1)} %slice.6), channel_id=1, source_target_pairs={{0,8},{2,6},{8,16},{10,2},{16,24},{18,10},{24,28},{26,18},{28,20},... | collective-permute-start | bytes 442376 | tf_op jit(solution)/shard_map/ppermute | solution.py:70
  29.4 1.4 %bundle.1 = bf16[16,144,128]{2,1,0:T(8,128)(2,1)} custom-call(bf16[512,256]{1,0:T(8,128)(2,1)S(1)} %get-tuple-element.87.send, bf16[256,512]{1,0:T(8,128)(2,1)S(1)} %get-tuple-element.88.kv, bf16[256,128]{1,0:T(8,128)(2,1)S(1)} %get-tuple-element.89.tags), custom_call_target="tpu_custom_call" | custom-call | flops 1 | bytes 1 | tf_op jit(solution)/shard_map/bundle/pallas_call | solution.py:589
  30.7 4.7 %collective-permute-done.12.refs_7_ = bf16[96,768]{1,0:T(8,128)(2,1)S(1)} collective-permute-done((bf16[96,768]{1,0:T(8,128)(2,1)S(1)}, bf16[96,768]{1,0:T(8,128)(2,1)S(1)}, u32[]{:S(2)}, u32[]{:S(2)}) %collective-permute-start.12) | collective-permute-done | bytes 147488 | tf_op jit(solution)/shard_map/ppermute | solution.py:70
  36.1 1.6 %collective-permute-start.14 = (bf16[576,512]{1,0:T(8,128)(2,1)}, bf16[576,512]{1,0:T(8,128)(2,1)S(1)}, u32[]{:S(2)}, u32[]{:S(2)}) collective-permute-start(bf16[576,512]{1,0:T(8,128)(2,1)} %collective-permute-done.8.refs_2_), channel_id=1, source_target_pairs={{0,8},{2,6},{8,16},{10,2},{16,24},{18,10},{24,28},{26,18},{28,20},... | collective-permute-start | bytes 1769480 | tf_op jit(solution)/shard_map/ppermute | solution.py:70
  37.7 4.8 %all-to-all-start = ((bf16[16,144,128]{2,1,0:T(8,128)(2,1)}), bf16[16,144,128]{2,1,0:T(8,128)(2,1)S(1)}, u32[]{:S(2)}, u32[]{:S(2)}) async-start(bf16[16,144,128]{2,1,0:T(8,128)(2,1)} %bundle.1), calls=%async_computation | async-start | bytes 1179648 | tf_op jit(solution)/shard_map/all_to_all | solution.py:704
  42.6 1.4 %collective-permute-done.15.refs_8_ = bf16[96,768]{1,0:T(8,128)(2,1)S(1)} collective-permute-done((bf16[96,768]{1,0:T(8,128)(2,1)}, bf16[96,768]{1,0:T(8,128)(2,1)S(1)}, u32[]{:S(2)}, u32[]{:S(2)}) %collective-permute-start.15) | collective-permute-done | bytes 147488 | tf_op jit(solution)/shard_map/ppermute | solution.py:79
  44.1 0.9 %copy-done.1 = bf16[128,768]{1,0:T(8,128)(2,1)S(1)} copy-done((bf16[128,768]{1,0:T(8,128)(2,1)S(1)}, bf16[128,768]{1,0:T(8,128)(2,1)}, u32[]{:S(2)}) %copy-start.1) | copy-done | bytes 196632
  45.9 1.2 %outward_send.1 = bf16[128,1536]{1,0:T(8,128)(2,1)S(1)} custom-call(bf16[128,768]{1,0:T(8,128)(2,1)S(1)} %copy-done.1, bf16[128,768]{1,0:T(8,128)(2,1)S(1)} %attend_late.1.late, bf16[192,768]{1,0:T(8,128)(2,1)S(1)} %get-tuple-element.62.refs_0_, bf16[192,768]{1,0:T(8,128)(2,1)S(1)} %collective-permute-done.4.refs_1_, ...), custom_call_target="tpu_custom_call" | custom-call | flops 1 | bytes 2359296 | tf_op jit(solution)/shard_map/outward_send/pallas_call | solution.py:415
  47.7 1.2 %outward_keep.1 = (f32[128,1536]{1,0:T(8,128)S(1)}, f32[1,1536]{1,0:T(1,128)S(1)}) custom-call(bf16[128,768]{1,0:T(8,128)(2,1)S(1)} %copy-done.2, bf16[128,768]{1,0:T(8,128)(2,1)S(1)} %attend_late.1.late, bf16[128,1536]{1,0:T(8,128)(2,1)S(1)} %copy-done.12, f32[1536]{0:T(1024)S(1)} %copy-done.15, bf16[192,768]{1,0:T(8,128)(2,1)S(1)} %get-tuple-element.62.refs_0_, ...), custom_call_target="tpu_custom_call" | custom-call | flops 1 | bytes 2359296 | tf_op jit(solution)/shard_map/outward_keep/pallas_call | solution.py:429
  49.7 1.3 %collective-permute-start.16 = (bf16[288,512]{1,0:T(8,128)(2,1)S(1)}, bf16[288,512]{1,0:T(8,128)(2,1)S(1)}, u32[]{:S(2)}, u32[]{:S(2)}) collective-permute-start(bf16[288,512]{1,0:T(8,128)(2,1)S(1)} %slice.7), channel_id=1, source_target_pairs={{0,8},{2,6},{8,16},{10,2},{16,24},{18,10},{24,28},{26,18},{28,20},... | collective-permute-start | bytes 884744 | tf_op jit(solution)/shard_map/ppermute | solution.py:70
  51.5 6.8 %collective-permute-done.17.arrived = bf16[128,1536]{1,0:T(8,128)(2,1)S(1)} collective-permute-done((bf16[128,1536]{1,0:T(8,128)(2,1)S(1)}, bf16[128,1536]{1,0:T(8,128)(2,1)S(1)}, u32[]{:S(2)}, u32[]{:S(2)}) %collective-permute-start.17) | collective-permute-done | bytes 393248 | tf_op jit(solution)/shard_map/ppermute | solution.py:711
  58.3 3.7 %collective-permute-done.16.refs_7_ = bf16[288,512]{1,0:T(8,128)(2,1)S(1)} collective-permute-done((bf16[288,512]{1,0:T(8,128)(2,1)S(1)}, bf16[288,512]{1,0:T(8,128)(2,1)S(1)}, u32[]{:S(2)}, u32[]{:S(2)}) %collective-permute-start.16) | collective-permute-done | bytes 294944 | tf_op jit(solution)/shard_map/ppermute | solution.py:70
  63.4 4.2 %collective-permute-done.18.other = bf16[32,1536]{1,0:T(8,128)(2,1)S(1)} collective-permute-done((bf16[32,1536]{1,0:T(8,128)(2,1)S(1)}, bf16[32,1536]{1,0:T(8,128)(2,1)S(1)}, u32[]{:S(2)}, u32[]{:S(2)}) %collective-permute-start.18) | collective-permute-done | bytes 98336 | tf_op jit(solution)/shard_map/ppermute | solution.py:723
  67.7 2.4 %expert.1 = (bf16[32,1536]{1,0:T(8,128)(2,1)S(1)}, bf16[32,1536]{1,0:T(8,128)(2,1)S(1)}) custom-call(bf16[32,1536]{1,0:T(8,128)(2,1)S(1)} %get-tuple-element.113.own, bf16[32,1536]{1,0:T(8,128)(2,1)S(1)} %collective-permute-done.18.other, bf16[576,512]{1,0:T(8,128)(2,1)S(1)} %copy-done.4, bf16[576,512]{1,0:T(8,128)(2,1)S(1)} %copy-done.6, ...), custom_call_target="tpu_custom_call" | custom-call | flops 1 | bytes 9437184 | tf_op jit(solution)/shard_map/expert/pallas_call | solution.py:527
  70.8 4.1 %collective-permute-done.23.returned = bf16[32,1536]{1,0:T(8,128)(2,1)S(1)} collective-permute-done((bf16[32,1536]{1,0:T(8,128)(2,1)S(1)}, bf16[32,1536]{1,0:T(8,128)(2,1)S(1)}, u32[]{:S(2)}, u32[]{:S(2)}) %collective-permute-start.23) | collective-permute-done | bytes 98336 | tf_op jit(solution)/shard_map/ppermute | solution.py:729
  74.9 1.1 %combine.1 = bf16[128,1536]{1,0:T(8,128)(2,1)} custom-call(bf16[128,1536]{1,0:T(8,128)(2,1)S(1)} %get-tuple-element.107.residual, f32[128,40]{1,0:T(8,128)S(1)} %get-tuple-element.109.gates, bf16[128,64]{1,0:T(8,128)(2,1)S(1)} %get-tuple-element.110.spread, bf16[32,1536]{1,0:T(8,128)(2,1)S(1)} %get-tuple-element.116.own, ...), custom_call_target="tpu_custom_call" | custom-call | flops 1 | bytes 1179648 | tf_op jit(solution)/shard_map/combine/pallas_call | solution.py:559
  76.0 1.5 %write.1 = bf16[2048,128]{1,0:T(8,128)(2,1)} custom-call(bf16[16,144,128]{2,1,0:T(8,128)(2,1)S(1)} %all-to-all-done.arrived, bf16[2048,128]{1,0:T(8,128)(2,1)S(1)} %bitcast.14), custom_call_target="tpu_custom_call" | custom-call | flops 1 | bytes 2097152 | tf_op jit(solution)/shard_map/write/pallas_call | solution.py:629
  (68 shorter events, 9.0 us)
Async XLA Ops:
  0.6 2.3 %collective-permute-start.2 = (bf16[96,1536]{1,0:T(8,128)(2,1)}, bf16[96,1536]{1,0:T(8,128)(2,1)S(1)}, u32[]{:S(2)}, u32[]{:S(2)}) collective-permute-start(bf16[96,1536]{1,0:T(8,128)(2,1)} %bitcast.20), channel_id=1, source_target_pairs={{0,2},{2,0},{4,6},{6,4},{8,10},{10,8},{12,14},{14,12},{16,18},{18,... | collective-permute-start | bytes 884744 | tf_op jit(solution)/shard_map/ppermute | solution.py:674
  0.7 2.2 %collective-permute-start = (bf16[96,1024]{1,0:T(8,128)(2,1)}, bf16[96,1024]{1,0:T(8,128)(2,1)S(1)}, u32[]{:S(2)}, u32[]{:S(2)}) collective-permute-start(bf16[96,1024]{1,0:T(8,128)(2,1)} %bitcast.22), channel_id=1, source_target_pairs={{0,2},{2,0},{4,6},{6,4},{8,10},{10,8},{12,14},{14,12},{16,18},{18,... | collective-permute-start | bytes 589832 | tf_op jit(solution)/shard_map/ppermute | solution.py:674
  1.2 1.7 %collective-permute-start.1 = (bf16[32,1536]{1,0:T(8,128)(2,1)}, bf16[32,1536]{1,0:T(8,128)(2,1)S(1)}, u32[]{:S(2)}, u32[]{:S(2)}) collective-permute-start(bf16[32,1536]{1,0:T(8,128)(2,1)} %bitcast.24), channel_id=1, source_target_pairs={{0,2},{2,0},{4,6},{6,4},{8,10},{10,8},{12,14},{14,12},{16,18},{18,... | collective-permute-start | bytes 294920 | tf_op jit(solution)/shard_map/ppermute | solution.py:674
  1.3 11.7 %collective-permute-start.5 = (bf16[128,1536]{1,0:T(8,128)(2,1)}, bf16[128,1536]{1,0:T(8,128)(2,1)S(1)}, u32[]{:S(2)}, u32[]{:S(2)}) collective-permute-start(bf16[128,1536]{1,0:T(8,128)(2,1)} %tokens.1), channel_id=1, source_target_pairs={{0,1},{1,0},{2,3},{3,2},{4,5},{5,4},{6,7},{7,6},{8,9},{9,8},{10,11... | collective-permute-start | bytes 1179656 | tf_op jit(solution)/shard_map/ppermute | solution.py:671
  4.1 6.5 %copy-start.3 = (bf16[576,512]{1,0:T(8,128)(2,1)}, bf16[576,512]{1,0:T(8,128)(2,1)S(1)}, u32[]{:S(2)}) copy-start(bf16[576,512]{1,0:T(8,128)(2,1)S(1)} %get-tuple-element.61.refs_0_) | copy-start | bytes 1769476
  4.1 8.9 %collective-permute-start.4 = (bf16[192,768]{1,0:T(8,128)(2,1)S(1)}, bf16[192,768]{1,0:T(8,128)(2,1)S(1)}, u32[]{:S(2)}, u32[]{:S(2)}) collective-permute-start(bf16[192,768]{1,0:T(8,128)(2,1)S(1)} %get-tuple-element.62.refs_0_), channel_id=1, source_target_pairs={{0,8},{2,6},{8,16},{10,2},{16,24},{18,10},{24,28},{26,18},{28,20},... | collective-permute-start | bytes 884744 | tf_op jit(solution)/shard_map/ppermute | solution.py:70
  5.7 18.3 %collective-permute-start.3 = (bf16[576,512]{1,0:T(8,128)(2,1)S(1)}, bf16[576,512]{1,0:T(8,128)(2,1)S(1)}, u32[]{:S(2)}, u32[]{:S(2)}) collective-permute-start(bf16[576,512]{1,0:T(8,128)(2,1)S(1)} %get-tuple-element.61.refs_0_), channel_id=1, source_target_pairs={{0,8},{2,6},{8,16},{10,2},{16,24},{18,10},{24,28},{26,18},{28,20},... | collective-permute-start | bytes 1769480 | tf_op jit(solution)/shard_map/ppermute | solution.py:70
  8.7 5.9 %copy-start.11 = (bf16[128,1536]{1,0:T(8,128)(2,1)S(1)}, bf16[128,1536]{1,0:T(8,128)(2,1)}, u32[]{:S(2)}) copy-start(bf16[128,1536]{1,0:T(8,128)(2,1)} %tokens.1) | copy-start | bytes 1179652
  8.7 5.9 %copy-start.16 = (bf16[1536,768]{1,0:T(8,128)(2,1)S(1)}, bf16[1536,768]{1,0:T(8,128)(2,1)}, u32[]{:S(2)}) copy-start(bf16[1536,768]{1,0:T(8,128)(2,1)} %w_query.1) | copy-start | bytes 7077892
  13.0 7.4 %collective-permute-start.7 = (bf16[192,768]{1,0:T(8,128)(2,1)S(1)}, bf16[192,768]{1,0:T(8,128)(2,1)S(1)}, u32[]{:S(2)}, u32[]{:S(2)}) collective-permute-start(bf16[192,768]{1,0:T(8,128)(2,1)S(1)} %collective-permute-done.4.refs_1_), channel_id=1, source_target_pairs={{0,8},{2,6},{8,16},{10,2},{16,24},{18,10},{24,28},{26,18},{28,20},... | collective-permute-start | bytes 884744 | tf_op jit(solution)/shard_map/ppermute | solution.py:70
  14.5 13.2 %collective-permute-start.10 = (bf16[192,768]{1,0:T(8,128)(2,1)S(1)}, bf16[192,768]{1,0:T(8,128)(2,1)S(1)}, u32[]{:S(2)}, u32[]{:S(2)}) collective-permute-start(bf16[192,768]{1,0:T(8,128)(2,1)S(1)} %collective-permute-done.4.refs_1_), channel_id=1, source_target_pairs={{0,2},{2,0},{4,6},{6,4},{8,10},{10,8},{12,14},{14,12},{16,18},{18,... | collective-permute-start | bytes 884744 | tf_op jit(solution)/shard_map/ppermute | solution.py:79
  16.8 7.2 %collective-permute-start.6 = (bf16[128,512]{1,0:T(8,128)(2,1)S(1)}, bf16[128,512]{1,0:T(8,128)(2,1)S(1)}, u32[]{:S(2)}, u32[]{:S(2)}) collective-permute-start(bf16[128,512]{1,0:T(8,128)(2,1)S(1)} %get-tuple-element.71), channel_id=1, source_target_pairs={{0,2},{2,4},{4,6},{6,8},{8,10},{10,12},{12,14},{14,16},{16,18},{18... | collective-permute-start | bytes 393224 | tf_op jit(solution)/shard_map/ppermute | solution.py:689
  20.3 7.4 %collective-permute-start.11 = (bf16[192,768]{1,0:T(8,128)(2,1)S(1)}, bf16[192,768]{1,0:T(8,128)(2,1)S(1)}, u32[]{:S(2)}, u32[]{:S(2)}) collective-permute-start(bf16[192,768]{1,0:T(8,128)(2,1)S(1)} %collective-permute-done.7.refs_2_), channel_id=1, source_target_pairs={{0,2},{2,0},{4,6},{6,4},{8,10},{10,8},{12,14},{14,12},{16,18},{18,... | collective-permute-start | bytes 884744 | tf_op jit(solution)/shard_map/ppermute | solution.py:79
  20.3 7.4 %collective-permute-start.9 = (bf16[192,768]{1,0:T(8,128)(2,1)S(1)}, bf16[192,768]{1,0:T(8,128)(2,1)S(1)}, u32[]{:S(2)}, u32[]{:S(2)}) collective-permute-start(bf16[192,768]{1,0:T(8,128)(2,1)S(1)} %collective-permute-done.7.refs_2_), channel_id=1, source_target_pairs={{0,8},{2,6},{8,16},{10,2},{16,24},{18,10},{24,28},{26,18},{28,20},... | collective-permute-start | bytes 884744 | tf_op jit(solution)/shard_map/ppermute | solution.py:70
  24.0 11.5 %collective-permute-start.8 = (bf16[576,512]{1,0:T(8,128)(2,1)S(1)}, bf16[576,512]{1,0:T(8,128)(2,1)}, u32[]{:S(2)}, u32[]{:S(2)}) collective-permute-start(bf16[576,512]{1,0:T(8,128)(2,1)S(1)} %collective-permute-done.3.refs_1_), channel_id=1, source_target_pairs={{0,8},{2,6},{8,16},{10,2},{16,24},{18,10},{24,28},{26,18},{28,20},... | collective-permute-start | bytes 1769480 | tf_op jit(solution)/shard_map/ppermute | solution.py:70
  27.7 1.6 %collective-permute-start.13 = (bf16[192,768]{1,0:T(8,128)(2,1)S(1)}, bf16[192,768]{1,0:T(8,128)(2,1)S(1)}, u32[]{:S(2)}, u32[]{:S(2)}) collective-permute-start(bf16[192,768]{1,0:T(8,128)(2,1)S(1)} %collective-permute-done.9.refs_3_), channel_id=1, source_target_pairs={{0,2},{2,0},{4,6},{6,4},{8,10},{10,8},{12,14},{14,12},{16,18},{18,... | collective-permute-start | bytes 884744 | tf_op jit(solution)/shard_map/ppermute | solution.py:79
  27.8 7.6 %collective-permute-start.12 = (bf16[96,768]{1,0:T(8,128)(2,1)S(1)}, bf16[96,768]{1,0:T(8,128)(2,1)S(1)}, u32[]{:S(2)}, u32[]{:S(2)}) collective-permute-start(bf16[96,768]{1,0:T(8,128)(2,1)S(1)} %slice.6), channel_id=1, source_target_pairs={{0,8},{2,6},{8,16},{10,2},{16,24},{18,10},{24,28},{26,18},{28,20},... | collective-permute-start | bytes 442376 | tf_op jit(solution)/shard_map/ppermute | solution.py:70
  36.1 13.6 %collective-permute-start.14 = (bf16[576,512]{1,0:T(8,128)(2,1)}, bf16[576,512]{1,0:T(8,128)(2,1)S(1)}, u32[]{:S(2)}, u32[]{:S(2)}) collective-permute-start(bf16[576,512]{1,0:T(8,128)(2,1)} %collective-permute-done.8.refs_2_), channel_id=1, source_target_pairs={{0,8},{2,6},{8,16},{10,2},{16,24},{18,10},{24,28},{26,18},{28,20},... | collective-permute-start | bytes 1769480 | tf_op jit(solution)/shard_map/ppermute | solution.py:70
  37.7 10.0 %copy-start.15 = (f32[1536]{0:T(1024)S(1)}, f32[1536]{0:T(1024)}, u32[]{:S(2)}) copy-start(f32[1536]{0:T(1024)} %flat_gain.1) | copy-start | bytes 18436
  37.7 38.3 %all-to-all-start = ((bf16[16,144,128]{2,1,0:T(8,128)(2,1)}), bf16[16,144,128]{2,1,0:T(8,128)(2,1)S(1)}, u32[]{:S(2)}, u32[]{:S(2)}) async-start(bf16[16,144,128]{2,1,0:T(8,128)(2,1)} %bundle.1), calls=%async_computation | async-start | bytes 1179648 | tf_op jit(solution)/shard_map/all_to_all | solution.py:704
  42.5 1.6 %collective-permute-start.15 = (bf16[96,768]{1,0:T(8,128)(2,1)}, bf16[96,768]{1,0:T(8,128)(2,1)S(1)}, u32[]{:S(2)}, u32[]{:S(2)}) collective-permute-start(bf16[96,768]{1,0:T(8,128)(2,1)} %copy-done.7), channel_id=1, source_target_pairs={{0,2},{2,0},{4,6},{6,4},{8,10},{10,8},{12,14},{14,12},{16,18},{18,... | collective-permute-start | bytes 442376 | tf_op jit(solution)/shard_map/ppermute | solution.py:79
  47.1 3.9 %copy-start.6 = (bf16[576,512]{1,0:T(8,128)(2,1)S(1)}, bf16[576,512]{1,0:T(8,128)(2,1)}, u32[]{:S(2)}) copy-start(bf16[576,512]{1,0:T(8,128)(2,1)} %copy-done.5) | copy-start | bytes 1769476
  47.1 11.2 %collective-permute-start.17 = (bf16[128,1536]{1,0:T(8,128)(2,1)S(1)}, bf16[128,1536]{1,0:T(8,128)(2,1)S(1)}, u32[]{:S(2)}, u32[]{:S(2)}) collective-permute-start(bf16[128,1536]{1,0:T(8,128)(2,1)S(1)} %outward_send.1), channel_id=1, source_target_pairs={{0,1},{1,0},{2,3},{3,2},{4,5},{5,4},{6,7},{7,6},{8,9},{9,8},{10,11... | collective-permute-start | bytes 1179656 | tf_op jit(solution)/shard_map/ppermute | solution.py:711
  49.7 12.3 %collective-permute-start.16 = (bf16[288,512]{1,0:T(8,128)(2,1)S(1)}, bf16[288,512]{1,0:T(8,128)(2,1)S(1)}, u32[]{:S(2)}, u32[]{:S(2)}) collective-permute-start(bf16[288,512]{1,0:T(8,128)(2,1)S(1)} %slice.7), channel_id=1, source_target_pairs={{0,8},{2,6},{8,16},{10,2},{16,24},{18,10},{24,28},{26,18},{28,20},... | collective-permute-start | bytes 884744 | tf_op jit(solution)/shard_map/ppermute | solution.py:70
  51.0 16.7 %collective-permute-start.19 = (bf16[576,512]{1,0:T(8,128)(2,1)S(1)}, bf16[576,512]{1,0:T(8,128)(2,1)S(1)}, u32[]{:S(2)}, u32[]{:S(2)}) collective-permute-start(bf16[576,512]{1,0:T(8,128)(2,1)S(1)} %copy-done.6), channel_id=1, source_target_pairs={{0,2},{2,0},{4,6},{6,4},{8,10},{10,8},{12,14},{14,12},{16,18},{18,... | collective-permute-start | bytes 1769480 | tf_op jit(solution)/shard_map/ppermute | solution.py:79
  51.0 16.7 %collective-permute-start.20 = (bf16[576,512]{1,0:T(8,128)(2,1)}, bf16[576,512]{1,0:T(8,128)(2,1)S(1)}, u32[]{:S(2)}, u32[]{:S(2)}) collective-permute-start(bf16[576,512]{1,0:T(8,128)(2,1)} %collective-permute-done.8.refs_2_), channel_id=1, source_target_pairs={{0,2},{2,0},{4,6},{6,4},{8,10},{10,8},{12,14},{14,12},{16,18},{18,... | collective-permute-start | bytes 1769480 | tf_op jit(solution)/shard_map/ppermute | solution.py:79
  51.5 16.2 %collective-permute-start.21 = (bf16[576,512]{1,0:T(8,128)(2,1)S(1)}, bf16[576,512]{1,0:T(8,128)(2,1)S(1)}, u32[]{:S(2)}, u32[]{:S(2)}) collective-permute-start(bf16[576,512]{1,0:T(8,128)(2,1)S(1)} %collective-permute-done.14.refs_3_), channel_id=1, source_target_pairs={{0,2},{2,0},{4,6},{6,4},{8,10},{10,8},{12,14},{14,12},{16,18},{18,... | collective-permute-start | bytes 1769480 | tf_op jit(solution)/shard_map/ppermute | solution.py:79
  62.0 5.7 %collective-permute-start.22 = (bf16[288,512]{1,0:T(8,128)(2,1)S(1)}, bf16[288,512]{1,0:T(8,128)(2,1)S(1)}, u32[]{:S(2)}, u32[]{:S(2)}) collective-permute-start(bf16[288,512]{1,0:T(8,128)(2,1)S(1)} %collective-permute-done.16.refs_7_), channel_id=1, source_target_pairs={{0,2},{2,0},{4,6},{6,4},{8,10},{10,8},{12,14},{14,12},{16,18},{18,... | collective-permute-start | bytes 884744 | tf_op jit(solution)/shard_map/ppermute | solution.py:79
  62.0 5.7 %copy-start.4 = (bf16[576,512]{1,0:T(8,128)(2,1)S(1)}, bf16[576,512]{1,0:T(8,128)(2,1)}, u32[]{:S(2)}) copy-start(bf16[576,512]{1,0:T(8,128)(2,1)} %copy-done.3) | copy-start | bytes 1769476
  62.4 5.3 %collective-permute-start.18 = (bf16[32,1536]{1,0:T(8,128)(2,1)S(1)}, bf16[32,1536]{1,0:T(8,128)(2,1)S(1)}, u32[]{:S(2)}, u32[]{:S(2)}) collective-permute-start(bf16[32,1536]{1,0:T(8,128)(2,1)S(1)} %get-tuple-element.111), channel_id=1, source_target_pairs={{0,1},{1,0},{2,3},{3,2},{4,5},{5,4},{6,7},{7,6},{8,9},{9,8},{10,11... | collective-permute-start | bytes 294920 | tf_op jit(solution)/shard_map/ppermute | solution.py:723
  67.7 8.3 %copy-start.10 = (bf16[512,4,128]{2,1,0:T(4,128)(2,1)S(1)}, bf16[512,4,128]{2,1,0:T(4,128)(2,1)}, u32[]{:S(2)}) copy-start(bf16[512,4,128]{2,1,0:T(4,128)(2,1)} %param.25) | copy-start | bytes 1572868
  70.2 4.7 %collective-permute-start.23 = (bf16[32,1536]{1,0:T(8,128)(2,1)S(1)}, bf16[32,1536]{1,0:T(8,128)(2,1)S(1)}, u32[]{:S(2)}, u32[]{:S(2)}) collective-permute-start(bf16[32,1536]{1,0:T(8,128)(2,1)S(1)} %get-tuple-element.117), channel_id=1, source_target_pairs={{0,1},{1,0},{2,3},{3,2},{4,5},{5,4},{6,7},{7,6},{8,9},{9,8},{10,11... | collective-permute-start | bytes 294920 | tf_op jit(solution)/shard_map/ppermute | solution.py:729
  (10 other events, 13.6 us)

commit v10 on v9

--- a/solution.py
+++ b/solution.py
@@ -404,10 +404,13 @@
 
 
 def keep_kernel(groups, unit_rows, n_parts, early, late, tokens, flat_gain, *refs):
-    parts, (out, gain, w_out, rows) = refs[:n_parts], refs[n_parts:]
+    parts, (out, gain, w_out, rows, total, sem) = refs[:n_parts], refs[n_parts:]
     gain[...] = flat_gain[...].reshape(gain.shape)
     made = outward_rows(False, groups, unit_rows, early, late, parts, w_out, rows)
-    out[...] = tokens[...].astype(f32) + made
+    total[...] = tokens[...].astype(f32) + made
+    copy = pltpu.make_async_copy(total, out, sem)
+    copy.start()
+    copy.wait()
 
 
 def outward_send(groups, early, late, parts, unit_rows):
@@ -429,20 +432,27 @@
     return pl.pallas_call(
         functools.partial(keep_kernel, groups, unit_rows, len(parts)),
         out_shape=(
-            jax.ShapeDtypeStruct(tokens.shape, f32),
+            pltpu.HBM(tokens.shape, f32),
             jax.ShapeDtypeStruct((1, width), f32),
         ),
         in_specs=[VMEM] * (4 + len(parts)),
-        out_specs=(VMEM, VMEM),
-        scratch_shapes=[pltpu.VMEM((width, depth), bf16), pltpu.VMEM(early.shape, bf16)],
+        out_specs=(HBM, VMEM),
+        scratch_shapes=[
+            pltpu.VMEM((width, depth), bf16),
+            pltpu.VMEM(early.shape, bf16),
+            pltpu.VMEM(tokens.shape, f32),
+            pltpu.SemaphoreType.DMA,
+        ],
         compiler_params=PARAMS,
         cost_estimate=reads(2 * width * depth),
         name="outward_keep",
     )(early, late, tokens, gain, *parts)
 
 
-def route_kernel(mine, arrived, gain, place, residual, moe_in, sent):
-    added = (mine[...] + arrived[...].astype(f32)).astype(bf16)
+def route_kernel(mine, arrived, gain, place, residual, moe_in, sent, kept, got, sems):
+    for copy in fetch([(mine, kept), (arrived, got)], sems):
+        copy.wait()
+    added = (kept[...] + got[...].astype(f32)).astype(bf16)
     residual[...] = added
     moe_in[...] = normalized(added.astype(f32), gain[...])
     cap = sent.shape[0]
@@ -459,12 +469,17 @@
             jax.ShapeDtypeStruct(mine.shape, bf16),
             jax.ShapeDtypeStruct((cap, mine.shape[1]), bf16),
         ),
-        in_specs=[VMEM] * 4,
+        in_specs=[HBM, ANY, VMEM, VMEM],
         out_specs=(VMEM,) * 3,
+        scratch_shapes=[
+            pltpu.VMEM(mine.shape, f32),
+            pltpu.VMEM(mine.shape, bf16),
+            pltpu.SemaphoreType.DMA((2,)),
+        ],
         compiler_params=PARAMS,
         cost_estimate=takes(2),
         name="route",
-    )(mine, arrived, gain, place)
+    )(pltpu.with_memory_space_constraint(mine, pltpu.HBM), arrived, gain, place)
 
 
 def gate_kernel(moe_in, router, ids, place, gates, own, spread):
@@ -535,7 +550,7 @@
             pltpu.VMEM((groups * down_rows, model), bf16),
         ],
         compiler_params=PARAMS,
-        cost_estimate=reads(2 * groups * 2 * (up_rows * 2 * width + down_rows * model)),
+        cost_estimate=takes(1.2),
         name="expert",
     )(own, other, *parts)
 
@@ -699,10 +714,7 @@
     early = out_ring.pin(early)
     out_ring.step()
     out_ring.share(3)
-    early, kv, out_ring.near = together((early, kv, out_ring.near))
-    outgoing = bundle(groups, send, kv, tags)
-    arrived_cache = lax.all_to_all(outgoing, "grp", split_axis=0, concat_axis=0, tiled=True)
-    early, outgoing = together((early, outgoing))
+    early, out_ring.near = together((early, out_ring.near))
     early = out_ring.pin(early)
     early = expert_ring.pin(early)
     expert_ring.step()
@@ -713,10 +725,12 @@
     mine, late_gain = outward_keep(
         groups, early, late, tokens, moe_gain, out_ring.parts(), out_ring.unit_rows
     )
-    mine = expert_ring.pin(mine)
+    kv, late_gain = expert_ring.pin(kv, late_gain)
     expert_ring.share()
     expert_ring.step()
-    arrived, mine = expert_ring.pin(arrived, mine)
+    outgoing = bundle(groups, send, kv, tags)
+    arrived_cache = lax.all_to_all(outgoing, "grp", split_axis=0, concat_axis=0, tiled=True)
+    arrived, late_gain, outgoing = expert_ring.pin(arrived, late_gain, outgoing)
     expert_ring.share()
 
     residual, moe_in, sent_rows = route(mine, arrived, late_gain, place)

time: 78 us -> 87 us (1.12)
  the two profiles are of different devices: /device:TPU:18 before, /device:TPU:14 now
where the time goes in v10:
time: 87 us; the launch traced here: 86.7 us
  waiting for transfers between devices  48.8 us (56%)
  Pallas kernels  18.2 us (21%)
  starting transfers between devices  16.9 us (19%)
  local copies, waits for them, and re-layouts  1.89 us (2%)
    ppermute x8, waiting for transfers between devices, step(): self.mine.append(self.across(held))  23.5 us
    ppermute x1, waiting for transfers between devices, two_lane_shards(): arrived = swap(sent)  8.99 us
    all_to_all x1, starting transfers between devices, two_lane_shards(): lax.all_to_all(outgoing, 'grp', split_axis=0, concat_axis=0, tiled=True)  6.16 us
    ppermute x1, waiting for transfers between devices, two_lane_shards(): other_tokens = swap(tokens)  4.57 us
    ppermute x1, waiting for transfers between devices, two_lane_shards(): landed = swap(sent_rows)  4.25 us
    ppermute x1, waiting for transfers between devices, two_lane_shards(): returned = swap(back)  4.08 us
    ppermute x8, starting transfers between devices, step(): self.mine.append(self.across(held))  3.92 us
    pallas_call x1, Pallas kernels, project(): pl.pallas_call(project_kernel, out_shape=(jax.ShapeDtypeStruct((2 * count...  2.2 us
  transfers between devices with their start and end apart: 25, of which 13 were waited for; matrix products, arithmetic and copies ran while one was open for 2% of the time, Pallas kernels for 18%

profile of v10, /device:TPU:14, one launch (start us, length us, event | category | flops | bytes accessed | tf_op | source)
XLA Modules:
  0.0 86.7 jit_solution(17384052143368970726)
XLA Ops:
  1.3 0.5 collective-permute-start.5
  1.8 1.1 %collective-permute-done.1.refs_4_ = bf16[32,1536]{1,0:T(8,128)(2,1)S(1)} collective-permute-done((bf16[32,1536]{1,0:T(8,128)(2,1)}, bf16[32,1536]{1,0:T(8,128)(2,1)S(1)}, u32[]{:S(2)}, u32[]{:S(2)}) %collective-permute-start.1) | collective-permute-done | bytes 98336 | tf_op jit(solution)/shard_map/ppermute | solution.py:689
  2.9 1.1 %pack.1 = (bf16[576,512]{1,0:T(8,128)(2,1)S(1)}, bf16[192,768]{1,0:T(8,128)(2,1)S(1)}) custom-call(bf16[96,1024]{1,0:T(8,128)(2,1)} %bitcast.23, bf16[32,1536]{1,0:T(8,128)(2,1)} %bitcast.25, bf16[96,1536]{1,0:T(8,128)(2,1)} %bitcast.21, bf16[96,1024]{1,0:T(8,128)(2,1)S(1)} %collective-permute-done.refs_3_, ...), custom_call_target="tpu_custom_call" | custom-call | flops 1 | bytes 1 | tf_op jit(solution)/shard_map/pack/pallas_call | solution.py:159
  5.1 1.5 %prepare.1 = (f32[256,128]{1,0:T(8,128)S(1)}, f32[256,128]{1,0:T(8,128)S(1)}, f32[256,128]{1,0:T(8,128)S(1)}, bf16[64,128]{1,0:T(8,128)(2,1)S(1)}, bf16[512,256]...) custom-call(s32[1,256]{1,0:T(1,128)} %bitcast.26, s32[1,256]{1,0:T(1,128)} %bitcast.27, ...), custom_call_target="tpu_custom_call" | custom-call | flops 1 | bytes 1 | tf_op jit(solution)/shard_map/prepare/pallas_call | solution.py:255
  6.6 1.8 %copy.17 = bf16[192,8,4,128]{3,1,2,0:T(8,128)(2,1)S(1)} copy(bf16[192,8,4,128]{3,2,1,0:T(4,128)(2,1)} %bitcast.18) | data formatting | bytes 3145728
  8.4 4.6 %collective-permute-done.5.other = bf16[128,1536]{1,0:T(8,128)(2,1)S(1)} collective-permute-done((bf16[128,1536]{1,0:T(8,128)(2,1)}, bf16[128,1536]{1,0:T(8,128)(2,1)S(1)}, u32[]{:S(2)}, u32[]{:S(2)}) %collective-permute-start.5) | collective-permute-done | bytes 393248 | tf_op jit(solution)/shard_map/ppermute | solution.py:686
  13.9 2.2 %project.1 = (bf16[256,768]{1,0:T(8,128)(2,1)S(1)}, bf16[256,512]{1,0:T(8,128)(2,1)S(1)}, bf16[128,512]{1,0:T(8,128)(2,1)S(1)}) custom-call(bf16[128,1536]{1,0:T(8,128)(2,1)S(1)} %copy-done.1, bf16[128,1536]{1,0:T(8,128)(2,1)S(1)} %collective-permute-done.5.other, f32[1,1536]{1,0:T(1,128)S(1)} %get-tuple-element.66.gain, ...), custom_call_target="tpu_custom_call" | custom-call | flops 9200000000 | bytes 64000000 | tf_op jit(solution)/shard_map/project/pallas_call | solution.py:305
  16.1 1.9 %collective-permute-start.6 = (bf16[128,512]{1,0:T(8,128)(2,1)S(1)}, bf16[128,512]{1,0:T(8,128)(2,1)S(1)}, u32[]{:S(2)}, u32[]{:S(2)}) collective-permute-start(bf16[128,512]{1,0:T(8,128)(2,1)S(1)} %get-tuple-element.70), channel_id=1, source_target_pairs={{0,2},{2,4},{4,6},{6,8},{8,10},{10,12},{12,14},{14,16},{16,18},{18... | collective-permute-start | bytes 393224 | tf_op jit(solution)/shard_map/ppermute | solution.py:704
  18.1 2.2 %collective-permute-done.7.refs_2_ = bf16[192,768]{1,0:T(8,128)(2,1)S(1)} collective-permute-done((bf16[192,768]{1,0:T(8,128)(2,1)S(1)}, bf16[192,768]{1,0:T(8,128)(2,1)S(1)}, u32[]{:S(2)}, u32[]{:S(2)}) %collective-permute-start.7) | collective-permute-done | bytes 294944 | tf_op jit(solution)/shard_map/ppermute | solution.py:70
  20.9 1.3 %attend_late.1.late = bf16[128,768]{1,0:T(8,128)(2,1)S(1)} custom-call(bf16[256,768]{1,0:T(8,128)(2,1)S(1)} %get-tuple-element.73.q, bf16[256,512]{1,0:T(8,128)(2,1)S(1)} %get-tuple-element.100.kv, f32[256,128]{1,0:T(8,128)S(1)} %get-tuple-element.75.past), custom_call_target="tpu_custom_call" | custom-call | flops 2300000000 | bytes 16000000 | tf_op jit(solution)/shard_map/attend_late/pallas_call | solution.py:361
  22.9 1.5 %attend_early.1.early = bf16[128,768]{1,0:T(8,128)(2,1)S(1)} custom-call(bf16[256,768]{1,0:T(8,128)(2,1)S(1)} %get-tuple-element.73.q, bf16[256,512]{1,0:T(8,128)(2,1)S(1)} %get-tuple-element.100.kv, bf16[128,512]{1,0:T(8,128)(2,1)S(1)} %collective-permute-done.6.seam, f32[256,128]{1,0:T(8,128)S(1)} %get-tuple-element.75.past), custom_call_target="tpu_custom_call" | custom-call | flops 2300000000 | bytes 16000000 | tf_op jit(solution)/shard_map/attend_early/pallas_call | solution.py:373
  24.4 2.8 %collective-permute-done.9.refs_3_ = bf16[192,768]{1,0:T(8,128)(2,1)S(1)} collective-permute-done((bf16[192,768]{1,0:T(8,128)(2,1)S(1)}, bf16[192,768]{1,0:T(8,128)(2,1)S(1)}, u32[]{:S(2)}, u32[]{:S(2)}) %collective-permute-start.9) | collective-permute-done | bytes 294944 | tf_op jit(solution)/shard_map/ppermute | solution.py:70
  27.7 1.1 %collective-permute-done.13.refs_6_ = bf16[192,768]{1,0:T(8,128)(2,1)S(1)} collective-permute-done((bf16[192,768]{1,0:T(8,128)(2,1)S(1)}, bf16[192,768]{1,0:T(8,128)(2,1)S(1)}, u32[]{:S(2)}, u32[]{:S(2)}) %collective-permute-start.13) | collective-permute-done | bytes 294944 | tf_op jit(solution)/shard_map/ppermute | solution.py:79
  28.7 6.3 %collective-permute-done.12.refs_7_ = bf16[96,768]{1,0:T(8,128)(2,1)S(1)} collective-permute-done((bf16[96,768]{1,0:T(8,128)(2,1)S(1)}, bf16[96,768]{1,0:T(8,128)(2,1)S(1)}, u32[]{:S(2)}, u32[]{:S(2)}) %collective-permute-start.12) | collective-permute-done | bytes 147488 | tf_op jit(solution)/shard_map/ppermute | solution.py:70
  35.9 1.0 %collective-permute-done.14.refs_8_ = bf16[96,768]{1,0:T(8,128)(2,1)S(1)} collective-permute-done((bf16[96,768]{1,0:T(8,128)(2,1)S(1)}, bf16[96,768]{1,0:T(8,128)(2,1)S(1)}, u32[]{:S(2)}, u32[]{:S(2)}) %collective-permute-start.14) | collective-permute-done | bytes 147488 | tf_op jit(solution)/shard_map/ppermute | solution.py:79
  36.9 1.2 %outward_send.1 = bf16[128,1536]{1,0:T(8,128)(2,1)S(1)} custom-call(bf16[128,768]{1,0:T(8,128)(2,1)S(1)} %attend_early.1.early, bf16[128,768]{1,0:T(8,128)(2,1)S(1)} %attend_late.1.late, bf16[192,768]{1,0:T(8,128)(2,1)S(1)} %get-tuple-element.61.refs_0_, bf16[192,768]{1,0:T(8,128)(2,1)S(1)} %collective-permute-done.4.refs_1_, ...), custom_call_target="tpu_custom_call" | custom-call | flops 1 | bytes 2359296 | tf_op jit(solution)/shard_map/outward_send/pallas_call | solution.py:418
  38.1 2.1 %outward_keep.1 = (f32[128,1536]{1,0:T(8,128)}, f32[1,1536]{1,0:T(1,128)S(1)}) custom-call(bf16[128,768]{1,0:T(8,128)(2,1)S(1)} %attend_early.1.early, bf16[128,768]{1,0:T(8,128)(2,1)S(1)} %attend_late.1.late, bf16[128,1536]{1,0:T(8,128)(2,1)S(1)} %copy-done.1, f32[1536]{0:T(1024)S(1)} %copy-done.4, bf16[192,768]{1,0:T(8,128)(2,1)S(1)} %get-tuple-element.61.refs_0_, ...), custom_call_target="tpu_custom_call" | custom-call | flops 1 | bytes 2359296 | tf_op jit(solution)/shard_map/outward_keep/pallas_call | solution.py:432
  40.1 4.8 %collective-permute-done.15.refs_3_ = bf16[576,512]{1,0:T(8,128)(2,1)S(1)} collective-permute-done((bf16[576,512]{1,0:T(8,128)(2,1)S(1)}, bf16[576,512]{1,0:T(8,128)(2,1)S(1)}, u32[]{:S(2)}, u32[]{:S(2)}) %collective-permute-start.15) | collective-permute-done | bytes 589856 | tf_op jit(solution)/shard_map/ppermute | solution.py:70
  44.9 1.4 %bundle.1 = bf16[16,144,128]{2,1,0:T(8,128)(2,1)} custom-call(bf16[512,256]{1,0:T(8,128)(2,1)S(1)} %get-tuple-element.99.send, bf16[256,512]{1,0:T(8,128)(2,1)S(1)} %get-tuple-element.100.kv, bf16[256,128]{1,0:T(8,128)(2,1)S(1)} %get-tuple-element.101.tags), custom_call_target="tpu_custom_call" | custom-call | flops 1 | bytes 1 | tf_op jit(solution)/shard_map/bundle/pallas_call | solution.py:604
  46.3 6.2 %all-to-all-start = ((bf16[16,144,128]{2,1,0:T(8,128)(2,1)}), bf16[16,144,128]{2,1,0:T(8,128)(2,1)S(1)}, u32[]{:S(2)}, u32[]{:S(2)}) async-start(bf16[16,144,128]{2,1,0:T(8,128)(2,1)} %bundle.1), calls=%async_computation | async-start | bytes 1179648 | tf_op jit(solution)/shard_map/all_to_all | solution.py:732
  52.5 0.5 collective-permute-start.17
  53.0 0.6 collective-permute-start.16
  54.6 9.0 %collective-permute-done.17.arrived = bf16[128,1536]{1,0:T(8,128)(2,1)S(1)} collective-permute-done((bf16[128,1536]{1,0:T(8,128)(2,1)S(1)}, bf16[128,1536]{1,0:T(8,128)(2,1)S(1)}, u32[]{:S(2)}, u32[]{:S(2)}) %collective-permute-start.17) | collective-permute-done | bytes 393248 | tf_op jit(solution)/shard_map/ppermute | solution.py:723
  63.6 7.4 %collective-permute-done.16.refs_7_ = bf16[288,512]{1,0:T(8,128)(2,1)S(1)} collective-permute-done((bf16[288,512]{1,0:T(8,128)(2,1)S(1)}, bf16[288,512]{1,0:T(8,128)(2,1)S(1)}, u32[]{:S(2)}, u32[]{:S(2)}) %collective-permute-start.16) | collective-permute-done | bytes 294944 | tf_op jit(solution)/shard_map/ppermute | solution.py:70
  71.0 1.6 %route.1 = (bf16[128,1536]{1,0:T(8,128)(2,1)S(1)}, bf16[128,1536]{1,0:T(8,128)(2,1)S(1)}, bf16[32,1536]{1,0:T(8,128)(2,1)S(1)}) custom-call(f32[128,1536]{1,0:T(8,128)} %get-tuple-element.94.mine, bf16[128,1536]{1,0:T(8,128)(2,1)S(1)} %collective-permute-done.17.arrived, f32[1,1536]{1,0:T(1,128)S(1)} %get-tuple-element.103.gain, ...), custom_call_target="tpu_custom_call" | custom-call | flops 2300000000 | bytes 16000000 | tf_op jit(solution)/shard_map/route/pallas_call | solution.py:465
  72.6 0.6 collective-permute-start.18
  73.7 4.3 %collective-permute-done.18.other = bf16[32,1536]{1,0:T(8,128)(2,1)S(1)} collective-permute-done((bf16[32,1536]{1,0:T(8,128)(2,1)S(1)}, bf16[32,1536]{1,0:T(8,128)(2,1)S(1)}, u32[]{:S(2)}, u32[]{:S(2)}) %collective-permute-start.18) | collective-permute-done | bytes 98336 | tf_op jit(solution)/shard_map/ppermute | solution.py:737
  77.9 1.3 %expert.1 = (bf16[32,1536]{1,0:T(8,128)(2,1)S(1)}, bf16[32,1536]{1,0:T(8,128)(2,1)S(1)}) custom-call(bf16[32,1536]{1,0:T(8,128)(2,1)S(1)} %get-tuple-element.111.own, bf16[32,1536]{1,0:T(8,128)(2,1)S(1)} %collective-permute-done.18.other, bf16[576,512]{1,0:T(8,128)(2,1)S(1)} %get-tuple-element.60.refs_0_, ...), custom_call_target="tpu_custom_call" | custom-call | flops 1380000000 | bytes 9600000 | tf_op jit(solution)/shard_map/expert/pallas_call | solution.py:542
  79.3 0.6 collective-permute-start.23
  79.9 4.1 %collective-permute-done.23.returned = bf16[32,1536]{1,0:T(8,128)(2,1)S(1)} collective-permute-done((bf16[32,1536]{1,0:T(8,128)(2,1)S(1)}, bf16[32,1536]{1,0:T(8,128)(2,1)S(1)}, u32[]{:S(2)}, u32[]{:S(2)}) %collective-permute-start.23) | collective-permute-done | bytes 98336 | tf_op jit(solution)/shard_map/ppermute | solution.py:743
  84.0 1.1 %combine.1 = bf16[128,1536]{1,0:T(8,128)(2,1)} custom-call(bf16[128,1536]{1,0:T(8,128)(2,1)S(1)} %get-tuple-element.105.residual, f32[128,40]{1,0:T(8,128)S(1)} %get-tuple-element.107.gates, bf16[128,64]{1,0:T(8,128)(2,1)S(1)} %get-tuple-element.108.spread, bf16[32,1536]{1,0:T(8,128)(2,1)S(1)} %get-tuple-element.114.own, ...), custom_call_target="tpu_custom_call" | custom-call | flops 1 | bytes 1179648 | tf_op jit(solution)/shard_map/combine/pallas_call | solution.py:574
  85.1 1.5 %write.1 = bf16[2048,128]{1,0:T(8,128)(2,1)} custom-call(bf16[16,144,128]{2,1,0:T(8,128)(2,1)S(1)} %all-to-all-done.arrived, bf16[2048,128]{1,0:T(8,128)(2,1)S(1)} %bitcast.14), custom_call_target="tpu_custom_call" | custom-call | flops 1 | bytes 2097152 | tf_op jit(solution)/shard_map/write/pallas_call | solution.py:644
  (46 shorter events, 6.7 us)
Async XLA Ops:
  0.6 2.3 %collective-permute-start.2 = (bf16[96,1536]{1,0:T(8,128)(2,1)}, bf16[96,1536]{1,0:T(8,128)(2,1)S(1)}, u32[]{:S(2)}, u32[]{:S(2)}) collective-permute-start(bf16[96,1536]{1,0:T(8,128)(2,1)} %bitcast.20), channel_id=1, source_target_pairs={{0,2},{2,0},{4,6},{6,4},{8,10},{10,8},{12,14},{14,12},{16,18},{18,... | collective-permute-start | bytes 884744 | tf_op jit(solution)/shard_map/ppermute | solution.py:689
  0.7 2.2 %collective-permute-start = (bf16[96,1024]{1,0:T(8,128)(2,1)}, bf16[96,1024]{1,0:T(8,128)(2,1)S(1)}, u32[]{:S(2)}, u32[]{:S(2)}) collective-permute-start(bf16[96,1024]{1,0:T(8,128)(2,1)} %bitcast.22), channel_id=1, source_target_pairs={{0,2},{2,0},{4,6},{6,4},{8,10},{10,8},{12,14},{14,12},{16,18},{18,... | collective-permute-start | bytes 589832 | tf_op jit(solution)/shard_map/ppermute | solution.py:689
  1.2 1.7 %collective-permute-start.1 = (bf16[32,1536]{1,0:T(8,128)(2,1)}, bf16[32,1536]{1,0:T(8,128)(2,1)S(1)}, u32[]{:S(2)}, u32[]{:S(2)}) collective-permute-start(bf16[32,1536]{1,0:T(8,128)(2,1)} %bitcast.24), channel_id=1, source_target_pairs={{0,2},{2,0},{4,6},{6,4},{8,10},{10,8},{12,14},{14,12},{16,18},{18,... | collective-permute-start | bytes 294920 | tf_op jit(solution)/shard_map/ppermute | solution.py:689
  1.3 11.7 %collective-permute-start.5 = (bf16[128,1536]{1,0:T(8,128)(2,1)}, bf16[128,1536]{1,0:T(8,128)(2,1)S(1)}, u32[]{:S(2)}, u32[]{:S(2)}) collective-permute-start(bf16[128,1536]{1,0:T(8,128)(2,1)} %tokens.1), channel_id=1, source_target_pairs={{0,1},{1,0},{2,3},{3,2},{4,5},{5,4},{6,7},{7,6},{8,9},{9,8},{10,11... | collective-permute-start | bytes 1179656 | tf_op jit(solution)/shard_map/ppermute | solution.py:686
  4.1 8.9 %collective-permute-start.4 = (bf16[192,768]{1,0:T(8,128)(2,1)S(1)}, bf16[192,768]{1,0:T(8,128)(2,1)S(1)}, u32[]{:S(2)}, u32[]{:S(2)}) collective-permute-start(bf16[192,768]{1,0:T(8,128)(2,1)S(1)} %get-tuple-element.61.refs_0_), channel_id=1, source_target_pairs={{0,8},{2,6},{8,16},{10,2},{16,24},{18,10},{24,28},{26,18},{28,20},... | collective-permute-start | bytes 884744 | tf_op jit(solution)/shard_map/ppermute | solution.py:70
  4.6 17.9 %collective-permute-start.3 = (bf16[576,512]{1,0:T(8,128)(2,1)S(1)}, bf16[576,512]{1,0:T(8,128)(2,1)S(1)}, u32[]{:S(2)}, u32[]{:S(2)}) collective-permute-start(bf16[576,512]{1,0:T(8,128)(2,1)S(1)} %get-tuple-element.60.refs_0_), channel_id=1, source_target_pairs={{0,8},{2,6},{8,16},{10,2},{16,24},{18,10},{24,28},{26,18},{28,20},... | collective-permute-start | bytes 1769480 | tf_op jit(solution)/shard_map/ppermute | solution.py:70
  6.5 7.4 %copy-start.1 = (bf16[128,1536]{1,0:T(8,128)(2,1)S(1)}, bf16[128,1536]{1,0:T(8,128)(2,1)}, u32[]{:S(2)}) copy-start(bf16[128,1536]{1,0:T(8,128)(2,1)} %tokens.1) | copy-start | bytes 1179652
  6.5 7.4 %copy-start.5 = (bf16[1536,768]{1,0:T(8,128)(2,1)S(1)}, bf16[1536,768]{1,0:T(8,128)(2,1)}, u32[]{:S(2)}) copy-start(bf16[1536,768]{1,0:T(8,128)(2,1)} %w_query.1) | copy-start | bytes 7077892
  13.0 7.3 %collective-permute-start.7 = (bf16[192,768]{1,0:T(8,128)(2,1)S(1)}, bf16[192,768]{1,0:T(8,128)(2,1)S(1)}, u32[]{:S(2)}, u32[]{:S(2)}) collective-permute-start(bf16[192,768]{1,0:T(8,128)(2,1)S(1)} %collective-permute-done.4.refs_1_), channel_id=1, source_target_pairs={{0,8},{2,6},{8,16},{10,2},{16,24},{18,10},{24,28},{26,18},{28,20},... | collective-permute-start | bytes 884744 | tf_op jit(solution)/shard_map/ppermute | solution.py:70
  13.4 10.9 %collective-permute-start.10 = (bf16[192,768]{1,0:T(8,128)(2,1)S(1)}, bf16[192,768]{1,0:T(8,128)(2,1)S(1)}, u32[]{:S(2)}, u32[]{:S(2)}) collective-permute-start(bf16[192,768]{1,0:T(8,128)(2,1)S(1)} %collective-permute-done.4.refs_1_), channel_id=1, source_target_pairs={{0,2},{2,0},{4,6},{6,4},{8,10},{10,8},{12,14},{14,12},{16,18},{18,... | collective-permute-start | bytes 884744 | tf_op jit(solution)/shard_map/ppermute | solution.py:79
  16.1 6.3 %collective-permute-start.6 = (bf16[128,512]{1,0:T(8,128)(2,1)S(1)}, bf16[128,512]{1,0:T(8,128)(2,1)S(1)}, u32[]{:S(2)}, u32[]{:S(2)}) collective-permute-start(bf16[128,512]{1,0:T(8,128)(2,1)S(1)} %get-tuple-element.70), channel_id=1, source_target_pairs={{0,2},{2,4},{4,6},{6,8},{8,10},{10,12},{12,14},{14,16},{16,18},{18... | collective-permute-start | bytes 393224 | tf_op jit(solution)/shard_map/ppermute | solution.py:704
  20.3 4.0 %collective-permute-start.11 = (bf16[192,768]{1,0:T(8,128)(2,1)S(1)}, bf16[192,768]{1,0:T(8,128)(2,1)S(1)}, u32[]{:S(2)}, u32[]{:S(2)}) collective-permute-start(bf16[192,768]{1,0:T(8,128)(2,1)S(1)} %collective-permute-done.7.refs_2_), channel_id=1, source_target_pairs={{0,2},{2,0},{4,6},{6,4},{8,10},{10,8},{12,14},{14,12},{16,18},{18,... | collective-permute-start | bytes 884744 | tf_op jit(solution)/shard_map/ppermute | solution.py:79
  20.4 6.7 %collective-permute-start.9 = (bf16[192,768]{1,0:T(8,128)(2,1)S(1)}, bf16[192,768]{1,0:T(8,128)(2,1)S(1)}, u32[]{:S(2)}, u32[]{:S(2)}) collective-permute-start(bf16[192,768]{1,0:T(8,128)(2,1)S(1)} %collective-permute-done.7.refs_2_), channel_id=1, source_target_pairs={{0,8},{2,6},{8,16},{10,2},{16,24},{18,10},{24,28},{26,18},{28,20},... | collective-permute-start | bytes 884744 | tf_op jit(solution)/shard_map/ppermute | solution.py:70
  22.4 12.6 %collective-permute-start.8 = (bf16[576,512]{1,0:T(8,128)(2,1)S(1)}, bf16[576,512]{1,0:T(8,128)(2,1)S(1)}, u32[]{:S(2)}, u32[]{:S(2)}) collective-permute-start(bf16[576,512]{1,0:T(8,128)(2,1)S(1)} %collective-permute-done.3.refs_1_), channel_id=1, source_target_pairs={{0,8},{2,6},{8,16},{10,2},{16,24},{18,10},{24,28},{26,18},{28,20},... | collective-permute-start | bytes 1769480 | tf_op jit(solution)/shard_map/ppermute | solution.py:70
  27.1 1.6 %collective-permute-start.13 = (bf16[192,768]{1,0:T(8,128)(2,1)S(1)}, bf16[192,768]{1,0:T(8,128)(2,1)S(1)}, u32[]{:S(2)}, u32[]{:S(2)}) collective-permute-start(bf16[192,768]{1,0:T(8,128)(2,1)S(1)} %collective-permute-done.9.refs_3_), channel_id=1, source_target_pairs={{0,2},{2,0},{4,6},{6,4},{8,10},{10,8},{12,14},{14,12},{16,18},{18,... | collective-permute-start | bytes 884744 | tf_op jit(solution)/shard_map/ppermute | solution.py:79
  27.1 10.9 %copy-start.4 = (f32[1536]{0:T(1024)S(1)}, f32[1536]{0:T(1024)}, u32[]{:S(2)}) copy-start(f32[1536]{0:T(1024)} %flat_gain.1) | copy-start | bytes 18436
  27.2 7.9 %collective-permute-start.12 = (bf16[96,768]{1,0:T(8,128)(2,1)S(1)}, bf16[96,768]{1,0:T(8,128)(2,1)S(1)}, u32[]{:S(2)}, u32[]{:S(2)}) collective-permute-start(bf16[96,768]{1,0:T(8,128)(2,1)S(1)} %slice.6), channel_id=1, source_target_pairs={{0,8},{2,6},{8,16},{10,2},{16,24},{18,10},{24,28},{26,18},{28,20},... | collective-permute-start | bytes 442376 | tf_op jit(solution)/shard_map/ppermute | solution.py:70
  35.0 9.9 %collective-permute-start.15 = (bf16[576,512]{1,0:T(8,128)(2,1)S(1)}, bf16[576,512]{1,0:T(8,128)(2,1)S(1)}, u32[]{:S(2)}, u32[]{:S(2)}) collective-permute-start(bf16[576,512]{1,0:T(8,128)(2,1)S(1)} %collective-permute-done.8.refs_2_), channel_id=1, source_target_pairs={{0,8},{2,6},{8,16},{10,2},{16,24},{18,10},{24,28},{26,18},{28,20},... | collective-permute-start | bytes 1769480 | tf_op jit(solution)/shard_map/ppermute | solution.py:70
  35.5 1.4 %collective-permute-start.14 = (bf16[96,768]{1,0:T(8,128)(2,1)S(1)}, bf16[96,768]{1,0:T(8,128)(2,1)S(1)}, u32[]{:S(2)}, u32[]{:S(2)}) collective-permute-start(bf16[96,768]{1,0:T(8,128)(2,1)S(1)} %collective-permute-done.12.refs_7_), channel_id=1, source_target_pairs={{0,2},{2,0},{4,6},{6,4},{8,10},{10,8},{12,14},{14,12},{16,18},{18,... | collective-permute-start | bytes 442376 | tf_op jit(solution)/shard_map/ppermute | solution.py:79
  46.3 38.8 %all-to-all-start = ((bf16[16,144,128]{2,1,0:T(8,128)(2,1)}), bf16[16,144,128]{2,1,0:T(8,128)(2,1)S(1)}, u32[]{:S(2)}, u32[]{:S(2)}) async-start(bf16[16,144,128]{2,1,0:T(8,128)(2,1)} %bundle.1), calls=%async_computation | async-start | bytes 1179648 | tf_op jit(solution)/shard_map/all_to_all | solution.py:732
  52.5 11.2 %collective-permute-start.17 = (bf16[128,1536]{1,0:T(8,128)(2,1)S(1)}, bf16[128,1536]{1,0:T(8,128)(2,1)S(1)}, u32[]{:S(2)}, u32[]{:S(2)}) collective-permute-start(bf16[128,1536]{1,0:T(8,128)(2,1)S(1)} %outward_send.1), channel_id=1, source_target_pairs={{0,1},{1,0},{2,3},{3,2},{4,5},{5,4},{6,7},{7,6},{8,9},{9,8},{10,11... | collective-permute-start | bytes 1179656 | tf_op jit(solution)/shard_map/ppermute | solution.py:723
  53.0 18.0 %collective-permute-start.16 = (bf16[288,512]{1,0:T(8,128)(2,1)S(1)}, bf16[288,512]{1,0:T(8,128)(2,1)S(1)}, u32[]{:S(2)}, u32[]{:S(2)}) collective-permute-start(bf16[288,512]{1,0:T(8,128)(2,1)S(1)} %slice.7), channel_id=1, source_target_pairs={{0,8},{2,6},{8,16},{10,2},{16,24},{18,10},{24,28},{26,18},{28,20},... | collective-permute-start | bytes 884744 | tf_op jit(solution)/shard_map/ppermute | solution.py:70
  53.6 24.3 %collective-permute-start.19 = (bf16[576,512]{1,0:T(8,128)(2,1)S(1)}, bf16[576,512]{1,0:T(8,128)(2,1)S(1)}, u32[]{:S(2)}, u32[]{:S(2)}) collective-permute-start(bf16[576,512]{1,0:T(8,128)(2,1)S(1)} %collective-permute-done.3.refs_1_), channel_id=1, source_target_pairs={{0,2},{2,0},{4,6},{6,4},{8,10},{10,8},{12,14},{14,12},{16,18},{18,... | collective-permute-start | bytes 1769480 | tf_op jit(solution)/shard_map/ppermute | solution.py:79
  54.1 23.8 %collective-permute-start.20 = (bf16[576,512]{1,0:T(8,128)(2,1)S(1)}, bf16[576,512]{1,0:T(8,128)(2,1)S(1)}, u32[]{:S(2)}, u32[]{:S(2)}) collective-permute-start(bf16[576,512]{1,0:T(8,128)(2,1)S(1)} %collective-permute-done.8.refs_2_), channel_id=1, source_target_pairs={{0,2},{2,0},{4,6},{6,4},{8,10},{10,8},{12,14},{14,12},{16,18},{18,... | collective-permute-start | bytes 1769480 | tf_op jit(solution)/shard_map/ppermute | solution.py:79
  54.1 23.8 %collective-permute-start.21 = (bf16[576,512]{1,0:T(8,128)(2,1)S(1)}, bf16[576,512]{1,0:T(8,128)(2,1)S(1)}, u32[]{:S(2)}, u32[]{:S(2)}) collective-permute-start(bf16[576,512]{1,0:T(8,128)(2,1)S(1)} %collective-permute-done.15.refs_3_), channel_id=1, source_target_pairs={{0,2},{2,0},{4,6},{6,4},{8,10},{10,8},{12,14},{14,12},{16,18},{18,... | collective-permute-start | bytes 1769480 | tf_op jit(solution)/shard_map/ppermute | solution.py:79
  71.0 6.9 %collective-permute-start.22 = (bf16[288,512]{1,0:T(8,128)(2,1)S(1)}, bf16[288,512]{1,0:T(8,128)(2,1)S(1)}, u32[]{:S(2)}, u32[]{:S(2)}) collective-permute-start(bf16[288,512]{1,0:T(8,128)(2,1)S(1)} %collective-permute-done.16.refs_7_), channel_id=1, source_target_pairs={{0,2},{2,0},{4,6},{6,4},{8,10},{10,8},{12,14},{14,12},{16,18},{18,... | collective-permute-start | bytes 884744 | tf_op jit(solution)/shard_map/ppermute | solution.py:79
  71.0 2.2 %copy-start.2 = (bf16[1536,40]{0,1:T(8,128)(2,1)S(1)}, bf16[1536,40]{0,1:T(8,128)(2,1)}, u32[]{:S(2)}) copy-start(bf16[1536,40]{0,1:T(8,128)(2,1)} %param.20) | copy-start | bytes 368644
  71.0 2.2 %copy-start.3 = (s32[128,8]{0,1:T(8,128)S(1)}, s32[128,8]{0,1:T(8,128)}, u32[]{:S(2)}) copy-start(s32[128,8]{0,1:T(8,128)} %param.23) | copy-start | bytes 12292
  72.6 5.3 %collective-permute-start.18 = (bf16[32,1536]{1,0:T(8,128)(2,1)S(1)}, bf16[32,1536]{1,0:T(8,128)(2,1)S(1)}, u32[]{:S(2)}, u32[]{:S(2)}) collective-permute-start(bf16[32,1536]{1,0:T(8,128)(2,1)S(1)} %get-tuple-element.109), channel_id=1, source_target_pairs={{0,1},{1,0},{2,3},{3,2},{4,5},{5,4},{6,7},{7,6},{8,9},{9,8},{10,11... | collective-permute-start | bytes 294920 | tf_op jit(solution)/shard_map/ppermute | solution.py:737
  77.9 7.2 %copy-start = (bf16[512,4,128]{2,1,0:T(4,128)(2,1)S(1)}, bf16[512,4,128]{2,1,0:T(4,128)(2,1)}, u32[]{:S(2)}) copy-start(bf16[512,4,128]{2,1,0:T(4,128)(2,1)} %param.25) | copy-start | bytes 1572868
  79.3 4.7 %collective-permute-start.23 = (bf16[32,1536]{1,0:T(8,128)(2,1)S(1)}, bf16[32,1536]{1,0:T(8,128)(2,1)S(1)}, u32[]{:S(2)}, u32[]{:S(2)}) collective-permute-start(bf16[32,1536]{1,0:T(8,128)(2,1)S(1)} %get-tuple-element.115), channel_id=1, source_target_pairs={{0,1},{1,0},{2,3},{3,2},{4,5},{5,4},{6,7},{7,6},{8,9},{9,8},{10,11... | collective-permute-start | bytes 294920 | tf_op jit(solution)/shard_map/ppermute | solution.py:743

commit v11 on v10

--- a/solution.py
+++ b/solution.py
@@ -550,7 +550,7 @@
             pltpu.VMEM((groups * down_rows, model), bf16),
         ],
         compiler_params=PARAMS,
-        cost_estimate=takes(1.2),
+        cost_estimate=takes(4.2),
         name="expert",
     )(own, other, *parts)
 

time: 87 us -> 73.2 us (0.84)
  the two profiles are of different devices: /device:TPU:14 before, /device:TPU:0 now
where the time goes in v11:
time: 73.2 us; the launch traced here: 72.8 us
  starting transfers between devices  31.4 us (43%)
  Pallas kernels  19.8 us (27%)
  waiting for transfers between devices  18.1 us (25%)
  local copies, waits for them, and re-layouts  2.61 us (4%)
  between operations  0.86 us (1%)
    ppermute x8, starting transfers between devices, step(): self.mine.append(self.across(held))  15.2 us
    ppermute x8, waiting for transfers between devices, step(): self.mine.append(self.across(held))  8.63 us
    all_to_all x1, starting transfers between devices, two_lane_shards(): lax.all_to_all(outgoing, 'grp', split_axis=0, concat_axis=0, tiled=True)  4.54 us
    ppermute x1, waiting for transfers between devices, two_lane_shards(): returned = swap(back)  3.11 us
    ppermute x1, waiting for transfers between devices, two_lane_shards(): landed = swap(sent_rows)  2.89 us
    pallas_call x1, Pallas kernels, expert(): pl.pallas_call(functools.partial(expert_kernel, groups, up_rows, down_row...  2.87 us
    ppermute x1, starting transfers between devices, two_lane_shards(): other_tokens = swap(tokens)  2.56 us
    ppermute x1, starting transfers between devices, two_lane_shards(): seam = lax.ppermute(tail, 'grp', [(g, g + 1) for g in range(groups - 1)])  2.39 us
  transfers between devices with their start and end apart: 25, of which 7 were waited for; matrix products, arithmetic and copies ran while one was open for 4% of the time, Pallas kernels for 25%

profile of v11, /device:TPU:0, one launch (start us, length us, event | category | flops | bytes accessed | tf_op | source)
XLA Modules:
  0.0 72.8 jit_solution(7676313329469593410)
XLA Ops:
  1.7 2.6 %collective-permute-start.5 = (bf16[128,1536]{1,0:T(8,128)(2,1)}, bf16[128,1536]{1,0:T(8,128)(2,1)S(1)}, u32[]{:S(2)}, u32[]{:S(2)}) collective-permute-start(bf16[128,1536]{1,0:T(8,128)(2,1)} %tokens.1), channel_id=1, source_target_pairs={{0,1},{1,0},{2,3},{3,2},{4,5},{5,4},{6,7},{7,6},{8,9},{9,8},{10,11... | collective-permute-start | bytes 1179656 | tf_op jit(solution)/shard_map/ppermute | solution.py:686
  4.2 1.1 %pack.1 = (bf16[576,512]{1,0:T(8,128)(2,1)S(1)}, bf16[192,768]{1,0:T(8,128)(2,1)S(1)}) custom-call(bf16[96,1024]{1,0:T(8,128)(2,1)} %bitcast.23, bf16[32,1536]{1,0:T(8,128)(2,1)} %bitcast.25, bf16[96,1536]{1,0:T(8,128)(2,1)} %bitcast.21, bf16[96,1024]{1,0:T(8,128)(2,1)S(1)} %collective-permute-done.refs_3_, ...), custom_call_target="tpu_custom_call" | custom-call | flops 1 | bytes 1 | tf_op jit(solution)/shard_map/pack/pallas_call | solution.py:159
  5.4 1.7 %collective-permute-start.4 = (bf16[192,768]{1,0:T(8,128)(2,1)S(1)}, bf16[192,768]{1,0:T(8,128)(2,1)S(1)}, u32[]{:S(2)}, u32[]{:S(2)}) collective-permute-start(bf16[192,768]{1,0:T(8,128)(2,1)S(1)} %get-tuple-element.61.refs_0_), channel_id=1, source_target_pairs={{0,8},{2,6},{8,16},{10,2},{16,24},{18,10},{24,28},{26,18},{28,20},... | collective-permute-start | bytes 884744 | tf_op jit(solution)/shard_map/ppermute | solution.py:70
  7.1 1.6 %collective-permute-start.3 = (bf16[576,512]{1,0:T(8,128)(2,1)S(1)}, bf16[576,512]{1,0:T(8,128)(2,1)S(1)}, u32[]{:S(2)}, u32[]{:S(2)}) collective-permute-start(bf16[576,512]{1,0:T(8,128)(2,1)S(1)} %get-tuple-element.60.refs_0_), channel_id=1, source_target_pairs={{0,8},{2,6},{8,16},{10,2},{16,24},{18,10},{24,28},{26,18},{28,20},... | collective-permute-start | bytes 1769480 | tf_op jit(solution)/shard_map/ppermute | solution.py:70
  8.7 1.5 %prepare.1 = (f32[256,128]{1,0:T(8,128)S(1)}, f32[256,128]{1,0:T(8,128)S(1)}, f32[256,128]{1,0:T(8,128)S(1)}, bf16[64,128]{1,0:T(8,128)(2,1)S(1)}, bf16[512,256]...) custom-call(s32[1,256]{1,0:T(1,128)} %bitcast.26, s32[1,256]{1,0:T(1,128)} %bitcast.27, ...), custom_call_target="tpu_custom_call" | custom-call | flops 1 | bytes 1 | tf_op jit(solution)/shard_map/prepare/pallas_call | solution.py:255
  10.2 1.8 %copy.17 = bf16[192,8,4,128]{3,1,2,0:T(8,128)(2,1)S(1)} copy(bf16[192,8,4,128]{3,2,1,0:T(4,128)(2,1)} %bitcast.18) | data formatting | bytes 3145728
  12.0 2.1 %collective-permute-done.5.other = bf16[128,1536]{1,0:T(8,128)(2,1)S(1)} collective-permute-done((bf16[128,1536]{1,0:T(8,128)(2,1)}, bf16[128,1536]{1,0:T(8,128)(2,1)S(1)}, u32[]{:S(2)}, u32[]{:S(2)}) %collective-permute-start.5) | collective-permute-done | bytes 393248 | tf_op jit(solution)/shard_map/ppermute | solution.py:686
  14.1 1.8 %collective-permute-start.7 = (bf16[192,768]{1,0:T(8,128)(2,1)S(1)}, bf16[192,768]{1,0:T(8,128)(2,1)S(1)}, u32[]{:S(2)}, u32[]{:S(2)}) collective-permute-start(bf16[192,768]{1,0:T(8,128)(2,1)S(1)} %collective-permute-done.4.refs_1_), channel_id=1, source_target_pairs={{0,8},{2,6},{8,16},{10,2},{16,24},{18,10},{24,28},{26,18},{28,20},... | collective-permute-start | bytes 884744 | tf_op jit(solution)/shard_map/ppermute | solution.py:70
  16.0 2.2 %project.1 = (bf16[256,768]{1,0:T(8,128)(2,1)S(1)}, bf16[256,512]{1,0:T(8,128)(2,1)S(1)}, bf16[128,512]{1,0:T(8,128)(2,1)S(1)}) custom-call(bf16[128,1536]{1,0:T(8,128)(2,1)S(1)} %copy-done.1, bf16[128,1536]{1,0:T(8,128)(2,1)S(1)} %collective-permute-done.5.other, f32[1,1536]{1,0:T(1,128)S(1)} %get-tuple-element.66.gain, ...), custom_call_target="tpu_custom_call" | custom-call | flops 9200000000 | bytes 64000000 | tf_op jit(solution)/shard_map/project/pallas_call | solution.py:305
  18.2 2.4 %collective-permute-start.6 = (bf16[128,512]{1,0:T(8,128)(2,1)S(1)}, bf16[128,512]{1,0:T(8,128)(2,1)S(1)}, u32[]{:S(2)}, u32[]{:S(2)}) collective-permute-start(bf16[128,512]{1,0:T(8,128)(2,1)S(1)} %get-tuple-element.70), channel_id=1, source_target_pairs={{0,2},{2,4},{4,6},{6,8},{8,10},{10,12},{12,14},{14,16},{16,18},{18... | collective-permute-start | bytes 393224 | tf_op jit(solution)/shard_map/ppermute | solution.py:704
  21.6 1.7 %collective-permute-start.9 = (bf16[192,768]{1,0:T(8,128)(2,1)S(1)}, bf16[192,768]{1,0:T(8,128)(2,1)S(1)}, u32[]{:S(2)}, u32[]{:S(2)}) collective-permute-start(bf16[192,768]{1,0:T(8,128)(2,1)S(1)} %collective-permute-done.7.refs_2_), channel_id=1, source_target_pairs={{0,8},{2,6},{8,16},{10,2},{16,24},{18,10},{24,28},{26,18},{28,20},... | collective-permute-start | bytes 884744 | tf_op jit(solution)/shard_map/ppermute | solution.py:70
  23.3 1.3 %attend_late.1.late = bf16[128,768]{1,0:T(8,128)(2,1)S(1)} custom-call(bf16[256,768]{1,0:T(8,128)(2,1)S(1)} %get-tuple-element.73.q, bf16[256,512]{1,0:T(8,128)(2,1)S(1)} %get-tuple-element.100.kv, f32[256,128]{1,0:T(8,128)S(1)} %get-tuple-element.75.past), custom_call_target="tpu_custom_call" | custom-call | flops 2300000000 | bytes 16000000 | tf_op jit(solution)/shard_map/attend_late/pallas_call | solution.py:361
  24.7 2.3 %collective-permute-start.8 = (bf16[576,512]{1,0:T(8,128)(2,1)S(1)}, bf16[576,512]{1,0:T(8,128)(2,1)S(1)}, u32[]{:S(2)}, u32[]{:S(2)}) collective-permute-start(bf16[576,512]{1,0:T(8,128)(2,1)S(1)} %collective-permute-done.3.refs_1_), channel_id=1, source_target_pairs={{0,8},{2,6},{8,16},{10,2},{16,24},{18,10},{24,28},{26,18},{28,20},... | collective-permute-start | bytes 1769480 | tf_op jit(solution)/shard_map/ppermute | solution.py:70
  27.0 1.5 %attend_early.1.early = bf16[128,768]{1,0:T(8,128)(2,1)S(1)} custom-call(bf16[256,768]{1,0:T(8,128)(2,1)S(1)} %get-tuple-element.73.q, bf16[256,512]{1,0:T(8,128)(2,1)S(1)} %get-tuple-element.100.kv, bf16[128,512]{1,0:T(8,128)(2,1)S(1)} %collective-permute-done.6.seam, f32[256,128]{1,0:T(8,128)S(1)} %get-tuple-element.75.past), custom_call_target="tpu_custom_call" | custom-call | flops 2300000000 | bytes 16000000 | tf_op jit(solution)/shard_map/attend_early/pallas_call | solution.py:373
  28.6 1.6 %collective-permute-start.12 = (bf16[96,768]{1,0:T(8,128)(2,1)S(1)}, bf16[96,768]{1,0:T(8,128)(2,1)S(1)}, u32[]{:S(2)}, u32[]{:S(2)}) collective-permute-start(bf16[96,768]{1,0:T(8,128)(2,1)S(1)} %slice.6), channel_id=1, source_target_pairs={{0,8},{2,6},{8,16},{10,2},{16,24},{18,10},{24,28},{26,18},{28,20},... | collective-permute-start | bytes 442376 | tf_op jit(solution)/shard_map/ppermute | solution.py:70
  30.2 6.0 %collective-permute-done.12.refs_7_ = bf16[96,768]{1,0:T(8,128)(2,1)S(1)} collective-permute-done((bf16[96,768]{1,0:T(8,128)(2,1)S(1)}, bf16[96,768]{1,0:T(8,128)(2,1)S(1)}, u32[]{:S(2)}, u32[]{:S(2)}) %collective-permute-start.12) | collective-permute-done | bytes 147488 | tf_op jit(solution)/shard_map/ppermute | solution.py:70
  36.3 2.2 %collective-permute-start.15 = (bf16[576,512]{1,0:T(8,128)(2,1)S(1)}, bf16[576,512]{1,0:T(8,128)(2,1)S(1)}, u32[]{:S(2)}, u32[]{:S(2)}) collective-permute-start(bf16[576,512]{1,0:T(8,128)(2,1)S(1)} %collective-permute-done.8.refs_2_), channel_id=1, source_target_pairs={{0,8},{2,6},{8,16},{10,2},{16,24},{18,10},{24,28},{26,18},{28,20},... | collective-permute-start | bytes 1769480 | tf_op jit(solution)/shard_map/ppermute | solution.py:70
  38.5 1.4 %collective-permute-done.14.refs_8_ = bf16[96,768]{1,0:T(8,128)(2,1)S(1)} collective-permute-done((bf16[96,768]{1,0:T(8,128)(2,1)S(1)}, bf16[96,768]{1,0:T(8,128)(2,1)S(1)}, u32[]{:S(2)}, u32[]{:S(2)}) %collective-permute-start.14) | collective-permute-done | bytes 147488 | tf_op jit(solution)/shard_map/ppermute | solution.py:79
  39.8 1.1 %outward_send.1 = bf16[128,1536]{1,0:T(8,128)(2,1)S(1)} custom-call(bf16[128,768]{1,0:T(8,128)(2,1)S(1)} %attend_early.1.early, bf16[128,768]{1,0:T(8,128)(2,1)S(1)} %attend_late.1.late, bf16[192,768]{1,0:T(8,128)(2,1)S(1)} %get-tuple-element.61.refs_0_, bf16[192,768]{1,0:T(8,128)(2,1)S(1)} %collective-permute-done.4.refs_1_, ...), custom_call_target="tpu_custom_call" | custom-call | flops 1 | bytes 2359296 | tf_op jit(solution)/shard_map/outward_send/pallas_call | solution.py:418
  41.0 1.5 %collective-permute-start.17 = (bf16[128,1536]{1,0:T(8,128)(2,1)S(1)}, bf16[128,1536]{1,0:T(8,128)(2,1)}, u32[]{:S(2)}, u32[]{:S(2)}) collective-permute-start(bf16[128,1536]{1,0:T(8,128)(2,1)S(1)} %outward_send.1), channel_id=1, source_target_pairs={{0,1},{1,0},{2,3},{3,2},{4,5},{5,4},{6,7},{7,6},{8,9},{9,8},{10,11... | collective-permute-start | bytes 1179656 | tf_op jit(solution)/shard_map/ppermute | solution.py:723
  42.5 2.1 %outward_keep.1 = (f32[128,1536]{1,0:T(8,128)}, f32[1,1536]{1,0:T(1,128)S(1)}) custom-call(bf16[128,768]{1,0:T(8,128)(2,1)S(1)} %attend_early.1.early, bf16[128,768]{1,0:T(8,128)(2,1)S(1)} %attend_late.1.late, bf16[128,1536]{1,0:T(8,128)(2,1)S(1)} %copy-done.1, f32[1536]{0:T(1024)S(1)} %copy-done.4, bf16[192,768]{1,0:T(8,128)(2,1)S(1)} %get-tuple-element.61.refs_0_, ...), custom_call_target="tpu_custom_call" | custom-call | flops 1 | bytes 2359296 | tf_op jit(solution)/shard_map/outward_keep/pallas_call | solution.py:432
  44.6 1.6 %collective-permute-done.15.refs_3_ = bf16[576,512]{1,0:T(8,128)(2,1)S(1)} collective-permute-done((bf16[576,512]{1,0:T(8,128)(2,1)S(1)}, bf16[576,512]{1,0:T(8,128)(2,1)S(1)}, u32[]{:S(2)}, u32[]{:S(2)}) %collective-permute-start.15) | collective-permute-done | bytes 589856 | tf_op jit(solution)/shard_map/ppermute | solution.py:70
  46.9 2.2 %collective-permute-start.16 = (bf16[288,512]{1,0:T(8,128)(2,1)}, bf16[288,512]{1,0:T(8,128)(2,1)}, u32[]{:S(2)}, u32[]{:S(2)}) collective-permute-start(bf16[288,512]{1,0:T(8,128)(2,1)} %slice.7), channel_id=1, source_target_pairs={{0,8},{2,6},{8,16},{10,2},{16,24},{18,10},{24,28},{26,18},{28,20},... | collective-permute-start | bytes 884744 | tf_op jit(solution)/shard_map/ppermute | solution.py:70
  49.6 1.4 %bundle.1 = bf16[16,144,128]{2,1,0:T(8,128)(2,1)} custom-call(bf16[512,256]{1,0:T(8,128)(2,1)S(1)} %get-tuple-element.99.send, bf16[256,512]{1,0:T(8,128)(2,1)S(1)} %get-tuple-element.100.kv, bf16[256,128]{1,0:T(8,128)(2,1)S(1)} %get-tuple-element.101.tags), custom_call_target="tpu_custom_call" | custom-call | flops 1 | bytes 1 | tf_op jit(solution)/shard_map/bundle/pallas_call | solution.py:604
  50.9 4.5 %all-to-all-start = ((bf16[16,144,128]{2,1,0:T(8,128)(2,1)}), bf16[16,144,128]{2,1,0:T(8,128)(2,1)S(1)}, u32[]{:S(2)}, u32[]{:S(2)}) async-start(bf16[16,144,128]{2,1,0:T(8,128)(2,1)} %bundle.1), calls=%async_computation | async-start | bytes 1179648 | tf_op jit(solution)/shard_map/all_to_all | solution.py:732
  56.0 1.7 %route.1 = (bf16[128,1536]{1,0:T(8,128)(2,1)S(1)}, bf16[128,1536]{1,0:T(8,128)(2,1)S(1)}, bf16[32,1536]{1,0:T(8,128)(2,1)S(1)}) custom-call(f32[128,1536]{1,0:T(8,128)} %get-tuple-element.94.mine, bf16[128,1536]{1,0:T(8,128)(2,1)} %collective-permute-done.17.arrived, f32[1,1536]{1,0:T(1,128)S(1)} %get-tuple-element.103.gain, ...), custom_call_target="tpu_custom_call" | custom-call | flops 2300000000 | bytes 16000000 | tf_op jit(solution)/shard_map/route/pallas_call | solution.py:465
  57.7 1.6 %collective-permute-start.18 = (bf16[32,1536]{1,0:T(8,128)(2,1)S(1)}, bf16[32,1536]{1,0:T(8,128)(2,1)S(1)}, u32[]{:S(2)}, u32[]{:S(2)}) collective-permute-start(bf16[32,1536]{1,0:T(8,128)(2,1)S(1)} %get-tuple-element.109), channel_id=1, source_target_pairs={{0,1},{1,0},{2,3},{3,2},{4,5},{5,4},{6,7},{7,6},{8,9},{9,8},{10,11... | collective-permute-start | bytes 294920 | tf_op jit(solution)/shard_map/ppermute | solution.py:737
  59.7 2.9 %collective-permute-done.18.other = bf16[32,1536]{1,0:T(8,128)(2,1)S(1)} collective-permute-done((bf16[32,1536]{1,0:T(8,128)(2,1)S(1)}, bf16[32,1536]{1,0:T(8,128)(2,1)S(1)}, u32[]{:S(2)}, u32[]{:S(2)}) %collective-permute-start.18) | collective-permute-done | bytes 98336 | tf_op jit(solution)/shard_map/ppermute | solution.py:737
  62.6 2.9 %expert.1 = (bf16[32,1536]{1,0:T(8,128)(2,1)S(1)}, bf16[32,1536]{1,0:T(8,128)(2,1)S(1)}) custom-call(bf16[32,1536]{1,0:T(8,128)(2,1)S(1)} %get-tuple-element.111.own, bf16[32,1536]{1,0:T(8,128)(2,1)S(1)} %collective-permute-done.18.other, bf16[576,512]{1,0:T(8,128)(2,1)S(1)} %get-tuple-element.60.refs_0_, ...), custom_call_target="tpu_custom_call" | custom-call | flops 4830000128 | bytes 33600000 | tf_op jit(solution)/shard_map/expert/pallas_call | solution.py:542
  65.5 1.6 %collective-permute-start.23 = (bf16[32,1536]{1,0:T(8,128)(2,1)S(1)}, bf16[32,1536]{1,0:T(8,128)(2,1)S(1)}, u32[]{:S(2)}, u32[]{:S(2)}) collective-permute-start(bf16[32,1536]{1,0:T(8,128)(2,1)S(1)} %get-tuple-element.115), channel_id=1, source_target_pairs={{0,1},{1,0},{2,3},{3,2},{4,5},{5,4},{6,7},{7,6},{8,9},{9,8},{10,11... | collective-permute-start | bytes 294920 | tf_op jit(solution)/shard_map/ppermute | solution.py:743
  67.1 3.1 %collective-permute-done.23.returned = bf16[32,1536]{1,0:T(8,128)(2,1)S(1)} collective-permute-done((bf16[32,1536]{1,0:T(8,128)(2,1)S(1)}, bf16[32,1536]{1,0:T(8,128)(2,1)S(1)}, u32[]{:S(2)}, u32[]{:S(2)}) %collective-permute-start.23) | collective-permute-done | bytes 98336 | tf_op jit(solution)/shard_map/ppermute | solution.py:743
  71.3 1.6 %write.1 = bf16[2048,128]{1,0:T(8,128)(2,1)} custom-call(bf16[16,144,128]{2,1,0:T(8,128)(2,1)S(1)} %all-to-all-done.arrived, bf16[2048,128]{1,0:T(8,128)(2,1)S(1)} %bitcast.14), custom_call_target="tpu_custom_call" | custom-call | flops 1 | bytes 2097152 | tf_op jit(solution)/shard_map/write/pallas_call | solution.py:644
  (46 shorter events, 5.5 us)
Async XLA Ops:
  0.6 3.6 %collective-permute-start.2 = (bf16[96,1536]{1,0:T(8,128)(2,1)}, bf16[96,1536]{1,0:T(8,128)(2,1)S(1)}, u32[]{:S(2)}, u32[]{:S(2)}) collective-permute-start(bf16[96,1536]{1,0:T(8,128)(2,1)} %bitcast.20), channel_id=1, source_target_pairs={{0,2},{2,0},{4,6},{6,4},{8,10},{10,8},{12,14},{14,12},{16,18},{18,... | collective-permute-start | bytes 884744 | tf_op jit(solution)/shard_map/ppermute | solution.py:689
  1.1 3.1 %collective-permute-start = (bf16[96,1024]{1,0:T(8,128)(2,1)}, bf16[96,1024]{1,0:T(8,128)(2,1)S(1)}, u32[]{:S(2)}, u32[]{:S(2)}) collective-permute-start(bf16[96,1024]{1,0:T(8,128)(2,1)} %bitcast.22), channel_id=1, source_target_pairs={{0,2},{2,0},{4,6},{6,4},{8,10},{10,8},{12,14},{14,12},{16,18},{18,... | collective-permute-start | bytes 589832 | tf_op jit(solution)/shard_map/ppermute | solution.py:689
  1.2 3.0 %collective-permute-start.1 = (bf16[32,1536]{1,0:T(8,128)(2,1)}, bf16[32,1536]{1,0:T(8,128)(2,1)S(1)}, u32[]{:S(2)}, u32[]{:S(2)}) collective-permute-start(bf16[32,1536]{1,0:T(8,128)(2,1)} %bitcast.24), channel_id=1, source_target_pairs={{0,2},{2,0},{4,6},{6,4},{8,10},{10,8},{12,14},{14,12},{16,18},{18,... | collective-permute-start | bytes 294920 | tf_op jit(solution)/shard_map/ppermute | solution.py:689
  1.7 12.5 %collective-permute-start.5 = (bf16[128,1536]{1,0:T(8,128)(2,1)}, bf16[128,1536]{1,0:T(8,128)(2,1)S(1)}, u32[]{:S(2)}, u32[]{:S(2)}) collective-permute-start(bf16[128,1536]{1,0:T(8,128)(2,1)} %tokens.1), channel_id=1, source_target_pairs={{0,1},{1,0},{2,3},{3,2},{4,5},{5,4},{6,7},{7,6},{8,9},{9,8},{10,11... | collective-permute-start | bytes 1179656 | tf_op jit(solution)/shard_map/ppermute | solution.py:686
  5.4 8.8 %collective-permute-start.4 = (bf16[192,768]{1,0:T(8,128)(2,1)S(1)}, bf16[192,768]{1,0:T(8,128)(2,1)S(1)}, u32[]{:S(2)}, u32[]{:S(2)}) collective-permute-start(bf16[192,768]{1,0:T(8,128)(2,1)S(1)} %get-tuple-element.61.refs_0_), channel_id=1, source_target_pairs={{0,8},{2,6},{8,16},{10,2},{16,24},{18,10},{24,28},{26,18},{28,20},... | collective-permute-start | bytes 884744 | tf_op jit(solution)/shard_map/ppermute | solution.py:70
  7.1 17.6 %collective-permute-start.3 = (bf16[576,512]{1,0:T(8,128)(2,1)S(1)}, bf16[576,512]{1,0:T(8,128)(2,1)S(1)}, u32[]{:S(2)}, u32[]{:S(2)}) collective-permute-start(bf16[576,512]{1,0:T(8,128)(2,1)S(1)} %get-tuple-element.60.refs_0_), channel_id=1, source_target_pairs={{0,8},{2,6},{8,16},{10,2},{16,24},{18,10},{24,28},{26,18},{28,20},... | collective-permute-start | bytes 1769480 | tf_op jit(solution)/shard_map/ppermute | solution.py:70
  10.2 5.8 %copy-start.1 = (bf16[128,1536]{1,0:T(8,128)(2,1)S(1)}, bf16[128,1536]{1,0:T(8,128)(2,1)}, u32[]{:S(2)}) copy-start(bf16[128,1536]{1,0:T(8,128)(2,1)} %tokens.1) | copy-start | bytes 1179652
  10.2 5.8 %copy-start.5 = (bf16[1536,768]{1,0:T(8,128)(2,1)S(1)}, bf16[1536,768]{1,0:T(8,128)(2,1)}, u32[]{:S(2)}) copy-start(bf16[1536,768]{1,0:T(8,128)(2,1)} %w_query.1) | copy-start | bytes 7077892
  14.1 7.5 %collective-permute-start.7 = (bf16[192,768]{1,0:T(8,128)(2,1)S(1)}, bf16[192,768]{1,0:T(8,128)(2,1)S(1)}, u32[]{:S(2)}, u32[]{:S(2)}) collective-permute-start(bf16[192,768]{1,0:T(8,128)(2,1)S(1)} %collective-permute-done.4.refs_1_), channel_id=1, source_target_pairs={{0,8},{2,6},{8,16},{10,2},{16,24},{18,10},{24,28},{26,18},{28,20},... | collective-permute-start | bytes 884744 | tf_op jit(solution)/shard_map/ppermute | solution.py:70
  16.0 12.5 %collective-permute-start.10 = (bf16[192,768]{1,0:T(8,128)(2,1)S(1)}, bf16[192,768]{1,0:T(8,128)(2,1)S(1)}, u32[]{:S(2)}, u32[]{:S(2)}) collective-permute-start(bf16[192,768]{1,0:T(8,128)(2,1)S(1)} %collective-permute-done.4.refs_1_), channel_id=1, source_target_pairs={{0,2},{2,0},{4,6},{6,4},{8,10},{10,8},{12,14},{14,12},{16,18},{18,... | collective-permute-start | bytes 884744 | tf_op jit(solution)/shard_map/ppermute | solution.py:79
  18.2 6.4 %collective-permute-start.6 = (bf16[128,512]{1,0:T(8,128)(2,1)S(1)}, bf16[128,512]{1,0:T(8,128)(2,1)S(1)}, u32[]{:S(2)}, u32[]{:S(2)}) collective-permute-start(bf16[128,512]{1,0:T(8,128)(2,1)S(1)} %get-tuple-element.70), channel_id=1, source_target_pairs={{0,2},{2,4},{4,6},{6,8},{8,10},{10,12},{12,14},{14,16},{16,18},{18... | collective-permute-start | bytes 393224 | tf_op jit(solution)/shard_map/ppermute | solution.py:704
  21.6 6.8 %collective-permute-start.11 = (bf16[192,768]{1,0:T(8,128)(2,1)S(1)}, bf16[192,768]{1,0:T(8,128)(2,1)S(1)}, u32[]{:S(2)}, u32[]{:S(2)}) collective-permute-start(bf16[192,768]{1,0:T(8,128)(2,1)S(1)} %collective-permute-done.7.refs_2_), channel_id=1, source_target_pairs={{0,2},{2,0},{4,6},{6,4},{8,10},{10,8},{12,14},{14,12},{16,18},{18,... | collective-permute-start | bytes 884744 | tf_op jit(solution)/shard_map/ppermute | solution.py:79
  21.6 6.8 %collective-permute-start.9 = (bf16[192,768]{1,0:T(8,128)(2,1)S(1)}, bf16[192,768]{1,0:T(8,128)(2,1)S(1)}, u32[]{:S(2)}, u32[]{:S(2)}) collective-permute-start(bf16[192,768]{1,0:T(8,128)(2,1)S(1)} %collective-permute-done.7.refs_2_), channel_id=1, source_target_pairs={{0,8},{2,6},{8,16},{10,2},{16,24},{18,10},{24,28},{26,18},{28,20},... | collective-permute-start | bytes 884744 | tf_op jit(solution)/shard_map/ppermute | solution.py:70
  24.7 11.6 %collective-permute-start.8 = (bf16[576,512]{1,0:T(8,128)(2,1)S(1)}, bf16[576,512]{1,0:T(8,128)(2,1)S(1)}, u32[]{:S(2)}, u32[]{:S(2)}) collective-permute-start(bf16[576,512]{1,0:T(8,128)(2,1)S(1)} %collective-permute-done.3.refs_1_), channel_id=1, source_target_pairs={{0,8},{2,6},{8,16},{10,2},{16,24},{18,10},{24,28},{26,18},{28,20},... | collective-permute-start | bytes 1769480 | tf_op jit(solution)/shard_map/ppermute | solution.py:70
  28.5 1.7 %collective-permute-start.13 = (bf16[192,768]{1,0:T(8,128)(2,1)S(1)}, bf16[192,768]{1,0:T(8,128)(2,1)S(1)}, u32[]{:S(2)}, u32[]{:S(2)}) collective-permute-start(bf16[192,768]{1,0:T(8,128)(2,1)S(1)} %collective-permute-done.9.refs_3_), channel_id=1, source_target_pairs={{0,2},{2,0},{4,6},{6,4},{8,10},{10,8},{12,14},{14,12},{16,18},{18,... | collective-permute-start | bytes 884744 | tf_op jit(solution)/shard_map/ppermute | solution.py:79
  28.6 13.9 %copy-start.4 = (f32[1536]{0:T(1024)S(1)}, f32[1536]{0:T(1024)}, u32[]{:S(2)}) copy-start(f32[1536]{0:T(1024)} %flat_gain.1) | copy-start | bytes 18436
  28.6 7.7 %collective-permute-start.12 = (bf16[96,768]{1,0:T(8,128)(2,1)S(1)}, bf16[96,768]{1,0:T(8,128)(2,1)S(1)}, u32[]{:S(2)}, u32[]{:S(2)}) collective-permute-start(bf16[96,768]{1,0:T(8,128)(2,1)S(1)} %slice.6), channel_id=1, source_target_pairs={{0,8},{2,6},{8,16},{10,2},{16,24},{18,10},{24,28},{26,18},{28,20},... | collective-permute-start | bytes 442376 | tf_op jit(solution)/shard_map/ppermute | solution.py:70
  36.3 9.9 %collective-permute-start.15 = (bf16[576,512]{1,0:T(8,128)(2,1)S(1)}, bf16[576,512]{1,0:T(8,128)(2,1)S(1)}, u32[]{:S(2)}, u32[]{:S(2)}) collective-permute-start(bf16[576,512]{1,0:T(8,128)(2,1)S(1)} %collective-permute-done.8.refs_2_), channel_id=1, source_target_pairs={{0,8},{2,6},{8,16},{10,2},{16,24},{18,10},{24,28},{26,18},{28,20},... | collective-permute-start | bytes 1769480 | tf_op jit(solution)/shard_map/ppermute | solution.py:70
  38.5 1.4 %collective-permute-start.14 = (bf16[96,768]{1,0:T(8,128)(2,1)S(1)}, bf16[96,768]{1,0:T(8,128)(2,1)S(1)}, u32[]{:S(2)}, u32[]{:S(2)}) collective-permute-start(bf16[96,768]{1,0:T(8,128)(2,1)S(1)} %collective-permute-done.12.refs_7_), channel_id=1, source_target_pairs={{0,2},{2,0},{4,6},{6,4},{8,10},{10,8},{12,14},{14,12},{16,18},{18,... | collective-permute-start | bytes 442376 | tf_op jit(solution)/shard_map/ppermute | solution.py:79
  41.0 14.5 %collective-permute-start.17 = (bf16[128,1536]{1,0:T(8,128)(2,1)S(1)}, bf16[128,1536]{1,0:T(8,128)(2,1)}, u32[]{:S(2)}, u32[]{:S(2)}) collective-permute-start(bf16[128,1536]{1,0:T(8,128)(2,1)S(1)} %outward_send.1), channel_id=1, source_target_pairs={{0,1},{1,0},{2,3},{3,2},{4,5},{5,4},{6,7},{7,6},{8,9},{9,8},{10,11... | collective-permute-start | bytes 1179656 | tf_op jit(solution)/shard_map/ppermute | solution.py:723
  46.9 8.6 %collective-permute-start.16 = (bf16[288,512]{1,0:T(8,128)(2,1)}, bf16[288,512]{1,0:T(8,128)(2,1)}, u32[]{:S(2)}, u32[]{:S(2)}) collective-permute-start(bf16[288,512]{1,0:T(8,128)(2,1)} %slice.7), channel_id=1, source_target_pairs={{0,8},{2,6},{8,16},{10,2},{16,24},{18,10},{24,28},{26,18},{28,20},... | collective-permute-start | bytes 884744 | tf_op jit(solution)/shard_map/ppermute | solution.py:70
  49.1 13.5 %collective-permute-start.19 = (bf16[576,512]{1,0:T(8,128)(2,1)S(1)}, bf16[576,512]{1,0:T(8,128)(2,1)}, u32[]{:S(2)}, u32[]{:S(2)}) collective-permute-start(bf16[576,512]{1,0:T(8,128)(2,1)S(1)} %collective-permute-done.3.refs_1_), channel_id=1, source_target_pairs={{0,2},{2,0},{4,6},{6,4},{8,10},{10,8},{12,14},{14,12},{16,18},{18,... | collective-permute-start | bytes 1769480 | tf_op jit(solution)/shard_map/ppermute | solution.py:79
  49.1 13.5 %collective-permute-start.20 = (bf16[576,512]{1,0:T(8,128)(2,1)S(1)}, bf16[576,512]{1,0:T(8,128)(2,1)}, u32[]{:S(2)}, u32[]{:S(2)}) collective-permute-start(bf16[576,512]{1,0:T(8,128)(2,1)S(1)} %collective-permute-done.8.refs_2_), channel_id=1, source_target_pairs={{0,2},{2,0},{4,6},{6,4},{8,10},{10,8},{12,14},{14,12},{16,18},{18,... | collective-permute-start | bytes 1769480 | tf_op jit(solution)/shard_map/ppermute | solution.py:79
  49.6 13.0 %collective-permute-start.21 = (bf16[576,512]{1,0:T(8,128)(2,1)S(1)}, bf16[576,512]{1,0:T(8,128)(2,1)}, u32[]{:S(2)}, u32[]{:S(2)}) collective-permute-start(bf16[576,512]{1,0:T(8,128)(2,1)S(1)} %collective-permute-done.15.refs_3_), channel_id=1, source_target_pairs={{0,2},{2,0},{4,6},{6,4},{8,10},{10,8},{12,14},{14,12},{16,18},{18,... | collective-permute-start | bytes 1769480 | tf_op jit(solution)/shard_map/ppermute | solution.py:79
  50.9 20.3 %all-to-all-start = ((bf16[16,144,128]{2,1,0:T(8,128)(2,1)}), bf16[16,144,128]{2,1,0:T(8,128)(2,1)S(1)}, u32[]{:S(2)}, u32[]{:S(2)}) async-start(bf16[16,144,128]{2,1,0:T(8,128)(2,1)} %bundle.1), calls=%async_computation | async-start | bytes 1179648 | tf_op jit(solution)/shard_map/all_to_all | solution.py:732
  55.5 7.1 %collective-permute-start.22 = (bf16[288,512]{1,0:T(8,128)(2,1)}, bf16[288,512]{1,0:T(8,128)(2,1)S(1)}, u32[]{:S(2)}, u32[]{:S(2)}) collective-permute-start(bf16[288,512]{1,0:T(8,128)(2,1)} %collective-permute-done.16.refs_7_), channel_id=1, source_target_pairs={{0,2},{2,0},{4,6},{6,4},{8,10},{10,8},{12,14},{14,12},{16,18},{18,... | collective-permute-start | bytes 884744 | tf_op jit(solution)/shard_map/ppermute | solution.py:79
  56.0 3.3 %copy-start.2 = (bf16[1536,40]{0,1:T(8,128)(2,1)S(1)}, bf16[1536,40]{0,1:T(8,128)(2,1)}, u32[]{:S(2)}) copy-start(bf16[1536,40]{0,1:T(8,128)(2,1)} %param.20) | copy-start | bytes 368644
  56.0 3.3 %copy-start.3 = (s32[128,8]{0,1:T(8,128)S(1)}, s32[128,8]{0,1:T(8,128)}, u32[]{:S(2)}) copy-start(s32[128,8]{0,1:T(8,128)} %param.23) | copy-start | bytes 12292
  57.7 4.9 %collective-permute-start.18 = (bf16[32,1536]{1,0:T(8,128)(2,1)S(1)}, bf16[32,1536]{1,0:T(8,128)(2,1)S(1)}, u32[]{:S(2)}, u32[]{:S(2)}) collective-permute-start(bf16[32,1536]{1,0:T(8,128)(2,1)S(1)} %get-tuple-element.109), channel_id=1, source_target_pairs={{0,1},{1,0},{2,3},{3,2},{4,5},{5,4},{6,7},{7,6},{8,9},{9,8},{10,11... | collective-permute-start | bytes 294920 | tf_op jit(solution)/shard_map/ppermute | solution.py:737
  62.6 8.7 %copy-start = (bf16[512,4,128]{2,1,0:T(4,128)(2,1)S(1)}, bf16[512,4,128]{2,1,0:T(4,128)(2,1)}, u32[]{:S(2)}) copy-start(bf16[512,4,128]{2,1,0:T(4,128)(2,1)} %param.25) | copy-start | bytes 1572868
  65.5 4.7 %collective-permute-start.23 = (bf16[32,1536]{1,0:T(8,128)(2,1)S(1)}, bf16[32,1536]{1,0:T(8,128)(2,1)S(1)}, u32[]{:S(2)}, u32[]{:S(2)}) collective-permute-start(bf16[32,1536]{1,0:T(8,128)(2,1)S(1)} %get-tuple-element.115), channel_id=1, source_target_pairs={{0,1},{1,0},{2,3},{3,2},{4,5},{5,4},{6,7},{7,6},{8,9},{9,8},{10,11... | collective-permute-start | bytes 294920 | tf_op jit(solution)/shard_map/ppermute | solution.py:743

commit v12 on v9

--- a/solution.py
+++ b/solution.py
@@ -434,7 +434,10 @@
         ),
         in_specs=[VMEM] * (4 + len(parts)),
         out_specs=(VMEM, VMEM),
-        scratch_shapes=[pltpu.VMEM((width, depth), bf16), pltpu.VMEM(early.shape, bf16)],
+        scratch_shapes=[
+            pltpu.VMEM((width, depth), bf16),
+            pltpu.VMEM(early.shape, bf16),
+        ],
         compiler_params=PARAMS,
         cost_estimate=reads(2 * width * depth),
         name="outward_keep",
@@ -462,7 +465,7 @@
         in_specs=[VMEM] * 4,
         out_specs=(VMEM,) * 3,
         compiler_params=PARAMS,
-        cost_estimate=takes(2),
+        cost_estimate=reads(10 * mine.shape[0] * mine.shape[1]),
         name="route",
     )(mine, arrived, gain, place)
 
@@ -535,7 +538,7 @@
             pltpu.VMEM((groups * down_rows, model), bf16),
         ],
         compiler_params=PARAMS,
-        cost_estimate=reads(2 * groups * 2 * (up_rows * 2 * width + down_rows * model)),
+        cost_estimate=takes(5.2),
         name="expert",
     )(own, other, *parts)
 
@@ -567,7 +570,7 @@
     )(residual, gates, spread, own, returned)
 
 
-def bundle_kernel(send, kv, tags, out):
+def bundle_kernel(send, kv, tags, result, out, sem):
     groups, rows, _ = out.shape
     heads = kv.shape[1] // 128
     capc = send.shape[0] // groups
@@ -582,15 +585,19 @@
         out[owner, heads * capc :, :] = lax.dot_general(
             one.astype(f32), wide, LAST_DIMS, preferred_element_type=f32
         ).astype(bf16)
+    copy = pltpu.make_async_copy(out, result, sem)
+    copy.start()
+    copy.wait()
 
 
 def bundle(groups, send, kv, tags):
     rows = send.shape[0] // groups * (kv.shape[1] // 128) + 16
     return pl.pallas_call(
         bundle_kernel,
-        out_shape=jax.ShapeDtypeStruct((groups, rows, 128), bf16),
+        out_shape=pltpu.HBM((groups, rows, 128), bf16),
         in_specs=[VMEM] * 3,
-        out_specs=VMEM,
+        out_specs=HBM,
+        scratch_shapes=[pltpu.VMEM((groups, rows, 128), bf16), pltpu.SemaphoreType.DMA],
         compiler_params=PARAMS,
         cost_estimate=LITTLE,
         name="bundle",
@@ -701,7 +708,6 @@
     out_ring.share(3)
     early, kv, out_ring.near = together((early, kv, out_ring.near))
     outgoing = bundle(groups, send, kv, tags)
-    arrived_cache = lax.all_to_all(outgoing, "grp", split_axis=0, concat_axis=0, tiled=True)
     early, outgoing = together((early, outgoing))
     early = out_ring.pin(early)
     early = expert_ring.pin(early)
@@ -713,16 +719,17 @@
     mine, late_gain = outward_keep(
         groups, early, late, tokens, moe_gain, out_ring.parts(), out_ring.unit_rows
     )
-    mine = expert_ring.pin(mine)
+    late_gain = expert_ring.pin(late_gain)
     expert_ring.share()
     expert_ring.step()
-    arrived, mine = expert_ring.pin(arrived, mine)
-    expert_ring.share()
+    outgoing = together((outgoing, sent))[0]
+    arrived_cache = lax.all_to_all(outgoing, "grp", split_axis=0, concat_axis=0, tiled=True)
 
     residual, moe_in, sent_rows = route(mine, arrived, late_gain, place)
     landed = swap(sent_rows)
     gates, own_rows, spread = gate(moe_in, router.T, expert_ids.T, place)
-    landed, own_rows = together((landed, own_rows))
+    landed, own_rows = expert_ring.pin(landed, own_rows)
+    expert_ring.share()
     own_made, back = expert(
         groups, own_rows, landed, expert_ring.parts(), up_rows, down_rows
     )

time: 78 us -> 72.9 us (0.935)
  the two profiles are of different devices: /device:TPU:18 before, /device:TPU:0 now
where the time goes in v12:
time: 72.9 us; the launch traced here: 72.5 us
  starting transfers between devices  30.9 us (42%)
  waiting for transfers between devices  20.2 us (28%)
  Pallas kernels  18 us (25%)
  local copies, waits for them, and re-layouts  2.61 us (4%)
  between operations  0.88 us (1%)
    ppermute x8, starting transfers between devices, step(): self.mine.append(self.across(held))  15.3 us
    ppermute x8, waiting for transfers between devices, step(): self.mine.append(self.across(held))  8.36 us
    all_to_all x1, starting transfers between devices, two_lane_shards(): lax.all_to_all(outgoing, 'grp', split_axis=0, concat_axis=0, tiled=True)  4.33 us
    ppermute x1, waiting for transfers between devices, two_lane_shards(): returned = swap(back)  3.35 us
    ppermute x1, waiting for transfers between devices, two_lane_shards(): landed = swap(sent_rows)  3.22 us
    pallas_call x1, Pallas kernels, expert(): pl.pallas_call(functools.partial(expert_kernel, groups, up_rows, down_row...  3.17 us
    ppermute x8, waiting for transfers between devices, share(): self.near.append(self.beside(self.mine[index]))  3.15 us
    ppermute x1, starting transfers between devices, two_lane_shards(): other_tokens = swap(tokens)  2.56 us
  transfers between devices with their start and end apart: 25, of which 8 were waited for; matrix products, arithmetic and copies ran while one was open for 4% of the time, Pallas kernels for 23%

profile of v12, /device:TPU:0, one launch (start us, length us, event | category | flops | bytes accessed | tf_op | source)
XLA Modules:
  0.0 72.5 jit_solution(638495653525803454)
XLA Ops:
  1.7 2.6 %collective-permute-start.5 = (bf16[128,1536]{1,0:T(8,128)(2,1)}, bf16[128,1536]{1,0:T(8,128)(2,1)S(1)}, u32[]{:S(2)}, u32[]{:S(2)}) collective-permute-start(bf16[128,1536]{1,0:T(8,128)(2,1)} %tokens.1), channel_id=1, source_target_pairs={{0,1},{1,0},{2,3},{3,2},{4,5},{5,4},{6,7},{7,6},{8,9},{9,8},{10,11... | collective-permute-start | bytes 1179656 | tf_op jit(solution)/shard_map/ppermute | solution.py:678
  4.2 1.1 %pack.1 = (bf16[576,512]{1,0:T(8,128)(2,1)S(1)}, bf16[192,768]{1,0:T(8,128)(2,1)S(1)}) custom-call(bf16[96,1024]{1,0:T(8,128)(2,1)} %bitcast.23, bf16[32,1536]{1,0:T(8,128)(2,1)} %bitcast.25, bf16[96,1536]{1,0:T(8,128)(2,1)} %bitcast.21, bf16[96,1024]{1,0:T(8,128)(2,1)S(1)} %collective-permute-done.refs_3_, ...), custom_call_target="tpu_custom_call" | custom-call | flops 1 | bytes 1 | tf_op jit(solution)/shard_map/pack/pallas_call | solution.py:159
  5.4 1.7 %collective-permute-start.4 = (bf16[192,768]{1,0:T(8,128)(2,1)S(1)}, bf16[192,768]{1,0:T(8,128)(2,1)S(1)}, u32[]{:S(2)}, u32[]{:S(2)}) collective-permute-start(bf16[192,768]{1,0:T(8,128)(2,1)S(1)} %get-tuple-element.62.refs_0_), channel_id=1, source_target_pairs={{0,8},{2,6},{8,16},{10,2},{16,24},{18,10},{24,28},{26,18},{28,20},... | collective-permute-start | bytes 884744 | tf_op jit(solution)/shard_map/ppermute | solution.py:70
  7.1 1.6 %collective-permute-start.3 = (bf16[576,512]{1,0:T(8,128)(2,1)S(1)}, bf16[576,512]{1,0:T(8,128)(2,1)}, u32[]{:S(2)}, u32[]{:S(2)}) collective-permute-start(bf16[576,512]{1,0:T(8,128)(2,1)S(1)} %get-tuple-element.61.refs_0_), channel_id=1, source_target_pairs={{0,8},{2,6},{8,16},{10,2},{16,24},{18,10},{24,28},{26,18},{28,20},... | collective-permute-start | bytes 1769480 | tf_op jit(solution)/shard_map/ppermute | solution.py:70
  8.7 1.5 %prepare.1 = (f32[256,128]{1,0:T(8,128)S(1)}, f32[256,128]{1,0:T(8,128)S(1)}, f32[256,128]{1,0:T(8,128)S(1)}, bf16[64,128]{1,0:T(8,128)(2,1)S(1)}, bf16[512,256]...) custom-call(s32[1,256]{1,0:T(1,128)} %bitcast.26, s32[1,256]{1,0:T(1,128)} %bitcast.27, ...), custom_call_target="tpu_custom_call" | custom-call | flops 1 | bytes 1 | tf_op jit(solution)/shard_map/prepare/pallas_call | solution.py:255
  10.2 1.8 %copy.17 = bf16[192,8,4,128]{3,1,2,0:T(8,128)(2,1)S(1)} copy(bf16[192,8,4,128]{3,2,1,0:T(4,128)(2,1)} %bitcast.18) | data formatting | bytes 3145728
  12.0 2.1 %collective-permute-done.5.other = bf16[128,1536]{1,0:T(8,128)(2,1)S(1)} collective-permute-done((bf16[128,1536]{1,0:T(8,128)(2,1)}, bf16[128,1536]{1,0:T(8,128)(2,1)S(1)}, u32[]{:S(2)}, u32[]{:S(2)}) %collective-permute-start.5) | collective-permute-done | bytes 393248 | tf_op jit(solution)/shard_map/ppermute | solution.py:678
  14.1 1.8 %collective-permute-start.7 = (bf16[192,768]{1,0:T(8,128)(2,1)S(1)}, bf16[192,768]{1,0:T(8,128)(2,1)S(1)}, u32[]{:S(2)}, u32[]{:S(2)}) collective-permute-start(bf16[192,768]{1,0:T(8,128)(2,1)S(1)} %collective-permute-done.4.refs_1_), channel_id=1, source_target_pairs={{0,8},{2,6},{8,16},{10,2},{16,24},{18,10},{24,28},{26,18},{28,20},... | collective-permute-start | bytes 884744 | tf_op jit(solution)/shard_map/ppermute | solution.py:70
  16.0 2.2 %project.1 = (bf16[256,768]{1,0:T(8,128)(2,1)S(1)}, bf16[256,512]{1,0:T(8,128)(2,1)S(1)}, bf16[128,512]{1,0:T(8,128)(2,1)S(1)}) custom-call(bf16[128,1536]{1,0:T(8,128)(2,1)S(1)} %copy-done.1, bf16[128,1536]{1,0:T(8,128)(2,1)S(1)} %collective-permute-done.5.other, f32[1,1536]{1,0:T(1,128)S(1)} %get-tuple-element.67.gain, ...), custom_call_target="tpu_custom_call" | custom-call | flops 9200000000 | bytes 64000000 | tf_op jit(solution)/shard_map/project/pallas_call | solution.py:305
  18.2 2.4 %collective-permute-start.6 = (bf16[128,512]{1,0:T(8,128)(2,1)S(1)}, bf16[128,512]{1,0:T(8,128)(2,1)S(1)}, u32[]{:S(2)}, u32[]{:S(2)}) collective-permute-start(bf16[128,512]{1,0:T(8,128)(2,1)S(1)} %get-tuple-element.71), channel_id=1, source_target_pairs={{0,2},{2,4},{4,6},{6,8},{8,10},{10,12},{12,14},{14,16},{16,18},{18... | collective-permute-start | bytes 393224 | tf_op jit(solution)/shard_map/ppermute | solution.py:696
  21.6 1.7 %collective-permute-start.9 = (bf16[192,768]{1,0:T(8,128)(2,1)S(1)}, bf16[192,768]{1,0:T(8,128)(2,1)S(1)}, u32[]{:S(2)}, u32[]{:S(2)}) collective-permute-start(bf16[192,768]{1,0:T(8,128)(2,1)S(1)} %collective-permute-done.7.refs_2_), channel_id=1, source_target_pairs={{0,8},{2,6},{8,16},{10,2},{16,24},{18,10},{24,28},{26,18},{28,20},... | collective-permute-start | bytes 884744 | tf_op jit(solution)/shard_map/ppermute | solution.py:70
  23.3 1.3 %attend_late.1.late = bf16[128,768]{1,0:T(8,128)(2,1)S(1)} custom-call(bf16[256,768]{1,0:T(8,128)(2,1)S(1)} %get-tuple-element.74.q, bf16[256,512]{1,0:T(8,128)(2,1)S(1)} %get-tuple-element.88.kv, f32[256,128]{1,0:T(8,128)S(1)} %get-tuple-element.76.past), custom_call_target="tpu_custom_call" | custom-call | flops 2300000000 | bytes 16000000 | tf_op jit(solution)/shard_map/attend_late/pallas_call | solution.py:361
  24.7 2.3 %collective-permute-start.8 = (bf16[576,512]{1,0:T(8,128)(2,1)}, bf16[576,512]{1,0:T(8,128)(2,1)}, u32[]{:S(2)}, u32[]{:S(2)}) collective-permute-start(bf16[576,512]{1,0:T(8,128)(2,1)} %collective-permute-done.3.refs_1_), channel_id=1, source_target_pairs={{0,8},{2,6},{8,16},{10,2},{16,24},{18,10},{24,28},{26,18},{28,20},... | collective-permute-start | bytes 1769480 | tf_op jit(solution)/shard_map/ppermute | solution.py:70
  27.0 1.5 %attend_early.1.early = bf16[128,768]{1,0:T(8,128)(2,1)S(1)} custom-call(bf16[256,768]{1,0:T(8,128)(2,1)S(1)} %get-tuple-element.74.q, bf16[256,512]{1,0:T(8,128)(2,1)S(1)} %get-tuple-element.88.kv, bf16[128,512]{1,0:T(8,128)(2,1)S(1)} %collective-permute-done.6.seam, f32[256,128]{1,0:T(8,128)S(1)} %get-tuple-element.76.past), custom_call_target="tpu_custom_call" | custom-call | flops 2300000000 | bytes 16000000 | tf_op jit(solution)/shard_map/attend_early/pallas_call | solution.py:373
  28.6 1.6 %collective-permute-start.12 = (bf16[96,768]{1,0:T(8,128)(2,1)S(1)}, bf16[96,768]{1,0:T(8,128)(2,1)S(1)}, u32[]{:S(2)}, u32[]{:S(2)}) collective-permute-start(bf16[96,768]{1,0:T(8,128)(2,1)S(1)} %slice.6), channel_id=1, source_target_pairs={{0,8},{2,6},{8,16},{10,2},{16,24},{18,10},{24,28},{26,18},{28,20},... | collective-permute-start | bytes 442376 | tf_op jit(solution)/shard_map/ppermute | solution.py:70
  30.2 1.4 %bundle.1 = bf16[16,144,128]{2,1,0:T(8,128)(2,1)} custom-call(bf16[512,256]{1,0:T(8,128)(2,1)S(1)} %get-tuple-element.87.send, bf16[256,512]{1,0:T(8,128)(2,1)S(1)} %get-tuple-element.88.kv, bf16[256,128]{1,0:T(8,128)(2,1)S(1)} %get-tuple-element.89.tags), custom_call_target="tpu_custom_call" | custom-call | flops 1 | bytes 1 | tf_op jit(solution)/shard_map/bundle/pallas_call | solution.py:595
  31.6 4.8 %collective-permute-done.12.refs_7_ = bf16[96,768]{1,0:T(8,128)(2,1)S(1)} collective-permute-done((bf16[96,768]{1,0:T(8,128)(2,1)S(1)}, bf16[96,768]{1,0:T(8,128)(2,1)S(1)}, u32[]{:S(2)}, u32[]{:S(2)}) %collective-permute-start.12) | collective-permute-done | bytes 147488 | tf_op jit(solution)/shard_map/ppermute | solution.py:70
  36.4 2.3 %collective-permute-start.16 = (bf16[576,512]{1,0:T(8,128)(2,1)}, bf16[576,512]{1,0:T(8,128)(2,1)S(1)}, u32[]{:S(2)}, u32[]{:S(2)}) collective-permute-start(bf16[576,512]{1,0:T(8,128)(2,1)} %collective-permute-done.8.refs_2_), channel_id=1, source_target_pairs={{0,8},{2,6},{8,16},{10,2},{16,24},{18,10},{24,28},{26,18},{28,20},... | collective-permute-start | bytes 1769480 | tf_op jit(solution)/shard_map/ppermute | solution.py:70
  38.7 1.4 %collective-permute-done.14.refs_8_ = bf16[96,768]{1,0:T(8,128)(2,1)S(1)} collective-permute-done((bf16[96,768]{1,0:T(8,128)(2,1)S(1)}, bf16[96,768]{1,0:T(8,128)(2,1)S(1)}, u32[]{:S(2)}, u32[]{:S(2)}) %collective-permute-start.14) | collective-permute-done | bytes 147488 | tf_op jit(solution)/shard_map/ppermute | solution.py:79
  40.1 1.2 %outward_send.1 = bf16[128,1536]{1,0:T(8,128)(2,1)S(1)} custom-call(bf16[128,768]{1,0:T(8,128)(2,1)S(1)} %attend_early.1.early, bf16[128,768]{1,0:T(8,128)(2,1)S(1)} %attend_late.1.late, bf16[192,768]{1,0:T(8,128)(2,1)S(1)} %get-tuple-element.62.refs_0_, bf16[192,768]{1,0:T(8,128)(2,1)S(1)} %collective-permute-done.4.refs_1_, ...), custom_call_target="tpu_custom_call" | custom-call | flops 1 | bytes 2359296 | tf_op jit(solution)/shard_map/outward_send/pallas_call | solution.py:415
  41.2 1.6 %collective-permute-start.15 = (bf16[128,1536]{1,0:T(8,128)(2,1)S(1)}, bf16[128,1536]{1,0:T(8,128)(2,1)S(1)}, u32[]{:S(2)}, u32[]{:S(2)}) collective-permute-start(bf16[128,1536]{1,0:T(8,128)(2,1)S(1)} %outward_send.1), channel_id=1, source_target_pairs={{0,1},{1,0},{2,3},{3,2},{4,5},{5,4},{6,7},{7,6},{8,9},{9,8},{10,11... | collective-permute-start | bytes 1179656 | tf_op jit(solution)/shard_map/ppermute | solution.py:717
  42.8 1.2 %outward_keep.1 = (f32[128,1536]{1,0:T(8,128)S(1)}, f32[1,1536]{1,0:T(1,128)S(1)}) custom-call(bf16[128,768]{1,0:T(8,128)(2,1)S(1)} %attend_early.1.early, bf16[128,768]{1,0:T(8,128)(2,1)S(1)} %attend_late.1.late, bf16[128,1536]{1,0:T(8,128)(2,1)S(1)} %copy-done.1, f32[1536]{0:T(1024)S(1)} %copy-done.4, bf16[192,768]{1,0:T(8,128)(2,1)S(1)} %get-tuple-element.62.refs_0_, ...), custom_call_target="tpu_custom_call" | custom-call | flops 1 | bytes 2359296 | tf_op jit(solution)/shard_map/outward_keep/pallas_call | solution.py:429
  44.0 2.6 %collective-permute-done.16.refs_3_ = bf16[576,512]{1,0:T(8,128)(2,1)S(1)} collective-permute-done((bf16[576,512]{1,0:T(8,128)(2,1)}, bf16[576,512]{1,0:T(8,128)(2,1)S(1)}, u32[]{:S(2)}, u32[]{:S(2)}) %collective-permute-start.16) | collective-permute-done | bytes 589856 | tf_op jit(solution)/shard_map/ppermute | solution.py:70
  47.3 2.3 %collective-permute-start.17 = (bf16[288,512]{1,0:T(8,128)(2,1)}, bf16[288,512]{1,0:T(8,128)(2,1)}, u32[]{:S(2)}, u32[]{:S(2)}) collective-permute-start(bf16[288,512]{1,0:T(8,128)(2,1)} %slice.7), channel_id=1, source_target_pairs={{0,8},{2,6},{8,16},{10,2},{16,24},{18,10},{24,28},{26,18},{28,20},... | collective-permute-start | bytes 884744 | tf_op jit(solution)/shard_map/ppermute | solution.py:70
  50.0 4.3 %all-to-all-start = ((bf16[16,144,128]{2,1,0:T(8,128)(2,1)}), bf16[16,144,128]{2,1,0:T(8,128)(2,1)S(1)}, u32[]{:S(2)}, u32[]{:S(2)}) async-start(bf16[16,144,128]{2,1,0:T(8,128)(2,1)} %bundle.1), calls=%async_computation | async-start | bytes 1179648 | tf_op jit(solution)/shard_map/all_to_all | solution.py:726
  54.8 1.6 %collective-permute-start.18 = (bf16[32,1536]{1,0:T(8,128)(2,1)S(1)}, bf16[32,1536]{1,0:T(8,128)(2,1)S(1)}, u32[]{:S(2)}, u32[]{:S(2)}) collective-permute-start(bf16[32,1536]{1,0:T(8,128)(2,1)S(1)} %get-tuple-element.109), channel_id=1, source_target_pairs={{0,1},{1,0},{2,3},{3,2},{4,5},{5,4},{6,7},{7,6},{8,9},{9,8},{10,11... | collective-permute-start | bytes 294920 | tf_op jit(solution)/shard_map/ppermute | solution.py:729
  56.8 3.2 %collective-permute-done.18.other = bf16[32,1536]{1,0:T(8,128)(2,1)S(1)} collective-permute-done((bf16[32,1536]{1,0:T(8,128)(2,1)S(1)}, bf16[32,1536]{1,0:T(8,128)(2,1)S(1)}, u32[]{:S(2)}, u32[]{:S(2)}) %collective-permute-start.18) | collective-permute-done | bytes 98336 | tf_op jit(solution)/shard_map/ppermute | solution.py:729
  60.0 1.8 %collective-permute-done.22.refs_8_ = bf16[288,512]{1,0:T(8,128)(2,1)S(1)} collective-permute-done((bf16[288,512]{1,0:T(8,128)(2,1)}, bf16[288,512]{1,0:T(8,128)(2,1)S(1)}, u32[]{:S(2)}, u32[]{:S(2)}) %collective-permute-start.22) | collective-permute-done | bytes 294944 | tf_op jit(solution)/shard_map/ppermute | solution.py:79
  61.8 3.2 %expert.1 = (bf16[32,1536]{1,0:T(8,128)(2,1)S(1)}, bf16[32,1536]{1,0:T(8,128)(2,1)S(1)}) custom-call(bf16[32,1536]{1,0:T(8,128)(2,1)S(1)} %get-tuple-element.111.own, bf16[32,1536]{1,0:T(8,128)(2,1)S(1)} %collective-permute-done.18.other, bf16[576,512]{1,0:T(8,128)(2,1)S(1)} %get-tuple-element.61.refs_0_, bf16[576,512]{1,0:T(8,128)(2,1)} %collective-permute-done.3.refs_1_, ...), custom_call_target="tpu_custom_call" | custom-call | flops 5980000256 | bytes 41600000 | tf_op jit(solution)/shard_map/expert/pallas_call | solution.py:530
  65.0 1.6 %collective-permute-start.23 = (bf16[32,1536]{1,0:T(8,128)(2,1)S(1)}, bf16[32,1536]{1,0:T(8,128)(2,1)S(1)}, u32[]{:S(2)}, u32[]{:S(2)}) collective-permute-start(bf16[32,1536]{1,0:T(8,128)(2,1)S(1)} %get-tuple-element.115), channel_id=1, source_target_pairs={{0,1},{1,0},{2,3},{3,2},{4,5},{5,4},{6,7},{7,6},{8,9},{9,8},{10,11... | collective-permute-start | bytes 294920 | tf_op jit(solution)/shard_map/ppermute | solution.py:736
  66.5 3.4 %collective-permute-done.23.returned = bf16[32,1536]{1,0:T(8,128)(2,1)S(1)} collective-permute-done((bf16[32,1536]{1,0:T(8,128)(2,1)S(1)}, bf16[32,1536]{1,0:T(8,128)(2,1)S(1)}, u32[]{:S(2)}, u32[]{:S(2)}) %collective-permute-start.23) | collective-permute-done | bytes 98336 | tf_op jit(solution)/shard_map/ppermute | solution.py:736
  71.0 1.6 %write.1 = bf16[2048,128]{1,0:T(8,128)(2,1)} custom-call(bf16[16,144,128]{2,1,0:T(8,128)(2,1)S(1)} %all-to-all-done.arrived, bf16[2048,128]{1,0:T(8,128)(2,1)S(1)} %bitcast.14), custom_call_target="tpu_custom_call" | custom-call | flops 1 | bytes 2097152 | tf_op jit(solution)/shard_map/write/pallas_call | solution.py:636
  (46 shorter events, 5.4 us)
Async XLA Ops:
  0.6 3.6 %collective-permute-start.2 = (bf16[96,1536]{1,0:T(8,128)(2,1)}, bf16[96,1536]{1,0:T(8,128)(2,1)S(1)}, u32[]{:S(2)}, u32[]{:S(2)}) collective-permute-start(bf16[96,1536]{1,0:T(8,128)(2,1)} %bitcast.20), channel_id=1, source_target_pairs={{0,2},{2,0},{4,6},{6,4},{8,10},{10,8},{12,14},{14,12},{16,18},{18,... | collective-permute-start | bytes 884744 | tf_op jit(solution)/shard_map/ppermute | solution.py:681
  1.1 3.1 %collective-permute-start = (bf16[96,1024]{1,0:T(8,128)(2,1)}, bf16[96,1024]{1,0:T(8,128)(2,1)S(1)}, u32[]{:S(2)}, u32[]{:S(2)}) collective-permute-start(bf16[96,1024]{1,0:T(8,128)(2,1)} %bitcast.22), channel_id=1, source_target_pairs={{0,2},{2,0},{4,6},{6,4},{8,10},{10,8},{12,14},{14,12},{16,18},{18,... | collective-permute-start | bytes 589832 | tf_op jit(solution)/shard_map/ppermute | solution.py:681
  1.2 3.0 %collective-permute-start.1 = (bf16[32,1536]{1,0:T(8,128)(2,1)}, bf16[32,1536]{1,0:T(8,128)(2,1)S(1)}, u32[]{:S(2)}, u32[]{:S(2)}) collective-permute-start(bf16[32,1536]{1,0:T(8,128)(2,1)} %bitcast.24), channel_id=1, source_target_pairs={{0,2},{2,0},{4,6},{6,4},{8,10},{10,8},{12,14},{14,12},{16,18},{18,... | collective-permute-start | bytes 294920 | tf_op jit(solution)/shard_map/ppermute | solution.py:681
  1.7 12.5 %collective-permute-start.5 = (bf16[128,1536]{1,0:T(8,128)(2,1)}, bf16[128,1536]{1,0:T(8,128)(2,1)S(1)}, u32[]{:S(2)}, u32[]{:S(2)}) collective-permute-start(bf16[128,1536]{1,0:T(8,128)(2,1)} %tokens.1), channel_id=1, source_target_pairs={{0,1},{1,0},{2,3},{3,2},{4,5},{5,4},{6,7},{7,6},{8,9},{9,8},{10,11... | collective-permute-start | bytes 1179656 | tf_op jit(solution)/shard_map/ppermute | solution.py:678
  5.4 8.8 %collective-permute-start.4 = (bf16[192,768]{1,0:T(8,128)(2,1)S(1)}, bf16[192,768]{1,0:T(8,128)(2,1)S(1)}, u32[]{:S(2)}, u32[]{:S(2)}) collective-permute-start(bf16[192,768]{1,0:T(8,128)(2,1)S(1)} %get-tuple-element.62.refs_0_), channel_id=1, source_target_pairs={{0,8},{2,6},{8,16},{10,2},{16,24},{18,10},{24,28},{26,18},{28,20},... | collective-permute-start | bytes 884744 | tf_op jit(solution)/shard_map/ppermute | solution.py:70
  7.1 17.5 %collective-permute-start.3 = (bf16[576,512]{1,0:T(8,128)(2,1)S(1)}, bf16[576,512]{1,0:T(8,128)(2,1)}, u32[]{:S(2)}, u32[]{:S(2)}) collective-permute-start(bf16[576,512]{1,0:T(8,128)(2,1)S(1)} %get-tuple-element.61.refs_0_), channel_id=1, source_target_pairs={{0,8},{2,6},{8,16},{10,2},{16,24},{18,10},{24,28},{26,18},{28,20},... | collective-permute-start | bytes 1769480 | tf_op jit(solution)/shard_map/ppermute | solution.py:70
  10.2 5.8 %copy-start.1 = (bf16[128,1536]{1,0:T(8,128)(2,1)S(1)}, bf16[128,1536]{1,0:T(8,128)(2,1)}, u32[]{:S(2)}) copy-start(bf16[128,1536]{1,0:T(8,128)(2,1)} %tokens.1) | copy-start | bytes 1179652
  10.2 5.8 %copy-start.5 = (bf16[1536,768]{1,0:T(8,128)(2,1)S(1)}, bf16[1536,768]{1,0:T(8,128)(2,1)}, u32[]{:S(2)}) copy-start(bf16[1536,768]{1,0:T(8,128)(2,1)} %w_query.1) | copy-start | bytes 7077892
  14.1 7.5 %collective-permute-start.7 = (bf16[192,768]{1,0:T(8,128)(2,1)S(1)}, bf16[192,768]{1,0:T(8,128)(2,1)S(1)}, u32[]{:S(2)}, u32[]{:S(2)}) collective-permute-start(bf16[192,768]{1,0:T(8,128)(2,1)S(1)} %collective-permute-done.4.refs_1_), channel_id=1, source_target_pairs={{0,8},{2,6},{8,16},{10,2},{16,24},{18,10},{24,28},{26,18},{28,20},... | collective-permute-start | bytes 884744 | tf_op jit(solution)/shard_map/ppermute | solution.py:70
  16.0 12.5 %collective-permute-start.10 = (bf16[192,768]{1,0:T(8,128)(2,1)S(1)}, bf16[192,768]{1,0:T(8,128)(2,1)S(1)}, u32[]{:S(2)}, u32[]{:S(2)}) collective-permute-start(bf16[192,768]{1,0:T(8,128)(2,1)S(1)} %collective-permute-done.4.refs_1_), channel_id=1, source_target_pairs={{0,2},{2,0},{4,6},{6,4},{8,10},{10,8},{12,14},{14,12},{16,18},{18,... | collective-permute-start | bytes 884744 | tf_op jit(solution)/shard_map/ppermute | solution.py:79
  18.2 6.4 %collective-permute-start.6 = (bf16[128,512]{1,0:T(8,128)(2,1)S(1)}, bf16[128,512]{1,0:T(8,128)(2,1)S(1)}, u32[]{:S(2)}, u32[]{:S(2)}) collective-permute-start(bf16[128,512]{1,0:T(8,128)(2,1)S(1)} %get-tuple-element.71), channel_id=1, source_target_pairs={{0,2},{2,4},{4,6},{6,8},{8,10},{10,12},{12,14},{14,16},{16,18},{18... | collective-permute-start | bytes 393224 | tf_op jit(solution)/shard_map/ppermute | solution.py:696
  21.6 6.8 %collective-permute-start.11 = (bf16[192,768]{1,0:T(8,128)(2,1)S(1)}, bf16[192,768]{1,0:T(8,128)(2,1)S(1)}, u32[]{:S(2)}, u32[]{:S(2)}) collective-permute-start(bf16[192,768]{1,0:T(8,128)(2,1)S(1)} %collective-permute-done.7.refs_2_), channel_id=1, source_target_pairs={{0,2},{2,0},{4,6},{6,4},{8,10},{10,8},{12,14},{14,12},{16,18},{18,... | collective-permute-start | bytes 884744 | tf_op jit(solution)/shard_map/ppermute | solution.py:79
  21.6 6.8 %collective-permute-start.9 = (bf16[192,768]{1,0:T(8,128)(2,1)S(1)}, bf16[192,768]{1,0:T(8,128)(2,1)S(1)}, u32[]{:S(2)}, u32[]{:S(2)}) collective-permute-start(bf16[192,768]{1,0:T(8,128)(2,1)S(1)} %collective-permute-done.7.refs_2_), channel_id=1, source_target_pairs={{0,8},{2,6},{8,16},{10,2},{16,24},{18,10},{24,28},{26,18},{28,20},... | collective-permute-start | bytes 884744 | tf_op jit(solution)/shard_map/ppermute | solution.py:70
  24.7 11.7 %collective-permute-start.8 = (bf16[576,512]{1,0:T(8,128)(2,1)}, bf16[576,512]{1,0:T(8,128)(2,1)}, u32[]{:S(2)}, u32[]{:S(2)}) collective-permute-start(bf16[576,512]{1,0:T(8,128)(2,1)} %collective-permute-done.3.refs_1_), channel_id=1, source_target_pairs={{0,8},{2,6},{8,16},{10,2},{16,24},{18,10},{24,28},{26,18},{28,20},... | collective-permute-start | bytes 1769480 | tf_op jit(solution)/shard_map/ppermute | solution.py:70
  28.5 1.7 %collective-permute-start.13 = (bf16[192,768]{1,0:T(8,128)(2,1)S(1)}, bf16[192,768]{1,0:T(8,128)(2,1)S(1)}, u32[]{:S(2)}, u32[]{:S(2)}) collective-permute-start(bf16[192,768]{1,0:T(8,128)(2,1)S(1)} %collective-permute-done.9.refs_3_), channel_id=1, source_target_pairs={{0,2},{2,0},{4,6},{6,4},{8,10},{10,8},{12,14},{14,12},{16,18},{18,... | collective-permute-start | bytes 884744 | tf_op jit(solution)/shard_map/ppermute | solution.py:79
  28.6 7.8 %collective-permute-start.12 = (bf16[96,768]{1,0:T(8,128)(2,1)S(1)}, bf16[96,768]{1,0:T(8,128)(2,1)S(1)}, u32[]{:S(2)}, u32[]{:S(2)}) collective-permute-start(bf16[96,768]{1,0:T(8,128)(2,1)S(1)} %slice.6), channel_id=1, source_target_pairs={{0,8},{2,6},{8,16},{10,2},{16,24},{18,10},{24,28},{26,18},{28,20},... | collective-permute-start | bytes 442376 | tf_op jit(solution)/shard_map/ppermute | solution.py:70
  31.6 11.2 %copy-start.4 = (f32[1536]{0:T(1024)S(1)}, f32[1536]{0:T(1024)}, u32[]{:S(2)}) copy-start(f32[1536]{0:T(1024)} %flat_gain.1) | copy-start | bytes 18436
  36.4 10.1 %collective-permute-start.16 = (bf16[576,512]{1,0:T(8,128)(2,1)}, bf16[576,512]{1,0:T(8,128)(2,1)S(1)}, u32[]{:S(2)}, u32[]{:S(2)}) collective-permute-start(bf16[576,512]{1,0:T(8,128)(2,1)} %collective-permute-done.8.refs_2_), channel_id=1, source_target_pairs={{0,8},{2,6},{8,16},{10,2},{16,24},{18,10},{24,28},{26,18},{28,20},... | collective-permute-start | bytes 1769480 | tf_op jit(solution)/shard_map/ppermute | solution.py:70
  38.7 1.4 %collective-permute-start.14 = (bf16[96,768]{1,0:T(8,128)(2,1)S(1)}, bf16[96,768]{1,0:T(8,128)(2,1)S(1)}, u32[]{:S(2)}, u32[]{:S(2)}) collective-permute-start(bf16[96,768]{1,0:T(8,128)(2,1)S(1)} %collective-permute-done.12.refs_7_), channel_id=1, source_target_pairs={{0,2},{2,0},{4,6},{6,4},{8,10},{10,8},{12,14},{14,12},{16,18},{18,... | collective-permute-start | bytes 442376 | tf_op jit(solution)/shard_map/ppermute | solution.py:79
  41.2 13.1 %collective-permute-start.15 = (bf16[128,1536]{1,0:T(8,128)(2,1)S(1)}, bf16[128,1536]{1,0:T(8,128)(2,1)S(1)}, u32[]{:S(2)}, u32[]{:S(2)}) collective-permute-start(bf16[128,1536]{1,0:T(8,128)(2,1)S(1)} %outward_send.1), channel_id=1, source_target_pairs={{0,1},{1,0},{2,3},{3,2},{4,5},{5,4},{6,7},{7,6},{8,9},{9,8},{10,11... | collective-permute-start | bytes 1179656 | tf_op jit(solution)/shard_map/ppermute | solution.py:717
  43.9 12.4 %copy-start.2 = (bf16[1536,40]{0,1:T(8,128)(2,1)S(1)}, bf16[1536,40]{0,1:T(8,128)(2,1)}, u32[]{:S(2)}) copy-start(bf16[1536,40]{0,1:T(8,128)(2,1)} %param.20) | copy-start | bytes 368644
  43.9 12.4 %copy-start.3 = (s32[128,8]{0,1:T(8,128)S(1)}, s32[128,8]{0,1:T(8,128)}, u32[]{:S(2)}) copy-start(s32[128,8]{0,1:T(8,128)} %param.23) | copy-start | bytes 12292
  47.3 12.7 %collective-permute-start.17 = (bf16[288,512]{1,0:T(8,128)(2,1)}, bf16[288,512]{1,0:T(8,128)(2,1)}, u32[]{:S(2)}, u32[]{:S(2)}) collective-permute-start(bf16[288,512]{1,0:T(8,128)(2,1)} %slice.7), channel_id=1, source_target_pairs={{0,8},{2,6},{8,16},{10,2},{16,24},{18,10},{24,28},{26,18},{28,20},... | collective-permute-start | bytes 884744 | tf_op jit(solution)/shard_map/ppermute | solution.py:70
  49.5 10.5 %collective-permute-start.19 = (bf16[576,512]{1,0:T(8,128)(2,1)}, bf16[576,512]{1,0:T(8,128)(2,1)}, u32[]{:S(2)}, u32[]{:S(2)}) collective-permute-start(bf16[576,512]{1,0:T(8,128)(2,1)} %collective-permute-done.3.refs_1_), channel_id=1, source_target_pairs={{0,2},{2,0},{4,6},{6,4},{8,10},{10,8},{12,14},{14,12},{16,18},{18,... | collective-permute-start | bytes 1769480 | tf_op jit(solution)/shard_map/ppermute | solution.py:79
  49.5 10.5 %collective-permute-start.20 = (bf16[576,512]{1,0:T(8,128)(2,1)}, bf16[576,512]{1,0:T(8,128)(2,1)}, u32[]{:S(2)}, u32[]{:S(2)}) collective-permute-start(bf16[576,512]{1,0:T(8,128)(2,1)} %collective-permute-done.8.refs_2_), channel_id=1, source_target_pairs={{0,2},{2,0},{4,6},{6,4},{8,10},{10,8},{12,14},{14,12},{16,18},{18,... | collective-permute-start | bytes 1769480 | tf_op jit(solution)/shard_map/ppermute | solution.py:79
  50.0 11.8 %collective-permute-start.21 = (bf16[576,512]{1,0:T(8,128)(2,1)S(1)}, bf16[576,512]{1,0:T(8,128)(2,1)}, u32[]{:S(2)}, u32[]{:S(2)}) collective-permute-start(bf16[576,512]{1,0:T(8,128)(2,1)S(1)} %collective-permute-done.16.refs_3_), channel_id=1, source_target_pairs={{0,2},{2,0},{4,6},{6,4},{8,10},{10,8},{12,14},{14,12},{16,18},{18,... | collective-permute-start | bytes 1769480 | tf_op jit(solution)/shard_map/ppermute | solution.py:79
  50.0 21.0 %all-to-all-start = ((bf16[16,144,128]{2,1,0:T(8,128)(2,1)}), bf16[16,144,128]{2,1,0:T(8,128)(2,1)S(1)}, u32[]{:S(2)}, u32[]{:S(2)}) async-start(bf16[16,144,128]{2,1,0:T(8,128)(2,1)} %bundle.1), calls=%async_computation | async-start | bytes 1179648 | tf_op jit(solution)/shard_map/all_to_all | solution.py:726
  54.8 5.2 %collective-permute-start.18 = (bf16[32,1536]{1,0:T(8,128)(2,1)S(1)}, bf16[32,1536]{1,0:T(8,128)(2,1)S(1)}, u32[]{:S(2)}, u32[]{:S(2)}) collective-permute-start(bf16[32,1536]{1,0:T(8,128)(2,1)S(1)} %get-tuple-element.109), channel_id=1, source_target_pairs={{0,1},{1,0},{2,3},{3,2},{4,5},{5,4},{6,7},{7,6},{8,9},{9,8},{10,11... | collective-permute-start | bytes 294920 | tf_op jit(solution)/shard_map/ppermute | solution.py:729
  60.0 11.0 %copy-start = (bf16[512,4,128]{2,1,0:T(4,128)(2,1)S(1)}, bf16[512,4,128]{2,1,0:T(4,128)(2,1)}, u32[]{:S(2)}) copy-start(bf16[512,4,128]{2,1,0:T(4,128)(2,1)} %param.25) | copy-start | bytes 1572868
  60.0 1.8 %collective-permute-start.22 = (bf16[288,512]{1,0:T(8,128)(2,1)}, bf16[288,512]{1,0:T(8,128)(2,1)S(1)}, u32[]{:S(2)}, u32[]{:S(2)}) collective-permute-start(bf16[288,512]{1,0:T(8,128)(2,1)} %collective-permute-done.17.refs_7_), channel_id=1, source_target_pairs={{0,2},{2,0},{4,6},{6,4},{8,10},{10,8},{12,14},{14,12},{16,18},{18,... | collective-permute-start | bytes 884744 | tf_op jit(solution)/shard_map/ppermute | solution.py:79
  65.0 4.9 %collective-permute-start.23 = (bf16[32,1536]{1,0:T(8,128)(2,1)S(1)}, bf16[32,1536]{1,0:T(8,128)(2,1)S(1)}, u32[]{:S(2)}, u32[]{:S(2)}) collective-permute-start(bf16[32,1536]{1,0:T(8,128)(2,1)S(1)} %get-tuple-element.115), channel_id=1, source_target_pairs={{0,1},{1,0},{2,3},{3,2},{4,5},{5,4},{6,7},{7,6},{8,9},{9,8},{10,11... | collective-permute-start | bytes 294920 | tf_op jit(solution)/shard_map/ppermute | solution.py:736

commit v13 on v12

--- a/solution.py
+++ b/solution.py
@@ -82,11 +82,22 @@
         full = self.full
         return self.mine[: full + 1] + self.near[:full] + [self.mine[full + 1], self.near[full]]
 
-
-def place_parts(groups, parts, unit_rows, pieces):
+    def split(self):
+        full = self.full
+        listed = [(part, 2 * index) for index, part in enumerate(self.parts()[:-1])]
+        listed.append((self.near[full], 4 * full + 3))
+        late = (full, 2 * full, 2 * full + 1, 2 * full + 2)
+        return (
+            [pair for index, pair in enumerate(listed) if index not in late],
+            [listed[index] for index in late],
+        )
+
+
+def place_parts(groups, parts, unit_rows, pieces, shards=None):
     sources = ring_sources(groups, lax.axis_index("grp"))
     shard = 0
-    for part in parts:
+    for index, part in enumerate(parts):
+        shard = shards[index] if shards else shard
         for unit in range(part.shape[0] // unit_rows):
             for first, rows, target, lane in pieces:
                 at = pl.multiple_of(sources[shard] * rows, rows)
@@ -503,19 +514,45 @@
     )(moe_in, router_t, ids_t, place)
 
 
-def expert_kernel(groups, up_rows, down_rows, n_parts, own, other, *refs):
-    parts = refs[:n_parts]
-    own_out, other_out, rows, gate_up, down = refs[n_parts:]
+def expert_pieces(gate_up, down, up_rows, down_rows, width):
+    pieces = [(i * up_rows, up_rows, gate_up, i * width) for i in range(2)]
+    pieces += [
+        (2 * up_rows + i * down_rows, down_rows, down, i * width) for i in range(down.shape[1] // width)
+    ]
+    return pieces, pieces[-1][0] + down_rows
+
+
+def stage_kernel(groups, up_rows, down_rows, shards, *refs):
+    parts, (gate_up, down) = refs[: len(shards)], refs[len(shards) :]
+    pieces, unit_rows = expert_pieces(gate_up, down, up_rows, down_rows, parts[0].shape[1])
+    place_parts(groups, parts, unit_rows, pieces, shards)
+
+
+def stage(groups, early, up_rows, down_rows, model):
+    width = early[0][0].shape[1]
+    return pl.pallas_call(
+        functools.partial(stage_kernel, groups, up_rows, down_rows, [shard for _, shard in early]),
+        out_shape=(
+            jax.ShapeDtypeStruct((groups * up_rows, 2 * width), bf16),
+            jax.ShapeDtypeStruct((groups * down_rows, model), bf16),
+        ),
+        in_specs=[VMEM] * len(early),
+        out_specs=(VMEM, VMEM),
+        compiler_params=PARAMS,
+        cost_estimate=reads(2 * groups * 2 * (up_rows * 2 * width + down_rows * model)),
+        name="stage",
+    )(*[part for part, _ in early])
+
+
+def expert_kernel(groups, up_rows, down_rows, shards, own, other, gate_up_in, down_in, *refs):
+    parts = refs[: len(shards)]
+    own_out, other_out, gate_up, down, rows = refs[len(shards) :]
     width = parts[0].shape[1]
     count = own.shape[0]
     rows[:count, :] = own[...]
     rows[count:, :] = other[...]
-    pieces = [(i * up_rows, up_rows, gate_up, i * width) for i in range(2)]
-    pieces += [
-        (2 * up_rows + i * down_rows, down_rows, down, i * width) for i in range(down.shape[1] // width)
-    ]
-    unit_rows = pieces[-1][0] + down_rows
-    place_parts(groups, parts, unit_rows, pieces)
+    pieces, unit_rows = expert_pieces(gate_up, down, up_rows, down_rows, width)
+    place_parts(groups, parts, unit_rows, pieces, shards)
     both = jnp.dot(rows[...], gate_up[...], preferred_element_type=f32)
     gate, up = both[:, :width], both[:, width:]
     hidden = (gate / (1.0 + jnp.exp(-gate)) * up).astype(bf16)
@@ -524,23 +561,21 @@
     other_out[...] = made[count:, :]
 
 
-def expert(groups, own, other, parts, up_rows, down_rows):
+def expert(groups, own, other, staged, late, up_rows, down_rows):
     count, model = own.shape
-    width = parts[0].shape[1]
-    return pl.pallas_call(
-        functools.partial(expert_kernel, groups, up_rows, down_rows, len(parts)),
-        out_shape=(jax.ShapeDtypeStruct(own.shape, bf16),) * 2,
-        in_specs=[VMEM] * (2 + len(parts)),
-        out_specs=(VMEM, VMEM),
-        scratch_shapes=[
-            pltpu.VMEM((2 * count, model), bf16),
-            pltpu.VMEM((groups * up_rows, 2 * width), bf16),
-            pltpu.VMEM((groups * down_rows, model), bf16),
-        ],
-        compiler_params=PARAMS,
-        cost_estimate=takes(5.2),
+    width = late[0][0].shape[1]
+    return pl.pallas_call(
+        functools.partial(expert_kernel, groups, up_rows, down_rows, [shard for _, shard in late]),
+        out_shape=(jax.ShapeDtypeStruct(own.shape, bf16),) * 2
+        + tuple(jax.ShapeDtypeStruct(part.shape, bf16) for part in staged),
+        in_specs=[VMEM] * (4 + len(late)),
+        out_specs=(VMEM,) * 4,
+        scratch_shapes=[pltpu.VMEM((2 * count, model), bf16)],
+        input_output_aliases={2: 2, 3: 3},
+        compiler_params=PARAMS,
+        cost_estimate=takes(6.2),
         name="expert",
-    )(own, other, *parts)
+    )(own, other, *staged, *[part for part, _ in late])[:2]
 
 
 def combine_kernel(residual, gates, spread, own, returned, out):
@@ -724,15 +759,18 @@
     expert_ring.step()
     outgoing = together((outgoing, sent))[0]
     arrived_cache = lax.all_to_all(outgoing, "grp", split_axis=0, concat_axis=0, tiled=True)
+    arrived, late_gain = expert_ring.pin(arrived, late_gain)
+    expert_ring.share()
 
     residual, moe_in, sent_rows = route(mine, arrived, late_gain, place)
     landed = swap(sent_rows)
     gates, own_rows, spread = gate(moe_in, router.T, expert_ids.T, place)
-    landed, own_rows = expert_ring.pin(landed, own_rows)
-    expert_ring.share()
-    own_made, back = expert(
-        groups, own_rows, landed, expert_ring.parts(), up_rows, down_rows
-    )
+    parts_early, parts_late = expert_ring.split()
+    first, own_rows = together((parts_early[0][0], own_rows))
+    parts_early[0] = (first, parts_early[0][1])
+    staged = stage(groups, parts_early, up_rows, down_rows, model)
+    landed, staged = together((landed, staged))
+    own_made, back = expert(groups, own_rows, landed, staged, parts_late, up_rows, down_rows)
     returned = swap(back)
     layer_out = combine(residual, gates, spread, own_made, returned)
     layer_out, arrived_cache = together((layer_out, arrived_cache))

time: 72.9 us -> 73 us (level)
  waiting for transfers between devices: 20.2 us -> 14.5 us
  local copies, waits for them, and re-layouts: 2.61 us -> 6.43 us
  Pallas kernels: 18 us -> 19.8 us
    ppermute x1, waiting for transfers between devices: 3.22 us -> 0.02 us  [two_lane_shards(): landed = swap(sent_rows)]
    unnamed x13 -> x17, local copies, waits for them, and re-layouts: 1.87 us -> 4.72 us
    ppermute x8, waiting for transfers between devices: 3.15 us -> 1.39 us  [share(): self.near.append(self.beside(self.mine[index]))]
    pallas_call x0 -> x1, Pallas kernels: none -> 1.47 us  [stage(): pl.pallas_call(functools.partial(stage_kernel, groups, up_rows, down_rows...]
    pallas_call x1, Pallas kernels: 0.42 us -> 1.4 us  [route(): pl.pallas_call(route_kernel, out_shape=(jax.ShapeDtypeStruct(mine.shape,...]
    slice x2, local copies, waits for them, and re-layouts: 0.74 us -> 1.71 us  [step(): held = held[:self.unit_rows]]
  transfers between devices with their start and end apart: 25 -> 25, of which waited for: 8 -> 7; matrix products, arithmetic and copies ran while one was open for 4% -> 5% of each run, Pallas kernels for 23% -> 25%
where the time goes in v13:
time: 73 us; the launch traced here: 72.5 us
  starting transfers between devices  31 us (42%)
  Pallas kernels  19.8 us (27%)
  waiting for transfers between devices  14.5 us (20%)
  local copies, waits for them, and re-layouts  6.43 us (9%)
  between operations  0.9 us (1%)
    ppermute x8, starting transfers between devices, step(): self.mine.append(self.across(held))  15.2 us
    ppermute x8, waiting for transfers between devices, step(): self.mine.append(self.across(held))  7.73 us
    unnamed x17, local copies, waits for them, and re-layouts  4.72 us
    all_to_all x1, starting transfers between devices, two_lane_shards(): lax.all_to_all(outgoing, 'grp', split_axis=0, concat_axis=0, tiled=True)  4.55 us
    ppermute x1, waiting for transfers between devices, two_lane_shards(): returned = swap(back)  3.25 us
    ppermute x1, starting transfers between devices, two_lane_shards(): other_tokens = swap(tokens)  2.56 us
    pallas_call x1, Pallas kernels, expert(): pl.pallas_call(functools.partial(expert_kernel, groups, up_rows, down_row...  2.52 us
    pallas_call x1, Pallas kernels, project(): pl.pallas_call(project_kernel, out_shape=(jax.ShapeDtypeStruct((2 * count...  2.21 us
  transfers between devices with their start and end apart: 25, of which 7 were waited for; matrix products, arithmetic and copies ran while one was open for 5% of the time, Pallas kernels for 25%

profile of v13, /device:TPU:0, one launch (start us, length us, event | category | flops | bytes accessed | tf_op | source)
XLA Modules:
  0.0 72.5 jit_solution(7217607865573447533)
XLA Ops:
  1.7 2.6 %collective-permute-start.5 = (bf16[128,1536]{1,0:T(8,128)(2,1)}, bf16[128,1536]{1,0:T(8,128)(2,1)S(1)}, u32[]{:S(2)}, u32[]{:S(2)}) collective-permute-start(bf16[128,1536]{1,0:T(8,128)(2,1)} %tokens.1), channel_id=1, source_target_pairs={{0,1},{1,0},{2,3},{3,2},{4,5},{5,4},{6,7},{7,6},{8,9},{9,8},{10,11... | collective-permute-start | bytes 1179656 | tf_op jit(solution)/shard_map/ppermute | solution.py:713
  5.4 1.7 %collective-permute-start.4 = (bf16[192,768]{1,0:T(8,128)(2,1)S(1)}, bf16[192,768]{1,0:T(8,128)(2,1)S(1)}, u32[]{:S(2)}, u32[]{:S(2)}) collective-permute-start(bf16[192,768]{1,0:T(8,128)(2,1)S(1)} %get-tuple-element.69.refs_0_), channel_id=1, source_target_pairs={{0,8},{2,6},{8,16},{10,2},{16,24},{18,10},{24,28},{26,18},{28,20},... | collective-permute-start | bytes 884744 | tf_op jit(solution)/shard_map/ppermute | solution.py:70
  7.1 1.6 %collective-permute-start.3 = (bf16[576,512]{1,0:T(8,128)(2,1)S(1)}, bf16[576,512]{1,0:T(8,128)(2,1)S(1)}, u32[]{:S(2)}, u32[]{:S(2)}) collective-permute-start(bf16[576,512]{1,0:T(8,128)(2,1)S(1)} %get-tuple-element.121.refs_0_), channel_id=1, source_target_pairs={{0,8},{2,6},{8,16},{10,2},{16,24},{18,10},{24,28},{26,18},{28,20},... | collective-permute-start | bytes 1769480 | tf_op jit(solution)/shard_map/ppermute | solution.py:70
  8.7 1.5 %prepare.1 = (f32[256,128]{1,0:T(8,128)S(1)}, f32[256,128]{1,0:T(8,128)S(1)}, f32[256,128]{1,0:T(8,128)S(1)}, bf16[64,128]{1,0:T(8,128)(2,1)S(1)}, bf16[512,256]...) custom-call(s32[1,256]{1,0:T(1,128)} %bitcast.26, s32[1,256]{1,0:T(1,128)} %bitcast.27, ...), custom_call_target="tpu_custom_call" | custom-call | flops 1 | bytes 1 | tf_op jit(solution)/shard_map/prepare/pallas_call | solution.py:266
  10.2 1.8 %copy.19 = bf16[192,8,4,128]{3,1,2,0:T(8,128)(2,1)S(1)} copy(bf16[192,8,4,128]{3,2,1,0:T(4,128)(2,1)} %bitcast.18) | data formatting | bytes 3145728
  12.0 2.1 %collective-permute-done.5.other = bf16[128,1536]{1,0:T(8,128)(2,1)S(1)} collective-permute-done((bf16[128,1536]{1,0:T(8,128)(2,1)}, bf16[128,1536]{1,0:T(8,128)(2,1)S(1)}, u32[]{:S(2)}, u32[]{:S(2)}) %collective-permute-start.5) | collective-permute-done | bytes 393248 | tf_op jit(solution)/shard_map/ppermute | solution.py:713
  14.1 1.8 %collective-permute-start.7 = (bf16[192,768]{1,0:T(8,128)(2,1)S(1)}, bf16[192,768]{1,0:T(8,128)(2,1)S(1)}, u32[]{:S(2)}, u32[]{:S(2)}) collective-permute-start(bf16[192,768]{1,0:T(8,128)(2,1)S(1)} %collective-permute-done.4.refs_1_), channel_id=1, source_target_pairs={{0,8},{2,6},{8,16},{10,2},{16,24},{18,10},{24,28},{26,18},{28,20},... | collective-permute-start | bytes 884744 | tf_op jit(solution)/shard_map/ppermute | solution.py:70
  16.0 2.2 %project.1 = (bf16[256,768]{1,0:T(8,128)(2,1)S(1)}, bf16[256,512]{1,0:T(8,128)(2,1)S(1)}, bf16[128,512]{1,0:T(8,128)(2,1)S(1)}) custom-call(bf16[128,1536]{1,0:T(8,128)(2,1)S(1)} %copy-done.1, bf16[128,1536]{1,0:T(8,128)(2,1)S(1)} %collective-permute-done.5.other, f32[1,1536]{1,0:T(1,128)S(1)} %get-tuple-element.74.gain, ...), custom_call_target="tpu_custom_call" | custom-call | flops 9200000000 | bytes 64000000 | tf_op jit(solution)/shard_map/project/pallas_call | solution.py:316
  18.2 2.1 %collective-permute-start.6 = (bf16[128,512]{1,0:T(8,128)(2,1)S(1)}, bf16[128,512]{1,0:T(8,128)(2,1)S(1)}, u32[]{:S(2)}, u32[]{:S(2)}) collective-permute-start(bf16[128,512]{1,0:T(8,128)(2,1)S(1)} %get-tuple-element.78), channel_id=1, source_target_pairs={{0,2},{2,4},{4,6},{6,8},{8,10},{10,12},{12,14},{14,16},{16,18},{18... | collective-permute-start | bytes 393224 | tf_op jit(solution)/shard_map/ppermute | solution.py:731
  20.3 1.3 %collective-permute-done.7.refs_2_ = bf16[192,768]{1,0:T(8,128)(2,1)S(1)} collective-permute-done((bf16[192,768]{1,0:T(8,128)(2,1)S(1)}, bf16[192,768]{1,0:T(8,128)(2,1)S(1)}, u32[]{:S(2)}, u32[]{:S(2)}) %collective-permute-start.7) | collective-permute-done | bytes 294944 | tf_op jit(solution)/shard_map/ppermute | solution.py:70
  21.6 1.7 %collective-permute-start.9 = (bf16[192,768]{1,0:T(8,128)(2,1)S(1)}, bf16[192,768]{1,0:T(8,128)(2,1)S(1)}, u32[]{:S(2)}, u32[]{:S(2)}) collective-permute-start(bf16[192,768]{1,0:T(8,128)(2,1)S(1)} %collective-permute-done.7.refs_2_), channel_id=1, source_target_pairs={{0,8},{2,6},{8,16},{10,2},{16,24},{18,10},{24,28},{26,18},{28,20},... | collective-permute-start | bytes 884744 | tf_op jit(solution)/shard_map/ppermute | solution.py:70
  23.3 1.3 %attend_late.1.late = bf16[128,768]{1,0:T(8,128)(2,1)S(1)} custom-call(bf16[256,768]{1,0:T(8,128)(2,1)S(1)} %get-tuple-element.81.q, bf16[256,512]{1,0:T(8,128)(2,1)S(1)} %get-tuple-element.95.kv, f32[256,128]{1,0:T(8,128)S(1)} %get-tuple-element.83.past), custom_call_target="tpu_custom_call" | custom-call | flops 2300000000 | bytes 16000000 | tf_op jit(solution)/shard_map/attend_late/pallas_call | solution.py:372
  24.7 2.3 %collective-permute-start.8 = (bf16[576,512]{1,0:T(8,128)(2,1)S(1)}, bf16[576,512]{1,0:T(8,128)(2,1)S(1)}, u32[]{:S(2)}, u32[]{:S(2)}) collective-permute-start(bf16[576,512]{1,0:T(8,128)(2,1)S(1)} %collective-permute-done.3.refs_1_), channel_id=1, source_target_pairs={{0,8},{2,6},{8,16},{10,2},{16,24},{18,10},{24,28},{26,18},{28,20},... | collective-permute-start | bytes 1769480 | tf_op jit(solution)/shard_map/ppermute | solution.py:70
  27.0 1.5 %attend_early.1.early = bf16[128,768]{1,0:T(8,128)(2,1)S(1)} custom-call(bf16[256,768]{1,0:T(8,128)(2,1)S(1)} %get-tuple-element.81.q, bf16[256,512]{1,0:T(8,128)(2,1)S(1)} %get-tuple-element.95.kv, bf16[128,512]{1,0:T(8,128)(2,1)S(1)} %collective-permute-done.6.seam, f32[256,128]{1,0:T(8,128)S(1)} %get-tuple-element.83.past), custom_call_target="tpu_custom_call" | custom-call | flops 2300000000 | bytes 16000000 | tf_op jit(solution)/shard_map/attend_early/pallas_call | solution.py:384
  28.6 1.6 %collective-permute-start.12 = (bf16[96,768]{1,0:T(8,128)(2,1)S(1)}, bf16[96,768]{1,0:T(8,128)(2,1)S(1)}, u32[]{:S(2)}, u32[]{:S(2)}) collective-permute-start(bf16[96,768]{1,0:T(8,128)(2,1)S(1)} %slice.6), channel_id=1, source_target_pairs={{0,8},{2,6},{8,16},{10,2},{16,24},{18,10},{24,28},{26,18},{28,20},... | collective-permute-start | bytes 442376 | tf_op jit(solution)/shard_map/ppermute | solution.py:70
  30.2 1.4 %bundle.1 = bf16[16,144,128]{2,1,0:T(8,128)(2,1)} custom-call(bf16[512,256]{1,0:T(8,128)(2,1)S(1)} %get-tuple-element.94.send, bf16[256,512]{1,0:T(8,128)(2,1)S(1)} %get-tuple-element.95.kv, bf16[256,128]{1,0:T(8,128)(2,1)S(1)} %get-tuple-element.96.tags), custom_call_target="tpu_custom_call" | custom-call | flops 1 | bytes 1 | tf_op jit(solution)/shard_map/bundle/pallas_call | solution.py:630
  31.6 4.7 %collective-permute-done.12.refs_7_ = bf16[96,768]{1,0:T(8,128)(2,1)S(1)} collective-permute-done((bf16[96,768]{1,0:T(8,128)(2,1)S(1)}, bf16[96,768]{1,0:T(8,128)(2,1)S(1)}, u32[]{:S(2)}, u32[]{:S(2)}) %collective-permute-start.12) | collective-permute-done | bytes 147488 | tf_op jit(solution)/shard_map/ppermute | solution.py:70
  36.3 2.2 %collective-permute-start.15 = (bf16[576,512]{1,0:T(8,128)(2,1)S(1)}, bf16[576,512]{1,0:T(8,128)(2,1)}, u32[]{:S(2)}, u32[]{:S(2)}) collective-permute-start(bf16[576,512]{1,0:T(8,128)(2,1)S(1)} %collective-permute-done.8.refs_2_), channel_id=1, source_target_pairs={{0,8},{2,6},{8,16},{10,2},{16,24},{18,10},{24,28},{26,18},{28,20},... | collective-permute-start | bytes 1769480 | tf_op jit(solution)/shard_map/ppermute | solution.py:70
  38.5 1.4 %collective-permute-done.14.refs_8_ = bf16[96,768]{1,0:T(8,128)(2,1)S(1)} collective-permute-done((bf16[96,768]{1,0:T(8,128)(2,1)S(1)}, bf16[96,768]{1,0:T(8,128)(2,1)S(1)}, u32[]{:S(2)}, u32[]{:S(2)}) %collective-permute-start.14) | collective-permute-done | bytes 147488 | tf_op jit(solution)/shard_map/ppermute | solution.py:79
  39.8 1.2 %outward_send.1 = bf16[128,1536]{1,0:T(8,128)(2,1)S(1)} custom-call(bf16[128,768]{1,0:T(8,128)(2,1)S(1)} %attend_early.1.early, bf16[128,768]{1,0:T(8,128)(2,1)S(1)} %attend_late.1.late, bf16[192,768]{1,0:T(8,128)(2,1)S(1)} %get-tuple-element.69.refs_0_, bf16[192,768]{1,0:T(8,128)(2,1)S(1)} %collective-permute-done.4.refs_1_, ...), custom_call_target="tpu_custom_call" | custom-call | flops 1 | bytes 2359296 | tf_op jit(solution)/shard_map/outward_send/pallas_call | solution.py:426
  41.0 1.6 %collective-permute-start.17 = (bf16[128,1536]{1,0:T(8,128)(2,1)S(1)}, bf16[128,1536]{1,0:T(8,128)(2,1)}, u32[]{:S(2)}, u32[]{:S(2)}) collective-permute-start(bf16[128,1536]{1,0:T(8,128)(2,1)S(1)} %outward_send.1), channel_id=1, source_target_pairs={{0,1},{1,0},{2,3},{3,2},{4,5},{5,4},{6,7},{7,6},{8,9},{9,8},{10,11... | collective-permute-start | bytes 1179656 | tf_op jit(solution)/shard_map/ppermute | solution.py:752
  44.8 1.5 %collective-permute-done.15.refs_0_ = bf16[576,512]{1,0:T(8,128)(2,1)} collective-permute-done((bf16[576,512]{1,0:T(8,128)(2,1)S(1)}, bf16[576,512]{1,0:T(8,128)(2,1)}, u32[]{:S(2)}, u32[]{:S(2)}) %collective-permute-start.15) | collective-permute-done | bytes 589856 | tf_op jit(solution)/shard_map/ppermute | solution.py:70
  46.3 1.7 %slice.7 = bf16[288,512]{1,0:T(8,128)(2,1)} slice(bf16[576,512]{1,0:T(8,128)(2,1)} %collective-permute-done.15.refs_0_), slice={[0:288], [0:512]} | slice | bytes 589824 | tf_op jit(solution)/shard_map/slice | solution.py:69
  48.0 2.2 %collective-permute-start.16 = (bf16[288,512]{1,0:T(8,128)(2,1)}, bf16[288,512]{1,0:T(8,128)(2,1)}, u32[]{:S(2)}, u32[]{:S(2)}) collective-permute-start(bf16[288,512]{1,0:T(8,128)(2,1)} %slice.7), channel_id=1, source_target_pairs={{0,8},{2,6},{8,16},{10,2},{16,24},{18,10},{24,28},{26,18},{28,20},... | collective-permute-start | bytes 884744 | tf_op jit(solution)/shard_map/ppermute | solution.py:70
  50.1 4.6 %all-to-all-start = ((bf16[16,144,128]{2,1,0:T(8,128)(2,1)}), bf16[16,144,128]{2,1,0:T(8,128)(2,1)S(1)}, u32[]{:S(2)}, u32[]{:S(2)}) async-start(bf16[16,144,128]{2,1,0:T(8,128)(2,1)} %bundle.1), calls=%async_computation | async-start | bytes 1179648 | tf_op jit(solution)/shard_map/all_to_all | solution.py:761
  55.9 1.4 %route.1 = (bf16[128,1536]{1,0:T(8,128)(2,1)S(1)}, bf16[128,1536]{1,0:T(8,128)(2,1)S(1)}, bf16[32,1536]{1,0:T(8,128)(2,1)S(1)}) custom-call(f32[128,1536]{1,0:T(8,128)S(1)} %get-tuple-element.106.mine, bf16[128,1536]{1,0:T(8,128)(2,1)} %collective-permute-done.17.arrived, f32[1,1536]{1,0:T(1,128)S(1)} %copy-done.6, bf16[64,128]{1,0:T(8,128)(2,1)S(1)} %get-tuple-element.113.place), custom_call_target="tpu_custom_call" | custom-call | flops 1 | bytes 1966080 | tf_op jit(solution)/shard_map/route/pallas_call | solution.py:469
  57.3 1.6 %collective-permute-start.18 = (bf16[32,1536]{1,0:T(8,128)(2,1)S(1)}, bf16[32,1536]{1,0:T(8,128)(2,1)S(1)}, u32[]{:S(2)}, u32[]{:S(2)}) collective-permute-start(bf16[32,1536]{1,0:T(8,128)(2,1)S(1)} %get-tuple-element.120), channel_id=1, source_target_pairs={{0,1},{1,0},{2,3},{3,2},{4,5},{5,4},{6,7},{7,6},{8,9},{9,8},{10,11... | collective-permute-start | bytes 294920 | tf_op jit(solution)/shard_map/ppermute | solution.py:766
  60.9 1.5 %stage.1 = (bf16[1536,1024]{1,0:T(8,128)(2,1)S(1)}, bf16[512,1536]{1,0:T(8,128)(2,1)S(1)}) custom-call(bf16[576,512]{1,0:T(8,128)(2,1)S(1)} %get-tuple-element.121.refs_0_, bf16[576,512]{1,0:T(8,128)(2,1)S(1)} %collective-permute-done.3.refs_1_, bf16[576,512]{1,0:T(8,128)(2,1)S(1)} %collective-permute-done.8.refs_2_, ...), custom_call_target="tpu_custom_call" | custom-call | flops 1 | bytes 9437184 | tf_op jit(solution)/shard_map/stage/pallas_call | solution.py:533
  62.4 2.5 %expert.1 = (bf16[32,1536]{1,0:T(8,128)(2,1)S(1)}, bf16[32,1536]{1,0:T(8,128)(2,1)S(1)}, bf16[1536,1024]{1,0:T(8,128)(2,1)S(1)}, bf16[512,1536]{1,0:T(8,128)(2,1)S(1)}) custom-call(bf16[32,1536]{1,0:T(8,128)(2,1)S(1)} %get-tuple-element.119.own, bf16[32,1536]{1,0:T(8,128)(2,1)S(1)} %collective-permute-done.18.other, ...), custom_call_target="tpu_custom_call", output_to_operand_aliasing={{2}: (2, {}), {3}: (3, {})} | custom-call | flops 7129999872 | bytes 49600000 | tf_op jit(solution)/shard_map/expert/pallas_call | solution.py:567
  64.9 1.7 %collective-permute-start.23 = (bf16[32,1536]{1,0:T(8,128)(2,1)S(1)}, bf16[32,1536]{1,0:T(8,128)(2,1)S(1)}, u32[]{:S(2)}, u32[]{:S(2)}) collective-permute-start(bf16[32,1536]{1,0:T(8,128)(2,1)S(1)} %get-tuple-element.129), channel_id=1, source_target_pairs={{0,1},{1,0},{2,3},{3,2},{4,5},{5,4},{6,7},{7,6},{8,9},{9,8},{10,11... | collective-permute-start | bytes 294920 | tf_op jit(solution)/shard_map/ppermute | solution.py:774
  66.6 3.3 %collective-permute-done.23.returned = bf16[32,1536]{1,0:T(8,128)(2,1)S(1)} collective-permute-done((bf16[32,1536]{1,0:T(8,128)(2,1)S(1)}, bf16[32,1536]{1,0:T(8,128)(2,1)S(1)}, u32[]{:S(2)}, u32[]{:S(2)}) %collective-permute-start.23) | collective-permute-done | bytes 98336 | tf_op jit(solution)/shard_map/ppermute | solution.py:774
  71.0 1.5 %write.1 = bf16[2048,128]{1,0:T(8,128)(2,1)} custom-call(bf16[16,144,128]{2,1,0:T(8,128)(2,1)S(1)} %all-to-all-done.arrived, bf16[2048,128]{1,0:T(8,128)(2,1)S(1)} %bitcast.14), custom_call_target="tpu_custom_call" | custom-call | flops 1 | bytes 2097152 | tf_op jit(solution)/shard_map/write/pallas_call | solution.py:671
  (51 shorter events, 8.9 us)
Async XLA Ops:
  0.6 3.6 %collective-permute-start.2 = (bf16[96,1536]{1,0:T(8,128)(2,1)}, bf16[96,1536]{1,0:T(8,128)(2,1)S(1)}, u32[]{:S(2)}, u32[]{:S(2)}) collective-permute-start(bf16[96,1536]{1,0:T(8,128)(2,1)} %bitcast.20), channel_id=1, source_target_pairs={{0,2},{2,0},{4,6},{6,4},{8,10},{10,8},{12,14},{14,12},{16,18},{18,... | collective-permute-start | bytes 884744 | tf_op jit(solution)/shard_map/ppermute | solution.py:716
  1.1 3.1 %collective-permute-start = (bf16[96,1024]{1,0:T(8,128)(2,1)}, bf16[96,1024]{1,0:T(8,128)(2,1)S(1)}, u32[]{:S(2)}, u32[]{:S(2)}) collective-permute-start(bf16[96,1024]{1,0:T(8,128)(2,1)} %bitcast.22), channel_id=1, source_target_pairs={{0,2},{2,0},{4,6},{6,4},{8,10},{10,8},{12,14},{14,12},{16,18},{18,... | collective-permute-start | bytes 589832 | tf_op jit(solution)/shard_map/ppermute | solution.py:716
  1.2 3.0 %collective-permute-start.1 = (bf16[32,1536]{1,0:T(8,128)(2,1)}, bf16[32,1536]{1,0:T(8,128)(2,1)S(1)}, u32[]{:S(2)}, u32[]{:S(2)}) collective-permute-start(bf16[32,1536]{1,0:T(8,128)(2,1)} %bitcast.24), channel_id=1, source_target_pairs={{0,2},{2,0},{4,6},{6,4},{8,10},{10,8},{12,14},{14,12},{16,18},{18,... | collective-permute-start | bytes 294920 | tf_op jit(solution)/shard_map/ppermute | solution.py:716
  1.7 12.5 %collective-permute-start.5 = (bf16[128,1536]{1,0:T(8,128)(2,1)}, bf16[128,1536]{1,0:T(8,128)(2,1)S(1)}, u32[]{:S(2)}, u32[]{:S(2)}) collective-permute-start(bf16[128,1536]{1,0:T(8,128)(2,1)} %tokens.1), channel_id=1, source_target_pairs={{0,1},{1,0},{2,3},{3,2},{4,5},{5,4},{6,7},{7,6},{8,9},{9,8},{10,11... | collective-permute-start | bytes 1179656 | tf_op jit(solution)/shard_map/ppermute | solution.py:713
  5.4 8.8 %collective-permute-start.4 = (bf16[192,768]{1,0:T(8,128)(2,1)S(1)}, bf16[192,768]{1,0:T(8,128)(2,1)S(1)}, u32[]{:S(2)}, u32[]{:S(2)}) collective-permute-start(bf16[192,768]{1,0:T(8,128)(2,1)S(1)} %get-tuple-element.69.refs_0_), channel_id=1, source_target_pairs={{0,8},{2,6},{8,16},{10,2},{16,24},{18,10},{24,28},{26,18},{28,20},... | collective-permute-start | bytes 884744 | tf_op jit(solution)/shard_map/ppermute | solution.py:70
  7.1 17.5 %collective-permute-start.3 = (bf16[576,512]{1,0:T(8,128)(2,1)S(1)}, bf16[576,512]{1,0:T(8,128)(2,1)S(1)}, u32[]{:S(2)}, u32[]{:S(2)}) collective-permute-start(bf16[576,512]{1,0:T(8,128)(2,1)S(1)} %get-tuple-element.121.refs_0_), channel_id=1, source_target_pairs={{0,8},{2,6},{8,16},{10,2},{16,24},{18,10},{24,28},{26,18},{28,20},... | collective-permute-start | bytes 1769480 | tf_op jit(solution)/shard_map/ppermute | solution.py:70
  10.2 5.8 %copy-start.1 = (bf16[128,1536]{1,0:T(8,128)(2,1)S(1)}, bf16[128,1536]{1,0:T(8,128)(2,1)}, u32[]{:S(2)}) copy-start(bf16[128,1536]{1,0:T(8,128)(2,1)} %tokens.1) | copy-start | bytes 1179652
  10.2 5.8 %copy-start.7 = (bf16[1536,768]{1,0:T(8,128)(2,1)S(1)}, bf16[1536,768]{1,0:T(8,128)(2,1)}, u32[]{:S(2)}) copy-start(bf16[1536,768]{1,0:T(8,128)(2,1)} %w_query.1) | copy-start | bytes 7077892
  14.1 14.3 %collective-permute-start.10 = (bf16[192,768]{1,0:T(8,128)(2,1)S(1)}, bf16[192,768]{1,0:T(8,128)(2,1)S(1)}, u32[]{:S(2)}, u32[]{:S(2)}) collective-permute-start(bf16[192,768]{1,0:T(8,128)(2,1)S(1)} %collective-permute-done.4.refs_1_), channel_id=1, source_target_pairs={{0,2},{2,0},{4,6},{6,4},{8,10},{10,8},{12,14},{14,12},{16,18},{18,... | collective-permute-start | bytes 884744 | tf_op jit(solution)/shard_map/ppermute | solution.py:79
  14.1 7.5 %collective-permute-start.7 = (bf16[192,768]{1,0:T(8,128)(2,1)S(1)}, bf16[192,768]{1,0:T(8,128)(2,1)S(1)}, u32[]{:S(2)}, u32[]{:S(2)}) collective-permute-start(bf16[192,768]{1,0:T(8,128)(2,1)S(1)} %collective-permute-done.4.refs_1_), channel_id=1, source_target_pairs={{0,8},{2,6},{8,16},{10,2},{16,24},{18,10},{24,28},{26,18},{28,20},... | collective-permute-start | bytes 884744 | tf_op jit(solution)/shard_map/ppermute | solution.py:70
  18.2 6.5 %collective-permute-start.6 = (bf16[128,512]{1,0:T(8,128)(2,1)S(1)}, bf16[128,512]{1,0:T(8,128)(2,1)S(1)}, u32[]{:S(2)}, u32[]{:S(2)}) collective-permute-start(bf16[128,512]{1,0:T(8,128)(2,1)S(1)} %get-tuple-element.78), channel_id=1, source_target_pairs={{0,2},{2,4},{4,6},{6,8},{8,10},{10,12},{12,14},{14,16},{16,18},{18... | collective-permute-start | bytes 393224 | tf_op jit(solution)/shard_map/ppermute | solution.py:731
  21.6 6.8 %collective-permute-start.11 = (bf16[192,768]{1,0:T(8,128)(2,1)S(1)}, bf16[192,768]{1,0:T(8,128)(2,1)S(1)}, u32[]{:S(2)}, u32[]{:S(2)}) collective-permute-start(bf16[192,768]{1,0:T(8,128)(2,1)S(1)} %collective-permute-done.7.refs_2_), channel_id=1, source_target_pairs={{0,2},{2,0},{4,6},{6,4},{8,10},{10,8},{12,14},{14,12},{16,18},{18,... | collective-permute-start | bytes 884744 | tf_op jit(solution)/shard_map/ppermute | solution.py:79
  21.6 6.8 %collective-permute-start.9 = (bf16[192,768]{1,0:T(8,128)(2,1)S(1)}, bf16[192,768]{1,0:T(8,128)(2,1)S(1)}, u32[]{:S(2)}, u32[]{:S(2)}) collective-permute-start(bf16[192,768]{1,0:T(8,128)(2,1)S(1)} %collective-permute-done.7.refs_2_), channel_id=1, source_target_pairs={{0,8},{2,6},{8,16},{10,2},{16,24},{18,10},{24,28},{26,18},{28,20},... | collective-permute-start | bytes 884744 | tf_op jit(solution)/shard_map/ppermute | solution.py:70
  24.7 11.6 %collective-permute-start.8 = (bf16[576,512]{1,0:T(8,128)(2,1)S(1)}, bf16[576,512]{1,0:T(8,128)(2,1)S(1)}, u32[]{:S(2)}, u32[]{:S(2)}) collective-permute-start(bf16[576,512]{1,0:T(8,128)(2,1)S(1)} %collective-permute-done.3.refs_1_), channel_id=1, source_target_pairs={{0,8},{2,6},{8,16},{10,2},{16,24},{18,10},{24,28},{26,18},{28,20},... | collective-permute-start | bytes 1769480 | tf_op jit(solution)/shard_map/ppermute | solution.py:70
  28.5 1.7 %collective-permute-start.13 = (bf16[192,768]{1,0:T(8,128)(2,1)S(1)}, bf16[192,768]{1,0:T(8,128)(2,1)S(1)}, u32[]{:S(2)}, u32[]{:S(2)}) collective-permute-start(bf16[192,768]{1,0:T(8,128)(2,1)S(1)} %collective-permute-done.9.refs_3_), channel_id=1, source_target_pairs={{0,2},{2,0},{4,6},{6,4},{8,10},{10,8},{12,14},{14,12},{16,18},{18,... | collective-permute-start | bytes 884744 | tf_op jit(solution)/shard_map/ppermute | solution.py:79
  28.6 7.7 %collective-permute-start.12 = (bf16[96,768]{1,0:T(8,128)(2,1)S(1)}, bf16[96,768]{1,0:T(8,128)(2,1)S(1)}, u32[]{:S(2)}, u32[]{:S(2)}) collective-permute-start(bf16[96,768]{1,0:T(8,128)(2,1)S(1)} %slice.6), channel_id=1, source_target_pairs={{0,8},{2,6},{8,16},{10,2},{16,24},{18,10},{24,28},{26,18},{28,20},... | collective-permute-start | bytes 442376 | tf_op jit(solution)/shard_map/ppermute | solution.py:70
  31.6 11.5 %copy-start.4 = (f32[1536]{0:T(1024)S(1)}, f32[1536]{0:T(1024)}, u32[]{:S(2)}) copy-start(f32[1536]{0:T(1024)} %flat_gain.1) | copy-start | bytes 18436
  36.3 10.0 %collective-permute-start.15 = (bf16[576,512]{1,0:T(8,128)(2,1)S(1)}, bf16[576,512]{1,0:T(8,128)(2,1)}, u32[]{:S(2)}, u32[]{:S(2)}) collective-permute-start(bf16[576,512]{1,0:T(8,128)(2,1)S(1)} %collective-permute-done.8.refs_2_), channel_id=1, source_target_pairs={{0,8},{2,6},{8,16},{10,2},{16,24},{18,10},{24,28},{26,18},{28,20},... | collective-permute-start | bytes 1769480 | tf_op jit(solution)/shard_map/ppermute | solution.py:70
  38.5 1.4 %collective-permute-start.14 = (bf16[96,768]{1,0:T(8,128)(2,1)S(1)}, bf16[96,768]{1,0:T(8,128)(2,1)S(1)}, u32[]{:S(2)}, u32[]{:S(2)}) collective-permute-start(bf16[96,768]{1,0:T(8,128)(2,1)S(1)} %collective-permute-done.12.refs_7_), channel_id=1, source_target_pairs={{0,2},{2,0},{4,6},{6,4},{8,10},{10,8},{12,14},{14,12},{16,18},{18,... | collective-permute-start | bytes 442376 | tf_op jit(solution)/shard_map/ppermute | solution.py:79
  41.0 13.7 %collective-permute-start.17 = (bf16[128,1536]{1,0:T(8,128)(2,1)S(1)}, bf16[128,1536]{1,0:T(8,128)(2,1)}, u32[]{:S(2)}, u32[]{:S(2)}) collective-permute-start(bf16[128,1536]{1,0:T(8,128)(2,1)S(1)} %outward_send.1), channel_id=1, source_target_pairs={{0,1},{1,0},{2,3},{3,2},{4,5},{5,4},{6,7},{7,6},{8,9},{9,8},{10,11... | collective-permute-start | bytes 1179656 | tf_op jit(solution)/shard_map/ppermute | solution.py:752
  42.5 18.3 %collective-permute-start.19 = (bf16[576,512]{1,0:T(8,128)(2,1)S(1)}, bf16[576,512]{1,0:T(8,128)(2,1)}, u32[]{:S(2)}, u32[]{:S(2)}) collective-permute-start(bf16[576,512]{1,0:T(8,128)(2,1)S(1)} %collective-permute-done.3.refs_1_), channel_id=1, source_target_pairs={{0,2},{2,0},{4,6},{6,4},{8,10},{10,8},{12,14},{14,12},{16,18},{18,... | collective-permute-start | bytes 1769480 | tf_op jit(solution)/shard_map/ppermute | solution.py:79
  42.5 18.3 %collective-permute-start.20 = (bf16[576,512]{1,0:T(8,128)(2,1)S(1)}, bf16[576,512]{1,0:T(8,128)(2,1)}, u32[]{:S(2)}, u32[]{:S(2)}) collective-permute-start(bf16[576,512]{1,0:T(8,128)(2,1)S(1)} %collective-permute-done.8.refs_2_), channel_id=1, source_target_pairs={{0,2},{2,0},{4,6},{6,4},{8,10},{10,8},{12,14},{14,12},{16,18},{18,... | collective-permute-start | bytes 1769480 | tf_op jit(solution)/shard_map/ppermute | solution.py:79
  48.0 7.0 %collective-permute-start.16 = (bf16[288,512]{1,0:T(8,128)(2,1)}, bf16[288,512]{1,0:T(8,128)(2,1)}, u32[]{:S(2)}, u32[]{:S(2)}) collective-permute-start(bf16[288,512]{1,0:T(8,128)(2,1)} %slice.7), channel_id=1, source_target_pairs={{0,8},{2,6},{8,16},{10,2},{16,24},{18,10},{24,28},{26,18},{28,20},... | collective-permute-start | bytes 884744 | tf_op jit(solution)/shard_map/ppermute | solution.py:70
  50.1 12.3 %collective-permute-start.21 = (bf16[576,512]{1,0:T(8,128)(2,1)}, bf16[576,512]{1,0:T(8,128)(2,1)}, u32[]{:S(2)}, u32[]{:S(2)}) collective-permute-start(bf16[576,512]{1,0:T(8,128)(2,1)} %collective-permute-done.15.refs_0_), channel_id=1, source_target_pairs={{0,2},{2,0},{4,6},{6,4},{8,10},{10,8},{12,14},{14,12},{16,18},{18,... | collective-permute-start | bytes 1769480 | tf_op jit(solution)/shard_map/ppermute | solution.py:79
  50.1 20.8 %all-to-all-start = ((bf16[16,144,128]{2,1,0:T(8,128)(2,1)}), bf16[16,144,128]{2,1,0:T(8,128)(2,1)S(1)}, u32[]{:S(2)}, u32[]{:S(2)}) async-start(bf16[16,144,128]{2,1,0:T(8,128)(2,1)} %bundle.1), calls=%async_computation | async-start | bytes 1179648 | tf_op jit(solution)/shard_map/all_to_all | solution.py:761
  55.0 7.4 %collective-permute-start.22 = (bf16[288,512]{1,0:T(8,128)(2,1)}, bf16[288,512]{1,0:T(8,128)(2,1)S(1)}, u32[]{:S(2)}, u32[]{:S(2)}) collective-permute-start(bf16[288,512]{1,0:T(8,128)(2,1)} %collective-permute-done.16.refs_2_), channel_id=1, source_target_pairs={{0,2},{2,0},{4,6},{6,4},{8,10},{10,8},{12,14},{14,12},{16,18},{18,... | collective-permute-start | bytes 884744 | tf_op jit(solution)/shard_map/ppermute | solution.py:79
  55.2 0.7 copy-start.6
  57.3 5.1 %collective-permute-start.18 = (bf16[32,1536]{1,0:T(8,128)(2,1)S(1)}, bf16[32,1536]{1,0:T(8,128)(2,1)S(1)}, u32[]{:S(2)}, u32[]{:S(2)}) collective-permute-start(bf16[32,1536]{1,0:T(8,128)(2,1)S(1)} %get-tuple-element.120), channel_id=1, source_target_pairs={{0,1},{1,0},{2,3},{3,2},{4,5},{5,4},{6,7},{7,6},{8,9},{9,8},{10,11... | collective-permute-start | bytes 294920 | tf_op jit(solution)/shard_map/ppermute | solution.py:766
  58.9 0.9 %copy-start.2 = (bf16[1536,40]{0,1:T(8,128)(2,1)S(1)}, bf16[1536,40]{0,1:T(8,128)(2,1)}, u32[]{:S(2)}) copy-start(bf16[1536,40]{0,1:T(8,128)(2,1)} %param.20) | copy-start | bytes 368644
  59.8 0.7 copy-start.3
  62.4 8.6 %copy-start = (bf16[512,4,128]{2,1,0:T(4,128)(2,1)S(1)}, bf16[512,4,128]{2,1,0:T(4,128)(2,1)}, u32[]{:S(2)}) copy-start(bf16[512,4,128]{2,1,0:T(4,128)(2,1)} %param.25) | copy-start | bytes 1572868
  64.9 4.9 %collective-permute-start.23 = (bf16[32,1536]{1,0:T(8,128)(2,1)S(1)}, bf16[32,1536]{1,0:T(8,128)(2,1)S(1)}, u32[]{:S(2)}, u32[]{:S(2)}) collective-permute-start(bf16[32,1536]{1,0:T(8,128)(2,1)S(1)} %get-tuple-element.129), channel_id=1, source_target_pairs={{0,1},{1,0},{2,3},{3,2},{4,5},{5,4},{6,7},{7,6},{8,9},{9,8},{10,11... | collective-permute-start | bytes 294920 | tf_op jit(solution)/shard_map/ppermute | solution.py:774
  (1 other events, 0.6 us)

commit v14 on v13

--- a/solution.py
+++ b/solution.py
@@ -481,39 +481,6 @@
     )(mine, arrived, gain, place)
 
 
-def gate_kernel(moe_in, router, ids, place, gates, own, spread):
-    cap = own.shape[0]
-    own[...] = jnp.dot(place[:cap, :], moe_in[...], preferred_element_type=f32).astype(bf16)
-    hit = named_experts(ids, router.shape[0])
-    tokens = ids.shape[1]
-    row = lax.broadcasted_iota(jnp.int32, (tokens, tokens), 0)
-    eye = (row == lax.broadcasted_iota(jnp.int32, (tokens, tokens), 1)).astype(f32)
-    named = lax.dot_general(eye, hit, LAST_DIMS, preferred_element_type=f32)
-    spread[...] = lax.dot_general(
-        eye.astype(bf16), place[...], LAST_DIMS, preferred_element_type=f32
-    ).astype(bf16)
-    logits = lax.dot_general(moe_in[...], router[...], LAST_DIMS, preferred_element_type=f32)
-    raised = jnp.where(named > 0, jnp.exp(logits), 0.0)
-    gates[...] = raised / jnp.sum(raised, axis=-1, keepdims=True)
-
-
-def gate(moe_in, router_t, ids_t, place):
-    cap = place.shape[0] // 2
-    return pl.pallas_call(
-        gate_kernel,
-        out_shape=(
-            jax.ShapeDtypeStruct((moe_in.shape[0], router_t.shape[0]), f32),
-            jax.ShapeDtypeStruct((cap, moe_in.shape[1]), bf16),
-            jax.ShapeDtypeStruct(place.shape[::-1], bf16),
-        ),
-        in_specs=[VMEM] * 4,
-        out_specs=(VMEM,) * 3,
-        compiler_params=PARAMS,
-        cost_estimate=LITTLE,
-        name="gate",
-    )(moe_in, router_t, ids_t, place)
-
-
 def expert_pieces(gate_up, down, up_rows, down_rows, width):
     pieces = [(i * up_rows, up_rows, gate_up, i * width) for i in range(2)]
     pieces += [
@@ -522,26 +489,73 @@
     return pieces, pieces[-1][0] + down_rows
 
 
-def stage_kernel(groups, up_rows, down_rows, shards, *refs):
-    parts, (gate_up, down) = refs[: len(shards)], refs[len(shards) :]
-    pieces, unit_rows = expert_pieces(gate_up, down, up_rows, down_rows, parts[0].shape[1])
-    place_parts(groups, parts, unit_rows, pieces, shards)
-
-
-def stage(groups, early, up_rows, down_rows, model):
+def gate_kernel(groups, up_rows, down_rows, shards, moe_in, router_in, ids_in, place, *refs):
+    parts, (gates, own, spread, gate_up, down, router, ids, sems, part_sems) = (
+        refs[: len(shards)],
+        refs[len(shards) :],
+    )
+    small = fetch([(router_in, router), (ids_in, ids)], sems)
+    width = parts[0].shape[1]
+    pieces, unit_rows = expert_pieces(gate_up, down, up_rows, down_rows, width)
+    sources = ring_sources(groups, lax.axis_index("grp"))
+    pairs = []
+    for part, shard in zip(parts, shards):
+        for unit in range(part.shape[0] // unit_rows):
+            for first, rows, target, lane in pieces:
+                at = pl.multiple_of(sources[shard + unit] * rows, rows)
+                pairs.append(
+                    (
+                        part.at[pl.ds(unit * unit_rows + first, rows), :],
+                        target.at[pl.ds(at, rows), pl.ds(lane, width)],
+                    )
+                )
+    copies = fetch(pairs, part_sems)
+    cap = own.shape[0]
+    own[...] = jnp.dot(place[:cap, :], moe_in[...], preferred_element_type=f32).astype(bf16)
+    tokens = ids.shape[1]
+    row = lax.broadcasted_iota(jnp.int32, (tokens, tokens), 0)
+    eye = (row == lax.broadcasted_iota(jnp.int32, (tokens, tokens), 1)).astype(f32)
+    spread[...] = lax.dot_general(
+        eye.astype(bf16), place[...], LAST_DIMS, preferred_element_type=f32
+    ).astype(bf16)
+    for copy in small:
+        copy.wait()
+    hit = named_experts(ids, router.shape[0])
+    named = lax.dot_general(eye, hit, LAST_DIMS, preferred_element_type=f32)
+    logits = lax.dot_general(moe_in[...], router[...], LAST_DIMS, preferred_element_type=f32)
+    raised = jnp.where(named > 0, jnp.exp(logits), 0.0)
+    gates[...] = raised / jnp.sum(raised, axis=-1, keepdims=True)
+    for copy in copies:
+        copy.wait()
+
+
+def gate(groups, moe_in, router_t, ids_t, place, early, up_rows, down_rows):
+    cap = place.shape[0] // 2
+    tokens, model = moe_in.shape
     width = early[0][0].shape[1]
-    return pl.pallas_call(
-        functools.partial(stage_kernel, groups, up_rows, down_rows, [shard for _, shard in early]),
+    units = 2 * len(early)
+    far = [pltpu.with_memory_space_constraint(part, pltpu.HBM) for part in (router_t, ids_t)]
+    return pl.pallas_call(
+        functools.partial(gate_kernel, groups, up_rows, down_rows, [shard for _, shard in early]),
         out_shape=(
+            jax.ShapeDtypeStruct((tokens, router_t.shape[0]), f32),
+            jax.ShapeDtypeStruct((cap, model), bf16),
+            jax.ShapeDtypeStruct(place.shape[::-1], bf16),
             jax.ShapeDtypeStruct((groups * up_rows, 2 * width), bf16),
             jax.ShapeDtypeStruct((groups * down_rows, model), bf16),
         ),
-        in_specs=[VMEM] * len(early),
-        out_specs=(VMEM, VMEM),
-        compiler_params=PARAMS,
-        cost_estimate=reads(2 * groups * 2 * (up_rows * 2 * width + down_rows * model)),
-        name="stage",
-    )(*[part for part, _ in early])
+        in_specs=[VMEM, ANY, ANY, VMEM] + [ANY] * len(early),
+        out_specs=(VMEM,) * 5,
+        scratch_shapes=[
+            pltpu.VMEM(router_t.shape, bf16),
+            pltpu.VMEM(ids_t.shape, jnp.int32),
+            pltpu.SemaphoreType.DMA((2,)),
+            pltpu.SemaphoreType.DMA((units * (2 + model // width),)),
+        ],
+        compiler_params=PARAMS,
+        cost_estimate=LITTLE,
+        name="gate",
+    )(moe_in, *far, place, *[part for part, _ in early])
 
 
 def expert_kernel(groups, up_rows, down_rows, shards, own, other, gate_up_in, down_in, *refs):
@@ -764,12 +778,11 @@
 
     residual, moe_in, sent_rows = route(mine, arrived, late_gain, place)
     landed = swap(sent_rows)
-    gates, own_rows, spread = gate(moe_in, router.T, expert_ids.T, place)
     parts_early, parts_late = expert_ring.split()
-    first, own_rows = together((parts_early[0][0], own_rows))
-    parts_early[0] = (first, parts_early[0][1])
-    staged = stage(groups, parts_early, up_rows, down_rows, model)
-    landed, staged = together((landed, staged))
+    gates, own_rows, spread, *staged = gate(
+        groups, moe_in, router.T, expert_ids.T, place, parts_early, up_rows, down_rows
+    )
+    landed, own_rows = together((landed, own_rows))
     own_made, back = expert(groups, own_rows, landed, staged, parts_late, up_rows, down_rows)
     returned = swap(back)
     layer_out = combine(residual, gates, spread, own_made, returned)

time: 73 us -> 72.8 us (level)
  local copies, waits for them, and re-layouts: 6.43 us -> 4.84 us
  waiting for transfers between devices: 14.5 us -> 15.6 us
    unnamed x17 -> x13, local copies, waits for them, and re-layouts: 4.72 us -> 3.13 us
    ppermute x1, waiting for transfers between devices: 0.02 us -> 1.33 us  [two_lane_shards(): landed = swap(sent_rows)]
    pallas_call x2 -> x1, Pallas kernels: 1.88 us -> 2.18 us  [gate(): pl.pallas_call(functools.partial(gate_kernel, groups, up_rows, down_rows,...]
  transfers between devices with their start and end apart: 25 -> 25, of which waited for: 7 -> 8; matrix products, arithmetic and copies ran while one was open for 5% -> 5% of each run, Pallas kernels for 25% -> 26%
where the time goes in v14:
time: 72.8 us; the launch traced here: 72.3 us
  starting transfers between devices  31 us (43%)
  Pallas kernels  20 us (27%)
  waiting for transfers between devices  15.6 us (21%)
  local copies, waits for them, and re-layouts  4.84 us (7%)
  between operations  0.86 us (1%)
    ppermute x8, starting transfers between devices, step(): self.mine.append(self.across(held))  15.2 us
    ppermute x8, waiting for transfers between devices, step(): self.mine.append(self.across(held))  7.73 us
    all_to_all x1, starting transfers between devices, two_lane_shards(): lax.all_to_all(outgoing, 'grp', split_axis=0, concat_axis=0, tiled=True)  4.56 us
    unnamed x13, local copies, waits for them, and re-layouts  3.13 us
    ppermute x1, waiting for transfers between devices, two_lane_shards(): returned = swap(back)  2.99 us
    ppermute x1, starting transfers between devices, two_lane_shards(): other_tokens = swap(tokens)  2.56 us
    pallas_call x1, Pallas kernels, expert(): pl.pallas_call(functools.partial(expert_kernel, groups, up_rows, down_row...  2.52 us
    pallas_call x1, Pallas kernels, project(): pl.pallas_call(project_kernel, out_shape=(jax.ShapeDtypeStruct((2 * count...  2.21 us
  transfers between devices with their start and end apart: 25, of which 8 were waited for; matrix products, arithmetic and copies ran while one was open for 5% of the time, Pallas kernels for 26%

profile of v14, /device:TPU:0, one launch (start us, length us, event | category | flops | bytes accessed | tf_op | source)
XLA Modules:
  0.0 72.3 jit_solution(7831501167263076907)
XLA Ops:
  1.7 2.6 %collective-permute-start.5 = (bf16[128,1536]{1,0:T(8,128)(2,1)}, bf16[128,1536]{1,0:T(8,128)(2,1)S(1)}, u32[]{:S(2)}, u32[]{:S(2)}) collective-permute-start(bf16[128,1536]{1,0:T(8,128)(2,1)} %tokens.1), channel_id=1, source_target_pairs={{0,1},{1,0},{2,3},{3,2},{4,5},{5,4},{6,7},{7,6},{8,9},{9,8},{10,11... | collective-permute-start | bytes 1179656 | tf_op jit(solution)/shard_map/ppermute | solution.py:727
  5.4 1.7 %collective-permute-start.4 = (bf16[192,768]{1,0:T(8,128)(2,1)S(1)}, bf16[192,768]{1,0:T(8,128)(2,1)S(1)}, u32[]{:S(2)}, u32[]{:S(2)}) collective-permute-start(bf16[192,768]{1,0:T(8,128)(2,1)S(1)} %get-tuple-element.66.refs_0_), channel_id=1, source_target_pairs={{0,8},{2,6},{8,16},{10,2},{16,24},{18,10},{24,28},{26,18},{28,20},... | collective-permute-start | bytes 884744 | tf_op jit(solution)/shard_map/ppermute | solution.py:70
  7.1 1.6 %collective-permute-start.3 = (bf16[576,512]{1,0:T(8,128)(2,1)S(1)}, bf16[576,512]{1,0:T(8,128)(2,1)S(1)}, u32[]{:S(2)}, u32[]{:S(2)}) collective-permute-start(bf16[576,512]{1,0:T(8,128)(2,1)S(1)} %get-tuple-element.65.refs_0_), channel_id=1, source_target_pairs={{0,8},{2,6},{8,16},{10,2},{16,24},{18,10},{24,28},{26,18},{28,20},... | collective-permute-start | bytes 1769480 | tf_op jit(solution)/shard_map/ppermute | solution.py:70
  8.7 1.5 %prepare.1 = (f32[256,128]{1,0:T(8,128)S(1)}, f32[256,128]{1,0:T(8,128)S(1)}, f32[256,128]{1,0:T(8,128)S(1)}, bf16[64,128]{1,0:T(8,128)(2,1)S(1)}, bf16[512,256]...) custom-call(s32[1,256]{1,0:T(1,128)} %bitcast.26, s32[1,256]{1,0:T(1,128)} %bitcast.27, ...), custom_call_target="tpu_custom_call" | custom-call | flops 1 | bytes 1 | tf_op jit(solution)/shard_map/prepare/pallas_call | solution.py:266
  10.2 1.8 %copy.19 = bf16[192,8,4,128]{3,1,2,0:T(8,128)(2,1)S(1)} copy(bf16[192,8,4,128]{3,2,1,0:T(4,128)(2,1)} %bitcast.15) | data formatting | bytes 3145728
  12.0 2.1 %collective-permute-done.5.other = bf16[128,1536]{1,0:T(8,128)(2,1)S(1)} collective-permute-done((bf16[128,1536]{1,0:T(8,128)(2,1)}, bf16[128,1536]{1,0:T(8,128)(2,1)S(1)}, u32[]{:S(2)}, u32[]{:S(2)}) %collective-permute-start.5) | collective-permute-done | bytes 393248 | tf_op jit(solution)/shard_map/ppermute | solution.py:727
  14.1 1.8 %collective-permute-start.7 = (bf16[192,768]{1,0:T(8,128)(2,1)S(1)}, bf16[192,768]{1,0:T(8,128)(2,1)S(1)}, u32[]{:S(2)}, u32[]{:S(2)}) collective-permute-start(bf16[192,768]{1,0:T(8,128)(2,1)S(1)} %collective-permute-done.4.refs_1_), channel_id=1, source_target_pairs={{0,8},{2,6},{8,16},{10,2},{16,24},{18,10},{24,28},{26,18},{28,20},... | collective-permute-start | bytes 884744 | tf_op jit(solution)/shard_map/ppermute | solution.py:70
  16.0 2.2 %project.1 = (bf16[256,768]{1,0:T(8,128)(2,1)S(1)}, bf16[256,512]{1,0:T(8,128)(2,1)S(1)}, bf16[128,512]{1,0:T(8,128)(2,1)S(1)}) custom-call(bf16[128,1536]{1,0:T(8,128)(2,1)S(1)} %copy-done.1, bf16[128,1536]{1,0:T(8,128)(2,1)S(1)} %collective-permute-done.5.other, f32[1,1536]{1,0:T(1,128)S(1)} %get-tuple-element.71.gain, ...), custom_call_target="tpu_custom_call" | custom-call | flops 9200000000 | bytes 64000000 | tf_op jit(solution)/shard_map/project/pallas_call | solution.py:316
  18.2 2.1 %collective-permute-start.6 = (bf16[128,512]{1,0:T(8,128)(2,1)S(1)}, bf16[128,512]{1,0:T(8,128)(2,1)S(1)}, u32[]{:S(2)}, u32[]{:S(2)}) collective-permute-start(bf16[128,512]{1,0:T(8,128)(2,1)S(1)} %get-tuple-element.75), channel_id=1, source_target_pairs={{0,2},{2,4},{4,6},{6,8},{8,10},{10,12},{12,14},{14,16},{16,18},{18... | collective-permute-start | bytes 393224 | tf_op jit(solution)/shard_map/ppermute | solution.py:745
  20.3 1.3 %collective-permute-done.7.refs_2_ = bf16[192,768]{1,0:T(8,128)(2,1)S(1)} collective-permute-done((bf16[192,768]{1,0:T(8,128)(2,1)S(1)}, bf16[192,768]{1,0:T(8,128)(2,1)S(1)}, u32[]{:S(2)}, u32[]{:S(2)}) %collective-permute-start.7) | collective-permute-done | bytes 294944 | tf_op jit(solution)/shard_map/ppermute | solution.py:70
  21.6 1.7 %collective-permute-start.9 = (bf16[192,768]{1,0:T(8,128)(2,1)S(1)}, bf16[192,768]{1,0:T(8,128)(2,1)S(1)}, u32[]{:S(2)}, u32[]{:S(2)}) collective-permute-start(bf16[192,768]{1,0:T(8,128)(2,1)S(1)} %collective-permute-done.7.refs_2_), channel_id=1, source_target_pairs={{0,8},{2,6},{8,16},{10,2},{16,24},{18,10},{24,28},{26,18},{28,20},... | collective-permute-start | bytes 884744 | tf_op jit(solution)/shard_map/ppermute | solution.py:70
  23.3 1.3 %attend_late.1.late = bf16[128,768]{1,0:T(8,128)(2,1)S(1)} custom-call(bf16[256,768]{1,0:T(8,128)(2,1)S(1)} %get-tuple-element.78.q, bf16[256,512]{1,0:T(8,128)(2,1)S(1)} %get-tuple-element.92.kv, f32[256,128]{1,0:T(8,128)S(1)} %get-tuple-element.80.past), custom_call_target="tpu_custom_call" | custom-call | flops 2300000000 | bytes 16000000 | tf_op jit(solution)/shard_map/attend_late/pallas_call | solution.py:372
  24.7 2.3 %collective-permute-start.8 = (bf16[576,512]{1,0:T(8,128)(2,1)S(1)}, bf16[576,512]{1,0:T(8,128)(2,1)S(1)}, u32[]{:S(2)}, u32[]{:S(2)}) collective-permute-start(bf16[576,512]{1,0:T(8,128)(2,1)S(1)} %collective-permute-done.3.refs_1_), channel_id=1, source_target_pairs={{0,8},{2,6},{8,16},{10,2},{16,24},{18,10},{24,28},{26,18},{28,20},... | collective-permute-start | bytes 1769480 | tf_op jit(solution)/shard_map/ppermute | solution.py:70
  27.0 1.5 %attend_early.1.early = bf16[128,768]{1,0:T(8,128)(2,1)S(1)} custom-call(bf16[256,768]{1,0:T(8,128)(2,1)S(1)} %get-tuple-element.78.q, bf16[256,512]{1,0:T(8,128)(2,1)S(1)} %get-tuple-element.92.kv, bf16[128,512]{1,0:T(8,128)(2,1)S(1)} %collective-permute-done.6.seam, f32[256,128]{1,0:T(8,128)S(1)} %get-tuple-element.80.past), custom_call_target="tpu_custom_call" | custom-call | flops 2300000000 | bytes 16000000 | tf_op jit(solution)/shard_map/attend_early/pallas_call | solution.py:384
  28.6 1.6 %collective-permute-start.12 = (bf16[96,768]{1,0:T(8,128)(2,1)S(1)}, bf16[96,768]{1,0:T(8,128)(2,1)S(1)}, u32[]{:S(2)}, u32[]{:S(2)}) collective-permute-start(bf16[96,768]{1,0:T(8,128)(2,1)S(1)} %slice.6), channel_id=1, source_target_pairs={{0,8},{2,6},{8,16},{10,2},{16,24},{18,10},{24,28},{26,18},{28,20},... | collective-permute-start | bytes 442376 | tf_op jit(solution)/shard_map/ppermute | solution.py:70
  30.2 1.4 %bundle.1 = bf16[16,144,128]{2,1,0:T(8,128)(2,1)} custom-call(bf16[512,256]{1,0:T(8,128)(2,1)S(1)} %get-tuple-element.91.send, bf16[256,512]{1,0:T(8,128)(2,1)S(1)} %get-tuple-element.92.kv, bf16[256,128]{1,0:T(8,128)(2,1)S(1)} %get-tuple-element.93.tags), custom_call_target="tpu_custom_call" | custom-call | flops 1 | bytes 1 | tf_op jit(solution)/shard_map/bundle/pallas_call | solution.py:644
  31.6 4.7 %collective-permute-done.12.refs_7_ = bf16[96,768]{1,0:T(8,128)(2,1)S(1)} collective-permute-done((bf16[96,768]{1,0:T(8,128)(2,1)S(1)}, bf16[96,768]{1,0:T(8,128)(2,1)S(1)}, u32[]{:S(2)}, u32[]{:S(2)}) %collective-permute-start.12) | collective-permute-done | bytes 147488 | tf_op jit(solution)/shard_map/ppermute | solution.py:70
  36.3 2.2 %collective-permute-start.15 = (bf16[576,512]{1,0:T(8,128)(2,1)S(1)}, bf16[576,512]{1,0:T(8,128)(2,1)}, u32[]{:S(2)}, u32[]{:S(2)}) collective-permute-start(bf16[576,512]{1,0:T(8,128)(2,1)S(1)} %collective-permute-done.8.refs_2_), channel_id=1, source_target_pairs={{0,8},{2,6},{8,16},{10,2},{16,24},{18,10},{24,28},{26,18},{28,20},... | collective-permute-start | bytes 1769480 | tf_op jit(solution)/shard_map/ppermute | solution.py:70
  38.5 1.4 %collective-permute-done.14.refs_8_ = bf16[96,768]{1,0:T(8,128)(2,1)S(1)} collective-permute-done((bf16[96,768]{1,0:T(8,128)(2,1)S(1)}, bf16[96,768]{1,0:T(8,128)(2,1)S(1)}, u32[]{:S(2)}, u32[]{:S(2)}) %collective-permute-start.14) | collective-permute-done | bytes 147488 | tf_op jit(solution)/shard_map/ppermute | solution.py:79
  41.0 1.6 %collective-permute-start.17 = (bf16[128,1536]{1,0:T(8,128)(2,1)S(1)}, bf16[128,1536]{1,0:T(8,128)(2,1)}, u32[]{:S(2)}, u32[]{:S(2)}) collective-permute-start(bf16[128,1536]{1,0:T(8,128)(2,1)S(1)} %outward_send.1), channel_id=1, source_target_pairs={{0,1},{1,0},{2,3},{3,2},{4,5},{5,4},{6,7},{7,6},{8,9},{9,8},{10,11... | collective-permute-start | bytes 1179656 | tf_op jit(solution)/shard_map/ppermute | solution.py:766
  44.8 1.4 %collective-permute-done.15.refs_0_ = bf16[576,512]{1,0:T(8,128)(2,1)} collective-permute-done((bf16[576,512]{1,0:T(8,128)(2,1)S(1)}, bf16[576,512]{1,0:T(8,128)(2,1)}, u32[]{:S(2)}, u32[]{:S(2)}) %collective-permute-start.15) | collective-permute-done | bytes 589856 | tf_op jit(solution)/shard_map/ppermute | solution.py:70
  46.3 1.7 %slice.7 = bf16[288,512]{1,0:T(8,128)(2,1)} slice(bf16[576,512]{1,0:T(8,128)(2,1)} %collective-permute-done.15.refs_0_), slice={[0:288], [0:512]} | slice | bytes 589824 | tf_op jit(solution)/shard_map/slice | solution.py:69
  48.0 2.2 %collective-permute-start.16 = (bf16[288,512]{1,0:T(8,128)(2,1)}, bf16[288,512]{1,0:T(8,128)(2,1)}, u32[]{:S(2)}, u32[]{:S(2)}) collective-permute-start(bf16[288,512]{1,0:T(8,128)(2,1)} %slice.7), channel_id=1, source_target_pairs={{0,8},{2,6},{8,16},{10,2},{16,24},{18,10},{24,28},{26,18},{28,20},... | collective-permute-start | bytes 884744 | tf_op jit(solution)/shard_map/ppermute | solution.py:70
  50.1 4.6 %all-to-all-start = ((bf16[16,144,128]{2,1,0:T(8,128)(2,1)}), bf16[16,144,128]{2,1,0:T(8,128)(2,1)S(1)}, u32[]{:S(2)}, u32[]{:S(2)}) async-start(bf16[16,144,128]{2,1,0:T(8,128)(2,1)} %bundle.1), calls=%async_computation | async-start | bytes 1179648 | tf_op jit(solution)/shard_map/all_to_all | solution.py:775
  55.9 1.4 %route.1 = (bf16[128,1536]{1,0:T(8,128)(2,1)S(1)}, bf16[128,1536]{1,0:T(8,128)(2,1)S(1)}, bf16[32,1536]{1,0:T(8,128)(2,1)S(1)}) custom-call(f32[128,1536]{1,0:T(8,128)S(1)} %get-tuple-element.103.mine, bf16[128,1536]{1,0:T(8,128)(2,1)} %collective-permute-done.17.arrived, f32[1,1536]{1,0:T(1,128)S(1)} %copy-done.4, bf16[64,128]{1,0:T(8,128)(2,1)S(1)} %get-tuple-element.110.place), custom_call_target="tpu_custom_call" | custom-call | flops 1 | bytes 1966080 | tf_op jit(solution)/shard_map/route/pallas_call | solution.py:469
  57.3 1.6 %collective-permute-start.20 = (bf16[32,1536]{1,0:T(8,128)(2,1)S(1)}, bf16[32,1536]{1,0:T(8,128)(2,1)S(1)}, u32[]{:S(2)}, u32[]{:S(2)}) collective-permute-start(bf16[32,1536]{1,0:T(8,128)(2,1)S(1)} %get-tuple-element.115), channel_id=1, source_target_pairs={{0,1},{1,0},{2,3},{3,2},{4,5},{5,4},{6,7},{7,6},{8,9},{9,8},{10,11... | collective-permute-start | bytes 294920 | tf_op jit(solution)/shard_map/ppermute | solution.py:780
  58.9 2.2 %gate.1 = (f32[128,40]{1,0:T(8,128)S(1)}, bf16[32,1536]{1,0:T(8,128)(2,1)S(1)}, bf16[128,64]{1,0:T(8,128)(2,1)S(1)}, bf16[1536,1024]{1,0:T(8,128)(2,1)S(1)}, bf16[512,1536]{1,0:T(8,128)(2,1)S(1)}) custom-call(bf16[128,1536]{1,0:T(8,128)(2,1)S(1)} %get-tuple-element.112.moe_in, bf16[40,1536]{1,0:T(8,128)(2,1)} %bitcast.21, s32[8,128]{1,0:T(8,128)} %bitcast.25, ...), custom_call_target="tpu_custom_call" | custom-call | flops 1 | bytes 1 | tf_op jit(solution)/shard_map/gate/pallas_call | solution.py:538
  61.0 1.3 %collective-permute-done.20.other = bf16[32,1536]{1,0:T(8,128)(2,1)S(1)} collective-permute-done((bf16[32,1536]{1,0:T(8,128)(2,1)S(1)}, bf16[32,1536]{1,0:T(8,128)(2,1)S(1)}, u32[]{:S(2)}, u32[]{:S(2)}) %collective-permute-start.20) | collective-permute-done | bytes 98336 | tf_op jit(solution)/shard_map/ppermute | solution.py:780
  62.4 2.5 %expert.1 = (bf16[32,1536]{1,0:T(8,128)(2,1)S(1)}, bf16[32,1536]{1,0:T(8,128)(2,1)S(1)}, bf16[1536,1024]{1,0:T(8,128)(2,1)S(1)}, bf16[512,1536]{1,0:T(8,128)(2,1)S(1)}) custom-call(bf16[32,1536]{1,0:T(8,128)(2,1)S(1)} %get-tuple-element.117.own, bf16[32,1536]{1,0:T(8,128)(2,1)S(1)} %collective-permute-done.20.other, ...), custom_call_target="tpu_custom_call", output_to_operand_aliasing={{2}: (2, {}), {3}: (3, {})} | custom-call | flops 7129999872 | bytes 49600000 | tf_op jit(solution)/shard_map/expert/pallas_call | solution.py:581
  64.9 1.7 %collective-permute-start.23 = (bf16[32,1536]{1,0:T(8,128)(2,1)S(1)}, bf16[32,1536]{1,0:T(8,128)(2,1)S(1)}, u32[]{:S(2)}, u32[]{:S(2)}) collective-permute-start(bf16[32,1536]{1,0:T(8,128)(2,1)S(1)} %get-tuple-element.123), channel_id=1, source_target_pairs={{0,1},{1,0},{2,3},{3,2},{4,5},{5,4},{6,7},{7,6},{8,9},{9,8},{10,11... | collective-permute-start | bytes 294920 | tf_op jit(solution)/shard_map/ppermute | solution.py:787
  66.6 3.0 %collective-permute-done.23.returned = bf16[32,1536]{1,0:T(8,128)(2,1)S(1)} collective-permute-done((bf16[32,1536]{1,0:T(8,128)(2,1)S(1)}, bf16[32,1536]{1,0:T(8,128)(2,1)S(1)}, u32[]{:S(2)}, u32[]{:S(2)}) %collective-permute-start.23) | collective-permute-done | bytes 98336 | tf_op jit(solution)/shard_map/ppermute | solution.py:787
  70.7 1.5 %write.1 = bf16[2048,128]{1,0:T(8,128)(2,1)} custom-call(bf16[16,144,128]{2,1,0:T(8,128)(2,1)S(1)} %all-to-all-done.arrived, bf16[2048,128]{1,0:T(8,128)(2,1)S(1)} %bitcast.14), custom_call_target="tpu_custom_call" | custom-call | flops 1 | bytes 2097152 | tf_op jit(solution)/shard_map/write/pallas_call | solution.py:685
  (46 shorter events, 8.0 us)
Async XLA Ops:
  0.6 3.6 %collective-permute-start.2 = (bf16[96,1536]{1,0:T(8,128)(2,1)}, bf16[96,1536]{1,0:T(8,128)(2,1)S(1)}, u32[]{:S(2)}, u32[]{:S(2)}) collective-permute-start(bf16[96,1536]{1,0:T(8,128)(2,1)} %bitcast.17), channel_id=1, source_target_pairs={{0,2},{2,0},{4,6},{6,4},{8,10},{10,8},{12,14},{14,12},{16,18},{18,... | collective-permute-start | bytes 884744 | tf_op jit(solution)/shard_map/ppermute | solution.py:730
  1.1 3.1 %collective-permute-start = (bf16[96,1024]{1,0:T(8,128)(2,1)}, bf16[96,1024]{1,0:T(8,128)(2,1)S(1)}, u32[]{:S(2)}, u32[]{:S(2)}) collective-permute-start(bf16[96,1024]{1,0:T(8,128)(2,1)} %bitcast.19), channel_id=1, source_target_pairs={{0,2},{2,0},{4,6},{6,4},{8,10},{10,8},{12,14},{14,12},{16,18},{18,... | collective-permute-start | bytes 589832 | tf_op jit(solution)/shard_map/ppermute | solution.py:730
  1.2 3.0 %collective-permute-start.1 = (bf16[32,1536]{1,0:T(8,128)(2,1)}, bf16[32,1536]{1,0:T(8,128)(2,1)S(1)}, u32[]{:S(2)}, u32[]{:S(2)}) collective-permute-start(bf16[32,1536]{1,0:T(8,128)(2,1)} %bitcast.22), channel_id=1, source_target_pairs={{0,2},{2,0},{4,6},{6,4},{8,10},{10,8},{12,14},{14,12},{16,18},{18,... | collective-permute-start | bytes 294920 | tf_op jit(solution)/shard_map/ppermute | solution.py:730
  1.7 12.5 %collective-permute-start.5 = (bf16[128,1536]{1,0:T(8,128)(2,1)}, bf16[128,1536]{1,0:T(8,128)(2,1)S(1)}, u32[]{:S(2)}, u32[]{:S(2)}) collective-permute-start(bf16[128,1536]{1,0:T(8,128)(2,1)} %tokens.1), channel_id=1, source_target_pairs={{0,1},{1,0},{2,3},{3,2},{4,5},{5,4},{6,7},{7,6},{8,9},{9,8},{10,11... | collective-permute-start | bytes 1179656 | tf_op jit(solution)/shard_map/ppermute | solution.py:727
  5.4 8.8 %collective-permute-start.4 = (bf16[192,768]{1,0:T(8,128)(2,1)S(1)}, bf16[192,768]{1,0:T(8,128)(2,1)S(1)}, u32[]{:S(2)}, u32[]{:S(2)}) collective-permute-start(bf16[192,768]{1,0:T(8,128)(2,1)S(1)} %get-tuple-element.66.refs_0_), channel_id=1, source_target_pairs={{0,8},{2,6},{8,16},{10,2},{16,24},{18,10},{24,28},{26,18},{28,20},... | collective-permute-start | bytes 884744 | tf_op jit(solution)/shard_map/ppermute | solution.py:70
  7.1 17.5 %collective-permute-start.3 = (bf16[576,512]{1,0:T(8,128)(2,1)S(1)}, bf16[576,512]{1,0:T(8,128)(2,1)S(1)}, u32[]{:S(2)}, u32[]{:S(2)}) collective-permute-start(bf16[576,512]{1,0:T(8,128)(2,1)S(1)} %get-tuple-element.65.refs_0_), channel_id=1, source_target_pairs={{0,8},{2,6},{8,16},{10,2},{16,24},{18,10},{24,28},{26,18},{28,20},... | collective-permute-start | bytes 1769480 | tf_op jit(solution)/shard_map/ppermute | solution.py:70
  10.2 5.8 %copy-start.1 = (bf16[128,1536]{1,0:T(8,128)(2,1)S(1)}, bf16[128,1536]{1,0:T(8,128)(2,1)}, u32[]{:S(2)}) copy-start(bf16[128,1536]{1,0:T(8,128)(2,1)} %tokens.1) | copy-start | bytes 1179652
  10.2 5.8 %copy-start.5 = (bf16[1536,768]{1,0:T(8,128)(2,1)S(1)}, bf16[1536,768]{1,0:T(8,128)(2,1)}, u32[]{:S(2)}) copy-start(bf16[1536,768]{1,0:T(8,128)(2,1)} %w_query.1) | copy-start | bytes 7077892
  14.1 14.3 %collective-permute-start.10 = (bf16[192,768]{1,0:T(8,128)(2,1)S(1)}, bf16[192,768]{1,0:T(8,128)(2,1)S(1)}, u32[]{:S(2)}, u32[]{:S(2)}) collective-permute-start(bf16[192,768]{1,0:T(8,128)(2,1)S(1)} %collective-permute-done.4.refs_1_), channel_id=1, source_target_pairs={{0,2},{2,0},{4,6},{6,4},{8,10},{10,8},{12,14},{14,12},{16,18},{18,... | collective-permute-start | bytes 884744 | tf_op jit(solution)/shard_map/ppermute | solution.py:79
  14.1 7.5 %collective-permute-start.7 = (bf16[192,768]{1,0:T(8,128)(2,1)S(1)}, bf16[192,768]{1,0:T(8,128)(2,1)S(1)}, u32[]{:S(2)}, u32[]{:S(2)}) collective-permute-start(bf16[192,768]{1,0:T(8,128)(2,1)S(1)} %collective-permute-done.4.refs_1_), channel_id=1, source_target_pairs={{0,8},{2,6},{8,16},{10,2},{16,24},{18,10},{24,28},{26,18},{28,20},... | collective-permute-start | bytes 884744 | tf_op jit(solution)/shard_map/ppermute | solution.py:70
  18.2 6.5 %collective-permute-start.6 = (bf16[128,512]{1,0:T(8,128)(2,1)S(1)}, bf16[128,512]{1,0:T(8,128)(2,1)S(1)}, u32[]{:S(2)}, u32[]{:S(2)}) collective-permute-start(bf16[128,512]{1,0:T(8,128)(2,1)S(1)} %get-tuple-element.75), channel_id=1, source_target_pairs={{0,2},{2,4},{4,6},{6,8},{8,10},{10,12},{12,14},{14,16},{16,18},{18... | collective-permute-start | bytes 393224 | tf_op jit(solution)/shard_map/ppermute | solution.py:745
  21.6 6.8 %collective-permute-start.11 = (bf16[192,768]{1,0:T(8,128)(2,1)S(1)}, bf16[192,768]{1,0:T(8,128)(2,1)S(1)}, u32[]{:S(2)}, u32[]{:S(2)}) collective-permute-start(bf16[192,768]{1,0:T(8,128)(2,1)S(1)} %collective-permute-done.7.refs_2_), channel_id=1, source_target_pairs={{0,2},{2,0},{4,6},{6,4},{8,10},{10,8},{12,14},{14,12},{16,18},{18,... | collective-permute-start | bytes 884744 | tf_op jit(solution)/shard_map/ppermute | solution.py:79
  21.6 6.8 %collective-permute-start.9 = (bf16[192,768]{1,0:T(8,128)(2,1)S(1)}, bf16[192,768]{1,0:T(8,128)(2,1)S(1)}, u32[]{:S(2)}, u32[]{:S(2)}) collective-permute-start(bf16[192,768]{1,0:T(8,128)(2,1)S(1)} %collective-permute-done.7.refs_2_), channel_id=1, source_target_pairs={{0,8},{2,6},{8,16},{10,2},{16,24},{18,10},{24,28},{26,18},{28,20},... | collective-permute-start | bytes 884744 | tf_op jit(solution)/shard_map/ppermute | solution.py:70
  24.7 11.6 %collective-permute-start.8 = (bf16[576,512]{1,0:T(8,128)(2,1)S(1)}, bf16[576,512]{1,0:T(8,128)(2,1)S(1)}, u32[]{:S(2)}, u32[]{:S(2)}) collective-permute-start(bf16[576,512]{1,0:T(8,128)(2,1)S(1)} %collective-permute-done.3.refs_1_), channel_id=1, source_target_pairs={{0,8},{2,6},{8,16},{10,2},{16,24},{18,10},{24,28},{26,18},{28,20},... | collective-permute-start | bytes 1769480 | tf_op jit(solution)/shard_map/ppermute | solution.py:70
  28.5 1.7 %collective-permute-start.13 = (bf16[192,768]{1,0:T(8,128)(2,1)S(1)}, bf16[192,768]{1,0:T(8,128)(2,1)S(1)}, u32[]{:S(2)}, u32[]{:S(2)}) collective-permute-start(bf16[192,768]{1,0:T(8,128)(2,1)S(1)} %collective-permute-done.9.refs_3_), channel_id=1, source_target_pairs={{0,2},{2,0},{4,6},{6,4},{8,10},{10,8},{12,14},{14,12},{16,18},{18,... | collective-permute-start | bytes 884744 | tf_op jit(solution)/shard_map/ppermute | solution.py:79
  28.6 7.7 %collective-permute-start.12 = (bf16[96,768]{1,0:T(8,128)(2,1)S(1)}, bf16[96,768]{1,0:T(8,128)(2,1)S(1)}, u32[]{:S(2)}, u32[]{:S(2)}) collective-permute-start(bf16[96,768]{1,0:T(8,128)(2,1)S(1)} %slice.6), channel_id=1, source_target_pairs={{0,8},{2,6},{8,16},{10,2},{16,24},{18,10},{24,28},{26,18},{28,20},... | collective-permute-start | bytes 442376 | tf_op jit(solution)/shard_map/ppermute | solution.py:70
  31.6 11.5 %copy-start.2 = (f32[1536]{0:T(1024)S(1)}, f32[1536]{0:T(1024)}, u32[]{:S(2)}) copy-start(f32[1536]{0:T(1024)} %flat_gain.1) | copy-start | bytes 18436
  36.3 10.0 %collective-permute-start.15 = (bf16[576,512]{1,0:T(8,128)(2,1)S(1)}, bf16[576,512]{1,0:T(8,128)(2,1)}, u32[]{:S(2)}, u32[]{:S(2)}) collective-permute-start(bf16[576,512]{1,0:T(8,128)(2,1)S(1)} %collective-permute-done.8.refs_2_), channel_id=1, source_target_pairs={{0,8},{2,6},{8,16},{10,2},{16,24},{18,10},{24,28},{26,18},{28,20},... | collective-permute-start | bytes 1769480 | tf_op jit(solution)/shard_map/ppermute | solution.py:70
  38.5 1.4 %collective-permute-start.14 = (bf16[96,768]{1,0:T(8,128)(2,1)S(1)}, bf16[96,768]{1,0:T(8,128)(2,1)S(1)}, u32[]{:S(2)}, u32[]{:S(2)}) collective-permute-start(bf16[96,768]{1,0:T(8,128)(2,1)S(1)} %collective-permute-done.12.refs_7_), channel_id=1, source_target_pairs={{0,2},{2,0},{4,6},{6,4},{8,10},{10,8},{12,14},{14,12},{16,18},{18,... | collective-permute-start | bytes 442376 | tf_op jit(solution)/shard_map/ppermute | solution.py:79
  41.0 13.7 %collective-permute-start.17 = (bf16[128,1536]{1,0:T(8,128)(2,1)S(1)}, bf16[128,1536]{1,0:T(8,128)(2,1)}, u32[]{:S(2)}, u32[]{:S(2)}) collective-permute-start(bf16[128,1536]{1,0:T(8,128)(2,1)S(1)} %outward_send.1), channel_id=1, source_target_pairs={{0,1},{1,0},{2,3},{3,2},{4,5},{5,4},{6,7},{7,6},{8,9},{9,8},{10,11... | collective-permute-start | bytes 1179656 | tf_op jit(solution)/shard_map/ppermute | solution.py:766
  42.5 16.3 %collective-permute-start.18 = (bf16[576,512]{1,0:T(8,128)(2,1)S(1)}, bf16[576,512]{1,0:T(8,128)(2,1)}, u32[]{:S(2)}, u32[]{:S(2)}) collective-permute-start(bf16[576,512]{1,0:T(8,128)(2,1)S(1)} %collective-permute-done.3.refs_1_), channel_id=1, source_target_pairs={{0,2},{2,0},{4,6},{6,4},{8,10},{10,8},{12,14},{14,12},{16,18},{18,... | collective-permute-start | bytes 1769480 | tf_op jit(solution)/shard_map/ppermute | solution.py:79
  42.6 16.3 %collective-permute-start.19 = (bf16[576,512]{1,0:T(8,128)(2,1)S(1)}, bf16[576,512]{1,0:T(8,128)(2,1)}, u32[]{:S(2)}, u32[]{:S(2)}) collective-permute-start(bf16[576,512]{1,0:T(8,128)(2,1)S(1)} %collective-permute-done.8.refs_2_), channel_id=1, source_target_pairs={{0,2},{2,0},{4,6},{6,4},{8,10},{10,8},{12,14},{14,12},{16,18},{18,... | collective-permute-start | bytes 1769480 | tf_op jit(solution)/shard_map/ppermute | solution.py:79
  44.2 0.6 copy-start.3
  48.0 7.0 %collective-permute-start.16 = (bf16[288,512]{1,0:T(8,128)(2,1)}, bf16[288,512]{1,0:T(8,128)(2,1)}, u32[]{:S(2)}, u32[]{:S(2)}) collective-permute-start(bf16[288,512]{1,0:T(8,128)(2,1)} %slice.7), channel_id=1, source_target_pairs={{0,8},{2,6},{8,16},{10,2},{16,24},{18,10},{24,28},{26,18},{28,20},... | collective-permute-start | bytes 884744 | tf_op jit(solution)/shard_map/ppermute | solution.py:70
  50.1 12.2 %collective-permute-start.21 = (bf16[576,512]{1,0:T(8,128)(2,1)}, bf16[576,512]{1,0:T(8,128)(2,1)}, u32[]{:S(2)}, u32[]{:S(2)}) collective-permute-start(bf16[576,512]{1,0:T(8,128)(2,1)} %collective-permute-done.15.refs_0_), channel_id=1, source_target_pairs={{0,2},{2,0},{4,6},{6,4},{8,10},{10,8},{12,14},{14,12},{16,18},{18,... | collective-permute-start | bytes 1769480 | tf_op jit(solution)/shard_map/ppermute | solution.py:79
  50.1 20.6 %all-to-all-start = ((bf16[16,144,128]{2,1,0:T(8,128)(2,1)}), bf16[16,144,128]{2,1,0:T(8,128)(2,1)S(1)}, u32[]{:S(2)}, u32[]{:S(2)}) async-start(bf16[16,144,128]{2,1,0:T(8,128)(2,1)} %bundle.1), calls=%async_computation | async-start | bytes 1179648 | tf_op jit(solution)/shard_map/all_to_all | solution.py:775
  55.0 7.4 %collective-permute-start.22 = (bf16[288,512]{1,0:T(8,128)(2,1)}, bf16[288,512]{1,0:T(8,128)(2,1)S(1)}, u32[]{:S(2)}, u32[]{:S(2)}) collective-permute-start(bf16[288,512]{1,0:T(8,128)(2,1)} %collective-permute-done.16.refs_2_), channel_id=1, source_target_pairs={{0,2},{2,0},{4,6},{6,4},{8,10},{10,8},{12,14},{14,12},{16,18},{18,... | collective-permute-start | bytes 884744 | tf_op jit(solution)/shard_map/ppermute | solution.py:79
  55.2 0.7 copy-start.4
  57.3 5.1 %collective-permute-start.20 = (bf16[32,1536]{1,0:T(8,128)(2,1)S(1)}, bf16[32,1536]{1,0:T(8,128)(2,1)S(1)}, u32[]{:S(2)}, u32[]{:S(2)}) collective-permute-start(bf16[32,1536]{1,0:T(8,128)(2,1)S(1)} %get-tuple-element.115), channel_id=1, source_target_pairs={{0,1},{1,0},{2,3},{3,2},{4,5},{5,4},{6,7},{7,6},{8,9},{9,8},{10,11... | collective-permute-start | bytes 294920 | tf_op jit(solution)/shard_map/ppermute | solution.py:780
  62.4 8.4 %copy-start = (bf16[512,4,128]{2,1,0:T(4,128)(2,1)S(1)}, bf16[512,4,128]{2,1,0:T(4,128)(2,1)}, u32[]{:S(2)}) copy-start(bf16[512,4,128]{2,1,0:T(4,128)(2,1)} %param.25) | copy-start | bytes 1572868
  64.9 4.7 %collective-permute-start.23 = (bf16[32,1536]{1,0:T(8,128)(2,1)S(1)}, bf16[32,1536]{1,0:T(8,128)(2,1)S(1)}, u32[]{:S(2)}, u32[]{:S(2)}) collective-permute-start(bf16[32,1536]{1,0:T(8,128)(2,1)S(1)} %get-tuple-element.123), channel_id=1, source_target_pairs={{0,1},{1,0},{2,3},{3,2},{4,5},{5,4},{6,7},{7,6},{8,9},{9,8},{10,11... | collective-permute-start | bytes 294920 | tf_op jit(solution)/shard_map/ppermute | solution.py:787

commit v15 on v14

--- a/solution.py
+++ b/solution.py
@@ -54,6 +54,24 @@
     return listed + [block(side, count // 2)[0], block(1 - side, count // 2)[0]]
 
 
+def cut_kernel(whole, out, sem):
+    copy = pltpu.make_async_copy(whole.at[pl.ds(0, out.shape[0]), :], out, sem)
+    copy.start()
+    copy.wait()
+
+
+def cut(whole, rows):
+    return pl.pallas_call(
+        cut_kernel,
+        out_shape=jax.ShapeDtypeStruct((rows, whole.shape[1]), whole.dtype),
+        in_specs=[pl.BlockSpec(memory_space=pl.ANY)],
+        out_specs=pl.BlockSpec(memory_space=pl.ANY),
+        scratch_shapes=[pltpu.SemaphoreType.DMA],
+        cost_estimate=pl.CostEstimate(flops=1, bytes_accessed=1, transcendentals=0),
+        name="cut",
+    )(whole)
+
+
 class Ring:
     def __init__(self, pair, groups):
         self.across = functools.partial(lax.ppermute, axis_name="grp", perm=ring_pairs(groups))
@@ -66,7 +84,7 @@
     def step(self):
         held = self.mine[-1]
         if len(self.mine) > self.full:
-            held = held[: self.unit_rows]
+            held = cut(held, self.unit_rows)
         self.mine.append(self.across(held))
 
     def pin(self, *others):
@@ -476,7 +494,7 @@
         in_specs=[VMEM] * 4,
         out_specs=(VMEM,) * 3,
         compiler_params=PARAMS,
-        cost_estimate=reads(10 * mine.shape[0] * mine.shape[1]),
+        cost_estimate=reads(16 << 20),
         name="route",
     )(mine, arrived, gain, place)
 
@@ -497,19 +515,7 @@
     small = fetch([(router_in, router), (ids_in, ids)], sems)
     width = parts[0].shape[1]
     pieces, unit_rows = expert_pieces(gate_up, down, up_rows, down_rows, width)
-    sources = ring_sources(groups, lax.axis_index("grp"))
-    pairs = []
-    for part, shard in zip(parts, shards):
-        for unit in range(part.shape[0] // unit_rows):
-            for first, rows, target, lane in pieces:
-                at = pl.multiple_of(sources[shard + unit] * rows, rows)
-                pairs.append(
-                    (
-                        part.at[pl.ds(unit * unit_rows + first, rows), :],
-                        target.at[pl.ds(at, rows), pl.ds(lane, width)],
-                    )
-                )
-    copies = fetch(pairs, part_sems)
+    copies = fetch(part_copies(groups, parts, shards, unit_rows, pieces), part_sems)
     cap = own.shape[0]
     own[...] = jnp.dot(place[:cap, :], moe_in[...], preferred_element_type=f32).astype(bf16)
     tokens = ids.shape[1]
@@ -558,18 +564,39 @@
     )(moe_in, *far, place, *[part for part, _ in early])
 
 
+def part_copies(groups, parts, shards, unit_rows, pieces):
+    sources = ring_sources(groups, lax.axis_index("grp"))
+    pairs = []
+    for part, shard in zip(parts, shards):
+        for unit in range(part.shape[0] // unit_rows):
+            for first, rows, target, lane in pieces:
+                at = pl.multiple_of(sources[shard + unit] * rows, rows)
+                pairs.append(
+                    (
+                        part.at[pl.ds(unit * unit_rows + first, rows), :],
+                        target.at[pl.ds(at, rows), pl.ds(lane, part.shape[1])],
+                    )
+                )
+    return pairs
+
+
 def expert_kernel(groups, up_rows, down_rows, shards, own, other, gate_up_in, down_in, *refs):
     parts = refs[: len(shards)]
-    own_out, other_out, gate_up, down, rows = refs[len(shards) :]
+    own_out, other_out, gate_up, down, rows, sems, down_sems = refs[len(shards) :]
     width = parts[0].shape[1]
+    pieces, unit_rows = expert_pieces(gate_up, down, up_rows, down_rows, width)
+    ups = fetch(part_copies(groups, parts, shards, unit_rows, pieces[:2]), sems)
+    downs = fetch(part_copies(groups, parts, shards, unit_rows, pieces[2:]), down_sems)
     count = own.shape[0]
     rows[:count, :] = own[...]
     rows[count:, :] = other[...]
-    pieces, unit_rows = expert_pieces(gate_up, down, up_rows, down_rows, width)
-    place_parts(groups, parts, unit_rows, pieces, shards)
+    for copy in ups:
+        copy.wait()
     both = jnp.dot(rows[...], gate_up[...], preferred_element_type=f32)
     gate, up = both[:, :width], both[:, width:]
     hidden = (gate / (1.0 + jnp.exp(-gate)) * up).astype(bf16)
+    for copy in downs:
+        copy.wait()
     made = jnp.dot(hidden, down[...], preferred_element_type=f32).astype(bf16)
     own_out[...] = made[:count, :]
     other_out[...] = made[count:, :]
@@ -578,16 +605,21 @@
 def expert(groups, own, other, staged, late, up_rows, down_rows):
     count, model = own.shape
     width = late[0][0].shape[1]
+    units = sum(part.shape[0] for part, _ in late) // (2 * up_rows + model // width * down_rows)
     return pl.pallas_call(
         functools.partial(expert_kernel, groups, up_rows, down_rows, [shard for _, shard in late]),
         out_shape=(jax.ShapeDtypeStruct(own.shape, bf16),) * 2
         + tuple(jax.ShapeDtypeStruct(part.shape, bf16) for part in staged),
-        in_specs=[VMEM] * (4 + len(late)),
+        in_specs=[VMEM] * 4 + [ANY] * len(late),
         out_specs=(VMEM,) * 4,
-        scratch_shapes=[pltpu.VMEM((2 * count, model), bf16)],
+        scratch_shapes=[
+            pltpu.VMEM((2 * count, model), bf16),
+            pltpu.SemaphoreType.DMA((2 * units,)),
+            pltpu.SemaphoreType.DMA((model // width * units,)),
+        ],
         input_output_aliases={2: 2, 3: 3},
         compiler_params=PARAMS,
-        cost_estimate=takes(6.2),
+        cost_estimate=pl.CostEstimate(flops=int(6.2 * 1.15e9), bytes_accessed=1, transcendentals=0),
         name="expert",
     )(own, other, *staged, *[part for part, _ in late])[:2]
 
@@ -738,7 +770,7 @@
     cosine, sine, past, place, send, tags, gain = prepare(
         groups, slots_dev, positions, cache_slot, expert_ids, attn_gain
     )
-    other_tokens, cosine, flat_kv = out_ring.pin(other_tokens, cosine, flat_kv)
+    cosine, flat_kv = out_ring.pin(cosine, flat_kv)
     out_ring.step()
 
     q, kv, tail = project(tokens, other_tokens, gain, cosine, sine, w_query, flat_kv)

time: 72.8 us -> 84.9 us (1.17)
  Pallas kernels: 20 us -> 36.8 us
  waiting for transfers between devices: 15.6 us -> 13.4 us
  local copies, waits for them, and re-layouts: 4.84 us -> 3.54 us
  starting transfers between devices: 31 us -> 29.9 us
    pallas_call x0 -> x2, Pallas kernels: none -> 15.6 us  [cut(): pl.pallas_call(cut_kernel, out_shape=jax.ShapeDtypeStruct((rows, whole.sh...]
    ppermute x1, waiting for transfers between devices: 2.11 us -> 0.27 us  [two_lane_shards(): other_tokens = swap(tokens)]
    slice x2 -> x0, local copies, waits for them, and re-layouts: 1.71 us -> none  [step(): held = held[:self.unit_rows]]
    ppermute x8, starting transfers between devices: 15.2 us -> 13.5 us  [step(): self.mine.append(self.across(held))]
    unnamed x13 -> x21, local copies, waits for them, and re-layouts: 3.13 us -> 3.54 us
  transfers between devices with their start and end apart: 25 -> 25, of which waited for: 8 -> 11; matrix products, arithmetic and copies ran while one was open for 5% -> 2% of each run, Pallas kernels for 26% -> 42%
where the time goes in v15:
time: 84.9 us; the launch traced here: 84.4 us
  Pallas kernels  36.8 us (43%)
  starting transfers between devices  29.9 us (35%)
  waiting for transfers between devices  13.4 us (16%)
  local copies, waits for them, and re-layouts  3.54 us (4%)
  between operations  0.86 us (1%)
    pallas_call x2, Pallas kernels, cut(): pl.pallas_call(cut_kernel, out_shape=jax.ShapeDtypeStruct((rows, whole.sh...  15.6 us
    ppermute x8, starting transfers between devices, step(): self.mine.append(self.across(held))  13.5 us
    ppermute x8, waiting for transfers between devices, step(): self.mine.append(self.across(held))  7.51 us
    all_to_all x1, starting transfers between devices, two_lane_shards(): lax.all_to_all(outgoing, 'grp', split_axis=0, concat_axis=0, tiled=True)  5.23 us
    unnamed x21, local copies, waits for them, and re-layouts  3.54 us
    ppermute x1, waiting for transfers between devices, two_lane_shards(): returned = swap(back)  3.01 us
    pallas_call x1, Pallas kernels, expert(): pl.pallas_call(functools.partial(expert_kernel, groups, up_rows, down_row...  2.7 us
    ppermute x1, starting transfers between devices, two_lane_shards(): other_tokens = swap(tokens)  2.56 us
  transfers between devices with their start and end apart: 25, of which 11 were waited for; matrix products, arithmetic and copies ran while one was open for 2% of the time, Pallas kernels for 42%

profile of v15, /device:TPU:0, one launch (start us, length us, event | category | flops | bytes accessed | tf_op | source)
XLA Modules:
  0.0 84.4 jit_solution(13516415729491827851)
XLA Ops:
  1.7 2.6 %collective-permute-start.4 = (bf16[128,1536]{1,0:T(8,128)(2,1)}, bf16[128,1536]{1,0:T(8,128)(2,1)S(1)}, u32[]{:S(2)}, u32[]{:S(2)}) collective-permute-start(bf16[128,1536]{1,0:T(8,128)(2,1)} %tokens.1), channel_id=1, source_target_pairs={{0,1},{1,0},{2,3},{3,2},{4,5},{5,4},{6,7},{7,6},{8,9},{9,8},{10,11... | collective-permute-start | bytes 1179656 | tf_op jit(solution)/shard_map/ppermute | solution.py:759
  5.4 1.7 %collective-permute-start.5 = (bf16[192,768]{1,0:T(8,128)(2,1)S(1)}, bf16[192,768]{1,0:T(8,128)(2,1)S(1)}, u32[]{:S(2)}, u32[]{:S(2)}) collective-permute-start(bf16[192,768]{1,0:T(8,128)(2,1)S(1)} %get-tuple-element.65.refs_0_), channel_id=1, source_target_pairs={{0,8},{2,6},{8,16},{10,2},{16,24},{18,10},{24,28},{26,18},{28,20},... | collective-permute-start | bytes 884744 | tf_op jit(solution)/shard_map/ppermute | solution.py:88
  7.1 1.6 %collective-permute-start.3 = (bf16[576,512]{1,0:T(8,128)(2,1)S(1)}, bf16[576,512]{1,0:T(8,128)(2,1)}, u32[]{:S(2)}, u32[]{:S(2)}) collective-permute-start(bf16[576,512]{1,0:T(8,128)(2,1)S(1)} %get-tuple-element.64.refs_0_), channel_id=1, source_target_pairs={{0,8},{2,6},{8,16},{10,2},{16,24},{18,10},{24,28},{26,18},{28,20},... | collective-permute-start | bytes 1769480 | tf_op jit(solution)/shard_map/ppermute | solution.py:88
  8.7 1.5 %prepare.1 = (f32[256,128]{1,0:T(8,128)S(1)}, f32[256,128]{1,0:T(8,128)S(1)}, f32[256,128]{1,0:T(8,128)S(1)}, bf16[64,128]{1,0:T(8,128)(2,1)S(1)}, bf16[512,256]...) custom-call(s32[1,256]{1,0:T(1,128)} %bitcast.26, s32[1,256]{1,0:T(1,128)} %bitcast.27, ...), custom_call_target="tpu_custom_call" | custom-call | flops 1 | bytes 1 | tf_op jit(solution)/shard_map/prepare/pallas_call | solution.py:284
  10.2 1.8 %copy.19 = bf16[192,8,4,128]{3,1,2,0:T(8,128)(2,1)S(1)} copy(bf16[192,8,4,128]{3,2,1,0:T(4,128)(2,1)} %bitcast.15) | data formatting | bytes 3145728
  12.2 1.7 %collective-permute-start.7 = (bf16[192,768]{1,0:T(8,128)(2,1)S(1)}, bf16[192,768]{1,0:T(8,128)(2,1)S(1)}, u32[]{:S(2)}, u32[]{:S(2)}) collective-permute-start(bf16[192,768]{1,0:T(8,128)(2,1)S(1)} %collective-permute-done.5.refs_1_), channel_id=1, source_target_pairs={{0,8},{2,6},{8,16},{10,2},{16,24},{18,10},{24,28},{26,18},{28,20},... | collective-permute-start | bytes 884744 | tf_op jit(solution)/shard_map/ppermute | solution.py:88
  14.1 2.2 %project.1 = (bf16[256,768]{1,0:T(8,128)(2,1)S(1)}, bf16[256,512]{1,0:T(8,128)(2,1)S(1)}, bf16[128,512]{1,0:T(8,128)(2,1)S(1)}) custom-call(bf16[128,1536]{1,0:T(8,128)(2,1)S(1)} %copy-done.6, bf16[128,1536]{1,0:T(8,128)(2,1)S(1)} %collective-permute-done.4.other, f32[1,1536]{1,0:T(1,128)S(1)} %get-tuple-element.67.gain, ...), custom_call_target="tpu_custom_call" | custom-call | flops 9200000000 | bytes 64000000 | tf_op jit(solution)/shard_map/project/pallas_call | solution.py:334
  16.4 1.9 %collective-permute-start.6 = (bf16[128,512]{1,0:T(8,128)(2,1)S(1)}, bf16[128,512]{1,0:T(8,128)(2,1)S(1)}, u32[]{:S(2)}, u32[]{:S(2)}) collective-permute-start(bf16[128,512]{1,0:T(8,128)(2,1)S(1)} %get-tuple-element.73), channel_id=1, source_target_pairs={{0,2},{2,4},{4,6},{6,8},{8,10},{10,12},{12,14},{14,16},{16,18},{18... | collective-permute-start | bytes 393224 | tf_op jit(solution)/shard_map/ppermute | solution.py:777
  18.2 3.4 %collective-permute-done.7.refs_2_ = bf16[192,768]{1,0:T(8,128)(2,1)S(1)} collective-permute-done((bf16[192,768]{1,0:T(8,128)(2,1)S(1)}, bf16[192,768]{1,0:T(8,128)(2,1)S(1)}, u32[]{:S(2)}, u32[]{:S(2)}) %collective-permute-start.7) | collective-permute-done | bytes 294944 | tf_op jit(solution)/shard_map/ppermute | solution.py:88
  21.7 1.7 %collective-permute-start.9 = (bf16[192,768]{1,0:T(8,128)(2,1)S(1)}, bf16[192,768]{1,0:T(8,128)(2,1)S(1)}, u32[]{:S(2)}, u32[]{:S(2)}) collective-permute-start(bf16[192,768]{1,0:T(8,128)(2,1)S(1)} %collective-permute-done.7.refs_2_), channel_id=1, source_target_pairs={{0,8},{2,6},{8,16},{10,2},{16,24},{18,10},{24,28},{26,18},{28,20},... | collective-permute-start | bytes 884744 | tf_op jit(solution)/shard_map/ppermute | solution.py:88
  23.4 1.3 %attend_late.1.late = bf16[128,768]{1,0:T(8,128)(2,1)S(1)} custom-call(bf16[256,768]{1,0:T(8,128)(2,1)S(1)} %get-tuple-element.76.q, bf16[256,512]{1,0:T(8,128)(2,1)S(1)} %get-tuple-element.90.kv, f32[256,128]{1,0:T(8,128)S(1)} %get-tuple-element.78.past), custom_call_target="tpu_custom_call" | custom-call | flops 2300000000 | bytes 16000000 | tf_op jit(solution)/shard_map/attend_late/pallas_call | solution.py:390
  24.7 1.6 %collective-permute-start.8 = (bf16[576,512]{1,0:T(8,128)(2,1)}, bf16[576,512]{1,0:T(8,128)(2,1)}, u32[]{:S(2)}, u32[]{:S(2)}) collective-permute-start(bf16[576,512]{1,0:T(8,128)(2,1)} %collective-permute-done.3.refs_1_), channel_id=1, source_target_pairs={{0,8},{2,6},{8,16},{10,2},{16,24},{18,10},{24,28},{26,18},{28,20},... | collective-permute-start | bytes 1769480 | tf_op jit(solution)/shard_map/ppermute | solution.py:88
  26.3 1.5 %attend_early.1.early = bf16[128,768]{1,0:T(8,128)(2,1)S(1)} custom-call(bf16[256,768]{1,0:T(8,128)(2,1)S(1)} %get-tuple-element.76.q, bf16[256,512]{1,0:T(8,128)(2,1)S(1)} %get-tuple-element.90.kv, bf16[128,512]{1,0:T(8,128)(2,1)S(1)} %collective-permute-done.6.seam, f32[256,128]{1,0:T(8,128)S(1)} %get-tuple-element.78.past), custom_call_target="tpu_custom_call" | custom-call | flops 2300000000 | bytes 16000000 | tf_op jit(solution)/shard_map/attend_early/pallas_call | solution.py:402
  29.1 5.6 %cut.2 = bf16[96,768]{1,0:T(8,128)(2,1)} custom-call(bf16[192,768]{1,0:T(8,128)(2,1)} %copy-done), custom_call_target="tpu_custom_call" | custom-call | flops 1 | bytes 1 | tf_op jit(solution)/shard_map/cut/pallas_call | solution.py:64
  34.7 1.7 %collective-permute-start.12 = (bf16[96,768]{1,0:T(8,128)(2,1)}, bf16[96,768]{1,0:T(8,128)(2,1)S(1)}, u32[]{:S(2)}, u32[]{:S(2)}) collective-permute-start(bf16[96,768]{1,0:T(8,128)(2,1)} %cut.2), channel_id=1, source_target_pairs={{0,8},{2,6},{8,16},{10,2},{16,24},{18,10},{24,28},{26,18},{28,20},... | collective-permute-start | bytes 442376 | tf_op jit(solution)/shard_map/ppermute | solution.py:88
  36.4 1.4 %bundle.1 = bf16[16,144,128]{2,1,0:T(8,128)(2,1)} custom-call(bf16[512,256]{1,0:T(8,128)(2,1)S(1)} %get-tuple-element.89.send, bf16[256,512]{1,0:T(8,128)(2,1)S(1)} %get-tuple-element.90.kv, bf16[256,128]{1,0:T(8,128)(2,1)S(1)} %get-tuple-element.91.tags), custom_call_target="tpu_custom_call" | custom-call | flops 1 | bytes 1 | tf_op jit(solution)/shard_map/bundle/pallas_call | solution.py:676
  37.8 2.2 %collective-permute-done.12.refs_7_ = bf16[96,768]{1,0:T(8,128)(2,1)S(1)} collective-permute-done((bf16[96,768]{1,0:T(8,128)(2,1)}, bf16[96,768]{1,0:T(8,128)(2,1)S(1)}, u32[]{:S(2)}, u32[]{:S(2)}) %collective-permute-start.12) | collective-permute-done | bytes 147488 | tf_op jit(solution)/shard_map/ppermute | solution.py:88
  40.1 1.7 %collective-permute-start.15 = (bf16[576,512]{1,0:T(8,128)(2,1)}, bf16[576,512]{1,0:T(8,128)(2,1)}, u32[]{:S(2)}, u32[]{:S(2)}) collective-permute-start(bf16[576,512]{1,0:T(8,128)(2,1)} %collective-permute-done.8.refs_2_), channel_id=1, source_target_pairs={{0,8},{2,6},{8,16},{10,2},{16,24},{18,10},{24,28},{26,18},{28,20},... | collective-permute-start | bytes 1769480 | tf_op jit(solution)/shard_map/ppermute | solution.py:88
  41.8 1.4 %collective-permute-done.14.refs_8_ = bf16[96,768]{1,0:T(8,128)(2,1)S(1)} collective-permute-done((bf16[96,768]{1,0:T(8,128)(2,1)S(1)}, bf16[96,768]{1,0:T(8,128)(2,1)S(1)}, u32[]{:S(2)}, u32[]{:S(2)}) %collective-permute-start.14) | collective-permute-done | bytes 147488 | tf_op jit(solution)/shard_map/ppermute | solution.py:97
  44.1 1.9 %outward_send.1 = bf16[128,1536]{1,0:T(8,128)(2,1)} custom-call(bf16[128,768]{1,0:T(8,128)(2,1)S(1)} %attend_early.1.early, bf16[128,768]{1,0:T(8,128)(2,1)S(1)} %attend_late.1.late, bf16[192,768]{1,0:T(8,128)(2,1)S(1)} %get-tuple-element.65.refs_0_, bf16[192,768]{1,0:T(8,128)(2,1)S(1)} %collective-permute-done.5.refs_1_, ...), custom_call_target="tpu_custom_call" | custom-call | flops 1 | bytes 2359296 | tf_op jit(solution)/shard_map/outward_send/pallas_call | solution.py:444
  46.0 1.5 %collective-permute-start.17 = (bf16[128,1536]{1,0:T(8,128)(2,1)}, bf16[128,1536]{1,0:T(8,128)(2,1)}, u32[]{:S(2)}, u32[]{:S(2)}) collective-permute-start(bf16[128,1536]{1,0:T(8,128)(2,1)} %outward_send.1), channel_id=1, source_target_pairs={{0,1},{1,0},{2,3},{3,2},{4,5},{5,4},{6,7},{7,6},{8,9},{9,8},{10,11... | collective-permute-start | bytes 1179656 | tf_op jit(solution)/shard_map/ppermute | solution.py:798
  48.0 1.2 %outward_keep.1 = (f32[128,1536]{1,0:T(8,128)S(1)}, f32[1,1536]{1,0:T(1,128)S(1)}) custom-call(bf16[128,768]{1,0:T(8,128)(2,1)S(1)} %attend_early.1.early, bf16[128,768]{1,0:T(8,128)(2,1)S(1)} %attend_late.1.late, bf16[128,1536]{1,0:T(8,128)(2,1)S(1)} %copy-done.7, f32[1536]{0:T(1024)S(1)} %copy-done.8, bf16[192,768]{1,0:T(8,128)(2,1)S(1)} %get-tuple-element.65.refs_0_, ...), custom_call_target="tpu_custom_call" | custom-call | flops 1 | bytes 2359296 | tf_op jit(solution)/shard_map/outward_keep/pallas_call | solution.py:458
  50.3 10.0 %cut.3 = bf16[288,512]{1,0:T(8,128)(2,1)} custom-call(bf16[576,512]{1,0:T(8,128)(2,1)} %collective-permute-done.15.whole.refs_0_), custom_call_target="tpu_custom_call" | custom-call | flops 1 | bytes 1 | tf_op jit(solution)/shard_map/cut/pallas_call | solution.py:64
  60.3 1.7 %collective-permute-start.16 = (bf16[288,512]{1,0:T(8,128)(2,1)}, bf16[288,512]{1,0:T(8,128)(2,1)}, u32[]{:S(2)}, u32[]{:S(2)}) collective-permute-start(bf16[288,512]{1,0:T(8,128)(2,1)} %cut.3), channel_id=1, source_target_pairs={{0,8},{2,6},{8,16},{10,2},{16,24},{18,10},{24,28},{26,18},{28,20},... | collective-permute-start | bytes 884744 | tf_op jit(solution)/shard_map/ppermute | solution.py:88
  62.1 5.2 %all-to-all-start = ((bf16[16,144,128]{2,1,0:T(8,128)(2,1)}), bf16[16,144,128]{2,1,0:T(8,128)(2,1)S(1)}, u32[]{:S(2)}, u32[]{:S(2)}) async-start(bf16[16,144,128]{2,1,0:T(8,128)(2,1)} %bundle.1), calls=%async_computation | async-start | bytes 1179648 | tf_op jit(solution)/shard_map/all_to_all | solution.py:807
  67.8 1.4 %route.1 = (bf16[128,1536]{1,0:T(8,128)(2,1)S(1)}, bf16[128,1536]{1,0:T(8,128)(2,1)S(1)}, bf16[32,1536]{1,0:T(8,128)(2,1)S(1)}) custom-call(f32[128,1536]{1,0:T(8,128)S(1)} %get-tuple-element.101.mine, bf16[128,1536]{1,0:T(8,128)(2,1)} %collective-permute-done.17.arrived, f32[1,1536]{1,0:T(1,128)S(1)} %get-tuple-element.107.gain, ...), custom_call_target="tpu_custom_call" | custom-call | flops 1 | bytes 16777216 | tf_op jit(solution)/shard_map/route/pallas_call | solution.py:487
  69.2 1.6 %collective-permute-start.20 = (bf16[32,1536]{1,0:T(8,128)(2,1)S(1)}, bf16[32,1536]{1,0:T(8,128)(2,1)S(1)}, u32[]{:S(2)}, u32[]{:S(2)}) collective-permute-start(bf16[32,1536]{1,0:T(8,128)(2,1)S(1)} %get-tuple-element.113), channel_id=1, source_target_pairs={{0,1},{1,0},{2,3},{3,2},{4,5},{5,4},{6,7},{7,6},{8,9},{9,8},{10,11... | collective-permute-start | bytes 294920 | tf_op jit(solution)/shard_map/ppermute | solution.py:812
  70.8 2.4 %gate.1 = (f32[128,40]{1,0:T(8,128)S(1)}, bf16[32,1536]{1,0:T(8,128)(2,1)S(1)}, bf16[128,64]{1,0:T(8,128)(2,1)S(1)}, bf16[1536,1024]{1,0:T(8,128)(2,1)S(1)}, bf16[512,1536]{1,0:T(8,128)(2,1)S(1)}) custom-call(bf16[128,1536]{1,0:T(8,128)(2,1)S(1)} %get-tuple-element.110.moe_in, bf16[40,1536]{1,0:T(8,128)(2,1)} %bitcast.21, s32[8,128]{1,0:T(8,128)} %bitcast.25, ...), custom_call_target="tpu_custom_call" | custom-call | flops 1 | bytes 1 | tf_op jit(solution)/shard_map/gate/pallas_call | solution.py:544
  74.1 2.7 %expert.1 = (bf16[32,1536]{1,0:T(8,128)(2,1)S(1)}, bf16[32,1536]{1,0:T(8,128)(2,1)S(1)}, bf16[1536,1024]{1,0:T(8,128)(2,1)S(1)}, bf16[512,1536]{1,0:T(8,128)(2,1)S(1)}) custom-call(bf16[32,1536]{1,0:T(8,128)(2,1)S(1)} %get-tuple-element.115.own, bf16[32,1536]{1,0:T(8,128)(2,1)S(1)} %collective-permute-done.20.other, ...), custom_call_target="tpu_custom_call", output_to_operand_aliasing={{2}: (2, {}), {3}: (3, {})} | custom-call | flops 7129999872 | bytes 1 | tf_op jit(solution)/shard_map/expert/pallas_call | solution.py:609
  76.8 1.7 %collective-permute-start.23 = (bf16[32,1536]{1,0:T(8,128)(2,1)S(1)}, bf16[32,1536]{1,0:T(8,128)(2,1)S(1)}, u32[]{:S(2)}, u32[]{:S(2)}) collective-permute-start(bf16[32,1536]{1,0:T(8,128)(2,1)S(1)} %get-tuple-element.121), channel_id=1, source_target_pairs={{0,1},{1,0},{2,3},{3,2},{4,5},{5,4},{6,7},{7,6},{8,9},{9,8},{10,11... | collective-permute-start | bytes 294920 | tf_op jit(solution)/shard_map/ppermute | solution.py:819
  78.5 3.0 %collective-permute-done.23.returned = bf16[32,1536]{1,0:T(8,128)(2,1)S(1)} collective-permute-done((bf16[32,1536]{1,0:T(8,128)(2,1)S(1)}, bf16[32,1536]{1,0:T(8,128)(2,1)S(1)}, u32[]{:S(2)}, u32[]{:S(2)}) %collective-permute-start.23) | collective-permute-done | bytes 98336 | tf_op jit(solution)/shard_map/ppermute | solution.py:819
  82.9 1.5 %write.1 = bf16[2048,128]{1,0:T(8,128)(2,1)} custom-call(bf16[16,144,128]{2,1,0:T(8,128)(2,1)S(1)} %all-to-all-done.arrived, bf16[2048,128]{1,0:T(8,128)(2,1)S(1)} %bitcast.14), custom_call_target="tpu_custom_call" | custom-call | flops 1 | bytes 2097152 | tf_op jit(solution)/shard_map/write/pallas_call | solution.py:717
  (54 shorter events, 9.2 us)
Async XLA Ops:
  0.6 3.6 %collective-permute-start.2 = (bf16[96,1536]{1,0:T(8,128)(2,1)}, bf16[96,1536]{1,0:T(8,128)(2,1)S(1)}, u32[]{:S(2)}, u32[]{:S(2)}) collective-permute-start(bf16[96,1536]{1,0:T(8,128)(2,1)} %bitcast.17), channel_id=1, source_target_pairs={{0,2},{2,0},{4,6},{6,4},{8,10},{10,8},{12,14},{14,12},{16,18},{18,... | collective-permute-start | bytes 884744 | tf_op jit(solution)/shard_map/ppermute | solution.py:762
  1.1 3.1 %collective-permute-start = (bf16[96,1024]{1,0:T(8,128)(2,1)}, bf16[96,1024]{1,0:T(8,128)(2,1)S(1)}, u32[]{:S(2)}, u32[]{:S(2)}) collective-permute-start(bf16[96,1024]{1,0:T(8,128)(2,1)} %bitcast.19), channel_id=1, source_target_pairs={{0,2},{2,0},{4,6},{6,4},{8,10},{10,8},{12,14},{14,12},{16,18},{18,... | collective-permute-start | bytes 589832 | tf_op jit(solution)/shard_map/ppermute | solution.py:762
  1.2 3.0 %collective-permute-start.1 = (bf16[32,1536]{1,0:T(8,128)(2,1)}, bf16[32,1536]{1,0:T(8,128)(2,1)S(1)}, u32[]{:S(2)}, u32[]{:S(2)}) collective-permute-start(bf16[32,1536]{1,0:T(8,128)(2,1)} %bitcast.22), channel_id=1, source_target_pairs={{0,2},{2,0},{4,6},{6,4},{8,10},{10,8},{12,14},{14,12},{16,18},{18,... | collective-permute-start | bytes 294920 | tf_op jit(solution)/shard_map/ppermute | solution.py:762
  1.7 12.5 %collective-permute-start.4 = (bf16[128,1536]{1,0:T(8,128)(2,1)}, bf16[128,1536]{1,0:T(8,128)(2,1)S(1)}, u32[]{:S(2)}, u32[]{:S(2)}) collective-permute-start(bf16[128,1536]{1,0:T(8,128)(2,1)} %tokens.1), channel_id=1, source_target_pairs={{0,1},{1,0},{2,3},{3,2},{4,5},{5,4},{6,7},{7,6},{8,9},{9,8},{10,11... | collective-permute-start | bytes 1179656 | tf_op jit(solution)/shard_map/ppermute | solution.py:759
  5.4 6.7 %copy-start.3 = (bf16[576,512]{1,0:T(8,128)(2,1)}, bf16[576,512]{1,0:T(8,128)(2,1)S(1)}, u32[]{:S(2)}) copy-start(bf16[576,512]{1,0:T(8,128)(2,1)S(1)} %get-tuple-element.64.refs_0_) | copy-start | bytes 1769476
  5.4 6.8 %collective-permute-start.5 = (bf16[192,768]{1,0:T(8,128)(2,1)S(1)}, bf16[192,768]{1,0:T(8,128)(2,1)S(1)}, u32[]{:S(2)}, u32[]{:S(2)}) collective-permute-start(bf16[192,768]{1,0:T(8,128)(2,1)S(1)} %get-tuple-element.65.refs_0_), channel_id=1, source_target_pairs={{0,8},{2,6},{8,16},{10,2},{16,24},{18,10},{24,28},{26,18},{28,20},... | collective-permute-start | bytes 884744 | tf_op jit(solution)/shard_map/ppermute | solution.py:88
  7.1 17.6 %collective-permute-start.3 = (bf16[576,512]{1,0:T(8,128)(2,1)S(1)}, bf16[576,512]{1,0:T(8,128)(2,1)}, u32[]{:S(2)}, u32[]{:S(2)}) collective-permute-start(bf16[576,512]{1,0:T(8,128)(2,1)S(1)} %get-tuple-element.64.refs_0_), channel_id=1, source_target_pairs={{0,8},{2,6},{8,16},{10,2},{16,24},{18,10},{24,28},{26,18},{28,20},... | collective-permute-start | bytes 1769480 | tf_op jit(solution)/shard_map/ppermute | solution.py:88
  10.2 4.0 %copy-start.6 = (bf16[128,1536]{1,0:T(8,128)(2,1)S(1)}, bf16[128,1536]{1,0:T(8,128)(2,1)}, u32[]{:S(2)}) copy-start(bf16[128,1536]{1,0:T(8,128)(2,1)} %tokens.1) | copy-start | bytes 1179652
  12.2 15.6 %collective-permute-start.10 = (bf16[192,768]{1,0:T(8,128)(2,1)S(1)}, bf16[192,768]{1,0:T(8,128)(2,1)S(1)}, u32[]{:S(2)}, u32[]{:S(2)}) collective-permute-start(bf16[192,768]{1,0:T(8,128)(2,1)S(1)} %collective-permute-done.5.refs_1_), channel_id=1, source_target_pairs={{0,2},{2,0},{4,6},{6,4},{8,10},{10,8},{12,14},{14,12},{16,18},{18,... | collective-permute-start | bytes 884744 | tf_op jit(solution)/shard_map/ppermute | solution.py:97
  12.2 9.5 %collective-permute-start.7 = (bf16[192,768]{1,0:T(8,128)(2,1)S(1)}, bf16[192,768]{1,0:T(8,128)(2,1)S(1)}, u32[]{:S(2)}, u32[]{:S(2)}) collective-permute-start(bf16[192,768]{1,0:T(8,128)(2,1)S(1)} %collective-permute-done.5.refs_1_), channel_id=1, source_target_pairs={{0,8},{2,6},{8,16},{10,2},{16,24},{18,10},{24,28},{26,18},{28,20},... | collective-permute-start | bytes 884744 | tf_op jit(solution)/shard_map/ppermute | solution.py:88
  16.4 8.3 %collective-permute-start.6 = (bf16[128,512]{1,0:T(8,128)(2,1)S(1)}, bf16[128,512]{1,0:T(8,128)(2,1)S(1)}, u32[]{:S(2)}, u32[]{:S(2)}) collective-permute-start(bf16[128,512]{1,0:T(8,128)(2,1)S(1)} %get-tuple-element.73), channel_id=1, source_target_pairs={{0,2},{2,4},{4,6},{6,8},{8,10},{10,12},{12,14},{14,16},{16,18},{18... | collective-permute-start | bytes 393224 | tf_op jit(solution)/shard_map/ppermute | solution.py:777
  21.7 6.2 %collective-permute-start.11 = (bf16[192,768]{1,0:T(8,128)(2,1)S(1)}, bf16[192,768]{1,0:T(8,128)(2,1)S(1)}, u32[]{:S(2)}, u32[]{:S(2)}) collective-permute-start(bf16[192,768]{1,0:T(8,128)(2,1)S(1)} %collective-permute-done.7.refs_2_), channel_id=1, source_target_pairs={{0,2},{2,0},{4,6},{6,4},{8,10},{10,8},{12,14},{14,12},{16,18},{18,... | collective-permute-start | bytes 884744 | tf_op jit(solution)/shard_map/ppermute | solution.py:97
  21.7 6.7 %collective-permute-start.9 = (bf16[192,768]{1,0:T(8,128)(2,1)S(1)}, bf16[192,768]{1,0:T(8,128)(2,1)S(1)}, u32[]{:S(2)}, u32[]{:S(2)}) collective-permute-start(bf16[192,768]{1,0:T(8,128)(2,1)S(1)} %collective-permute-done.7.refs_2_), channel_id=1, source_target_pairs={{0,8},{2,6},{8,16},{10,2},{16,24},{18,10},{24,28},{26,18},{28,20},... | collective-permute-start | bytes 884744 | tf_op jit(solution)/shard_map/ppermute | solution.py:88
  24.7 15.4 %collective-permute-start.8 = (bf16[576,512]{1,0:T(8,128)(2,1)}, bf16[576,512]{1,0:T(8,128)(2,1)}, u32[]{:S(2)}, u32[]{:S(2)}) collective-permute-start(bf16[576,512]{1,0:T(8,128)(2,1)} %collective-permute-done.3.refs_1_), channel_id=1, source_target_pairs={{0,8},{2,6},{8,16},{10,2},{16,24},{18,10},{24,28},{26,18},{28,20},... | collective-permute-start | bytes 1769480 | tf_op jit(solution)/shard_map/ppermute | solution.py:88
  28.4 8.0 %collective-permute-start.13 = (bf16[192,768]{1,0:T(8,128)(2,1)S(1)}, bf16[192,768]{1,0:T(8,128)(2,1)S(1)}, u32[]{:S(2)}, u32[]{:S(2)}) collective-permute-start(bf16[192,768]{1,0:T(8,128)(2,1)S(1)} %collective-permute-done.9.whole.refs_3_), channel_id=1, source_target_pairs={{0,2},{2,0},{4,6},{6,4},{8,10},{10,8},{12,14},{14,12},{16,18},{18,... | collective-permute-start | bytes 884744 | tf_op jit(solution)/shard_map/ppermute | solution.py:97
  34.7 5.4 %collective-permute-start.12 = (bf16[96,768]{1,0:T(8,128)(2,1)}, bf16[96,768]{1,0:T(8,128)(2,1)S(1)}, u32[]{:S(2)}, u32[]{:S(2)}) collective-permute-start(bf16[96,768]{1,0:T(8,128)(2,1)} %cut.2), channel_id=1, source_target_pairs={{0,8},{2,6},{8,16},{10,2},{16,24},{18,10},{24,28},{26,18},{28,20},... | collective-permute-start | bytes 442376 | tf_op jit(solution)/shard_map/ppermute | solution.py:88
  36.4 11.6 %copy-start.2 = (bf16[192,768]{1,0:T(8,128)(2,1)S(1)}, bf16[192,768]{1,0:T(8,128)(2,1)}, u32[]{:S(2)}) copy-start(bf16[192,768]{1,0:T(8,128)(2,1)} %copy-done) | copy-start | bytes 884740
  36.4 11.6 %copy-start.7 = (bf16[128,1536]{1,0:T(8,128)(2,1)S(1)}, bf16[128,1536]{1,0:T(8,128)(2,1)}, u32[]{:S(2)}) copy-start(bf16[128,1536]{1,0:T(8,128)(2,1)} %tokens.1) | copy-start | bytes 1179652
  36.4 11.6 %copy-start.8 = (f32[1536]{0:T(1024)S(1)}, f32[1536]{0:T(1024)}, u32[]{:S(2)}) copy-start(f32[1536]{0:T(1024)} %flat_gain.1) | copy-start | bytes 18436
  40.1 10.2 %collective-permute-start.15 = (bf16[576,512]{1,0:T(8,128)(2,1)}, bf16[576,512]{1,0:T(8,128)(2,1)}, u32[]{:S(2)}, u32[]{:S(2)}) collective-permute-start(bf16[576,512]{1,0:T(8,128)(2,1)} %collective-permute-done.8.refs_2_), channel_id=1, source_target_pairs={{0,8},{2,6},{8,16},{10,2},{16,24},{18,10},{24,28},{26,18},{28,20},... | collective-permute-start | bytes 1769480 | tf_op jit(solution)/shard_map/ppermute | solution.py:88
  41.8 1.4 %collective-permute-start.14 = (bf16[96,768]{1,0:T(8,128)(2,1)S(1)}, bf16[96,768]{1,0:T(8,128)(2,1)S(1)}, u32[]{:S(2)}, u32[]{:S(2)}) collective-permute-start(bf16[96,768]{1,0:T(8,128)(2,1)S(1)} %collective-permute-done.12.refs_7_), channel_id=1, source_target_pairs={{0,2},{2,0},{4,6},{6,4},{8,10},{10,8},{12,14},{14,12},{16,18},{18,... | collective-permute-start | bytes 442376 | tf_op jit(solution)/shard_map/ppermute | solution.py:97
  46.0 21.3 %collective-permute-start.17 = (bf16[128,1536]{1,0:T(8,128)(2,1)}, bf16[128,1536]{1,0:T(8,128)(2,1)}, u32[]{:S(2)}, u32[]{:S(2)}) collective-permute-start(bf16[128,1536]{1,0:T(8,128)(2,1)} %outward_send.1), channel_id=1, source_target_pairs={{0,1},{1,0},{2,3},{3,2},{4,5},{5,4},{6,7},{7,6},{8,9},{9,8},{10,11... | collective-permute-start | bytes 1179656 | tf_op jit(solution)/shard_map/ppermute | solution.py:798
  47.5 23.3 %collective-permute-start.18 = (bf16[576,512]{1,0:T(8,128)(2,1)}, bf16[576,512]{1,0:T(8,128)(2,1)}, u32[]{:S(2)}, u32[]{:S(2)}) collective-permute-start(bf16[576,512]{1,0:T(8,128)(2,1)} %collective-permute-done.3.refs_1_), channel_id=1, source_target_pairs={{0,2},{2,0},{4,6},{6,4},{8,10},{10,8},{12,14},{14,12},{16,18},{18,... | collective-permute-start | bytes 1769480 | tf_op jit(solution)/shard_map/ppermute | solution.py:97
  47.5 23.3 %collective-permute-start.19 = (bf16[576,512]{1,0:T(8,128)(2,1)}, bf16[576,512]{1,0:T(8,128)(2,1)}, u32[]{:S(2)}, u32[]{:S(2)}) collective-permute-start(bf16[576,512]{1,0:T(8,128)(2,1)} %collective-permute-done.8.refs_2_), channel_id=1, source_target_pairs={{0,2},{2,0},{4,6},{6,4},{8,10},{10,8},{12,14},{14,12},{16,18},{18,... | collective-permute-start | bytes 1769480 | tf_op jit(solution)/shard_map/ppermute | solution.py:97
  50.3 20.5 %copy-start.4 = (bf16[576,512]{1,0:T(8,128)(2,1)S(1)}, bf16[576,512]{1,0:T(8,128)(2,1)}, u32[]{:S(2)}) copy-start(bf16[576,512]{1,0:T(8,128)(2,1)} %copy-done.3) | copy-start | bytes 1769476
  60.3 7.1 %collective-permute-start.16 = (bf16[288,512]{1,0:T(8,128)(2,1)}, bf16[288,512]{1,0:T(8,128)(2,1)}, u32[]{:S(2)}, u32[]{:S(2)}) collective-permute-start(bf16[288,512]{1,0:T(8,128)(2,1)} %cut.3), channel_id=1, source_target_pairs={{0,8},{2,6},{8,16},{10,2},{16,24},{18,10},{24,28},{26,18},{28,20},... | collective-permute-start | bytes 884744 | tf_op jit(solution)/shard_map/ppermute | solution.py:88
  62.1 12.0 %collective-permute-start.21 = (bf16[576,512]{1,0:T(8,128)(2,1)}, bf16[576,512]{1,0:T(8,128)(2,1)}, u32[]{:S(2)}, u32[]{:S(2)}) collective-permute-start(bf16[576,512]{1,0:T(8,128)(2,1)} %collective-permute-done.15.whole.refs_0_), channel_id=1, source_target_pairs={{0,2},{2,0},{4,6},{6,4},{8,10},{10,8},{12,14},{14,12},{16,18},{18,... | collective-permute-start | bytes 1769480 | tf_op jit(solution)/shard_map/ppermute | solution.py:97
  62.1 20.8 %all-to-all-start = ((bf16[16,144,128]{2,1,0:T(8,128)(2,1)}), bf16[16,144,128]{2,1,0:T(8,128)(2,1)S(1)}, u32[]{:S(2)}, u32[]{:S(2)}) async-start(bf16[16,144,128]{2,1,0:T(8,128)(2,1)} %bundle.1), calls=%async_computation | async-start | bytes 1179648 | tf_op jit(solution)/shard_map/all_to_all | solution.py:807
  67.4 6.7 %collective-permute-start.22 = (bf16[288,512]{1,0:T(8,128)(2,1)}, bf16[288,512]{1,0:T(8,128)(2,1)S(1)}, u32[]{:S(2)}, u32[]{:S(2)}) collective-permute-start(bf16[288,512]{1,0:T(8,128)(2,1)} %collective-permute-done.16.refs_2_), channel_id=1, source_target_pairs={{0,2},{2,0},{4,6},{6,4},{8,10},{10,8},{12,14},{14,12},{16,18},{18,... | collective-permute-start | bytes 884744 | tf_op jit(solution)/shard_map/ppermute | solution.py:97
  69.2 4.9 %collective-permute-start.20 = (bf16[32,1536]{1,0:T(8,128)(2,1)S(1)}, bf16[32,1536]{1,0:T(8,128)(2,1)S(1)}, u32[]{:S(2)}, u32[]{:S(2)}) collective-permute-start(bf16[32,1536]{1,0:T(8,128)(2,1)S(1)} %get-tuple-element.113), channel_id=1, source_target_pairs={{0,1},{1,0},{2,3},{3,2},{4,5},{5,4},{6,7},{7,6},{8,9},{9,8},{10,11... | collective-permute-start | bytes 294920 | tf_op jit(solution)/shard_map/ppermute | solution.py:812
  74.1 8.8 %copy-start.5 = (bf16[512,4,128]{2,1,0:T(4,128)(2,1)S(1)}, bf16[512,4,128]{2,1,0:T(4,128)(2,1)}, u32[]{:S(2)}) copy-start(bf16[512,4,128]{2,1,0:T(4,128)(2,1)} %param.25) | copy-start | bytes 1572868
  76.8 4.7 %collective-permute-start.23 = (bf16[32,1536]{1,0:T(8,128)(2,1)S(1)}, bf16[32,1536]{1,0:T(8,128)(2,1)S(1)}, u32[]{:S(2)}, u32[]{:S(2)}) collective-permute-start(bf16[32,1536]{1,0:T(8,128)(2,1)S(1)} %get-tuple-element.121), channel_id=1, source_target_pairs={{0,1},{1,0},{2,3},{3,2},{4,5},{5,4},{6,7},{7,6},{8,9},{9,8},{10,11... | collective-permute-start | bytes 294920 | tf_op jit(solution)/shard_map/ppermute | solution.py:819
  (3 other events, 5.6 us)

commit v16 on v14

--- a/solution.py
+++ b/solution.py
@@ -54,8 +54,27 @@
     return listed + [block(side, count // 2)[0], block(1 - side, count // 2)[0]]
 
 
+def cut_kernel(whole, out, sem):
+    copy = pltpu.make_async_copy(whole.at[pl.ds(0, out.shape[0]), :], out, sem)
+    copy.start()
+    copy.wait()
+
+
+def cut(whole, rows):
+    return pl.pallas_call(
+        cut_kernel,
+        out_shape=jax.ShapeDtypeStruct((rows, whole.shape[1]), whole.dtype),
+        in_specs=[pl.BlockSpec(memory_space=pl.ANY)],
+        out_specs=pl.BlockSpec(memory_space=pltpu.VMEM),
+        scratch_shapes=[pltpu.SemaphoreType.DMA],
+        cost_estimate=pl.CostEstimate(flops=1, bytes_accessed=1 << 22, transcendentals=0),
+        name="cut",
+    )(whole)
+
+
 class Ring:
-    def __init__(self, pair, groups):
+    def __init__(self, pair, groups, first):
+        self.first = first
         self.across = functools.partial(lax.ppermute, axis_name="grp", perm=ring_pairs(groups))
         self.beside = functools.partial(lax.ppermute, axis_name="grp", perm=sibling_pairs(groups))
         self.full = (groups // 2 - 1) // 2
@@ -66,7 +85,7 @@
     def step(self):
         held = self.mine[-1]
         if len(self.mine) > self.full:
-            held = held[: self.unit_rows]
+            held = self.first(held, self.unit_rows)
         self.mine.append(self.across(held))
 
     def pin(self, *others):
@@ -414,9 +433,8 @@
     out[...] = outward_rows(True, groups, unit_rows, early, late, parts, w_out, rows).astype(bf16)
 
 
-def keep_kernel(groups, unit_rows, n_parts, early, late, tokens, flat_gain, *refs):
-    parts, (out, gain, w_out, rows) = refs[:n_parts], refs[n_parts:]
-    gain[...] = flat_gain[...].reshape(gain.shape)
+def keep_kernel(groups, unit_rows, n_parts, early, late, tokens, *refs):
+    parts, (out, w_out, rows) = refs[:n_parts], refs[n_parts:]
     made = outward_rows(False, groups, unit_rows, early, late, parts, w_out, rows)
     out[...] = tokens[...].astype(f32) + made
 
@@ -435,16 +453,13 @@
     )(early, late, *parts)
 
 
-def outward_keep(groups, early, late, tokens, gain, parts, unit_rows):
+def outward_keep(groups, early, late, tokens, parts, unit_rows):
     width, depth = groups * unit_rows, parts[0].shape[1]
     return pl.pallas_call(
         functools.partial(keep_kernel, groups, unit_rows, len(parts)),
-        out_shape=(
-            jax.ShapeDtypeStruct(tokens.shape, f32),
-            jax.ShapeDtypeStruct((1, width), f32),
-        ),
-        in_specs=[VMEM] * (4 + len(parts)),
-        out_specs=(VMEM, VMEM),
+        out_shape=jax.ShapeDtypeStruct(tokens.shape, f32),
+        in_specs=[VMEM] * (3 + len(parts)),
+        out_specs=VMEM,
         scratch_shapes=[
             pltpu.VMEM((width, depth), bf16),
             pltpu.VMEM(early.shape, bf16),
@@ -452,19 +467,28 @@
         compiler_params=PARAMS,
         cost_estimate=reads(2 * width * depth),
         name="outward_keep",
-    )(early, late, tokens, gain, *parts)
-
-
-def route_kernel(mine, arrived, gain, place, residual, moe_in, sent):
-    added = (mine[...] + arrived[...].astype(f32)).astype(bf16)
-    residual[...] = added
-    moe_in[...] = normalized(added.astype(f32), gain[...])
+    )(early, late, tokens, *parts)
+
+
+def route_kernel(mine, arrived, flat_gain, place, residual, moe_in, sent, got, gain, sems, gain_sem):
+    count = got.shape[0] // 4
+    spans = [pl.ds(index * count, count) for index in range(4)]
+    copies = fetch([(arrived.at[span, :], got.at[span, :]) for span in spans], sems)
+    gain_copy = pltpu.make_async_copy(flat_gain, gain, gain_sem)
+    gain_copy.start()
+    gain_copy.wait()
+    gains = gain[...].reshape(1, gain.shape[0])
+    for span, copy in zip(spans, copies):
+        copy.wait()
+        added = (mine[span, :] + got[span, :].astype(f32)).astype(bf16)
+        residual[span, :] = added
+        moe_in[span, :] = normalized(added.astype(f32), gains)
     cap = sent.shape[0]
     rows = jnp.dot(place[cap:, :], moe_in[...], preferred_element_type=f32)
     sent[...] = rows.astype(bf16)
 
 
-def route(mine, arrived, gain, place):
+def route(mine, arrived, flat_gain, place):
     cap = place.shape[0] // 2
     return pl.pallas_call(
         route_kernel,
@@ -473,12 +497,18 @@
             jax.ShapeDtypeStruct(mine.shape, bf16),
             jax.ShapeDtypeStruct((cap, mine.shape[1]), bf16),
         ),
-        in_specs=[VMEM] * 4,
+        in_specs=[VMEM, ANY, ANY, VMEM],
         out_specs=(VMEM,) * 3,
-        compiler_params=PARAMS,
-        cost_estimate=reads(10 * mine.shape[0] * mine.shape[1]),
+        scratch_shapes=[
+            pltpu.VMEM(mine.shape, bf16),
+            pltpu.VMEM(flat_gain.shape, f32),
+            pltpu.SemaphoreType.DMA((4,)),
+            pltpu.SemaphoreType.DMA,
+        ],
+        compiler_params=PARAMS,
+        cost_estimate=reads(16 << 20),
         name="route",
-    )(mine, arrived, gain, place)
+    )(mine, arrived, pltpu.with_memory_space_constraint(flat_gain, pltpu.HBM), place)
 
 
 def expert_pieces(gate_up, down, up_rows, down_rows, width):
@@ -587,7 +617,7 @@
         scratch_shapes=[pltpu.VMEM((2 * count, model), bf16)],
         input_output_aliases={2: 2, 3: 3},
         compiler_params=PARAMS,
-        cost_estimate=takes(6.2),
+        cost_estimate=pl.CostEstimate(flops=int(6.2 * 1.15e9), bytes_accessed=1, transcendentals=0),
         name="expert",
     )(own, other, *staged, *[part for part, _ in late])[:2]
 
@@ -729,24 +759,24 @@
     up_rows, down_rows = own[0].shape[0], own[1].shape[0]
     beside = [lax.ppermute(part, "grp", sibling_pairs(groups)) for part in own]
     expert_pair, out_pair = pack(own, beside)
-    out_ring = Ring(out_pair, groups)
+    out_ring = Ring(out_pair, groups, lambda held, rows: held[:rows])
     out_ring.step()
-    expert_ring = Ring(expert_pair, groups)
+    expert_ring = Ring(expert_pair, groups, cut)
     expert_ring.step()
     w_keyval, positions = together((w_keyval, positions, out_pair))[:2]
     flat_kv = w_keyval.reshape(model, kv_width)
     cosine, sine, past, place, send, tags, gain = prepare(
         groups, slots_dev, positions, cache_slot, expert_ids, attn_gain
     )
-    other_tokens, cosine, flat_kv = out_ring.pin(other_tokens, cosine, flat_kv)
+    cosine, flat_kv = out_ring.pin(cosine, flat_kv)
     out_ring.step()
 
     q, kv, tail = project(tokens, other_tokens, gain, cosine, sine, w_query, flat_kv)
     seam = lax.ppermute(tail, "grp", [(g, g + 1) for g in range(groups - 1)])
-    q = out_ring.pin(q)
+    late = attend_late(q, kv, past)
+    late = out_ring.pin(late)
     out_ring.step()
     out_ring.share(2)
-    late = attend_late(q, kv, past)
     seam, late = together((seam, late))
     seam = expert_ring.pin(seam)
     expert_ring.step()
@@ -765,18 +795,16 @@
     sent = outward_send(groups, early, late, out_ring.parts(), out_ring.unit_rows)
     arrived = swap(sent)
     early = together((early, sent))[0]
-    mine, late_gain = outward_keep(
-        groups, early, late, tokens, moe_gain, out_ring.parts(), out_ring.unit_rows
-    )
-    late_gain = expert_ring.pin(late_gain)
+    mine = outward_keep(groups, early, late, tokens, out_ring.parts(), out_ring.unit_rows)
+    mine = expert_ring.pin(mine)
     expert_ring.share()
     expert_ring.step()
     outgoing = together((outgoing, sent))[0]
     arrived_cache = lax.all_to_all(outgoing, "grp", split_axis=0, concat_axis=0, tiled=True)
-    arrived, late_gain = expert_ring.pin(arrived, late_gain)
+    arrived, mine = expert_ring.pin(arrived, mine)
     expert_ring.share()
 
-    residual, moe_in, sent_rows = route(mine, arrived, late_gain, place)
+    residual, moe_in, sent_rows = route(mine, arrived, moe_gain, place)
     landed = swap(sent_rows)
     parts_early, parts_late = expert_ring.split()
     gates, own_rows, spread, *staged = gate(

time: 72.8 us -> 73.4 us (level)
  local copies, waits for them, and re-layouts: 4.84 us -> 2.68 us
  Pallas kernels: 20 us -> 21.9 us
  waiting for transfers between devices: 15.6 us -> 17.2 us
    ppermute x8, waiting for transfers between devices: 7.73 us -> 11.2 us  [step(): self.mine.append(self.across(held))]
    ppermute x1, waiting for transfers between devices: 2.11 us -> 0.28 us  [two_lane_shards(): other_tokens = swap(tokens)]
    slice x2 -> x1, local copies, waits for them, and re-layouts: 1.71 us -> 0.01 us  [two_lane_shards(): out_ring = Ring(out_pair, groups, lambda held, rows: held[:rows])]
    pallas_call x0 -> x1, Pallas kernels: none -> 1.68 us  [cut(): pl.pallas_call(cut_kernel, out_shape=jax.ShapeDtypeStruct((rows, whole.sh...]
    ppermute x8, starting transfers between devices: 15.2 us -> 14 us  [step(): self.mine.append(self.across(held))]
    unnamed x13 -> x11, local copies, waits for them, and re-layouts: 3.13 us -> 2.67 us
  transfers between devices with their start and end apart: 25 -> 25, of which waited for: 8 -> 11; matrix products, arithmetic and copies ran while one was open for 5% -> 3% of each run, Pallas kernels for 26% -> 28%
where the time goes in v16:
time: 73.4 us; the launch traced here: 72.9 us
  starting transfers between devices  30.3 us (41%)
  Pallas kernels  21.9 us (30%)
  waiting for transfers between devices  17.2 us (23%)
  local copies, waits for them, and re-layouts  2.68 us (4%)
  between operations  0.83 us (1%)
    ppermute x8, starting transfers between devices, step(): self.mine.append(self.across(held))  14 us
    ppermute x8, waiting for transfers between devices, step(): self.mine.append(self.across(held))  11.2 us
    all_to_all x1, starting transfers between devices, two_lane_shards(): lax.all_to_all(outgoing, 'grp', split_axis=0, concat_axis=0, tiled=True)  5.22 us
    ppermute x1, waiting for transfers between devices, two_lane_shards(): returned = swap(back)  3 us
    unnamed x11, local copies, waits for them, and re-layouts  2.67 us
    ppermute x1, starting transfers between devices, two_lane_shards(): other_tokens = swap(tokens)  2.56 us
    pallas_call x1, Pallas kernels, expert(): pl.pallas_call(functools.partial(expert_kernel, groups, up_rows, down_row...  2.34 us
    pallas_call x1, Pallas kernels, gate(): pl.pallas_call(functools.partial(gate_kernel, groups, up_rows, down_rows,...  2.3 us
  transfers between devices with their start and end apart: 25, of which 11 were waited for; matrix products, arithmetic and copies ran while one was open for 3% of the time, Pallas kernels for 28%

profile of v16, /device:TPU:0, one launch (start us, length us, event | category | flops | bytes accessed | tf_op | source)
XLA Modules:
  0.0 72.9 jit_solution(10706490520830889012)
XLA Ops:
  1.7 2.6 %collective-permute-start.4 = (bf16[128,1536]{1,0:T(8,128)(2,1)}, bf16[128,1536]{1,0:T(8,128)(2,1)S(1)}, u32[]{:S(2)}, u32[]{:S(2)}) collective-permute-start(bf16[128,1536]{1,0:T(8,128)(2,1)} %tokens.1), channel_id=1, source_target_pairs={{0,1},{1,0},{2,3},{3,2},{4,5},{5,4},{6,7},{7,6},{8,9},{9,8},{10,11... | collective-permute-start | bytes 1179656 | tf_op jit(solution)/shard_map/ppermute | solution.py:757
  5.4 1.7 %collective-permute-start.5 = (bf16[192,768]{1,0:T(8,128)(2,1)S(1)}, bf16[192,768]{1,0:T(8,128)(2,1)S(1)}, u32[]{:S(2)}, u32[]{:S(2)}) collective-permute-start(bf16[192,768]{1,0:T(8,128)(2,1)S(1)} %get-tuple-element.63.refs_0_), channel_id=1, source_target_pairs={{0,8},{2,6},{8,16},{10,2},{16,24},{18,10},{24,28},{26,18},{28,20},... | collective-permute-start | bytes 884744 | tf_op jit(solution)/shard_map/ppermute | solution.py:89
  7.1 1.6 %collective-permute-start.3 = (bf16[576,512]{1,0:T(8,128)(2,1)S(1)}, bf16[576,512]{1,0:T(8,128)(2,1)S(1)}, u32[]{:S(2)}, u32[]{:S(2)}) collective-permute-start(bf16[576,512]{1,0:T(8,128)(2,1)S(1)} %get-tuple-element.62.refs_0_), channel_id=1, source_target_pairs={{0,8},{2,6},{8,16},{10,2},{16,24},{18,10},{24,28},{26,18},{28,20},... | collective-permute-start | bytes 1769480 | tf_op jit(solution)/shard_map/ppermute | solution.py:89
  8.7 1.5 %prepare.1 = (f32[256,128]{1,0:T(8,128)S(1)}, f32[256,128]{1,0:T(8,128)S(1)}, f32[256,128]{1,0:T(8,128)S(1)}, bf16[64,128]{1,0:T(8,128)(2,1)S(1)}, bf16[512,256]...) custom-call(s32[1,256]{1,0:T(1,128)} %bitcast.26, s32[1,256]{1,0:T(1,128)} %bitcast.27, ...), custom_call_target="tpu_custom_call" | custom-call | flops 1 | bytes 1 | tf_op jit(solution)/shard_map/prepare/pallas_call | solution.py:285
  10.2 1.8 %copy.19 = bf16[192,8,4,128]{3,1,2,0:T(8,128)(2,1)S(1)} copy(bf16[192,8,4,128]{3,2,1,0:T(4,128)(2,1)} %bitcast.15) | data formatting | bytes 3145728
  12.2 1.7 %collective-permute-start.7 = (bf16[192,768]{1,0:T(8,128)(2,1)S(1)}, bf16[192,768]{1,0:T(8,128)(2,1)S(1)}, u32[]{:S(2)}, u32[]{:S(2)}) collective-permute-start(bf16[192,768]{1,0:T(8,128)(2,1)S(1)} %collective-permute-done.5.refs_1_), channel_id=1, source_target_pairs={{0,8},{2,6},{8,16},{10,2},{16,24},{18,10},{24,28},{26,18},{28,20},... | collective-permute-start | bytes 884744 | tf_op jit(solution)/shard_map/ppermute | solution.py:89
  14.1 2.2 %project.1 = (bf16[256,768]{1,0:T(8,128)(2,1)S(1)}, bf16[256,512]{1,0:T(8,128)(2,1)S(1)}, bf16[128,512]{1,0:T(8,128)(2,1)S(1)}) custom-call(bf16[128,1536]{1,0:T(8,128)(2,1)S(1)} %copy-done.3, bf16[128,1536]{1,0:T(8,128)(2,1)S(1)} %collective-permute-done.4.other, f32[1,1536]{1,0:T(1,128)S(1)} %get-tuple-element.65.gain, ...), custom_call_target="tpu_custom_call" | custom-call | flops 9200000000 | bytes 64000000 | tf_op jit(solution)/shard_map/project/pallas_call | solution.py:335
  16.4 1.8 %collective-permute-start.6 = (bf16[128,512]{1,0:T(8,128)(2,1)S(1)}, bf16[128,512]{1,0:T(8,128)(2,1)S(1)}, u32[]{:S(2)}, u32[]{:S(2)}) collective-permute-start(bf16[128,512]{1,0:T(8,128)(2,1)S(1)} %get-tuple-element.71), channel_id=1, source_target_pairs={{0,2},{2,4},{4,6},{6,8},{8,10},{10,12},{12,14},{14,16},{16,18},{18... | collective-permute-start | bytes 393224 | tf_op jit(solution)/shard_map/ppermute | solution.py:775
  18.2 1.3 %attend_late.1.late = bf16[128,768]{1,0:T(8,128)(2,1)S(1)} custom-call(bf16[256,768]{1,0:T(8,128)(2,1)S(1)} %get-tuple-element.73.q, bf16[256,512]{1,0:T(8,128)(2,1)S(1)} %get-tuple-element.88.kv, f32[256,128]{1,0:T(8,128)S(1)} %get-tuple-element.75.past), custom_call_target="tpu_custom_call" | custom-call | flops 2300000000 | bytes 16000000 | tf_op jit(solution)/shard_map/attend_late/pallas_call | solution.py:391
  19.5 2.1 %collective-permute-done.7.refs_2_ = bf16[192,768]{1,0:T(8,128)(2,1)S(1)} collective-permute-done((bf16[192,768]{1,0:T(8,128)(2,1)S(1)}, bf16[192,768]{1,0:T(8,128)(2,1)S(1)}, u32[]{:S(2)}, u32[]{:S(2)}) %collective-permute-start.7) | collective-permute-done | bytes 294944 | tf_op jit(solution)/shard_map/ppermute | solution.py:89
  21.6 1.7 %collective-permute-start.9 = (bf16[192,768]{1,0:T(8,128)(2,1)S(1)}, bf16[192,768]{1,0:T(8,128)(2,1)S(1)}, u32[]{:S(2)}, u32[]{:S(2)}) collective-permute-start(bf16[192,768]{1,0:T(8,128)(2,1)S(1)} %collective-permute-done.7.refs_2_), channel_id=1, source_target_pairs={{0,8},{2,6},{8,16},{10,2},{16,24},{18,10},{24,28},{26,18},{28,20},... | collective-permute-start | bytes 884744 | tf_op jit(solution)/shard_map/ppermute | solution.py:89
  23.3 2.1 %collective-permute-start.8 = (bf16[576,512]{1,0:T(8,128)(2,1)S(1)}, bf16[576,512]{1,0:T(8,128)(2,1)}, u32[]{:S(2)}, u32[]{:S(2)}) collective-permute-start(bf16[576,512]{1,0:T(8,128)(2,1)S(1)} %collective-permute-done.3.refs_1_), channel_id=1, source_target_pairs={{0,8},{2,6},{8,16},{10,2},{16,24},{18,10},{24,28},{26,18},{28,20},... | collective-permute-start | bytes 1769480 | tf_op jit(solution)/shard_map/ppermute | solution.py:89
  25.4 1.5 %attend_early.1.early = bf16[128,768]{1,0:T(8,128)(2,1)S(1)} custom-call(bf16[256,768]{1,0:T(8,128)(2,1)S(1)} %get-tuple-element.73.q, bf16[256,512]{1,0:T(8,128)(2,1)S(1)} %get-tuple-element.88.kv, bf16[128,512]{1,0:T(8,128)(2,1)S(1)} %collective-permute-done.6.seam, f32[256,128]{1,0:T(8,128)S(1)} %get-tuple-element.75.past), custom_call_target="tpu_custom_call" | custom-call | flops 2300000000 | bytes 16000000 | tf_op jit(solution)/shard_map/attend_early/pallas_call | solution.py:403
  26.9 1.5 %collective-permute-done.9.refs_3_ = bf16[192,768]{1,0:T(8,128)(2,1)S(1)} collective-permute-done((bf16[192,768]{1,0:T(8,128)(2,1)S(1)}, bf16[192,768]{1,0:T(8,128)(2,1)S(1)}, u32[]{:S(2)}, u32[]{:S(2)}) %collective-permute-start.9) | collective-permute-done | bytes 294944 | tf_op jit(solution)/shard_map/ppermute | solution.py:89
  28.4 1.7 %collective-permute-start.12 = (bf16[96,768]{1,0:T(8,128)(2,1)S(1)}, bf16[96,768]{1,0:T(8,128)(2,1)S(1)}, u32[]{:S(2)}, u32[]{:S(2)}) collective-permute-start(bf16[96,768]{1,0:T(8,128)(2,1)S(1)} %slice.3), channel_id=1, source_target_pairs={{0,8},{2,6},{8,16},{10,2},{16,24},{18,10},{24,28},{26,18},{28,20},... | collective-permute-start | bytes 442376 | tf_op jit(solution)/shard_map/ppermute | solution.py:89
  30.1 1.4 %bundle.1 = bf16[16,144,128]{2,1,0:T(8,128)(2,1)} custom-call(bf16[512,256]{1,0:T(8,128)(2,1)S(1)} %get-tuple-element.87.send, bf16[256,512]{1,0:T(8,128)(2,1)S(1)} %get-tuple-element.88.kv, bf16[256,128]{1,0:T(8,128)(2,1)S(1)} %get-tuple-element.89.tags), custom_call_target="tpu_custom_call" | custom-call | flops 1 | bytes 1 | tf_op jit(solution)/shard_map/bundle/pallas_call | solution.py:674
  31.5 4.7 %collective-permute-done.12.refs_7_ = bf16[96,768]{1,0:T(8,128)(2,1)S(1)} collective-permute-done((bf16[96,768]{1,0:T(8,128)(2,1)S(1)}, bf16[96,768]{1,0:T(8,128)(2,1)S(1)}, u32[]{:S(2)}, u32[]{:S(2)}) %collective-permute-start.12) | collective-permute-done | bytes 147488 | tf_op jit(solution)/shard_map/ppermute | solution.py:89
  36.3 1.7 %collective-permute-start.14 = (bf16[576,512]{1,0:T(8,128)(2,1)}, bf16[576,512]{1,0:T(8,128)(2,1)S(1)}, u32[]{:S(2)}, u32[]{:S(2)}) collective-permute-start(bf16[576,512]{1,0:T(8,128)(2,1)} %collective-permute-done.8.refs_2_), channel_id=1, source_target_pairs={{0,8},{2,6},{8,16},{10,2},{16,24},{18,10},{24,28},{26,18},{28,20},... | collective-permute-start | bytes 1769480 | tf_op jit(solution)/shard_map/ppermute | solution.py:89
  38.0 1.4 %collective-permute-done.15.refs_8_ = bf16[96,768]{1,0:T(8,128)(2,1)S(1)} collective-permute-done((bf16[96,768]{1,0:T(8,128)(2,1)S(1)}, bf16[96,768]{1,0:T(8,128)(2,1)S(1)}, u32[]{:S(2)}, u32[]{:S(2)}) %collective-permute-start.15) | collective-permute-done | bytes 147488 | tf_op jit(solution)/shard_map/ppermute | solution.py:98
  40.5 1.6 %collective-permute-start.17 = (bf16[128,1536]{1,0:T(8,128)(2,1)S(1)}, bf16[128,1536]{1,0:T(8,128)(2,1)}, u32[]{:S(2)}, u32[]{:S(2)}) collective-permute-start(bf16[128,1536]{1,0:T(8,128)(2,1)S(1)} %outward_send.1), channel_id=1, source_target_pairs={{0,1},{1,0},{2,3},{3,2},{4,5},{5,4},{6,7},{7,6},{8,9},{9,8},{10,11... | collective-permute-start | bytes 1179656 | tf_op jit(solution)/shard_map/ppermute | solution.py:796
  42.6 1.2 %outward_keep.1.mine = f32[128,1536]{1,0:T(8,128)S(1)} custom-call(bf16[128,768]{1,0:T(8,128)(2,1)S(1)} %attend_early.1.early, bf16[128,768]{1,0:T(8,128)(2,1)S(1)} %attend_late.1.late, bf16[128,1536]{1,0:T(8,128)(2,1)S(1)} %copy-done.3, bf16[192,768]{1,0:T(8,128)(2,1)S(1)} %get-tuple-element.63.refs_0_, ...), custom_call_target="tpu_custom_call" | custom-call | flops 1 | bytes 2359296 | tf_op jit(solution)/shard_map/outward_keep/pallas_call | solution.py:458
  43.7 2.6 %collective-permute-done.14.whole.refs_0_ = bf16[576,512]{1,0:T(8,128)(2,1)S(1)} collective-permute-done((bf16[576,512]{1,0:T(8,128)(2,1)}, bf16[576,512]{1,0:T(8,128)(2,1)S(1)}, u32[]{:S(2)}, u32[]{:S(2)}) %collective-permute-start.14) | collective-permute-done | bytes 589856 | tf_op jit(solution)/shard_map/ppermute | solution.py:89
  47.2 1.7 %cut.1 = bf16[288,512]{1,0:T(8,128)(2,1)} custom-call(bf16[576,512]{1,0:T(8,128)(2,1)} %copy-done), custom_call_target="tpu_custom_call" | custom-call | flops 1 | bytes 4194304 | tf_op jit(solution)/shard_map/cut/pallas_call | solution.py:64
  48.9 1.7 %collective-permute-start.16 = (bf16[288,512]{1,0:T(8,128)(2,1)}, bf16[288,512]{1,0:T(8,128)(2,1)}, u32[]{:S(2)}, u32[]{:S(2)}) collective-permute-start(bf16[288,512]{1,0:T(8,128)(2,1)} %cut.1), channel_id=1, source_target_pairs={{0,8},{2,6},{8,16},{10,2},{16,24},{18,10},{24,28},{26,18},{28,20},... | collective-permute-start | bytes 884744 | tf_op jit(solution)/shard_map/ppermute | solution.py:89
  50.6 5.2 %all-to-all-start = ((bf16[16,144,128]{2,1,0:T(8,128)(2,1)}), bf16[16,144,128]{2,1,0:T(8,128)(2,1)S(1)}, u32[]{:S(2)}, u32[]{:S(2)}) async-start(bf16[16,144,128]{2,1,0:T(8,128)(2,1)} %bundle.1), calls=%async_computation | async-start | bytes 1179648 | tf_op jit(solution)/shard_map/all_to_all | solution.py:803
  56.3 1.6 %route.1 = (bf16[128,1536]{1,0:T(8,128)(2,1)S(1)}, bf16[128,1536]{1,0:T(8,128)(2,1)S(1)}, bf16[32,1536]{1,0:T(8,128)(2,1)S(1)}) custom-call(f32[128,1536]{1,0:T(8,128)S(1)} %outward_keep.1.mine, bf16[128,1536]{1,0:T(8,128)(2,1)} %collective-permute-done.17.arrived, f32[1536]{0:T(1024)} %flat_gain.1, bf16[64,128]{1,0:T(8,128)(2,1)S(1)} %get-tuple-element.104.place), custom_call_target="tpu_custom_call" | custom-call | flops 1 | bytes 16777216 | tf_op jit(solution)/shard_map/route/pallas_call | solution.py:493
  58.0 1.5 %collective-permute-start.20 = (bf16[32,1536]{1,0:T(8,128)(2,1)S(1)}, bf16[32,1536]{1,0:T(8,128)(2,1)S(1)}, u32[]{:S(2)}, u32[]{:S(2)}) collective-permute-start(bf16[32,1536]{1,0:T(8,128)(2,1)S(1)} %get-tuple-element.109), channel_id=1, source_target_pairs={{0,1},{1,0},{2,3},{3,2},{4,5},{5,4},{6,7},{7,6},{8,9},{9,8},{10,11... | collective-permute-start | bytes 294920 | tf_op jit(solution)/shard_map/ppermute | solution.py:808
  59.5 2.3 %gate.1 = (f32[128,40]{1,0:T(8,128)S(1)}, bf16[32,1536]{1,0:T(8,128)(2,1)S(1)}, bf16[128,64]{1,0:T(8,128)(2,1)S(1)}, bf16[1536,1024]{1,0:T(8,128)(2,1)S(1)}, bf16[512,1536]{1,0:T(8,128)(2,1)S(1)}) custom-call(bf16[128,1536]{1,0:T(8,128)(2,1)S(1)} %get-tuple-element.106.moe_in, bf16[40,1536]{1,0:T(8,128)(2,1)} %bitcast.21, s32[8,128]{1,0:T(8,128)} %bitcast.25, ...), custom_call_target="tpu_custom_call" | custom-call | flops 1 | bytes 1 | tf_op jit(solution)/shard_map/gate/pallas_call | solution.py:568
  62.9 2.3 %expert.1 = (bf16[32,1536]{1,0:T(8,128)(2,1)S(1)}, bf16[32,1536]{1,0:T(8,128)(2,1)S(1)}, bf16[1536,1024]{1,0:T(8,128)(2,1)S(1)}, bf16[512,1536]{1,0:T(8,128)(2,1)S(1)}) custom-call(bf16[32,1536]{1,0:T(8,128)(2,1)S(1)} %get-tuple-element.111.own, bf16[32,1536]{1,0:T(8,128)(2,1)S(1)} %collective-permute-done.20.other, ...), custom_call_target="tpu_custom_call", output_to_operand_aliasing={{2}: (2, {}), {3}: (3, {})} | custom-call | flops 7129999872 | bytes 1 | tf_op jit(solution)/shard_map/expert/pallas_call | solution.py:611
  65.3 1.7 %collective-permute-start.23 = (bf16[32,1536]{1,0:T(8,128)(2,1)S(1)}, bf16[32,1536]{1,0:T(8,128)(2,1)S(1)}, u32[]{:S(2)}, u32[]{:S(2)}) collective-permute-start(bf16[32,1536]{1,0:T(8,128)(2,1)S(1)} %get-tuple-element.117), channel_id=1, source_target_pairs={{0,1},{1,0},{2,3},{3,2},{4,5},{5,4},{6,7},{7,6},{8,9},{9,8},{10,11... | collective-permute-start | bytes 294920 | tf_op jit(solution)/shard_map/ppermute | solution.py:815
  66.9 3.0 %collective-permute-done.23.returned = bf16[32,1536]{1,0:T(8,128)(2,1)S(1)} collective-permute-done((bf16[32,1536]{1,0:T(8,128)(2,1)S(1)}, bf16[32,1536]{1,0:T(8,128)(2,1)S(1)}, u32[]{:S(2)}, u32[]{:S(2)}) %collective-permute-start.23) | collective-permute-done | bytes 98336 | tf_op jit(solution)/shard_map/ppermute | solution.py:815
  71.4 1.5 %write.1 = bf16[2048,128]{1,0:T(8,128)(2,1)} custom-call(bf16[16,144,128]{2,1,0:T(8,128)(2,1)S(1)} %all-to-all-done.arrived, bf16[2048,128]{1,0:T(8,128)(2,1)S(1)} %bitcast.14), custom_call_target="tpu_custom_call" | custom-call | flops 1 | bytes 2097152 | tf_op jit(solution)/shard_map/write/pallas_call | solution.py:715
  (44 shorter events, 8.1 us)
Async XLA Ops:
  0.6 3.6 %collective-permute-start.2 = (bf16[96,1536]{1,0:T(8,128)(2,1)}, bf16[96,1536]{1,0:T(8,128)(2,1)S(1)}, u32[]{:S(2)}, u32[]{:S(2)}) collective-permute-start(bf16[96,1536]{1,0:T(8,128)(2,1)} %bitcast.17), channel_id=1, source_target_pairs={{0,2},{2,0},{4,6},{6,4},{8,10},{10,8},{12,14},{14,12},{16,18},{18,... | collective-permute-start | bytes 884744 | tf_op jit(solution)/shard_map/ppermute | solution.py:760
  1.1 3.1 %collective-permute-start = (bf16[96,1024]{1,0:T(8,128)(2,1)}, bf16[96,1024]{1,0:T(8,128)(2,1)S(1)}, u32[]{:S(2)}, u32[]{:S(2)}) collective-permute-start(bf16[96,1024]{1,0:T(8,128)(2,1)} %bitcast.19), channel_id=1, source_target_pairs={{0,2},{2,0},{4,6},{6,4},{8,10},{10,8},{12,14},{14,12},{16,18},{18,... | collective-permute-start | bytes 589832 | tf_op jit(solution)/shard_map/ppermute | solution.py:760
  1.2 3.0 %collective-permute-start.1 = (bf16[32,1536]{1,0:T(8,128)(2,1)}, bf16[32,1536]{1,0:T(8,128)(2,1)S(1)}, u32[]{:S(2)}, u32[]{:S(2)}) collective-permute-start(bf16[32,1536]{1,0:T(8,128)(2,1)} %bitcast.22), channel_id=1, source_target_pairs={{0,2},{2,0},{4,6},{6,4},{8,10},{10,8},{12,14},{14,12},{16,18},{18,... | collective-permute-start | bytes 294920 | tf_op jit(solution)/shard_map/ppermute | solution.py:760
  1.7 12.5 %collective-permute-start.4 = (bf16[128,1536]{1,0:T(8,128)(2,1)}, bf16[128,1536]{1,0:T(8,128)(2,1)S(1)}, u32[]{:S(2)}, u32[]{:S(2)}) collective-permute-start(bf16[128,1536]{1,0:T(8,128)(2,1)} %tokens.1), channel_id=1, source_target_pairs={{0,1},{1,0},{2,3},{3,2},{4,5},{5,4},{6,7},{7,6},{8,9},{9,8},{10,11... | collective-permute-start | bytes 1179656 | tf_op jit(solution)/shard_map/ppermute | solution.py:757
  5.4 6.8 %collective-permute-start.5 = (bf16[192,768]{1,0:T(8,128)(2,1)S(1)}, bf16[192,768]{1,0:T(8,128)(2,1)S(1)}, u32[]{:S(2)}, u32[]{:S(2)}) collective-permute-start(bf16[192,768]{1,0:T(8,128)(2,1)S(1)} %get-tuple-element.63.refs_0_), channel_id=1, source_target_pairs={{0,8},{2,6},{8,16},{10,2},{16,24},{18,10},{24,28},{26,18},{28,20},... | collective-permute-start | bytes 884744 | tf_op jit(solution)/shard_map/ppermute | solution.py:89
  7.1 16.2 %collective-permute-start.3 = (bf16[576,512]{1,0:T(8,128)(2,1)S(1)}, bf16[576,512]{1,0:T(8,128)(2,1)S(1)}, u32[]{:S(2)}, u32[]{:S(2)}) collective-permute-start(bf16[576,512]{1,0:T(8,128)(2,1)S(1)} %get-tuple-element.62.refs_0_), channel_id=1, source_target_pairs={{0,8},{2,6},{8,16},{10,2},{16,24},{18,10},{24,28},{26,18},{28,20},... | collective-permute-start | bytes 1769480 | tf_op jit(solution)/shard_map/ppermute | solution.py:89
  10.2 4.0 %copy-start.3 = (bf16[128,1536]{1,0:T(8,128)(2,1)S(1)}, bf16[128,1536]{1,0:T(8,128)(2,1)}, u32[]{:S(2)}) copy-start(bf16[128,1536]{1,0:T(8,128)(2,1)} %tokens.1) | copy-start | bytes 1179652
  10.2 4.0 %copy-start.4 = (bf16[1536,768]{1,0:T(8,128)(2,1)S(1)}, bf16[1536,768]{1,0:T(8,128)(2,1)}, u32[]{:S(2)}) copy-start(bf16[1536,768]{1,0:T(8,128)(2,1)} %w_query.1) | copy-start | bytes 7077892
  12.2 14.7 %collective-permute-start.10 = (bf16[192,768]{1,0:T(8,128)(2,1)S(1)}, bf16[192,768]{1,0:T(8,128)(2,1)S(1)}, u32[]{:S(2)}, u32[]{:S(2)}) collective-permute-start(bf16[192,768]{1,0:T(8,128)(2,1)S(1)} %collective-permute-done.5.refs_1_), channel_id=1, source_target_pairs={{0,2},{2,0},{4,6},{6,4},{8,10},{10,8},{12,14},{14,12},{16,18},{18,... | collective-permute-start | bytes 884744 | tf_op jit(solution)/shard_map/ppermute | solution.py:98
  12.2 9.5 %collective-permute-start.7 = (bf16[192,768]{1,0:T(8,128)(2,1)S(1)}, bf16[192,768]{1,0:T(8,128)(2,1)S(1)}, u32[]{:S(2)}, u32[]{:S(2)}) collective-permute-start(bf16[192,768]{1,0:T(8,128)(2,1)S(1)} %collective-permute-done.5.refs_1_), channel_id=1, source_target_pairs={{0,8},{2,6},{8,16},{10,2},{16,24},{18,10},{24,28},{26,18},{28,20},... | collective-permute-start | bytes 884744 | tf_op jit(solution)/shard_map/ppermute | solution.py:89
  16.4 7.0 %collective-permute-start.6 = (bf16[128,512]{1,0:T(8,128)(2,1)S(1)}, bf16[128,512]{1,0:T(8,128)(2,1)S(1)}, u32[]{:S(2)}, u32[]{:S(2)}) collective-permute-start(bf16[128,512]{1,0:T(8,128)(2,1)S(1)} %get-tuple-element.71), channel_id=1, source_target_pairs={{0,2},{2,4},{4,6},{6,8},{8,10},{10,12},{12,14},{14,16},{16,18},{18... | collective-permute-start | bytes 393224 | tf_op jit(solution)/shard_map/ppermute | solution.py:775
  21.6 5.2 %collective-permute-start.11 = (bf16[192,768]{1,0:T(8,128)(2,1)S(1)}, bf16[192,768]{1,0:T(8,128)(2,1)S(1)}, u32[]{:S(2)}, u32[]{:S(2)}) collective-permute-start(bf16[192,768]{1,0:T(8,128)(2,1)S(1)} %collective-permute-done.7.refs_2_), channel_id=1, source_target_pairs={{0,2},{2,0},{4,6},{6,4},{8,10},{10,8},{12,14},{14,12},{16,18},{18,... | collective-permute-start | bytes 884744 | tf_op jit(solution)/shard_map/ppermute | solution.py:98
  21.6 6.7 %collective-permute-start.9 = (bf16[192,768]{1,0:T(8,128)(2,1)S(1)}, bf16[192,768]{1,0:T(8,128)(2,1)S(1)}, u32[]{:S(2)}, u32[]{:S(2)}) collective-permute-start(bf16[192,768]{1,0:T(8,128)(2,1)S(1)} %collective-permute-done.7.refs_2_), channel_id=1, source_target_pairs={{0,8},{2,6},{8,16},{10,2},{16,24},{18,10},{24,28},{26,18},{28,20},... | collective-permute-start | bytes 884744 | tf_op jit(solution)/shard_map/ppermute | solution.py:89
  23.3 12.9 %collective-permute-start.8 = (bf16[576,512]{1,0:T(8,128)(2,1)S(1)}, bf16[576,512]{1,0:T(8,128)(2,1)}, u32[]{:S(2)}, u32[]{:S(2)}) collective-permute-start(bf16[576,512]{1,0:T(8,128)(2,1)S(1)} %collective-permute-done.3.refs_1_), channel_id=1, source_target_pairs={{0,8},{2,6},{8,16},{10,2},{16,24},{18,10},{24,28},{26,18},{28,20},... | collective-permute-start | bytes 1769480 | tf_op jit(solution)/shard_map/ppermute | solution.py:89
  28.4 1.8 %collective-permute-start.13 = (bf16[192,768]{1,0:T(8,128)(2,1)S(1)}, bf16[192,768]{1,0:T(8,128)(2,1)S(1)}, u32[]{:S(2)}, u32[]{:S(2)}) collective-permute-start(bf16[192,768]{1,0:T(8,128)(2,1)S(1)} %collective-permute-done.9.refs_3_), channel_id=1, source_target_pairs={{0,2},{2,0},{4,6},{6,4},{8,10},{10,8},{12,14},{14,12},{16,18},{18,... | collective-permute-start | bytes 884744 | tf_op jit(solution)/shard_map/ppermute | solution.py:98
  28.4 7.9 %collective-permute-start.12 = (bf16[96,768]{1,0:T(8,128)(2,1)S(1)}, bf16[96,768]{1,0:T(8,128)(2,1)S(1)}, u32[]{:S(2)}, u32[]{:S(2)}) collective-permute-start(bf16[96,768]{1,0:T(8,128)(2,1)S(1)} %slice.3), channel_id=1, source_target_pairs={{0,8},{2,6},{8,16},{10,2},{16,24},{18,10},{24,28},{26,18},{28,20},... | collective-permute-start | bytes 442376 | tf_op jit(solution)/shard_map/ppermute | solution.py:89
  36.3 10.1 %collective-permute-start.14 = (bf16[576,512]{1,0:T(8,128)(2,1)}, bf16[576,512]{1,0:T(8,128)(2,1)S(1)}, u32[]{:S(2)}, u32[]{:S(2)}) collective-permute-start(bf16[576,512]{1,0:T(8,128)(2,1)} %collective-permute-done.8.refs_2_), channel_id=1, source_target_pairs={{0,8},{2,6},{8,16},{10,2},{16,24},{18,10},{24,28},{26,18},{28,20},... | collective-permute-start | bytes 1769480 | tf_op jit(solution)/shard_map/ppermute | solution.py:89
  38.0 1.4 %collective-permute-start.15 = (bf16[96,768]{1,0:T(8,128)(2,1)S(1)}, bf16[96,768]{1,0:T(8,128)(2,1)S(1)}, u32[]{:S(2)}, u32[]{:S(2)}) collective-permute-start(bf16[96,768]{1,0:T(8,128)(2,1)S(1)} %collective-permute-done.12.refs_7_), channel_id=1, source_target_pairs={{0,2},{2,0},{4,6},{6,4},{8,10},{10,8},{12,14},{14,12},{16,18},{18,... | collective-permute-start | bytes 442376 | tf_op jit(solution)/shard_map/ppermute | solution.py:98
  40.5 15.4 %collective-permute-start.17 = (bf16[128,1536]{1,0:T(8,128)(2,1)S(1)}, bf16[128,1536]{1,0:T(8,128)(2,1)}, u32[]{:S(2)}, u32[]{:S(2)}) collective-permute-start(bf16[128,1536]{1,0:T(8,128)(2,1)S(1)} %outward_send.1), channel_id=1, source_target_pairs={{0,1},{1,0},{2,3},{3,2},{4,5},{5,4},{6,7},{7,6},{8,9},{9,8},{10,11... | collective-permute-start | bytes 1179656 | tf_op jit(solution)/shard_map/ppermute | solution.py:796
  42.1 17.5 %collective-permute-start.18 = (bf16[576,512]{1,0:T(8,128)(2,1)S(1)}, bf16[576,512]{1,0:T(8,128)(2,1)}, u32[]{:S(2)}, u32[]{:S(2)}) collective-permute-start(bf16[576,512]{1,0:T(8,128)(2,1)S(1)} %collective-permute-done.3.refs_1_), channel_id=1, source_target_pairs={{0,2},{2,0},{4,6},{6,4},{8,10},{10,8},{12,14},{14,12},{16,18},{18,... | collective-permute-start | bytes 1769480 | tf_op jit(solution)/shard_map/ppermute | solution.py:98
  42.1 17.5 %collective-permute-start.19 = (bf16[576,512]{1,0:T(8,128)(2,1)}, bf16[576,512]{1,0:T(8,128)(2,1)}, u32[]{:S(2)}, u32[]{:S(2)}) collective-permute-start(bf16[576,512]{1,0:T(8,128)(2,1)} %collective-permute-done.8.refs_2_), channel_id=1, source_target_pairs={{0,2},{2,0},{4,6},{6,4},{8,10},{10,8},{12,14},{14,12},{16,18},{18,... | collective-permute-start | bytes 1769480 | tf_op jit(solution)/shard_map/ppermute | solution.py:98
  46.4 0.8 %copy-start = (bf16[576,512]{1,0:T(8,128)(2,1)}, bf16[576,512]{1,0:T(8,128)(2,1)S(1)}, u32[]{:S(2)}) copy-start(bf16[576,512]{1,0:T(8,128)(2,1)S(1)} %collective-permute-done.14.whole.refs_0_) | copy-start | bytes 1769476
  48.9 7.1 %collective-permute-start.16 = (bf16[288,512]{1,0:T(8,128)(2,1)}, bf16[288,512]{1,0:T(8,128)(2,1)}, u32[]{:S(2)}, u32[]{:S(2)}) collective-permute-start(bf16[288,512]{1,0:T(8,128)(2,1)} %cut.1), channel_id=1, source_target_pairs={{0,8},{2,6},{8,16},{10,2},{16,24},{18,10},{24,28},{26,18},{28,20},... | collective-permute-start | bytes 884744 | tf_op jit(solution)/shard_map/ppermute | solution.py:89
  50.6 12.3 %collective-permute-start.21 = (bf16[576,512]{1,0:T(8,128)(2,1)}, bf16[576,512]{1,0:T(8,128)(2,1)}, u32[]{:S(2)}, u32[]{:S(2)}) collective-permute-start(bf16[576,512]{1,0:T(8,128)(2,1)} %copy-done), channel_id=1, source_target_pairs={{0,2},{2,0},{4,6},{6,4},{8,10},{10,8},{12,14},{14,12},{16,18},{18,... | collective-permute-start | bytes 1769480 | tf_op jit(solution)/shard_map/ppermute | solution.py:98
  50.6 20.8 %all-to-all-start = ((bf16[16,144,128]{2,1,0:T(8,128)(2,1)}), bf16[16,144,128]{2,1,0:T(8,128)(2,1)S(1)}, u32[]{:S(2)}, u32[]{:S(2)}) async-start(bf16[16,144,128]{2,1,0:T(8,128)(2,1)} %bundle.1), calls=%async_computation | async-start | bytes 1179648 | tf_op jit(solution)/shard_map/all_to_all | solution.py:803
  56.0 6.9 %collective-permute-start.22 = (bf16[288,512]{1,0:T(8,128)(2,1)}, bf16[288,512]{1,0:T(8,128)(2,1)S(1)}, u32[]{:S(2)}, u32[]{:S(2)}) collective-permute-start(bf16[288,512]{1,0:T(8,128)(2,1)} %collective-permute-done.16.refs_2_), channel_id=1, source_target_pairs={{0,2},{2,0},{4,6},{6,4},{8,10},{10,8},{12,14},{14,12},{16,18},{18,... | collective-permute-start | bytes 884744 | tf_op jit(solution)/shard_map/ppermute | solution.py:98
  58.0 4.9 %collective-permute-start.20 = (bf16[32,1536]{1,0:T(8,128)(2,1)S(1)}, bf16[32,1536]{1,0:T(8,128)(2,1)S(1)}, u32[]{:S(2)}, u32[]{:S(2)}) collective-permute-start(bf16[32,1536]{1,0:T(8,128)(2,1)S(1)} %get-tuple-element.109), channel_id=1, source_target_pairs={{0,1},{1,0},{2,3},{3,2},{4,5},{5,4},{6,7},{7,6},{8,9},{9,8},{10,11... | collective-permute-start | bytes 294920 | tf_op jit(solution)/shard_map/ppermute | solution.py:808
  59.5 3.4 %copy-start.1 = (bf16[576,512]{1,0:T(8,128)(2,1)S(1)}, bf16[576,512]{1,0:T(8,128)(2,1)}, u32[]{:S(2)}) copy-start(bf16[576,512]{1,0:T(8,128)(2,1)} %copy-done) | copy-start | bytes 1769476
  62.9 8.5 %copy-start.2 = (bf16[512,4,128]{2,1,0:T(4,128)(2,1)S(1)}, bf16[512,4,128]{2,1,0:T(4,128)(2,1)}, u32[]{:S(2)}) copy-start(bf16[512,4,128]{2,1,0:T(4,128)(2,1)} %param.25) | copy-start | bytes 1572868
  65.3 4.7 %collective-permute-start.23 = (bf16[32,1536]{1,0:T(8,128)(2,1)S(1)}, bf16[32,1536]{1,0:T(8,128)(2,1)S(1)}, u32[]{:S(2)}, u32[]{:S(2)}) collective-permute-start(bf16[32,1536]{1,0:T(8,128)(2,1)S(1)} %get-tuple-element.117), channel_id=1, source_target_pairs={{0,1},{1,0},{2,3},{3,2},{4,5},{5,4},{6,7},{7,6},{8,9},{9,8},{10,11... | collective-permute-start | bytes 294920 | tf_op jit(solution)/shard_map/ppermute | solution.py:815

commit v17 on v14

--- a/solution.py
+++ b/solution.py
@@ -414,9 +414,8 @@
     out[...] = outward_rows(True, groups, unit_rows, early, late, parts, w_out, rows).astype(bf16)
 
 
-def keep_kernel(groups, unit_rows, n_parts, early, late, tokens, flat_gain, *refs):
-    parts, (out, gain, w_out, rows) = refs[:n_parts], refs[n_parts:]
-    gain[...] = flat_gain[...].reshape(gain.shape)
+def keep_kernel(groups, unit_rows, n_parts, early, late, tokens, *refs):
+    parts, (out, w_out, rows) = refs[:n_parts], refs[n_parts:]
     made = outward_rows(False, groups, unit_rows, early, late, parts, w_out, rows)
     out[...] = tokens[...].astype(f32) + made
 
@@ -435,16 +434,13 @@
     )(early, late, *parts)
 
 
-def outward_keep(groups, early, late, tokens, gain, parts, unit_rows):
+def outward_keep(groups, early, late, tokens, parts, unit_rows):
     width, depth = groups * unit_rows, parts[0].shape[1]
     return pl.pallas_call(
         functools.partial(keep_kernel, groups, unit_rows, len(parts)),
-        out_shape=(
-            jax.ShapeDtypeStruct(tokens.shape, f32),
-            jax.ShapeDtypeStruct((1, width), f32),
-        ),
-        in_specs=[VMEM] * (4 + len(parts)),
-        out_specs=(VMEM, VMEM),
+        out_shape=jax.ShapeDtypeStruct(tokens.shape, f32),
+        in_specs=[VMEM] * (3 + len(parts)),
+        out_specs=VMEM,
         scratch_shapes=[
             pltpu.VMEM((width, depth), bf16),
             pltpu.VMEM(early.shape, bf16),
@@ -452,19 +448,22 @@
         compiler_params=PARAMS,
         cost_estimate=reads(2 * width * depth),
         name="outward_keep",
-    )(early, late, tokens, gain, *parts)
-
-
-def route_kernel(mine, arrived, gain, place, residual, moe_in, sent):
+    )(early, late, tokens, *parts)
+
+
+def route_kernel(mine, arrived, flat_gain, place, residual, moe_in, sent, gain, gain_sem):
+    copy = pltpu.make_async_copy(flat_gain, gain, gain_sem)
+    copy.start()
     added = (mine[...] + arrived[...].astype(f32)).astype(bf16)
     residual[...] = added
-    moe_in[...] = normalized(added.astype(f32), gain[...])
+    copy.wait()
+    moe_in[...] = normalized(added.astype(f32), gain[...].reshape(1, gain.shape[0]))
     cap = sent.shape[0]
     rows = jnp.dot(place[cap:, :], moe_in[...], preferred_element_type=f32)
     sent[...] = rows.astype(bf16)
 
 
-def route(mine, arrived, gain, place):
+def route(mine, arrived, flat_gain, place):
     cap = place.shape[0] // 2
     return pl.pallas_call(
         route_kernel,
@@ -473,12 +472,13 @@
             jax.ShapeDtypeStruct(mine.shape, bf16),
             jax.ShapeDtypeStruct((cap, mine.shape[1]), bf16),
         ),
-        in_specs=[VMEM] * 4,
+        in_specs=[VMEM, VMEM, ANY, VMEM],
         out_specs=(VMEM,) * 3,
-        compiler_params=PARAMS,
-        cost_estimate=reads(10 * mine.shape[0] * mine.shape[1]),
+        scratch_shapes=[pltpu.VMEM(flat_gain.shape, f32), pltpu.SemaphoreType.DMA],
+        compiler_params=PARAMS,
+        cost_estimate=reads(16 << 20),
         name="route",
-    )(mine, arrived, gain, place)
+    )(mine, arrived, pltpu.with_memory_space_constraint(flat_gain, pltpu.HBM), place)
 
 
 def expert_pieces(gate_up, down, up_rows, down_rows, width):
@@ -587,7 +587,7 @@
         scratch_shapes=[pltpu.VMEM((2 * count, model), bf16)],
         input_output_aliases={2: 2, 3: 3},
         compiler_params=PARAMS,
-        cost_estimate=takes(6.2),
+        cost_estimate=pl.CostEstimate(flops=int(5.7 * 1.15e9), bytes_accessed=1, transcendentals=0),
         name="expert",
     )(own, other, *staged, *[part for part, _ in late])[:2]
 
@@ -738,15 +738,15 @@
     cosine, sine, past, place, send, tags, gain = prepare(
         groups, slots_dev, positions, cache_slot, expert_ids, attn_gain
     )
-    other_tokens, cosine, flat_kv = out_ring.pin(other_tokens, cosine, flat_kv)
+    cosine, flat_kv = out_ring.pin(cosine, flat_kv)
     out_ring.step()
 
     q, kv, tail = project(tokens, other_tokens, gain, cosine, sine, w_query, flat_kv)
     seam = lax.ppermute(tail, "grp", [(g, g + 1) for g in range(groups - 1)])
-    q = out_ring.pin(q)
+    late = attend_late(q, kv, past)
+    late = out_ring.pin(late)
     out_ring.step()
     out_ring.share(2)
-    late = attend_late(q, kv, past)
     seam, late = together((seam, late))
     seam = expert_ring.pin(seam)
     expert_ring.step()
@@ -765,18 +765,15 @@
     sent = outward_send(groups, early, late, out_ring.parts(), out_ring.unit_rows)
     arrived = swap(sent)
     early = together((early, sent))[0]
-    mine, late_gain = outward_keep(
-        groups, early, late, tokens, moe_gain, out_ring.parts(), out_ring.unit_rows
-    )
-    late_gain = expert_ring.pin(late_gain)
-    expert_ring.share()
+    mine = outward_keep(groups, early, late, tokens, out_ring.parts(), out_ring.unit_rows)
+    mine = expert_ring.pin(mine)
     expert_ring.step()
     outgoing = together((outgoing, sent))[0]
     arrived_cache = lax.all_to_all(outgoing, "grp", split_axis=0, concat_axis=0, tiled=True)
-    arrived, late_gain = expert_ring.pin(arrived, late_gain)
+    arrived, mine, expert_ring.mine[1:] = together((arrived, mine, expert_ring.mine[1:]))
     expert_ring.share()
 
-    residual, moe_in, sent_rows = route(mine, arrived, late_gain, place)
+    residual, moe_in, sent_rows = route(mine, arrived, moe_gain, place)
     landed = swap(sent_rows)
     parts_early, parts_late = expert_ring.split()
     gates, own_rows, spread, *staged = gate(

time: 72.8 us -> 79.1 us (1.087)
  waiting for transfers between devices: 15.6 us -> 23.3 us
  local copies, waits for them, and re-layouts: 4.84 us -> 3.56 us
    ppermute x8, waiting for transfers between devices: 7.73 us -> 13.8 us  [step(): self.mine.append(self.across(held))]
    ppermute x1, waiting for transfers between devices: 0.01 us -> 2.74 us  [two_lane_shards(): arrived = swap(sent)]
    ppermute x1, waiting for transfers between devices: 2.11 us -> 0.28 us  [two_lane_shards(): other_tokens = swap(tokens)]
    all_to_all x1, starting transfers between devices: 4.56 us -> 6.35 us  [two_lane_shards(): lax.all_to_all(outgoing, 'grp', split_axis=0, concat_axis=0, tiled=True)]
    ppermute x8, starting transfers between devices: 15.2 us -> 14 us  [step(): self.mine.append(self.across(held))]
    all_to_all x1, waiting for transfers between devices: 0.01 us -> 0.85 us  [two_lane_shards(): lax.all_to_all(outgoing, 'grp', split_axis=0, concat_axis=0, tiled=True)]
    unnamed x13 -> x11, local copies, waits for them, and re-layouts: 3.13 us -> 2.57 us
  transfers between devices with their start and end apart: 25 -> 25, of which waited for: 8 -> 12; matrix products, arithmetic and copies ran while one was open for 5% -> 4% of each run, Pallas kernels for 26% -> 23%
where the time goes in v17:
time: 79.1 us; the launch traced here: 78.7 us
  starting transfers between devices  31.4 us (40%)
  waiting for transfers between devices  23.3 us (29%)
  Pallas kernels  19.7 us (25%)
  local copies, waits for them, and re-layouts  3.56 us (5%)
  between operations  0.82 us (1%)
    ppermute x8, starting transfers between devices, step(): self.mine.append(self.across(held))  14 us
    ppermute x8, waiting for transfers between devices, step(): self.mine.append(self.across(held))  13.8 us
    all_to_all x1, starting transfers between devices, two_lane_shards(): lax.all_to_all(outgoing, 'grp', split_axis=0, concat_axis=0, tiled=True)  6.35 us
    ppermute x1, waiting for transfers between devices, two_lane_shards(): returned = swap(back)  3.13 us
    ppermute x1, waiting for transfers between devices, two_lane_shards(): arrived = swap(sent)  2.74 us
    unnamed x11, local copies, waits for them, and re-layouts  2.57 us
    ppermute x1, starting transfers between devices, two_lane_shards(): other_tokens = swap(tokens)  2.56 us
    pallas_call x1, Pallas kernels, expert(): pl.pallas_call(functools.partial(expert_kernel, groups, up_rows, down_row...  2.44 us
  transfers between devices with their start and end apart: 25, of which 12 were waited for; matrix products, arithmetic and copies ran while one was open for 4% of the time, Pallas kernels for 23%

profile of v17, /device:TPU:0, one launch (start us, length us, event | category | flops | bytes accessed | tf_op | source)
XLA Modules:
  0.0 78.7 jit_solution(7091776953677804239)
XLA Ops:
  1.7 2.6 %collective-permute-start.4 = (bf16[128,1536]{1,0:T(8,128)(2,1)}, bf16[128,1536]{1,0:T(8,128)(2,1)S(1)}, u32[]{:S(2)}, u32[]{:S(2)}) collective-permute-start(bf16[128,1536]{1,0:T(8,128)(2,1)} %tokens.1), channel_id=1, source_target_pairs={{0,1},{1,0},{2,3},{3,2},{4,5},{5,4},{6,7},{7,6},{8,9},{9,8},{10,11... | collective-permute-start | bytes 1179656 | tf_op jit(solution)/shard_map/ppermute | solution.py:727
  5.4 1.7 %collective-permute-start.5 = (bf16[192,768]{1,0:T(8,128)(2,1)S(1)}, bf16[192,768]{1,0:T(8,128)(2,1)S(1)}, u32[]{:S(2)}, u32[]{:S(2)}) collective-permute-start(bf16[192,768]{1,0:T(8,128)(2,1)S(1)} %get-tuple-element.66.refs_0_), channel_id=1, source_target_pairs={{0,8},{2,6},{8,16},{10,2},{16,24},{18,10},{24,28},{26,18},{28,20},... | collective-permute-start | bytes 884744 | tf_op jit(solution)/shard_map/ppermute | solution.py:70
  7.1 1.6 %collective-permute-start.3 = (bf16[576,512]{1,0:T(8,128)(2,1)S(1)}, bf16[576,512]{1,0:T(8,128)(2,1)S(1)}, u32[]{:S(2)}, u32[]{:S(2)}) collective-permute-start(bf16[576,512]{1,0:T(8,128)(2,1)S(1)} %get-tuple-element.65.refs_0_), channel_id=1, source_target_pairs={{0,8},{2,6},{8,16},{10,2},{16,24},{18,10},{24,28},{26,18},{28,20},... | collective-permute-start | bytes 1769480 | tf_op jit(solution)/shard_map/ppermute | solution.py:70
  8.7 1.5 %prepare.1 = (f32[256,128]{1,0:T(8,128)S(1)}, f32[256,128]{1,0:T(8,128)S(1)}, f32[256,128]{1,0:T(8,128)S(1)}, bf16[64,128]{1,0:T(8,128)(2,1)S(1)}, bf16[512,256]...) custom-call(s32[1,256]{1,0:T(1,128)} %bitcast.26, s32[1,256]{1,0:T(1,128)} %bitcast.27, ...), custom_call_target="tpu_custom_call" | custom-call | flops 1 | bytes 1 | tf_op jit(solution)/shard_map/prepare/pallas_call | solution.py:266
  10.2 1.8 %copy.19 = bf16[192,8,4,128]{3,1,2,0:T(8,128)(2,1)S(1)} copy(bf16[192,8,4,128]{3,2,1,0:T(4,128)(2,1)} %bitcast.15) | data formatting | bytes 3145728
  12.2 1.7 %collective-permute-start.7 = (bf16[192,768]{1,0:T(8,128)(2,1)S(1)}, bf16[192,768]{1,0:T(8,128)(2,1)S(1)}, u32[]{:S(2)}, u32[]{:S(2)}) collective-permute-start(bf16[192,768]{1,0:T(8,128)(2,1)S(1)} %collective-permute-done.5.refs_1_), channel_id=1, source_target_pairs={{0,8},{2,6},{8,16},{10,2},{16,24},{18,10},{24,28},{26,18},{28,20},... | collective-permute-start | bytes 884744 | tf_op jit(solution)/shard_map/ppermute | solution.py:70
  14.1 2.2 %project.1 = (bf16[256,768]{1,0:T(8,128)(2,1)S(1)}, bf16[256,512]{1,0:T(8,128)(2,1)S(1)}, bf16[128,512]{1,0:T(8,128)(2,1)S(1)}) custom-call(bf16[128,1536]{1,0:T(8,128)(2,1)S(1)} %copy-done.1, bf16[128,1536]{1,0:T(8,128)(2,1)S(1)} %collective-permute-done.4.other, f32[1,1536]{1,0:T(1,128)S(1)} %get-tuple-element.68.gain, ...), custom_call_target="tpu_custom_call" | custom-call | flops 9200000000 | bytes 64000000 | tf_op jit(solution)/shard_map/project/pallas_call | solution.py:316
  16.4 1.8 %collective-permute-start.6 = (bf16[128,512]{1,0:T(8,128)(2,1)S(1)}, bf16[128,512]{1,0:T(8,128)(2,1)S(1)}, u32[]{:S(2)}, u32[]{:S(2)}) collective-permute-start(bf16[128,512]{1,0:T(8,128)(2,1)S(1)} %get-tuple-element.74), channel_id=1, source_target_pairs={{0,2},{2,4},{4,6},{6,8},{8,10},{10,12},{12,14},{14,16},{16,18},{18... | collective-permute-start | bytes 393224 | tf_op jit(solution)/shard_map/ppermute | solution.py:745
  18.2 1.3 %attend_late.1.late = bf16[128,768]{1,0:T(8,128)(2,1)S(1)} custom-call(bf16[256,768]{1,0:T(8,128)(2,1)S(1)} %get-tuple-element.76.q, bf16[256,512]{1,0:T(8,128)(2,1)S(1)} %get-tuple-element.91.kv, f32[256,128]{1,0:T(8,128)S(1)} %get-tuple-element.78.past), custom_call_target="tpu_custom_call" | custom-call | flops 2300000000 | bytes 16000000 | tf_op jit(solution)/shard_map/attend_late/pallas_call | solution.py:372
  19.5 2.1 %collective-permute-done.7.refs_2_ = bf16[192,768]{1,0:T(8,128)(2,1)S(1)} collective-permute-done((bf16[192,768]{1,0:T(8,128)(2,1)S(1)}, bf16[192,768]{1,0:T(8,128)(2,1)S(1)}, u32[]{:S(2)}, u32[]{:S(2)}) %collective-permute-start.7) | collective-permute-done | bytes 294944 | tf_op jit(solution)/shard_map/ppermute | solution.py:70
  21.6 1.7 %collective-permute-start.9 = (bf16[192,768]{1,0:T(8,128)(2,1)S(1)}, bf16[192,768]{1,0:T(8,128)(2,1)S(1)}, u32[]{:S(2)}, u32[]{:S(2)}) collective-permute-start(bf16[192,768]{1,0:T(8,128)(2,1)S(1)} %collective-permute-done.7.refs_2_), channel_id=1, source_target_pairs={{0,8},{2,6},{8,16},{10,2},{16,24},{18,10},{24,28},{26,18},{28,20},... | collective-permute-start | bytes 884744 | tf_op jit(solution)/shard_map/ppermute | solution.py:70
  23.3 2.1 %collective-permute-start.8 = (bf16[576,512]{1,0:T(8,128)(2,1)S(1)}, bf16[576,512]{1,0:T(8,128)(2,1)S(1)}, u32[]{:S(2)}, u32[]{:S(2)}) collective-permute-start(bf16[576,512]{1,0:T(8,128)(2,1)S(1)} %collective-permute-done.3.refs_1_), channel_id=1, source_target_pairs={{0,8},{2,6},{8,16},{10,2},{16,24},{18,10},{24,28},{26,18},{28,20},... | collective-permute-start | bytes 1769480 | tf_op jit(solution)/shard_map/ppermute | solution.py:70
  25.4 1.5 %attend_early.1.early = bf16[128,768]{1,0:T(8,128)(2,1)S(1)} custom-call(bf16[256,768]{1,0:T(8,128)(2,1)S(1)} %get-tuple-element.76.q, bf16[256,512]{1,0:T(8,128)(2,1)S(1)} %get-tuple-element.91.kv, bf16[128,512]{1,0:T(8,128)(2,1)S(1)} %collective-permute-done.6.seam, f32[256,128]{1,0:T(8,128)S(1)} %get-tuple-element.78.past), custom_call_target="tpu_custom_call" | custom-call | flops 2300000000 | bytes 16000000 | tf_op jit(solution)/shard_map/attend_early/pallas_call | solution.py:384
  26.9 1.5 %collective-permute-done.9.refs_3_ = bf16[192,768]{1,0:T(8,128)(2,1)S(1)} collective-permute-done((bf16[192,768]{1,0:T(8,128)(2,1)S(1)}, bf16[192,768]{1,0:T(8,128)(2,1)S(1)}, u32[]{:S(2)}, u32[]{:S(2)}) %collective-permute-start.9) | collective-permute-done | bytes 294944 | tf_op jit(solution)/shard_map/ppermute | solution.py:70
  28.4 1.7 %collective-permute-start.12 = (bf16[96,768]{1,0:T(8,128)(2,1)S(1)}, bf16[96,768]{1,0:T(8,128)(2,1)S(1)}, u32[]{:S(2)}, u32[]{:S(2)}) collective-permute-start(bf16[96,768]{1,0:T(8,128)(2,1)S(1)} %slice.6), channel_id=1, source_target_pairs={{0,8},{2,6},{8,16},{10,2},{16,24},{18,10},{24,28},{26,18},{28,20},... | collective-permute-start | bytes 442376 | tf_op jit(solution)/shard_map/ppermute | solution.py:70
  30.1 1.4 %bundle.1 = bf16[16,144,128]{2,1,0:T(8,128)(2,1)} custom-call(bf16[512,256]{1,0:T(8,128)(2,1)S(1)} %get-tuple-element.90.send, bf16[256,512]{1,0:T(8,128)(2,1)S(1)} %get-tuple-element.91.kv, bf16[256,128]{1,0:T(8,128)(2,1)S(1)} %get-tuple-element.92.tags), custom_call_target="tpu_custom_call" | custom-call | flops 1 | bytes 1 | tf_op jit(solution)/shard_map/bundle/pallas_call | solution.py:644
  31.5 4.7 %collective-permute-done.12.refs_7_ = bf16[96,768]{1,0:T(8,128)(2,1)S(1)} collective-permute-done((bf16[96,768]{1,0:T(8,128)(2,1)S(1)}, bf16[96,768]{1,0:T(8,128)(2,1)S(1)}, u32[]{:S(2)}, u32[]{:S(2)}) %collective-permute-start.12) | collective-permute-done | bytes 147488 | tf_op jit(solution)/shard_map/ppermute | solution.py:70
  36.3 1.7 %collective-permute-start.16 = (bf16[576,512]{1,0:T(8,128)(2,1)S(1)}, bf16[576,512]{1,0:T(8,128)(2,1)}, u32[]{:S(2)}, u32[]{:S(2)}) collective-permute-start(bf16[576,512]{1,0:T(8,128)(2,1)S(1)} %collective-permute-done.8.refs_2_), channel_id=1, source_target_pairs={{0,8},{2,6},{8,16},{10,2},{16,24},{18,10},{24,28},{26,18},{28,20},... | collective-permute-start | bytes 1769480 | tf_op jit(solution)/shard_map/ppermute | solution.py:70
  38.0 1.4 %collective-permute-done.14.refs_8_ = bf16[96,768]{1,0:T(8,128)(2,1)S(1)} collective-permute-done((bf16[96,768]{1,0:T(8,128)(2,1)S(1)}, bf16[96,768]{1,0:T(8,128)(2,1)S(1)}, u32[]{:S(2)}, u32[]{:S(2)}) %collective-permute-start.14) | collective-permute-done | bytes 147488 | tf_op jit(solution)/shard_map/ppermute | solution.py:79
  40.5 1.6 %collective-permute-start.15 = (bf16[128,1536]{1,0:T(8,128)(2,1)S(1)}, bf16[128,1536]{1,0:T(8,128)(2,1)S(1)}, u32[]{:S(2)}, u32[]{:S(2)}) collective-permute-start(bf16[128,1536]{1,0:T(8,128)(2,1)S(1)} %outward_send.1), channel_id=1, source_target_pairs={{0,1},{1,0},{2,3},{3,2},{4,5},{5,4},{6,7},{7,6},{8,9},{9,8},{10,11... | collective-permute-start | bytes 1179656 | tf_op jit(solution)/shard_map/ppermute | solution.py:766
  42.1 1.1 %outward_keep.1.mine = f32[128,1536]{1,0:T(8,128)S(1)} custom-call(bf16[128,768]{1,0:T(8,128)(2,1)S(1)} %attend_early.1.early, bf16[128,768]{1,0:T(8,128)(2,1)S(1)} %attend_late.1.late, bf16[128,1536]{1,0:T(8,128)(2,1)S(1)} %copy-done.1, bf16[192,768]{1,0:T(8,128)(2,1)S(1)} %get-tuple-element.66.refs_0_, ...), custom_call_target="tpu_custom_call" | custom-call | flops 1 | bytes 2359296 | tf_op jit(solution)/shard_map/outward_keep/pallas_call | solution.py:439
  43.2 3.0 %collective-permute-done.16.refs_0_ = bf16[576,512]{1,0:T(8,128)(2,1)} collective-permute-done((bf16[576,512]{1,0:T(8,128)(2,1)S(1)}, bf16[576,512]{1,0:T(8,128)(2,1)}, u32[]{:S(2)}, u32[]{:S(2)}) %collective-permute-start.16) | collective-permute-done | bytes 589856 | tf_op jit(solution)/shard_map/ppermute | solution.py:70
  47.2 1.7 %collective-permute-start.17 = (bf16[288,512]{1,0:T(8,128)(2,1)S(1)}, bf16[288,512]{1,0:T(8,128)(2,1)S(1)}, u32[]{:S(2)}, u32[]{:S(2)}) collective-permute-start(bf16[288,512]{1,0:T(8,128)(2,1)S(1)} %slice.7), channel_id=1, source_target_pairs={{0,8},{2,6},{8,16},{10,2},{16,24},{18,10},{24,28},{26,18},{28,20},... | collective-permute-start | bytes 884744 | tf_op jit(solution)/shard_map/ppermute | solution.py:70
  49.0 2.7 %collective-permute-done.15.arrived = bf16[128,1536]{1,0:T(8,128)(2,1)S(1)} collective-permute-done((bf16[128,1536]{1,0:T(8,128)(2,1)S(1)}, bf16[128,1536]{1,0:T(8,128)(2,1)S(1)}, u32[]{:S(2)}, u32[]{:S(2)}) %collective-permute-start.15) | collective-permute-done | bytes 393248 | tf_op jit(solution)/shard_map/ppermute | solution.py:766
  51.7 2.3 %collective-permute-done.17.refs_2_ = bf16[288,512]{1,0:T(8,128)(2,1)S(1)} collective-permute-done((bf16[288,512]{1,0:T(8,128)(2,1)S(1)}, bf16[288,512]{1,0:T(8,128)(2,1)S(1)}, u32[]{:S(2)}, u32[]{:S(2)}) %collective-permute-start.17) | collective-permute-done | bytes 294944 | tf_op jit(solution)/shard_map/ppermute | solution.py:70
  55.3 6.4 %all-to-all-start = ((bf16[16,144,128]{2,1,0:T(8,128)(2,1)}), bf16[16,144,128]{2,1,0:T(8,128)(2,1)S(1)}, u32[]{:S(2)}, u32[]{:S(2)}) async-start(bf16[16,144,128]{2,1,0:T(8,128)(2,1)} %bundle.1), calls=%async_computation | async-start | bytes 1179648 | tf_op jit(solution)/shard_map/all_to_all | solution.py:772
  63.1 1.6 %collective-permute-start.20 = (bf16[32,1536]{1,0:T(8,128)(2,1)S(1)}, bf16[32,1536]{1,0:T(8,128)(2,1)S(1)}, u32[]{:S(2)}, u32[]{:S(2)}) collective-permute-start(bf16[32,1536]{1,0:T(8,128)(2,1)S(1)} %get-tuple-element.114), channel_id=1, source_target_pairs={{0,1},{1,0},{2,3},{3,2},{4,5},{5,4},{6,7},{7,6},{8,9},{9,8},{10,11... | collective-permute-start | bytes 294920 | tf_op jit(solution)/shard_map/ppermute | solution.py:777
  64.7 2.2 %gate.1 = (f32[128,40]{1,0:T(8,128)S(1)}, bf16[32,1536]{1,0:T(8,128)(2,1)S(1)}, bf16[128,64]{1,0:T(8,128)(2,1)S(1)}, bf16[1536,1024]{1,0:T(8,128)(2,1)S(1)}, bf16[512,1536]{1,0:T(8,128)(2,1)S(1)}) custom-call(bf16[128,1536]{1,0:T(8,128)(2,1)S(1)} %get-tuple-element.109.moe_in, bf16[40,1536]{1,0:T(8,128)(2,1)} %bitcast.21, s32[8,128]{1,0:T(8,128)} %bitcast.25, ...), custom_call_target="tpu_custom_call" | custom-call | flops 1 | bytes 1 | tf_op jit(solution)/shard_map/gate/pallas_call | solution.py:538
  68.0 2.4 %expert.1 = (bf16[32,1536]{1,0:T(8,128)(2,1)S(1)}, bf16[32,1536]{1,0:T(8,128)(2,1)S(1)}, bf16[1536,1024]{1,0:T(8,128)(2,1)S(1)}, bf16[512,1536]{1,0:T(8,128)(2,1)S(1)}) custom-call(bf16[32,1536]{1,0:T(8,128)(2,1)S(1)} %get-tuple-element.116.own, bf16[32,1536]{1,0:T(8,128)(2,1)S(1)} %collective-permute-done.20.other, ...), custom_call_target="tpu_custom_call", output_to_operand_aliasing={{2}: (2, {}), {3}: (3, {})} | custom-call | flops 6554999808 | bytes 1 | tf_op jit(solution)/shard_map/expert/pallas_call | solution.py:581
  70.5 1.6 %collective-permute-start.23 = (bf16[32,1536]{1,0:T(8,128)(2,1)S(1)}, bf16[32,1536]{1,0:T(8,128)(2,1)S(1)}, u32[]{:S(2)}, u32[]{:S(2)}) collective-permute-start(bf16[32,1536]{1,0:T(8,128)(2,1)S(1)} %get-tuple-element.123), channel_id=1, source_target_pairs={{0,1},{1,0},{2,3},{3,2},{4,5},{5,4},{6,7},{7,6},{8,9},{9,8},{10,11... | collective-permute-start | bytes 294920 | tf_op jit(solution)/shard_map/ppermute | solution.py:784
  72.0 3.1 %collective-permute-done.23.returned = bf16[32,1536]{1,0:T(8,128)(2,1)S(1)} collective-permute-done((bf16[32,1536]{1,0:T(8,128)(2,1)S(1)}, bf16[32,1536]{1,0:T(8,128)(2,1)S(1)}, u32[]{:S(2)}, u32[]{:S(2)}) %collective-permute-start.23) | collective-permute-done | bytes 98336 | tf_op jit(solution)/shard_map/ppermute | solution.py:784
  77.2 1.5 %write.1 = bf16[2048,128]{1,0:T(8,128)(2,1)} custom-call(bf16[16,144,128]{2,1,0:T(8,128)(2,1)S(1)} %all-to-all-done.arrived, bf16[2048,128]{1,0:T(8,128)(2,1)S(1)} %bitcast.14), custom_call_target="tpu_custom_call" | custom-call | flops 1 | bytes 2097152 | tf_op jit(solution)/shard_map/write/pallas_call | solution.py:685
  (44 shorter events, 10.6 us)
Async XLA Ops:
  0.6 3.6 %collective-permute-start.2 = (bf16[96,1536]{1,0:T(8,128)(2,1)}, bf16[96,1536]{1,0:T(8,128)(2,1)S(1)}, u32[]{:S(2)}, u32[]{:S(2)}) collective-permute-start(bf16[96,1536]{1,0:T(8,128)(2,1)} %bitcast.17), channel_id=1, source_target_pairs={{0,2},{2,0},{4,6},{6,4},{8,10},{10,8},{12,14},{14,12},{16,18},{18,... | collective-permute-start | bytes 884744 | tf_op jit(solution)/shard_map/ppermute | solution.py:730
  1.1 3.1 %collective-permute-start = (bf16[96,1024]{1,0:T(8,128)(2,1)}, bf16[96,1024]{1,0:T(8,128)(2,1)S(1)}, u32[]{:S(2)}, u32[]{:S(2)}) collective-permute-start(bf16[96,1024]{1,0:T(8,128)(2,1)} %bitcast.19), channel_id=1, source_target_pairs={{0,2},{2,0},{4,6},{6,4},{8,10},{10,8},{12,14},{14,12},{16,18},{18,... | collective-permute-start | bytes 589832 | tf_op jit(solution)/shard_map/ppermute | solution.py:730
  1.2 3.0 %collective-permute-start.1 = (bf16[32,1536]{1,0:T(8,128)(2,1)}, bf16[32,1536]{1,0:T(8,128)(2,1)S(1)}, u32[]{:S(2)}, u32[]{:S(2)}) collective-permute-start(bf16[32,1536]{1,0:T(8,128)(2,1)} %bitcast.22), channel_id=1, source_target_pairs={{0,2},{2,0},{4,6},{6,4},{8,10},{10,8},{12,14},{14,12},{16,18},{18,... | collective-permute-start | bytes 294920 | tf_op jit(solution)/shard_map/ppermute | solution.py:730
  1.7 12.5 %collective-permute-start.4 = (bf16[128,1536]{1,0:T(8,128)(2,1)}, bf16[128,1536]{1,0:T(8,128)(2,1)S(1)}, u32[]{:S(2)}, u32[]{:S(2)}) collective-permute-start(bf16[128,1536]{1,0:T(8,128)(2,1)} %tokens.1), channel_id=1, source_target_pairs={{0,1},{1,0},{2,3},{3,2},{4,5},{5,4},{6,7},{7,6},{8,9},{9,8},{10,11... | collective-permute-start | bytes 1179656 | tf_op jit(solution)/shard_map/ppermute | solution.py:727
  5.4 6.8 %collective-permute-start.5 = (bf16[192,768]{1,0:T(8,128)(2,1)S(1)}, bf16[192,768]{1,0:T(8,128)(2,1)S(1)}, u32[]{:S(2)}, u32[]{:S(2)}) collective-permute-start(bf16[192,768]{1,0:T(8,128)(2,1)S(1)} %get-tuple-element.66.refs_0_), channel_id=1, source_target_pairs={{0,8},{2,6},{8,16},{10,2},{16,24},{18,10},{24,28},{26,18},{28,20},... | collective-permute-start | bytes 884744 | tf_op jit(solution)/shard_map/ppermute | solution.py:70
  7.1 16.2 %collective-permute-start.3 = (bf16[576,512]{1,0:T(8,128)(2,1)S(1)}, bf16[576,512]{1,0:T(8,128)(2,1)S(1)}, u32[]{:S(2)}, u32[]{:S(2)}) collective-permute-start(bf16[576,512]{1,0:T(8,128)(2,1)S(1)} %get-tuple-element.65.refs_0_), channel_id=1, source_target_pairs={{0,8},{2,6},{8,16},{10,2},{16,24},{18,10},{24,28},{26,18},{28,20},... | collective-permute-start | bytes 1769480 | tf_op jit(solution)/shard_map/ppermute | solution.py:70
  10.2 4.0 %copy-start.1 = (bf16[128,1536]{1,0:T(8,128)(2,1)S(1)}, bf16[128,1536]{1,0:T(8,128)(2,1)}, u32[]{:S(2)}) copy-start(bf16[128,1536]{1,0:T(8,128)(2,1)} %tokens.1) | copy-start | bytes 1179652
  10.2 4.0 %copy-start.2 = (bf16[1536,768]{1,0:T(8,128)(2,1)S(1)}, bf16[1536,768]{1,0:T(8,128)(2,1)}, u32[]{:S(2)}) copy-start(bf16[1536,768]{1,0:T(8,128)(2,1)} %w_query.1) | copy-start | bytes 7077892
  12.2 14.7 %collective-permute-start.10 = (bf16[192,768]{1,0:T(8,128)(2,1)S(1)}, bf16[192,768]{1,0:T(8,128)(2,1)S(1)}, u32[]{:S(2)}, u32[]{:S(2)}) collective-permute-start(bf16[192,768]{1,0:T(8,128)(2,1)S(1)} %collective-permute-done.5.refs_1_), channel_id=1, source_target_pairs={{0,2},{2,0},{4,6},{6,4},{8,10},{10,8},{12,14},{14,12},{16,18},{18,... | collective-permute-start | bytes 884744 | tf_op jit(solution)/shard_map/ppermute | solution.py:79
  12.2 9.5 %collective-permute-start.7 = (bf16[192,768]{1,0:T(8,128)(2,1)S(1)}, bf16[192,768]{1,0:T(8,128)(2,1)S(1)}, u32[]{:S(2)}, u32[]{:S(2)}) collective-permute-start(bf16[192,768]{1,0:T(8,128)(2,1)S(1)} %collective-permute-done.5.refs_1_), channel_id=1, source_target_pairs={{0,8},{2,6},{8,16},{10,2},{16,24},{18,10},{24,28},{26,18},{28,20},... | collective-permute-start | bytes 884744 | tf_op jit(solution)/shard_map/ppermute | solution.py:70
  16.4 7.0 %collective-permute-start.6 = (bf16[128,512]{1,0:T(8,128)(2,1)S(1)}, bf16[128,512]{1,0:T(8,128)(2,1)S(1)}, u32[]{:S(2)}, u32[]{:S(2)}) collective-permute-start(bf16[128,512]{1,0:T(8,128)(2,1)S(1)} %get-tuple-element.74), channel_id=1, source_target_pairs={{0,2},{2,4},{4,6},{6,8},{8,10},{10,12},{12,14},{14,16},{16,18},{18... | collective-permute-start | bytes 393224 | tf_op jit(solution)/shard_map/ppermute | solution.py:745
  21.6 5.2 %collective-permute-start.11 = (bf16[192,768]{1,0:T(8,128)(2,1)S(1)}, bf16[192,768]{1,0:T(8,128)(2,1)S(1)}, u32[]{:S(2)}, u32[]{:S(2)}) collective-permute-start(bf16[192,768]{1,0:T(8,128)(2,1)S(1)} %collective-permute-done.7.refs_2_), channel_id=1, source_target_pairs={{0,2},{2,0},{4,6},{6,4},{8,10},{10,8},{12,14},{14,12},{16,18},{18,... | collective-permute-start | bytes 884744 | tf_op jit(solution)/shard_map/ppermute | solution.py:79
  21.6 6.7 %collective-permute-start.9 = (bf16[192,768]{1,0:T(8,128)(2,1)S(1)}, bf16[192,768]{1,0:T(8,128)(2,1)S(1)}, u32[]{:S(2)}, u32[]{:S(2)}) collective-permute-start(bf16[192,768]{1,0:T(8,128)(2,1)S(1)} %collective-permute-done.7.refs_2_), channel_id=1, source_target_pairs={{0,8},{2,6},{8,16},{10,2},{16,24},{18,10},{24,28},{26,18},{28,20},... | collective-permute-start | bytes 884744 | tf_op jit(solution)/shard_map/ppermute | solution.py:70
  23.3 12.9 %collective-permute-start.8 = (bf16[576,512]{1,0:T(8,128)(2,1)S(1)}, bf16[576,512]{1,0:T(8,128)(2,1)S(1)}, u32[]{:S(2)}, u32[]{:S(2)}) collective-permute-start(bf16[576,512]{1,0:T(8,128)(2,1)S(1)} %collective-permute-done.3.refs_1_), channel_id=1, source_target_pairs={{0,8},{2,6},{8,16},{10,2},{16,24},{18,10},{24,28},{26,18},{28,20},... | collective-permute-start | bytes 1769480 | tf_op jit(solution)/shard_map/ppermute | solution.py:70
  28.4 1.8 %collective-permute-start.13 = (bf16[192,768]{1,0:T(8,128)(2,1)S(1)}, bf16[192,768]{1,0:T(8,128)(2,1)S(1)}, u32[]{:S(2)}, u32[]{:S(2)}) collective-permute-start(bf16[192,768]{1,0:T(8,128)(2,1)S(1)} %collective-permute-done.9.refs_3_), channel_id=1, source_target_pairs={{0,2},{2,0},{4,6},{6,4},{8,10},{10,8},{12,14},{14,12},{16,18},{18,... | collective-permute-start | bytes 884744 | tf_op jit(solution)/shard_map/ppermute | solution.py:79
  28.4 7.9 %collective-permute-start.12 = (bf16[96,768]{1,0:T(8,128)(2,1)S(1)}, bf16[96,768]{1,0:T(8,128)(2,1)S(1)}, u32[]{:S(2)}, u32[]{:S(2)}) collective-permute-start(bf16[96,768]{1,0:T(8,128)(2,1)S(1)} %slice.6), channel_id=1, source_target_pairs={{0,8},{2,6},{8,16},{10,2},{16,24},{18,10},{24,28},{26,18},{28,20},... | collective-permute-start | bytes 442376 | tf_op jit(solution)/shard_map/ppermute | solution.py:70
  36.3 10.0 %collective-permute-start.16 = (bf16[576,512]{1,0:T(8,128)(2,1)S(1)}, bf16[576,512]{1,0:T(8,128)(2,1)}, u32[]{:S(2)}, u32[]{:S(2)}) collective-permute-start(bf16[576,512]{1,0:T(8,128)(2,1)S(1)} %collective-permute-done.8.refs_2_), channel_id=1, source_target_pairs={{0,8},{2,6},{8,16},{10,2},{16,24},{18,10},{24,28},{26,18},{28,20},... | collective-permute-start | bytes 1769480 | tf_op jit(solution)/shard_map/ppermute | solution.py:70
  38.0 1.4 %collective-permute-start.14 = (bf16[96,768]{1,0:T(8,128)(2,1)S(1)}, bf16[96,768]{1,0:T(8,128)(2,1)S(1)}, u32[]{:S(2)}, u32[]{:S(2)}) collective-permute-start(bf16[96,768]{1,0:T(8,128)(2,1)S(1)} %collective-permute-done.12.refs_7_), channel_id=1, source_target_pairs={{0,2},{2,0},{4,6},{6,4},{8,10},{10,8},{12,14},{14,12},{16,18},{18,... | collective-permute-start | bytes 442376 | tf_op jit(solution)/shard_map/ppermute | solution.py:79
  40.5 11.2 %collective-permute-start.15 = (bf16[128,1536]{1,0:T(8,128)(2,1)S(1)}, bf16[128,1536]{1,0:T(8,128)(2,1)S(1)}, u32[]{:S(2)}, u32[]{:S(2)}) collective-permute-start(bf16[128,1536]{1,0:T(8,128)(2,1)S(1)} %outward_send.1), channel_id=1, source_target_pairs={{0,1},{1,0},{2,3},{3,2},{4,5},{5,4},{6,7},{7,6},{8,9},{9,8},{10,11... | collective-permute-start | bytes 1179656 | tf_op jit(solution)/shard_map/ppermute | solution.py:766
  47.2 6.8 %collective-permute-start.17 = (bf16[288,512]{1,0:T(8,128)(2,1)S(1)}, bf16[288,512]{1,0:T(8,128)(2,1)S(1)}, u32[]{:S(2)}, u32[]{:S(2)}) collective-permute-start(bf16[288,512]{1,0:T(8,128)(2,1)S(1)} %slice.7), channel_id=1, source_target_pairs={{0,8},{2,6},{8,16},{10,2},{16,24},{18,10},{24,28},{26,18},{28,20},... | collective-permute-start | bytes 884744 | tf_op jit(solution)/shard_map/ppermute | solution.py:70
  54.0 0.7 copy-start.3
  54.7 9.9 %collective-permute-start.18 = (bf16[576,512]{1,0:T(8,128)(2,1)S(1)}, bf16[576,512]{1,0:T(8,128)(2,1)}, u32[]{:S(2)}, u32[]{:S(2)}) collective-permute-start(bf16[576,512]{1,0:T(8,128)(2,1)S(1)} %collective-permute-done.3.refs_1_), channel_id=1, source_target_pairs={{0,2},{2,0},{4,6},{6,4},{8,10},{10,8},{12,14},{14,12},{16,18},{18,... | collective-permute-start | bytes 1769480 | tf_op jit(solution)/shard_map/ppermute | solution.py:79
  54.7 9.9 %collective-permute-start.19 = (bf16[576,512]{1,0:T(8,128)(2,1)S(1)}, bf16[576,512]{1,0:T(8,128)(2,1)}, u32[]{:S(2)}, u32[]{:S(2)}) collective-permute-start(bf16[576,512]{1,0:T(8,128)(2,1)S(1)} %collective-permute-done.8.refs_2_), channel_id=1, source_target_pairs={{0,2},{2,0},{4,6},{6,4},{8,10},{10,8},{12,14},{14,12},{16,18},{18,... | collective-permute-start | bytes 1769480 | tf_op jit(solution)/shard_map/ppermute | solution.py:79
  55.2 12.8 %collective-permute-start.21 = (bf16[576,512]{1,0:T(8,128)(2,1)}, bf16[576,512]{1,0:T(8,128)(2,1)}, u32[]{:S(2)}, u32[]{:S(2)}) collective-permute-start(bf16[576,512]{1,0:T(8,128)(2,1)} %collective-permute-done.16.refs_0_), channel_id=1, source_target_pairs={{0,2},{2,0},{4,6},{6,4},{8,10},{10,8},{12,14},{14,12},{16,18},{18,... | collective-permute-start | bytes 1769480 | tf_op jit(solution)/shard_map/ppermute | solution.py:79
  55.3 21.9 %all-to-all-start = ((bf16[16,144,128]{2,1,0:T(8,128)(2,1)}), bf16[16,144,128]{2,1,0:T(8,128)(2,1)S(1)}, u32[]{:S(2)}, u32[]{:S(2)}) async-start(bf16[16,144,128]{2,1,0:T(8,128)(2,1)} %bundle.1), calls=%async_computation | async-start | bytes 1179648 | tf_op jit(solution)/shard_map/all_to_all | solution.py:772
  61.6 6.4 %collective-permute-start.22 = (bf16[288,512]{1,0:T(8,128)(2,1)}, bf16[288,512]{1,0:T(8,128)(2,1)S(1)}, u32[]{:S(2)}, u32[]{:S(2)}) collective-permute-start(bf16[288,512]{1,0:T(8,128)(2,1)} %copy-done.3), channel_id=1, source_target_pairs={{0,2},{2,0},{4,6},{6,4},{8,10},{10,8},{12,14},{14,12},{16,18},{18,... | collective-permute-start | bytes 884744 | tf_op jit(solution)/shard_map/ppermute | solution.py:79
  63.1 4.9 %collective-permute-start.20 = (bf16[32,1536]{1,0:T(8,128)(2,1)S(1)}, bf16[32,1536]{1,0:T(8,128)(2,1)S(1)}, u32[]{:S(2)}, u32[]{:S(2)}) collective-permute-start(bf16[32,1536]{1,0:T(8,128)(2,1)S(1)} %get-tuple-element.114), channel_id=1, source_target_pairs={{0,1},{1,0},{2,3},{3,2},{4,5},{5,4},{6,7},{7,6},{8,9},{9,8},{10,11... | collective-permute-start | bytes 294920 | tf_op jit(solution)/shard_map/ppermute | solution.py:777
  64.7 3.3 %copy-start.4 = (bf16[288,512]{1,0:T(8,128)(2,1)S(1)}, bf16[288,512]{1,0:T(8,128)(2,1)}, u32[]{:S(2)}) copy-start(bf16[288,512]{1,0:T(8,128)(2,1)} %copy-done.3) | copy-start | bytes 884740
  68.0 9.1 %copy-start = (bf16[512,4,128]{2,1,0:T(4,128)(2,1)S(1)}, bf16[512,4,128]{2,1,0:T(4,128)(2,1)}, u32[]{:S(2)}) copy-start(bf16[512,4,128]{2,1,0:T(4,128)(2,1)} %param.25) | copy-start | bytes 1572868
  70.5 4.7 %collective-permute-start.23 = (bf16[32,1536]{1,0:T(8,128)(2,1)S(1)}, bf16[32,1536]{1,0:T(8,128)(2,1)S(1)}, u32[]{:S(2)}, u32[]{:S(2)}) collective-permute-start(bf16[32,1536]{1,0:T(8,128)(2,1)S(1)} %get-tuple-element.123), channel_id=1, source_target_pairs={{0,1},{1,0},{2,3},{3,2},{4,5},{5,4},{6,7},{7,6},{8,9},{9,8},{10,11... | collective-permute-start | bytes 294920 | tf_op jit(solution)/shard_map/ppermute | solution.py:784

commit v18 on v17

--- a/solution.py
+++ b/solution.py
@@ -587,7 +587,7 @@
         scratch_shapes=[pltpu.VMEM((2 * count, model), bf16)],
         input_output_aliases={2: 2, 3: 3},
         compiler_params=PARAMS,
-        cost_estimate=pl.CostEstimate(flops=int(5.7 * 1.15e9), bytes_accessed=1, transcendentals=0),
+        cost_estimate=pl.CostEstimate(flops=int(4.2 * 1.15e9), bytes_accessed=1, transcendentals=0),
         name="expert",
     )(own, other, *staged, *[part for part, _ in late])[:2]
 

time: 79.1 us -> 79.1 us (level)
  no operation moved by 1% of the time
where the time goes in v18:
time: 79.1 us; the launch traced here: 78.7 us
  starting transfers between devices  31.4 us (40%)
  waiting for transfers between devices  23.3 us (29%)
  Pallas kernels  19.7 us (25%)
  local copies, waits for them, and re-layouts  3.56 us (5%)
  between operations  0.82 us (1%)
    ppermute x8, starting transfers between devices, step(): self.mine.append(self.across(held))  14 us
    ppermute x8, waiting for transfers between devices, step(): self.mine.append(self.across(held))  13.8 us
    all_to_all x1, starting transfers between devices, two_lane_shards(): lax.all_to_all(outgoing, 'grp', split_axis=0, concat_axis=0, tiled=True)  6.35 us
    ppermute x1, waiting for transfers between devices, two_lane_shards(): returned = swap(back)  3.13 us
    ppermute x1, waiting for transfers between devices, two_lane_shards(): arrived = swap(sent)  2.74 us
    unnamed x11, local copies, waits for them, and re-layouts  2.57 us
    ppermute x1, starting transfers between devices, two_lane_shards(): other_tokens = swap(tokens)  2.56 us
    pallas_call x1, Pallas kernels, expert(): pl.pallas_call(functools.partial(expert_kernel, groups, up_rows, down_row...  2.44 us
  transfers between devices with their start and end apart: 25, of which 12 were waited for; matrix products, arithmetic and copies ran while one was open for 4% of the time, Pallas kernels for 23%

profile of v18, /device:TPU:0, one launch (start us, length us, event | category | flops | bytes accessed | tf_op | source)
XLA Modules:
  0.0 78.7 jit_solution(7091776953677804239)
XLA Ops:
  1.7 2.6 %collective-permute-start.4 = (bf16[128,1536]{1,0:T(8,128)(2,1)}, bf16[128,1536]{1,0:T(8,128)(2,1)S(1)}, u32[]{:S(2)}, u32[]{:S(2)}) collective-permute-start(bf16[128,1536]{1,0:T(8,128)(2,1)} %tokens.1), channel_id=1, source_target_pairs={{0,1},{1,0},{2,3},{3,2},{4,5},{5,4},{6,7},{7,6},{8,9},{9,8},{10,11... | collective-permute-start | bytes 1179656 | tf_op jit(solution)/shard_map/ppermute | solution.py:727
  5.4 1.7 %collective-permute-start.5 = (bf16[192,768]{1,0:T(8,128)(2,1)S(1)}, bf16[192,768]{1,0:T(8,128)(2,1)S(1)}, u32[]{:S(2)}, u32[]{:S(2)}) collective-permute-start(bf16[192,768]{1,0:T(8,128)(2,1)S(1)} %get-tuple-element.66.refs_0_), channel_id=1, source_target_pairs={{0,8},{2,6},{8,16},{10,2},{16,24},{18,10},{24,28},{26,18},{28,20},... | collective-permute-start | bytes 884744 | tf_op jit(solution)/shard_map/ppermute | solution.py:70
  7.1 1.6 %collective-permute-start.3 = (bf16[576,512]{1,0:T(8,128)(2,1)S(1)}, bf16[576,512]{1,0:T(8,128)(2,1)S(1)}, u32[]{:S(2)}, u32[]{:S(2)}) collective-permute-start(bf16[576,512]{1,0:T(8,128)(2,1)S(1)} %get-tuple-element.65.refs_0_), channel_id=1, source_target_pairs={{0,8},{2,6},{8,16},{10,2},{16,24},{18,10},{24,28},{26,18},{28,20},... | collective-permute-start | bytes 1769480 | tf_op jit(solution)/shard_map/ppermute | solution.py:70
  8.7 1.5 %prepare.1 = (f32[256,128]{1,0:T(8,128)S(1)}, f32[256,128]{1,0:T(8,128)S(1)}, f32[256,128]{1,0:T(8,128)S(1)}, bf16[64,128]{1,0:T(8,128)(2,1)S(1)}, bf16[512,256]...) custom-call(s32[1,256]{1,0:T(1,128)} %bitcast.26, s32[1,256]{1,0:T(1,128)} %bitcast.27, ...), custom_call_target="tpu_custom_call" | custom-call | flops 1 | bytes 1 | tf_op jit(solution)/shard_map/prepare/pallas_call | solution.py:266
  10.2 1.8 %copy.19 = bf16[192,8,4,128]{3,1,2,0:T(8,128)(2,1)S(1)} copy(bf16[192,8,4,128]{3,2,1,0:T(4,128)(2,1)} %bitcast.15) | data formatting | bytes 3145728
  12.2 1.7 %collective-permute-start.7 = (bf16[192,768]{1,0:T(8,128)(2,1)S(1)}, bf16[192,768]{1,0:T(8,128)(2,1)S(1)}, u32[]{:S(2)}, u32[]{:S(2)}) collective-permute-start(bf16[192,768]{1,0:T(8,128)(2,1)S(1)} %collective-permute-done.5.refs_1_), channel_id=1, source_target_pairs={{0,8},{2,6},{8,16},{10,2},{16,24},{18,10},{24,28},{26,18},{28,20},... | collective-permute-start | bytes 884744 | tf_op jit(solution)/shard_map/ppermute | solution.py:70
  14.1 2.2 %project.1 = (bf16[256,768]{1,0:T(8,128)(2,1)S(1)}, bf16[256,512]{1,0:T(8,128)(2,1)S(1)}, bf16[128,512]{1,0:T(8,128)(2,1)S(1)}) custom-call(bf16[128,1536]{1,0:T(8,128)(2,1)S(1)} %copy-done.1, bf16[128,1536]{1,0:T(8,128)(2,1)S(1)} %collective-permute-done.4.other, f32[1,1536]{1,0:T(1,128)S(1)} %get-tuple-element.68.gain, ...), custom_call_target="tpu_custom_call" | custom-call | flops 9200000000 | bytes 64000000 | tf_op jit(solution)/shard_map/project/pallas_call | solution.py:316
  16.4 1.8 %collective-permute-start.6 = (bf16[128,512]{1,0:T(8,128)(2,1)S(1)}, bf16[128,512]{1,0:T(8,128)(2,1)S(1)}, u32[]{:S(2)}, u32[]{:S(2)}) collective-permute-start(bf16[128,512]{1,0:T(8,128)(2,1)S(1)} %get-tuple-element.74), channel_id=1, source_target_pairs={{0,2},{2,4},{4,6},{6,8},{8,10},{10,12},{12,14},{14,16},{16,18},{18... | collective-permute-start | bytes 393224 | tf_op jit(solution)/shard_map/ppermute | solution.py:745
  18.2 1.3 %attend_late.1.late = bf16[128,768]{1,0:T(8,128)(2,1)S(1)} custom-call(bf16[256,768]{1,0:T(8,128)(2,1)S(1)} %get-tuple-element.76.q, bf16[256,512]{1,0:T(8,128)(2,1)S(1)} %get-tuple-element.91.kv, f32[256,128]{1,0:T(8,128)S(1)} %get-tuple-element.78.past), custom_call_target="tpu_custom_call" | custom-call | flops 2300000000 | bytes 16000000 | tf_op jit(solution)/shard_map/attend_late/pallas_call | solution.py:372
  19.5 2.1 %collective-permute-done.7.refs_2_ = bf16[192,768]{1,0:T(8,128)(2,1)S(1)} collective-permute-done((bf16[192,768]{1,0:T(8,128)(2,1)S(1)}, bf16[192,768]{1,0:T(8,128)(2,1)S(1)}, u32[]{:S(2)}, u32[]{:S(2)}) %collective-permute-start.7) | collective-permute-done | bytes 294944 | tf_op jit(solution)/shard_map/ppermute | solution.py:70
  21.6 1.7 %collective-permute-start.9 = (bf16[192,768]{1,0:T(8,128)(2,1)S(1)}, bf16[192,768]{1,0:T(8,128)(2,1)S(1)}, u32[]{:S(2)}, u32[]{:S(2)}) collective-permute-start(bf16[192,768]{1,0:T(8,128)(2,1)S(1)} %collective-permute-done.7.refs_2_), channel_id=1, source_target_pairs={{0,8},{2,6},{8,16},{10,2},{16,24},{18,10},{24,28},{26,18},{28,20},... | collective-permute-start | bytes 884744 | tf_op jit(solution)/shard_map/ppermute | solution.py:70
  23.3 2.1 %collective-permute-start.8 = (bf16[576,512]{1,0:T(8,128)(2,1)S(1)}, bf16[576,512]{1,0:T(8,128)(2,1)S(1)}, u32[]{:S(2)}, u32[]{:S(2)}) collective-permute-start(bf16[576,512]{1,0:T(8,128)(2,1)S(1)} %collective-permute-done.3.refs_1_), channel_id=1, source_target_pairs={{0,8},{2,6},{8,16},{10,2},{16,24},{18,10},{24,28},{26,18},{28,20},... | collective-permute-start | bytes 1769480 | tf_op jit(solution)/shard_map/ppermute | solution.py:70
  25.4 1.5 %attend_early.1.early = bf16[128,768]{1,0:T(8,128)(2,1)S(1)} custom-call(bf16[256,768]{1,0:T(8,128)(2,1)S(1)} %get-tuple-element.76.q, bf16[256,512]{1,0:T(8,128)(2,1)S(1)} %get-tuple-element.91.kv, bf16[128,512]{1,0:T(8,128)(2,1)S(1)} %collective-permute-done.6.seam, f32[256,128]{1,0:T(8,128)S(1)} %get-tuple-element.78.past), custom_call_target="tpu_custom_call" | custom-call | flops 2300000000 | bytes 16000000 | tf_op jit(solution)/shard_map/attend_early/pallas_call | solution.py:384
  26.9 1.5 %collective-permute-done.9.refs_3_ = bf16[192,768]{1,0:T(8,128)(2,1)S(1)} collective-permute-done((bf16[192,768]{1,0:T(8,128)(2,1)S(1)}, bf16[192,768]{1,0:T(8,128)(2,1)S(1)}, u32[]{:S(2)}, u32[]{:S(2)}) %collective-permute-start.9) | collective-permute-done | bytes 294944 | tf_op jit(solution)/shard_map/ppermute | solution.py:70
  28.4 1.7 %collective-permute-start.12 = (bf16[96,768]{1,0:T(8,128)(2,1)S(1)}, bf16[96,768]{1,0:T(8,128)(2,1)S(1)}, u32[]{:S(2)}, u32[]{:S(2)}) collective-permute-start(bf16[96,768]{1,0:T(8,128)(2,1)S(1)} %slice.6), channel_id=1, source_target_pairs={{0,8},{2,6},{8,16},{10,2},{16,24},{18,10},{24,28},{26,18},{28,20},... | collective-permute-start | bytes 442376 | tf_op jit(solution)/shard_map/ppermute | solution.py:70
  30.1 1.4 %bundle.1 = bf16[16,144,128]{2,1,0:T(8,128)(2,1)} custom-call(bf16[512,256]{1,0:T(8,128)(2,1)S(1)} %get-tuple-element.90.send, bf16[256,512]{1,0:T(8,128)(2,1)S(1)} %get-tuple-element.91.kv, bf16[256,128]{1,0:T(8,128)(2,1)S(1)} %get-tuple-element.92.tags), custom_call_target="tpu_custom_call" | custom-call | flops 1 | bytes 1 | tf_op jit(solution)/shard_map/bundle/pallas_call | solution.py:644
  31.5 4.7 %collective-permute-done.12.refs_7_ = bf16[96,768]{1,0:T(8,128)(2,1)S(1)} collective-permute-done((bf16[96,768]{1,0:T(8,128)(2,1)S(1)}, bf16[96,768]{1,0:T(8,128)(2,1)S(1)}, u32[]{:S(2)}, u32[]{:S(2)}) %collective-permute-start.12) | collective-permute-done | bytes 147488 | tf_op jit(solution)/shard_map/ppermute | solution.py:70
  36.3 1.7 %collective-permute-start.16 = (bf16[576,512]{1,0:T(8,128)(2,1)S(1)}, bf16[576,512]{1,0:T(8,128)(2,1)}, u32[]{:S(2)}, u32[]{:S(2)}) collective-permute-start(bf16[576,512]{1,0:T(8,128)(2,1)S(1)} %collective-permute-done.8.refs_2_), channel_id=1, source_target_pairs={{0,8},{2,6},{8,16},{10,2},{16,24},{18,10},{24,28},{26,18},{28,20},... | collective-permute-start | bytes 1769480 | tf_op jit(solution)/shard_map/ppermute | solution.py:70
  38.0 1.4 %collective-permute-done.14.refs_8_ = bf16[96,768]{1,0:T(8,128)(2,1)S(1)} collective-permute-done((bf16[96,768]{1,0:T(8,128)(2,1)S(1)}, bf16[96,768]{1,0:T(8,128)(2,1)S(1)}, u32[]{:S(2)}, u32[]{:S(2)}) %collective-permute-start.14) | collective-permute-done | bytes 147488 | tf_op jit(solution)/shard_map/ppermute | solution.py:79
  40.5 1.6 %collective-permute-start.15 = (bf16[128,1536]{1,0:T(8,128)(2,1)S(1)}, bf16[128,1536]{1,0:T(8,128)(2,1)S(1)}, u32[]{:S(2)}, u32[]{:S(2)}) collective-permute-start(bf16[128,1536]{1,0:T(8,128)(2,1)S(1)} %outward_send.1), channel_id=1, source_target_pairs={{0,1},{1,0},{2,3},{3,2},{4,5},{5,4},{6,7},{7,6},{8,9},{9,8},{10,11... | collective-permute-start | bytes 1179656 | tf_op jit(solution)/shard_map/ppermute | solution.py:766
  42.1 1.1 %outward_keep.1.mine = f32[128,1536]{1,0:T(8,128)S(1)} custom-call(bf16[128,768]{1,0:T(8,128)(2,1)S(1)} %attend_early.1.early, bf16[128,768]{1,0:T(8,128)(2,1)S(1)} %attend_late.1.late, bf16[128,1536]{1,0:T(8,128)(2,1)S(1)} %copy-done.1, bf16[192,768]{1,0:T(8,128)(2,1)S(1)} %get-tuple-element.66.refs_0_, ...), custom_call_target="tpu_custom_call" | custom-call | flops 1 | bytes 2359296 | tf_op jit(solution)/shard_map/outward_keep/pallas_call | solution.py:439
  43.2 3.0 %collective-permute-done.16.refs_0_ = bf16[576,512]{1,0:T(8,128)(2,1)} collective-permute-done((bf16[576,512]{1,0:T(8,128)(2,1)S(1)}, bf16[576,512]{1,0:T(8,128)(2,1)}, u32[]{:S(2)}, u32[]{:S(2)}) %collective-permute-start.16) | collective-permute-done | bytes 589856 | tf_op jit(solution)/shard_map/ppermute | solution.py:70
  47.2 1.7 %collective-permute-start.17 = (bf16[288,512]{1,0:T(8,128)(2,1)S(1)}, bf16[288,512]{1,0:T(8,128)(2,1)S(1)}, u32[]{:S(2)}, u32[]{:S(2)}) collective-permute-start(bf16[288,512]{1,0:T(8,128)(2,1)S(1)} %slice.7), channel_id=1, source_target_pairs={{0,8},{2,6},{8,16},{10,2},{16,24},{18,10},{24,28},{26,18},{28,20},... | collective-permute-start | bytes 884744 | tf_op jit(solution)/shard_map/ppermute | solution.py:70
  49.0 2.7 %collective-permute-done.15.arrived = bf16[128,1536]{1,0:T(8,128)(2,1)S(1)} collective-permute-done((bf16[128,1536]{1,0:T(8,128)(2,1)S(1)}, bf16[128,1536]{1,0:T(8,128)(2,1)S(1)}, u32[]{:S(2)}, u32[]{:S(2)}) %collective-permute-start.15) | collective-permute-done | bytes 393248 | tf_op jit(solution)/shard_map/ppermute | solution.py:766
  51.7 2.3 %collective-permute-done.17.refs_2_ = bf16[288,512]{1,0:T(8,128)(2,1)S(1)} collective-permute-done((bf16[288,512]{1,0:T(8,128)(2,1)S(1)}, bf16[288,512]{1,0:T(8,128)(2,1)S(1)}, u32[]{:S(2)}, u32[]{:S(2)}) %collective-permute-start.17) | collective-permute-done | bytes 294944 | tf_op jit(solution)/shard_map/ppermute | solution.py:70
  55.3 6.4 %all-to-all-start = ((bf16[16,144,128]{2,1,0:T(8,128)(2,1)}), bf16[16,144,128]{2,1,0:T(8,128)(2,1)S(1)}, u32[]{:S(2)}, u32[]{:S(2)}) async-start(bf16[16,144,128]{2,1,0:T(8,128)(2,1)} %bundle.1), calls=%async_computation | async-start | bytes 1179648 | tf_op jit(solution)/shard_map/all_to_all | solution.py:772
  63.1 1.6 %collective-permute-start.20 = (bf16[32,1536]{1,0:T(8,128)(2,1)S(1)}, bf16[32,1536]{1,0:T(8,128)(2,1)S(1)}, u32[]{:S(2)}, u32[]{:S(2)}) collective-permute-start(bf16[32,1536]{1,0:T(8,128)(2,1)S(1)} %get-tuple-element.114), channel_id=1, source_target_pairs={{0,1},{1,0},{2,3},{3,2},{4,5},{5,4},{6,7},{7,6},{8,9},{9,8},{10,11... | collective-permute-start | bytes 294920 | tf_op jit(solution)/shard_map/ppermute | solution.py:777
  64.7 2.2 %gate.1 = (f32[128,40]{1,0:T(8,128)S(1)}, bf16[32,1536]{1,0:T(8,128)(2,1)S(1)}, bf16[128,64]{1,0:T(8,128)(2,1)S(1)}, bf16[1536,1024]{1,0:T(8,128)(2,1)S(1)}, bf16[512,1536]{1,0:T(8,128)(2,1)S(1)}) custom-call(bf16[128,1536]{1,0:T(8,128)(2,1)S(1)} %get-tuple-element.109.moe_in, bf16[40,1536]{1,0:T(8,128)(2,1)} %bitcast.21, s32[8,128]{1,0:T(8,128)} %bitcast.25, ...), custom_call_target="tpu_custom_call" | custom-call | flops 1 | bytes 1 | tf_op jit(solution)/shard_map/gate/pallas_call | solution.py:538
  68.0 2.4 %expert.1 = (bf16[32,1536]{1,0:T(8,128)(2,1)S(1)}, bf16[32,1536]{1,0:T(8,128)(2,1)S(1)}, bf16[1536,1024]{1,0:T(8,128)(2,1)S(1)}, bf16[512,1536]{1,0:T(8,128)(2,1)S(1)}) custom-call(bf16[32,1536]{1,0:T(8,128)(2,1)S(1)} %get-tuple-element.116.own, bf16[32,1536]{1,0:T(8,128)(2,1)S(1)} %collective-permute-done.20.other, ...), custom_call_target="tpu_custom_call", output_to_operand_aliasing={{2}: (2, {}), {3}: (3, {})} | custom-call | flops 4830000128 | bytes 1 | tf_op jit(solution)/shard_map/expert/pallas_call | solution.py:581
  70.5 1.6 %collective-permute-start.23 = (bf16[32,1536]{1,0:T(8,128)(2,1)S(1)}, bf16[32,1536]{1,0:T(8,128)(2,1)S(1)}, u32[]{:S(2)}, u32[]{:S(2)}) collective-permute-start(bf16[32,1536]{1,0:T(8,128)(2,1)S(1)} %get-tuple-element.123), channel_id=1, source_target_pairs={{0,1},{1,0},{2,3},{3,2},{4,5},{5,4},{6,7},{7,6},{8,9},{9,8},{10,11... | collective-permute-start | bytes 294920 | tf_op jit(solution)/shard_map/ppermute | solution.py:784
  72.0 3.1 %collective-permute-done.23.returned = bf16[32,1536]{1,0:T(8,128)(2,1)S(1)} collective-permute-done((bf16[32,1536]{1,0:T(8,128)(2,1)S(1)}, bf16[32,1536]{1,0:T(8,128)(2,1)S(1)}, u32[]{:S(2)}, u32[]{:S(2)}) %collective-permute-start.23) | collective-permute-done | bytes 98336 | tf_op jit(solution)/shard_map/ppermute | solution.py:784
  77.2 1.5 %write.1 = bf16[2048,128]{1,0:T(8,128)(2,1)} custom-call(bf16[16,144,128]{2,1,0:T(8,128)(2,1)S(1)} %all-to-all-done.arrived, bf16[2048,128]{1,0:T(8,128)(2,1)S(1)} %bitcast.14), custom_call_target="tpu_custom_call" | custom-call | flops 1 | bytes 2097152 | tf_op jit(solution)/shard_map/write/pallas_call | solution.py:685
  (44 shorter events, 10.6 us)
Async XLA Ops:
  0.6 3.6 %collective-permute-start.2 = (bf16[96,1536]{1,0:T(8,128)(2,1)}, bf16[96,1536]{1,0:T(8,128)(2,1)S(1)}, u32[]{:S(2)}, u32[]{:S(2)}) collective-permute-start(bf16[96,1536]{1,0:T(8,128)(2,1)} %bitcast.17), channel_id=1, source_target_pairs={{0,2},{2,0},{4,6},{6,4},{8,10},{10,8},{12,14},{14,12},{16,18},{18,... | collective-permute-start | bytes 884744 | tf_op jit(solution)/shard_map/ppermute | solution.py:730
  1.1 3.1 %collective-permute-start = (bf16[96,1024]{1,0:T(8,128)(2,1)}, bf16[96,1024]{1,0:T(8,128)(2,1)S(1)}, u32[]{:S(2)}, u32[]{:S(2)}) collective-permute-start(bf16[96,1024]{1,0:T(8,128)(2,1)} %bitcast.19), channel_id=1, source_target_pairs={{0,2},{2,0},{4,6},{6,4},{8,10},{10,8},{12,14},{14,12},{16,18},{18,... | collective-permute-start | bytes 589832 | tf_op jit(solution)/shard_map/ppermute | solution.py:730
  1.2 3.0 %collective-permute-start.1 = (bf16[32,1536]{1,0:T(8,128)(2,1)}, bf16[32,1536]{1,0:T(8,128)(2,1)S(1)}, u32[]{:S(2)}, u32[]{:S(2)}) collective-permute-start(bf16[32,1536]{1,0:T(8,128)(2,1)} %bitcast.22), channel_id=1, source_target_pairs={{0,2},{2,0},{4,6},{6,4},{8,10},{10,8},{12,14},{14,12},{16,18},{18,... | collective-permute-start | bytes 294920 | tf_op jit(solution)/shard_map/ppermute | solution.py:730
  1.7 12.5 %collective-permute-start.4 = (bf16[128,1536]{1,0:T(8,128)(2,1)}, bf16[128,1536]{1,0:T(8,128)(2,1)S(1)}, u32[]{:S(2)}, u32[]{:S(2)}) collective-permute-start(bf16[128,1536]{1,0:T(8,128)(2,1)} %tokens.1), channel_id=1, source_target_pairs={{0,1},{1,0},{2,3},{3,2},{4,5},{5,4},{6,7},{7,6},{8,9},{9,8},{10,11... | collective-permute-start | bytes 1179656 | tf_op jit(solution)/shard_map/ppermute | solution.py:727
  5.4 6.8 %collective-permute-start.5 = (bf16[192,768]{1,0:T(8,128)(2,1)S(1)}, bf16[192,768]{1,0:T(8,128)(2,1)S(1)}, u32[]{:S(2)}, u32[]{:S(2)}) collective-permute-start(bf16[192,768]{1,0:T(8,128)(2,1)S(1)} %get-tuple-element.66.refs_0_), channel_id=1, source_target_pairs={{0,8},{2,6},{8,16},{10,2},{16,24},{18,10},{24,28},{26,18},{28,20},... | collective-permute-start | bytes 884744 | tf_op jit(solution)/shard_map/ppermute | solution.py:70
  7.1 16.2 %collective-permute-start.3 = (bf16[576,512]{1,0:T(8,128)(2,1)S(1)}, bf16[576,512]{1,0:T(8,128)(2,1)S(1)}, u32[]{:S(2)}, u32[]{:S(2)}) collective-permute-start(bf16[576,512]{1,0:T(8,128)(2,1)S(1)} %get-tuple-element.65.refs_0_), channel_id=1, source_target_pairs={{0,8},{2,6},{8,16},{10,2},{16,24},{18,10},{24,28},{26,18},{28,20},... | collective-permute-start | bytes 1769480 | tf_op jit(solution)/shard_map/ppermute | solution.py:70
  10.2 4.0 %copy-start.1 = (bf16[128,1536]{1,0:T(8,128)(2,1)S(1)}, bf16[128,1536]{1,0:T(8,128)(2,1)}, u32[]{:S(2)}) copy-start(bf16[128,1536]{1,0:T(8,128)(2,1)} %tokens.1) | copy-start | bytes 1179652
  10.2 4.0 %copy-start.2 = (bf16[1536,768]{1,0:T(8,128)(2,1)S(1)}, bf16[1536,768]{1,0:T(8,128)(2,1)}, u32[]{:S(2)}) copy-start(bf16[1536,768]{1,0:T(8,128)(2,1)} %w_query.1) | copy-start | bytes 7077892
  12.2 14.7 %collective-permute-start.10 = (bf16[192,768]{1,0:T(8,128)(2,1)S(1)}, bf16[192,768]{1,0:T(8,128)(2,1)S(1)}, u32[]{:S(2)}, u32[]{:S(2)}) collective-permute-start(bf16[192,768]{1,0:T(8,128)(2,1)S(1)} %collective-permute-done.5.refs_1_), channel_id=1, source_target_pairs={{0,2},{2,0},{4,6},{6,4},{8,10},{10,8},{12,14},{14,12},{16,18},{18,... | collective-permute-start | bytes 884744 | tf_op jit(solution)/shard_map/ppermute | solution.py:79
  12.2 9.5 %collective-permute-start.7 = (bf16[192,768]{1,0:T(8,128)(2,1)S(1)}, bf16[192,768]{1,0:T(8,128)(2,1)S(1)}, u32[]{:S(2)}, u32[]{:S(2)}) collective-permute-start(bf16[192,768]{1,0:T(8,128)(2,1)S(1)} %collective-permute-done.5.refs_1_), channel_id=1, source_target_pairs={{0,8},{2,6},{8,16},{10,2},{16,24},{18,10},{24,28},{26,18},{28,20},... | collective-permute-start | bytes 884744 | tf_op jit(solution)/shard_map/ppermute | solution.py:70
  16.4 7.0 %collective-permute-start.6 = (bf16[128,512]{1,0:T(8,128)(2,1)S(1)}, bf16[128,512]{1,0:T(8,128)(2,1)S(1)}, u32[]{:S(2)}, u32[]{:S(2)}) collective-permute-start(bf16[128,512]{1,0:T(8,128)(2,1)S(1)} %get-tuple-element.74), channel_id=1, source_target_pairs={{0,2},{2,4},{4,6},{6,8},{8,10},{10,12},{12,14},{14,16},{16,18},{18... | collective-permute-start | bytes 393224 | tf_op jit(solution)/shard_map/ppermute | solution.py:745
  21.6 5.2 %collective-permute-start.11 = (bf16[192,768]{1,0:T(8,128)(2,1)S(1)}, bf16[192,768]{1,0:T(8,128)(2,1)S(1)}, u32[]{:S(2)}, u32[]{:S(2)}) collective-permute-start(bf16[192,768]{1,0:T(8,128)(2,1)S(1)} %collective-permute-done.7.refs_2_), channel_id=1, source_target_pairs={{0,2},{2,0},{4,6},{6,4},{8,10},{10,8},{12,14},{14,12},{16,18},{18,... | collective-permute-start | bytes 884744 | tf_op jit(solution)/shard_map/ppermute | solution.py:79
  21.6 6.7 %collective-permute-start.9 = (bf16[192,768]{1,0:T(8,128)(2,1)S(1)}, bf16[192,768]{1,0:T(8,128)(2,1)S(1)}, u32[]{:S(2)}, u32[]{:S(2)}) collective-permute-start(bf16[192,768]{1,0:T(8,128)(2,1)S(1)} %collective-permute-done.7.refs_2_), channel_id=1, source_target_pairs={{0,8},{2,6},{8,16},{10,2},{16,24},{18,10},{24,28},{26,18},{28,20},... | collective-permute-start | bytes 884744 | tf_op jit(solution)/shard_map/ppermute | solution.py:70
  23.3 12.9 %collective-permute-start.8 = (bf16[576,512]{1,0:T(8,128)(2,1)S(1)}, bf16[576,512]{1,0:T(8,128)(2,1)S(1)}, u32[]{:S(2)}, u32[]{:S(2)}) collective-permute-start(bf16[576,512]{1,0:T(8,128)(2,1)S(1)} %collective-permute-done.3.refs_1_), channel_id=1, source_target_pairs={{0,8},{2,6},{8,16},{10,2},{16,24},{18,10},{24,28},{26,18},{28,20},... | collective-permute-start | bytes 1769480 | tf_op jit(solution)/shard_map/ppermute | solution.py:70
  28.4 1.8 %collective-permute-start.13 = (bf16[192,768]{1,0:T(8,128)(2,1)S(1)}, bf16[192,768]{1,0:T(8,128)(2,1)S(1)}, u32[]{:S(2)}, u32[]{:S(2)}) collective-permute-start(bf16[192,768]{1,0:T(8,128)(2,1)S(1)} %collective-permute-done.9.refs_3_), channel_id=1, source_target_pairs={{0,2},{2,0},{4,6},{6,4},{8,10},{10,8},{12,14},{14,12},{16,18},{18,... | collective-permute-start | bytes 884744 | tf_op jit(solution)/shard_map/ppermute | solution.py:79
  28.4 7.9 %collective-permute-start.12 = (bf16[96,768]{1,0:T(8,128)(2,1)S(1)}, bf16[96,768]{1,0:T(8,128)(2,1)S(1)}, u32[]{:S(2)}, u32[]{:S(2)}) collective-permute-start(bf16[96,768]{1,0:T(8,128)(2,1)S(1)} %slice.6), channel_id=1, source_target_pairs={{0,8},{2,6},{8,16},{10,2},{16,24},{18,10},{24,28},{26,18},{28,20},... | collective-permute-start | bytes 442376 | tf_op jit(solution)/shard_map/ppermute | solution.py:70
  36.3 10.0 %collective-permute-start.16 = (bf16[576,512]{1,0:T(8,128)(2,1)S(1)}, bf16[576,512]{1,0:T(8,128)(2,1)}, u32[]{:S(2)}, u32[]{:S(2)}) collective-permute-start(bf16[576,512]{1,0:T(8,128)(2,1)S(1)} %collective-permute-done.8.refs_2_), channel_id=1, source_target_pairs={{0,8},{2,6},{8,16},{10,2},{16,24},{18,10},{24,28},{26,18},{28,20},... | collective-permute-start | bytes 1769480 | tf_op jit(solution)/shard_map/ppermute | solution.py:70
  38.0 1.4 %collective-permute-start.14 = (bf16[96,768]{1,0:T(8,128)(2,1)S(1)}, bf16[96,768]{1,0:T(8,128)(2,1)S(1)}, u32[]{:S(2)}, u32[]{:S(2)}) collective-permute-start(bf16[96,768]{1,0:T(8,128)(2,1)S(1)} %collective-permute-done.12.refs_7_), channel_id=1, source_target_pairs={{0,2},{2,0},{4,6},{6,4},{8,10},{10,8},{12,14},{14,12},{16,18},{18,... | collective-permute-start | bytes 442376 | tf_op jit(solution)/shard_map/ppermute | solution.py:79
  40.5 11.2 %collective-permute-start.15 = (bf16[128,1536]{1,0:T(8,128)(2,1)S(1)}, bf16[128,1536]{1,0:T(8,128)(2,1)S(1)}, u32[]{:S(2)}, u32[]{:S(2)}) collective-permute-start(bf16[128,1536]{1,0:T(8,128)(2,1)S(1)} %outward_send.1), channel_id=1, source_target_pairs={{0,1},{1,0},{2,3},{3,2},{4,5},{5,4},{6,7},{7,6},{8,9},{9,8},{10,11... | collective-permute-start | bytes 1179656 | tf_op jit(solution)/shard_map/ppermute | solution.py:766
  47.2 6.8 %collective-permute-start.17 = (bf16[288,512]{1,0:T(8,128)(2,1)S(1)}, bf16[288,512]{1,0:T(8,128)(2,1)S(1)}, u32[]{:S(2)}, u32[]{:S(2)}) collective-permute-start(bf16[288,512]{1,0:T(8,128)(2,1)S(1)} %slice.7), channel_id=1, source_target_pairs={{0,8},{2,6},{8,16},{10,2},{16,24},{18,10},{24,28},{26,18},{28,20},... | collective-permute-start | bytes 884744 | tf_op jit(solution)/shard_map/ppermute | solution.py:70
  54.0 0.7 copy-start.3
  54.7 9.9 %collective-permute-start.18 = (bf16[576,512]{1,0:T(8,128)(2,1)S(1)}, bf16[576,512]{1,0:T(8,128)(2,1)}, u32[]{:S(2)}, u32[]{:S(2)}) collective-permute-start(bf16[576,512]{1,0:T(8,128)(2,1)S(1)} %collective-permute-done.3.refs_1_), channel_id=1, source_target_pairs={{0,2},{2,0},{4,6},{6,4},{8,10},{10,8},{12,14},{14,12},{16,18},{18,... | collective-permute-start | bytes 1769480 | tf_op jit(solution)/shard_map/ppermute | solution.py:79
  54.7 9.9 %collective-permute-start.19 = (bf16[576,512]{1,0:T(8,128)(2,1)S(1)}, bf16[576,512]{1,0:T(8,128)(2,1)}, u32[]{:S(2)}, u32[]{:S(2)}) collective-permute-start(bf16[576,512]{1,0:T(8,128)(2,1)S(1)} %collective-permute-done.8.refs_2_), channel_id=1, source_target_pairs={{0,2},{2,0},{4,6},{6,4},{8,10},{10,8},{12,14},{14,12},{16,18},{18,... | collective-permute-start | bytes 1769480 | tf_op jit(solution)/shard_map/ppermute | solution.py:79
  55.2 12.8 %collective-permute-start.21 = (bf16[576,512]{1,0:T(8,128)(2,1)}, bf16[576,512]{1,0:T(8,128)(2,1)}, u32[]{:S(2)}, u32[]{:S(2)}) collective-permute-start(bf16[576,512]{1,0:T(8,128)(2,1)} %collective-permute-done.16.refs_0_), channel_id=1, source_target_pairs={{0,2},{2,0},{4,6},{6,4},{8,10},{10,8},{12,14},{14,12},{16,18},{18,... | collective-permute-start | bytes 1769480 | tf_op jit(solution)/shard_map/ppermute | solution.py:79
  55.3 21.9 %all-to-all-start = ((bf16[16,144,128]{2,1,0:T(8,128)(2,1)}), bf16[16,144,128]{2,1,0:T(8,128)(2,1)S(1)}, u32[]{:S(2)}, u32[]{:S(2)}) async-start(bf16[16,144,128]{2,1,0:T(8,128)(2,1)} %bundle.1), calls=%async_computation | async-start | bytes 1179648 | tf_op jit(solution)/shard_map/all_to_all | solution.py:772
  61.6 6.4 %collective-permute-start.22 = (bf16[288,512]{1,0:T(8,128)(2,1)}, bf16[288,512]{1,0:T(8,128)(2,1)S(1)}, u32[]{:S(2)}, u32[]{:S(2)}) collective-permute-start(bf16[288,512]{1,0:T(8,128)(2,1)} %copy-done.3), channel_id=1, source_target_pairs={{0,2},{2,0},{4,6},{6,4},{8,10},{10,8},{12,14},{14,12},{16,18},{18,... | collective-permute-start | bytes 884744 | tf_op jit(solution)/shard_map/ppermute | solution.py:79
  63.1 4.9 %collective-permute-start.20 = (bf16[32,1536]{1,0:T(8,128)(2,1)S(1)}, bf16[32,1536]{1,0:T(8,128)(2,1)S(1)}, u32[]{:S(2)}, u32[]{:S(2)}) collective-permute-start(bf16[32,1536]{1,0:T(8,128)(2,1)S(1)} %get-tuple-element.114), channel_id=1, source_target_pairs={{0,1},{1,0},{2,3},{3,2},{4,5},{5,4},{6,7},{7,6},{8,9},{9,8},{10,11... | collective-permute-start | bytes 294920 | tf_op jit(solution)/shard_map/ppermute | solution.py:777
  64.7 3.3 %copy-start.4 = (bf16[288,512]{1,0:T(8,128)(2,1)S(1)}, bf16[288,512]{1,0:T(8,128)(2,1)}, u32[]{:S(2)}) copy-start(bf16[288,512]{1,0:T(8,128)(2,1)} %copy-done.3) | copy-start | bytes 884740
  68.0 9.1 %copy-start = (bf16[512,4,128]{2,1,0:T(4,128)(2,1)S(1)}, bf16[512,4,128]{2,1,0:T(4,128)(2,1)}, u32[]{:S(2)}) copy-start(bf16[512,4,128]{2,1,0:T(4,128)(2,1)} %param.25) | copy-start | bytes 1572868
  70.5 4.7 %collective-permute-start.23 = (bf16[32,1536]{1,0:T(8,128)(2,1)S(1)}, bf16[32,1536]{1,0:T(8,128)(2,1)S(1)}, u32[]{:S(2)}, u32[]{:S(2)}) collective-permute-start(bf16[32,1536]{1,0:T(8,128)(2,1)S(1)} %get-tuple-element.123), channel_id=1, source_target_pairs={{0,1},{1,0},{2,3},{3,2},{4,5},{5,4},{6,7},{7,6},{8,9},{9,8},{10,11... | collective-permute-start | bytes 294920 | tf_op jit(solution)/shard_map/ppermute | solution.py:784

commit v19 on v18

--- a/solution.py
+++ b/solution.py
@@ -587,7 +587,7 @@
         scratch_shapes=[pltpu.VMEM((2 * count, model), bf16)],
         input_output_aliases={2: 2, 3: 3},
         compiler_params=PARAMS,
-        cost_estimate=pl.CostEstimate(flops=int(4.2 * 1.15e9), bytes_accessed=1, transcendentals=0),
+        cost_estimate=pl.CostEstimate(flops=int(2.2 * 1.15e9), bytes_accessed=1, transcendentals=0),
         name="expert",
     )(own, other, *staged, *[part for part, _ in late])[:2]
 

time: 79.1 us -> 72.9 us (0.922)
  waiting for transfers between devices: 23.3 us -> 17.9 us
  starting transfers between devices: 31.4 us -> 30.3 us
    ppermute x1, waiting for transfers between devices: 2.74 us -> 0.01 us  [two_lane_shards(): arrived = swap(sent)]
    ppermute x8, waiting for transfers between devices: 13.8 us -> 11.6 us  [step(): self.mine.append(self.across(held))]
    all_to_all x1, starting transfers between devices: 6.35 us -> 5.11 us  [two_lane_shards(): lax.all_to_all(outgoing, 'grp', split_axis=0, concat_axis=0, tiled=True)]
    pallas_call x1, Pallas kernels: 1.05 us -> 2.04 us  [route(): pl.pallas_call(route_kernel, out_shape=(jax.ShapeDtypeStruct(mine.shape,...]
    all_to_all x1, waiting for transfers between devices: 0.85 us -> 0.01 us  [two_lane_shards(): lax.all_to_all(outgoing, 'grp', split_axis=0, concat_axis=0, tiled=True)]
  transfers between devices with their start and end apart: 25 -> 25, of which waited for: 12 -> 10; matrix products, arithmetic and copies ran while one was open for 4% -> 4% of each run, Pallas kernels for 23% -> 26%
where the time goes in v19:
time: 72.9 us; the launch traced here: 72.4 us
  starting transfers between devices  30.3 us (42%)
  Pallas kernels  20 us (27%)
  waiting for transfers between devices  17.9 us (25%)
  local copies, waits for them, and re-layouts  3.44 us (5%)
  between operations  0.82 us (1%)
    ppermute x8, starting transfers between devices, step(): self.mine.append(self.across(held))  13.9 us
    ppermute x8, waiting for transfers between devices, step(): self.mine.append(self.across(held))  11.6 us
    all_to_all x1, starting transfers between devices, two_lane_shards(): lax.all_to_all(outgoing, 'grp', split_axis=0, concat_axis=0, tiled=True)  5.11 us
    ppermute x1, waiting for transfers between devices, two_lane_shards(): returned = swap(back)  3.13 us
    unnamed x11, local copies, waits for them, and re-layouts  2.7 us
    ppermute x1, starting transfers between devices, two_lane_shards(): other_tokens = swap(tokens)  2.56 us
    pallas_call x1, Pallas kernels, project(): pl.pallas_call(project_kernel, out_shape=(jax.ShapeDtypeStruct((2 * count...  2.21 us
    pallas_call x1, Pallas kernels, expert(): pl.pallas_call(functools.partial(expert_kernel, groups, up_rows, down_row...  2.17 us
  transfers between devices with their start and end apart: 25, of which 10 were waited for; matrix products, arithmetic and copies ran while one was open for 4% of the time, Pallas kernels for 26%

profile of v19, /device:TPU:0, one launch (start us, length us, event | category | flops | bytes accessed | tf_op | source)
XLA Modules:
  0.0 72.4 jit_solution(4369920102606859814)
XLA Ops:
  1.7 2.6 %collective-permute-start.4 = (bf16[128,1536]{1,0:T(8,128)(2,1)}, bf16[128,1536]{1,0:T(8,128)(2,1)S(1)}, u32[]{:S(2)}, u32[]{:S(2)}) collective-permute-start(bf16[128,1536]{1,0:T(8,128)(2,1)} %tokens.1), channel_id=1, source_target_pairs={{0,1},{1,0},{2,3},{3,2},{4,5},{5,4},{6,7},{7,6},{8,9},{9,8},{10,11... | collective-permute-start | bytes 1179656 | tf_op jit(solution)/shard_map/ppermute | solution.py:727
  5.4 1.7 %collective-permute-start.5 = (bf16[192,768]{1,0:T(8,128)(2,1)S(1)}, bf16[192,768]{1,0:T(8,128)(2,1)S(1)}, u32[]{:S(2)}, u32[]{:S(2)}) collective-permute-start(bf16[192,768]{1,0:T(8,128)(2,1)S(1)} %get-tuple-element.66.refs_0_), channel_id=1, source_target_pairs={{0,8},{2,6},{8,16},{10,2},{16,24},{18,10},{24,28},{26,18},{28,20},... | collective-permute-start | bytes 884744 | tf_op jit(solution)/shard_map/ppermute | solution.py:70
  7.1 1.6 %collective-permute-start.3 = (bf16[576,512]{1,0:T(8,128)(2,1)S(1)}, bf16[576,512]{1,0:T(8,128)(2,1)S(1)}, u32[]{:S(2)}, u32[]{:S(2)}) collective-permute-start(bf16[576,512]{1,0:T(8,128)(2,1)S(1)} %get-tuple-element.65.refs_0_), channel_id=1, source_target_pairs={{0,8},{2,6},{8,16},{10,2},{16,24},{18,10},{24,28},{26,18},{28,20},... | collective-permute-start | bytes 1769480 | tf_op jit(solution)/shard_map/ppermute | solution.py:70
  8.7 1.5 %prepare.1 = (f32[256,128]{1,0:T(8,128)S(1)}, f32[256,128]{1,0:T(8,128)S(1)}, f32[256,128]{1,0:T(8,128)S(1)}, bf16[64,128]{1,0:T(8,128)(2,1)S(1)}, bf16[512,256]...) custom-call(s32[1,256]{1,0:T(1,128)} %bitcast.26, s32[1,256]{1,0:T(1,128)} %bitcast.27, ...), custom_call_target="tpu_custom_call" | custom-call | flops 1 | bytes 1 | tf_op jit(solution)/shard_map/prepare/pallas_call | solution.py:266
  10.2 1.8 %copy.19 = bf16[192,8,4,128]{3,1,2,0:T(8,128)(2,1)S(1)} copy(bf16[192,8,4,128]{3,2,1,0:T(4,128)(2,1)} %bitcast.15) | data formatting | bytes 3145728
  12.2 1.7 %collective-permute-start.7 = (bf16[192,768]{1,0:T(8,128)(2,1)S(1)}, bf16[192,768]{1,0:T(8,128)(2,1)S(1)}, u32[]{:S(2)}, u32[]{:S(2)}) collective-permute-start(bf16[192,768]{1,0:T(8,128)(2,1)S(1)} %collective-permute-done.5.refs_1_), channel_id=1, source_target_pairs={{0,8},{2,6},{8,16},{10,2},{16,24},{18,10},{24,28},{26,18},{28,20},... | collective-permute-start | bytes 884744 | tf_op jit(solution)/shard_map/ppermute | solution.py:70
  14.1 2.2 %project.1 = (bf16[256,768]{1,0:T(8,128)(2,1)S(1)}, bf16[256,512]{1,0:T(8,128)(2,1)S(1)}, bf16[128,512]{1,0:T(8,128)(2,1)S(1)}) custom-call(bf16[128,1536]{1,0:T(8,128)(2,1)S(1)} %copy-done.1, bf16[128,1536]{1,0:T(8,128)(2,1)S(1)} %collective-permute-done.4.other, f32[1,1536]{1,0:T(1,128)S(1)} %get-tuple-element.68.gain, ...), custom_call_target="tpu_custom_call" | custom-call | flops 9200000000 | bytes 64000000 | tf_op jit(solution)/shard_map/project/pallas_call | solution.py:316
  16.4 1.8 %collective-permute-start.6 = (bf16[128,512]{1,0:T(8,128)(2,1)S(1)}, bf16[128,512]{1,0:T(8,128)(2,1)S(1)}, u32[]{:S(2)}, u32[]{:S(2)}) collective-permute-start(bf16[128,512]{1,0:T(8,128)(2,1)S(1)} %get-tuple-element.74), channel_id=1, source_target_pairs={{0,2},{2,4},{4,6},{6,8},{8,10},{10,12},{12,14},{14,16},{16,18},{18... | collective-permute-start | bytes 393224 | tf_op jit(solution)/shard_map/ppermute | solution.py:745
  18.2 1.3 %attend_late.1.late = bf16[128,768]{1,0:T(8,128)(2,1)S(1)} custom-call(bf16[256,768]{1,0:T(8,128)(2,1)S(1)} %get-tuple-element.76.q, bf16[256,512]{1,0:T(8,128)(2,1)S(1)} %get-tuple-element.91.kv, f32[256,128]{1,0:T(8,128)S(1)} %get-tuple-element.78.past), custom_call_target="tpu_custom_call" | custom-call | flops 2300000000 | bytes 16000000 | tf_op jit(solution)/shard_map/attend_late/pallas_call | solution.py:372
  19.5 2.1 %collective-permute-done.7.refs_2_ = bf16[192,768]{1,0:T(8,128)(2,1)S(1)} collective-permute-done((bf16[192,768]{1,0:T(8,128)(2,1)S(1)}, bf16[192,768]{1,0:T(8,128)(2,1)S(1)}, u32[]{:S(2)}, u32[]{:S(2)}) %collective-permute-start.7) | collective-permute-done | bytes 294944 | tf_op jit(solution)/shard_map/ppermute | solution.py:70
  21.6 1.7 %collective-permute-start.9 = (bf16[192,768]{1,0:T(8,128)(2,1)S(1)}, bf16[192,768]{1,0:T(8,128)(2,1)S(1)}, u32[]{:S(2)}, u32[]{:S(2)}) collective-permute-start(bf16[192,768]{1,0:T(8,128)(2,1)S(1)} %collective-permute-done.7.refs_2_), channel_id=1, source_target_pairs={{0,8},{2,6},{8,16},{10,2},{16,24},{18,10},{24,28},{26,18},{28,20},... | collective-permute-start | bytes 884744 | tf_op jit(solution)/shard_map/ppermute | solution.py:70
  23.3 2.1 %collective-permute-start.8 = (bf16[576,512]{1,0:T(8,128)(2,1)S(1)}, bf16[576,512]{1,0:T(8,128)(2,1)S(1)}, u32[]{:S(2)}, u32[]{:S(2)}) collective-permute-start(bf16[576,512]{1,0:T(8,128)(2,1)S(1)} %collective-permute-done.3.refs_1_), channel_id=1, source_target_pairs={{0,8},{2,6},{8,16},{10,2},{16,24},{18,10},{24,28},{26,18},{28,20},... | collective-permute-start | bytes 1769480 | tf_op jit(solution)/shard_map/ppermute | solution.py:70
  25.4 1.5 %attend_early.1.early = bf16[128,768]{1,0:T(8,128)(2,1)S(1)} custom-call(bf16[256,768]{1,0:T(8,128)(2,1)S(1)} %get-tuple-element.76.q, bf16[256,512]{1,0:T(8,128)(2,1)S(1)} %get-tuple-element.91.kv, bf16[128,512]{1,0:T(8,128)(2,1)S(1)} %collective-permute-done.6.seam, f32[256,128]{1,0:T(8,128)S(1)} %get-tuple-element.78.past), custom_call_target="tpu_custom_call" | custom-call | flops 2300000000 | bytes 16000000 | tf_op jit(solution)/shard_map/attend_early/pallas_call | solution.py:384
  26.9 1.5 %collective-permute-done.9.refs_3_ = bf16[192,768]{1,0:T(8,128)(2,1)S(1)} collective-permute-done((bf16[192,768]{1,0:T(8,128)(2,1)S(1)}, bf16[192,768]{1,0:T(8,128)(2,1)S(1)}, u32[]{:S(2)}, u32[]{:S(2)}) %collective-permute-start.9) | collective-permute-done | bytes 294944 | tf_op jit(solution)/shard_map/ppermute | solution.py:70
  28.4 1.7 %collective-permute-start.12 = (bf16[96,768]{1,0:T(8,128)(2,1)S(1)}, bf16[96,768]{1,0:T(8,128)(2,1)S(1)}, u32[]{:S(2)}, u32[]{:S(2)}) collective-permute-start(bf16[96,768]{1,0:T(8,128)(2,1)S(1)} %slice.6), channel_id=1, source_target_pairs={{0,8},{2,6},{8,16},{10,2},{16,24},{18,10},{24,28},{26,18},{28,20},... | collective-permute-start | bytes 442376 | tf_op jit(solution)/shard_map/ppermute | solution.py:70
  30.1 1.4 %bundle.1 = bf16[16,144,128]{2,1,0:T(8,128)(2,1)} custom-call(bf16[512,256]{1,0:T(8,128)(2,1)S(1)} %get-tuple-element.90.send, bf16[256,512]{1,0:T(8,128)(2,1)S(1)} %get-tuple-element.91.kv, bf16[256,128]{1,0:T(8,128)(2,1)S(1)} %get-tuple-element.92.tags), custom_call_target="tpu_custom_call" | custom-call | flops 1 | bytes 1 | tf_op jit(solution)/shard_map/bundle/pallas_call | solution.py:644
  31.5 4.7 %collective-permute-done.12.refs_7_ = bf16[96,768]{1,0:T(8,128)(2,1)S(1)} collective-permute-done((bf16[96,768]{1,0:T(8,128)(2,1)S(1)}, bf16[96,768]{1,0:T(8,128)(2,1)S(1)}, u32[]{:S(2)}, u32[]{:S(2)}) %collective-permute-start.12) | collective-permute-done | bytes 147488 | tf_op jit(solution)/shard_map/ppermute | solution.py:70
  36.3 1.7 %collective-permute-start.16 = (bf16[576,512]{1,0:T(8,128)(2,1)S(1)}, bf16[576,512]{1,0:T(8,128)(2,1)S(1)}, u32[]{:S(2)}, u32[]{:S(2)}) collective-permute-start(bf16[576,512]{1,0:T(8,128)(2,1)S(1)} %collective-permute-done.8.refs_2_), channel_id=1, source_target_pairs={{0,8},{2,6},{8,16},{10,2},{16,24},{18,10},{24,28},{26,18},{28,20},... | collective-permute-start | bytes 1769480 | tf_op jit(solution)/shard_map/ppermute | solution.py:70
  38.0 1.4 %collective-permute-done.14.refs_8_ = bf16[96,768]{1,0:T(8,128)(2,1)S(1)} collective-permute-done((bf16[96,768]{1,0:T(8,128)(2,1)S(1)}, bf16[96,768]{1,0:T(8,128)(2,1)S(1)}, u32[]{:S(2)}, u32[]{:S(2)}) %collective-permute-start.14) | collective-permute-done | bytes 147488 | tf_op jit(solution)/shard_map/ppermute | solution.py:79
  40.5 1.6 %collective-permute-start.15 = (bf16[128,1536]{1,0:T(8,128)(2,1)S(1)}, bf16[128,1536]{1,0:T(8,128)(2,1)}, u32[]{:S(2)}, u32[]{:S(2)}) collective-permute-start(bf16[128,1536]{1,0:T(8,128)(2,1)S(1)} %outward_send.1), channel_id=1, source_target_pairs={{0,1},{1,0},{2,3},{3,2},{4,5},{5,4},{6,7},{7,6},{8,9},{9,8},{10,11... | collective-permute-start | bytes 1179656 | tf_op jit(solution)/shard_map/ppermute | solution.py:766
  42.1 1.1 %outward_keep.1.mine = f32[128,1536]{1,0:T(8,128)S(1)} custom-call(bf16[128,768]{1,0:T(8,128)(2,1)S(1)} %attend_early.1.early, bf16[128,768]{1,0:T(8,128)(2,1)S(1)} %attend_late.1.late, bf16[128,1536]{1,0:T(8,128)(2,1)S(1)} %copy-done.1, bf16[192,768]{1,0:T(8,128)(2,1)S(1)} %get-tuple-element.66.refs_0_, ...), custom_call_target="tpu_custom_call" | custom-call | flops 1 | bytes 2359296 | tf_op jit(solution)/shard_map/outward_keep/pallas_call | solution.py:439
  43.2 2.9 %collective-permute-done.16.refs_0_ = bf16[576,512]{1,0:T(8,128)(2,1)S(1)} collective-permute-done((bf16[576,512]{1,0:T(8,128)(2,1)S(1)}, bf16[576,512]{1,0:T(8,128)(2,1)S(1)}, u32[]{:S(2)}, u32[]{:S(2)}) %collective-permute-start.16) | collective-permute-done | bytes 589856 | tf_op jit(solution)/shard_map/ppermute | solution.py:70
  47.7 1.7 %collective-permute-start.17 = (bf16[288,512]{1,0:T(8,128)(2,1)}, bf16[288,512]{1,0:T(8,128)(2,1)}, u32[]{:S(2)}, u32[]{:S(2)}) collective-permute-start(bf16[288,512]{1,0:T(8,128)(2,1)} %slice.7), channel_id=1, source_target_pairs={{0,8},{2,6},{8,16},{10,2},{16,24},{18,10},{24,28},{26,18},{28,20},... | collective-permute-start | bytes 884744 | tf_op jit(solution)/shard_map/ppermute | solution.py:70
  49.4 5.1 %all-to-all-start = ((bf16[16,144,128]{2,1,0:T(8,128)(2,1)}), bf16[16,144,128]{2,1,0:T(8,128)(2,1)S(1)}, u32[]{:S(2)}, u32[]{:S(2)}) async-start(bf16[16,144,128]{2,1,0:T(8,128)(2,1)} %bundle.1), calls=%async_computation | async-start | bytes 1179648 | tf_op jit(solution)/shard_map/all_to_all | solution.py:772
  55.8 2.0 %route.1 = (bf16[128,1536]{1,0:T(8,128)(2,1)S(1)}, bf16[128,1536]{1,0:T(8,128)(2,1)S(1)}, bf16[32,1536]{1,0:T(8,128)(2,1)S(1)}) custom-call(f32[128,1536]{1,0:T(8,128)S(1)} %outward_keep.1.mine, bf16[128,1536]{1,0:T(8,128)(2,1)} %collective-permute-done.15.arrived, f32[1536]{0:T(1024)} %flat_gain.1, bf16[64,128]{1,0:T(8,128)(2,1)S(1)} %get-tuple-element.107.place), custom_call_target="tpu_custom_call" | custom-call | flops 1 | bytes 16777216 | tf_op jit(solution)/shard_map/route/pallas_call | solution.py:468
  57.8 1.7 %collective-permute-start.20 = (bf16[32,1536]{1,0:T(8,128)(2,1)S(1)}, bf16[32,1536]{1,0:T(8,128)(2,1)S(1)}, u32[]{:S(2)}, u32[]{:S(2)}) collective-permute-start(bf16[32,1536]{1,0:T(8,128)(2,1)S(1)} %get-tuple-element.114), channel_id=1, source_target_pairs={{0,1},{1,0},{2,3},{3,2},{4,5},{5,4},{6,7},{7,6},{8,9},{9,8},{10,11... | collective-permute-start | bytes 294920 | tf_op jit(solution)/shard_map/ppermute | solution.py:777
  59.5 1.9 %gate.1 = (f32[128,40]{1,0:T(8,128)S(1)}, bf16[32,1536]{1,0:T(8,128)(2,1)S(1)}, bf16[128,64]{1,0:T(8,128)(2,1)S(1)}, bf16[1536,1024]{1,0:T(8,128)(2,1)S(1)}, bf16[512,1536]{1,0:T(8,128)(2,1)S(1)}) custom-call(bf16[128,1536]{1,0:T(8,128)(2,1)S(1)} %get-tuple-element.109.moe_in, bf16[40,1536]{1,0:T(8,128)(2,1)} %bitcast.21, s32[8,128]{1,0:T(8,128)} %bitcast.25, ...), custom_call_target="tpu_custom_call" | custom-call | flops 1 | bytes 1 | tf_op jit(solution)/shard_map/gate/pallas_call | solution.py:538
  61.4 1.5 %collective-permute-done.20.other = bf16[32,1536]{1,0:T(8,128)(2,1)S(1)} collective-permute-done((bf16[32,1536]{1,0:T(8,128)(2,1)S(1)}, bf16[32,1536]{1,0:T(8,128)(2,1)S(1)}, u32[]{:S(2)}, u32[]{:S(2)}) %collective-permute-start.20) | collective-permute-done | bytes 98336 | tf_op jit(solution)/shard_map/ppermute | solution.py:777
  62.9 2.2 %expert.1 = (bf16[32,1536]{1,0:T(8,128)(2,1)S(1)}, bf16[32,1536]{1,0:T(8,128)(2,1)S(1)}, bf16[1536,1024]{1,0:T(8,128)(2,1)S(1)}, bf16[512,1536]{1,0:T(8,128)(2,1)S(1)}) custom-call(bf16[32,1536]{1,0:T(8,128)(2,1)S(1)} %get-tuple-element.116.own, bf16[32,1536]{1,0:T(8,128)(2,1)S(1)} %collective-permute-done.20.other, ...), custom_call_target="tpu_custom_call", output_to_operand_aliasing={{2}: (2, {}), {3}: (3, {})} | custom-call | flops 2529999872 | bytes 1 | tf_op jit(solution)/shard_map/expert/pallas_call | solution.py:581
  65.1 1.5 %collective-permute-start.23 = (bf16[32,1536]{1,0:T(8,128)(2,1)S(1)}, bf16[32,1536]{1,0:T(8,128)(2,1)S(1)}, u32[]{:S(2)}, u32[]{:S(2)}) collective-permute-start(bf16[32,1536]{1,0:T(8,128)(2,1)S(1)} %get-tuple-element.123), channel_id=1, source_target_pairs={{0,1},{1,0},{2,3},{3,2},{4,5},{5,4},{6,7},{7,6},{8,9},{9,8},{10,11... | collective-permute-start | bytes 294920 | tf_op jit(solution)/shard_map/ppermute | solution.py:784
  66.6 3.1 %collective-permute-done.23.returned = bf16[32,1536]{1,0:T(8,128)(2,1)S(1)} collective-permute-done((bf16[32,1536]{1,0:T(8,128)(2,1)S(1)}, bf16[32,1536]{1,0:T(8,128)(2,1)S(1)}, u32[]{:S(2)}, u32[]{:S(2)}) %collective-permute-start.23) | collective-permute-done | bytes 98336 | tf_op jit(solution)/shard_map/ppermute | solution.py:784
  70.9 1.5 %write.1 = bf16[2048,128]{1,0:T(8,128)(2,1)} custom-call(bf16[16,144,128]{2,1,0:T(8,128)(2,1)S(1)} %all-to-all-done.arrived, bf16[2048,128]{1,0:T(8,128)(2,1)S(1)} %bitcast.14), custom_call_target="tpu_custom_call" | custom-call | flops 1 | bytes 2097152 | tf_op jit(solution)/shard_map/write/pallas_call | solution.py:685
  (44 shorter events, 7.7 us)
Async XLA Ops:
  0.6 3.6 %collective-permute-start.2 = (bf16[96,1536]{1,0:T(8,128)(2,1)}, bf16[96,1536]{1,0:T(8,128)(2,1)S(1)}, u32[]{:S(2)}, u32[]{:S(2)}) collective-permute-start(bf16[96,1536]{1,0:T(8,128)(2,1)} %bitcast.17), channel_id=1, source_target_pairs={{0,2},{2,0},{4,6},{6,4},{8,10},{10,8},{12,14},{14,12},{16,18},{18,... | collective-permute-start | bytes 884744 | tf_op jit(solution)/shard_map/ppermute | solution.py:730
  1.1 3.1 %collective-permute-start = (bf16[96,1024]{1,0:T(8,128)(2,1)}, bf16[96,1024]{1,0:T(8,128)(2,1)S(1)}, u32[]{:S(2)}, u32[]{:S(2)}) collective-permute-start(bf16[96,1024]{1,0:T(8,128)(2,1)} %bitcast.19), channel_id=1, source_target_pairs={{0,2},{2,0},{4,6},{6,4},{8,10},{10,8},{12,14},{14,12},{16,18},{18,... | collective-permute-start | bytes 589832 | tf_op jit(solution)/shard_map/ppermute | solution.py:730
  1.2 3.0 %collective-permute-start.1 = (bf16[32,1536]{1,0:T(8,128)(2,1)}, bf16[32,1536]{1,0:T(8,128)(2,1)S(1)}, u32[]{:S(2)}, u32[]{:S(2)}) collective-permute-start(bf16[32,1536]{1,0:T(8,128)(2,1)} %bitcast.22), channel_id=1, source_target_pairs={{0,2},{2,0},{4,6},{6,4},{8,10},{10,8},{12,14},{14,12},{16,18},{18,... | collective-permute-start | bytes 294920 | tf_op jit(solution)/shard_map/ppermute | solution.py:730
  1.7 12.5 %collective-permute-start.4 = (bf16[128,1536]{1,0:T(8,128)(2,1)}, bf16[128,1536]{1,0:T(8,128)(2,1)S(1)}, u32[]{:S(2)}, u32[]{:S(2)}) collective-permute-start(bf16[128,1536]{1,0:T(8,128)(2,1)} %tokens.1), channel_id=1, source_target_pairs={{0,1},{1,0},{2,3},{3,2},{4,5},{5,4},{6,7},{7,6},{8,9},{9,8},{10,11... | collective-permute-start | bytes 1179656 | tf_op jit(solution)/shard_map/ppermute | solution.py:727
  5.4 6.8 %collective-permute-start.5 = (bf16[192,768]{1,0:T(8,128)(2,1)S(1)}, bf16[192,768]{1,0:T(8,128)(2,1)S(1)}, u32[]{:S(2)}, u32[]{:S(2)}) collective-permute-start(bf16[192,768]{1,0:T(8,128)(2,1)S(1)} %get-tuple-element.66.refs_0_), channel_id=1, source_target_pairs={{0,8},{2,6},{8,16},{10,2},{16,24},{18,10},{24,28},{26,18},{28,20},... | collective-permute-start | bytes 884744 | tf_op jit(solution)/shard_map/ppermute | solution.py:70
  7.1 16.2 %collective-permute-start.3 = (bf16[576,512]{1,0:T(8,128)(2,1)S(1)}, bf16[576,512]{1,0:T(8,128)(2,1)S(1)}, u32[]{:S(2)}, u32[]{:S(2)}) collective-permute-start(bf16[576,512]{1,0:T(8,128)(2,1)S(1)} %get-tuple-element.65.refs_0_), channel_id=1, source_target_pairs={{0,8},{2,6},{8,16},{10,2},{16,24},{18,10},{24,28},{26,18},{28,20},... | collective-permute-start | bytes 1769480 | tf_op jit(solution)/shard_map/ppermute | solution.py:70
  10.2 4.0 %copy-start.1 = (bf16[128,1536]{1,0:T(8,128)(2,1)S(1)}, bf16[128,1536]{1,0:T(8,128)(2,1)}, u32[]{:S(2)}) copy-start(bf16[128,1536]{1,0:T(8,128)(2,1)} %tokens.1) | copy-start | bytes 1179652
  10.2 4.0 %copy-start.4 = (bf16[1536,768]{1,0:T(8,128)(2,1)S(1)}, bf16[1536,768]{1,0:T(8,128)(2,1)}, u32[]{:S(2)}) copy-start(bf16[1536,768]{1,0:T(8,128)(2,1)} %w_query.1) | copy-start | bytes 7077892
  12.2 14.7 %collective-permute-start.10 = (bf16[192,768]{1,0:T(8,128)(2,1)S(1)}, bf16[192,768]{1,0:T(8,128)(2,1)S(1)}, u32[]{:S(2)}, u32[]{:S(2)}) collective-permute-start(bf16[192,768]{1,0:T(8,128)(2,1)S(1)} %collective-permute-done.5.refs_1_), channel_id=1, source_target_pairs={{0,2},{2,0},{4,6},{6,4},{8,10},{10,8},{12,14},{14,12},{16,18},{18,... | collective-permute-start | bytes 884744 | tf_op jit(solution)/shard_map/ppermute | solution.py:79
  12.2 9.5 %collective-permute-start.7 = (bf16[192,768]{1,0:T(8,128)(2,1)S(1)}, bf16[192,768]{1,0:T(8,128)(2,1)S(1)}, u32[]{:S(2)}, u32[]{:S(2)}) collective-permute-start(bf16[192,768]{1,0:T(8,128)(2,1)S(1)} %collective-permute-done.5.refs_1_), channel_id=1, source_target_pairs={{0,8},{2,6},{8,16},{10,2},{16,24},{18,10},{24,28},{26,18},{28,20},... | collective-permute-start | bytes 884744 | tf_op jit(solution)/shard_map/ppermute | solution.py:70
  16.4 7.0 %collective-permute-start.6 = (bf16[128,512]{1,0:T(8,128)(2,1)S(1)}, bf16[128,512]{1,0:T(8,128)(2,1)S(1)}, u32[]{:S(2)}, u32[]{:S(2)}) collective-permute-start(bf16[128,512]{1,0:T(8,128)(2,1)S(1)} %get-tuple-element.74), channel_id=1, source_target_pairs={{0,2},{2,4},{4,6},{6,8},{8,10},{10,12},{12,14},{14,16},{16,18},{18... | collective-permute-start | bytes 393224 | tf_op jit(solution)/shard_map/ppermute | solution.py:745
  21.6 5.2 %collective-permute-start.11 = (bf16[192,768]{1,0:T(8,128)(2,1)S(1)}, bf16[192,768]{1,0:T(8,128)(2,1)S(1)}, u32[]{:S(2)}, u32[]{:S(2)}) collective-permute-start(bf16[192,768]{1,0:T(8,128)(2,1)S(1)} %collective-permute-done.7.refs_2_), channel_id=1, source_target_pairs={{0,2},{2,0},{4,6},{6,4},{8,10},{10,8},{12,14},{14,12},{16,18},{18,... | collective-permute-start | bytes 884744 | tf_op jit(solution)/shard_map/ppermute | solution.py:79
  21.6 6.7 %collective-permute-start.9 = (bf16[192,768]{1,0:T(8,128)(2,1)S(1)}, bf16[192,768]{1,0:T(8,128)(2,1)S(1)}, u32[]{:S(2)}, u32[]{:S(2)}) collective-permute-start(bf16[192,768]{1,0:T(8,128)(2,1)S(1)} %collective-permute-done.7.refs_2_), channel_id=1, source_target_pairs={{0,8},{2,6},{8,16},{10,2},{16,24},{18,10},{24,28},{26,18},{28,20},... | collective-permute-start | bytes 884744 | tf_op jit(solution)/shard_map/ppermute | solution.py:70
  23.3 12.9 %collective-permute-start.8 = (bf16[576,512]{1,0:T(8,128)(2,1)S(1)}, bf16[576,512]{1,0:T(8,128)(2,1)S(1)}, u32[]{:S(2)}, u32[]{:S(2)}) collective-permute-start(bf16[576,512]{1,0:T(8,128)(2,1)S(1)} %collective-permute-done.3.refs_1_), channel_id=1, source_target_pairs={{0,8},{2,6},{8,16},{10,2},{16,24},{18,10},{24,28},{26,18},{28,20},... | collective-permute-start | bytes 1769480 | tf_op jit(solution)/shard_map/ppermute | solution.py:70
  28.4 1.8 %collective-permute-start.13 = (bf16[192,768]{1,0:T(8,128)(2,1)S(1)}, bf16[192,768]{1,0:T(8,128)(2,1)S(1)}, u32[]{:S(2)}, u32[]{:S(2)}) collective-permute-start(bf16[192,768]{1,0:T(8,128)(2,1)S(1)} %collective-permute-done.9.refs_3_), channel_id=1, source_target_pairs={{0,2},{2,0},{4,6},{6,4},{8,10},{10,8},{12,14},{14,12},{16,18},{18,... | collective-permute-start | bytes 884744 | tf_op jit(solution)/shard_map/ppermute | solution.py:79
  28.4 7.9 %collective-permute-start.12 = (bf16[96,768]{1,0:T(8,128)(2,1)S(1)}, bf16[96,768]{1,0:T(8,128)(2,1)S(1)}, u32[]{:S(2)}, u32[]{:S(2)}) collective-permute-start(bf16[96,768]{1,0:T(8,128)(2,1)S(1)} %slice.6), channel_id=1, source_target_pairs={{0,8},{2,6},{8,16},{10,2},{16,24},{18,10},{24,28},{26,18},{28,20},... | collective-permute-start | bytes 442376 | tf_op jit(solution)/shard_map/ppermute | solution.py:70
  36.3 9.9 %collective-permute-start.16 = (bf16[576,512]{1,0:T(8,128)(2,1)S(1)}, bf16[576,512]{1,0:T(8,128)(2,1)S(1)}, u32[]{:S(2)}, u32[]{:S(2)}) collective-permute-start(bf16[576,512]{1,0:T(8,128)(2,1)S(1)} %collective-permute-done.8.refs_2_), channel_id=1, source_target_pairs={{0,8},{2,6},{8,16},{10,2},{16,24},{18,10},{24,28},{26,18},{28,20},... | collective-permute-start | bytes 1769480 | tf_op jit(solution)/shard_map/ppermute | solution.py:70
  38.0 1.4 %collective-permute-start.14 = (bf16[96,768]{1,0:T(8,128)(2,1)S(1)}, bf16[96,768]{1,0:T(8,128)(2,1)S(1)}, u32[]{:S(2)}, u32[]{:S(2)}) collective-permute-start(bf16[96,768]{1,0:T(8,128)(2,1)S(1)} %collective-permute-done.12.refs_7_), channel_id=1, source_target_pairs={{0,2},{2,0},{4,6},{6,4},{8,10},{10,8},{12,14},{14,12},{16,18},{18,... | collective-permute-start | bytes 442376 | tf_op jit(solution)/shard_map/ppermute | solution.py:79
  40.5 14.1 %collective-permute-start.15 = (bf16[128,1536]{1,0:T(8,128)(2,1)S(1)}, bf16[128,1536]{1,0:T(8,128)(2,1)}, u32[]{:S(2)}, u32[]{:S(2)}) collective-permute-start(bf16[128,1536]{1,0:T(8,128)(2,1)S(1)} %outward_send.1), channel_id=1, source_target_pairs={{0,1},{1,0},{2,3},{3,2},{4,5},{5,4},{6,7},{7,6},{8,9},{9,8},{10,11... | collective-permute-start | bytes 1179656 | tf_op jit(solution)/shard_map/ppermute | solution.py:766
  46.2 0.8 %copy-start.2 = (bf16[576,512]{1,0:T(8,128)(2,1)}, bf16[576,512]{1,0:T(8,128)(2,1)S(1)}, u32[]{:S(2)}) copy-start(bf16[576,512]{1,0:T(8,128)(2,1)S(1)} %collective-permute-done.16.refs_0_) | copy-start | bytes 1769476
  47.7 7.0 %collective-permute-start.17 = (bf16[288,512]{1,0:T(8,128)(2,1)}, bf16[288,512]{1,0:T(8,128)(2,1)}, u32[]{:S(2)}, u32[]{:S(2)}) collective-permute-start(bf16[288,512]{1,0:T(8,128)(2,1)} %slice.7), channel_id=1, source_target_pairs={{0,8},{2,6},{8,16},{10,2},{16,24},{18,10},{24,28},{26,18},{28,20},... | collective-permute-start | bytes 884744 | tf_op jit(solution)/shard_map/ppermute | solution.py:70
  49.4 21.5 %all-to-all-start = ((bf16[16,144,128]{2,1,0:T(8,128)(2,1)}), bf16[16,144,128]{2,1,0:T(8,128)(2,1)S(1)}, u32[]{:S(2)}, u32[]{:S(2)}) async-start(bf16[16,144,128]{2,1,0:T(8,128)(2,1)} %bundle.1), calls=%async_computation | async-start | bytes 1179648 | tf_op jit(solution)/shard_map/all_to_all | solution.py:772
  54.8 4.8 %collective-permute-start.18 = (bf16[576,512]{1,0:T(8,128)(2,1)S(1)}, bf16[576,512]{1,0:T(8,128)(2,1)S(1)}, u32[]{:S(2)}, u32[]{:S(2)}) collective-permute-start(bf16[576,512]{1,0:T(8,128)(2,1)S(1)} %collective-permute-done.3.refs_1_), channel_id=1, source_target_pairs={{0,2},{2,0},{4,6},{6,4},{8,10},{10,8},{12,14},{14,12},{16,18},{18,... | collective-permute-start | bytes 1769480 | tf_op jit(solution)/shard_map/ppermute | solution.py:79
  55.0 4.5 %collective-permute-start.19 = (bf16[576,512]{1,0:T(8,128)(2,1)S(1)}, bf16[576,512]{1,0:T(8,128)(2,1)S(1)}, u32[]{:S(2)}, u32[]{:S(2)}) collective-permute-start(bf16[576,512]{1,0:T(8,128)(2,1)S(1)} %collective-permute-done.8.refs_2_), channel_id=1, source_target_pairs={{0,2},{2,0},{4,6},{6,4},{8,10},{10,8},{12,14},{14,12},{16,18},{18,... | collective-permute-start | bytes 1769480 | tf_op jit(solution)/shard_map/ppermute | solution.py:79
  55.3 7.6 %collective-permute-start.21 = (bf16[576,512]{1,0:T(8,128)(2,1)}, bf16[576,512]{1,0:T(8,128)(2,1)S(1)}, u32[]{:S(2)}, u32[]{:S(2)}) collective-permute-start(bf16[576,512]{1,0:T(8,128)(2,1)} %copy-done.2), channel_id=1, source_target_pairs={{0,2},{2,0},{4,6},{6,4},{8,10},{10,8},{12,14},{14,12},{16,18},{18,... | collective-permute-start | bytes 1769480 | tf_op jit(solution)/shard_map/ppermute | solution.py:79
  55.5 7.3 %collective-permute-start.22 = (bf16[288,512]{1,0:T(8,128)(2,1)}, bf16[288,512]{1,0:T(8,128)(2,1)S(1)}, u32[]{:S(2)}, u32[]{:S(2)}) collective-permute-start(bf16[288,512]{1,0:T(8,128)(2,1)} %collective-permute-done.17.refs_2_), channel_id=1, source_target_pairs={{0,2},{2,0},{4,6},{6,4},{8,10},{10,8},{12,14},{14,12},{16,18},{18,... | collective-permute-start | bytes 884744 | tf_op jit(solution)/shard_map/ppermute | solution.py:79
  57.8 5.0 %collective-permute-start.20 = (bf16[32,1536]{1,0:T(8,128)(2,1)S(1)}, bf16[32,1536]{1,0:T(8,128)(2,1)S(1)}, u32[]{:S(2)}, u32[]{:S(2)}) collective-permute-start(bf16[32,1536]{1,0:T(8,128)(2,1)S(1)} %get-tuple-element.114), channel_id=1, source_target_pairs={{0,1},{1,0},{2,3},{3,2},{4,5},{5,4},{6,7},{7,6},{8,9},{9,8},{10,11... | collective-permute-start | bytes 294920 | tf_op jit(solution)/shard_map/ppermute | solution.py:777
  59.5 3.4 %copy-start.3 = (bf16[576,512]{1,0:T(8,128)(2,1)S(1)}, bf16[576,512]{1,0:T(8,128)(2,1)}, u32[]{:S(2)}) copy-start(bf16[576,512]{1,0:T(8,128)(2,1)} %copy-done.2) | copy-start | bytes 1769476
  62.9 8.0 %copy-start = (bf16[512,4,128]{2,1,0:T(4,128)(2,1)S(1)}, bf16[512,4,128]{2,1,0:T(4,128)(2,1)}, u32[]{:S(2)}) copy-start(bf16[512,4,128]{2,1,0:T(4,128)(2,1)} %param.25) | copy-start | bytes 1572868
  65.1 4.7 %collective-permute-start.23 = (bf16[32,1536]{1,0:T(8,128)(2,1)S(1)}, bf16[32,1536]{1,0:T(8,128)(2,1)S(1)}, u32[]{:S(2)}, u32[]{:S(2)}) collective-permute-start(bf16[32,1536]{1,0:T(8,128)(2,1)S(1)} %get-tuple-element.123), channel_id=1, source_target_pairs={{0,1},{1,0},{2,3},{3,2},{4,5},{5,4},{6,7},{7,6},{8,9},{9,8},{10,11... | collective-permute-start | bytes 294920 | tf_op jit(solution)/shard_map/ppermute | solution.py:784

commit v20 on v12

--- a/solution.py
+++ b/solution.py
@@ -538,7 +538,7 @@
             pltpu.VMEM((groups * down_rows, model), bf16),
         ],
         compiler_params=PARAMS,
-        cost_estimate=takes(5.2),
+        cost_estimate=takes(4.0),
         name="expert",
     )(own, other, *parts)
 

time: 72.9 us -> 72.9 us (level)
  no operation moved by 1% of the time
where the time goes in v20:
time: 72.9 us; the launch traced here: 72.5 us
  starting transfers between devices  30.9 us (42%)
  waiting for transfers between devices  20.2 us (28%)
  Pallas kernels  18 us (25%)
  local copies, waits for them, and re-layouts  2.61 us (4%)
  between operations  0.88 us (1%)
    ppermute x8, starting transfers between devices, step(): self.mine.append(self.across(held))  15.3 us
    ppermute x8, waiting for transfers between devices, step(): self.mine.append(self.across(held))  8.36 us
    all_to_all x1, starting transfers between devices, two_lane_shards(): lax.all_to_all(outgoing, 'grp', split_axis=0, concat_axis=0, tiled=True)  4.33 us
    ppermute x1, waiting for transfers between devices, two_lane_shards(): returned = swap(back)  3.35 us
    ppermute x1, waiting for transfers between devices, two_lane_shards(): landed = swap(sent_rows)  3.22 us
    pallas_call x1, Pallas kernels, expert(): pl.pallas_call(functools.partial(expert_kernel, groups, up_rows, down_row...  3.17 us
    ppermute x8, waiting for transfers between devices, share(): self.near.append(self.beside(self.mine[index]))  3.15 us
    ppermute x1, starting transfers between devices, two_lane_shards(): other_tokens = swap(tokens)  2.56 us
  transfers between devices with their start and end apart: 25, of which 8 were waited for; matrix products, arithmetic and copies ran while one was open for 4% of the time, Pallas kernels for 23%

profile of v20, /device:TPU:0, one launch (start us, length us, event | category | flops | bytes accessed | tf_op | source)
XLA Modules:
  0.0 72.5 jit_solution(638495653525803454)
XLA Ops:
  1.7 2.6 %collective-permute-start.5 = (bf16[128,1536]{1,0:T(8,128)(2,1)}, bf16[128,1536]{1,0:T(8,128)(2,1)S(1)}, u32[]{:S(2)}, u32[]{:S(2)}) collective-permute-start(bf16[128,1536]{1,0:T(8,128)(2,1)} %tokens.1), channel_id=1, source_target_pairs={{0,1},{1,0},{2,3},{3,2},{4,5},{5,4},{6,7},{7,6},{8,9},{9,8},{10,11... | collective-permute-start | bytes 1179656 | tf_op jit(solution)/shard_map/ppermute | solution.py:678
  4.2 1.1 %pack.1 = (bf16[576,512]{1,0:T(8,128)(2,1)S(1)}, bf16[192,768]{1,0:T(8,128)(2,1)S(1)}) custom-call(bf16[96,1024]{1,0:T(8,128)(2,1)} %bitcast.23, bf16[32,1536]{1,0:T(8,128)(2,1)} %bitcast.25, bf16[96,1536]{1,0:T(8,128)(2,1)} %bitcast.21, bf16[96,1024]{1,0:T(8,128)(2,1)S(1)} %collective-permute-done.refs_3_, ...), custom_call_target="tpu_custom_call" | custom-call | flops 1 | bytes 1 | tf_op jit(solution)/shard_map/pack/pallas_call | solution.py:159
  5.4 1.7 %collective-permute-start.4 = (bf16[192,768]{1,0:T(8,128)(2,1)S(1)}, bf16[192,768]{1,0:T(8,128)(2,1)S(1)}, u32[]{:S(2)}, u32[]{:S(2)}) collective-permute-start(bf16[192,768]{1,0:T(8,128)(2,1)S(1)} %get-tuple-element.62.refs_0_), channel_id=1, source_target_pairs={{0,8},{2,6},{8,16},{10,2},{16,24},{18,10},{24,28},{26,18},{28,20},... | collective-permute-start | bytes 884744 | tf_op jit(solution)/shard_map/ppermute | solution.py:70
  7.1 1.6 %collective-permute-start.3 = (bf16[576,512]{1,0:T(8,128)(2,1)S(1)}, bf16[576,512]{1,0:T(8,128)(2,1)}, u32[]{:S(2)}, u32[]{:S(2)}) collective-permute-start(bf16[576,512]{1,0:T(8,128)(2,1)S(1)} %get-tuple-element.61.refs_0_), channel_id=1, source_target_pairs={{0,8},{2,6},{8,16},{10,2},{16,24},{18,10},{24,28},{26,18},{28,20},... | collective-permute-start | bytes 1769480 | tf_op jit(solution)/shard_map/ppermute | solution.py:70
  8.7 1.5 %prepare.1 = (f32[256,128]{1,0:T(8,128)S(1)}, f32[256,128]{1,0:T(8,128)S(1)}, f32[256,128]{1,0:T(8,128)S(1)}, bf16[64,128]{1,0:T(8,128)(2,1)S(1)}, bf16[512,256]...) custom-call(s32[1,256]{1,0:T(1,128)} %bitcast.26, s32[1,256]{1,0:T(1,128)} %bitcast.27, ...), custom_call_target="tpu_custom_call" | custom-call | flops 1 | bytes 1 | tf_op jit(solution)/shard_map/prepare/pallas_call | solution.py:255
  10.2 1.8 %copy.17 = bf16[192,8,4,128]{3,1,2,0:T(8,128)(2,1)S(1)} copy(bf16[192,8,4,128]{3,2,1,0:T(4,128)(2,1)} %bitcast.18) | data formatting | bytes 3145728
  12.0 2.1 %collective-permute-done.5.other = bf16[128,1536]{1,0:T(8,128)(2,1)S(1)} collective-permute-done((bf16[128,1536]{1,0:T(8,128)(2,1)}, bf16[128,1536]{1,0:T(8,128)(2,1)S(1)}, u32[]{:S(2)}, u32[]{:S(2)}) %collective-permute-start.5) | collective-permute-done | bytes 393248 | tf_op jit(solution)/shard_map/ppermute | solution.py:678
  14.1 1.8 %collective-permute-start.7 = (bf16[192,768]{1,0:T(8,128)(2,1)S(1)}, bf16[192,768]{1,0:T(8,128)(2,1)S(1)}, u32[]{:S(2)}, u32[]{:S(2)}) collective-permute-start(bf16[192,768]{1,0:T(8,128)(2,1)S(1)} %collective-permute-done.4.refs_1_), channel_id=1, source_target_pairs={{0,8},{2,6},{8,16},{10,2},{16,24},{18,10},{24,28},{26,18},{28,20},... | collective-permute-start | bytes 884744 | tf_op jit(solution)/shard_map/ppermute | solution.py:70
  16.0 2.2 %project.1 = (bf16[256,768]{1,0:T(8,128)(2,1)S(1)}, bf16[256,512]{1,0:T(8,128)(2,1)S(1)}, bf16[128,512]{1,0:T(8,128)(2,1)S(1)}) custom-call(bf16[128,1536]{1,0:T(8,128)(2,1)S(1)} %copy-done.1, bf16[128,1536]{1,0:T(8,128)(2,1)S(1)} %collective-permute-done.5.other, f32[1,1536]{1,0:T(1,128)S(1)} %get-tuple-element.67.gain, ...), custom_call_target="tpu_custom_call" | custom-call | flops 9200000000 | bytes 64000000 | tf_op jit(solution)/shard_map/project/pallas_call | solution.py:305
  18.2 2.4 %collective-permute-start.6 = (bf16[128,512]{1,0:T(8,128)(2,1)S(1)}, bf16[128,512]{1,0:T(8,128)(2,1)S(1)}, u32[]{:S(2)}, u32[]{:S(2)}) collective-permute-start(bf16[128,512]{1,0:T(8,128)(2,1)S(1)} %get-tuple-element.71), channel_id=1, source_target_pairs={{0,2},{2,4},{4,6},{6,8},{8,10},{10,12},{12,14},{14,16},{16,18},{18... | collective-permute-start | bytes 393224 | tf_op jit(solution)/shard_map/ppermute | solution.py:696
  21.6 1.7 %collective-permute-start.9 = (bf16[192,768]{1,0:T(8,128)(2,1)S(1)}, bf16[192,768]{1,0:T(8,128)(2,1)S(1)}, u32[]{:S(2)}, u32[]{:S(2)}) collective-permute-start(bf16[192,768]{1,0:T(8,128)(2,1)S(1)} %collective-permute-done.7.refs_2_), channel_id=1, source_target_pairs={{0,8},{2,6},{8,16},{10,2},{16,24},{18,10},{24,28},{26,18},{28,20},... | collective-permute-start | bytes 884744 | tf_op jit(solution)/shard_map/ppermute | solution.py:70
  23.3 1.3 %attend_late.1.late = bf16[128,768]{1,0:T(8,128)(2,1)S(1)} custom-call(bf16[256,768]{1,0:T(8,128)(2,1)S(1)} %get-tuple-element.74.q, bf16[256,512]{1,0:T(8,128)(2,1)S(1)} %get-tuple-element.88.kv, f32[256,128]{1,0:T(8,128)S(1)} %get-tuple-element.76.past), custom_call_target="tpu_custom_call" | custom-call | flops 2300000000 | bytes 16000000 | tf_op jit(solution)/shard_map/attend_late/pallas_call | solution.py:361
  24.7 2.3 %collective-permute-start.8 = (bf16[576,512]{1,0:T(8,128)(2,1)}, bf16[576,512]{1,0:T(8,128)(2,1)}, u32[]{:S(2)}, u32[]{:S(2)}) collective-permute-start(bf16[576,512]{1,0:T(8,128)(2,1)} %collective-permute-done.3.refs_1_), channel_id=1, source_target_pairs={{0,8},{2,6},{8,16},{10,2},{16,24},{18,10},{24,28},{26,18},{28,20},... | collective-permute-start | bytes 1769480 | tf_op jit(solution)/shard_map/ppermute | solution.py:70
  27.0 1.5 %attend_early.1.early = bf16[128,768]{1,0:T(8,128)(2,1)S(1)} custom-call(bf16[256,768]{1,0:T(8,128)(2,1)S(1)} %get-tuple-element.74.q, bf16[256,512]{1,0:T(8,128)(2,1)S(1)} %get-tuple-element.88.kv, bf16[128,512]{1,0:T(8,128)(2,1)S(1)} %collective-permute-done.6.seam, f32[256,128]{1,0:T(8,128)S(1)} %get-tuple-element.76.past), custom_call_target="tpu_custom_call" | custom-call | flops 2300000000 | bytes 16000000 | tf_op jit(solution)/shard_map/attend_early/pallas_call | solution.py:373
  28.6 1.6 %collective-permute-start.12 = (bf16[96,768]{1,0:T(8,128)(2,1)S(1)}, bf16[96,768]{1,0:T(8,128)(2,1)S(1)}, u32[]{:S(2)}, u32[]{:S(2)}) collective-permute-start(bf16[96,768]{1,0:T(8,128)(2,1)S(1)} %slice.6), channel_id=1, source_target_pairs={{0,8},{2,6},{8,16},{10,2},{16,24},{18,10},{24,28},{26,18},{28,20},... | collective-permute-start | bytes 442376 | tf_op jit(solution)/shard_map/ppermute | solution.py:70
  30.2 1.4 %bundle.1 = bf16[16,144,128]{2,1,0:T(8,128)(2,1)} custom-call(bf16[512,256]{1,0:T(8,128)(2,1)S(1)} %get-tuple-element.87.send, bf16[256,512]{1,0:T(8,128)(2,1)S(1)} %get-tuple-element.88.kv, bf16[256,128]{1,0:T(8,128)(2,1)S(1)} %get-tuple-element.89.tags), custom_call_target="tpu_custom_call" | custom-call | flops 1 | bytes 1 | tf_op jit(solution)/shard_map/bundle/pallas_call | solution.py:595
  31.6 4.8 %collective-permute-done.12.refs_7_ = bf16[96,768]{1,0:T(8,128)(2,1)S(1)} collective-permute-done((bf16[96,768]{1,0:T(8,128)(2,1)S(1)}, bf16[96,768]{1,0:T(8,128)(2,1)S(1)}, u32[]{:S(2)}, u32[]{:S(2)}) %collective-permute-start.12) | collective-permute-done | bytes 147488 | tf_op jit(solution)/shard_map/ppermute | solution.py:70
  36.4 2.3 %collective-permute-start.16 = (bf16[576,512]{1,0:T(8,128)(2,1)}, bf16[576,512]{1,0:T(8,128)(2,1)S(1)}, u32[]{:S(2)}, u32[]{:S(2)}) collective-permute-start(bf16[576,512]{1,0:T(8,128)(2,1)} %collective-permute-done.8.refs_2_), channel_id=1, source_target_pairs={{0,8},{2,6},{8,16},{10,2},{16,24},{18,10},{24,28},{26,18},{28,20},... | collective-permute-start | bytes 1769480 | tf_op jit(solution)/shard_map/ppermute | solution.py:70
  38.7 1.4 %collective-permute-done.14.refs_8_ = bf16[96,768]{1,0:T(8,128)(2,1)S(1)} collective-permute-done((bf16[96,768]{1,0:T(8,128)(2,1)S(1)}, bf16[96,768]{1,0:T(8,128)(2,1)S(1)}, u32[]{:S(2)}, u32[]{:S(2)}) %collective-permute-start.14) | collective-permute-done | bytes 147488 | tf_op jit(solution)/shard_map/ppermute | solution.py:79
  40.1 1.2 %outward_send.1 = bf16[128,1536]{1,0:T(8,128)(2,1)S(1)} custom-call(bf16[128,768]{1,0:T(8,128)(2,1)S(1)} %attend_early.1.early, bf16[128,768]{1,0:T(8,128)(2,1)S(1)} %attend_late.1.late, bf16[192,768]{1,0:T(8,128)(2,1)S(1)} %get-tuple-element.62.refs_0_, bf16[192,768]{1,0:T(8,128)(2,1)S(1)} %collective-permute-done.4.refs_1_, ...), custom_call_target="tpu_custom_call" | custom-call | flops 1 | bytes 2359296 | tf_op jit(solution)/shard_map/outward_send/pallas_call | solution.py:415
  41.2 1.6 %collective-permute-start.15 = (bf16[128,1536]{1,0:T(8,128)(2,1)S(1)}, bf16[128,1536]{1,0:T(8,128)(2,1)S(1)}, u32[]{:S(2)}, u32[]{:S(2)}) collective-permute-start(bf16[128,1536]{1,0:T(8,128)(2,1)S(1)} %outward_send.1), channel_id=1, source_target_pairs={{0,1},{1,0},{2,3},{3,2},{4,5},{5,4},{6,7},{7,6},{8,9},{9,8},{10,11... | collective-permute-start | bytes 1179656 | tf_op jit(solution)/shard_map/ppermute | solution.py:717
  42.8 1.2 %outward_keep.1 = (f32[128,1536]{1,0:T(8,128)S(1)}, f32[1,1536]{1,0:T(1,128)S(1)}) custom-call(bf16[128,768]{1,0:T(8,128)(2,1)S(1)} %attend_early.1.early, bf16[128,768]{1,0:T(8,128)(2,1)S(1)} %attend_late.1.late, bf16[128,1536]{1,0:T(8,128)(2,1)S(1)} %copy-done.1, f32[1536]{0:T(1024)S(1)} %copy-done.4, bf16[192,768]{1,0:T(8,128)(2,1)S(1)} %get-tuple-element.62.refs_0_, ...), custom_call_target="tpu_custom_call" | custom-call | flops 1 | bytes 2359296 | tf_op jit(solution)/shard_map/outward_keep/pallas_call | solution.py:429
  44.0 2.6 %collective-permute-done.16.refs_3_ = bf16[576,512]{1,0:T(8,128)(2,1)S(1)} collective-permute-done((bf16[576,512]{1,0:T(8,128)(2,1)}, bf16[576,512]{1,0:T(8,128)(2,1)S(1)}, u32[]{:S(2)}, u32[]{:S(2)}) %collective-permute-start.16) | collective-permute-done | bytes 589856 | tf_op jit(solution)/shard_map/ppermute | solution.py:70
  47.3 2.3 %collective-permute-start.17 = (bf16[288,512]{1,0:T(8,128)(2,1)}, bf16[288,512]{1,0:T(8,128)(2,1)}, u32[]{:S(2)}, u32[]{:S(2)}) collective-permute-start(bf16[288,512]{1,0:T(8,128)(2,1)} %slice.7), channel_id=1, source_target_pairs={{0,8},{2,6},{8,16},{10,2},{16,24},{18,10},{24,28},{26,18},{28,20},... | collective-permute-start | bytes 884744 | tf_op jit(solution)/shard_map/ppermute | solution.py:70
  50.0 4.3 %all-to-all-start = ((bf16[16,144,128]{2,1,0:T(8,128)(2,1)}), bf16[16,144,128]{2,1,0:T(8,128)(2,1)S(1)}, u32[]{:S(2)}, u32[]{:S(2)}) async-start(bf16[16,144,128]{2,1,0:T(8,128)(2,1)} %bundle.1), calls=%async_computation | async-start | bytes 1179648 | tf_op jit(solution)/shard_map/all_to_all | solution.py:726
  54.8 1.6 %collective-permute-start.18 = (bf16[32,1536]{1,0:T(8,128)(2,1)S(1)}, bf16[32,1536]{1,0:T(8,128)(2,1)S(1)}, u32[]{:S(2)}, u32[]{:S(2)}) collective-permute-start(bf16[32,1536]{1,0:T(8,128)(2,1)S(1)} %get-tuple-element.109), channel_id=1, source_target_pairs={{0,1},{1,0},{2,3},{3,2},{4,5},{5,4},{6,7},{7,6},{8,9},{9,8},{10,11... | collective-permute-start | bytes 294920 | tf_op jit(solution)/shard_map/ppermute | solution.py:729
  56.8 3.2 %collective-permute-done.18.other = bf16[32,1536]{1,0:T(8,128)(2,1)S(1)} collective-permute-done((bf16[32,1536]{1,0:T(8,128)(2,1)S(1)}, bf16[32,1536]{1,0:T(8,128)(2,1)S(1)}, u32[]{:S(2)}, u32[]{:S(2)}) %collective-permute-start.18) | collective-permute-done | bytes 98336 | tf_op jit(solution)/shard_map/ppermute | solution.py:729
  60.0 1.8 %collective-permute-done.22.refs_8_ = bf16[288,512]{1,0:T(8,128)(2,1)S(1)} collective-permute-done((bf16[288,512]{1,0:T(8,128)(2,1)}, bf16[288,512]{1,0:T(8,128)(2,1)S(1)}, u32[]{:S(2)}, u32[]{:S(2)}) %collective-permute-start.22) | collective-permute-done | bytes 294944 | tf_op jit(solution)/shard_map/ppermute | solution.py:79
  61.8 3.2 %expert.1 = (bf16[32,1536]{1,0:T(8,128)(2,1)S(1)}, bf16[32,1536]{1,0:T(8,128)(2,1)S(1)}) custom-call(bf16[32,1536]{1,0:T(8,128)(2,1)S(1)} %get-tuple-element.111.own, bf16[32,1536]{1,0:T(8,128)(2,1)S(1)} %collective-permute-done.18.other, bf16[576,512]{1,0:T(8,128)(2,1)S(1)} %get-tuple-element.61.refs_0_, bf16[576,512]{1,0:T(8,128)(2,1)} %collective-permute-done.3.refs_1_, ...), custom_call_target="tpu_custom_call" | custom-call | flops 4600000000 | bytes 32000000 | tf_op jit(solution)/shard_map/expert/pallas_call | solution.py:530
  65.0 1.6 %collective-permute-start.23 = (bf16[32,1536]{1,0:T(8,128)(2,1)S(1)}, bf16[32,1536]{1,0:T(8,128)(2,1)S(1)}, u32[]{:S(2)}, u32[]{:S(2)}) collective-permute-start(bf16[32,1536]{1,0:T(8,128)(2,1)S(1)} %get-tuple-element.115), channel_id=1, source_target_pairs={{0,1},{1,0},{2,3},{3,2},{4,5},{5,4},{6,7},{7,6},{8,9},{9,8},{10,11... | collective-permute-start | bytes 294920 | tf_op jit(solution)/shard_map/ppermute | solution.py:736
  66.5 3.4 %collective-permute-done.23.returned = bf16[32,1536]{1,0:T(8,128)(2,1)S(1)} collective-permute-done((bf16[32,1536]{1,0:T(8,128)(2,1)S(1)}, bf16[32,1536]{1,0:T(8,128)(2,1)S(1)}, u32[]{:S(2)}, u32[]{:S(2)}) %collective-permute-start.23) | collective-permute-done | bytes 98336 | tf_op jit(solution)/shard_map/ppermute | solution.py:736
  71.0 1.6 %write.1 = bf16[2048,128]{1,0:T(8,128)(2,1)} custom-call(bf16[16,144,128]{2,1,0:T(8,128)(2,1)S(1)} %all-to-all-done.arrived, bf16[2048,128]{1,0:T(8,128)(2,1)S(1)} %bitcast.14), custom_call_target="tpu_custom_call" | custom-call | flops 1 | bytes 2097152 | tf_op jit(solution)/shard_map/write/pallas_call | solution.py:636
  (46 shorter events, 5.4 us)
Async XLA Ops:
  0.6 3.6 %collective-permute-start.2 = (bf16[96,1536]{1,0:T(8,128)(2,1)}, bf16[96,1536]{1,0:T(8,128)(2,1)S(1)}, u32[]{:S(2)}, u32[]{:S(2)}) collective-permute-start(bf16[96,1536]{1,0:T(8,128)(2,1)} %bitcast.20), channel_id=1, source_target_pairs={{0,2},{2,0},{4,6},{6,4},{8,10},{10,8},{12,14},{14,12},{16,18},{18,... | collective-permute-start | bytes 884744 | tf_op jit(solution)/shard_map/ppermute | solution.py:681
  1.1 3.1 %collective-permute-start = (bf16[96,1024]{1,0:T(8,128)(2,1)}, bf16[96,1024]{1,0:T(8,128)(2,1)S(1)}, u32[]{:S(2)}, u32[]{:S(2)}) collective-permute-start(bf16[96,1024]{1,0:T(8,128)(2,1)} %bitcast.22), channel_id=1, source_target_pairs={{0,2},{2,0},{4,6},{6,4},{8,10},{10,8},{12,14},{14,12},{16,18},{18,... | collective-permute-start | bytes 589832 | tf_op jit(solution)/shard_map/ppermute | solution.py:681
  1.2 3.0 %collective-permute-start.1 = (bf16[32,1536]{1,0:T(8,128)(2,1)}, bf16[32,1536]{1,0:T(8,128)(2,1)S(1)}, u32[]{:S(2)}, u32[]{:S(2)}) collective-permute-start(bf16[32,1536]{1,0:T(8,128)(2,1)} %bitcast.24), channel_id=1, source_target_pairs={{0,2},{2,0},{4,6},{6,4},{8,10},{10,8},{12,14},{14,12},{16,18},{18,... | collective-permute-start | bytes 294920 | tf_op jit(solution)/shard_map/ppermute | solution.py:681
  1.7 12.5 %collective-permute-start.5 = (bf16[128,1536]{1,0:T(8,128)(2,1)}, bf16[128,1536]{1,0:T(8,128)(2,1)S(1)}, u32[]{:S(2)}, u32[]{:S(2)}) collective-permute-start(bf16[128,1536]{1,0:T(8,128)(2,1)} %tokens.1), channel_id=1, source_target_pairs={{0,1},{1,0},{2,3},{3,2},{4,5},{5,4},{6,7},{7,6},{8,9},{9,8},{10,11... | collective-permute-start | bytes 1179656 | tf_op jit(solution)/shard_map/ppermute | solution.py:678
  5.4 8.8 %collective-permute-start.4 = (bf16[192,768]{1,0:T(8,128)(2,1)S(1)}, bf16[192,768]{1,0:T(8,128)(2,1)S(1)}, u32[]{:S(2)}, u32[]{:S(2)}) collective-permute-start(bf16[192,768]{1,0:T(8,128)(2,1)S(1)} %get-tuple-element.62.refs_0_), channel_id=1, source_target_pairs={{0,8},{2,6},{8,16},{10,2},{16,24},{18,10},{24,28},{26,18},{28,20},... | collective-permute-start | bytes 884744 | tf_op jit(solution)/shard_map/ppermute | solution.py:70
  7.1 17.5 %collective-permute-start.3 = (bf16[576,512]{1,0:T(8,128)(2,1)S(1)}, bf16[576,512]{1,0:T(8,128)(2,1)}, u32[]{:S(2)}, u32[]{:S(2)}) collective-permute-start(bf16[576,512]{1,0:T(8,128)(2,1)S(1)} %get-tuple-element.61.refs_0_), channel_id=1, source_target_pairs={{0,8},{2,6},{8,16},{10,2},{16,24},{18,10},{24,28},{26,18},{28,20},... | collective-permute-start | bytes 1769480 | tf_op jit(solution)/shard_map/ppermute | solution.py:70
  10.2 5.8 %copy-start.1 = (bf16[128,1536]{1,0:T(8,128)(2,1)S(1)}, bf16[128,1536]{1,0:T(8,128)(2,1)}, u32[]{:S(2)}) copy-start(bf16[128,1536]{1,0:T(8,128)(2,1)} %tokens.1) | copy-start | bytes 1179652
  10.2 5.8 %copy-start.5 = (bf16[1536,768]{1,0:T(8,128)(2,1)S(1)}, bf16[1536,768]{1,0:T(8,128)(2,1)}, u32[]{:S(2)}) copy-start(bf16[1536,768]{1,0:T(8,128)(2,1)} %w_query.1) | copy-start | bytes 7077892
  14.1 7.5 %collective-permute-start.7 = (bf16[192,768]{1,0:T(8,128)(2,1)S(1)}, bf16[192,768]{1,0:T(8,128)(2,1)S(1)}, u32[]{:S(2)}, u32[]{:S(2)}) collective-permute-start(bf16[192,768]{1,0:T(8,128)(2,1)S(1)} %collective-permute-done.4.refs_1_), channel_id=1, source_target_pairs={{0,8},{2,6},{8,16},{10,2},{16,24},{18,10},{24,28},{26,18},{28,20},... | collective-permute-start | bytes 884744 | tf_op jit(solution)/shard_map/ppermute | solution.py:70
  16.0 12.5 %collective-permute-start.10 = (bf16[192,768]{1,0:T(8,128)(2,1)S(1)}, bf16[192,768]{1,0:T(8,128)(2,1)S(1)}, u32[]{:S(2)}, u32[]{:S(2)}) collective-permute-start(bf16[192,768]{1,0:T(8,128)(2,1)S(1)} %collective-permute-done.4.refs_1_), channel_id=1, source_target_pairs={{0,2},{2,0},{4,6},{6,4},{8,10},{10,8},{12,14},{14,12},{16,18},{18,... | collective-permute-start | bytes 884744 | tf_op jit(solution)/shard_map/ppermute | solution.py:79
  18.2 6.4 %collective-permute-start.6 = (bf16[128,512]{1,0:T(8,128)(2,1)S(1)}, bf16[128,512]{1,0:T(8,128)(2,1)S(1)}, u32[]{:S(2)}, u32[]{:S(2)}) collective-permute-start(bf16[128,512]{1,0:T(8,128)(2,1)S(1)} %get-tuple-element.71), channel_id=1, source_target_pairs={{0,2},{2,4},{4,6},{6,8},{8,10},{10,12},{12,14},{14,16},{16,18},{18... | collective-permute-start | bytes 393224 | tf_op jit(solution)/shard_map/ppermute | solution.py:696
  21.6 6.8 %collective-permute-start.11 = (bf16[192,768]{1,0:T(8,128)(2,1)S(1)}, bf16[192,768]{1,0:T(8,128)(2,1)S(1)}, u32[]{:S(2)}, u32[]{:S(2)}) collective-permute-start(bf16[192,768]{1,0:T(8,128)(2,1)S(1)} %collective-permute-done.7.refs_2_), channel_id=1, source_target_pairs={{0,2},{2,0},{4,6},{6,4},{8,10},{10,8},{12,14},{14,12},{16,18},{18,... | collective-permute-start | bytes 884744 | tf_op jit(solution)/shard_map/ppermute | solution.py:79
  21.6 6.8 %collective-permute-start.9 = (bf16[192,768]{1,0:T(8,128)(2,1)S(1)}, bf16[192,768]{1,0:T(8,128)(2,1)S(1)}, u32[]{:S(2)}, u32[]{:S(2)}) collective-permute-start(bf16[192,768]{1,0:T(8,128)(2,1)S(1)} %collective-permute-done.7.refs_2_), channel_id=1, source_target_pairs={{0,8},{2,6},{8,16},{10,2},{16,24},{18,10},{24,28},{26,18},{28,20},... | collective-permute-start | bytes 884744 | tf_op jit(solution)/shard_map/ppermute | solution.py:70
  24.7 11.7 %collective-permute-start.8 = (bf16[576,512]{1,0:T(8,128)(2,1)}, bf16[576,512]{1,0:T(8,128)(2,1)}, u32[]{:S(2)}, u32[]{:S(2)}) collective-permute-start(bf16[576,512]{1,0:T(8,128)(2,1)} %collective-permute-done.3.refs_1_), channel_id=1, source_target_pairs={{0,8},{2,6},{8,16},{10,2},{16,24},{18,10},{24,28},{26,18},{28,20},... | collective-permute-start | bytes 1769480 | tf_op jit(solution)/shard_map/ppermute | solution.py:70
  28.5 1.7 %collective-permute-start.13 = (bf16[192,768]{1,0:T(8,128)(2,1)S(1)}, bf16[192,768]{1,0:T(8,128)(2,1)S(1)}, u32[]{:S(2)}, u32[]{:S(2)}) collective-permute-start(bf16[192,768]{1,0:T(8,128)(2,1)S(1)} %collective-permute-done.9.refs_3_), channel_id=1, source_target_pairs={{0,2},{2,0},{4,6},{6,4},{8,10},{10,8},{12,14},{14,12},{16,18},{18,... | collective-permute-start | bytes 884744 | tf_op jit(solution)/shard_map/ppermute | solution.py:79
  28.6 7.8 %collective-permute-start.12 = (bf16[96,768]{1,0:T(8,128)(2,1)S(1)}, bf16[96,768]{1,0:T(8,128)(2,1)S(1)}, u32[]{:S(2)}, u32[]{:S(2)}) collective-permute-start(bf16[96,768]{1,0:T(8,128)(2,1)S(1)} %slice.6), channel_id=1, source_target_pairs={{0,8},{2,6},{8,16},{10,2},{16,24},{18,10},{24,28},{26,18},{28,20},... | collective-permute-start | bytes 442376 | tf_op jit(solution)/shard_map/ppermute | solution.py:70
  31.6 11.2 %copy-start.4 = (f32[1536]{0:T(1024)S(1)}, f32[1536]{0:T(1024)}, u32[]{:S(2)}) copy-start(f32[1536]{0:T(1024)} %flat_gain.1) | copy-start | bytes 18436
  36.4 10.1 %collective-permute-start.16 = (bf16[576,512]{1,0:T(8,128)(2,1)}, bf16[576,512]{1,0:T(8,128)(2,1)S(1)}, u32[]{:S(2)}, u32[]{:S(2)}) collective-permute-start(bf16[576,512]{1,0:T(8,128)(2,1)} %collective-permute-done.8.refs_2_), channel_id=1, source_target_pairs={{0,8},{2,6},{8,16},{10,2},{16,24},{18,10},{24,28},{26,18},{28,20},... | collective-permute-start | bytes 1769480 | tf_op jit(solution)/shard_map/ppermute | solution.py:70
  38.7 1.4 %collective-permute-start.14 = (bf16[96,768]{1,0:T(8,128)(2,1)S(1)}, bf16[96,768]{1,0:T(8,128)(2,1)S(1)}, u32[]{:S(2)}, u32[]{:S(2)}) collective-permute-start(bf16[96,768]{1,0:T(8,128)(2,1)S(1)} %collective-permute-done.12.refs_7_), channel_id=1, source_target_pairs={{0,2},{2,0},{4,6},{6,4},{8,10},{10,8},{12,14},{14,12},{16,18},{18,... | collective-permute-start | bytes 442376 | tf_op jit(solution)/shard_map/ppermute | solution.py:79
  41.2 13.1 %collective-permute-start.15 = (bf16[128,1536]{1,0:T(8,128)(2,1)S(1)}, bf16[128,1536]{1,0:T(8,128)(2,1)S(1)}, u32[]{:S(2)}, u32[]{:S(2)}) collective-permute-start(bf16[128,1536]{1,0:T(8,128)(2,1)S(1)} %outward_send.1), channel_id=1, source_target_pairs={{0,1},{1,0},{2,3},{3,2},{4,5},{5,4},{6,7},{7,6},{8,9},{9,8},{10,11... | collective-permute-start | bytes 1179656 | tf_op jit(solution)/shard_map/ppermute | solution.py:717
  43.9 12.4 %copy-start.2 = (bf16[1536,40]{0,1:T(8,128)(2,1)S(1)}, bf16[1536,40]{0,1:T(8,128)(2,1)}, u32[]{:S(2)}) copy-start(bf16[1536,40]{0,1:T(8,128)(2,1)} %param.20) | copy-start | bytes 368644
  43.9 12.4 %copy-start.3 = (s32[128,8]{0,1:T(8,128)S(1)}, s32[128,8]{0,1:T(8,128)}, u32[]{:S(2)}) copy-start(s32[128,8]{0,1:T(8,128)} %param.23) | copy-start | bytes 12292
  47.3 12.7 %collective-permute-start.17 = (bf16[288,512]{1,0:T(8,128)(2,1)}, bf16[288,512]{1,0:T(8,128)(2,1)}, u32[]{:S(2)}, u32[]{:S(2)}) collective-permute-start(bf16[288,512]{1,0:T(8,128)(2,1)} %slice.7), channel_id=1, source_target_pairs={{0,8},{2,6},{8,16},{10,2},{16,24},{18,10},{24,28},{26,18},{28,20},... | collective-permute-start | bytes 884744 | tf_op jit(solution)/shard_map/ppermute | solution.py:70
  49.5 10.5 %collective-permute-start.19 = (bf16[576,512]{1,0:T(8,128)(2,1)}, bf16[576,512]{1,0:T(8,128)(2,1)}, u32[]{:S(2)}, u32[]{:S(2)}) collective-permute-start(bf16[576,512]{1,0:T(8,128)(2,1)} %collective-permute-done.3.refs_1_), channel_id=1, source_target_pairs={{0,2},{2,0},{4,6},{6,4},{8,10},{10,8},{12,14},{14,12},{16,18},{18,... | collective-permute-start | bytes 1769480 | tf_op jit(solution)/shard_map/ppermute | solution.py:79
  49.5 10.5 %collective-permute-start.20 = (bf16[576,512]{1,0:T(8,128)(2,1)}, bf16[576,512]{1,0:T(8,128)(2,1)}, u32[]{:S(2)}, u32[]{:S(2)}) collective-permute-start(bf16[576,512]{1,0:T(8,128)(2,1)} %collective-permute-done.8.refs_2_), channel_id=1, source_target_pairs={{0,2},{2,0},{4,6},{6,4},{8,10},{10,8},{12,14},{14,12},{16,18},{18,... | collective-permute-start | bytes 1769480 | tf_op jit(solution)/shard_map/ppermute | solution.py:79
  50.0 11.8 %collective-permute-start.21 = (bf16[576,512]{1,0:T(8,128)(2,1)S(1)}, bf16[576,512]{1,0:T(8,128)(2,1)}, u32[]{:S(2)}, u32[]{:S(2)}) collective-permute-start(bf16[576,512]{1,0:T(8,128)(2,1)S(1)} %collective-permute-done.16.refs_3_), channel_id=1, source_target_pairs={{0,2},{2,0},{4,6},{6,4},{8,10},{10,8},{12,14},{14,12},{16,18},{18,... | collective-permute-start | bytes 1769480 | tf_op jit(solution)/shard_map/ppermute | solution.py:79
  50.0 21.0 %all-to-all-start = ((bf16[16,144,128]{2,1,0:T(8,128)(2,1)}), bf16[16,144,128]{2,1,0:T(8,128)(2,1)S(1)}, u32[]{:S(2)}, u32[]{:S(2)}) async-start(bf16[16,144,128]{2,1,0:T(8,128)(2,1)} %bundle.1), calls=%async_computation | async-start | bytes 1179648 | tf_op jit(solution)/shard_map/all_to_all | solution.py:726
  54.8 5.2 %collective-permute-start.18 = (bf16[32,1536]{1,0:T(8,128)(2,1)S(1)}, bf16[32,1536]{1,0:T(8,128)(2,1)S(1)}, u32[]{:S(2)}, u32[]{:S(2)}) collective-permute-start(bf16[32,1536]{1,0:T(8,128)(2,1)S(1)} %get-tuple-element.109), channel_id=1, source_target_pairs={{0,1},{1,0},{2,3},{3,2},{4,5},{5,4},{6,7},{7,6},{8,9},{9,8},{10,11... | collective-permute-start | bytes 294920 | tf_op jit(solution)/shard_map/ppermute | solution.py:729
  60.0 11.0 %copy-start = (bf16[512,4,128]{2,1,0:T(4,128)(2,1)S(1)}, bf16[512,4,128]{2,1,0:T(4,128)(2,1)}, u32[]{:S(2)}) copy-start(bf16[512,4,128]{2,1,0:T(4,128)(2,1)} %param.25) | copy-start | bytes 1572868
  60.0 1.8 %collective-permute-start.22 = (bf16[288,512]{1,0:T(8,128)(2,1)}, bf16[288,512]{1,0:T(8,128)(2,1)S(1)}, u32[]{:S(2)}, u32[]{:S(2)}) collective-permute-start(bf16[288,512]{1,0:T(8,128)(2,1)} %collective-permute-done.17.refs_7_), channel_id=1, source_target_pairs={{0,2},{2,0},{4,6},{6,4},{8,10},{10,8},{12,14},{14,12},{16,18},{18,... | collective-permute-start | bytes 884744 | tf_op jit(solution)/shard_map/ppermute | solution.py:79
  65.0 4.9 %collective-permute-start.23 = (bf16[32,1536]{1,0:T(8,128)(2,1)S(1)}, bf16[32,1536]{1,0:T(8,128)(2,1)S(1)}, u32[]{:S(2)}, u32[]{:S(2)}) collective-permute-start(bf16[32,1536]{1,0:T(8,128)(2,1)S(1)} %get-tuple-element.115), channel_id=1, source_target_pairs={{0,1},{1,0},{2,3},{3,2},{4,5},{5,4},{6,7},{7,6},{8,9},{9,8},{10,11... | collective-permute-start | bytes 294920 | tf_op jit(solution)/shard_map/ppermute | solution.py:736

commit v21 on v20

--- a/solution.py
+++ b/solution.py
@@ -538,7 +538,7 @@
             pltpu.VMEM((groups * down_rows, model), bf16),
         ],
         compiler_params=PARAMS,
-        cost_estimate=takes(4.0),
+        cost_estimate=takes(2.6),
         name="expert",
     )(own, other, *parts)
 
@@ -728,8 +728,9 @@
     residual, moe_in, sent_rows = route(mine, arrived, late_gain, place)
     landed = swap(sent_rows)
     gates, own_rows, spread = gate(moe_in, router.T, expert_ids.T, place)
-    landed, own_rows = expert_ring.pin(landed, own_rows)
+    own_rows = expert_ring.pin(own_rows)
     expert_ring.share()
+    landed, own_rows = together((landed, own_rows))
     own_made, back = expert(
         groups, own_rows, landed, expert_ring.parts(), up_rows, down_rows
     )

time: 72.9 us -> 79.2 us (1.086)
  the two profiles are of different devices: /device:TPU:0 before, /device:TPU:12 now
where the time goes in v21:
time: 79.2 us; the launch traced here: 78.8 us
  waiting for transfers between devices  35.2 us (44%)
  starting transfers between devices  20.6 us (26%)
  Pallas kernels  17.4 us (22%)
  local copies, waits for them, and re-layouts  4.68 us (6%)
  between operations  0.9 us (1%)
    ppermute x8, waiting for transfers between devices, step(): self.mine.append(self.across(held))  16.2 us
    all_to_all x1, starting transfers between devices, two_lane_shards(): lax.all_to_all(outgoing, 'grp', split_axis=0, concat_axis=0, tiled=True)  6.22 us
    ppermute x1, waiting for transfers between devices, two_lane_shards(): arrived = swap(sent)  5.01 us
    ppermute x1, waiting for transfers between devices, two_lane_shards(): other_tokens = swap(tokens)  4.67 us
    ppermute x8, starting transfers between devices, step(): self.mine.append(self.across(held))  3.81 us
    ppermute x1, waiting for transfers between devices, two_lane_shards(): landed = swap(sent_rows)  3.72 us
    unnamed x25, local copies, waits for them, and re-layouts  3.63 us
    ppermute x1, waiting for transfers between devices, two_lane_shards(): returned = swap(back)  3.13 us
  transfers between devices with their start and end apart: 25, of which 12 were waited for; matrix products, arithmetic and copies ran while one was open for 4% of the time, Pallas kernels for 20%

profile of v21, /device:TPU:12, one launch (start us, length us, event | category | flops | bytes accessed | tf_op | source)
XLA Modules:
  0.0 78.8 jit_solution(14349228299984890712)
XLA Ops:
  1.3 1.5 %collective-permute-start.5 = (bf16[128,1536]{1,0:T(8,128)(2,1)}, bf16[128,1536]{1,0:T(8,128)(2,1)S(1)}, u32[]{:S(2)}, u32[]{:S(2)}) collective-permute-start(bf16[128,1536]{1,0:T(8,128)(2,1)} %tokens.1), channel_id=1, source_target_pairs={{0,1},{1,0},{2,3},{3,2},{4,5},{5,4},{6,7},{7,6},{8,9},{9,8},{10,11... | collective-permute-start | bytes 1179656 | tf_op jit(solution)/shard_map/ppermute | solution.py:678
  2.9 1.1 %pack.1 = (bf16[576,512]{1,0:T(8,128)(2,1)S(1)}, bf16[192,768]{1,0:T(8,128)(2,1)S(1)}) custom-call(bf16[96,1024]{1,0:T(8,128)(2,1)} %bitcast.23, bf16[32,1536]{1,0:T(8,128)(2,1)} %bitcast.25, bf16[96,1536]{1,0:T(8,128)(2,1)} %bitcast.21, bf16[96,1024]{1,0:T(8,128)(2,1)S(1)} %collective-permute-done.refs_3_, ...), custom_call_target="tpu_custom_call" | custom-call | flops 1 | bytes 1 | tf_op jit(solution)/shard_map/pack/pallas_call | solution.py:159
  5.0 1.5 %prepare.1 = (f32[256,128]{1,0:T(8,128)S(1)}, f32[256,128]{1,0:T(8,128)S(1)}, f32[256,128]{1,0:T(8,128)S(1)}, bf16[64,128]{1,0:T(8,128)(2,1)S(1)}, bf16[512,256]...) custom-call(s32[1,256]{1,0:T(1,128)} %bitcast.26, s32[1,256]{1,0:T(1,128)} %bitcast.27, ...), custom_call_target="tpu_custom_call" | custom-call | flops 1 | bytes 1 | tf_op jit(solution)/shard_map/prepare/pallas_call | solution.py:255
  6.4 1.8 %copy.17 = bf16[192,8,4,128]{3,1,2,0:T(8,128)(2,1)S(1)} copy(bf16[192,8,4,128]{3,2,1,0:T(4,128)(2,1)} %bitcast.18) | data formatting | bytes 3145728
  8.3 4.7 %collective-permute-done.5.other = bf16[128,1536]{1,0:T(8,128)(2,1)S(1)} collective-permute-done((bf16[128,1536]{1,0:T(8,128)(2,1)}, bf16[128,1536]{1,0:T(8,128)(2,1)S(1)}, u32[]{:S(2)}, u32[]{:S(2)}) %collective-permute-start.5) | collective-permute-done | bytes 393248 | tf_op jit(solution)/shard_map/ppermute | solution.py:678
  13.9 2.2 %project.1 = (bf16[256,768]{1,0:T(8,128)(2,1)S(1)}, bf16[256,512]{1,0:T(8,128)(2,1)S(1)}, bf16[128,512]{1,0:T(8,128)(2,1)S(1)}) custom-call(bf16[128,1536]{1,0:T(8,128)(2,1)S(1)} %copy-done.1, bf16[128,1536]{1,0:T(8,128)(2,1)S(1)} %collective-permute-done.5.other, f32[1,1536]{1,0:T(1,128)S(1)} %get-tuple-element.68.gain, ...), custom_call_target="tpu_custom_call" | custom-call | flops 9200000000 | bytes 64000000 | tf_op jit(solution)/shard_map/project/pallas_call | solution.py:305
  16.1 1.9 %collective-permute-start.6 = (bf16[128,512]{1,0:T(8,128)(2,1)S(1)}, bf16[128,512]{1,0:T(8,128)(2,1)S(1)}, u32[]{:S(2)}, u32[]{:S(2)}) collective-permute-start(bf16[128,512]{1,0:T(8,128)(2,1)S(1)} %get-tuple-element.72), channel_id=1, source_target_pairs={{0,2},{2,4},{4,6},{6,8},{8,10},{10,12},{12,14},{14,16},{16,18},{18... | collective-permute-start | bytes 393224 | tf_op jit(solution)/shard_map/ppermute | solution.py:696
  18.1 2.2 %collective-permute-done.7.refs_2_ = bf16[192,768]{1,0:T(8,128)(2,1)S(1)} collective-permute-done((bf16[192,768]{1,0:T(8,128)(2,1)S(1)}, bf16[192,768]{1,0:T(8,128)(2,1)S(1)}, u32[]{:S(2)}, u32[]{:S(2)}) %collective-permute-start.7) | collective-permute-done | bytes 294944 | tf_op jit(solution)/shard_map/ppermute | solution.py:70
  20.9 1.3 %attend_late.1.late = bf16[128,768]{1,0:T(8,128)(2,1)S(1)} custom-call(bf16[256,768]{1,0:T(8,128)(2,1)S(1)} %get-tuple-element.75.q, bf16[256,512]{1,0:T(8,128)(2,1)S(1)} %get-tuple-element.89.kv, f32[256,128]{1,0:T(8,128)S(1)} %get-tuple-element.77.past), custom_call_target="tpu_custom_call" | custom-call | flops 2300000000 | bytes 16000000 | tf_op jit(solution)/shard_map/attend_late/pallas_call | solution.py:361
  22.9 1.5 %attend_early.1.early = bf16[128,768]{1,0:T(8,128)(2,1)S(1)} custom-call(bf16[256,768]{1,0:T(8,128)(2,1)S(1)} %get-tuple-element.75.q, bf16[256,512]{1,0:T(8,128)(2,1)S(1)} %get-tuple-element.89.kv, bf16[128,512]{1,0:T(8,128)(2,1)S(1)} %collective-permute-done.6.seam, f32[256,128]{1,0:T(8,128)S(1)} %get-tuple-element.77.past), custom_call_target="tpu_custom_call" | custom-call | flops 2300000000 | bytes 16000000 | tf_op jit(solution)/shard_map/attend_early/pallas_call | solution.py:373
  24.4 2.8 %collective-permute-done.9.refs_3_ = bf16[192,768]{1,0:T(8,128)(2,1)S(1)} collective-permute-done((bf16[192,768]{1,0:T(8,128)(2,1)S(1)}, bf16[192,768]{1,0:T(8,128)(2,1)S(1)}, u32[]{:S(2)}, u32[]{:S(2)}) %collective-permute-start.9) | collective-permute-done | bytes 294944 | tf_op jit(solution)/shard_map/ppermute | solution.py:70
  27.7 1.1 %collective-permute-done.13.refs_6_ = bf16[192,768]{1,0:T(8,128)(2,1)S(1)} collective-permute-done((bf16[192,768]{1,0:T(8,128)(2,1)S(1)}, bf16[192,768]{1,0:T(8,128)(2,1)S(1)}, u32[]{:S(2)}, u32[]{:S(2)}) %collective-permute-start.13) | collective-permute-done | bytes 294944 | tf_op jit(solution)/shard_map/ppermute | solution.py:79
  28.7 1.4 %bundle.1 = bf16[16,144,128]{2,1,0:T(8,128)(2,1)} custom-call(bf16[512,256]{1,0:T(8,128)(2,1)S(1)} %get-tuple-element.88.send, bf16[256,512]{1,0:T(8,128)(2,1)S(1)} %get-tuple-element.89.kv, bf16[256,128]{1,0:T(8,128)(2,1)S(1)} %get-tuple-element.90.tags), custom_call_target="tpu_custom_call" | custom-call | flops 1 | bytes 1 | tf_op jit(solution)/shard_map/bundle/pallas_call | solution.py:595
  30.1 4.9 %collective-permute-done.12.refs_7_ = bf16[96,768]{1,0:T(8,128)(2,1)S(1)} collective-permute-done((bf16[96,768]{1,0:T(8,128)(2,1)S(1)}, bf16[96,768]{1,0:T(8,128)(2,1)S(1)}, u32[]{:S(2)}, u32[]{:S(2)}) %collective-permute-start.12) | collective-permute-done | bytes 147488 | tf_op jit(solution)/shard_map/ppermute | solution.py:70
  35.9 1.0 %collective-permute-done.14.refs_8_ = bf16[96,768]{1,0:T(8,128)(2,1)S(1)} collective-permute-done((bf16[96,768]{1,0:T(8,128)(2,1)S(1)}, bf16[96,768]{1,0:T(8,128)(2,1)S(1)}, u32[]{:S(2)}, u32[]{:S(2)}) %collective-permute-start.14) | collective-permute-done | bytes 147488 | tf_op jit(solution)/shard_map/ppermute | solution.py:79
  36.9 1.1 %outward_send.1 = bf16[128,1536]{1,0:T(8,128)(2,1)S(1)} custom-call(bf16[128,768]{1,0:T(8,128)(2,1)S(1)} %attend_early.1.early, bf16[128,768]{1,0:T(8,128)(2,1)S(1)} %attend_late.1.late, bf16[192,768]{1,0:T(8,128)(2,1)S(1)} %get-tuple-element.63.refs_0_, bf16[192,768]{1,0:T(8,128)(2,1)S(1)} %collective-permute-done.4.refs_1_, ...), custom_call_target="tpu_custom_call" | custom-call | flops 1 | bytes 2359296 | tf_op jit(solution)/shard_map/outward_send/pallas_call | solution.py:415
  38.1 0.7 copy-done.3
  38.8 6.2 %all-to-all-start = ((bf16[16,144,128]{2,1,0:T(8,128)(2,1)}), bf16[16,144,128]{2,1,0:T(8,128)(2,1)S(1)}, u32[]{:S(2)}, u32[]{:S(2)}) async-start(bf16[16,144,128]{2,1,0:T(8,128)(2,1)} %bundle.1), calls=%async_computation | async-start | bytes 1179648 | tf_op jit(solution)/shard_map/all_to_all | solution.py:726
  45.0 1.5 %collective-permute-start.15 = (bf16[128,1536]{1,0:T(8,128)(2,1)}, bf16[128,1536]{1,0:T(8,128)(2,1)S(1)}, u32[]{:S(2)}, u32[]{:S(2)}) collective-permute-start(bf16[128,1536]{1,0:T(8,128)(2,1)} %copy-done.3), channel_id=1, source_target_pairs={{0,1},{1,0},{2,3},{3,2},{4,5},{5,4},{6,7},{7,6},{8,9},{9,8},{10,11... | collective-permute-start | bytes 1179656 | tf_op jit(solution)/shard_map/ppermute | solution.py:717
  46.5 1.0 %copy-done.2 = bf16[128,1536]{1,0:T(8,128)(2,1)S(1)} copy-done((bf16[128,1536]{1,0:T(8,128)(2,1)S(1)}, bf16[128,1536]{1,0:T(8,128)(2,1)}, u32[]{:S(2)}) %copy-start.2) | copy-done | bytes 393240
  47.5 1.1 %outward_keep.1 = (f32[128,1536]{1,0:T(8,128)S(1)}, f32[1,1536]{1,0:T(1,128)S(1)}) custom-call(bf16[128,768]{1,0:T(8,128)(2,1)S(1)} %attend_early.1.early, bf16[128,768]{1,0:T(8,128)(2,1)S(1)} %attend_late.1.late, bf16[128,1536]{1,0:T(8,128)(2,1)S(1)} %copy-done.2, f32[1536]{0:T(1024)S(1)} %copy-done.6, bf16[192,768]{1,0:T(8,128)(2,1)S(1)} %get-tuple-element.63.refs_0_, ...), custom_call_target="tpu_custom_call" | custom-call | flops 1 | bytes 2359296 | tf_op jit(solution)/shard_map/outward_keep/pallas_call | solution.py:429
  48.7 1.0 %slice.7 = bf16[288,512]{1,0:T(8,128)(2,1)S(1)} slice(bf16[576,512]{1,0:T(8,128)(2,1)} %collective-permute-done.16.refs_3_), slice={[0:288], [0:512]} | slice | bytes 589824 | tf_op jit(solution)/shard_map/slice | solution.py:69
  49.8 0.6 collective-permute-start.18
  51.4 5.0 %collective-permute-done.15.arrived = bf16[128,1536]{1,0:T(8,128)(2,1)S(1)} collective-permute-done((bf16[128,1536]{1,0:T(8,128)(2,1)}, bf16[128,1536]{1,0:T(8,128)(2,1)S(1)}, u32[]{:S(2)}, u32[]{:S(2)}) %collective-permute-start.15) | collective-permute-done | bytes 393248 | tf_op jit(solution)/shard_map/ppermute | solution.py:717
  57.3 6.3 %collective-permute-done.18.refs_7_ = bf16[288,512]{1,0:T(8,128)(2,1)S(1)} collective-permute-done((bf16[288,512]{1,0:T(8,128)(2,1)S(1)}, bf16[288,512]{1,0:T(8,128)(2,1)S(1)}, u32[]{:S(2)}, u32[]{:S(2)}) %collective-permute-start.18) | collective-permute-done | bytes 294944 | tf_op jit(solution)/shard_map/ppermute | solution.py:70
  63.6 1.5 %collective-permute-start.17 = (bf16[32,1536]{1,0:T(8,128)(2,1)S(1)}, bf16[32,1536]{1,0:T(8,128)(2,1)S(1)}, u32[]{:S(2)}, u32[]{:S(2)}) collective-permute-start(bf16[32,1536]{1,0:T(8,128)(2,1)S(1)} %get-tuple-element.109), channel_id=1, source_target_pairs={{0,1},{1,0},{2,3},{3,2},{4,5},{5,4},{6,7},{7,6},{8,9},{9,8},{10,11... | collective-permute-start | bytes 294920 | tf_op jit(solution)/shard_map/ppermute | solution.py:729
  65.1 3.7 %collective-permute-done.17.other = bf16[32,1536]{1,0:T(8,128)(2,1)S(1)} collective-permute-done((bf16[32,1536]{1,0:T(8,128)(2,1)S(1)}, bf16[32,1536]{1,0:T(8,128)(2,1)S(1)}, u32[]{:S(2)}, u32[]{:S(2)}) %collective-permute-start.17) | collective-permute-done | bytes 98336 | tf_op jit(solution)/shard_map/ppermute | solution.py:729
  68.8 2.6 %expert.1 = (bf16[32,1536]{1,0:T(8,128)(2,1)S(1)}, bf16[32,1536]{1,0:T(8,128)(2,1)S(1)}) custom-call(bf16[32,1536]{1,0:T(8,128)(2,1)S(1)} %get-tuple-element.113.own, bf16[32,1536]{1,0:T(8,128)(2,1)S(1)} %collective-permute-done.17.other, bf16[576,512]{1,0:T(8,128)(2,1)S(1)} %copy-done.9, bf16[576,512]{1,0:T(8,128)(2,1)S(1)} %copy-done.11, ...), custom_call_target="tpu_custom_call" | custom-call | flops 2990000128 | bytes 20800000 | tf_op jit(solution)/shard_map/expert/pallas_call | solution.py:530
  71.4 1.6 %collective-permute-start.23 = (bf16[32,1536]{1,0:T(8,128)(2,1)S(1)}, bf16[32,1536]{1,0:T(8,128)(2,1)S(1)}, u32[]{:S(2)}, u32[]{:S(2)}) collective-permute-start(bf16[32,1536]{1,0:T(8,128)(2,1)S(1)} %get-tuple-element.117), channel_id=1, source_target_pairs={{0,1},{1,0},{2,3},{3,2},{4,5},{5,4},{6,7},{7,6},{8,9},{9,8},{10,11... | collective-permute-start | bytes 294920 | tf_op jit(solution)/shard_map/ppermute | solution.py:737
  73.0 3.1 %collective-permute-done.23.returned = bf16[32,1536]{1,0:T(8,128)(2,1)S(1)} collective-permute-done((bf16[32,1536]{1,0:T(8,128)(2,1)S(1)}, bf16[32,1536]{1,0:T(8,128)(2,1)S(1)}, u32[]{:S(2)}, u32[]{:S(2)}) %collective-permute-start.23) | collective-permute-done | bytes 98336 | tf_op jit(solution)/shard_map/ppermute | solution.py:737
  76.1 1.1 %combine.1 = bf16[128,1536]{1,0:T(8,128)(2,1)} custom-call(bf16[128,1536]{1,0:T(8,128)(2,1)S(1)} %get-tuple-element.105.residual, f32[128,40]{1,0:T(8,128)S(1)} %get-tuple-element.107.gates, bf16[128,64]{1,0:T(8,128)(2,1)S(1)} %get-tuple-element.108.spread, bf16[32,1536]{1,0:T(8,128)(2,1)S(1)} %get-tuple-element.116.own, ...), custom_call_target="tpu_custom_call" | custom-call | flops 1 | bytes 1179648 | tf_op jit(solution)/shard_map/combine/pallas_call | solution.py:562
  77.3 1.5 %write.1 = bf16[2048,128]{1,0:T(8,128)(2,1)} custom-call(bf16[16,144,128]{2,1,0:T(8,128)(2,1)S(1)} %all-to-all-done.arrived, bf16[2048,128]{1,0:T(8,128)(2,1)S(1)} %bitcast.14), custom_call_target="tpu_custom_call" | custom-call | flops 1 | bytes 2097152 | tf_op jit(solution)/shard_map/write/pallas_call | solution.py:636
  (58 shorter events, 7.2 us)
Async XLA Ops:
  0.6 2.3 %collective-permute-start.2 = (bf16[96,1536]{1,0:T(8,128)(2,1)}, bf16[96,1536]{1,0:T(8,128)(2,1)S(1)}, u32[]{:S(2)}, u32[]{:S(2)}) collective-permute-start(bf16[96,1536]{1,0:T(8,128)(2,1)} %bitcast.20), channel_id=1, source_target_pairs={{0,2},{2,0},{4,6},{6,4},{8,10},{10,8},{12,14},{14,12},{16,18},{18,... | collective-permute-start | bytes 884744 | tf_op jit(solution)/shard_map/ppermute | solution.py:681
  0.7 2.2 %collective-permute-start = (bf16[96,1024]{1,0:T(8,128)(2,1)}, bf16[96,1024]{1,0:T(8,128)(2,1)S(1)}, u32[]{:S(2)}, u32[]{:S(2)}) collective-permute-start(bf16[96,1024]{1,0:T(8,128)(2,1)} %bitcast.22), channel_id=1, source_target_pairs={{0,2},{2,0},{4,6},{6,4},{8,10},{10,8},{12,14},{14,12},{16,18},{18,... | collective-permute-start | bytes 589832 | tf_op jit(solution)/shard_map/ppermute | solution.py:681
  1.2 1.7 %collective-permute-start.1 = (bf16[32,1536]{1,0:T(8,128)(2,1)}, bf16[32,1536]{1,0:T(8,128)(2,1)S(1)}, u32[]{:S(2)}, u32[]{:S(2)}) collective-permute-start(bf16[32,1536]{1,0:T(8,128)(2,1)} %bitcast.24), channel_id=1, source_target_pairs={{0,2},{2,0},{4,6},{6,4},{8,10},{10,8},{12,14},{14,12},{16,18},{18,... | collective-permute-start | bytes 294920 | tf_op jit(solution)/shard_map/ppermute | solution.py:681
  1.3 11.7 %collective-permute-start.5 = (bf16[128,1536]{1,0:T(8,128)(2,1)}, bf16[128,1536]{1,0:T(8,128)(2,1)S(1)}, u32[]{:S(2)}, u32[]{:S(2)}) collective-permute-start(bf16[128,1536]{1,0:T(8,128)(2,1)} %tokens.1), channel_id=1, source_target_pairs={{0,1},{1,0},{2,3},{3,2},{4,5},{5,4},{6,7},{7,6},{8,9},{9,8},{10,11... | collective-permute-start | bytes 1179656 | tf_op jit(solution)/shard_map/ppermute | solution.py:678
  4.1 8.9 %collective-permute-start.4 = (bf16[192,768]{1,0:T(8,128)(2,1)S(1)}, bf16[192,768]{1,0:T(8,128)(2,1)S(1)}, u32[]{:S(2)}, u32[]{:S(2)}) collective-permute-start(bf16[192,768]{1,0:T(8,128)(2,1)S(1)} %get-tuple-element.63.refs_0_), channel_id=1, source_target_pairs={{0,8},{2,6},{8,16},{10,2},{16,24},{18,10},{24,28},{26,18},{28,20},... | collective-permute-start | bytes 884744 | tf_op jit(solution)/shard_map/ppermute | solution.py:70
  4.6 17.9 %collective-permute-start.3 = (bf16[576,512]{1,0:T(8,128)(2,1)S(1)}, bf16[576,512]{1,0:T(8,128)(2,1)S(1)}, u32[]{:S(2)}, u32[]{:S(2)}) collective-permute-start(bf16[576,512]{1,0:T(8,128)(2,1)S(1)} %get-tuple-element.62.refs_0_), channel_id=1, source_target_pairs={{0,8},{2,6},{8,16},{10,2},{16,24},{18,10},{24,28},{26,18},{28,20},... | collective-permute-start | bytes 1769480 | tf_op jit(solution)/shard_map/ppermute | solution.py:70
  6.4 7.5 %copy-start.1 = (bf16[128,1536]{1,0:T(8,128)(2,1)S(1)}, bf16[128,1536]{1,0:T(8,128)(2,1)}, u32[]{:S(2)}) copy-start(bf16[128,1536]{1,0:T(8,128)(2,1)} %tokens.1) | copy-start | bytes 1179652
  6.4 7.5 %copy-start.7 = (bf16[1536,768]{1,0:T(8,128)(2,1)S(1)}, bf16[1536,768]{1,0:T(8,128)(2,1)}, u32[]{:S(2)}) copy-start(bf16[1536,768]{1,0:T(8,128)(2,1)} %w_query.1) | copy-start | bytes 7077892
  13.0 7.4 %collective-permute-start.7 = (bf16[192,768]{1,0:T(8,128)(2,1)S(1)}, bf16[192,768]{1,0:T(8,128)(2,1)S(1)}, u32[]{:S(2)}, u32[]{:S(2)}) collective-permute-start(bf16[192,768]{1,0:T(8,128)(2,1)S(1)} %collective-permute-done.4.refs_1_), channel_id=1, source_target_pairs={{0,8},{2,6},{8,16},{10,2},{16,24},{18,10},{24,28},{26,18},{28,20},... | collective-permute-start | bytes 884744 | tf_op jit(solution)/shard_map/ppermute | solution.py:70
  13.4 11.0 %collective-permute-start.10 = (bf16[192,768]{1,0:T(8,128)(2,1)S(1)}, bf16[192,768]{1,0:T(8,128)(2,1)S(1)}, u32[]{:S(2)}, u32[]{:S(2)}) collective-permute-start(bf16[192,768]{1,0:T(8,128)(2,1)S(1)} %collective-permute-done.4.refs_1_), channel_id=1, source_target_pairs={{0,2},{2,0},{4,6},{6,4},{8,10},{10,8},{12,14},{14,12},{16,18},{18,... | collective-permute-start | bytes 884744 | tf_op jit(solution)/shard_map/ppermute | solution.py:79
  16.1 6.3 %collective-permute-start.6 = (bf16[128,512]{1,0:T(8,128)(2,1)S(1)}, bf16[128,512]{1,0:T(8,128)(2,1)S(1)}, u32[]{:S(2)}, u32[]{:S(2)}) collective-permute-start(bf16[128,512]{1,0:T(8,128)(2,1)S(1)} %get-tuple-element.72), channel_id=1, source_target_pairs={{0,2},{2,4},{4,6},{6,8},{8,10},{10,12},{12,14},{14,16},{16,18},{18... | collective-permute-start | bytes 393224 | tf_op jit(solution)/shard_map/ppermute | solution.py:696
  20.3 4.1 %collective-permute-start.11 = (bf16[192,768]{1,0:T(8,128)(2,1)S(1)}, bf16[192,768]{1,0:T(8,128)(2,1)S(1)}, u32[]{:S(2)}, u32[]{:S(2)}) collective-permute-start(bf16[192,768]{1,0:T(8,128)(2,1)S(1)} %collective-permute-done.7.refs_2_), channel_id=1, source_target_pairs={{0,2},{2,0},{4,6},{6,4},{8,10},{10,8},{12,14},{14,12},{16,18},{18,... | collective-permute-start | bytes 884744 | tf_op jit(solution)/shard_map/ppermute | solution.py:79
  20.4 6.7 %collective-permute-start.9 = (bf16[192,768]{1,0:T(8,128)(2,1)S(1)}, bf16[192,768]{1,0:T(8,128)(2,1)S(1)}, u32[]{:S(2)}, u32[]{:S(2)}) collective-permute-start(bf16[192,768]{1,0:T(8,128)(2,1)S(1)} %collective-permute-done.7.refs_2_), channel_id=1, source_target_pairs={{0,8},{2,6},{8,16},{10,2},{16,24},{18,10},{24,28},{26,18},{28,20},... | collective-permute-start | bytes 884744 | tf_op jit(solution)/shard_map/ppermute | solution.py:70
  22.4 12.6 %collective-permute-start.8 = (bf16[576,512]{1,0:T(8,128)(2,1)S(1)}, bf16[576,512]{1,0:T(8,128)(2,1)}, u32[]{:S(2)}, u32[]{:S(2)}) collective-permute-start(bf16[576,512]{1,0:T(8,128)(2,1)S(1)} %collective-permute-done.3.refs_1_), channel_id=1, source_target_pairs={{0,8},{2,6},{8,16},{10,2},{16,24},{18,10},{24,28},{26,18},{28,20},... | collective-permute-start | bytes 1769480 | tf_op jit(solution)/shard_map/ppermute | solution.py:70
  27.1 1.6 %collective-permute-start.13 = (bf16[192,768]{1,0:T(8,128)(2,1)S(1)}, bf16[192,768]{1,0:T(8,128)(2,1)S(1)}, u32[]{:S(2)}, u32[]{:S(2)}) collective-permute-start(bf16[192,768]{1,0:T(8,128)(2,1)S(1)} %collective-permute-done.9.refs_3_), channel_id=1, source_target_pairs={{0,2},{2,0},{4,6},{6,4},{8,10},{10,8},{12,14},{14,12},{16,18},{18,... | collective-permute-start | bytes 884744 | tf_op jit(solution)/shard_map/ppermute | solution.py:79
  27.2 7.9 %collective-permute-start.12 = (bf16[96,768]{1,0:T(8,128)(2,1)S(1)}, bf16[96,768]{1,0:T(8,128)(2,1)S(1)}, u32[]{:S(2)}, u32[]{:S(2)}) collective-permute-start(bf16[96,768]{1,0:T(8,128)(2,1)S(1)} %slice.6), channel_id=1, source_target_pairs={{0,8},{2,6},{8,16},{10,2},{16,24},{18,10},{24,28},{26,18},{28,20},... | collective-permute-start | bytes 442376 | tf_op jit(solution)/shard_map/ppermute | solution.py:70
  30.1 16.4 %copy-start.6 = (f32[1536]{0:T(1024)S(1)}, f32[1536]{0:T(1024)}, u32[]{:S(2)}) copy-start(f32[1536]{0:T(1024)} %flat_gain.1) | copy-start | bytes 18436
  35.0 13.7 %collective-permute-start.16 = (bf16[576,512]{1,0:T(8,128)(2,1)}, bf16[576,512]{1,0:T(8,128)(2,1)}, u32[]{:S(2)}, u32[]{:S(2)}) collective-permute-start(bf16[576,512]{1,0:T(8,128)(2,1)} %collective-permute-done.8.refs_2_), channel_id=1, source_target_pairs={{0,8},{2,6},{8,16},{10,2},{16,24},{18,10},{24,28},{26,18},{28,20},... | collective-permute-start | bytes 1769480 | tf_op jit(solution)/shard_map/ppermute | solution.py:70
  35.5 1.4 %collective-permute-start.14 = (bf16[96,768]{1,0:T(8,128)(2,1)S(1)}, bf16[96,768]{1,0:T(8,128)(2,1)S(1)}, u32[]{:S(2)}, u32[]{:S(2)}) collective-permute-start(bf16[96,768]{1,0:T(8,128)(2,1)S(1)} %collective-permute-done.12.refs_7_), channel_id=1, source_target_pairs={{0,2},{2,0},{4,6},{6,4},{8,10},{10,8},{12,14},{14,12},{16,18},{18,... | collective-permute-start | bytes 442376 | tf_op jit(solution)/shard_map/ppermute | solution.py:79
  38.8 38.4 %all-to-all-start = ((bf16[16,144,128]{2,1,0:T(8,128)(2,1)}), bf16[16,144,128]{2,1,0:T(8,128)(2,1)S(1)}, u32[]{:S(2)}, u32[]{:S(2)}) async-start(bf16[16,144,128]{2,1,0:T(8,128)(2,1)} %bundle.1), calls=%async_computation | async-start | bytes 1179648 | tf_op jit(solution)/shard_map/all_to_all | solution.py:726
  45.0 11.4 %collective-permute-start.15 = (bf16[128,1536]{1,0:T(8,128)(2,1)}, bf16[128,1536]{1,0:T(8,128)(2,1)S(1)}, u32[]{:S(2)}, u32[]{:S(2)}) collective-permute-start(bf16[128,1536]{1,0:T(8,128)(2,1)} %copy-done.3), channel_id=1, source_target_pairs={{0,1},{1,0},{2,3},{3,2},{4,5},{5,4},{6,7},{7,6},{8,9},{9,8},{10,11... | collective-permute-start | bytes 1179656 | tf_op jit(solution)/shard_map/ppermute | solution.py:717
  48.7 8.2 %copy-start.4 = (bf16[1536,40]{0,1:T(8,128)(2,1)S(1)}, bf16[1536,40]{0,1:T(8,128)(2,1)}, u32[]{:S(2)}) copy-start(bf16[1536,40]{0,1:T(8,128)(2,1)} %param.20) | copy-start | bytes 368644
  48.7 8.2 %copy-start.5 = (s32[128,8]{0,1:T(8,128)S(1)}, s32[128,8]{0,1:T(8,128)}, u32[]{:S(2)}) copy-start(s32[128,8]{0,1:T(8,128)} %param.23) | copy-start | bytes 12292
  48.7 20.1 %copy-start.9 = (bf16[576,512]{1,0:T(8,128)(2,1)S(1)}, bf16[576,512]{1,0:T(8,128)(2,1)}, u32[]{:S(2)}) copy-start(bf16[576,512]{1,0:T(8,128)(2,1)} %copy-done.8) | copy-start | bytes 1769476
  49.8 13.8 %collective-permute-start.18 = (bf16[288,512]{1,0:T(8,128)(2,1)S(1)}, bf16[288,512]{1,0:T(8,128)(2,1)S(1)}, u32[]{:S(2)}, u32[]{:S(2)}) collective-permute-start(bf16[288,512]{1,0:T(8,128)(2,1)S(1)} %slice.7), channel_id=1, source_target_pairs={{0,8},{2,6},{8,16},{10,2},{16,24},{18,10},{24,28},{26,18},{28,20},... | collective-permute-start | bytes 884744 | tf_op jit(solution)/shard_map/ppermute | solution.py:70
  50.4 18.4 %collective-permute-start.19 = (bf16[576,512]{1,0:T(8,128)(2,1)S(1)}, bf16[576,512]{1,0:T(8,128)(2,1)S(1)}, u32[]{:S(2)}, u32[]{:S(2)}) collective-permute-start(bf16[576,512]{1,0:T(8,128)(2,1)S(1)} %copy-done.11), channel_id=1, source_target_pairs={{0,2},{2,0},{4,6},{6,4},{8,10},{10,8},{12,14},{14,12},{16,18},{18,... | collective-permute-start | bytes 1769480 | tf_op jit(solution)/shard_map/ppermute | solution.py:79
  50.9 17.9 %collective-permute-start.20 = (bf16[576,512]{1,0:T(8,128)(2,1)}, bf16[576,512]{1,0:T(8,128)(2,1)S(1)}, u32[]{:S(2)}, u32[]{:S(2)}) collective-permute-start(bf16[576,512]{1,0:T(8,128)(2,1)} %collective-permute-done.8.refs_2_), channel_id=1, source_target_pairs={{0,2},{2,0},{4,6},{6,4},{8,10},{10,8},{12,14},{14,12},{16,18},{18,... | collective-permute-start | bytes 1769480 | tf_op jit(solution)/shard_map/ppermute | solution.py:79
  50.9 17.9 %collective-permute-start.21 = (bf16[576,512]{1,0:T(8,128)(2,1)}, bf16[576,512]{1,0:T(8,128)(2,1)S(1)}, u32[]{:S(2)}, u32[]{:S(2)}) collective-permute-start(bf16[576,512]{1,0:T(8,128)(2,1)} %collective-permute-done.16.refs_3_), channel_id=1, source_target_pairs={{0,2},{2,0},{4,6},{6,4},{8,10},{10,8},{12,14},{14,12},{16,18},{18,... | collective-permute-start | bytes 1769480 | tf_op jit(solution)/shard_map/ppermute | solution.py:79
  63.6 5.2 %collective-permute-start.22 = (bf16[288,512]{1,0:T(8,128)(2,1)S(1)}, bf16[288,512]{1,0:T(8,128)(2,1)S(1)}, u32[]{:S(2)}, u32[]{:S(2)}) collective-permute-start(bf16[288,512]{1,0:T(8,128)(2,1)S(1)} %collective-permute-done.18.refs_7_), channel_id=1, source_target_pairs={{0,2},{2,0},{4,6},{6,4},{8,10},{10,8},{12,14},{14,12},{16,18},{18,... | collective-permute-start | bytes 884744 | tf_op jit(solution)/shard_map/ppermute | solution.py:79
  63.6 13.7 %copy-start = (bf16[512,4,128]{2,1,0:T(4,128)(2,1)S(1)}, bf16[512,4,128]{2,1,0:T(4,128)(2,1)}, u32[]{:S(2)}) copy-start(bf16[512,4,128]{2,1,0:T(4,128)(2,1)} %param.25) | copy-start | bytes 1572868
  63.6 5.2 %collective-permute-start.17 = (bf16[32,1536]{1,0:T(8,128)(2,1)S(1)}, bf16[32,1536]{1,0:T(8,128)(2,1)S(1)}, u32[]{:S(2)}, u32[]{:S(2)}) collective-permute-start(bf16[32,1536]{1,0:T(8,128)(2,1)S(1)} %get-tuple-element.109), channel_id=1, source_target_pairs={{0,1},{1,0},{2,3},{3,2},{4,5},{5,4},{6,7},{7,6},{8,9},{9,8},{10,11... | collective-permute-start | bytes 294920 | tf_op jit(solution)/shard_map/ppermute | solution.py:729
  71.4 4.7 %collective-permute-start.23 = (bf16[32,1536]{1,0:T(8,128)(2,1)S(1)}, bf16[32,1536]{1,0:T(8,128)(2,1)S(1)}, u32[]{:S(2)}, u32[]{:S(2)}) collective-permute-start(bf16[32,1536]{1,0:T(8,128)(2,1)S(1)} %get-tuple-element.117), channel_id=1, source_target_pairs={{0,1},{1,0},{2,3},{3,2},{4,5},{5,4},{6,7},{7,6},{8,9},{9,8},{10,11... | collective-permute-start | bytes 294920 | tf_op jit(solution)/shard_map/ppermute | solution.py:737
  (5 other events, 10.8 us)
